TPU v7x, 32 devices: a whole 2x2x4 slice. The times are simulated.
32 devices in a mesh: groups: 2 (over x), dp: 16 (over z, y, core).
Axes of the slice: x: 2, y: 2, z: 4, core: 2. Of those that a mesh axis runs over, the one named last changes fastest.
Arguments:
- hidden: bfloat16 [16384, 5120], P(('groups', 'dp')), parts along dimension 0, may hold values from -6 to 6
- queries: bfloat16 [16384, 2560], P(('groups', 'dp')), parts along dimension 0, may hold values from -84 to 84
- route: int32 [16384], P(('groups', 'dp')), parts along dimension 0, may hold values from 0 to 16383, as said below
- positions: int32 [32768], P(('groups', 'dp')), parts along dimension 0, may hold values from 0 to 383, as said below
- key_matrix: bfloat16 [5120, 512], P('dp'), may hold values from -0.078125 to 0.078125
- value_matrix: bfloat16 [5120, 512], P('dp'), may hold values from -0.078125 to 0.078125
- key_projection_bias: bfloat16 [512], replicated, may hold values from -3 to 3
- value_projection_bias: bfloat16 [512], replicated, may hold values from -3 to 3
Outputs:
- attended: bfloat16 [16384, 2560], P(('groups', 'dp')), parts along dimension 0
There are 2 independent parts, one for each index of `groups`. A program takes and returns all parts, laid end to end along the dimension named above; an argument that names none is the same for every part. Nothing has to cross between parts.
Inputs may be any that keep to these rules, and one draw needn't show every extreme that they name: `route`: all values differ. Device r of dp owns slots r * 1024 to (r + 1) * 1024 - 1, in blocks of 512, and receives exactly 512 tokens. The tokens of one device go to one device at most 34 at a time, and this is reached. A rollout fills consecutive slots of one block with positions 0, 1, 2 and so on; the slots that route names are the live ones; a block's unnamed slots come before its rollouts and hold 0. Some block holds a rollout of exactly 384 tokens.
All inputs are finite; a program needn't handle non-finite values.
Results may differ from a plain program's by a relative error of at most 0.012.
Values may be sent and summed in bfloat16 or wider, within the bound.
No kernel may reach another device: no remote copies, remote signals or barrier semaphores. Data moves between devices by JAX's collectives and lax.ppermute only.
A program may use at most 128 MiB of HBM per device.

v0:
```python
import math

import jax
import jax.numpy as jnp
from jax import lax
from jax.sharding import PartitionSpec as P

QUERY_HEADS = 20
KEY_VALUE_HEADS = 4
HEAD_SIZE = 128
BLOCK_SLOTS = 512


def apply_rotary(rows, slot_offset, heads):
    block_count = rows.shape[0]
    half = HEAD_SIZE // 2
    frequency = 1000000.0 ** (-(jnp.arange(half, dtype=jnp.float32) * 2.0 / HEAD_SIZE))
    angle = slot_offset.astype(jnp.float32)[:, None] * frequency[None, :]
    cosine = jnp.cos(angle)[:, None, :]
    sine = jnp.sin(angle)[:, None, :]
    grid = rows.astype(jnp.float32).reshape(block_count, heads, HEAD_SIZE)
    first = grid[:, :, :half]
    second = grid[:, :, half:]
    turned = jnp.concatenate(
        [first * cosine - second * sine, second * cosine + first * sine], axis=2
    )
    return turned.reshape(block_count, heads * HEAD_SIZE).astype(jnp.bfloat16)


def causal_block_attention(pieces):
    query_tile_rows, key_tile_rows, value_tile_rows, spot_block = pieces
    block_count = query_tile_rows.shape[0]
    head_groups = QUERY_HEADS // KEY_VALUE_HEADS
    query_block_grid = query_tile_rows.reshape(block_count, KEY_VALUE_HEADS, head_groups, HEAD_SIZE)
    key_block_grid = key_tile_rows.reshape(block_count, KEY_VALUE_HEADS, HEAD_SIZE)
    value_block_grid = value_tile_rows.reshape(block_count, KEY_VALUE_HEADS, HEAD_SIZE)
    scores = jnp.einsum(
        "qhgd,khd->hgqk", query_block_grid, key_block_grid, preferred_element_type=jnp.float32
    ) / math.sqrt(HEAD_SIZE)
    inner = jnp.arange(block_count, dtype=jnp.int32)
    visible = (inner[None, :] <= inner[:, None]) & (
        inner[None, :] >= inner[:, None] - spot_block[:, None]
    )
    scores = jnp.where(visible, scores, -jnp.inf)
    top = jnp.max(scores, axis=3, keepdims=True)
    weights = jnp.exp(scores - top)
    totals = jnp.sum(weights, axis=3)
    probs = weights.astype(jnp.bfloat16)
    mixed = jnp.einsum(
        "hgqk,khd->qhgd", probs, value_block_grid, preferred_element_type=jnp.float32
    )
    mixed = mixed / jnp.transpose(totals, (2, 0, 1))[:, :, :, None]
    return mixed.reshape(block_count, QUERY_HEADS * HEAD_SIZE).astype(jnp.bfloat16)


def add_projection(left, pieces):
    return (
        jnp.dot(left, pieces[0], preferred_element_type=jnp.float32),
        jnp.dot(left, pieces[1], preferred_element_type=jnp.float32),
    )


def project_own(hidden, key_matrix, value_matrix, key_projection_bias, value_projection_bias):
    totals = add_projection(
        hidden,
        (
            lax.all_gather(key_matrix, "dp", axis=0, tiled=True),
            lax.all_gather(value_matrix, "dp", axis=0, tiled=True),
        ),
    )
    key_rows = (totals[0] + key_projection_bias.astype(jnp.float32)).astype(jnp.bfloat16)
    value_rows = (totals[1] + value_projection_bias.astype(jnp.float32)).astype(jnp.bfloat16)
    return jnp.concatenate([key_rows, value_rows], axis=1)


def local(
    hidden,
    queries,
    route,
    positions,
    key_matrix,
    value_matrix,
    key_projection_bias,
    value_projection_bias,
):
    ranks = lax.axis_size("dp")
    rows = hidden.shape[0]
    slots = positions.shape[0]
    spare = rows // ranks + 2
    width = ranks * spare
    paired_width = key_matrix.shape[1]
    target = route // slots
    place = route - target * slots
    member = (target[:, None] == jnp.arange(ranks, dtype=jnp.int32)[None, :]).astype(jnp.int32)
    order = jnp.sum(jnp.cumsum(member, axis=0) * member, axis=1) - 1
    bucket = target * spare + order
    outgoing = jnp.full((width,), slots, jnp.int32).at[bucket].set(place)
    arrived = lax.all_to_all(
        outgoing.reshape(ranks, spare), "dp", split_axis=0, concat_axis=0, tiled=True
    ).reshape(width)
    query_buf = jnp.zeros((width, queries.shape[1]), jnp.bfloat16).at[bucket].set(queries)
    own_pairs = project_own(
        hidden, key_matrix, value_matrix, key_projection_bias, value_projection_bias
    )
    pair_buf = jnp.zeros((width, 2 * paired_width), jnp.bfloat16).at[bucket].set(own_pairs)
    got_query, got_pairs = (
        lax.all_to_all(
            query_buf.reshape(ranks, spare, -1), "dp", split_axis=0, concat_axis=0, tiled=True
        ),
        lax.all_to_all(
            pair_buf.reshape(ranks, spare, -1), "dp", split_axis=0, concat_axis=0, tiled=True
        ),
    )
    got_query = got_query.reshape(width, -1)
    got_pairs = got_pairs.reshape(width, -1)
    query_slot_rows = (
        jnp.zeros((slots, got_query.shape[1]), jnp.bfloat16).at[arrived].set(got_query, mode="drop")
    )
    paired_slot_rows = (
        jnp.zeros((slots, 2 * paired_width), jnp.bfloat16).at[arrived].set(got_pairs, mode="drop")
    )
    query_turned = apply_rotary(query_slot_rows, positions, QUERY_HEADS)
    key_rotated = apply_rotary(paired_slot_rows[:, :paired_width], positions, KEY_VALUE_HEADS)
    block_list = slots // BLOCK_SLOTS
    attended = lax.map(
        causal_block_attention,
        (
            query_turned.reshape(block_list, BLOCK_SLOTS, -1),
            key_rotated.reshape(block_list, BLOCK_SLOTS, -1),
            paired_slot_rows[:, paired_width:].reshape(block_list, BLOCK_SLOTS, -1),
            positions.reshape(block_list, BLOCK_SLOTS),
        ),
    )
    attended = attended.reshape(slots, -1)
    leaving = attended[jnp.minimum(arrived, slots - 1)]
    returned = lax.all_to_all(
        leaving.reshape(ranks, spare, -1), "dp", split_axis=0, concat_axis=0, tiled=True
    ).reshape(width, -1)
    return returned[bucket]


def solution(mesh):
    placed = (
        P(("groups", "dp"), None),
        P(("groups", "dp"), None),
        P(("groups", "dp")),
        P(("groups", "dp")),
        P("dp", None),
        P("dp", None),
        P(),
        P(),
    )
    return jax.shard_map(
        local, mesh=mesh, in_specs=placed, out_specs=P(("groups", "dp"), None), check_vma=False
    )
```

profile of v0, /device:TPU:13, one launch (start us, length us, event | category | flops | bytes accessed | tf_op | source)
XLA Modules:
  0.0 430.8 jit_solution(10257486969026635308)
XLA Ops:
  10.2 2.4 scatter_custom_fusion
  13.4 6.6 %all-to-all-start = ((s32[16,1,34]{2,1,0:T(1,128)}), s32[16,1,34]{2,1,0:T(1,128)S(1)}, u32[]{:S(2)}, u32[]{:S(2)}) async-start(s32[16,1,34]{2,1,0:T(1,128)} %all_to_all.15), calls=%async_computation | async-start | bytes 16384 | tf_op jit(solution)/shard_map/all_to_all | solution.py:98
  19.9 6.2 %scatter_custom_fusion.3 = bf16[544,2560]{1,0:T(8,128)(2,1)S(1)} fusion(s32[512]{0:T(512)S(1)} %compare_select_fusion.2, bf16[512,2560]{1,0:T(8,128)(2,1)} %param.11, bf16[]{:T(256)} %constant.32.clone.1), kind=kCustom, calls=%fused_computation.34 | custom fusion | bytes 2785792 | tf_op jit(solution)/shard_map/scatter | solution.py:101
  26.2 2.6 reshape.217
  28.8 6.5 %all-to-all-start.2 = ((bf16[16,34,2560]{2,1,0:T(8,128)(2,1)}), bf16[16,34,2560]{2,1,0:T(8,128)(2,1)S(1)}, u32[]{:S(2)}, u32[]{:S(2)}) async-start(bf16[16,34,2560]{2,1,0:T(8,128)(2,1)} %reshape.217), calls=%async_computation.2 | async-start | bytes 6553600 | tf_op jit(solution)/shard_map/all_to_all | solution.py:107
  35.3 70.2 %all-gather.3.cloned.1.call-done = bf16[5120,512]{1,0:T(8,128)(2,1)} async-done(((bf16[320,512]{1,0:T(8,128)(2,1)}), bf16[5120,512]{1,0:T(8,128)(2,1)}) %all-gather.3.cloned.1.call-update) | async-done | bytes 5242896 | tf_op jit(solution)/shard_map/all_gather | solution.py:67
  105.5 7.8 %fusion.16 = bf16[512,512]{0,1:T(8,128)(2,1)} fusion(bf16[512,5120]{1,0:T(8,128)(2,1)} %param.10, bf16[5120,512]{1,0:T(8,128)(2,1)} %all-gather.3.cloned.1.call-done, f32[512]{0:T(512)S(1)} %convert_element_type.50), kind=kOutput, calls=%fused_computation.38 | convolution fusion | flops 2684878848 | bytes 11012096 | tf_op jit(solution)/shard_map/dot_general | solution.py:58
  113.3 58.8 %all-gather.5.cloned.1.call-done = bf16[5120,512]{1,0:T(8,128)(2,1)} async-done(((bf16[320,512]{1,0:T(8,128)(2,1)}), bf16[5120,512]{1,0:T(8,128)(2,1)}) %all-gather.5.cloned.1.call-update) | async-done | bytes 5242896 | tf_op jit(solution)/shard_map/all_gather | solution.py:68
  172.0 7.0 %fusion.17 = bf16[512,512]{0,1:T(8,128)(2,1)S(1)} fusion(bf16[512,5120]{1,0:T(8,128)(2,1)} %param.10, bf16[5120,512]{1,0:T(8,128)(2,1)} %all-gather.5.cloned.1.call-done, f32[512]{0:T(512)S(1)} %convert_element_type.52), kind=kOutput, calls=%fused_computation.39 | convolution fusion | flops 2684878848 | bytes 11012096 | tf_op jit(solution)/shard_map/dot_general | solution.py:59
  180.1 2.3 copy.25
  182.4 4.2 scatter_custom_fusion.1
  186.6 2.3 reshape.211
  188.9 5.9 %all-to-all-start.1 = ((bf16[16,34,1024]{2,1,0:T(8,128)(2,1)}), bf16[16,34,1024]{2,1,0:T(8,128)(2,1)}, u32[]{:S(2)}, u32[]{:S(2)}) async-start(bf16[16,34,1024]{2,1,0:T(8,128)(2,1)} %reshape.211), calls=%async_computation.1 | async-start | bytes 2621440 | tf_op jit(solution)/shard_map/all_to_all | solution.py:110
  194.8 1.8 multiply_cosine_fusion
  197.6 1.9 copy.27
  202.6 2.4 reshape.280
  204.9 12.9 %scatter_custom_fusion.4 = bf16[1024,2560]{1,0:T(8,128)(2,1)} fusion(s32[544]{0:T(1024)S(1)} %get-tuple-element.51, bf16[544,2560]{1,0:T(8,128)(2,1)} %reshape.280, bf16[]{:T(256)} %constant.32.clone.1), kind=kCustom, calls=%fused_computation.30 | custom fusion | bytes 5243392 | tf_op jit(solution)/shard_map/scatter | solution.py:117
  217.8 8.3 %copy.28 = f32[1024,2560]{0,1:T(8,128)} copy(bf16[1024,2560]{1,0:T(8,128)(2,1)} %scatter_custom_fusion.4) | data formatting | bytes 15728640 | tf_op jit(solution)/shard_map/reshape | solution.py:21
  226.1 5.0 %subtract_convert_fusion = (bf16[1024,20,64]{0,2,1:T(8,128)(2,1)S(1)}, bf16[1024,20,64]{0,2,1:T(8,128)(2,1)S(1)}) fusion(f32[1024,20,128]{0,2,1:T(8,128)} %bitcast.87, f32[1024,64]{0,1:T(8,128)S(1)} %copy-done.1, f32[1024,64]{0,1:T(8,128)S(1)} %get-tuple-element.76), kind=kLoop, calls=%fused_computation.29 | loop fusion | flops 10485760 | bytes 16252928 | tf_op jit(solution)/shard_map/convert.4
  231.0 2.9 pad_maximum_fusion
  234.0 9.5 %convert_element_type.56 = bf16[2,512,2560]{1,0,2:T(2,128)(2,1)} reshape(bf16[1024,20,128]{0,2,1:T(8,128)(2,1)} %pad_maximum_fusion) | data formatting | bytes 10485760 | tf_op jit(solution)/shard_map/convert_element_type | solution.py:27
  243.4 5.7 %copy.31 = bf16[2,512,2560]{1,2,0:T(8,128)(2,1)} copy(bf16[2,512,2560]{1,0,2:T(2,128)(2,1)} %convert_element_type.56) | data formatting | bytes 10485760 | tf_op jit(solution)/shard_map/while | solution.py:125
  249.2 1.5 reshape.264
  250.6 6.4 %scatter_custom_fusion.2 = bf16[1024,1024]{1,0:T(8,128)(2,1)S(1)} fusion(s32[544]{0:T(1024)S(1)} %get-tuple-element.51, bf16[544,1024]{1,0:T(8,128)(2,1)S(1)} %reshape.264, bf16[]{:T(256)} %constant.32.clone.1), kind=kCustom, calls=%fused_computation.43 | custom fusion | bytes 2097154 | tf_op jit(solution)/shard_map/scatter | solution.py:120
  257.0 2.0 slice_convert_fusion
  259.0 2.2 reshape.225
  261.2 1.6 subtract_convert_fusion.1
  265.5 59.3 %while.10 = (s32[]{:T(128)}, bf16[2,512,2560]{2,1,0:T(8,128)(2,1)}, bf16[2,512,512]{2,1,0:T(8,128)(2,1)}, s32[2,512]{1,0:T(2,128)S(1)}, bf16[2,512,512]{2,1,0:T(...) while((s32[]{:T(128)}, bf16[2,512,2560]{2,1,0:T(8,128)(2,1)}, bf16[2,512,512]{2,1,0:T(8,128)(2,1)}, ...), condition=%wide.region_11.12_spmd, body=%wide.region_8.11_spmd.sunk | while | flops 2745414144 | bytes 174279312 | solution.py:125
  267.1 1.9 constant_dynamic-slice_fusion.9
  269.0 3.4 fusion.51
  272.5 4.6 %fusion.52 = f32[4,5,512]{2,1,0:T(8,128)S(1)} fusion(f32[4,512,512,5]{2,1,3,0:T(8,128)S(1)} %get-tuple-element.120, f32[4,5,512]{2,1,0:T(8,128)S(1)} %get-tuple-element.121, pred[512,512]{0,1:T(8,128)(4,1)S(1)} %fusion.50), kind=kLoop, calls=%fused_computation.9.clone.1 | loop fusion | flops 20961280 | bytes 21315584 | tf_op jit(solution)/shard_map/while/body/eval_jaxpr/reduce_sum | solution.py:47
  277.1 2.4 copy-done
  279.7 10.7 %fusion.53 = bf16[512,4,5,128]{0,3,2,1:T(8,128)(2,1)} fusion(f32[512,4,5]{0,2,1:T(8,128)S(1)} %bitcast.89, bf16[512,4,128,1]{0,2,3,1:T(8,128)(2,1)S(1)} %bitcast.88, f32[4,512,512,5]{2,1,3,0:T(8,128)} %copy-done, f32[4,5,512]{2,1,0:T(8,128)S(1)} %get-tuple-element.121, pred[512,512]{0,1:T(8,128)(4,1)S(1)} %fusion.50), kind=kOutput, calls=%fused_computation.15.clone.1 | convolution fusion | flops 1365770240 | bytes 24461312 | tf_op jit(solution)/shard_map/while/body/eval_jaxpr/hgqk,khd->qhgd/dot_general | solution.py:49
  290.4 3.0 copy.50
  293.4 1.7 constant_dynamic-update-slice_fusion.2
  296.8 1.9 constant_dynamic-slice_fusion.9
  298.7 3.5 fusion.51
  302.2 4.6 %fusion.52 = f32[4,5,512]{2,1,0:T(8,128)S(1)} fusion(f32[4,512,512,5]{2,1,3,0:T(8,128)S(1)} %get-tuple-element.120, f32[4,5,512]{2,1,0:T(8,128)S(1)} %get-tuple-element.121, pred[512,512]{0,1:T(8,128)(4,1)S(1)} %fusion.50), kind=kLoop, calls=%fused_computation.9.clone.1 | loop fusion | flops 20961280 | bytes 21315584 | tf_op jit(solution)/shard_map/while/body/eval_jaxpr/reduce_sum | solution.py:47
  306.8 2.4 copy-done
  309.4 10.7 %fusion.53 = bf16[512,4,5,128]{0,3,2,1:T(8,128)(2,1)} fusion(f32[512,4,5]{0,2,1:T(8,128)S(1)} %bitcast.89, bf16[512,4,128,1]{0,2,3,1:T(8,128)(2,1)S(1)} %bitcast.88, f32[4,512,512,5]{2,1,3,0:T(8,128)} %copy-done, f32[4,5,512]{2,1,0:T(8,128)S(1)} %get-tuple-element.121, pred[512,512]{0,1:T(8,128)(4,1)S(1)} %fusion.50), kind=kOutput, calls=%fused_computation.15.clone.1 | convolution fusion | flops 1365770240 | bytes 24461312 | tf_op jit(solution)/shard_map/while/body/eval_jaxpr/hgqk,khd->qhgd/dot_general | solution.py:49
  320.1 3.0 copy.50
  323.1 1.7 constant_dynamic-update-slice_fusion.2
  324.8 10.9 %gather_fusion = bf16[544,2560]{1,0:T(8,128)(2,1)S(1)} fusion(bf16[1024,2560]{1,0:T(8,128)(2,1)} %bitcast.84, s32[1024]{0:T(1024)S(1)} %copy-done.6), kind=kCustom, calls=%fused_computation | custom fusion | bytes 5572736 | tf_op jit(solution)/shard_map/gather | solution.py:135
  335.7 2.5 reshape.222
  338.3 6.2 %all-to-all-start.3 = ((bf16[16,34,2560]{2,1,0:T(8,128)(2,1)}), bf16[16,34,2560]{2,1,0:T(8,128)(2,1)}, u32[]{:S(2)}, u32[]{:S(2)}) async-start(bf16[16,34,2560]{2,1,0:T(8,128)(2,1)} %reshape.222), calls=%async_computation.3 | async-start | bytes 6553600 | tf_op jit(solution)/shard_map/all_to_all | solution.py:136
  344.5 72.8 %all-to-all-done.3 = bf16[16,34,2560]{2,1,0:T(8,128)(2,1)} async-done(((bf16[16,34,2560]{2,1,0:T(8,128)(2,1)}), bf16[16,34,2560]{2,1,0:T(8,128)(2,1)}, u32[]{:S(2)}, u32[]{:S(2)}) %all-to-all-start.3) | async-done | bytes 2785312 | tf_op jit(solution)/shard_map/all_to_all | solution.py:136
  417.3 3.0 reshape.223
  420.3 3.5 gather_fusion.1
  (66 shorter events, 15.9 us)
Async XLA Ops:
  6.5 99.0 %all-gather.3.cloned.1.call-start = ((), (), s32[]{:S(2)}) async-start(), calls=%async_computation.4 | async-start | bytes 5570560 | tf_op jit(solution)/shard_map/all_gather | solution.py:67
  7.3 164.8 %all-gather.5.cloned.1.call-start = ((), (), s32[]{:S(2)}) async-start(), calls=%async_computation.5 | async-start | bytes 5570560 | tf_op jit(solution)/shard_map/all_gather | solution.py:68
  10.2 172.1 %copy-start.7 = (s32[512]{0:T(512)}, s32[512]{0:T(512)S(1)}, u32[]{:S(2)}) copy-start(s32[512]{0:T(512)S(1)} %compare_select_fusion.2) | copy-start | bytes 6148
  13.4 15.4 %all-to-all-start = ((s32[16,1,34]{2,1,0:T(1,128)}), s32[16,1,34]{2,1,0:T(1,128)S(1)}, u32[]{:S(2)}, u32[]{:S(2)}) async-start(s32[16,1,34]{2,1,0:T(1,128)} %all_to_all.15), calls=%async_computation | async-start | bytes 16384 | tf_op jit(solution)/shard_map/all_to_all | solution.py:98
  28.7 6.5 %copy-start.9 = (bf16[512]{0:T(512)(128)(2,1)S(1)}, bf16[512]{0:T(512)(128)(2,1)}, u32[]{:S(2)}) copy-start(bf16[512]{0:T(512)(128)(2,1)} %param.16) | copy-start | bytes 3076
  28.8 6.5 %copy-start.10 = (bf16[512]{0:T(512)(128)(2,1)S(1)}, bf16[512]{0:T(512)(128)(2,1)}, u32[]{:S(2)}) copy-start(bf16[512]{0:T(512)(128)(2,1)} %param.17) | copy-start | bytes 3076
  28.8 160.1 %all-to-all-start.2 = ((bf16[16,34,2560]{2,1,0:T(8,128)(2,1)}), bf16[16,34,2560]{2,1,0:T(8,128)(2,1)S(1)}, u32[]{:S(2)}, u32[]{:S(2)}) async-start(bf16[16,34,2560]{2,1,0:T(8,128)(2,1)} %reshape.217), calls=%async_computation.2 | async-start | bytes 6553600 | tf_op jit(solution)/shard_map/all_to_all | solution.py:107
  172.0 7.0 %copy-start.4 = (bf16[512,512]{0,1:T(8,128)(2,1)S(1)}, bf16[512,512]{0,1:T(8,128)(2,1)}, u32[]{:S(2)}) copy-start(bf16[512,512]{0,1:T(8,128)(2,1)} %fusion.16) | copy-start | bytes 1572868
  182.4 12.4 %copy-start.5 = (s32[1024]{0:T(1024)S(1)}, s32[1024]{0:T(1024)}, u32[]{:S(2)}) copy-start(s32[1024]{0:T(1024)} %param.13) | copy-start | bytes 12292
  188.9 60.3 %all-to-all-start.1 = ((bf16[16,34,1024]{2,1,0:T(8,128)(2,1)}), bf16[16,34,1024]{2,1,0:T(8,128)(2,1)}, u32[]{:S(2)}, u32[]{:S(2)}) async-start(bf16[16,34,1024]{2,1,0:T(8,128)(2,1)} %reshape.211), calls=%async_computation.1 | async-start | bytes 2621440 | tf_op jit(solution)/shard_map/all_to_all | solution.py:110
  217.8 8.3 %copy-start.1 = (f32[1024,64]{0,1:T(8,128)S(1)}, f32[1024,64]{0,1:T(8,128)}, u32[]{:S(2)}) copy-start(f32[1024,64]{0,1:T(8,128)} %get-tuple-element.77) | copy-start | bytes 786436
  259.0 2.2 copy-start.2
  259.0 2.2 copy-start.3
  265.5 59.4 %copy-start.6 = (s32[1024]{0:T(1024)S(1)}, s32[1024]{0:T(1024)}, u32[]{:S(2)}) copy-start(s32[1024]{0:T(1024)} %pad_clamp_fusion.1) | copy-start | bytes 12292
  272.5 7.0 %copy-start = (f32[4,512,512,5]{2,1,3,0:T(8,128)}, f32[4,512,512,5]{2,1,3,0:T(8,128)S(1)}, u32[]{:S(2)}) copy-start(f32[4,512,512,5]{2,1,3,0:T(8,128)S(1)} %get-tuple-element.120) | copy-start | bytes 62914564 | tf_op jit(solution)/shard_map/while
  302.2 7.0 %copy-start = (f32[4,512,512,5]{2,1,3,0:T(8,128)}, f32[4,512,512,5]{2,1,3,0:T(8,128)S(1)}, u32[]{:S(2)}) copy-start(f32[4,512,512,5]{2,1,3,0:T(8,128)S(1)} %get-tuple-element.120) | copy-start | bytes 62914564 | tf_op jit(solution)/shard_map/while
  338.3 6.2 %copy-start.8 = (s32[512]{0:T(512)S(1)}, s32[512]{0:T(512)}, u32[]{:S(2)}) copy-start(s32[512]{0:T(512)} %copy-done.7) | copy-start | bytes 6148
  338.3 79.0 %all-to-all-start.3 = ((bf16[16,34,2560]{2,1,0:T(8,128)(2,1)}), bf16[16,34,2560]{2,1,0:T(8,128)(2,1)}, u32[]{:S(2)}, u32[]{:S(2)}) async-start(bf16[16,34,2560]{2,1,0:T(8,128)(2,1)} %reshape.222), calls=%async_computation.3 | async-start | bytes 6553600 | tf_op jit(solution)/shard_map/all_to_all | solution.py:136
Sparse Core Ops, SparseCore 0:
  9.6 95.8 all-gather.2
  107.8 64.2 all-gather.4
where the time goes:
time: 438 us; the launch traced here: 431 us
  waiting for transfers between devices  203 us (46%)
  local copies, waits for them, and re-layouts  116 us (26%)
  matrix products  43.2 us (10%)
  other arithmetic  28.9 us (7%)
  starting transfers between devices  25.1 us (6%)
  between operations  13.9 us (3%)
    all_to_all x1, waiting for transfers between devices, local(): lax.all_to_all(leaving.reshape(ranks, spare, -1), 'dp', split_axis=0, con...  72.8 us
    all_gather x1, waiting for transfers between devices, project_own(): lax.all_gather(key_matrix, 'dp', axis=0, tiled=True)  70.2 us
    all_gather x1, waiting for transfers between devices, project_own(): lax.all_gather(value_matrix, 'dp', axis=0, tiled=True)  58.8 us
    dot_general x2, matrix products, causal_block_attention(): jnp.einsum('hgqk,khd->qhgd', probs, value_block_grid, preferred_element_t...  21.5 us
    scatter x1, local copies, waits for them, and re-layouts, local(): jnp.zeros((slots, got_query.shape[1]), jnp.bfloat16).at[arrived]  12.9 us
    gather x1, local copies, waits for them, and re-layouts, local(): leaving = attended[jnp.minimum(arrived, slots - 1)]  10.9 us
    convert_element_type x2, local copies, waits for them, and re-layouts, apply_rotary(): return turned.reshape(block_count, heads * HEAD_SIZE).astype(jnp.bfloat16)  10.7 us
    reshape x2, local copies, waits for them, and re-layouts, apply_rotary(): grid = rows.astype(jnp.float32).reshape(block_count, heads, HEAD_SIZE)  10.5 us
  transfers between devices with their start and end apart: 6, of which 3 were waited for; matrix products, arithmetic and copies ran while one was open for 21% of the time, Pallas kernels for 0%

commit v1 on v0

--- a/solution.py
+++ b/solution.py
@@ -1,14 +1,329 @@
+import functools
 import math
 
 import jax
 import jax.numpy as jnp
 from jax import lax
+from jax.experimental import pallas as pl
+from jax.experimental.pallas import tpu as pltpu
 from jax.sharding import PartitionSpec as P
 
 QUERY_HEADS = 20
 KEY_VALUE_HEADS = 4
 HEAD_SIZE = 128
 BLOCK_SLOTS = 512
+HEAD_GROUPS = QUERY_HEADS // KEY_VALUE_HEADS
+CHUNKS = 2
+CHUNK_HEADS = KEY_VALUE_HEADS // CHUNKS
+PLANE = 4
+GATHER_LIMIT = 40 * 2**20
+MASKED = -1e30
+VMEM = pl.BlockSpec(memory_space=pltpu.VMEM)
+SMEM = pl.BlockSpec(memory_space=pltpu.SMEM)
+ANY = pl.BlockSpec(memory_space=pl.ANY)
+
+
+def grant(mebibytes):
+    return pltpu.CompilerParams(vmem_limit_bytes=mebibytes * 2**20)
+
+
+def one_hot_rows(count, index_row):
+    rows = lax.broadcasted_iota(jnp.int32, (count, index_row.shape[1]), 0)
+    return (rows == index_row).astype(jnp.float32).astype(jnp.bfloat16)
+
+
+def contract(left, right, left_dim, right_dim):
+    return lax.dot_general(
+        left, right, (((left_dim,), (right_dim,)), ((), ())), preferred_element_type=jnp.float32
+    )
+
+
+def turn(rows, cosine, sine):
+    return (rows * cosine + pltpu.roll(rows, HEAD_SIZE // 2, 1) * sine).astype(jnp.bfloat16)
+
+
+def order_kernel(ranks, slots, spare, stride, route_ref, bucket_ref, seat_ref, sorted_ref):
+    route = route_ref[...]
+    count = route.shape[1]
+    target = lax.div(route, slots)
+    member = (lax.broadcasted_iota(jnp.int32, (ranks, count), 0) == target).astype(jnp.float32)
+    before = lax.broadcasted_iota(jnp.int32, (count, count), 0) < lax.broadcasted_iota(
+        jnp.int32, (count, count), 1
+    )
+    ahead = contract(
+        member.astype(jnp.bfloat16), before.astype(jnp.float32).astype(jnp.bfloat16), 1, 0
+    )
+    order = jnp.sum(member * ahead, axis=0, keepdims=True).astype(jnp.int32)
+    bucket = target * spare + order
+    bucket_ref[...] = bucket
+    seat_ref[...] = target * stride + order
+    high = lax.div(route, HEAD_SIZE)
+    low = route - high * HEAD_SIZE
+    line = lax.broadcasted_iota(jnp.int32, (8, count), 0)
+    digits = jnp.where(line == 0, high, jnp.where(line == 1, low, jnp.where(line == 2, 1, 0)))
+    placed = contract(
+        digits.astype(jnp.float32).astype(jnp.bfloat16), one_hot_rows(ranks * spare, bucket), 1, 1
+    )
+    found = placed[0:1] * HEAD_SIZE + placed[1:2] + placed[2:3] - 1.0
+    sorted_ref[...] = found.astype(jnp.int32)
+
+
+def query_kernel(
+    route_ref, seat_ref, positions_ref, frequency_ref, queries_ref,
+    turned_ref, bounds_ref, cosine_ref, sine_ref,
+):
+    route = route_ref[...]
+    count = route.shape[0]
+    lines = positions_ref.shape[0]
+    line = lax.div(route, HEAD_SIZE)
+    lane = route - line * HEAD_SIZE
+    pick = (lax.broadcasted_iota(jnp.int32, (count, lines), 1) == line).astype(jnp.float32)
+    pick = pick.astype(jnp.bfloat16)
+    positions = positions_ref[...]
+    half = lax.div(positions, 2)
+    rest = positions - half * 2
+    rows = 2.0 * contract(pick, half.astype(jnp.float32).astype(jnp.bfloat16), 1, 0) + contract(
+        pick, rest.astype(jnp.float32).astype(jnp.bfloat16), 1, 0
+    )
+    lanes = lax.broadcasted_iota(jnp.int32, (count, HEAD_SIZE), 1)
+    spot = jnp.sum(jnp.where(lanes == lane, rows, 0.0), axis=1, keepdims=True)
+    angle = spot * frequency_ref[...]
+    cosine = jnp.cos(angle)
+    sine = jnp.sin(angle)
+    sine = jnp.where(lanes < HEAD_SIZE // 2, -sine, sine)
+    cosine_ref[...] = cosine
+    sine_ref[...] = sine
+    seats = one_hot_rows(turned_ref.shape[0], seat_ref[...])
+    first = route - spot.astype(jnp.int32)
+    first_line = lax.div(first, HEAD_SIZE)
+    first_lane = first - first_line * HEAD_SIZE
+    digits = jnp.where(lanes == 0, line, 0)
+    digits = jnp.where(lanes == 1, lane, digits)
+    digits = jnp.where(lanes == 2, first_line, digits)
+    digits = jnp.where(lanes == 3, first_lane, digits)
+    digits = jnp.where(lanes == 4, 1, digits)
+    placed = contract(seats, digits.astype(jnp.float32).astype(jnp.bfloat16), 1, 0)
+    live = placed[:, 4:5] - 1.0
+    last = placed[:, 0:1] * HEAD_SIZE + placed[:, 1:2] + live
+    start = placed[:, 2:3] * HEAD_SIZE + placed[:, 3:4] + live
+    seat_lanes = lax.broadcasted_iota(jnp.int32, placed.shape, 1)
+    bounds_ref[...] = jnp.where(seat_lanes == 0, last, start).astype(jnp.int32)
+    for head in range(queries_ref.shape[1] // HEAD_SIZE):
+        span = slice(head * HEAD_SIZE, (head + 1) * HEAD_SIZE)
+        turned = turn(queries_ref[:, span].astype(jnp.float32), cosine, sine)
+        turned_ref[:, span] = contract(seats, turned, 1, 0).astype(jnp.bfloat16)
+
+
+def project_kernel(
+    owners_ref, hidden_ref, bias_ref, cosine_ref, sine_ref, bucket_ref, *refs
+):
+    ranks = owners_ref.shape[0]
+    blocks, outs = refs[:ranks], refs[ranks : ranks + CHUNKS]
+    matrix, done = refs[ranks + CHUNKS :]
+    depth = blocks[0].shape[0]
+    copies = [
+        pltpu.make_async_copy(
+            blocks[j],
+            matrix.at[pl.ds(pl.multiple_of(owners_ref[j] * depth, 16), depth)],
+            done.at[j],
+        )
+        for j in range(ranks)
+    ]
+    for copy in copies:
+        copy.start()
+    places = one_hot_rows(outs[0].shape[0], bucket_ref[...])
+    for copy in copies:
+        copy.wait()
+    wide = CHUNK_HEADS * HEAD_SIZE
+    for chunk in range(CHUNKS):
+        for part in range(2):
+            first = part * KEY_VALUE_HEADS * HEAD_SIZE + chunk * wide
+            span = slice(first, first + wide)
+            rows = contract(hidden_ref[...], matrix[:, span], 1, 0) + bias_ref[:, span]
+            rows = rows.astype(jnp.bfloat16)
+            for head in range(CHUNK_HEADS):
+                one = rows[:, head * HEAD_SIZE : (head + 1) * HEAD_SIZE]
+                if part == 0:
+                    one = turn(one.astype(jnp.float32), cosine_ref[...], sine_ref[...])
+                at = part * wide + head * HEAD_SIZE
+                outs[chunk][:, at : at + HEAD_SIZE] = contract(places, one, 1, 0).astype(
+                    jnp.bfloat16
+                )
+
+
+def attend_kernel(
+    chunk, spare, window, stride, queries_ref, bounds_ref, routes_ref, seat_ref, *refs
+):
+    ranks = routes_ref.shape[0]
+    blocks, out_ref, mixed_ref = refs[:ranks], refs[ranks], refs[ranks + 1]
+    wide = CHUNK_HEADS * HEAD_SIZE
+    scale = math.log2(math.e) / math.sqrt(HEAD_SIZE)
+
+    def one_group(group, carry):
+        seats = pl.ds(pl.multiple_of(group * stride, 16), stride)
+        start = pl.multiple_of(lax.div(group * spare, 16) * 16, 16)
+        keys_at = pl.ds(start, window)
+        routes = routes_ref[group]
+        visible = (routes <= bounds_ref[seats, 0:1]) & (routes >= bounds_ref[seats, 1:2])
+        veil = jnp.where(visible, 0.0, MASKED)
+        veil = jnp.concatenate([veil] * HEAD_GROUPS, axis=0)
+        for head in range(CHUNK_HEADS):
+            span = slice(head * HEAD_SIZE, (head + 1) * HEAD_SIZE)
+            value_span = slice(wide + head * HEAD_SIZE, wide + (head + 1) * HEAD_SIZE)
+            heads = [
+                slice(at * HEAD_SIZE, (at + 1) * HEAD_SIZE)
+                for at in range(head * HEAD_GROUPS, (head + 1) * HEAD_GROUPS)
+            ]
+            query = jnp.concatenate([queries_ref[seats, one] for one in heads], axis=0)
+            keys = jnp.concatenate([block[keys_at, span] for block in blocks], axis=0)
+            values = jnp.concatenate([block[keys_at, value_span] for block in blocks], axis=0)
+            scores = contract(query, keys, 1, 1) * scale + veil
+            weights = jnp.exp2(scores - jnp.max(scores, axis=1, keepdims=True))
+            totals = jnp.sum(weights, axis=1, keepdims=True)
+            mixed = contract(weights.astype(jnp.bfloat16), values, 1, 0) / totals
+            mixed = mixed.astype(jnp.bfloat16)
+            for place, one in enumerate(heads):
+                mixed_ref[seats, one] = mixed[place * stride : (place + 1) * stride]
+        return carry
+
+    lax.fori_loop(0, ranks, one_group, 0)
+    seats = one_hot_rows(mixed_ref.shape[0], seat_ref[...])
+    for head in range(out_ref.shape[1] // HEAD_SIZE):
+        span = slice(head * HEAD_SIZE, (head + 1) * HEAD_SIZE)
+        out_ref[:, span] = contract(seats, mixed_ref[:, span], 0, 0).astype(jnp.bfloat16)
+
+
+def spread(block, ranks):
+    ring = [(rank, (rank + PLANE) % ranks) for rank in range(ranks)]
+    across = [(rank, rank ^ 2) for rank in range(ranks)]
+    beside = [(rank, rank ^ 1) for rank in range(ranks)]
+    lanes = [block]
+    for _ in range(ranks // PLANE - 1):
+        lanes.append(lax.ppermute(lanes[-1], "dp", ring))
+    others = [lax.ppermute(lane, "dp", across) for lane in lanes]
+    held = lanes + others
+    return held + [lax.ppermute(one, "dp", beside) for one in held]
+
+
+def source_order(ranks):
+    me = lax.axis_index("dp")
+    lane, plane = me % PLANE, me // PLANE
+    steps = ranks // PLANE
+    planes = (plane - jnp.arange(steps, dtype=jnp.int32)) % steps
+    return jnp.concatenate([planes * PLANE + (lane ^ flip) for flip in (0, 2, 1, 3)])
+
+
+def gather_plan(
+    hidden,
+    queries,
+    route,
+    positions,
+    key_matrix,
+    value_matrix,
+    key_projection_bias,
+    value_projection_bias,
+):
+    ranks = lax.axis_size("dp")
+    rows = hidden.shape[0]
+    slots = positions.shape[0]
+    spare = rows // ranks + 2
+    width = ranks * spare
+    stride = -(-spare // 16) * 16
+    starts = [group * spare // 16 * 16 for group in range(ranks)]
+    window = max(
+        -(-(group + 1) * spare // 16) * 16 - starts[group] for group in range(ranks)
+    )
+    pair_width = 2 * key_matrix.shape[1]
+    chunk_width = pair_width // CHUNKS
+    query_width = queries.shape[1]
+    shape = jax.ShapeDtypeStruct
+
+    matrices = spread(jnp.concatenate([key_matrix, value_matrix], axis=1), ranks)
+
+    bucket, seat, sorted_route = pl.pallas_call(
+        functools.partial(order_kernel, ranks, slots, spare, stride),
+        out_shape=(
+            shape((1, rows), jnp.int32),
+            shape((1, rows), jnp.int32),
+            shape((1, width), jnp.int32),
+        ),
+        in_specs=[VMEM],
+        out_specs=(VMEM, VMEM, VMEM),
+        compiler_params=grant(16),
+        name="order",
+    )(route.reshape(1, rows))
+    plan = lax.all_gather(
+        jnp.concatenate([sorted_route.reshape(width), positions]), "dp", axis=0, tiled=False
+    )
+    all_positions = plan[:, width:].reshape(-1, HEAD_SIZE)
+    owners = source_order(ranks)
+    key_routes = plan[:, :width][owners]
+    key_routes = jnp.stack(
+        [key_routes[:, at : at + window].reshape(1, ranks * window) for at in starts]
+    )
+
+    half = HEAD_SIZE // 2
+    frequency = 1000000.0 ** (-(jnp.arange(half, dtype=jnp.float32) * 2.0 / HEAD_SIZE))
+    turned, bounds, cosine, sine = pl.pallas_call(
+        query_kernel,
+        out_shape=(
+            shape((ranks * stride, query_width), jnp.bfloat16),
+            shape((ranks * stride, HEAD_SIZE), jnp.int32),
+            shape((rows, HEAD_SIZE), jnp.float32),
+            shape((rows, HEAD_SIZE), jnp.float32),
+        ),
+        in_specs=[VMEM] * 5,
+        out_specs=(VMEM,) * 4,
+        compiler_params=grant(32),
+        name="turn_queries",
+    )(
+        route.reshape(rows, 1),
+        seat,
+        all_positions,
+        jnp.concatenate([frequency, frequency]).reshape(1, HEAD_SIZE),
+        queries,
+    )
+
+    bias = jnp.concatenate([key_projection_bias, value_projection_bias])
+    pairs = pl.pallas_call(
+        project_kernel,
+        out_shape=(shape((width, chunk_width), jnp.bfloat16),) * CHUNKS,
+        in_specs=[SMEM] + [VMEM] * 5 + [ANY] * ranks,
+        out_specs=(VMEM,) * CHUNKS,
+        scratch_shapes=[
+            pltpu.VMEM((hidden.shape[1], pair_width), jnp.bfloat16),
+            pltpu.SemaphoreType.DMA((ranks,)),
+        ],
+        compiler_params=grant(44),
+        name="project",
+    )(
+        owners,
+        hidden,
+        bias.astype(jnp.float32).reshape(1, pair_width),
+        cosine,
+        sine,
+        bucket,
+        *matrices,
+    )
+
+    outs = []
+    for chunk in range(CHUNKS):
+        columns = query_width // CHUNKS
+        blocks = spread(pairs[chunk], ranks)
+        outs.append(
+            pl.pallas_call(
+                functools.partial(attend_kernel, chunk, spare, window, stride),
+                grid=(1,),
+                out_shape=shape((rows, columns), jnp.bfloat16),
+                in_specs=[pl.BlockSpec((ranks * stride, columns), lambda i, c=chunk: (0, c))]
+                + [VMEM] * (3 + ranks),
+                out_specs=VMEM,
+                scratch_shapes=[pltpu.VMEM((ranks * stride, columns), jnp.bfloat16)],
+                compiler_params=grant(40),
+                name="attend",
+            )(turned, bounds, key_routes, seat, *blocks)
+        )
+    return jnp.concatenate(outs, axis=1)
 
 
 def apply_rotary(rows, slot_offset, heads):
@@ -73,7 +388,7 @@
     return jnp.concatenate([key_rows, value_rows], axis=1)
 
 
-def local(
+def send_plan(
     hidden,
     queries,
     route,
@@ -139,6 +454,16 @@
     return returned[bucket]
 
 
+def local(*args):
+    hidden, queries, _, positions, key_matrix = args[:5]
+    ranks = lax.axis_size("dp")
+    rows = hidden.shape[0]
+    gathered = ranks * ranks * (rows // ranks + 2) * 4 * key_matrix.shape[1]
+    if ranks % PLANE == 0 and rows % ranks == 0 and gathered <= GATHER_LIMIT:
+        return gather_plan(*args)
+    return send_plan(*args)
+
+
 def solution(mesh):
     placed = (
         P(("groups", "dp"), None),

time: 438 us -> 345 us (0.79)
  the two profiles are of different devices: /device:TPU:13 before, /device:TPU:1 now
where the time goes in v1:
time: 345 us; the launch traced here: 344 us
  waiting for transfers between devices  165 us (48%)
  starting transfers between devices  69.5 us (20%)
  Pallas kernels  67.1 us (19%)
  local copies, waits for them, and re-layouts  25.4 us (7%)
  between operations  14.5 us (4%)
    ppermute x9, waiting for transfers between devices, spread(): lanes.append(lax.ppermute(lanes[-1], 'dp', ring))  64.4 us
    unnamed x2, waiting for transfers between devices  59.3 us
    ppermute x24, starting transfers between devices, spread(): return held + [lax.ppermute(one, 'dp', beside) for one in held]  48.8 us
    ppermute x12, waiting for transfers between devices, spread(): others = [lax.ppermute(lane, 'dp', across) for lane in lanes]  40.8 us
    pallas_call x2, Pallas kernels, gather_plan(): pl.pallas_call(functools.partial(attend_kernel, chunk, spare, window, str...  40 us
    pallas_call x1, Pallas kernels, gather_plan(): pl.pallas_call(project_kernel, out_shape=(shape((width, chunk_width), jnp...  20.4 us
    unnamed x68, local copies, waits for them, and re-layouts  19.8 us
    ppermute x9, starting transfers between devices, spread(): lanes.append(lax.ppermute(lanes[-1], 'dp', ring))  10.9 us
  transfers between devices with their start and end apart: 46, of which 16 were waited for; matrix products, arithmetic and copies ran while one was open for 2% of the time, Pallas kernels for 8%

profile of v1, /device:TPU:1, one launch (start us, length us, event | category | flops | bytes accessed | tf_op | source)
XLA Modules:
  0.0 343.9 jit_solution(5834491667281278319)
XLA Ops:
  8.6 2.2 collective-permute-start
  10.7 16.5 %collective-permute-done.refs_1_ = bf16[320,1024]{1,0:T(8,128)(2,1)S(1)} collective-permute-done((bf16[320,1024]{1,0:T(8,128)(2,1)S(1)}, bf16[320,1024]{1,0:T(8,128)(2,1)S(1)}, u32[]{:S(2)}, u32[]{:S(2)}) %collective-permute-start) | collective-permute-done | bytes 655392 | tf_op jit(solution)/shard_map/ppermute | solution.py:202
  28.2 1.8 collective-permute-start.7
  30.0 14.0 %collective-permute-done.1.refs_2_ = bf16[320,1024]{1,0:T(8,128)(2,1)S(1)} collective-permute-done((bf16[320,1024]{1,0:T(8,128)(2,1)S(1)}, bf16[320,1024]{1,0:T(8,128)(2,1)S(1)}, u32[]{:S(2)}, u32[]{:S(2)}) %collective-permute-start.1) | collective-permute-done | bytes 655392 | tf_op jit(solution)/shard_map/ppermute | solution.py:202
  44.0 2.2 collective-permute-start.11
  48.8 11.2 %collective-permute-done.2.refs_3_ = bf16[320,1024]{1,0:T(8,128)(2,1)} collective-permute-done((bf16[320,1024]{1,0:T(8,128)(2,1)S(1)}, bf16[320,1024]{1,0:T(8,128)(2,1)}, u32[]{:S(2)}, u32[]{:S(2)}) %collective-permute-start.2) | collective-permute-done | bytes 655392 | tf_op jit(solution)/shard_map/ppermute | solution.py:202
  61.7 1.3 dynamic-slice
  66.5 3.6 %collective-permute-start.9 = (bf16[320,1024]{1,0:T(8,128)(2,1)S(1)}, bf16[320,1024]{1,0:T(8,128)(2,1)}, u32[]{:S(2)}, u32[]{:S(2)}) collective-permute-start(bf16[320,1024]{1,0:T(8,128)(2,1)S(1)} %collective-permute-done.1.refs_2_), channel_id=1, source_target_pairs={{0,1},{1,0},{2,3},{3,2},{4,5},{5,4},{6,7},{7,6},{8,9},{9,8},{10,11... | collective-permute-start | bytes 1966088 | tf_op jit(solution)/shard_map/ppermute | solution.py:205
  70.6 6.2 %collective-permute-done.5.refs_6_ = bf16[320,1024]{1,0:T(8,128)(2,1)} collective-permute-done((bf16[320,1024]{1,0:T(8,128)(2,1)S(1)}, bf16[320,1024]{1,0:T(8,128)(2,1)}, u32[]{:S(2)}, u32[]{:S(2)}) %collective-permute-start.5) | collective-permute-done | bytes 655392 | tf_op jit(solution)/shard_map/ppermute | solution.py:203
  76.8 1.4 collective-permute-start.13
  78.2 12.9 %collective-permute-done.6.refs_7_ = bf16[320,1024]{1,0:T(8,128)(2,1)} collective-permute-done((bf16[320,1024]{1,0:T(8,128)(2,1)}, bf16[320,1024]{1,0:T(8,128)(2,1)}, u32[]{:S(2)}, u32[]{:S(2)}) %collective-permute-start.6) | collective-permute-done | bytes 655392 | tf_op jit(solution)/shard_map/ppermute | solution.py:203
  92.4 59.3 %all-reduce.3.cloned.1.call-done = s32[25088]{0:T(1024)} async-done(((s32[25088]{0:T(1024)}), s32[25088]{0:T(1024)}) %all-reduce.3.cloned.1.call-update) | async-done | bytes 100368
  152.8 1.7 copy-done.2
  154.6 6.3 %turn_queries.1 = (bf16[768,2560]{1,0:T(8,128)(2,1)S(1)}, s32[768,128]{1,0:T(8,128)S(1)}, f32[512,128]{1,0:T(8,128)S(1)}, f32[512,128]{1,0:T(8,128)S(1)}) custom-call(s32[512,1]{1,0:T(8,128)S(1)} %copy.9.route_ref, s32[1,512]{1,0:T(1,128)S(1)} %get-tuple-element.14.seat_ref, s32[128,128]{1,0:T(8,128)S(1)} %reshape.145.positions_ref, ...), custom_call_target="tpu_custom_call" | custom-call | tf_op jit(solution)/shard_map/turn_queries/pallas_call | solution.py:267
  160.8 1.9 copy-done
  162.8 20.4 %project.1 = (bf16[544,512]{1,0:T(8,128)(2,1)S(1)}, bf16[544,512]{1,0:T(8,128)(2,1)S(1)}) custom-call(s32[16]{0:T(128)S(1)} %pad_add_fusion.owners_ref, bf16[512,5120]{1,0:T(8,128)(2,1)} %hidden_ref.1, f32[1,1024]{1,0:T(1,128)S(1)} %maximum_convert_fusion.bias_ref, f32[512,128]{1,0:T(8,128)S(1)} %get-tuple-element.18.cosine_ref, ...), custom_call_target="tpu_custom_call" | custom-call | tf_op jit(solution)/shard_map/project/pallas_call | solution.py:288
  184.2 3.3 collective-permute-start.15
  190.1 7.0 %collective-permute-done.18.refs_4_ = bf16[544,512]{1,0:T(8,128)(2,1)S(1)} collective-permute-done((bf16[544,512]{1,0:T(8,128)(2,1)S(1)}, bf16[544,512]{1,0:T(8,128)(2,1)S(1)}, u32[]{:S(2)}, u32[]{:S(2)}) %collective-permute-start.18) | collective-permute-done | bytes 557088 | tf_op jit(solution)/shard_map/ppermute | solution.py:203
  197.1 2.1 collective-permute-start.26
  199.2 1.8 collective-permute-done.15.refs_1_
  201.1 1.3 collective-permute-start.23
  202.7 6.3 %collective-permute-done.33.refs_4_ = bf16[544,512]{1,0:T(8,128)(2,1)S(1)} collective-permute-done((bf16[544,512]{1,0:T(8,128)(2,1)S(1)}, bf16[544,512]{1,0:T(8,128)(2,1)S(1)}, u32[]{:S(2)}, u32[]{:S(2)}) %collective-permute-start.33) | collective-permute-done | bytes 557088 | tf_op jit(solution)/shard_map/ppermute | solution.py:203
  209.0 3.4 %collective-permute-start.16 = (bf16[544,512]{1,0:T(8,128)(2,1)S(1)}, bf16[544,512]{1,0:T(8,128)(2,1)}, u32[]{:S(2)}, u32[]{:S(2)}) collective-permute-start(bf16[544,512]{1,0:T(8,128)(2,1)S(1)} %collective-permute-done.15.refs_1_), channel_id=1, source_target_pairs={{0,4},{1,5},{2,6},{3,7},{4,8},{5,9},{6,10},{7,11},{8,12},{9,13},{1... | collective-permute-start | bytes 1671176 | tf_op jit(solution)/shard_map/ppermute | solution.py:202
  213.3 1.6 collective-permute-start.38
  215.8 1.2 collective-permute-start.34
  217.8 3.3 collective-permute-done.19.refs_5_
  221.1 2.0 collective-permute-start.41
  223.1 1.7 collective-permute-done.16.refs_2_
  227.9 4.1 %collective-permute-start.24 = (bf16[544,512]{1,0:T(8,128)(2,1)}, bf16[544,512]{1,0:T(8,128)(2,1)S(1)}, u32[]{:S(2)}, u32[]{:S(2)}) collective-permute-start(bf16[544,512]{1,0:T(8,128)(2,1)} %collective-permute-done.16.refs_2_), channel_id=1, source_target_pairs={{0,1},{1,0},{2,3},{3,2},{4,5},{5,4},{6,7},{7,6},{8,9},{9,8},{10,11... | collective-permute-start | bytes 1671176 | tf_op jit(solution)/shard_map/ppermute | solution.py:205
  231.9 1.2 collective-permute-start.20
  233.2 1.1 collective-permute-start.27
  234.3 2.5 collective-permute-done.31.refs_2_
  237.8 10.9 %collective-permute-done.17.refs_3_ = bf16[544,512]{1,0:T(8,128)(2,1)} collective-permute-done((bf16[544,512]{1,0:T(8,128)(2,1)}, bf16[544,512]{1,0:T(8,128)(2,1)}, u32[]{:S(2)}, u32[]{:S(2)}) %collective-permute-start.17) | collective-permute-done | bytes 557088 | tf_op jit(solution)/shard_map/ppermute | solution.py:202
  248.7 1.4 collective-permute-start.21
  250.3 4.4 %collective-permute-start.25 = (bf16[544,512]{1,0:T(8,128)(2,1)}, bf16[544,512]{1,0:T(8,128)(2,1)S(1)}, u32[]{:S(2)}, u32[]{:S(2)}) collective-permute-start(bf16[544,512]{1,0:T(8,128)(2,1)} %collective-permute-done.17.refs_3_), channel_id=1, source_target_pairs={{0,1},{1,0},{2,3},{3,2},{4,5},{5,4},{6,7},{7,6},{8,9},{9,8},{10,11... | collective-permute-start | bytes 1671176 | tf_op jit(solution)/shard_map/ppermute | solution.py:205
  254.7 5.8 %collective-permute-done.32.refs_3_ = bf16[544,512]{1,0:T(8,128)(2,1)S(1)} collective-permute-done((bf16[544,512]{1,0:T(8,128)(2,1)}, bf16[544,512]{1,0:T(8,128)(2,1)S(1)}, u32[]{:S(2)}, u32[]{:S(2)}) %collective-permute-start.32) | collective-permute-done | bytes 557088 | tf_op jit(solution)/shard_map/ppermute | solution.py:202
  260.5 1.4 collective-permute-start.36
  261.9 6.4 %collective-permute-start.29 = (bf16[544,512]{1,0:T(8,128)(2,1)S(1)}, bf16[544,512]{1,0:T(8,128)(2,1)S(1)}, u32[]{:S(2)}, u32[]{:S(2)}) collective-permute-start(bf16[544,512]{1,0:T(8,128)(2,1)S(1)} %collective-permute-done.21.refs_7_), channel_id=1, source_target_pairs={{0,1},{1,0},{2,3},{3,2},{4,5},{5,4},{6,7},{7,6},{8,9},{9,8},{10,11... | collective-permute-start | bytes 1671176 | tf_op jit(solution)/shard_map/ppermute | solution.py:205
  268.3 2.8 collective-permute-done.35.refs_6_
  271.1 9.1 %collective-permute-start.39 = (bf16[544,512]{1,0:T(8,128)(2,1)}, bf16[544,512]{1,0:T(8,128)(2,1)S(1)}, u32[]{:S(2)}, u32[]{:S(2)}) collective-permute-start(bf16[544,512]{1,0:T(8,128)(2,1)} %collective-permute-done.31.refs_2_), channel_id=1, source_target_pairs={{0,1},{1,0},{2,3},{3,2},{4,5},{5,4},{6,7},{7,6},{8,9},{9,8},{10,11... | collective-permute-start | bytes 1671176 | tf_op jit(solution)/shard_map/ppermute | solution.py:205
  280.7 2.3 collective-permute-done.36.refs_7_
  283.1 4.7 %collective-permute-start.43 = (bf16[544,512]{1,0:T(8,128)(2,1)S(1)}, bf16[544,512]{1,0:T(8,128)(2,1)S(1)}, u32[]{:S(2)}, u32[]{:S(2)}) collective-permute-start(bf16[544,512]{1,0:T(8,128)(2,1)S(1)} %collective-permute-done.35.refs_6_), channel_id=1, source_target_pairs={{0,1},{1,0},{2,3},{3,2},{4,5},{5,4},{6,7},{7,6},{8,9},{9,8},{10,11... | collective-permute-start | bytes 1671176 | tf_op jit(solution)/shard_map/ppermute | solution.py:205
  287.9 2.1 copy-done.1
  290.0 1.1 copy-done.8
  291.1 1.1 copy-done.10
  295.3 19.8 %attend.2 = bf16[512,1280]{1,0:T(8,128)(2,1)S(1)} custom-call(bf16[768,2560]{1,0:T(8,128)(2,1)S(1)} %copy-done.1, s32[768,128]{1,0:T(8,128)S(1)} %get-tuple-element.17.bounds_ref, s32[16,1,768]{2,1,0:T(1,128)S(1)} %constant_dynamic-update-slice_fusion.routes_ref, s32[1,512]{1,0:T(1,128)S(1)} %get-tuple-element.14.seat_ref, bf16[544,512]{1,0:T(8,128)(2,1)S(1)} %copy-done.8, ...), custom_call_target="tpu_custom_call" | custom-call | tf_op jit(solution)/shard_map/attend/pallas_call | solution.py:314
  315.1 20.2 %attend.3 = bf16[512,1280]{1,0:T(8,128)(2,1)S(1)} custom-call(bf16[768,2560]{1,0:T(8,128)(2,1)S(1)} %copy-done.1, s32[768,128]{1,0:T(8,128)S(1)} %get-tuple-element.17.bounds_ref, s32[16,1,768]{2,1,0:T(1,128)S(1)} %constant_dynamic-update-slice_fusion.routes_ref, s32[1,512]{1,0:T(1,128)S(1)} %get-tuple-element.14.seat_ref, bf16[544,512]{1,0:T(8,128)(2,1)S(1)} %copy-done.6, ...), custom_call_target="tpu_custom_call" | custom-call | tf_op jit(solution)/shard_map/attend/pallas_call | solution.py:314
  335.3 1.7 pad_maximum_fusion
  (156 shorter events, 27.7 us)
Async XLA Ops:
  6.5 145.1 %all-reduce.3.cloned.1.call-start = ((), (), s32[]{:S(2)}) async-start(), calls=%async_computation | async-start | bytes 204800
  8.6 18.7 %collective-permute-start = (bf16[320,1024]{1,0:T(8,128)(2,1)S(1)}, bf16[320,1024]{1,0:T(8,128)(2,1)S(1)}, u32[]{:S(2)}, u32[]{:S(2)}) collective-permute-start(bf16[320,1024]{1,0:T(8,128)(2,1)S(1)} %constant_dynamic-update-slice_fusion.16.refs_0_), channel_id=1, source_target_pairs={{0,4},{1,5},{2,6},{3,7},{4,8},{5,9},{6,10},{7,11},{8,12},{9,13},{1... | collective-permute-start | bytes 1966088 | tf_op jit(solution)/shard_map/ppermute | solution.py:202
  27.2 16.8 %collective-permute-start.1 = (bf16[320,1024]{1,0:T(8,128)(2,1)S(1)}, bf16[320,1024]{1,0:T(8,128)(2,1)S(1)}, u32[]{:S(2)}, u32[]{:S(2)}) collective-permute-start(bf16[320,1024]{1,0:T(8,128)(2,1)S(1)} %collective-permute-done.refs_1_), channel_id=1, source_target_pairs={{0,4},{1,5},{2,6},{3,7},{4,8},{5,9},{6,10},{7,11},{8,12},{9,13},{1... | collective-permute-start | bytes 1966088 | tf_op jit(solution)/shard_map/ppermute | solution.py:202
  27.2 16.8 %collective-permute-start.3 = (bf16[320,1024]{1,0:T(8,128)(2,1)S(1)}, bf16[320,1024]{1,0:T(8,128)(2,1)S(1)}, u32[]{:S(2)}, u32[]{:S(2)}) collective-permute-start(bf16[320,1024]{1,0:T(8,128)(2,1)S(1)} %constant_dynamic-update-slice_fusion.16.refs_0_), channel_id=1, source_target_pairs={{0,2},{1,3},{2,0},{3,1},{4,6},{5,7},{6,4},{7,5},{8,10},{9,11},{10,... | collective-permute-start | bytes 1966088 | tf_op jit(solution)/shard_map/ppermute | solution.py:203
  28.2 19.3 %collective-permute-start.7 = (bf16[320,1024]{1,0:T(8,128)(2,1)S(1)}, bf16[320,1024]{1,0:T(8,128)(2,1)S(1)}, u32[]{:S(2)}, u32[]{:S(2)}) collective-permute-start(bf16[320,1024]{1,0:T(8,128)(2,1)S(1)} %constant_dynamic-update-slice_fusion.16.refs_0_), channel_id=1, source_target_pairs={{0,1},{1,0},{2,3},{3,2},{4,5},{5,4},{6,7},{7,6},{8,9},{9,8},{10,11... | collective-permute-start | bytes 1966088 | tf_op jit(solution)/shard_map/ppermute | solution.py:205
  44.0 16.0 %collective-permute-start.2 = (bf16[320,1024]{1,0:T(8,128)(2,1)S(1)}, bf16[320,1024]{1,0:T(8,128)(2,1)}, u32[]{:S(2)}, u32[]{:S(2)}) collective-permute-start(bf16[320,1024]{1,0:T(8,128)(2,1)S(1)} %collective-permute-done.1.refs_2_), channel_id=1, source_target_pairs={{0,4},{1,5},{2,6},{3,7},{4,8},{5,9},{6,10},{7,11},{8,12},{9,13},{1... | collective-permute-start | bytes 1966088 | tf_op jit(solution)/shard_map/ppermute | solution.py:202
  44.0 22.5 %collective-permute-start.11 = (bf16[320,1024]{1,0:T(8,128)(2,1)S(1)}, bf16[320,1024]{1,0:T(8,128)(2,1)}, u32[]{:S(2)}, u32[]{:S(2)}) collective-permute-start(bf16[320,1024]{1,0:T(8,128)(2,1)S(1)} %collective-permute-done.3.refs_4_), channel_id=1, source_target_pairs={{0,1},{1,0},{2,3},{3,2},{4,5},{5,4},{6,7},{7,6},{8,9},{9,8},{10,11... | collective-permute-start | bytes 1966088 | tf_op jit(solution)/shard_map/ppermute | solution.py:205
  46.2 23.9 %collective-permute-start.4 = (bf16[320,1024]{1,0:T(8,128)(2,1)S(1)}, bf16[320,1024]{1,0:T(8,128)(2,1)}, u32[]{:S(2)}, u32[]{:S(2)}) collective-permute-start(bf16[320,1024]{1,0:T(8,128)(2,1)S(1)} %collective-permute-done.refs_1_), channel_id=1, source_target_pairs={{0,2},{1,3},{2,0},{3,1},{4,6},{5,7},{6,4},{7,5},{8,10},{9,11},{10,... | collective-permute-start | bytes 1966088 | tf_op jit(solution)/shard_map/ppermute | solution.py:203
  47.2 23.0 %collective-permute-start.8 = (bf16[320,1024]{1,0:T(8,128)(2,1)S(1)}, bf16[320,1024]{1,0:T(8,128)(2,1)}, u32[]{:S(2)}, u32[]{:S(2)}) collective-permute-start(bf16[320,1024]{1,0:T(8,128)(2,1)S(1)} %collective-permute-done.refs_1_), channel_id=1, source_target_pairs={{0,1},{1,0},{2,3},{3,2},{4,5},{5,4},{6,7},{7,6},{8,9},{9,8},{10,11... | collective-permute-start | bytes 1966088 | tf_op jit(solution)/shard_map/ppermute | solution.py:205
  48.4 28.4 %collective-permute-start.5 = (bf16[320,1024]{1,0:T(8,128)(2,1)S(1)}, bf16[320,1024]{1,0:T(8,128)(2,1)}, u32[]{:S(2)}, u32[]{:S(2)}) collective-permute-start(bf16[320,1024]{1,0:T(8,128)(2,1)S(1)} %collective-permute-done.1.refs_2_), channel_id=1, source_target_pairs={{0,2},{1,3},{2,0},{3,1},{4,6},{5,7},{6,4},{7,5},{8,10},{9,11},{10,... | collective-permute-start | bytes 1966088 | tf_op jit(solution)/shard_map/ppermute | solution.py:203
  60.0 31.1 %collective-permute-start.6 = (bf16[320,1024]{1,0:T(8,128)(2,1)}, bf16[320,1024]{1,0:T(8,128)(2,1)}, u32[]{:S(2)}, u32[]{:S(2)}) collective-permute-start(bf16[320,1024]{1,0:T(8,128)(2,1)} %collective-permute-done.2.refs_3_), channel_id=1, source_target_pairs={{0,2},{1,3},{2,0},{3,1},{4,6},{5,7},{6,4},{7,5},{8,10},{9,11},{10,... | collective-permute-start | bytes 1966088 | tf_op jit(solution)/shard_map/ppermute | solution.py:203
  66.5 96.2 %collective-permute-start.9 = (bf16[320,1024]{1,0:T(8,128)(2,1)S(1)}, bf16[320,1024]{1,0:T(8,128)(2,1)}, u32[]{:S(2)}, u32[]{:S(2)}) collective-permute-start(bf16[320,1024]{1,0:T(8,128)(2,1)S(1)} %collective-permute-done.1.refs_2_), channel_id=1, source_target_pairs={{0,1},{1,0},{2,3},{3,2},{4,5},{5,4},{6,7},{7,6},{8,9},{9,8},{10,11... | collective-permute-start | bytes 1966088 | tf_op jit(solution)/shard_map/ppermute | solution.py:205
  70.1 92.6 %collective-permute-start.12 = (bf16[320,1024]{1,0:T(8,128)(2,1)}, bf16[320,1024]{1,0:T(8,128)(2,1)}, u32[]{:S(2)}, u32[]{:S(2)}) collective-permute-start(bf16[320,1024]{1,0:T(8,128)(2,1)} %collective-permute-done.4.refs_5_), channel_id=1, source_target_pairs={{0,1},{1,0},{2,3},{3,2},{4,5},{5,4},{6,7},{7,6},{8,9},{9,8},{10,11... | collective-permute-start | bytes 1966088 | tf_op jit(solution)/shard_map/ppermute | solution.py:205
  70.2 92.6 %collective-permute-start.10 = (bf16[320,1024]{1,0:T(8,128)(2,1)}, bf16[320,1024]{1,0:T(8,128)(2,1)}, u32[]{:S(2)}, u32[]{:S(2)}) collective-permute-start(bf16[320,1024]{1,0:T(8,128)(2,1)} %collective-permute-done.2.refs_3_), channel_id=1, source_target_pairs={{0,1},{1,0},{2,3},{3,2},{4,5},{5,4},{6,7},{7,6},{8,9},{9,8},{10,11... | collective-permute-start | bytes 1966088 | tf_op jit(solution)/shard_map/ppermute | solution.py:205
  76.8 85.9 %collective-permute-start.13 = (bf16[320,1024]{1,0:T(8,128)(2,1)}, bf16[320,1024]{1,0:T(8,128)(2,1)}, u32[]{:S(2)}, u32[]{:S(2)}) collective-permute-start(bf16[320,1024]{1,0:T(8,128)(2,1)} %collective-permute-done.5.refs_6_), channel_id=1, source_target_pairs={{0,1},{1,0},{2,3},{3,2},{4,5},{5,4},{6,7},{7,6},{8,9},{9,8},{10,11... | collective-permute-start | bytes 1966088 | tf_op jit(solution)/shard_map/ppermute | solution.py:205
  91.1 71.6 %collective-permute-start.14 = (bf16[320,1024]{1,0:T(8,128)(2,1)}, bf16[320,1024]{1,0:T(8,128)(2,1)}, u32[]{:S(2)}, u32[]{:S(2)}) collective-permute-start(bf16[320,1024]{1,0:T(8,128)(2,1)} %collective-permute-done.6.refs_7_), channel_id=1, source_target_pairs={{0,1},{1,0},{2,3},{3,2},{4,5},{5,4},{6,7},{7,6},{8,9},{9,8},{10,11... | collective-permute-start | bytes 1966088 | tf_op jit(solution)/shard_map/ppermute | solution.py:205
  162.8 62.9 %copy-start.20 = (s32[4]{0:T(128)S(1)}, s32[4]{0:T(128)}, u32[]{:S(2)}) copy-start(s32[4]{0:T(128)} %copy-done.19) | copy-start | bytes 52
  162.8 62.9 %copy-start.22 = (s32[4]{0:T(128)S(1)}, s32[4]{0:T(128)}, u32[]{:S(2)}) copy-start(s32[4]{0:T(128)} %copy-done.21) | copy-start | bytes 52
  183.2 6.1 %collective-permute-start.22 = (bf16[544,512]{1,0:T(8,128)(2,1)S(1)}, bf16[544,512]{1,0:T(8,128)(2,1)S(1)}, u32[]{:S(2)}, u32[]{:S(2)}) collective-permute-start(bf16[544,512]{1,0:T(8,128)(2,1)S(1)} %get-tuple-element.21.refs_0_), channel_id=1, source_target_pairs={{0,1},{1,0},{2,3},{3,2},{4,5},{5,4},{6,7},{7,6},{8,9},{9,8},{10,11... | collective-permute-start | bytes 1671176 | tf_op jit(solution)/shard_map/ppermute | solution.py:205
  183.3 13.8 %collective-permute-start.18 = (bf16[544,512]{1,0:T(8,128)(2,1)S(1)}, bf16[544,512]{1,0:T(8,128)(2,1)S(1)}, u32[]{:S(2)}, u32[]{:S(2)}) collective-permute-start(bf16[544,512]{1,0:T(8,128)(2,1)S(1)} %get-tuple-element.21.refs_0_), channel_id=1, source_target_pairs={{0,2},{1,3},{2,0},{3,1},{4,6},{5,7},{6,4},{7,5},{8,10},{9,11},{10,... | collective-permute-start | bytes 1671176 | tf_op jit(solution)/shard_map/ppermute | solution.py:203
  184.2 16.8 %collective-permute-start.15 = (bf16[544,512]{1,0:T(8,128)(2,1)S(1)}, bf16[544,512]{1,0:T(8,128)(2,1)S(1)}, u32[]{:S(2)}, u32[]{:S(2)}) collective-permute-start(bf16[544,512]{1,0:T(8,128)(2,1)S(1)} %get-tuple-element.21.refs_0_), channel_id=1, source_target_pairs={{0,4},{1,5},{2,6},{3,7},{4,8},{5,9},{6,10},{7,11},{8,12},{9,13},{1... | collective-permute-start | bytes 1671176 | tf_op jit(solution)/shard_map/ppermute | solution.py:202
  188.4 13.9 %collective-permute-start.37 = (bf16[544,512]{1,0:T(8,128)(2,1)S(1)}, bf16[544,512]{1,0:T(8,128)(2,1)S(1)}, u32[]{:S(2)}, u32[]{:S(2)}) collective-permute-start(bf16[544,512]{1,0:T(8,128)(2,1)S(1)} %get-tuple-element.22.refs_0_), channel_id=1, source_target_pairs={{0,1},{1,0},{2,3},{3,2},{4,5},{5,4},{6,7},{7,6},{8,9},{9,8},{10,11... | collective-permute-start | bytes 1671176 | tf_op jit(solution)/shard_map/ppermute | solution.py:205
  189.0 20.0 %collective-permute-start.33 = (bf16[544,512]{1,0:T(8,128)(2,1)S(1)}, bf16[544,512]{1,0:T(8,128)(2,1)S(1)}, u32[]{:S(2)}, u32[]{:S(2)}) collective-permute-start(bf16[544,512]{1,0:T(8,128)(2,1)S(1)} %get-tuple-element.22.refs_0_), channel_id=1, source_target_pairs={{0,2},{1,3},{2,0},{3,1},{4,6},{5,7},{6,4},{7,5},{8,10},{9,11},{10,... | collective-permute-start | bytes 1671176 | tf_op jit(solution)/shard_map/ppermute | solution.py:203
  189.3 24.0 %collective-permute-start.30 = (bf16[544,512]{1,0:T(8,128)(2,1)S(1)}, bf16[544,512]{1,0:T(8,128)(2,1)S(1)}, u32[]{:S(2)}, u32[]{:S(2)}) collective-permute-start(bf16[544,512]{1,0:T(8,128)(2,1)S(1)} %get-tuple-element.22.refs_0_), channel_id=1, source_target_pairs={{0,4},{1,5},{2,6},{3,7},{4,8},{5,9},{6,10},{7,11},{8,12},{9,13},{1... | collective-permute-start | bytes 1671176 | tf_op jit(solution)/shard_map/ppermute | solution.py:202
  197.1 17.8 %collective-permute-start.26 = (bf16[544,512]{1,0:T(8,128)(2,1)S(1)}, bf16[544,512]{1,0:T(8,128)(2,1)S(1)}, u32[]{:S(2)}, u32[]{:S(2)}) collective-permute-start(bf16[544,512]{1,0:T(8,128)(2,1)S(1)} %collective-permute-done.18.refs_4_), channel_id=1, source_target_pairs={{0,1},{1,0},{2,3},{3,2},{4,5},{5,4},{6,7},{7,6},{8,9},{9,8},{10,11... | collective-permute-start | bytes 1671176 | tf_op jit(solution)/shard_map/ppermute | solution.py:205
  201.1 15.9 %collective-permute-start.23 = (bf16[544,512]{1,0:T(8,128)(2,1)S(1)}, bf16[544,512]{1,0:T(8,128)(2,1)S(1)}, u32[]{:S(2)}, u32[]{:S(2)}) collective-permute-start(bf16[544,512]{1,0:T(8,128)(2,1)S(1)} %collective-permute-done.15.refs_1_), channel_id=1, source_target_pairs={{0,1},{1,0},{2,3},{3,2},{4,5},{5,4},{6,7},{7,6},{8,9},{9,8},{10,11... | collective-permute-start | bytes 1671176 | tf_op jit(solution)/shard_map/ppermute | solution.py:205
  202.4 18.7 %collective-permute-start.19 = (bf16[544,512]{1,0:T(8,128)(2,1)S(1)}, bf16[544,512]{1,0:T(8,128)(2,1)S(1)}, u32[]{:S(2)}, u32[]{:S(2)}) collective-permute-start(bf16[544,512]{1,0:T(8,128)(2,1)S(1)} %collective-permute-done.15.refs_1_), channel_id=1, source_target_pairs={{0,2},{1,3},{2,0},{3,1},{4,6},{5,7},{6,4},{7,5},{8,10},{9,11},{10,... | collective-permute-start | bytes 1671176 | tf_op jit(solution)/shard_map/ppermute | solution.py:203
  209.0 15.8 %collective-permute-start.16 = (bf16[544,512]{1,0:T(8,128)(2,1)S(1)}, bf16[544,512]{1,0:T(8,128)(2,1)}, u32[]{:S(2)}, u32[]{:S(2)}) collective-permute-start(bf16[544,512]{1,0:T(8,128)(2,1)S(1)} %collective-permute-done.15.refs_1_), channel_id=1, source_target_pairs={{0,4},{1,5},{2,6},{3,7},{4,8},{5,9},{6,10},{7,11},{8,12},{9,13},{1... | collective-permute-start | bytes 1671176 | tf_op jit(solution)/shard_map/ppermute | solution.py:202
  213.3 18.6 %collective-permute-start.38 = (bf16[544,512]{1,0:T(8,128)(2,1)S(1)}, bf16[544,512]{1,0:T(8,128)(2,1)}, u32[]{:S(2)}, u32[]{:S(2)}) collective-permute-start(bf16[544,512]{1,0:T(8,128)(2,1)S(1)} %collective-permute-done.30.refs_1_), channel_id=1, source_target_pairs={{0,1},{1,0},{2,3},{3,2},{4,5},{5,4},{6,7},{7,6},{8,9},{9,8},{10,11... | collective-permute-start | bytes 1671176 | tf_op jit(solution)/shard_map/ppermute | solution.py:205
  215.8 17.4 %collective-permute-start.34 = (bf16[544,512]{1,0:T(8,128)(2,1)S(1)}, bf16[544,512]{1,0:T(8,128)(2,1)}, u32[]{:S(2)}, u32[]{:S(2)}) collective-permute-start(bf16[544,512]{1,0:T(8,128)(2,1)S(1)} %collective-permute-done.30.refs_1_), channel_id=1, source_target_pairs={{0,2},{1,3},{2,0},{3,1},{4,6},{5,7},{6,4},{7,5},{8,10},{9,11},{10,... | collective-permute-start | bytes 1671176 | tf_op jit(solution)/shard_map/ppermute | solution.py:203
  217.8 19.0 %collective-permute-start.31 = (bf16[544,512]{1,0:T(8,128)(2,1)S(1)}, bf16[544,512]{1,0:T(8,128)(2,1)}, u32[]{:S(2)}, u32[]{:S(2)}) collective-permute-start(bf16[544,512]{1,0:T(8,128)(2,1)S(1)} %collective-permute-done.30.refs_1_), channel_id=1, source_target_pairs={{0,4},{1,5},{2,6},{3,7},{4,8},{5,9},{6,10},{7,11},{8,12},{9,13},{1... | collective-permute-start | bytes 1671176 | tf_op jit(solution)/shard_map/ppermute | solution.py:202
  221.1 6.8 %collective-permute-start.41 = (bf16[544,512]{1,0:T(8,128)(2,1)S(1)}, bf16[544,512]{1,0:T(8,128)(2,1)}, u32[]{:S(2)}, u32[]{:S(2)}) collective-permute-start(bf16[544,512]{1,0:T(8,128)(2,1)S(1)} %collective-permute-done.33.refs_4_), channel_id=1, source_target_pairs={{0,1},{1,0},{2,3},{3,2},{4,5},{5,4},{6,7},{7,6},{8,9},{9,8},{10,11... | collective-permute-start | bytes 1671176 | tf_op jit(solution)/shard_map/ppermute | solution.py:205
  224.8 23.9 %collective-permute-start.17 = (bf16[544,512]{1,0:T(8,128)(2,1)}, bf16[544,512]{1,0:T(8,128)(2,1)}, u32[]{:S(2)}, u32[]{:S(2)}) collective-permute-start(bf16[544,512]{1,0:T(8,128)(2,1)} %collective-permute-done.16.refs_2_), channel_id=1, source_target_pairs={{0,4},{1,5},{2,6},{3,7},{4,8},{5,9},{6,10},{7,11},{8,12},{9,13},{1... | collective-permute-start | bytes 1671176 | tf_op jit(solution)/shard_map/ppermute | solution.py:202
  227.9 22.4 %collective-permute-start.24 = (bf16[544,512]{1,0:T(8,128)(2,1)}, bf16[544,512]{1,0:T(8,128)(2,1)S(1)}, u32[]{:S(2)}, u32[]{:S(2)}) collective-permute-start(bf16[544,512]{1,0:T(8,128)(2,1)} %collective-permute-done.16.refs_2_), channel_id=1, source_target_pairs={{0,1},{1,0},{2,3},{3,2},{4,5},{5,4},{6,7},{7,6},{8,9},{9,8},{10,11... | collective-permute-start | bytes 1671176 | tf_op jit(solution)/shard_map/ppermute | solution.py:205
  231.9 22.7 %collective-permute-start.20 = (bf16[544,512]{1,0:T(8,128)(2,1)}, bf16[544,512]{1,0:T(8,128)(2,1)S(1)}, u32[]{:S(2)}, u32[]{:S(2)}) collective-permute-start(bf16[544,512]{1,0:T(8,128)(2,1)} %collective-permute-done.16.refs_2_), channel_id=1, source_target_pairs={{0,2},{1,3},{2,0},{3,1},{4,6},{5,7},{6,4},{7,5},{8,10},{9,11},{10,... | collective-permute-start | bytes 1671176 | tf_op jit(solution)/shard_map/ppermute | solution.py:203
  233.2 16.9 %collective-permute-start.27 = (bf16[544,512]{1,0:T(8,128)(2,1)}, bf16[544,512]{1,0:T(8,128)(2,1)S(1)}, u32[]{:S(2)}, u32[]{:S(2)}) collective-permute-start(bf16[544,512]{1,0:T(8,128)(2,1)} %copy-done.15), channel_id=1, source_target_pairs={{0,1},{1,0},{2,3},{3,2},{4,5},{5,4},{6,7},{7,6},{8,9},{9,8},{10,11... | collective-permute-start | bytes 1671176 | tf_op jit(solution)/shard_map/ppermute | solution.py:205
  236.8 23.8 %collective-permute-start.32 = (bf16[544,512]{1,0:T(8,128)(2,1)}, bf16[544,512]{1,0:T(8,128)(2,1)S(1)}, u32[]{:S(2)}, u32[]{:S(2)}) collective-permute-start(bf16[544,512]{1,0:T(8,128)(2,1)} %collective-permute-done.31.refs_2_), channel_id=1, source_target_pairs={{0,4},{1,5},{2,6},{3,7},{4,8},{5,9},{6,10},{7,11},{8,12},{9,13},{1... | collective-permute-start | bytes 1671176 | tf_op jit(solution)/shard_map/ppermute | solution.py:202
  248.7 13.2 %collective-permute-start.21 = (bf16[544,512]{1,0:T(8,128)(2,1)}, bf16[544,512]{1,0:T(8,128)(2,1)S(1)}, u32[]{:S(2)}, u32[]{:S(2)}) collective-permute-start(bf16[544,512]{1,0:T(8,128)(2,1)} %collective-permute-done.17.refs_3_), channel_id=1, source_target_pairs={{0,2},{1,3},{2,0},{3,1},{4,6},{5,7},{6,4},{7,5},{8,10},{9,11},{10,... | collective-permute-start | bytes 1671176 | tf_op jit(solution)/shard_map/ppermute | solution.py:203
  250.1 21.0 %collective-permute-start.35 = (bf16[544,512]{1,0:T(8,128)(2,1)}, bf16[544,512]{1,0:T(8,128)(2,1)S(1)}, u32[]{:S(2)}, u32[]{:S(2)}) collective-permute-start(bf16[544,512]{1,0:T(8,128)(2,1)} %collective-permute-done.31.refs_2_), channel_id=1, source_target_pairs={{0,2},{1,3},{2,0},{3,1},{4,6},{5,7},{6,4},{7,5},{8,10},{9,11},{10,... | collective-permute-start | bytes 1671176 | tf_op jit(solution)/shard_map/ppermute | solution.py:203
  250.3 30.0 %collective-permute-start.25 = (bf16[544,512]{1,0:T(8,128)(2,1)}, bf16[544,512]{1,0:T(8,128)(2,1)S(1)}, u32[]{:S(2)}, u32[]{:S(2)}) collective-permute-start(bf16[544,512]{1,0:T(8,128)(2,1)} %collective-permute-done.17.refs_3_), channel_id=1, source_target_pairs={{0,1},{1,0},{2,3},{3,2},{4,5},{5,4},{6,7},{7,6},{8,9},{9,8},{10,11... | collective-permute-start | bytes 1671176 | tf_op jit(solution)/shard_map/ppermute | solution.py:205
  254.7 25.6 %collective-permute-start.28 = (bf16[544,512]{1,0:T(8,128)(2,1)S(1)}, bf16[544,512]{1,0:T(8,128)(2,1)S(1)}, u32[]{:S(2)}, u32[]{:S(2)}) collective-permute-start(bf16[544,512]{1,0:T(8,128)(2,1)S(1)} %collective-permute-done.20.refs_6_), channel_id=1, source_target_pairs={{0,1},{1,0},{2,3},{3,2},{4,5},{5,4},{6,7},{7,6},{8,9},{9,8},{10,11... | collective-permute-start | bytes 1671176 | tf_op jit(solution)/shard_map/ppermute | solution.py:205
  260.5 22.5 %collective-permute-start.36 = (bf16[544,512]{1,0:T(8,128)(2,1)S(1)}, bf16[544,512]{1,0:T(8,128)(2,1)S(1)}, u32[]{:S(2)}, u32[]{:S(2)}) collective-permute-start(bf16[544,512]{1,0:T(8,128)(2,1)S(1)} %collective-permute-done.32.refs_3_), channel_id=1, source_target_pairs={{0,2},{1,3},{2,0},{3,1},{4,6},{5,7},{6,4},{7,5},{8,10},{9,11},{10,... | collective-permute-start | bytes 1671176 | tf_op jit(solution)/shard_map/ppermute | solution.py:203
  261.9 25.9 %collective-permute-start.29 = (bf16[544,512]{1,0:T(8,128)(2,1)S(1)}, bf16[544,512]{1,0:T(8,128)(2,1)S(1)}, u32[]{:S(2)}, u32[]{:S(2)}) collective-permute-start(bf16[544,512]{1,0:T(8,128)(2,1)S(1)} %collective-permute-done.21.refs_7_), channel_id=1, source_target_pairs={{0,1},{1,0},{2,3},{3,2},{4,5},{5,4},{6,7},{7,6},{8,9},{9,8},{10,11... | collective-permute-start | bytes 1671176 | tf_op jit(solution)/shard_map/ppermute | solution.py:205
  271.1 43.9 %collective-permute-start.39 = (bf16[544,512]{1,0:T(8,128)(2,1)}, bf16[544,512]{1,0:T(8,128)(2,1)S(1)}, u32[]{:S(2)}, u32[]{:S(2)}) collective-permute-start(bf16[544,512]{1,0:T(8,128)(2,1)} %collective-permute-done.31.refs_2_), channel_id=1, source_target_pairs={{0,1},{1,0},{2,3},{3,2},{4,5},{5,4},{6,7},{7,6},{8,9},{9,8},{10,11... | collective-permute-start | bytes 1671176 | tf_op jit(solution)/shard_map/ppermute | solution.py:205
  280.2 34.8 %collective-permute-start.42 = (bf16[544,512]{1,0:T(8,128)(2,1)}, bf16[544,512]{1,0:T(8,128)(2,1)S(1)}, u32[]{:S(2)}, u32[]{:S(2)}) collective-permute-start(bf16[544,512]{1,0:T(8,128)(2,1)} %collective-permute-done.34.refs_5_), channel_id=1, source_target_pairs={{0,1},{1,0},{2,3},{3,2},{4,5},{5,4},{6,7},{7,6},{8,9},{9,8},{10,11... | collective-permute-start | bytes 1671176 | tf_op jit(solution)/shard_map/ppermute | solution.py:205
  280.2 34.9 %collective-permute-start.40 = (bf16[544,512]{1,0:T(8,128)(2,1)S(1)}, bf16[544,512]{1,0:T(8,128)(2,1)S(1)}, u32[]{:S(2)}, u32[]{:S(2)}) collective-permute-start(bf16[544,512]{1,0:T(8,128)(2,1)S(1)} %collective-permute-done.32.refs_3_), channel_id=1, source_target_pairs={{0,1},{1,0},{2,3},{3,2},{4,5},{5,4},{6,7},{7,6},{8,9},{9,8},{10,11... | collective-permute-start | bytes 1671176 | tf_op jit(solution)/shard_map/ppermute | solution.py:205
  283.1 32.0 %collective-permute-start.43 = (bf16[544,512]{1,0:T(8,128)(2,1)S(1)}, bf16[544,512]{1,0:T(8,128)(2,1)S(1)}, u32[]{:S(2)}, u32[]{:S(2)}) collective-permute-start(bf16[544,512]{1,0:T(8,128)(2,1)S(1)} %collective-permute-done.35.refs_6_), channel_id=1, source_target_pairs={{0,1},{1,0},{2,3},{3,2},{4,5},{5,4},{6,7},{7,6},{8,9},{9,8},{10,11... | collective-permute-start | bytes 1671176 | tf_op jit(solution)/shard_map/ppermute | solution.py:205
  287.8 27.3 %collective-permute-start.44 = (bf16[544,512]{1,0:T(8,128)(2,1)S(1)}, bf16[544,512]{1,0:T(8,128)(2,1)S(1)}, u32[]{:S(2)}, u32[]{:S(2)}) collective-permute-start(bf16[544,512]{1,0:T(8,128)(2,1)S(1)} %collective-permute-done.36.refs_7_), channel_id=1, source_target_pairs={{0,1},{1,0},{2,3},{3,2},{4,5},{5,4},{6,7},{7,6},{8,9},{9,8},{10,11... | collective-permute-start | bytes 1671176 | tf_op jit(solution)/shard_map/ppermute | solution.py:205
  (23 other events, 294.2 us)
Sparse Core Ops, SparseCore 0:
  65.3 86.3 all-reduce.2

commit v2 on v1

--- a/solution.py
+++ b/solution.py
@@ -13,18 +13,21 @@
 HEAD_SIZE = 128
 BLOCK_SLOTS = 512
 HEAD_GROUPS = QUERY_HEADS // KEY_VALUE_HEADS
-CHUNKS = 2
-CHUNK_HEADS = KEY_VALUE_HEADS // CHUNKS
+CHUNKS = ((0, 3), (3, 1))
 PLANE = 4
 GATHER_LIMIT = 40 * 2**20
 MASKED = -1e30
 VMEM = pl.BlockSpec(memory_space=pltpu.VMEM)
 SMEM = pl.BlockSpec(memory_space=pltpu.SMEM)
-ANY = pl.BlockSpec(memory_space=pl.ANY)
+HBM = pl.BlockSpec(memory_space=pltpu.HBM)
 
 
 def grant(mebibytes):
     return pltpu.CompilerParams(vmem_limit_bytes=mebibytes * 2**20)
+
+
+def cost(flops, moved):
+    return pl.CostEstimate(flops=flops, bytes_accessed=moved, transcendentals=0)
 
 
 def one_hot_rows(count, index_row):
@@ -69,9 +72,9 @@
 
 
 def query_kernel(
-    route_ref, seat_ref, positions_ref, frequency_ref, queries_ref,
-    turned_ref, bounds_ref, cosine_ref, sine_ref,
+    route_ref, seat_ref, positions_ref, frequency_ref, queries_ref, *refs
 ):
+    turned_refs, (bounds_ref, cosine_ref, sine_ref) = refs[: len(CHUNKS)], refs[len(CHUNKS) :]
     route = route_ref[...]
     count = route.shape[0]
     lines = positions_ref.shape[0]
@@ -93,7 +96,7 @@
     sine = jnp.where(lanes < HEAD_SIZE // 2, -sine, sine)
     cosine_ref[...] = cosine
     sine_ref[...] = sine
-    seats = one_hot_rows(turned_ref.shape[0], seat_ref[...])
+    seats = one_hot_rows(bounds_ref.shape[0], seat_ref[...])
     first = route - spot.astype(jnp.int32)
     first_line = lax.div(first, HEAD_SIZE)
     first_lane = first - first_line * HEAD_SIZE
@@ -108,101 +111,137 @@
     start = placed[:, 2:3] * HEAD_SIZE + placed[:, 3:4] + live
     seat_lanes = lax.broadcasted_iota(jnp.int32, placed.shape, 1)
     bounds_ref[...] = jnp.where(seat_lanes == 0, last, start).astype(jnp.int32)
-    for head in range(queries_ref.shape[1] // HEAD_SIZE):
-        span = slice(head * HEAD_SIZE, (head + 1) * HEAD_SIZE)
-        turned = turn(queries_ref[:, span].astype(jnp.float32), cosine, sine)
-        turned_ref[:, span] = contract(seats, turned, 1, 0).astype(jnp.bfloat16)
+    for (first_head, heads), turned_ref in zip(CHUNKS, turned_refs):
+        for head in range(heads * HEAD_GROUPS):
+            at = (first_head * HEAD_GROUPS + head) * HEAD_SIZE
+            one = queries_ref[:, at : at + HEAD_SIZE].astype(jnp.float32)
+            turned_ref[:, head * HEAD_SIZE : (head + 1) * HEAD_SIZE] = contract(
+                seats, turn(one, cosine, sine), 1, 0
+            ).astype(jnp.bfloat16)
+
+
+def fetch(pieces, refs, place, done):
+    copies = []
+    for at, ((source, first), ref) in enumerate(zip(pieces, refs)):
+        copies.append(
+            pltpu.make_async_copy(ref, place(source, first, ref.shape[0]), done.at[at])
+        )
+        copies[-1].start()
+    return copies
 
 
 def project_kernel(
-    owners_ref, hidden_ref, bias_ref, cosine_ref, sine_ref, bucket_ref, *refs
+    heads, pieces, owners_ref, hidden_ref, bias_ref, cosine_ref, sine_ref, bucket_ref, *refs
 ):
-    ranks = owners_ref.shape[0]
-    blocks, outs = refs[:ranks], refs[ranks : ranks + CHUNKS]
-    matrix, done = refs[ranks + CHUNKS :]
-    depth = blocks[0].shape[0]
-    copies = [
-        pltpu.make_async_copy(
-            blocks[j],
-            matrix.at[pl.ds(pl.multiple_of(owners_ref[j] * depth, 16), depth)],
-            done.at[j],
-        )
-        for j in range(ranks)
-    ]
-    for copy in copies:
-        copy.start()
-    places = one_hot_rows(outs[0].shape[0], bucket_ref[...])
+    parts, out_ref, matrix, done = refs[: len(pieces)], *refs[len(pieces) :]
+    depth = matrix.shape[0] // owners_ref.shape[0]
+    copies = fetch(
+        pieces,
+        parts,
+        lambda source, first, rows: matrix.at[
+            pl.ds(pl.multiple_of(owners_ref[source] * depth + first, 16), rows)
+        ],
+        done,
+    )
+    places = one_hot_rows(out_ref.shape[0], bucket_ref[...])
     for copy in copies:
         copy.wait()
-    wide = CHUNK_HEADS * HEAD_SIZE
-    for chunk in range(CHUNKS):
-        for part in range(2):
-            first = part * KEY_VALUE_HEADS * HEAD_SIZE + chunk * wide
-            span = slice(first, first + wide)
-            rows = contract(hidden_ref[...], matrix[:, span], 1, 0) + bias_ref[:, span]
-            rows = rows.astype(jnp.bfloat16)
-            for head in range(CHUNK_HEADS):
-                one = rows[:, head * HEAD_SIZE : (head + 1) * HEAD_SIZE]
-                if part == 0:
-                    one = turn(one.astype(jnp.float32), cosine_ref[...], sine_ref[...])
-                at = part * wide + head * HEAD_SIZE
-                outs[chunk][:, at : at + HEAD_SIZE] = contract(places, one, 1, 0).astype(
-                    jnp.bfloat16
-                )
+    wide = heads * HEAD_SIZE
+    for part in range(2):
+        span = slice(part * wide, (part + 1) * wide)
+        rows = contract(hidden_ref[...], matrix[:, span], 1, 0) + bias_ref[:, span]
+        rows = rows.astype(jnp.bfloat16)
+        for head in range(heads):
+            one = rows[:, head * HEAD_SIZE : (head + 1) * HEAD_SIZE]
+            if part == 0:
+                one = turn(one.astype(jnp.float32), cosine_ref[...], sine_ref[...])
+            at = part * wide + head * HEAD_SIZE
+            out_ref[:, at : at + HEAD_SIZE] = contract(places, one, 1, 0).astype(jnp.bfloat16)
 
 
 def attend_kernel(
-    chunk, spare, window, stride, queries_ref, bounds_ref, routes_ref, seat_ref, *refs
+    chunk, pieces, spare, window, stride, queries_ref, bounds_ref, routes_ref, seat_ref, *refs
 ):
+    first_head, heads = chunk
     ranks = routes_ref.shape[0]
-    blocks, out_ref, mixed_ref = refs[:ranks], refs[ranks], refs[ranks + 1]
-    wide = CHUNK_HEADS * HEAD_SIZE
+    parts, out_ref, blocks, mixed_ref, result_ref, done = refs[: len(pieces)], *refs[-5:]
+    copies = fetch(
+        pieces, parts, lambda source, first, rows: blocks.at[source, pl.ds(first, rows)], done
+    )
+    for copy in copies:
+        copy.wait()
+    wide = heads * HEAD_SIZE
     scale = math.log2(math.e) / math.sqrt(HEAD_SIZE)
 
     def one_group(group, carry):
         seats = pl.ds(pl.multiple_of(group * stride, 16), stride)
-        start = pl.multiple_of(lax.div(group * spare, 16) * 16, 16)
-        keys_at = pl.ds(start, window)
+        keys_at = pl.ds(pl.multiple_of(lax.div(group * spare, 16) * 16, 16), window)
         routes = routes_ref[group]
         visible = (routes <= bounds_ref[seats, 0:1]) & (routes >= bounds_ref[seats, 1:2])
         veil = jnp.where(visible, 0.0, MASKED)
         veil = jnp.concatenate([veil] * HEAD_GROUPS, axis=0)
-        for head in range(CHUNK_HEADS):
+        for head in range(heads):
             span = slice(head * HEAD_SIZE, (head + 1) * HEAD_SIZE)
             value_span = slice(wide + head * HEAD_SIZE, wide + (head + 1) * HEAD_SIZE)
-            heads = [
+            turns = [
                 slice(at * HEAD_SIZE, (at + 1) * HEAD_SIZE)
                 for at in range(head * HEAD_GROUPS, (head + 1) * HEAD_GROUPS)
             ]
-            query = jnp.concatenate([queries_ref[seats, one] for one in heads], axis=0)
-            keys = jnp.concatenate([block[keys_at, span] for block in blocks], axis=0)
-            values = jnp.concatenate([block[keys_at, value_span] for block in blocks], axis=0)
+            query = jnp.concatenate([queries_ref[seats, one] for one in turns], axis=0)
+            keys = jnp.concatenate([blocks[j, keys_at, span] for j in range(ranks)], axis=0)
+            values = jnp.concatenate(
+                [blocks[j, keys_at, value_span] for j in range(ranks)], axis=0
+            )
             scores = contract(query, keys, 1, 1) * scale + veil
             weights = jnp.exp2(scores - jnp.max(scores, axis=1, keepdims=True))
             totals = jnp.sum(weights, axis=1, keepdims=True)
             mixed = contract(weights.astype(jnp.bfloat16), values, 1, 0) / totals
             mixed = mixed.astype(jnp.bfloat16)
-            for place, one in enumerate(heads):
+            for place, one in enumerate(turns):
                 mixed_ref[seats, one] = mixed[place * stride : (place + 1) * stride]
         return carry
 
     lax.fori_loop(0, ranks, one_group, 0)
     seats = one_hot_rows(mixed_ref.shape[0], seat_ref[...])
-    for head in range(out_ref.shape[1] // HEAD_SIZE):
+    for head in range(result_ref.shape[1] // HEAD_SIZE):
         span = slice(head * HEAD_SIZE, (head + 1) * HEAD_SIZE)
-        out_ref[:, span] = contract(seats, mixed_ref[:, span], 0, 0).astype(jnp.bfloat16)
-
-
-def spread(block, ranks):
+        result_ref[:, span] = contract(seats, mixed_ref[:, span], 0, 0).astype(jnp.bfloat16)
+    columns = pl.ds(first_head * HEAD_GROUPS * HEAD_SIZE, result_ref.shape[1])
+    leave = pltpu.make_async_copy(result_ref, out_ref.at[:, columns], done.at[len(pieces)])
+    leave.start()
+    leave.wait()
+
+
+def spread(block, ranks, after=None):
     ring = [(rank, (rank + PLANE) % ranks) for rank in range(ranks)]
     across = [(rank, rank ^ 2) for rank in range(ranks)]
     beside = [(rank, rank ^ 1) for rank in range(ranks)]
-    lanes = [block]
-    for _ in range(ranks // PLANE - 1):
-        lanes.append(lax.ppermute(lanes[-1], "dp", ring))
-    others = [lax.ppermute(lane, "dp", across) for lane in lanes]
-    held = lanes + others
-    return held + [lax.ppermute(one, "dp", beside) for one in held]
+    steps = ranks // PLANE
+    half = block.shape[0] // 32 * 16
+    if after is not None:
+        block, after = lax.optimization_barrier((block, after))
+    pieces, arrays = [], []
+
+    def keep(source, first, array):
+        pieces.extend([(source, first), (source + 2 * steps, first)])
+        arrays.extend([array, lax.ppermute(array, "dp", beside)])
+
+    lane, other = block, None
+    for step in range(steps - 1):
+        lane_next = lax.ppermute(lane, "dp", ring)
+        other_next = lax.ppermute(lane, "dp", across)
+        keep(step, 0, lane)
+        if step:
+            keep(steps + step - 1, 0, other)
+        lane, other = lax.optimization_barrier((lane_next, other_next))
+    mark = other
+    over = lax.ppermute(lane[:half], "dp", across)
+    round_ = lax.ppermute(other[half:], "dp", ring)
+    keep(steps - 1, 0, lane)
+    keep(2 * steps - 2, 0, other)
+    keep(2 * steps - 1, 0, over)
+    keep(2 * steps - 1, half, round_)
+    return pieces, arrays, mark
 
 
 def source_order(ranks):
@@ -233,12 +272,18 @@
     window = max(
         -(-(group + 1) * spare // 16) * 16 - starts[group] for group in range(ranks)
     )
-    pair_width = 2 * key_matrix.shape[1]
-    chunk_width = pair_width // CHUNKS
-    query_width = queries.shape[1]
+    depth, query_width = hidden.shape[1], queries.shape[1]
     shape = jax.ShapeDtypeStruct
 
-    matrices = spread(jnp.concatenate([key_matrix, value_matrix], axis=1), ranks)
+    def columns(array, chunk):
+        first, heads = chunk
+        return array[..., first * HEAD_SIZE : (first + heads) * HEAD_SIZE]
+
+    matrices, mark = [], None
+    for chunk in CHUNKS:
+        block = jnp.concatenate([columns(key_matrix, chunk), columns(value_matrix, chunk)], axis=1)
+        *matrix, mark = spread(block, ranks, mark)
+        matrices.append(matrix)
 
     bucket, seat, sorted_route = pl.pallas_call(
         functools.partial(order_kernel, ranks, slots, spare, stride),
@@ -252,8 +297,9 @@
         compiler_params=grant(16),
         name="order",
     )(route.reshape(1, rows))
-    plan = lax.all_gather(
-        jnp.concatenate([sorted_route.reshape(width), positions]), "dp", axis=0, tiled=False
+    plan = jnp.concatenate([sorted_route.reshape(width), positions])
+    plan = lax.all_to_all(
+        jnp.broadcast_to(plan, (ranks, width + slots)), "dp", split_axis=0, concat_axis=0, tiled=True
     )
     all_positions = plan[:, width:].reshape(-1, HEAD_SIZE)
     owners = source_order(ranks)
@@ -264,17 +310,21 @@
 
     half = HEAD_SIZE // 2
     frequency = 1000000.0 ** (-(jnp.arange(half, dtype=jnp.float32) * 2.0 / HEAD_SIZE))
-    turned, bounds, cosine, sine = pl.pallas_call(
+    *turned, bounds, cosine, sine = pl.pallas_call(
         query_kernel,
-        out_shape=(
-            shape((ranks * stride, query_width), jnp.bfloat16),
+        out_shape=tuple(
+            shape((ranks * stride, heads * HEAD_GROUPS * HEAD_SIZE), jnp.bfloat16)
+            for _, heads in CHUNKS
+        )
+        + (
             shape((ranks * stride, HEAD_SIZE), jnp.int32),
             shape((rows, HEAD_SIZE), jnp.float32),
             shape((rows, HEAD_SIZE), jnp.float32),
         ),
         in_specs=[VMEM] * 5,
-        out_specs=(VMEM,) * 4,
+        out_specs=(VMEM,) * (len(CHUNKS) + 3),
         compiler_params=grant(32),
+        cost_estimate=cost(4 * stride * ranks * rows * query_width, 4 * rows * query_width),
         name="turn_queries",
     )(
         route.reshape(rows, 1),
@@ -284,46 +334,62 @@
         queries,
     )
 
-    bias = jnp.concatenate([key_projection_bias, value_projection_bias])
-    pairs = pl.pallas_call(
-        project_kernel,
-        out_shape=(shape((width, chunk_width), jnp.bfloat16),) * CHUNKS,
-        in_specs=[SMEM] + [VMEM] * 5 + [ANY] * ranks,
-        out_specs=(VMEM,) * CHUNKS,
-        scratch_shapes=[
-            pltpu.VMEM((hidden.shape[1], pair_width), jnp.bfloat16),
-            pltpu.SemaphoreType.DMA((ranks,)),
-        ],
-        compiler_params=grant(44),
-        name="project",
-    )(
-        owners,
-        hidden,
-        bias.astype(jnp.float32).reshape(1, pair_width),
-        cosine,
-        sine,
-        bucket,
-        *matrices,
-    )
-
-    outs = []
-    for chunk in range(CHUNKS):
-        columns = query_width // CHUNKS
-        blocks = spread(pairs[chunk], ranks)
-        outs.append(
+    pairs = []
+    for chunk, (pieces, arrays) in zip(CHUNKS, matrices):
+        bias = jnp.concatenate(
+            [columns(key_projection_bias, chunk), columns(value_projection_bias, chunk)]
+        )
+        wide = bias.shape[0]
+        pairs.append(
             pl.pallas_call(
-                functools.partial(attend_kernel, chunk, spare, window, stride),
-                grid=(1,),
-                out_shape=shape((rows, columns), jnp.bfloat16),
-                in_specs=[pl.BlockSpec((ranks * stride, columns), lambda i, c=chunk: (0, c))]
-                + [VMEM] * (3 + ranks),
+                functools.partial(project_kernel, chunk[1], pieces),
+                out_shape=shape((width, wide), jnp.bfloat16),
+                in_specs=[SMEM] + [VMEM] * 5 + [HBM] * len(pieces),
                 out_specs=VMEM,
-                scratch_shapes=[pltpu.VMEM((ranks * stride, columns), jnp.bfloat16)],
-                compiler_params=grant(40),
-                name="attend",
-            )(turned, bounds, key_routes, seat, *blocks)
+                scratch_shapes=[
+                    pltpu.VMEM((depth, wide), jnp.bfloat16),
+                    pltpu.SemaphoreType.DMA((len(pieces),)),
+                ],
+                compiler_params=grant(36),
+                cost_estimate=cost(2 * rows * depth * wide, 2 * depth * (rows + wide)),
+                name="project",
+            )(
+                owners,
+                hidden,
+                bias.astype(jnp.float32).reshape(1, wide),
+                cosine,
+                sine,
+                bucket,
+                *arrays,
+            )
         )
-    return jnp.concatenate(outs, axis=1)
+
+    out, mark = None, None
+    for index, chunk in enumerate(CHUNKS):
+        query_heads = chunk[1] * HEAD_GROUPS
+        pieces, arrays, mark = spread(pairs[index], ranks, mark)
+        wide = pairs[index].shape[1]
+        taken = [] if out is None else [out]
+        fixed = [turned[index], bounds, key_routes, seat]
+        out = pl.pallas_call(
+            functools.partial(attend_kernel, chunk, pieces, spare, window, stride),
+            out_shape=shape((rows, query_width), jnp.bfloat16),
+            in_specs=[VMEM] * len(fixed) + [HBM] * (len(pieces) + len(taken)),
+            out_specs=HBM,
+            scratch_shapes=[
+                pltpu.VMEM((ranks, width, wide), jnp.bfloat16),
+                pltpu.VMEM((ranks * stride, query_heads * HEAD_SIZE), jnp.bfloat16),
+                pltpu.VMEM((rows, query_heads * HEAD_SIZE), jnp.bfloat16),
+                pltpu.SemaphoreType.DMA((len(pieces) + 1,)),
+            ],
+            input_output_aliases={len(fixed) + len(pieces): 0} if taken else {},
+            compiler_params=grant(32),
+            cost_estimate=cost(
+                16 * rows * stride * ranks * query_heads * HEAD_SIZE, 2 * ranks * width * wide
+            ),
+            name="attend",
+        )(*fixed, *arrays, *taken)
+    return out
 
 
 def apply_rotary(rows, slot_offset, heads):

time: 345 us -> 287 us (0.83)
  waiting for transfers between devices: 165 us -> 116 us
  between operations: 14.5 us -> 0.9 us
  Pallas kernels: 67.1 us -> 73.5 us
    unnamed x2 -> x0, waiting for transfers between devices: 59.3 us -> none
    ppermute x45 -> x68, waiting for transfers between devices: 105 us -> 115 us  [the longest x12 87.4 us: spread(): lane_next = lax.ppermute(lane, 'dp', ring)]
    unnamed x68 -> x74, local copies, waits for them, and re-layouts: 19.8 us -> 11 us
    pallas_call x4 -> x5, Pallas kernels: 66.6 us -> 73.1 us  [the longest x2 44.2 us: gather_plan(): pl.pallas_call(functools.partial(attend_kernel, chunk, pieces, spare, win...]
    slice x0 -> x14, local copies, waits for them, and re-layouts: none -> 6.37 us  [the longest x4 2.19 us: spread(): round_ = lax.ppermute(other[half:], 'dp', ring)]
    all_to_all x0 -> x1, starting transfers between devices: none -> 4.05 us  [gather_plan(): lax.all_to_all(jnp.broadcast_to(plan, (ranks, width + slots)), 'dp', spli...]
    ppermute x45 -> x68, starting transfers between devices: 69.5 us -> 67.9 us  [the longest x36 47.2 us: keep(): arrays.extend([array, lax.ppermute(array, 'dp', beside)])]
  transfers between devices with their start and end apart: 46 -> 69, of which waited for: 16 -> 19; matrix products, arithmetic and copies ran while one was open for 2% -> 4% of each run, Pallas kernels for 8% -> 17%
where the time goes in v2:
time: 287 us; the launch traced here: 286 us
  waiting for transfers between devices  116 us (40%)
  Pallas kernels  73.5 us (26%)
  starting transfers between devices  72 us (25%)
  local copies, waits for them, and re-layouts  22.5 us (8%)
    ppermute x12, waiting for transfers between devices, spread(): lane_next = lax.ppermute(lane, 'dp', ring)  87.4 us
    ppermute x36, starting transfers between devices, keep(): arrays.extend([array, lax.ppermute(array, 'dp', beside)])  47.2 us
    pallas_call x2, Pallas kernels, gather_plan(): pl.pallas_call(functools.partial(attend_kernel, chunk, pieces, spare, win...  44.2 us
    pallas_call x2, Pallas kernels, gather_plan(): pl.pallas_call(functools.partial(project_kernel, chunk[1], pieces), out_s...  22.6 us
    ppermute x4, waiting for transfers between devices, spread(): over = lax.ppermute(lane[:half], 'dp', across)  17.5 us
    unnamed x74, local copies, waits for them, and re-layouts  11 us
    ppermute x12, starting transfers between devices, spread(): other_next = lax.ppermute(lane, 'dp', across)  9.71 us
    pallas_call x1, Pallas kernels, gather_plan(): pl.pallas_call(query_kernel, out_shape=tuple((shape((ranks * stride, head...  6.29 us
  transfers between devices with their start and end apart: 69, of which 19 were waited for; matrix products, arithmetic and copies ran while one was open for 4% of the time, Pallas kernels for 17%

profile of v2, /device:TPU:1, one launch (start us, length us, event | category | flops | bytes accessed | tf_op | source)
XLA Modules:
  0.0 286.4 jit_solution(1444979445063129113)
XLA Ops:
  2.0 2.2 collective-permute-start
  4.2 1.2 collective-permute-start.1
  5.5 11.7 %collective-permute-done.refs_2_ = bf16[320,768]{1,0:T(8,128)(2,1)S(1)} collective-permute-done((bf16[320,768]{1,0:T(8,128)(2,1)S(1)}, bf16[320,768]{1,0:T(8,128)(2,1)S(1)}, u32[]{:S(2)}, u32[]{:S(2)}) %collective-permute-start) | collective-permute-done | bytes 491552 | tf_op jit(solution)/shard_map/ppermute | solution.py:231
  17.3 1.2 collective-permute-start.3
  18.5 12.0 %collective-permute-done.2.refs_6_ = bf16[320,768]{1,0:T(8,128)(2,1)S(1)} collective-permute-done((bf16[320,768]{1,0:T(8,128)(2,1)S(1)}, bf16[320,768]{1,0:T(8,128)(2,1)S(1)}, u32[]{:S(2)}, u32[]{:S(2)}) %collective-permute-start.2) | collective-permute-done | bytes 491552 | tf_op jit(solution)/shard_map/ppermute | solution.py:231
  31.3 2.8 collective-permute-start.23
  35.9 7.0 %collective-permute-done.4.refs_10_ = bf16[320,768]{1,0:T(8,128)(2,1)S(1)} collective-permute-done((bf16[320,768]{1,0:T(8,128)(2,1)S(1)}, bf16[320,768]{1,0:T(8,128)(2,1)S(1)}, u32[]{:S(2)}, u32[]{:S(2)}) %collective-permute-start.4) | collective-permute-done | bytes 491552 | tf_op jit(solution)/shard_map/ppermute | solution.py:231
  42.9 3.1 %collective-permute-start.26 = (bf16[320,768]{1,0:T(8,128)(2,1)S(1)}, bf16[320,768]{1,0:T(8,128)(2,1)}, u32[]{:S(2)}, u32[]{:S(2)}) collective-permute-start(bf16[320,768]{1,0:T(8,128)(2,1)S(1)} %collective-permute-done.2.refs_6_), channel_id=1, source_target_pairs={{0,1},{1,0},{2,3},{3,2},{4,5},{5,4},{6,7},{7,6},{8,9},{9,8},{10,11... | collective-permute-start | bytes 1474568 | tf_op jit(solution)/shard_map/ppermute | solution.py:227
  47.4 4.1 %all-to-all-start = ((s32[16,1,1568]{2,1,0:T(1,128)}), s32[16,1,1568]{2,1,0:T(1,128)}, u32[]{:S(2)}, u32[]{:S(2)}) async-start(s32[16,1,1568]{2,1,0:T(1,128)} %broadcast_in_dim.4), calls=%async_computation | async-start | bytes 212992 | tf_op jit(solution)/shard_map/all_to_all | solution.py:301
  52.3 1.2 collective-permute-start.32
  54.2 1.2 collective-permute-start.30
  60.6 2.0 collective-permute-done.32.refs_16_
  63.5 1.7 copy-done.2
  65.2 6.3 %turn_queries.1 = (bf16[768,1920]{1,0:T(8,128)(2,1)S(1)}, bf16[768,640]{1,0:T(8,128)(2,1)S(1)}, s32[768,128]{1,0:T(8,128)S(1)}, f32[512,128]{1,0:T(8,128)S(1)}, f32[512,128]{1,0:T(8,128)S(1)}) custom-call(s32[512,1]{1,0:T(8,128)S(1)} %copy.11.route_ref, s32[1,512]{1,0:T(1,128)S(1)} %get-tuple-element.39.seat_ref, s32[128,128]{1,0:T(8,128)S(1)} %reshape.179.positions_ref, ...), custom_call_target="tpu_custom_call" | custom-call | flops 4026531840 | bytes 5242880 | tf_op jit(solution)/shard_map/turn_queries/pallas_call | solution.py:313
  71.6 1.6 copy-done.22
  73.2 11.8 %project.3.refs_0_ = bf16[544,768]{1,0:T(8,128)(2,1)} custom-call(s32[16]{0:T(128)S(1)} %pad_add_fusion.1.owners_ref, bf16[512,5120]{1,0:T(8,128)(2,1)S(1)} %bitcast.20, f32[1,768]{1,0:T(1,128)S(1)} %maximum_convert_fusion.bias_ref, f32[512,128]{1,0:T(8,128)S(1)} %get-tuple-element.43.cosine_ref, f32[512,128]{1,0:T(8,128)S(1)} %get-tuple-element.44.sine_ref, ...), custom_call_target="tpu_custom_call" | custom-call | flops 4026531840 | bytes 13107200 | tf_op jit(solution)/shard_map/project/pallas_call | solution.py:344
  85.8 1.1 collective-permute-start.35
  86.9 20.0 %collective-permute-done.34.refs_2_ = bf16[544,768]{1,0:T(8,128)(2,1)} collective-permute-done((bf16[544,768]{1,0:T(8,128)(2,1)}, bf16[544,768]{1,0:T(8,128)(2,1)}, u32[]{:S(2)}, u32[]{:S(2)}) %collective-permute-start.34) | collective-permute-done | bytes 835616 | tf_op jit(solution)/shard_map/ppermute | solution.py:231
  107.1 1.2 collective-permute-start.37
  109.2 21.9 %collective-permute-done.7.refs_2_ = bf16[320,256]{1,0:T(8,128)(2,1)S(1)} collective-permute-done((bf16[320,256]{1,0:T(8,128)(2,1)S(1)}, bf16[320,256]{1,0:T(8,128)(2,1)S(1)}, u32[]{:S(2)}, u32[]{:S(2)}) %collective-permute-start.7) | collective-permute-done | bytes 163872 | tf_op jit(solution)/shard_map/ppermute | solution.py:231
  131.1 1.2 collective-permute-start.12
  132.3 2.6 collective-permute-start.6
  134.9 2.2 collective-permute-done.11.refs_6_
  137.1 1.2 collective-permute-start.16
  138.9 4.8 %collective-permute-start.9 = (bf16[320,256]{1,0:T(8,128)(2,1)S(1)}, bf16[320,256]{1,0:T(8,128)(2,1)S(1)}, u32[]{:S(2)}, u32[]{:S(2)}) collective-permute-start(bf16[320,256]{1,0:T(8,128)(2,1)S(1)} %collective-permute-done.7.refs_2_), channel_id=1, source_target_pairs={{0,1},{1,0},{2,3},{3,2},{4,5},{5,4},{6,7},{7,6},{8,9},{9,8},{10,11... | collective-permute-start | bytes 491528 | tf_op jit(solution)/shard_map/ppermute | solution.py:227
  143.7 5.8 %collective-permute-start.10 = (bf16[320,256]{1,0:T(8,128)(2,1)S(1)}, bf16[320,256]{1,0:T(8,128)(2,1)S(1)}, u32[]{:S(2)}, u32[]{:S(2)}) collective-permute-start(bf16[320,256]{1,0:T(8,128)(2,1)S(1)} %collective-permute-done.8.refs_4_), channel_id=1, source_target_pairs={{0,1},{1,0},{2,3},{3,2},{4,5},{5,4},{6,7},{7,6},{8,9},{9,8},{10,11... | collective-permute-start | bytes 491528 | tf_op jit(solution)/shard_map/ppermute | solution.py:227
  150.5 1.2 collective-permute-start.19
  151.8 7.3 %collective-permute-done.19.refs_14_ = bf16[160,256]{1,0:T(8,128)(2,1)S(1)} collective-permute-done((bf16[160,256]{1,0:T(8,128)(2,1)S(1)}, bf16[160,256]{1,0:T(8,128)(2,1)S(1)}, u32[]{:S(2)}, u32[]{:S(2)}) %collective-permute-start.19) | collective-permute-done | bytes 81952 | tf_op jit(solution)/shard_map/ppermute | solution.py:238
  159.0 4.3 %collective-permute-start.20 = (bf16[160,256]{1,0:T(8,128)(2,1)S(1)}, bf16[160,256]{1,0:T(8,128)(2,1)S(1)}, u32[]{:S(2)}, u32[]{:S(2)}) collective-permute-start(bf16[160,256]{1,0:T(8,128)(2,1)S(1)} %collective-permute-done.19.refs_14_), channel_id=1, source_target_pairs={{0,1},{1,0},{2,3},{3,2},{4,5},{5,4},{6,7},{7,6},{8,9},{9,8},{10,11... | collective-permute-start | bytes 245768 | tf_op jit(solution)/shard_map/ppermute | solution.py:227
  163.4 1.8 collective-permute-start.18
  165.2 1.3 collective-permute-done.22.refs_17_
  167.0 10.8 %project.2.refs_0_ = bf16[544,256]{1,0:T(8,128)(2,1)S(1)} custom-call(s32[16]{0:T(128)S(1)} %pad_add_fusion.1.owners_ref, bf16[512,5120]{1,0:T(8,128)(2,1)S(1)} %bitcast.20, f32[1,256]{1,0:T(1,128)S(1)} %maximum_convert_fusion.1.bias_ref, f32[512,128]{1,0:T(8,128)S(1)} %get-tuple-element.43.cosine_ref, f32[512,128]{1,0:T(8,128)S(1)} %get-tuple-element.44.sine_ref, ...), custom_call_target="tpu_custom_call" | custom-call | flops 1342177280 | bytes 7864320 | tf_op jit(solution)/shard_map/project/pallas_call | solution.py:344
  181.5 6.2 %collective-permute-done.41.refs_2_ = bf16[544,256]{1,0:T(8,128)(2,1)S(1)} collective-permute-done((bf16[544,256]{1,0:T(8,128)(2,1)S(1)}, bf16[544,256]{1,0:T(8,128)(2,1)S(1)}, u32[]{:S(2)}, u32[]{:S(2)}) %collective-permute-start.41) | collective-permute-done | bytes 278560 | tf_op jit(solution)/shard_map/ppermute | solution.py:231
  193.1 5.8 %collective-permute-done.45.refs_6_ = bf16[544,256]{1,0:T(8,128)(2,1)} collective-permute-done((bf16[544,256]{1,0:T(8,128)(2,1)S(1)}, bf16[544,256]{1,0:T(8,128)(2,1)}, u32[]{:S(2)}, u32[]{:S(2)}) %collective-permute-start.45) | collective-permute-done | bytes 278560 | tf_op jit(solution)/shard_map/ppermute | solution.py:231
  198.8 1.2 collective-permute-start.64
  200.3 1.6 collective-permute-start.43
  202.9 6.0 %collective-permute-done.64.refs_14_ = bf16[272,768]{1,0:T(8,128)(2,1)S(1)} collective-permute-done((bf16[272,768]{1,0:T(8,128)(2,1)}, bf16[272,768]{1,0:T(8,128)(2,1)S(1)}, u32[]{:S(2)}, u32[]{:S(2)}) %collective-permute-start.64) | collective-permute-done | bytes 417824 | tf_op jit(solution)/shard_map/ppermute | solution.py:238
  208.9 2.2 collective-permute-start.62
  211.6 4.6 %collective-permute-start.63 = (bf16[544,768]{1,0:T(8,128)(2,1)S(1)}, bf16[544,768]{1,0:T(8,128)(2,1)}, u32[]{:S(2)}, u32[]{:S(2)}) collective-permute-start(bf16[544,768]{1,0:T(8,128)(2,1)S(1)} %collective-permute-done.39.refs_12_), channel_id=1, source_target_pairs={{0,1},{1,0},{2,3},{3,2},{4,5},{5,4},{6,7},{7,6},{8,9},{9,8},{10,11... | collective-permute-start | bytes 2506760 | tf_op jit(solution)/shard_map/ppermute | solution.py:227
  218.1 5.1 %collective-permute-done.50.refs_12_ = bf16[544,256]{1,0:T(8,128)(2,1)S(1)} collective-permute-done((bf16[544,256]{1,0:T(8,128)(2,1)}, bf16[544,256]{1,0:T(8,128)(2,1)S(1)}, u32[]{:S(2)}, u32[]{:S(2)}) %collective-permute-start.50) | collective-permute-done | bytes 278560 | tf_op jit(solution)/shard_map/ppermute | solution.py:232
  223.2 3.7 %collective-permute-start.47 = (bf16[544,256]{1,0:T(8,128)(2,1)}, bf16[544,256]{1,0:T(8,128)(2,1)}, u32[]{:S(2)}, u32[]{:S(2)}) collective-permute-start(bf16[544,256]{1,0:T(8,128)(2,1)} %collective-permute-done.45.refs_6_), channel_id=1, source_target_pairs={{0,1},{1,0},{2,3},{3,2},{4,5},{5,4},{6,7},{7,6},{8,9},{9,8},{10,11... | collective-permute-start | bytes 835592 | tf_op jit(solution)/shard_map/ppermute | solution.py:227
  229.6 4.3 %collective-permute-done.53.refs_14_ = bf16[272,256]{1,0:T(8,128)(2,1)S(1)} collective-permute-done((bf16[272,256]{1,0:T(8,128)(2,1)}, bf16[272,256]{1,0:T(8,128)(2,1)S(1)}, u32[]{:S(2)}, u32[]{:S(2)}) %collective-permute-start.53) | collective-permute-done | bytes 139296 | tf_op jit(solution)/shard_map/ppermute | solution.py:238
  235.7 1.1 collective-permute-start.56
  236.8 1.1 copy-done.4
  237.9 1.1 copy-done.6
  240.1 1.8 copy-done.23
  241.9 30.4 %attend.2.refs_18_ = bf16[512,2560]{1,0:T(8,128)(2,1)} custom-call(bf16[768,1920]{1,0:T(8,128)(2,1)S(1)} %copy-done.23, s32[768,128]{1,0:T(8,128)S(1)} %copy-done.20, s32[16,1,768]{2,1,0:T(1,128)S(1)} %constant_dynamic-update-slice_fusion.routes_ref, s32[1,512]{1,0:T(1,128)S(1)} %copy-done.16, bf16[544,768]{1,0:T(8,128)(2,1)} %project.3.refs_0_, ...), custom_call_target="tpu_custom_call" | custom-call | flops 12079595520 | bytes 13369344 | tf_op jit(solution)/shard_map/attend/pallas_call | solution.py:374
  272.4 13.8 %attend.3 = bf16[512,2560]{1,0:T(8,128)(2,1)} custom-call(bf16[768,640]{1,0:T(8,128)(2,1)S(1)} %copy-done.18, s32[768,128]{1,0:T(8,128)S(1)} %copy-done.21, s32[16,1,768]{2,1,0:T(1,128)S(1)} %constant_dynamic-update-slice_fusion.routes_ref, s32[1,512]{1,0:T(1,128)S(1)} %copy-done.16, ...), custom_call_target="tpu_custom_call", output_to_operand_aliasing={{}: (22, {})} | custom-call | flops 4026531840 | bytes 4456448 | tf_op jit(solution)/shard_map/attend/pallas_call | solution.py:374
  (225 shorter events, 35.8 us)
Async XLA Ops:
  2.0 15.2 %collective-permute-start = (bf16[320,768]{1,0:T(8,128)(2,1)S(1)}, bf16[320,768]{1,0:T(8,128)(2,1)S(1)}, u32[]{:S(2)}, u32[]{:S(2)}) collective-permute-start(bf16[320,768]{1,0:T(8,128)(2,1)S(1)} %pad_maximum_fusion.refs_0_), channel_id=1, source_target_pairs={{0,4},{1,5},{2,6},{3,7},{4,8},{5,9},{6,10},{7,11},{8,12},{9,13},{1... | collective-permute-start | bytes 1474568 | tf_op jit(solution)/shard_map/ppermute | solution.py:231
  4.2 13.0 %collective-permute-start.1 = (bf16[320,768]{1,0:T(8,128)(2,1)S(1)}, bf16[320,768]{1,0:T(8,128)(2,1)S(1)}, u32[]{:S(2)}, u32[]{:S(2)}) collective-permute-start(bf16[320,768]{1,0:T(8,128)(2,1)S(1)} %pad_maximum_fusion.refs_0_), channel_id=1, source_target_pairs={{0,2},{1,3},{2,0},{3,1},{4,6},{5,7},{6,4},{7,5},{8,10},{9,11},{10,... | collective-permute-start | bytes 1474568 | tf_op jit(solution)/shard_map/ppermute | solution.py:232
  17.2 13.3 %collective-permute-start.2 = (bf16[320,768]{1,0:T(8,128)(2,1)S(1)}, bf16[320,768]{1,0:T(8,128)(2,1)S(1)}, u32[]{:S(2)}, u32[]{:S(2)}) collective-permute-start(bf16[320,768]{1,0:T(8,128)(2,1)S(1)} %collective-permute-done.refs_2_), channel_id=1, source_target_pairs={{0,4},{1,5},{2,6},{3,7},{4,8},{5,9},{6,10},{7,11},{8,12},{9,13},{1... | collective-permute-start | bytes 1474568 | tf_op jit(solution)/shard_map/ppermute | solution.py:231
  17.3 13.2 %collective-permute-start.3 = (bf16[320,768]{1,0:T(8,128)(2,1)S(1)}, bf16[320,768]{1,0:T(8,128)(2,1)}, u32[]{:S(2)}, u32[]{:S(2)}) collective-permute-start(bf16[320,768]{1,0:T(8,128)(2,1)S(1)} %collective-permute-done.refs_2_), channel_id=1, source_target_pairs={{0,2},{1,3},{2,0},{3,1},{4,6},{5,7},{6,4},{7,5},{8,10},{9,11},{10,... | collective-permute-start | bytes 1474568 | tf_op jit(solution)/shard_map/ppermute | solution.py:232
  30.5 12.4 %collective-permute-start.4 = (bf16[320,768]{1,0:T(8,128)(2,1)S(1)}, bf16[320,768]{1,0:T(8,128)(2,1)S(1)}, u32[]{:S(2)}, u32[]{:S(2)}) collective-permute-start(bf16[320,768]{1,0:T(8,128)(2,1)S(1)} %collective-permute-done.2.refs_6_), channel_id=1, source_target_pairs={{0,4},{1,5},{2,6},{3,7},{4,8},{5,9},{6,10},{7,11},{8,12},{9,13},{1... | collective-permute-start | bytes 1474568 | tf_op jit(solution)/shard_map/ppermute | solution.py:231
  30.5 21.0 %collective-permute-start.5 = (bf16[320,768]{1,0:T(8,128)(2,1)S(1)}, bf16[320,768]{1,0:T(8,128)(2,1)S(1)}, u32[]{:S(2)}, u32[]{:S(2)}) collective-permute-start(bf16[320,768]{1,0:T(8,128)(2,1)S(1)} %collective-permute-done.2.refs_6_), channel_id=1, source_target_pairs={{0,2},{1,3},{2,0},{3,1},{4,6},{5,7},{6,4},{7,5},{8,10},{9,11},{10,... | collective-permute-start | bytes 1474568 | tf_op jit(solution)/shard_map/ppermute | solution.py:232
  31.3 22.9 %collective-permute-start.23 = (bf16[320,768]{1,0:T(8,128)(2,1)S(1)}, bf16[320,768]{1,0:T(8,128)(2,1)}, u32[]{:S(2)}, u32[]{:S(2)}) collective-permute-start(bf16[320,768]{1,0:T(8,128)(2,1)S(1)} %pad_maximum_fusion.refs_0_), channel_id=1, source_target_pairs={{0,1},{1,0},{2,3},{3,2},{4,5},{5,4},{6,7},{7,6},{8,9},{9,8},{10,11... | collective-permute-start | bytes 1474568 | tf_op jit(solution)/shard_map/ppermute | solution.py:227
  35.3 20.1 %collective-permute-start.24 = (bf16[320,768]{1,0:T(8,128)(2,1)S(1)}, bf16[320,768]{1,0:T(8,128)(2,1)}, u32[]{:S(2)}, u32[]{:S(2)}) collective-permute-start(bf16[320,768]{1,0:T(8,128)(2,1)S(1)} %collective-permute-done.refs_2_), channel_id=1, source_target_pairs={{0,1},{1,0},{2,3},{3,2},{4,5},{5,4},{6,7},{7,6},{8,9},{9,8},{10,11... | collective-permute-start | bytes 1474568 | tf_op jit(solution)/shard_map/ppermute | solution.py:227
  35.4 21.0 %collective-permute-start.25 = (bf16[320,768]{1,0:T(8,128)(2,1)S(1)}, bf16[320,768]{1,0:T(8,128)(2,1)}, u32[]{:S(2)}, u32[]{:S(2)}) collective-permute-start(bf16[320,768]{1,0:T(8,128)(2,1)S(1)} %collective-permute-done.1.refs_4_), channel_id=1, source_target_pairs={{0,1},{1,0},{2,3},{3,2},{4,5},{5,4},{6,7},{7,6},{8,9},{9,8},{10,11... | collective-permute-start | bytes 1474568 | tf_op jit(solution)/shard_map/ppermute | solution.py:227
  42.9 13.6 %collective-permute-start.26 = (bf16[320,768]{1,0:T(8,128)(2,1)S(1)}, bf16[320,768]{1,0:T(8,128)(2,1)}, u32[]{:S(2)}, u32[]{:S(2)}) collective-permute-start(bf16[320,768]{1,0:T(8,128)(2,1)S(1)} %collective-permute-done.2.refs_6_), channel_id=1, source_target_pairs={{0,1},{1,0},{2,3},{3,2},{4,5},{5,4},{6,7},{7,6},{8,9},{9,8},{10,11... | collective-permute-start | bytes 1474568 | tf_op jit(solution)/shard_map/ppermute | solution.py:227
  47.4 10.7 %all-to-all-start = ((s32[16,1,1568]{2,1,0:T(1,128)}), s32[16,1,1568]{2,1,0:T(1,128)}, u32[]{:S(2)}, u32[]{:S(2)}) async-start(s32[16,1,1568]{2,1,0:T(1,128)} %broadcast_in_dim.4), calls=%async_computation | async-start | bytes 212992 | tf_op jit(solution)/shard_map/all_to_all | solution.py:301
  52.3 10.3 %collective-permute-start.32 = (bf16[160,768]{1,0:T(8,128)(2,1)}, bf16[160,768]{1,0:T(8,128)(2,1)}, u32[]{:S(2)}, u32[]{:S(2)}) collective-permute-start(bf16[160,768]{1,0:T(8,128)(2,1)} %slice.131), channel_id=1, source_target_pairs={{0,4},{1,5},{2,6},{3,7},{4,8},{5,9},{6,10},{7,11},{8,12},{9,13},{1... | collective-permute-start | bytes 737288 | tf_op jit(solution)/shard_map/ppermute | solution.py:239
  55.5 17.7 %collective-permute-start.27 = (bf16[320,768]{1,0:T(8,128)(2,1)}, bf16[320,768]{1,0:T(8,128)(2,1)}, u32[]{:S(2)}, u32[]{:S(2)}) collective-permute-start(bf16[320,768]{1,0:T(8,128)(2,1)} %collective-permute-done.3.refs_8_), channel_id=1, source_target_pairs={{0,1},{1,0},{2,3},{3,2},{4,5},{5,4},{6,7},{7,6},{8,9},{9,8},{10,11... | collective-permute-start | bytes 1474568 | tf_op jit(solution)/shard_map/ppermute | solution.py:227
  56.4 16.8 %collective-permute-start.29 = (bf16[320,768]{1,0:T(8,128)(2,1)S(1)}, bf16[320,768]{1,0:T(8,128)(2,1)}, u32[]{:S(2)}, u32[]{:S(2)}) collective-permute-start(bf16[320,768]{1,0:T(8,128)(2,1)S(1)} %collective-permute-done.5.refs_12_), channel_id=1, source_target_pairs={{0,1},{1,0},{2,3},{3,2},{4,5},{5,4},{6,7},{7,6},{8,9},{9,8},{10,11... | collective-permute-start | bytes 1474568 | tf_op jit(solution)/shard_map/ppermute | solution.py:227
  56.5 16.7 %collective-permute-start.28 = (bf16[320,768]{1,0:T(8,128)(2,1)S(1)}, bf16[320,768]{1,0:T(8,128)(2,1)}, u32[]{:S(2)}, u32[]{:S(2)}) collective-permute-start(bf16[320,768]{1,0:T(8,128)(2,1)S(1)} %collective-permute-done.4.refs_10_), channel_id=1, source_target_pairs={{0,1},{1,0},{2,3},{3,2},{4,5},{5,4},{6,7},{7,6},{8,9},{9,8},{10,11... | collective-permute-start | bytes 1474568 | tf_op jit(solution)/shard_map/ppermute | solution.py:227
  62.6 10.5 %collective-permute-start.33 = (bf16[160,768]{1,0:T(8,128)(2,1)}, bf16[160,768]{1,0:T(8,128)(2,1)S(1)}, u32[]{:S(2)}, u32[]{:S(2)}) collective-permute-start(bf16[160,768]{1,0:T(8,128)(2,1)} %collective-permute-done.32.refs_16_), channel_id=1, source_target_pairs={{0,1},{1,0},{2,3},{3,2},{4,5},{5,4},{6,7},{7,6},{8,9},{9,8},{10,11... | collective-permute-start | bytes 737288 | tf_op jit(solution)/shard_map/ppermute | solution.py:227
  85.0 21.8 %collective-permute-start.34 = (bf16[544,768]{1,0:T(8,128)(2,1)}, bf16[544,768]{1,0:T(8,128)(2,1)}, u32[]{:S(2)}, u32[]{:S(2)}) collective-permute-start(bf16[544,768]{1,0:T(8,128)(2,1)} %project.3.refs_0_), channel_id=1, source_target_pairs={{0,4},{1,5},{2,6},{3,7},{4,8},{5,9},{6,10},{7,11},{8,12},{9,13},{1... | collective-permute-start | bytes 2506760 | tf_op jit(solution)/shard_map/ppermute | solution.py:231
  85.8 21.1 %collective-permute-start.35 = (bf16[544,768]{1,0:T(8,128)(2,1)}, bf16[544,768]{1,0:T(8,128)(2,1)}, u32[]{:S(2)}, u32[]{:S(2)}) collective-permute-start(bf16[544,768]{1,0:T(8,128)(2,1)} %project.3.refs_0_), channel_id=1, source_target_pairs={{0,2},{1,3},{2,0},{3,1},{4,6},{5,7},{6,4},{7,5},{8,10},{9,11},{10,... | collective-permute-start | bytes 2506760 | tf_op jit(solution)/shard_map/ppermute | solution.py:232
  106.9 31.4 %collective-permute-start.36 = (bf16[544,768]{1,0:T(8,128)(2,1)}, bf16[544,768]{1,0:T(8,128)(2,1)S(1)}, u32[]{:S(2)}, u32[]{:S(2)}) collective-permute-start(bf16[544,768]{1,0:T(8,128)(2,1)} %collective-permute-done.34.refs_2_), channel_id=1, source_target_pairs={{0,4},{1,5},{2,6},{3,7},{4,8},{5,9},{6,10},{7,11},{8,12},{9,13},{1... | collective-permute-start | bytes 2506760 | tf_op jit(solution)/shard_map/ppermute | solution.py:231
  107.1 31.2 %collective-permute-start.37 = (bf16[544,768]{1,0:T(8,128)(2,1)}, bf16[544,768]{1,0:T(8,128)(2,1)S(1)}, u32[]{:S(2)}, u32[]{:S(2)}) collective-permute-start(bf16[544,768]{1,0:T(8,128)(2,1)} %collective-permute-done.34.refs_2_), channel_id=1, source_target_pairs={{0,2},{1,3},{2,0},{3,1},{4,6},{5,7},{6,4},{7,5},{8,10},{9,11},{10,... | collective-permute-start | bytes 2506760 | tf_op jit(solution)/shard_map/ppermute | solution.py:232
  108.3 22.8 %collective-permute-start.7 = (bf16[320,256]{1,0:T(8,128)(2,1)S(1)}, bf16[320,256]{1,0:T(8,128)(2,1)S(1)}, u32[]{:S(2)}, u32[]{:S(2)}) collective-permute-start(bf16[320,256]{1,0:T(8,128)(2,1)S(1)} %pad_maximum_fusion.1.refs_0_), channel_id=1, source_target_pairs={{0,4},{1,5},{2,6},{3,7},{4,8},{5,9},{6,10},{7,11},{8,12},{9,13},{1... | collective-permute-start | bytes 491528 | tf_op jit(solution)/shard_map/ppermute | solution.py:231
  108.9 22.2 %collective-permute-start.8 = (bf16[320,256]{1,0:T(8,128)(2,1)S(1)}, bf16[320,256]{1,0:T(8,128)(2,1)S(1)}, u32[]{:S(2)}, u32[]{:S(2)}) collective-permute-start(bf16[320,256]{1,0:T(8,128)(2,1)S(1)} %pad_maximum_fusion.1.refs_0_), channel_id=1, source_target_pairs={{0,2},{1,3},{2,0},{3,1},{4,6},{5,7},{6,4},{7,5},{8,10},{9,11},{10,... | collective-permute-start | bytes 491528 | tf_op jit(solution)/shard_map/ppermute | solution.py:232
  137.1 12.4 %collective-permute-start.16 = (bf16[320,256]{1,0:T(8,128)(2,1)S(1)}, bf16[320,256]{1,0:T(8,128)(2,1)S(1)}, u32[]{:S(2)}, u32[]{:S(2)}) collective-permute-start(bf16[320,256]{1,0:T(8,128)(2,1)S(1)} %collective-permute-done.11.refs_6_), channel_id=1, source_target_pairs={{0,2},{1,3},{2,0},{3,1},{4,6},{5,7},{6,4},{7,5},{8,10},{9,11},{10,... | collective-permute-start | bytes 491528 | tf_op jit(solution)/shard_map/ppermute | solution.py:232
  138.3 39.5 %collective-permute-start.38 = (bf16[544,768]{1,0:T(8,128)(2,1)S(1)}, bf16[544,768]{1,0:T(8,128)(2,1)S(1)}, u32[]{:S(2)}, u32[]{:S(2)}) collective-permute-start(bf16[544,768]{1,0:T(8,128)(2,1)S(1)} %collective-permute-done.36.refs_6_), channel_id=1, source_target_pairs={{0,4},{1,5},{2,6},{3,7},{4,8},{5,9},{6,10},{7,11},{8,12},{9,13},{1... | collective-permute-start | bytes 2506760 | tf_op jit(solution)/shard_map/ppermute | solution.py:231
  138.6 39.2 %collective-permute-start.39 = (bf16[544,768]{1,0:T(8,128)(2,1)S(1)}, bf16[544,768]{1,0:T(8,128)(2,1)S(1)}, u32[]{:S(2)}, u32[]{:S(2)}) collective-permute-start(bf16[544,768]{1,0:T(8,128)(2,1)S(1)} %collective-permute-done.36.refs_6_), channel_id=1, source_target_pairs={{0,2},{1,3},{2,0},{3,1},{4,6},{5,7},{6,4},{7,5},{8,10},{9,11},{10,... | collective-permute-start | bytes 2506760 | tf_op jit(solution)/shard_map/ppermute | solution.py:232
  138.9 10.6 %collective-permute-start.9 = (bf16[320,256]{1,0:T(8,128)(2,1)S(1)}, bf16[320,256]{1,0:T(8,128)(2,1)S(1)}, u32[]{:S(2)}, u32[]{:S(2)}) collective-permute-start(bf16[320,256]{1,0:T(8,128)(2,1)S(1)} %collective-permute-done.7.refs_2_), channel_id=1, source_target_pairs={{0,1},{1,0},{2,3},{3,2},{4,5},{5,4},{6,7},{7,6},{8,9},{9,8},{10,11... | collective-permute-start | bytes 491528 | tf_op jit(solution)/shard_map/ppermute | solution.py:227
  149.5 13.9 %collective-permute-start.14 = (bf16[320,256]{1,0:T(8,128)(2,1)S(1)}, bf16[320,256]{1,0:T(8,128)(2,1)S(1)}, u32[]{:S(2)}, u32[]{:S(2)}) collective-permute-start(bf16[320,256]{1,0:T(8,128)(2,1)S(1)} %collective-permute-done.12.refs_8_), channel_id=1, source_target_pairs={{0,1},{1,0},{2,3},{3,2},{4,5},{5,4},{6,7},{7,6},{8,9},{9,8},{10,11... | collective-permute-start | bytes 491528 | tf_op jit(solution)/shard_map/ppermute | solution.py:227
  151.7 11.7 %collective-permute-start.21 = (bf16[160,256]{1,0:T(8,128)(2,1)S(1)}, bf16[160,256]{1,0:T(8,128)(2,1)S(1)}, u32[]{:S(2)}, u32[]{:S(2)}) collective-permute-start(bf16[160,256]{1,0:T(8,128)(2,1)S(1)} %slice.127), channel_id=1, source_target_pairs={{0,4},{1,5},{2,6},{3,7},{4,8},{5,9},{6,10},{7,11},{8,12},{9,13},{1... | collective-permute-start | bytes 245768 | tf_op jit(solution)/shard_map/ppermute | solution.py:239
  166.4 22.6 %collective-permute-start.57 = (bf16[544,768]{1,0:T(8,128)(2,1)}, bf16[544,768]{1,0:T(8,128)(2,1)}, u32[]{:S(2)}, u32[]{:S(2)}) collective-permute-start(bf16[544,768]{1,0:T(8,128)(2,1)} %project.3.refs_0_), channel_id=1, source_target_pairs={{0,1},{1,0},{2,3},{3,2},{4,5},{5,4},{6,7},{7,6},{8,9},{9,8},{10,11... | collective-permute-start | bytes 2506760 | tf_op jit(solution)/shard_map/ppermute | solution.py:227
  166.7 23.2 %collective-permute-start.58 = (bf16[544,768]{1,0:T(8,128)(2,1)}, bf16[544,768]{1,0:T(8,128)(2,1)}, u32[]{:S(2)}, u32[]{:S(2)}) collective-permute-start(bf16[544,768]{1,0:T(8,128)(2,1)} %collective-permute-done.34.refs_2_), channel_id=1, source_target_pairs={{0,1},{1,0},{2,3},{3,2},{4,5},{5,4},{6,7},{7,6},{8,9},{9,8},{10,11... | collective-permute-start | bytes 2506760 | tf_op jit(solution)/shard_map/ppermute | solution.py:227
  179.2 13.2 %collective-permute-start.59 = (bf16[544,768]{1,0:T(8,128)(2,1)}, bf16[544,768]{1,0:T(8,128)(2,1)}, u32[]{:S(2)}, u32[]{:S(2)}) collective-permute-start(bf16[544,768]{1,0:T(8,128)(2,1)} %collective-permute-done.35.refs_4_), channel_id=1, source_target_pairs={{0,1},{1,0},{2,3},{3,2},{4,5},{5,4},{6,7},{7,6},{8,9},{9,8},{10,11... | collective-permute-start | bytes 2506760 | tf_op jit(solution)/shard_map/ppermute | solution.py:227
  187.7 12.6 %collective-permute-start.60 = (bf16[544,768]{1,0:T(8,128)(2,1)}, bf16[544,768]{1,0:T(8,128)(2,1)}, u32[]{:S(2)}, u32[]{:S(2)}) collective-permute-start(bf16[544,768]{1,0:T(8,128)(2,1)} %copy-done.3), channel_id=1, source_target_pairs={{0,1},{1,0},{2,3},{3,2},{4,5},{5,4},{6,7},{7,6},{8,9},{9,8},{10,11... | collective-permute-start | bytes 2506760 | tf_op jit(solution)/shard_map/ppermute | solution.py:227
  188.7 13.2 %collective-permute-start.61 = (bf16[544,768]{1,0:T(8,128)(2,1)}, bf16[544,768]{1,0:T(8,128)(2,1)}, u32[]{:S(2)}, u32[]{:S(2)}) collective-permute-start(bf16[544,768]{1,0:T(8,128)(2,1)} %copy-done.5), channel_id=1, source_target_pairs={{0,1},{1,0},{2,3},{3,2},{4,5},{5,4},{6,7},{7,6},{8,9},{9,8},{10,11... | collective-permute-start | bytes 2506760 | tf_op jit(solution)/shard_map/ppermute | solution.py:227
  189.9 10.2 %collective-permute-start.46 = (bf16[544,256]{1,0:T(8,128)(2,1)S(1)}, bf16[544,256]{1,0:T(8,128)(2,1)}, u32[]{:S(2)}, u32[]{:S(2)}) collective-permute-start(bf16[544,256]{1,0:T(8,128)(2,1)S(1)} %collective-permute-done.41.refs_2_), channel_id=1, source_target_pairs={{0,2},{1,3},{2,0},{3,1},{4,6},{5,7},{6,4},{7,5},{8,10},{9,11},{10,... | collective-permute-start | bytes 835592 | tf_op jit(solution)/shard_map/ppermute | solution.py:232
  198.8 10.1 %collective-permute-start.64 = (bf16[272,768]{1,0:T(8,128)(2,1)}, bf16[272,768]{1,0:T(8,128)(2,1)S(1)}, u32[]{:S(2)}, u32[]{:S(2)}) collective-permute-start(bf16[272,768]{1,0:T(8,128)(2,1)} %slice.134), channel_id=1, source_target_pairs={{0,2},{1,3},{2,0},{3,1},{4,6},{5,7},{6,4},{7,5},{8,10},{9,11},{10,... | collective-permute-start | bytes 1253384 | tf_op jit(solution)/shard_map/ppermute | solution.py:238
  200.0 11.6 %collective-permute-start.66 = (bf16[272,768]{1,0:T(8,128)(2,1)}, bf16[272,768]{1,0:T(8,128)(2,1)S(1)}, u32[]{:S(2)}, u32[]{:S(2)}) collective-permute-start(bf16[272,768]{1,0:T(8,128)(2,1)} %slice.135), channel_id=1, source_target_pairs={{0,4},{1,5},{2,6},{3,7},{4,8},{5,9},{6,10},{7,11},{8,12},{9,13},{1... | collective-permute-start | bytes 1253384 | tf_op jit(solution)/shard_map/ppermute | solution.py:239
  200.3 16.0 %collective-permute-start.43 = (bf16[544,256]{1,0:T(8,128)(2,1)S(1)}, bf16[544,256]{1,0:T(8,128)(2,1)}, u32[]{:S(2)}, u32[]{:S(2)}) collective-permute-start(bf16[544,256]{1,0:T(8,128)(2,1)S(1)} %collective-permute-done.41.refs_2_), channel_id=1, source_target_pairs={{0,1},{1,0},{2,3},{3,2},{4,5},{5,4},{6,7},{7,6},{8,9},{9,8},{10,11... | collective-permute-start | bytes 835592 | tf_op jit(solution)/shard_map/ppermute | solution.py:227
  202.0 14.5 %collective-permute-start.44 = (bf16[544,256]{1,0:T(8,128)(2,1)}, bf16[544,256]{1,0:T(8,128)(2,1)}, u32[]{:S(2)}, u32[]{:S(2)}) collective-permute-start(bf16[544,256]{1,0:T(8,128)(2,1)} %collective-permute-done.42.refs_4_), channel_id=1, source_target_pairs={{0,1},{1,0},{2,3},{3,2},{4,5},{5,4},{6,7},{7,6},{8,9},{9,8},{10,11... | collective-permute-start | bytes 835592 | tf_op jit(solution)/shard_map/ppermute | solution.py:227
  202.8 14.8 %collective-permute-start.49 = (bf16[544,256]{1,0:T(8,128)(2,1)}, bf16[544,256]{1,0:T(8,128)(2,1)S(1)}, u32[]{:S(2)}, u32[]{:S(2)}) collective-permute-start(bf16[544,256]{1,0:T(8,128)(2,1)} %collective-permute-done.45.refs_6_), channel_id=1, source_target_pairs={{0,4},{1,5},{2,6},{3,7},{4,8},{5,9},{6,10},{7,11},{8,12},{9,13},{1... | collective-permute-start | bytes 835592 | tf_op jit(solution)/shard_map/ppermute | solution.py:231
  208.9 19.8 %collective-permute-start.62 = (bf16[544,768]{1,0:T(8,128)(2,1)S(1)}, bf16[544,768]{1,0:T(8,128)(2,1)}, u32[]{:S(2)}, u32[]{:S(2)}) collective-permute-start(bf16[544,768]{1,0:T(8,128)(2,1)S(1)} %collective-permute-done.38.refs_10_), channel_id=1, source_target_pairs={{0,1},{1,0},{2,3},{3,2},{4,5},{5,4},{6,7},{7,6},{8,9},{9,8},{10,11... | collective-permute-start | bytes 2506760 | tf_op jit(solution)/shard_map/ppermute | solution.py:227
  211.6 17.4 %collective-permute-start.63 = (bf16[544,768]{1,0:T(8,128)(2,1)S(1)}, bf16[544,768]{1,0:T(8,128)(2,1)}, u32[]{:S(2)}, u32[]{:S(2)}) collective-permute-start(bf16[544,768]{1,0:T(8,128)(2,1)S(1)} %collective-permute-done.39.refs_12_), channel_id=1, source_target_pairs={{0,1},{1,0},{2,3},{3,2},{4,5},{5,4},{6,7},{7,6},{8,9},{9,8},{10,11... | collective-permute-start | bytes 2506760 | tf_op jit(solution)/shard_map/ppermute | solution.py:227
  216.4 11.9 %collective-permute-start.65 = (bf16[272,768]{1,0:T(8,128)(2,1)S(1)}, bf16[272,768]{1,0:T(8,128)(2,1)}, u32[]{:S(2)}, u32[]{:S(2)}) collective-permute-start(bf16[272,768]{1,0:T(8,128)(2,1)S(1)} %collective-permute-done.64.refs_14_), channel_id=1, source_target_pairs={{0,1},{1,0},{2,3},{3,2},{4,5},{5,4},{6,7},{7,6},{8,9},{9,8},{10,11... | collective-permute-start | bytes 1253384 | tf_op jit(solution)/shard_map/ppermute | solution.py:227
  216.5 12.1 %collective-permute-start.67 = (bf16[272,768]{1,0:T(8,128)(2,1)S(1)}, bf16[272,768]{1,0:T(8,128)(2,1)}, u32[]{:S(2)}, u32[]{:S(2)}) collective-permute-start(bf16[272,768]{1,0:T(8,128)(2,1)S(1)} %collective-permute-done.66.refs_16_), channel_id=1, source_target_pairs={{0,1},{1,0},{2,3},{3,2},{4,5},{5,4},{6,7},{7,6},{8,9},{9,8},{10,11... | collective-permute-start | bytes 1253384 | tf_op jit(solution)/shard_map/ppermute | solution.py:227
  228.7 43.6 %collective-permute-start.48 = (bf16[544,256]{1,0:T(8,128)(2,1)}, bf16[544,256]{1,0:T(8,128)(2,1)S(1)}, u32[]{:S(2)}, u32[]{:S(2)}) collective-permute-start(bf16[544,256]{1,0:T(8,128)(2,1)} %collective-permute-done.46.refs_8_), channel_id=1, source_target_pairs={{0,1},{1,0},{2,3},{3,2},{4,5},{5,4},{6,7},{7,6},{8,9},{9,8},{10,11... | collective-permute-start | bytes 835592 | tf_op jit(solution)/shard_map/ppermute | solution.py:227
  229.0 43.3 %collective-permute-start.51 = (bf16[544,256]{1,0:T(8,128)(2,1)S(1)}, bf16[544,256]{1,0:T(8,128)(2,1)S(1)}, u32[]{:S(2)}, u32[]{:S(2)}) collective-permute-start(bf16[544,256]{1,0:T(8,128)(2,1)S(1)} %collective-permute-done.49.refs_10_), channel_id=1, source_target_pairs={{0,1},{1,0},{2,3},{3,2},{4,5},{5,4},{6,7},{7,6},{8,9},{9,8},{10,11... | collective-permute-start | bytes 835592 | tf_op jit(solution)/shard_map/ppermute | solution.py:227
  229.3 43.1 %collective-permute-start.52 = (bf16[544,256]{1,0:T(8,128)(2,1)S(1)}, bf16[544,256]{1,0:T(8,128)(2,1)S(1)}, u32[]{:S(2)}, u32[]{:S(2)}) collective-permute-start(bf16[544,256]{1,0:T(8,128)(2,1)S(1)} %collective-permute-done.50.refs_12_), channel_id=1, source_target_pairs={{0,1},{1,0},{2,3},{3,2},{4,5},{5,4},{6,7},{7,6},{8,9},{9,8},{10,11... | collective-permute-start | bytes 835592 | tf_op jit(solution)/shard_map/ppermute | solution.py:227
  233.8 38.5 %collective-permute-start.54 = (bf16[272,256]{1,0:T(8,128)(2,1)S(1)}, bf16[272,256]{1,0:T(8,128)(2,1)S(1)}, u32[]{:S(2)}, u32[]{:S(2)}) collective-permute-start(bf16[272,256]{1,0:T(8,128)(2,1)S(1)} %collective-permute-done.53.refs_14_), channel_id=1, source_target_pairs={{0,1},{1,0},{2,3},{3,2},{4,5},{5,4},{6,7},{7,6},{8,9},{9,8},{10,11... | collective-permute-start | bytes 417800 | tf_op jit(solution)/shard_map/ppermute | solution.py:227
  235.7 36.7 %collective-permute-start.56 = (bf16[272,256]{1,0:T(8,128)(2,1)}, bf16[272,256]{1,0:T(8,128)(2,1)S(1)}, u32[]{:S(2)}, u32[]{:S(2)}) collective-permute-start(bf16[272,256]{1,0:T(8,128)(2,1)} %collective-permute-done.55.refs_16_), channel_id=1, source_target_pairs={{0,1},{1,0},{2,3},{3,2},{4,5},{5,4},{6,7},{7,6},{8,9},{9,8},{10,11... | collective-permute-start | bytes 417800 | tf_op jit(solution)/shard_map/ppermute | solution.py:227
  (52 other events, 862.1 us)

commit v3 on v2

--- a/solution.py
+++ b/solution.py
@@ -15,6 +15,7 @@
 HEAD_GROUPS = QUERY_HEADS // KEY_VALUE_HEADS
 CHUNKS = ((0, 3), (3, 1))
 PLANE = 4
+PLANES = 4
 GATHER_LIMIT = 40 * 2**20
 MASKED = -1e30
 VMEM = pl.BlockSpec(memory_space=pltpu.VMEM)
@@ -120,58 +121,103 @@
             ).astype(jnp.bfloat16)
 
 
-def fetch(pieces, refs, place, done):
-    copies = []
-    for at, ((source, first), ref) in enumerate(zip(pieces, refs)):
+def add_products(chips, owners_ref, hidden_ref, refs, columns, matrix, done):
+    shard = matrix.shape[1] // 2
+    copies, at, taken = [], 0, 0
+    for place, chip in enumerate(chips):
+        first = pl.multiple_of(lax.div(owners_ref[chip[0][0]], 2) * (2 * shard), HEAD_SIZE)
         copies.append(
-            pltpu.make_async_copy(ref, place(source, first, ref.shape[0]), done.at[at])
+            (hidden_ref.at[:, pl.ds(first, 2 * shard)], columns.at[place])
         )
-        copies[-1].start()
-    return copies
-
-
-def project_kernel(
-    heads, pieces, owners_ref, hidden_ref, bias_ref, cosine_ref, sine_ref, bucket_ref, *refs
-):
-    parts, out_ref, matrix, done = refs[: len(pieces)], *refs[len(pieces) :]
-    depth = matrix.shape[0] // owners_ref.shape[0]
-    copies = fetch(
-        pieces,
-        parts,
-        lambda source, first, rows: matrix.at[
-            pl.ds(pl.multiple_of(owners_ref[source] * depth + first, 16), rows)
-        ],
-        done,
-    )
-    places = one_hot_rows(out_ref.shape[0], bucket_ref[...])
+        for source, row in chip:
+            core = lax.rem(owners_ref[source], 2)
+            rows = pl.ds(pl.multiple_of(core * shard + row, 16), refs[taken].shape[0])
+            copies.append((refs[taken], matrix.at[place, rows]))
+            taken += 1
+    copies = [pltpu.make_async_copy(*pair, done.at[at]) for at, pair in enumerate(copies)]
+    for copy in copies:
+        copy.start()
+
+    def product(span):
+        total = contract(columns[0], matrix[0, :, span], 1, 0)
+        for place in range(1, len(chips)):
+            total = total + contract(columns[place], matrix[place, :, span], 1, 0)
+        return total
+
+    return copies, product
+
+
+def part_kernel(chips, more, owners_ref, hidden_ref, *refs):
+    count = sum(len(chip) for chip in chips)
+    parts, refs = refs[:count], refs[count:]
+    if more:
+        total_ref, refs = refs[0], refs[1:]
+    out_ref, columns, matrix, done = refs
+    copies, product = add_products(chips, owners_ref, hidden_ref, parts, columns, matrix, done)
     for copy in copies:
         copy.wait()
-    wide = heads * HEAD_SIZE
-    for part in range(2):
-        span = slice(part * wide, (part + 1) * wide)
-        rows = contract(hidden_ref[...], matrix[:, span], 1, 0) + bias_ref[:, span]
-        rows = rows.astype(jnp.bfloat16)
-        for head in range(heads):
-            one = rows[:, head * HEAD_SIZE : (head + 1) * HEAD_SIZE]
-            if part == 0:
-                one = turn(one.astype(jnp.float32), cosine_ref[...], sine_ref[...])
-            at = part * wide + head * HEAD_SIZE
-            out_ref[:, at : at + HEAD_SIZE] = contract(places, one, 1, 0).astype(jnp.bfloat16)
+    for first in range(0, out_ref.shape[1], 2 * HEAD_SIZE):
+        span = slice(first, first + 2 * HEAD_SIZE)
+        if more:
+            out_ref[:, span] = total_ref[:, span] + product(span)
+        else:
+            out_ref[:, span] = product(span)
+
+
+def finish_kernel(
+    chips, owners_ref, hidden_ref, bias_ref, cosine_ref, sine_ref, bucket_ref, *refs
+):
+    count = sum(len(chip) for chip in chips)
+    parts, total_ref = refs[:count], refs[count]
+    outs, (columns, matrix, done) = refs[count + 1 : -3], refs[-3:]
+    copies, product = add_products(chips, owners_ref, hidden_ref, parts, columns, matrix, done)
+    places = one_hot_rows(outs[0].shape[0], bucket_ref[...])
+    for copy in copies:
+        copy.wait()
+    wide = KEY_VALUE_HEADS * HEAD_SIZE
+    for first in range(0, 2 * wide, 2 * HEAD_SIZE):
+        span = slice(first, first + 2 * HEAD_SIZE)
+        rows = (total_ref[:, span] + product(span) + bias_ref[:, span]).astype(jnp.bfloat16)
+        if first < wide:
+            cosine, sine = cosine_ref[...], sine_ref[...]
+            halves = [
+                turn(rows[:, at : at + HEAD_SIZE].astype(jnp.float32), cosine, sine)
+                for at in (0, HEAD_SIZE)
+            ]
+            rows = jnp.concatenate(halves, axis=1)
+        rows = contract(places, rows, 1, 0).astype(jnp.bfloat16)
+        for half in range(2):
+            head = first % wide // HEAD_SIZE + half
+            for (first_head, heads), out_ref in zip(CHUNKS, outs):
+                if first_head <= head < first_head + heads:
+                    at = (head - first_head + first // wide * heads) * HEAD_SIZE
+                    out_ref[:, at : at + HEAD_SIZE] = rows[
+                        :, half * HEAD_SIZE : (half + 1) * HEAD_SIZE
+                    ]
 
 
 def attend_kernel(
-    chunk, pieces, spare, window, stride, queries_ref, bounds_ref, routes_ref, seat_ref, *refs
+    head, heads, pieces, spare, window, stride, queries_ref, bounds_ref, routes_ref, seat_ref, *refs
 ):
-    first_head, heads = chunk
+    first_head, place = head
     ranks = routes_ref.shape[0]
     parts, out_ref, blocks, mixed_ref, result_ref, done = refs[: len(pieces)], *refs[-5:]
-    copies = fetch(
-        pieces, parts, lambda source, first, rows: blocks.at[source, pl.ds(first, rows)], done
-    )
+    copies = []
+    for at, ((source, first), ref) in enumerate(zip(pieces, parts)):
+        for part in range(2):
+            lanes = pl.ds((part * heads + place) * HEAD_SIZE, HEAD_SIZE)
+            copies.append(
+                pltpu.make_async_copy(
+                    ref.at[:, lanes],
+                    blocks.at[part, source, pl.ds(first, ref.shape[0])],
+                    done.at[2 * at + part],
+                )
+            )
+            copies[-1].start()
     for copy in copies:
         copy.wait()
-    wide = heads * HEAD_SIZE
     scale = math.log2(math.e) / math.sqrt(HEAD_SIZE)
+    turns = [slice(at * HEAD_SIZE, (at + 1) * HEAD_SIZE) for at in range(HEAD_GROUPS)]
 
     def one_group(group, carry):
         seats = pl.ds(pl.multiple_of(group * stride, 16), stride)
@@ -180,68 +226,54 @@
         visible = (routes <= bounds_ref[seats, 0:1]) & (routes >= bounds_ref[seats, 1:2])
         veil = jnp.where(visible, 0.0, MASKED)
         veil = jnp.concatenate([veil] * HEAD_GROUPS, axis=0)
-        for head in range(heads):
-            span = slice(head * HEAD_SIZE, (head + 1) * HEAD_SIZE)
-            value_span = slice(wide + head * HEAD_SIZE, wide + (head + 1) * HEAD_SIZE)
-            turns = [
-                slice(at * HEAD_SIZE, (at + 1) * HEAD_SIZE)
-                for at in range(head * HEAD_GROUPS, (head + 1) * HEAD_GROUPS)
-            ]
-            query = jnp.concatenate([queries_ref[seats, one] for one in turns], axis=0)
-            keys = jnp.concatenate([blocks[j, keys_at, span] for j in range(ranks)], axis=0)
-            values = jnp.concatenate(
-                [blocks[j, keys_at, value_span] for j in range(ranks)], axis=0
-            )
-            scores = contract(query, keys, 1, 1) * scale + veil
-            weights = jnp.exp2(scores - jnp.max(scores, axis=1, keepdims=True))
-            totals = jnp.sum(weights, axis=1, keepdims=True)
-            mixed = contract(weights.astype(jnp.bfloat16), values, 1, 0) / totals
-            mixed = mixed.astype(jnp.bfloat16)
-            for place, one in enumerate(turns):
-                mixed_ref[seats, one] = mixed[place * stride : (place + 1) * stride]
+        query = jnp.concatenate([queries_ref[seats, one] for one in turns], axis=0)
+        keys = jnp.concatenate([blocks[0, j, keys_at] for j in range(ranks)], axis=0)
+        values = jnp.concatenate([blocks[1, j, keys_at] for j in range(ranks)], axis=0)
+        scores = contract(query, keys, 1, 1) * scale + veil
+        weights = jnp.exp2(scores - jnp.max(scores, axis=1, keepdims=True))
+        totals = jnp.sum(weights, axis=1, keepdims=True)
+        mixed = contract(weights.astype(jnp.bfloat16), values, 1, 0) / totals
+        mixed = mixed.astype(jnp.bfloat16)
+        for at, one in enumerate(turns):
+            mixed_ref[seats, one] = mixed[at * stride : (at + 1) * stride]
         return carry
 
     lax.fori_loop(0, ranks, one_group, 0)
     seats = one_hot_rows(mixed_ref.shape[0], seat_ref[...])
-    for head in range(result_ref.shape[1] // HEAD_SIZE):
-        span = slice(head * HEAD_SIZE, (head + 1) * HEAD_SIZE)
-        result_ref[:, span] = contract(seats, mixed_ref[:, span], 0, 0).astype(jnp.bfloat16)
-    columns = pl.ds(first_head * HEAD_GROUPS * HEAD_SIZE, result_ref.shape[1])
-    leave = pltpu.make_async_copy(result_ref, out_ref.at[:, columns], done.at[len(pieces)])
+    result_ref[...] = contract(seats, mixed_ref[...], 0, 0).astype(jnp.bfloat16)
+    lanes = pl.ds((first_head + place) * HEAD_GROUPS * HEAD_SIZE, HEAD_GROUPS * HEAD_SIZE)
+    leave = pltpu.make_async_copy(result_ref, out_ref.at[:, lanes], done.at[2 * len(pieces)])
     leave.start()
     leave.wait()
 
 
-def spread(block, ranks, after=None):
+def spread(block, ranks, held):
     ring = [(rank, (rank + PLANE) % ranks) for rank in range(ranks)]
     across = [(rank, rank ^ 2) for rank in range(ranks)]
     beside = [(rank, rank ^ 1) for rank in range(ranks)]
     steps = ranks // PLANE
     half = block.shape[0] // 32 * 16
-    if after is not None:
-        block, after = lax.optimization_barrier((block, after))
-    pieces, arrays = [], []
 
     def keep(source, first, array):
-        pieces.extend([(source, first), (source + 2 * steps, first)])
-        arrays.extend([array, lax.ppermute(array, "dp", beside)])
+        held.setdefault(source, []).append((first, array))
+        held.setdefault(source + 2 * steps, []).append((first, lax.ppermute(array, "dp", beside)))
 
     lane, other = block, None
     for step in range(steps - 1):
-        lane_next = lax.ppermute(lane, "dp", ring)
-        other_next = lax.ppermute(lane, "dp", across)
+        following = lax.ppermute(lane, "dp", ring), lax.ppermute(lane, "dp", across)
         keep(step, 0, lane)
         if step:
             keep(steps + step - 1, 0, other)
-        lane, other = lax.optimization_barrier((lane_next, other_next))
-    mark = other
+        extra = yield
+        lane, other, extra = lax.optimization_barrier((*following, extra))
+        yield extra
     over = lax.ppermute(lane[:half], "dp", across)
-    round_ = lax.ppermute(other[half:], "dp", ring)
+    around = lax.ppermute(other[half:], "dp", ring)
     keep(steps - 1, 0, lane)
     keep(2 * steps - 2, 0, other)
     keep(2 * steps - 1, 0, over)
-    keep(2 * steps - 1, half, round_)
-    return pieces, arrays, mark
+    keep(2 * steps - 1, half, around)
+    yield other
 
 
 def source_order(ranks):
@@ -279,12 +311,9 @@
         first, heads = chunk
         return array[..., first * HEAD_SIZE : (first + heads) * HEAD_SIZE]
 
-    matrices, mark = [], None
-    for chunk in CHUNKS:
-        block = jnp.concatenate([columns(key_matrix, chunk), columns(value_matrix, chunk)], axis=1)
-        *matrix, mark = spread(block, ranks, mark)
-        matrices.append(matrix)
-
+    matrices = {}
+    sending = spread(jnp.concatenate([key_matrix, value_matrix], axis=1), ranks, matrices)
+    next(sending)
     bucket, seat, sorted_route = pl.pallas_call(
         functools.partial(order_kernel, ranks, slots, spare, stride),
         out_shape=(
@@ -301,6 +330,8 @@
     plan = lax.all_to_all(
         jnp.broadcast_to(plan, (ranks, width + slots)), "dp", split_axis=0, concat_axis=0, tiled=True
     )
+    plan, bucket, seat = sending.send((plan, bucket, seat))
+    next(sending)
     all_positions = plan[:, width:].reshape(-1, HEAD_SIZE)
     owners = source_order(ranks)
     key_routes = plan[:, :width][owners]
@@ -334,62 +365,128 @@
         queries,
     )
 
-    pairs = []
-    for chunk, (pieces, arrays) in zip(CHUNKS, matrices):
-        bias = jnp.concatenate(
-            [columns(key_projection_bias, chunk), columns(value_projection_bias, chunk)]
-        )
-        wide = bias.shape[0]
-        pairs.append(
-            pl.pallas_call(
-                functools.partial(project_kernel, chunk[1], pieces),
-                out_shape=shape((width, wide), jnp.bfloat16),
-                in_specs=[SMEM] + [VMEM] * 5 + [HBM] * len(pieces),
-                out_specs=VMEM,
-                scratch_shapes=[
-                    pltpu.VMEM((depth, wide), jnp.bfloat16),
-                    pltpu.SemaphoreType.DMA((len(pieces),)),
-                ],
-                compiler_params=grant(36),
-                cost_estimate=cost(2 * rows * depth * wide, 2 * depth * (rows + wide)),
-                name="project",
-            )(
-                owners,
-                hidden,
-                bias.astype(jnp.float32).reshape(1, wide),
-                cosine,
-                sine,
-                bucket,
-                *arrays,
-            )
-        )
-
-    out, mark = None, None
-    for index, chunk in enumerate(CHUNKS):
-        query_heads = chunk[1] * HEAD_GROUPS
-        pieces, arrays, mark = spread(pairs[index], ranks, mark)
-        wide = pairs[index].shape[1]
+    turned, bounds, cosine, sine, key_routes = sending.send(
+        (turned, bounds, cosine, sine, key_routes)
+    )
+    next(sending)
+
+    shard, wide = key_matrix.shape[0], 2 * key_matrix.shape[1]
+    planes = ranks // PLANE
+
+    def chip_parts(sources):
+        chips, arrays = [], []
+        for source in sources:
+            chip = []
+            for one in (source, source + 2 * planes):
+                for first, array in matrices[one]:
+                    chip.append((one, first))
+                    arrays.append(array)
+            chips.append(tuple(chip))
+        return chips, arrays
+
+    def scratch(chips, arrays):
+        return [
+            pltpu.VMEM((len(chips), rows, 2 * shard), jnp.bfloat16),
+            pltpu.VMEM((len(chips), 2 * shard, wide), jnp.bfloat16),
+            pltpu.SemaphoreType.DMA((len(chips) + len(arrays),)),
+        ]
+
+    def product_cost(chips):
+        depth = 2 * shard * len(chips)
+        return cost(2 * rows * depth * wide, 2 * depth * (rows + wide) + 8 * rows * wide)
+
+    def add_part(total, sources):
+        chips, arrays = chip_parts(sources)
+        more = [] if total is None else [total]
+        return pl.pallas_call(
+            functools.partial(part_kernel, chips, bool(more)),
+            out_shape=shape((rows, wide), jnp.float32),
+            in_specs=[SMEM] + [HBM] * (1 + len(arrays)) + [VMEM] * len(more),
+            out_specs=VMEM,
+            scratch_shapes=scratch(chips, arrays),
+            compiler_params=grant(28),
+            cost_estimate=product_cost(chips),
+            name="add_part",
+        )(owners, hidden, *arrays, *more)
+
+    total = add_part(None, (0, 1, planes))
+    (total,) = sending.send((total,))
+    next(sending)
+    total = add_part(total, (2, planes + 1))
+    total = add_part(total, (3, planes + 2))
+    chips, arrays = chip_parts((planes + 3,))
+    bias = jnp.concatenate([key_projection_bias, value_projection_bias])
+    pairs = pl.pallas_call(
+        functools.partial(finish_kernel, chips),
+        out_shape=tuple(
+            shape((width, 2 * heads * HEAD_SIZE), jnp.bfloat16) for _, heads in CHUNKS
+        ),
+        in_specs=[SMEM, HBM] + [VMEM] * 4 + [HBM] * len(arrays) + [VMEM],
+        out_specs=(VMEM,) * len(CHUNKS),
+        scratch_shapes=scratch(chips, arrays),
+        compiler_params=grant(28),
+        cost_estimate=product_cost(chips),
+        name="finish",
+    )(
+        owners,
+        hidden,
+        bias.astype(jnp.float32).reshape(1, wide),
+        cosine,
+        sine,
+        bucket,
+        *arrays,
+        total,
+    )
+
+    def attend(out, chunk, held, place):
+        first_head, heads = CHUNKS[chunk]
+        pieces = [(source, first) for source in held for first, _ in held[source]]
+        arrays = [array for source in held for _, array in held[source]]
         taken = [] if out is None else [out]
-        fixed = [turned[index], bounds, key_routes, seat]
-        out = pl.pallas_call(
-            functools.partial(attend_kernel, chunk, pieces, spare, window, stride),
+        fixed = [turned[chunk], bounds, key_routes, seat]
+        span = HEAD_GROUPS * HEAD_SIZE
+        return pl.pallas_call(
+            functools.partial(
+                attend_kernel, (first_head, place), heads, pieces, spare, window, stride
+            ),
+            grid=(1,),
             out_shape=shape((rows, query_width), jnp.bfloat16),
-            in_specs=[VMEM] * len(fixed) + [HBM] * (len(pieces) + len(taken)),
+            in_specs=[pl.BlockSpec((ranks * stride, span), lambda i, p=place: (0, p))]
+            + [VMEM] * 3
+            + [HBM] * (len(pieces) + len(taken)),
             out_specs=HBM,
             scratch_shapes=[
-                pltpu.VMEM((ranks, width, wide), jnp.bfloat16),
-                pltpu.VMEM((ranks * stride, query_heads * HEAD_SIZE), jnp.bfloat16),
-                pltpu.VMEM((rows, query_heads * HEAD_SIZE), jnp.bfloat16),
-                pltpu.SemaphoreType.DMA((len(pieces) + 1,)),
+                pltpu.VMEM((2, ranks, width, HEAD_SIZE), jnp.bfloat16),
+                pltpu.VMEM((ranks * stride, span), jnp.bfloat16),
+                pltpu.VMEM((rows, span), jnp.bfloat16),
+                pltpu.SemaphoreType.DMA((2 * len(pieces) + 1,)),
             ],
             input_output_aliases={len(fixed) + len(pieces): 0} if taken else {},
-            compiler_params=grant(32),
+            compiler_params=grant(28),
             cost_estimate=cost(
-                16 * rows * stride * ranks * query_heads * HEAD_SIZE, 2 * ranks * width * wide
+                16 * rows * stride * ranks * span, 4 * ranks * width * HEAD_SIZE
             ),
             name="attend",
         )(*fixed, *arrays, *taken)
-    return out
+
+    early, late = {}, {}
+    sending = spread(pairs[0], ranks, early)
+    for _ in range(planes - 1):
+        next(sending)
+        sending.send(())
+    mark = next(sending)
+    last, _ = lax.optimization_barrier((pairs[1], mark))
+    sending = spread(last, ranks, late)
+    out = None
+    next(sending)
+    sending.send(())
+    for place in range(2):
+        next(sending)
+        out = attend(out, 0, early, place)
+        (out,) = sending.send((out,))
+    next(sending)
+    out = attend(out, 0, early, 2)
+    return attend(out, 1, late, 0)
 
 
 def apply_rotary(rows, slot_offset, heads):
@@ -525,7 +622,9 @@
     ranks = lax.axis_size("dp")
     rows = hidden.shape[0]
     gathered = ranks * ranks * (rows // ranks + 2) * 4 * key_matrix.shape[1]
-    if ranks % PLANE == 0 and rows % ranks == 0 and gathered <= GATHER_LIMIT:
+    chip_rows = 2 * key_matrix.shape[0]
+    fits = rows % ranks == 0 and chip_rows % HEAD_SIZE == 0 and gathered <= GATHER_LIMIT
+    if ranks == PLANES * PLANE and fits:
         return gather_plan(*args)
     return send_plan(*args)
 

time: 287 us -> 246 us (0.86)
  starting transfers between devices: 72 us -> 39.4 us
  local copies, waits for them, and re-layouts: 22.5 us -> 8.36 us
  waiting for transfers between devices: 116 us -> 121 us
    ppermute x64 -> x48, starting transfers between devices: 64.1 us -> 33.4 us  [the longest x27 21.7 us: keep(): lax.ppermute(array, 'dp', beside)]
    all_to_all x1, waiting for transfers between devices: 0.91 us -> 9.96 us  [gather_plan(): lax.all_to_all(jnp.broadcast_to(plan, (ranks, width + slots)), 'dp', spli...]
    unnamed x74 -> x29, local copies, waits for them, and re-layouts: 11 us -> 3.65 us
    ppermute x64 -> x48, waiting for transfers between devices: 97.9 us -> 93.4 us  [the longest x9 89.5 us: spread(): lax.ppermute(lane, 'dp', ring)]
    slice x10 -> x3, local copies, waits for them, and re-layouts: 4.19 us -> 0.06 us  [spread(): around = lax.ppermute(other[half:], 'dp', ring)]
    pallas_call x4 -> x8, Pallas kernels: 66.8 us -> 68 us  [the longest x4 50.7 us: attend(): pl.pallas_call(functools.partial(attend_kernel, (first_head, place), head...]
    ppermute x4 -> x3, waiting for transfers between devices: 17.5 us -> 17.4 us  [spread(): over = lax.ppermute(lane[:half], 'dp', across)]
  transfers between devices with their start and end apart: 69 -> 52, of which waited for: 19 -> 15; matrix products, arithmetic and copies ran while one was open for 4% -> 2% of each run, Pallas kernels for 17% -> 23%
where the time goes in v3:
time: 246 us; the launch traced here: 245 us
  waiting for transfers between devices  121 us (49%)
  Pallas kernels  74.7 us (30%)
  starting transfers between devices  39.4 us (16%)
  local copies, waits for them, and re-layouts  8.36 us (3%)
    ppermute x9, waiting for transfers between devices, spread(): lax.ppermute(lane, 'dp', ring)  89.5 us
    pallas_call x4, Pallas kernels, attend(): pl.pallas_call(functools.partial(attend_kernel, (first_head, place), head...  50.7 us
    ppermute x27, starting transfers between devices, keep(): lax.ppermute(array, 'dp', beside)  21.7 us
    ppermute x3, waiting for transfers between devices, spread(): over = lax.ppermute(lane[:half], 'dp', across)  17.4 us
    pallas_call x3, Pallas kernels, add_part(): pl.pallas_call(functools.partial(part_kernel, chips, bool(more)), out_sha...  12.7 us
    all_to_all x1, waiting for transfers between devices, gather_plan(): lax.all_to_all(jnp.broadcast_to(plan, (ranks, width + slots)), 'dp', spli...  9.96 us
    ppermute x9, starting transfers between devices, spread(): lax.ppermute(lane, 'dp', across)  8.44 us
    pallas_call x1, Pallas kernels, gather_plan(): pl.pallas_call(query_kernel, out_shape=tuple((shape((ranks * stride, head...  6.3 us
  transfers between devices with their start and end apart: 52, of which 15 were waited for; matrix products, arithmetic and copies ran while one was open for 2% of the time, Pallas kernels for 23%

profile of v3, /device:TPU:1, one launch (start us, length us, event | category | flops | bytes accessed | tf_op | source)
XLA Modules:
  0.0 245.1 jit_solution(7148183572406940802)
XLA Ops:
  0.0 1.0 constant_dynamic-update-slice_fusion.1
  1.0 1.0 constant_dynamic-update-slice_fusion.refs_0_
  2.0 2.2 collective-permute-start
  4.2 1.2 collective-permute-start.1
  5.4 1.2 collective-permute-start.6
  9.3 4.0 %all-to-all-start = ((s32[16,1,1568]{2,1,0:T(1,128)}), s32[16,1,1568]{2,1,0:T(1,128)S(1)}, u32[]{:S(2)}, u32[]{:S(2)}) async-start(s32[16,1,1568]{2,1,0:T(1,128)} %broadcast_in_dim.4), calls=%async_computation | async-start | bytes 212992 | tf_op jit(solution)/shard_map/all_to_all | solution.py:330
  13.3 0.8 copy.13.route_ref
  14.4 10.0 %all-to-all-done = s32[16,1,1568]{2,1,0:T(1,128)S(1)} async-done(((s32[16,1,1568]{2,1,0:T(1,128)}), s32[16,1,1568]{2,1,0:T(1,128)S(1)}, u32[]{:S(2)}, u32[]{:S(2)}) %all-to-all-start) | async-done | bytes 100384 | tf_op jit(solution)/shard_map/all_to_all | solution.py:330
  28.8 1.8 copy-done.1
  30.6 6.3 %turn_queries.1 = (bf16[768,1920]{1,0:T(8,128)(2,1)S(1)}, bf16[768,640]{1,0:T(8,128)(2,1)S(1)}, s32[768,128]{1,0:T(8,128)S(1)}, f32[512,128]{1,0:T(8,128)S(1)}, f32[512,128]{1,0:T(8,128)S(1)}) custom-call(s32[512,1]{1,0:T(8,128)S(1)} %copy.13.route_ref, s32[1,512]{1,0:T(1,128)S(1)} %get-tuple-element.50.seat_ref, s32[128,128]{1,0:T(8,128)S(1)} %reshape.149.positions_ref, ...), custom_call_target="tpu_custom_call" | custom-call | flops 4026531840 | bytes 5242880 | tf_op jit(solution)/shard_map/turn_queries/pallas_call | solution.py:344
  37.0 6.0 %collective-permute-done.2.refs_0_ = bf16[320,1024]{1,0:T(8,128)(2,1)} collective-permute-done((bf16[320,1024]{1,0:T(8,128)(2,1)S(1)}, bf16[320,1024]{1,0:T(8,128)(2,1)}, u32[]{:S(2)}, u32[]{:S(2)}) %collective-permute-start.2) | collective-permute-done | bytes 655392 | tf_op jit(solution)/shard_map/ppermute | solution.py:263
  43.4 1.2 collective-permute-start.15
  44.9 5.3 %add_part.3.refs_4_ = f32[512,1024]{1,0:T(8,128)S(1)} custom-call(s32[16]{0:T(128)S(1)} %pad_add_fusion.1.owners_ref, bf16[512,5120]{1,0:T(8,128)(2,1)S(1)} %bitcast.14, bf16[320,1024]{1,0:T(8,128)(2,1)S(1)} %constant_dynamic-update-slice_fusion.refs_0_, bf16[320,1024]{1,0:T(8,128)(2,1)} %collective-permute-done.6.refs_1_, ...), custom_call_target="tpu_custom_call" | custom-call | flops 2013265920 | bytes 10092544 | tf_op jit(solution)/shard_map/add_part/pallas_call | solution.py:401
  50.2 10.1 %collective-permute-done.4.refs_0_ = bf16[320,1024]{1,0:T(8,128)(2,1)S(1)} collective-permute-done((bf16[320,1024]{1,0:T(8,128)(2,1)}, bf16[320,1024]{1,0:T(8,128)(2,1)S(1)}, u32[]{:S(2)}, u32[]{:S(2)}) %collective-permute-start.4) | collective-permute-done | bytes 655392 | tf_op jit(solution)/shard_map/ppermute | solution.py:263
  60.3 1.9 collective-permute-start.13
  62.8 8.3 %collective-permute-done.9.refs_0_ = bf16[160,1024]{1,0:T(8,128)(2,1)S(1)} collective-permute-done((bf16[160,1024]{1,0:T(8,128)(2,1)S(1)}, bf16[160,1024]{1,0:T(8,128)(2,1)S(1)}, u32[]{:S(2)}, u32[]{:S(2)}) %collective-permute-start.9) | collective-permute-done | bytes 327712 | tf_op jit(solution)/shard_map/ppermute | solution.py:270
  71.0 1.4 collective-permute-start.11
  73.0 1.7 collective-permute-start.12
  74.6 3.9 %add_part.4.refs_4_ = f32[512,1024]{1,0:T(8,128)S(1)} custom-call(s32[16]{0:T(128)S(1)} %pad_add_fusion.1.owners_ref, bf16[512,5120]{1,0:T(8,128)(2,1)S(1)} %bitcast.14, bf16[320,1024]{1,0:T(8,128)(2,1)} %collective-permute-done.2.refs_0_, bf16[320,1024]{1,0:T(8,128)(2,1)S(1)} %collective-permute-done.15.refs_1_, ...), custom_call_target="tpu_custom_call" | custom-call | flops 1342177280 | bytes 8126464 | tf_op jit(solution)/shard_map/add_part/pallas_call | solution.py:401
  78.6 3.4 %add_part.5.refs_4_ = f32[512,1024]{1,0:T(8,128)S(1)} custom-call(s32[16]{0:T(128)S(1)} %pad_add_fusion.1.owners_ref, bf16[512,5120]{1,0:T(8,128)(2,1)S(1)} %bitcast.14, bf16[320,1024]{1,0:T(8,128)(2,1)S(1)} %collective-permute-done.4.refs_0_, bf16[320,1024]{1,0:T(8,128)(2,1)S(1)} %collective-permute-done.13.refs_1_, ...), custom_call_target="tpu_custom_call" | custom-call | flops 1342177280 | bytes 8126464 | tf_op jit(solution)/shard_map/add_part/pallas_call | solution.py:401
  82.1 4.5 %finish.1 = (bf16[544,768]{1,0:T(8,128)(2,1)S(1)}, bf16[544,256]{1,0:T(8,128)(2,1)S(1)}) custom-call(s32[16]{0:T(128)S(1)} %pad_add_fusion.1.owners_ref, bf16[512,5120]{1,0:T(8,128)(2,1)S(1)} %bitcast.14, f32[1,1024]{1,0:T(1,128)S(1)} %maximum_convert_fusion.bias_ref, f32[512,128]{1,0:T(8,128)S(1)} %get-tuple-element.60.cosine_ref, ...), custom_call_target="tpu_custom_call" | custom-call | flops 671088640 | bytes 6160384 | tf_op jit(solution)/shard_map/finish/pallas_call | solution.py:419
  86.7 1.1 collective-permute-start.18
  87.8 20.9 %collective-permute-done.17.refs_2_ = bf16[544,768]{1,0:T(8,128)(2,1)S(1)} collective-permute-done((bf16[544,768]{1,0:T(8,128)(2,1)S(1)}, bf16[544,768]{1,0:T(8,128)(2,1)S(1)}, u32[]{:S(2)}, u32[]{:S(2)}) %collective-permute-start.17) | collective-permute-done | bytes 835616 | tf_op jit(solution)/shard_map/ppermute | solution.py:263
  108.7 1.0 collective-permute-start.20
  109.7 20.1 %collective-permute-done.19.refs_6_ = bf16[544,768]{1,0:T(8,128)(2,1)S(1)} collective-permute-done((bf16[544,768]{1,0:T(8,128)(2,1)S(1)}, bf16[544,768]{1,0:T(8,128)(2,1)S(1)}, u32[]{:S(2)}, u32[]{:S(2)}) %collective-permute-start.19) | collective-permute-done | bytes 835616 | tf_op jit(solution)/shard_map/ppermute | solution.py:263
  129.9 1.0 collective-permute-start.22
  130.9 2.0 collective-permute-start.30
  133.4 16.7 %collective-permute-done.21.refs_10_ = bf16[544,768]{1,0:T(8,128)(2,1)S(1)} collective-permute-done((bf16[544,768]{1,0:T(8,128)(2,1)S(1)}, bf16[544,768]{1,0:T(8,128)(2,1)S(1)}, u32[]{:S(2)}, u32[]{:S(2)}) %collective-permute-start.21) | collective-permute-done | bytes 835616 | tf_op jit(solution)/shard_map/ppermute | solution.py:263
  150.1 2.6 %collective-permute-start.33 = (bf16[544,768]{1,0:T(8,128)(2,1)S(1)}, bf16[544,768]{1,0:T(8,128)(2,1)S(1)}, u32[]{:S(2)}, u32[]{:S(2)}) collective-permute-start(bf16[544,768]{1,0:T(8,128)(2,1)S(1)} %collective-permute-done.19.refs_6_), channel_id=1, source_target_pairs={{0,1},{1,0},{2,3},{3,2},{4,5},{5,4},{6,7},{7,6},{8,9},{9,8},{10,11... | collective-permute-start | bytes 2506760 | tf_op jit(solution)/shard_map/ppermute | solution.py:259
  152.7 1.1 collective-permute-start.25
  154.8 8.0 %collective-permute-done.24.refs_2_ = bf16[544,256]{1,0:T(8,128)(2,1)S(1)} collective-permute-done((bf16[544,256]{1,0:T(8,128)(2,1)S(1)}, bf16[544,256]{1,0:T(8,128)(2,1)S(1)}, u32[]{:S(2)}, u32[]{:S(2)}) %collective-permute-start.24) | collective-permute-done | bytes 278560 | tf_op jit(solution)/shard_map/ppermute | solution.py:263
  162.7 1.2 collective-permute-start.35
  163.9 6.0 %collective-permute-done.37.refs_14_ = bf16[272,768]{1,0:T(8,128)(2,1)S(1)} collective-permute-done((bf16[272,768]{1,0:T(8,128)(2,1)S(1)}, bf16[272,768]{1,0:T(8,128)(2,1)S(1)}, u32[]{:S(2)}, u32[]{:S(2)}) %collective-permute-start.37) | collective-permute-done | bytes 417824 | tf_op jit(solution)/shard_map/ppermute | solution.py:270
  170.0 0.8 collective-permute-start.39
  170.8 0.9 collective-permute-done.38.refs_15_
  172.5 1.1 collective-permute-start.29
  173.9 12.7 %attend.4.refs_18_ = bf16[512,2560]{1,0:T(8,128)(2,1)} custom-call(bf16[768,1920]{1,0:T(8,128)(2,1)S(1)} %get-tuple-element.77.queries_ref, s32[768,128]{1,0:T(8,128)S(1)} %get-tuple-element.58.bounds_ref, s32[16,1,768]{2,1,0:T(1,128)S(1)} %constant_dynamic-update-slice_fusion.2.routes_ref, s32[1,512]{1,0:T(1,128)S(1)} %get-tuple-element.50.seat_ref, ...), custom_call_target="tpu_custom_call" | custom-call | flops 4026531840 | bytes 4456448 | tf_op jit(solution)/shard_map/attend/pallas_call | solution.py:448
  187.6 1.0 collective-permute-start.44
  188.6 7.7 %collective-permute-done.43.refs_10_ = bf16[544,256]{1,0:T(8,128)(2,1)S(1)} collective-permute-done((bf16[544,256]{1,0:T(8,128)(2,1)S(1)}, bf16[544,256]{1,0:T(8,128)(2,1)S(1)}, u32[]{:S(2)}, u32[]{:S(2)}) %collective-permute-start.43) | collective-permute-done | bytes 278560 | tf_op jit(solution)/shard_map/ppermute | solution.py:263
  196.3 1.2 collective-permute-start.41
  197.5 12.7 %attend.5.refs_18_ = bf16[512,2560]{1,0:T(8,128)(2,1)} custom-call(bf16[768,1920]{1,0:T(8,128)(2,1)S(1)} %get-tuple-element.77.queries_ref, s32[768,128]{1,0:T(8,128)S(1)} %get-tuple-element.58.bounds_ref, s32[16,1,768]{2,1,0:T(1,128)S(1)} %constant_dynamic-update-slice_fusion.2.routes_ref, ...), custom_call_target="tpu_custom_call", output_to_operand_aliasing={{}: (22, {})} | custom-call | flops 4026531840 | bytes 4456448 | tf_op jit(solution)/shard_map/attend/pallas_call | solution.py:448
  210.3 1.1 collective-permute-start.47
  212.5 3.1 %collective-permute-done.47.refs_14_ = bf16[272,256]{1,0:T(8,128)(2,1)S(1)} collective-permute-done((bf16[272,256]{1,0:T(8,128)(2,1)S(1)}, bf16[272,256]{1,0:T(8,128)(2,1)S(1)}, u32[]{:S(2)}, u32[]{:S(2)}) %collective-permute-start.47) | collective-permute-done | bytes 139296 | tf_op jit(solution)/shard_map/ppermute | solution.py:270
  215.6 0.8 collective-permute-start.49
  216.4 2.0 collective-permute-done.48.refs_15_
  218.4 1.1 collective-permute-start.50
  219.5 12.7 %attend.6.refs_18_ = bf16[512,2560]{1,0:T(8,128)(2,1)} custom-call(bf16[768,1920]{1,0:T(8,128)(2,1)S(1)} %get-tuple-element.77.queries_ref, s32[768,128]{1,0:T(8,128)S(1)} %get-tuple-element.58.bounds_ref, s32[16,1,768]{2,1,0:T(1,128)S(1)} %constant_dynamic-update-slice_fusion.2.routes_ref, ...), custom_call_target="tpu_custom_call", output_to_operand_aliasing={{}: (22, {})} | custom-call | flops 4026531840 | bytes 4456448 | tf_op jit(solution)/shard_map/attend/pallas_call | solution.py:448
  232.3 12.6 %attend.7 = bf16[512,2560]{1,0:T(8,128)(2,1)} custom-call(bf16[768,640]{1,0:T(8,128)(2,1)S(1)} %get-tuple-element.57.queries_ref, s32[768,128]{1,0:T(8,128)S(1)} %get-tuple-element.58.bounds_ref, s32[16,1,768]{2,1,0:T(1,128)S(1)} %constant_dynamic-update-slice_fusion.2.routes_ref, ...), custom_call_target="tpu_custom_call", output_to_operand_aliasing={{}: (22, {})} | custom-call | flops 4026531840 | bytes 4456448 | tf_op jit(solution)/shard_map/attend/pallas_call | solution.py:448
  (139 shorter events, 13.8 us)
Async XLA Ops:
  2.0 22.3 %collective-permute-start = (bf16[320,1024]{1,0:T(8,128)(2,1)S(1)}, bf16[320,1024]{1,0:T(8,128)(2,1)S(1)}, u32[]{:S(2)}, u32[]{:S(2)}) collective-permute-start(bf16[320,1024]{1,0:T(8,128)(2,1)S(1)} %constant_dynamic-update-slice_fusion.refs_0_), channel_id=1, source_target_pairs={{0,4},{1,5},{2,6},{3,7},{4,8},{5,9},{6,10},{7,11},{8,12},{9,13},{1... | collective-permute-start | bytes 1966088 | tf_op jit(solution)/shard_map/ppermute | solution.py:263
  4.2 20.1 %collective-permute-start.1 = (bf16[320,1024]{1,0:T(8,128)(2,1)S(1)}, bf16[320,1024]{1,0:T(8,128)(2,1)S(1)}, u32[]{:S(2)}, u32[]{:S(2)}) collective-permute-start(bf16[320,1024]{1,0:T(8,128)(2,1)S(1)} %constant_dynamic-update-slice_fusion.refs_0_), channel_id=1, source_target_pairs={{0,2},{1,3},{2,0},{3,1},{4,6},{5,7},{6,4},{7,5},{8,10},{9,11},{10,... | collective-permute-start | bytes 1966088 | tf_op jit(solution)/shard_map/ppermute | solution.py:263
  5.4 38.0 %collective-permute-start.6 = (bf16[320,1024]{1,0:T(8,128)(2,1)S(1)}, bf16[320,1024]{1,0:T(8,128)(2,1)}, u32[]{:S(2)}, u32[]{:S(2)}) collective-permute-start(bf16[320,1024]{1,0:T(8,128)(2,1)S(1)} %constant_dynamic-update-slice_fusion.refs_0_), channel_id=1, source_target_pairs={{0,1},{1,0},{2,3},{3,2},{4,5},{5,4},{6,7},{7,6},{8,9},{9,8},{10,11... | collective-permute-start | bytes 1966088 | tf_op jit(solution)/shard_map/ppermute | solution.py:259
  9.3 15.0 %all-to-all-start = ((s32[16,1,1568]{2,1,0:T(1,128)}), s32[16,1,1568]{2,1,0:T(1,128)S(1)}, u32[]{:S(2)}, u32[]{:S(2)}) async-start(s32[16,1,1568]{2,1,0:T(1,128)} %broadcast_in_dim.4), calls=%async_computation | async-start | bytes 212992 | tf_op jit(solution)/shard_map/all_to_all | solution.py:330
  24.5 20.3 %collective-permute-start.7 = (bf16[320,1024]{1,0:T(8,128)(2,1)S(1)}, bf16[320,1024]{1,0:T(8,128)(2,1)}, u32[]{:S(2)}, u32[]{:S(2)}) collective-permute-start(bf16[320,1024]{1,0:T(8,128)(2,1)S(1)} %collective-permute-done.refs_2_), channel_id=1, source_target_pairs={{0,1},{1,0},{2,3},{3,2},{4,5},{5,4},{6,7},{7,6},{8,9},{9,8},{10,11... | collective-permute-start | bytes 1966088 | tf_op jit(solution)/shard_map/ppermute | solution.py:259
  24.9 18.1 %collective-permute-start.2 = (bf16[320,1024]{1,0:T(8,128)(2,1)S(1)}, bf16[320,1024]{1,0:T(8,128)(2,1)}, u32[]{:S(2)}, u32[]{:S(2)}) collective-permute-start(bf16[320,1024]{1,0:T(8,128)(2,1)S(1)} %collective-permute-done.refs_2_), channel_id=1, source_target_pairs={{0,4},{1,5},{2,6},{3,7},{4,8},{5,9},{6,10},{7,11},{8,12},{9,13},{1... | collective-permute-start | bytes 1966088 | tf_op jit(solution)/shard_map/ppermute | solution.py:263
  25.5 17.5 %collective-permute-start.3 = (bf16[320,1024]{1,0:T(8,128)(2,1)S(1)}, bf16[320,1024]{1,0:T(8,128)(2,1)}, u32[]{:S(2)}, u32[]{:S(2)}) collective-permute-start(bf16[320,1024]{1,0:T(8,128)(2,1)S(1)} %collective-permute-done.refs_2_), channel_id=1, source_target_pairs={{0,2},{1,3},{2,0},{3,1},{4,6},{5,7},{6,4},{7,5},{8,10},{9,11},{10,... | collective-permute-start | bytes 1966088 | tf_op jit(solution)/shard_map/ppermute | solution.py:263
  25.9 18.9 %collective-permute-start.8 = (bf16[320,1024]{1,0:T(8,128)(2,1)S(1)}, bf16[320,1024]{1,0:T(8,128)(2,1)}, u32[]{:S(2)}, u32[]{:S(2)}) collective-permute-start(bf16[320,1024]{1,0:T(8,128)(2,1)S(1)} %collective-permute-done.1.refs_4_), channel_id=1, source_target_pairs={{0,1},{1,0},{2,3},{3,2},{4,5},{5,4},{6,7},{7,6},{8,9},{9,8},{10,11... | collective-permute-start | bytes 1966088 | tf_op jit(solution)/shard_map/ppermute | solution.py:259
  43.0 17.3 %collective-permute-start.4 = (bf16[320,1024]{1,0:T(8,128)(2,1)}, bf16[320,1024]{1,0:T(8,128)(2,1)S(1)}, u32[]{:S(2)}, u32[]{:S(2)}) collective-permute-start(bf16[320,1024]{1,0:T(8,128)(2,1)} %collective-permute-done.2.refs_0_), channel_id=1, source_target_pairs={{0,4},{1,5},{2,6},{3,7},{4,8},{5,9},{6,10},{7,11},{8,12},{9,13},{1... | collective-permute-start | bytes 1966088 | tf_op jit(solution)/shard_map/ppermute | solution.py:263
  43.0 17.3 %collective-permute-start.5 = (bf16[320,1024]{1,0:T(8,128)(2,1)}, bf16[320,1024]{1,0:T(8,128)(2,1)S(1)}, u32[]{:S(2)}, u32[]{:S(2)}) collective-permute-start(bf16[320,1024]{1,0:T(8,128)(2,1)} %collective-permute-done.2.refs_0_), channel_id=1, source_target_pairs={{0,2},{1,3},{2,0},{3,1},{4,6},{5,7},{6,4},{7,5},{8,10},{9,11},{10,... | collective-permute-start | bytes 1966088 | tf_op jit(solution)/shard_map/ppermute | solution.py:263
  43.4 19.3 %collective-permute-start.15 = (bf16[320,1024]{1,0:T(8,128)(2,1)}, bf16[320,1024]{1,0:T(8,128)(2,1)S(1)}, u32[]{:S(2)}, u32[]{:S(2)}) collective-permute-start(bf16[320,1024]{1,0:T(8,128)(2,1)} %collective-permute-done.2.refs_0_), channel_id=1, source_target_pairs={{0,1},{1,0},{2,3},{3,2},{4,5},{5,4},{6,7},{7,6},{8,9},{9,8},{10,11... | collective-permute-start | bytes 1966088 | tf_op jit(solution)/shard_map/ppermute | solution.py:259
  44.7 29.9 %collective-permute-start.16 = (bf16[320,1024]{1,0:T(8,128)(2,1)}, bf16[320,1024]{1,0:T(8,128)(2,1)S(1)}, u32[]{:S(2)}, u32[]{:S(2)}) collective-permute-start(bf16[320,1024]{1,0:T(8,128)(2,1)} %collective-permute-done.3.refs_2_), channel_id=1, source_target_pairs={{0,1},{1,0},{2,3},{3,2},{4,5},{5,4},{6,7},{7,6},{8,9},{9,8},{10,11... | collective-permute-start | bytes 1966088 | tf_op jit(solution)/shard_map/ppermute | solution.py:259
  60.3 18.3 %collective-permute-start.13 = (bf16[320,1024]{1,0:T(8,128)(2,1)S(1)}, bf16[320,1024]{1,0:T(8,128)(2,1)S(1)}, u32[]{:S(2)}, u32[]{:S(2)}) collective-permute-start(bf16[320,1024]{1,0:T(8,128)(2,1)S(1)} %collective-permute-done.4.refs_0_), channel_id=1, source_target_pairs={{0,1},{1,0},{2,3},{3,2},{4,5},{5,4},{6,7},{7,6},{8,9},{9,8},{10,11... | collective-permute-start | bytes 1966088 | tf_op jit(solution)/shard_map/ppermute | solution.py:259
  62.2 16.5 %collective-permute-start.14 = (bf16[320,1024]{1,0:T(8,128)(2,1)S(1)}, bf16[320,1024]{1,0:T(8,128)(2,1)S(1)}, u32[]{:S(2)}, u32[]{:S(2)}) collective-permute-start(bf16[320,1024]{1,0:T(8,128)(2,1)S(1)} %collective-permute-done.5.refs_2_), channel_id=1, source_target_pairs={{0,1},{1,0},{2,3},{3,2},{4,5},{5,4},{6,7},{7,6},{8,9},{9,8},{10,11... | collective-permute-start | bytes 1966088 | tf_op jit(solution)/shard_map/ppermute | solution.py:259
  62.2 8.8 %collective-permute-start.9 = (bf16[160,1024]{1,0:T(8,128)(2,1)S(1)}, bf16[160,1024]{1,0:T(8,128)(2,1)S(1)}, u32[]{:S(2)}, u32[]{:S(2)}) collective-permute-start(bf16[160,1024]{1,0:T(8,128)(2,1)S(1)} %slice.90), channel_id=1, source_target_pairs={{0,2},{1,3},{2,0},{3,1},{4,6},{5,7},{6,4},{7,5},{8,10},{9,11},{10,... | collective-permute-start | bytes 983048 | tf_op jit(solution)/shard_map/ppermute | solution.py:270
  62.7 10.2 %collective-permute-start.10 = (bf16[160,1024]{1,0:T(8,128)(2,1)S(1)}, bf16[160,1024]{1,0:T(8,128)(2,1)S(1)}, u32[]{:S(2)}, u32[]{:S(2)}) collective-permute-start(bf16[160,1024]{1,0:T(8,128)(2,1)S(1)} %slice.91), channel_id=1, source_target_pairs={{0,4},{1,5},{2,6},{3,7},{4,8},{5,9},{6,10},{7,11},{8,12},{9,13},{1... | collective-permute-start | bytes 983048 | tf_op jit(solution)/shard_map/ppermute | solution.py:271
  71.0 11.0 %collective-permute-start.11 = (bf16[160,1024]{1,0:T(8,128)(2,1)S(1)}, bf16[160,1024]{1,0:T(8,128)(2,1)S(1)}, u32[]{:S(2)}, u32[]{:S(2)}) collective-permute-start(bf16[160,1024]{1,0:T(8,128)(2,1)S(1)} %collective-permute-done.9.refs_0_), channel_id=1, source_target_pairs={{0,1},{1,0},{2,3},{3,2},{4,5},{5,4},{6,7},{7,6},{8,9},{9,8},{10,11... | collective-permute-start | bytes 983048 | tf_op jit(solution)/shard_map/ppermute | solution.py:259
  73.0 9.1 %collective-permute-start.12 = (bf16[160,1024]{1,0:T(8,128)(2,1)S(1)}, bf16[160,1024]{1,0:T(8,128)(2,1)S(1)}, u32[]{:S(2)}, u32[]{:S(2)}) collective-permute-start(bf16[160,1024]{1,0:T(8,128)(2,1)S(1)} %collective-permute-done.10.refs_1_), channel_id=1, source_target_pairs={{0,1},{1,0},{2,3},{3,2},{4,5},{5,4},{6,7},{7,6},{8,9},{9,8},{10,11... | collective-permute-start | bytes 983048 | tf_op jit(solution)/shard_map/ppermute | solution.py:259
  86.6 22.1 %collective-permute-start.17 = (bf16[544,768]{1,0:T(8,128)(2,1)S(1)}, bf16[544,768]{1,0:T(8,128)(2,1)S(1)}, u32[]{:S(2)}, u32[]{:S(2)}) collective-permute-start(bf16[544,768]{1,0:T(8,128)(2,1)S(1)} %get-tuple-element.70.refs_0_), channel_id=1, source_target_pairs={{0,4},{1,5},{2,6},{3,7},{4,8},{5,9},{6,10},{7,11},{8,12},{9,13},{1... | collective-permute-start | bytes 2506760 | tf_op jit(solution)/shard_map/ppermute | solution.py:263
  86.7 22.0 %collective-permute-start.18 = (bf16[544,768]{1,0:T(8,128)(2,1)S(1)}, bf16[544,768]{1,0:T(8,128)(2,1)S(1)}, u32[]{:S(2)}, u32[]{:S(2)}) collective-permute-start(bf16[544,768]{1,0:T(8,128)(2,1)S(1)} %get-tuple-element.70.refs_0_), channel_id=1, source_target_pairs={{0,2},{1,3},{2,0},{3,1},{4,6},{5,7},{6,4},{7,5},{8,10},{9,11},{10,... | collective-permute-start | bytes 2506760 | tf_op jit(solution)/shard_map/ppermute | solution.py:263
  108.7 21.1 %collective-permute-start.19 = (bf16[544,768]{1,0:T(8,128)(2,1)S(1)}, bf16[544,768]{1,0:T(8,128)(2,1)S(1)}, u32[]{:S(2)}, u32[]{:S(2)}) collective-permute-start(bf16[544,768]{1,0:T(8,128)(2,1)S(1)} %collective-permute-done.17.refs_2_), channel_id=1, source_target_pairs={{0,4},{1,5},{2,6},{3,7},{4,8},{5,9},{6,10},{7,11},{8,12},{9,13},{1... | collective-permute-start | bytes 2506760 | tf_op jit(solution)/shard_map/ppermute | solution.py:263
  108.7 21.1 %collective-permute-start.20 = (bf16[544,768]{1,0:T(8,128)(2,1)S(1)}, bf16[544,768]{1,0:T(8,128)(2,1)S(1)}, u32[]{:S(2)}, u32[]{:S(2)}) collective-permute-start(bf16[544,768]{1,0:T(8,128)(2,1)S(1)} %collective-permute-done.17.refs_2_), channel_id=1, source_target_pairs={{0,2},{1,3},{2,0},{3,1},{4,6},{5,7},{6,4},{7,5},{8,10},{9,11},{10,... | collective-permute-start | bytes 2506760 | tf_op jit(solution)/shard_map/ppermute | solution.py:263
  129.8 20.2 %collective-permute-start.21 = (bf16[544,768]{1,0:T(8,128)(2,1)S(1)}, bf16[544,768]{1,0:T(8,128)(2,1)S(1)}, u32[]{:S(2)}, u32[]{:S(2)}) collective-permute-start(bf16[544,768]{1,0:T(8,128)(2,1)S(1)} %collective-permute-done.19.refs_6_), channel_id=1, source_target_pairs={{0,4},{1,5},{2,6},{3,7},{4,8},{5,9},{6,10},{7,11},{8,12},{9,13},{1... | collective-permute-start | bytes 2506760 | tf_op jit(solution)/shard_map/ppermute | solution.py:263
  129.9 22.8 %collective-permute-start.22 = (bf16[544,768]{1,0:T(8,128)(2,1)S(1)}, bf16[544,768]{1,0:T(8,128)(2,1)S(1)}, u32[]{:S(2)}, u32[]{:S(2)}) collective-permute-start(bf16[544,768]{1,0:T(8,128)(2,1)S(1)} %collective-permute-done.19.refs_6_), channel_id=1, source_target_pairs={{0,2},{1,3},{2,0},{3,1},{4,6},{5,7},{6,4},{7,5},{8,10},{9,11},{10,... | collective-permute-start | bytes 2506760 | tf_op jit(solution)/shard_map/ppermute | solution.py:263
  130.9 21.8 %collective-permute-start.30 = (bf16[544,768]{1,0:T(8,128)(2,1)S(1)}, bf16[544,768]{1,0:T(8,128)(2,1)S(1)}, u32[]{:S(2)}, u32[]{:S(2)}) collective-permute-start(bf16[544,768]{1,0:T(8,128)(2,1)S(1)} %get-tuple-element.70.refs_0_), channel_id=1, source_target_pairs={{0,1},{1,0},{2,3},{3,2},{4,5},{5,4},{6,7},{7,6},{8,9},{9,8},{10,11... | collective-permute-start | bytes 2506760 | tf_op jit(solution)/shard_map/ppermute | solution.py:259
  132.8 21.0 %collective-permute-start.31 = (bf16[544,768]{1,0:T(8,128)(2,1)S(1)}, bf16[544,768]{1,0:T(8,128)(2,1)S(1)}, u32[]{:S(2)}, u32[]{:S(2)}) collective-permute-start(bf16[544,768]{1,0:T(8,128)(2,1)S(1)} %collective-permute-done.17.refs_2_), channel_id=1, source_target_pairs={{0,1},{1,0},{2,3},{3,2},{4,5},{5,4},{6,7},{7,6},{8,9},{9,8},{10,11... | collective-permute-start | bytes 2506760 | tf_op jit(solution)/shard_map/ppermute | solution.py:259
  132.8 21.4 %collective-permute-start.32 = (bf16[544,768]{1,0:T(8,128)(2,1)S(1)}, bf16[544,768]{1,0:T(8,128)(2,1)S(1)}, u32[]{:S(2)}, u32[]{:S(2)}) collective-permute-start(bf16[544,768]{1,0:T(8,128)(2,1)S(1)} %collective-permute-done.18.refs_4_), channel_id=1, source_target_pairs={{0,1},{1,0},{2,3},{3,2},{4,5},{5,4},{6,7},{7,6},{8,9},{9,8},{10,11... | collective-permute-start | bytes 2506760 | tf_op jit(solution)/shard_map/ppermute | solution.py:259
  152.7 10.1 %collective-permute-start.24 = (bf16[544,256]{1,0:T(8,128)(2,1)S(1)}, bf16[544,256]{1,0:T(8,128)(2,1)S(1)}, u32[]{:S(2)}, u32[]{:S(2)}) collective-permute-start(bf16[544,256]{1,0:T(8,128)(2,1)S(1)} %get-tuple-element.74.refs_0_), channel_id=1, source_target_pairs={{0,4},{1,5},{2,6},{3,7},{4,8},{5,9},{6,10},{7,11},{8,12},{9,13},{1... | collective-permute-start | bytes 835592 | tf_op jit(solution)/shard_map/ppermute | solution.py:263
  152.7 11.2 %collective-permute-start.25 = (bf16[544,256]{1,0:T(8,128)(2,1)S(1)}, bf16[544,256]{1,0:T(8,128)(2,1)S(1)}, u32[]{:S(2)}, u32[]{:S(2)}) collective-permute-start(bf16[544,256]{1,0:T(8,128)(2,1)S(1)} %get-tuple-element.74.refs_0_), channel_id=1, source_target_pairs={{0,2},{1,3},{2,0},{3,1},{4,6},{5,7},{6,4},{7,5},{8,10},{9,11},{10,... | collective-permute-start | bytes 835592 | tf_op jit(solution)/shard_map/ppermute | solution.py:263
  153.8 18.7 %collective-permute-start.34 = (bf16[544,768]{1,0:T(8,128)(2,1)S(1)}, bf16[544,768]{1,0:T(8,128)(2,1)S(1)}, u32[]{:S(2)}, u32[]{:S(2)}) collective-permute-start(bf16[544,768]{1,0:T(8,128)(2,1)S(1)} %collective-permute-done.20.refs_8_), channel_id=1, source_target_pairs={{0,1},{1,0},{2,3},{3,2},{4,5},{5,4},{6,7},{7,6},{8,9},{9,8},{10,11... | collective-permute-start | bytes 2506760 | tf_op jit(solution)/shard_map/ppermute | solution.py:259
  154.2 15.8 %collective-permute-start.37 = (bf16[272,768]{1,0:T(8,128)(2,1)S(1)}, bf16[272,768]{1,0:T(8,128)(2,1)S(1)}, u32[]{:S(2)}, u32[]{:S(2)}) collective-permute-start(bf16[272,768]{1,0:T(8,128)(2,1)S(1)} %slice.92), channel_id=1, source_target_pairs={{0,2},{1,3},{2,0},{3,1},{4,6},{5,7},{6,4},{7,5},{8,10},{9,11},{10,... | collective-permute-start | bytes 1253384 | tf_op jit(solution)/shard_map/ppermute | solution.py:270
  154.6 17.1 %collective-permute-start.38 = (bf16[272,768]{1,0:T(8,128)(2,1)S(1)}, bf16[272,768]{1,0:T(8,128)(2,1)S(1)}, u32[]{:S(2)}, u32[]{:S(2)}) collective-permute-start(bf16[272,768]{1,0:T(8,128)(2,1)S(1)} %slice.93), channel_id=1, source_target_pairs={{0,4},{1,5},{2,6},{3,7},{4,8},{5,9},{6,10},{7,11},{8,12},{9,13},{1... | collective-permute-start | bytes 1253384 | tf_op jit(solution)/shard_map/ppermute | solution.py:271
  162.7 11.1 %collective-permute-start.35 = (bf16[544,768]{1,0:T(8,128)(2,1)S(1)}, bf16[544,768]{1,0:T(8,128)(2,1)S(1)}, u32[]{:S(2)}, u32[]{:S(2)}) collective-permute-start(bf16[544,768]{1,0:T(8,128)(2,1)S(1)} %collective-permute-done.21.refs_10_), channel_id=1, source_target_pairs={{0,1},{1,0},{2,3},{3,2},{4,5},{5,4},{6,7},{7,6},{8,9},{9,8},{10,11... | collective-permute-start | bytes 2506760 | tf_op jit(solution)/shard_map/ppermute | solution.py:259
  163.9 10.0 %collective-permute-start.36 = (bf16[544,768]{1,0:T(8,128)(2,1)S(1)}, bf16[544,768]{1,0:T(8,128)(2,1)S(1)}, u32[]{:S(2)}, u32[]{:S(2)}) collective-permute-start(bf16[544,768]{1,0:T(8,128)(2,1)S(1)} %collective-permute-done.22.refs_12_), channel_id=1, source_target_pairs={{0,1},{1,0},{2,3},{3,2},{4,5},{5,4},{6,7},{7,6},{8,9},{9,8},{10,11... | collective-permute-start | bytes 2506760 | tf_op jit(solution)/shard_map/ppermute | solution.py:259
  172.5 14.1 %collective-permute-start.28 = (bf16[544,256]{1,0:T(8,128)(2,1)S(1)}, bf16[544,256]{1,0:T(8,128)(2,1)S(1)}, u32[]{:S(2)}, u32[]{:S(2)}) collective-permute-start(bf16[544,256]{1,0:T(8,128)(2,1)S(1)} %collective-permute-done.24.refs_2_), channel_id=1, source_target_pairs={{0,4},{1,5},{2,6},{3,7},{4,8},{5,9},{6,10},{7,11},{8,12},{9,13},{1... | collective-permute-start | bytes 835592 | tf_op jit(solution)/shard_map/ppermute | solution.py:263
  172.5 14.1 %collective-permute-start.29 = (bf16[544,256]{1,0:T(8,128)(2,1)S(1)}, bf16[544,256]{1,0:T(8,128)(2,1)S(1)}, u32[]{:S(2)}, u32[]{:S(2)}) collective-permute-start(bf16[544,256]{1,0:T(8,128)(2,1)S(1)} %collective-permute-done.24.refs_2_), channel_id=1, source_target_pairs={{0,2},{1,3},{2,0},{3,1},{4,6},{5,7},{6,4},{7,5},{8,10},{9,11},{10,... | collective-permute-start | bytes 835592 | tf_op jit(solution)/shard_map/ppermute | solution.py:263
  186.6 9.7 %collective-permute-start.43 = (bf16[544,256]{1,0:T(8,128)(2,1)S(1)}, bf16[544,256]{1,0:T(8,128)(2,1)S(1)}, u32[]{:S(2)}, u32[]{:S(2)}) collective-permute-start(bf16[544,256]{1,0:T(8,128)(2,1)S(1)} %collective-permute-done.28.refs_6_), channel_id=1, source_target_pairs={{0,4},{1,5},{2,6},{3,7},{4,8},{5,9},{6,10},{7,11},{8,12},{9,13},{1... | collective-permute-start | bytes 835592 | tf_op jit(solution)/shard_map/ppermute | solution.py:263
  186.7 24.7 %collective-permute-start.23 = (bf16[544,256]{1,0:T(8,128)(2,1)S(1)}, bf16[544,256]{1,0:T(8,128)(2,1)S(1)}, u32[]{:S(2)}, u32[]{:S(2)}) collective-permute-start(bf16[544,256]{1,0:T(8,128)(2,1)S(1)} %get-tuple-element.74.refs_0_), channel_id=1, source_target_pairs={{0,1},{1,0},{2,3},{3,2},{4,5},{5,4},{6,7},{7,6},{8,9},{9,8},{10,11... | collective-permute-start | bytes 835592 | tf_op jit(solution)/shard_map/ppermute | solution.py:259
  187.1 24.6 %collective-permute-start.26 = (bf16[544,256]{1,0:T(8,128)(2,1)S(1)}, bf16[544,256]{1,0:T(8,128)(2,1)S(1)}, u32[]{:S(2)}, u32[]{:S(2)}) collective-permute-start(bf16[544,256]{1,0:T(8,128)(2,1)S(1)} %collective-permute-done.24.refs_2_), channel_id=1, source_target_pairs={{0,1},{1,0},{2,3},{3,2},{4,5},{5,4},{6,7},{7,6},{8,9},{9,8},{10,11... | collective-permute-start | bytes 835592 | tf_op jit(solution)/shard_map/ppermute | solution.py:259
  187.2 24.8 %collective-permute-start.27 = (bf16[544,256]{1,0:T(8,128)(2,1)S(1)}, bf16[544,256]{1,0:T(8,128)(2,1)S(1)}, u32[]{:S(2)}, u32[]{:S(2)}) collective-permute-start(bf16[544,256]{1,0:T(8,128)(2,1)S(1)} %collective-permute-done.25.refs_4_), channel_id=1, source_target_pairs={{0,1},{1,0},{2,3},{3,2},{4,5},{5,4},{6,7},{7,6},{8,9},{9,8},{10,11... | collective-permute-start | bytes 835592 | tf_op jit(solution)/shard_map/ppermute | solution.py:259
  187.6 22.6 %collective-permute-start.44 = (bf16[544,256]{1,0:T(8,128)(2,1)S(1)}, bf16[544,256]{1,0:T(8,128)(2,1)S(1)}, u32[]{:S(2)}, u32[]{:S(2)}) collective-permute-start(bf16[544,256]{1,0:T(8,128)(2,1)S(1)} %collective-permute-done.28.refs_6_), channel_id=1, source_target_pairs={{0,2},{1,3},{2,0},{3,1},{4,6},{5,7},{6,4},{7,5},{8,10},{9,11},{10,... | collective-permute-start | bytes 835592 | tf_op jit(solution)/shard_map/ppermute | solution.py:263
  196.3 15.9 %collective-permute-start.41 = (bf16[544,256]{1,0:T(8,128)(2,1)S(1)}, bf16[544,256]{1,0:T(8,128)(2,1)S(1)}, u32[]{:S(2)}, u32[]{:S(2)}) collective-permute-start(bf16[544,256]{1,0:T(8,128)(2,1)S(1)} %collective-permute-done.28.refs_6_), channel_id=1, source_target_pairs={{0,1},{1,0},{2,3},{3,2},{4,5},{5,4},{6,7},{7,6},{8,9},{9,8},{10,11... | collective-permute-start | bytes 835592 | tf_op jit(solution)/shard_map/ppermute | solution.py:259
  211.4 7.1 %collective-permute-start.48 = (bf16[272,256]{1,0:T(8,128)(2,1)S(1)}, bf16[272,256]{1,0:T(8,128)(2,1)S(1)}, u32[]{:S(2)}, u32[]{:S(2)}) collective-permute-start(bf16[272,256]{1,0:T(8,128)(2,1)S(1)} %slice.95), channel_id=1, source_target_pairs={{0,4},{1,5},{2,6},{3,7},{4,8},{5,9},{6,10},{7,11},{8,12},{9,13},{1... | collective-permute-start | bytes 417800 | tf_op jit(solution)/shard_map/ppermute | solution.py:271
  211.7 20.6 %collective-permute-start.42 = (bf16[544,256]{1,0:T(8,128)(2,1)S(1)}, bf16[544,256]{1,0:T(8,128)(2,1)S(1)}, u32[]{:S(2)}, u32[]{:S(2)}) collective-permute-start(bf16[544,256]{1,0:T(8,128)(2,1)S(1)} %collective-permute-done.29.refs_8_), channel_id=1, source_target_pairs={{0,1},{1,0},{2,3},{3,2},{4,5},{5,4},{6,7},{7,6},{8,9},{9,8},{10,11... | collective-permute-start | bytes 835592 | tf_op jit(solution)/shard_map/ppermute | solution.py:259
  212.0 20.2 %collective-permute-start.45 = (bf16[544,256]{1,0:T(8,128)(2,1)S(1)}, bf16[544,256]{1,0:T(8,128)(2,1)S(1)}, u32[]{:S(2)}, u32[]{:S(2)}) collective-permute-start(bf16[544,256]{1,0:T(8,128)(2,1)S(1)} %collective-permute-done.43.refs_10_), channel_id=1, source_target_pairs={{0,1},{1,0},{2,3},{3,2},{4,5},{5,4},{6,7},{7,6},{8,9},{9,8},{10,11... | collective-permute-start | bytes 835592 | tf_op jit(solution)/shard_map/ppermute | solution.py:259
  212.3 20.0 %collective-permute-start.46 = (bf16[544,256]{1,0:T(8,128)(2,1)S(1)}, bf16[544,256]{1,0:T(8,128)(2,1)S(1)}, u32[]{:S(2)}, u32[]{:S(2)}) collective-permute-start(bf16[544,256]{1,0:T(8,128)(2,1)S(1)} %collective-permute-done.44.refs_12_), channel_id=1, source_target_pairs={{0,1},{1,0},{2,3},{3,2},{4,5},{5,4},{6,7},{7,6},{8,9},{9,8},{10,11... | collective-permute-start | bytes 835592 | tf_op jit(solution)/shard_map/ppermute | solution.py:259
  215.6 16.6 %collective-permute-start.49 = (bf16[272,256]{1,0:T(8,128)(2,1)S(1)}, bf16[272,256]{1,0:T(8,128)(2,1)S(1)}, u32[]{:S(2)}, u32[]{:S(2)}) collective-permute-start(bf16[272,256]{1,0:T(8,128)(2,1)S(1)} %collective-permute-done.47.refs_14_), channel_id=1, source_target_pairs={{0,1},{1,0},{2,3},{3,2},{4,5},{5,4},{6,7},{7,6},{8,9},{9,8},{10,11... | collective-permute-start | bytes 417800 | tf_op jit(solution)/shard_map/ppermute | solution.py:259
  218.4 13.8 %collective-permute-start.50 = (bf16[272,256]{1,0:T(8,128)(2,1)S(1)}, bf16[272,256]{1,0:T(8,128)(2,1)S(1)}, u32[]{:S(2)}, u32[]{:S(2)}) collective-permute-start(bf16[272,256]{1,0:T(8,128)(2,1)S(1)} %collective-permute-done.48.refs_15_), channel_id=1, source_target_pairs={{0,1},{1,0},{2,3},{3,2},{4,5},{5,4},{6,7},{7,6},{8,9},{9,8},{10,11... | collective-permute-start | bytes 417800 | tf_op jit(solution)/shard_map/ppermute | solution.py:259
  (10 other events, 83.4 us)

commit v4 on v3

--- a/solution.py
+++ b/solution.py
@@ -16,6 +16,7 @@
 CHUNKS = ((0, 3), (3, 1))
 PLANE = 4
 PLANES = 4
+UNROLL = 4
 GATHER_LIMIT = 40 * 2**20
 MASKED = -1e30
 VMEM = pl.BlockSpec(memory_space=pltpu.VMEM)
@@ -46,36 +47,56 @@
     return (rows * cosine + pltpu.roll(rows, HEAD_SIZE // 2, 1) * sine).astype(jnp.bfloat16)
 
 
-def order_kernel(ranks, slots, spare, stride, route_ref, bucket_ref, seat_ref, sorted_ref):
+def order_kernel(
+    ranks, slots, extra, stride, route_ref, bucket_ref, seat_ref, sorted_ref, more_ref
+):
     route = route_ref[...]
     count = route.shape[1]
+    share = count // ranks
     target = lax.div(route, slots)
     member = (lax.broadcasted_iota(jnp.int32, (ranks, count), 0) == target).astype(jnp.float32)
     before = lax.broadcasted_iota(jnp.int32, (count, count), 0) < lax.broadcasted_iota(
         jnp.int32, (count, count), 1
     )
-    ahead = contract(
-        member.astype(jnp.bfloat16), before.astype(jnp.float32).astype(jnp.bfloat16), 1, 0
-    )
+    before = before.astype(jnp.float32).astype(jnp.bfloat16)
+    ahead = contract(member.astype(jnp.bfloat16), before, 1, 0)
     order = jnp.sum(member * ahead, axis=0, keepdims=True).astype(jnp.int32)
-    bucket = target * spare + order
+    beyond = order >= share
+    beyond_rows = jnp.broadcast_to(beyond.astype(jnp.float32), (8, count)).astype(jnp.bfloat16)
+    number = contract(beyond_rows, before, 1, 0)[0:1]
+    counts = jnp.sum(member, axis=1, keepdims=True)
+    free = jnp.maximum(share - counts, 0.0)
+    group = lax.broadcasted_iota(jnp.int32, (ranks, ranks), 0)
+    lower = (group > lax.broadcasted_iota(jnp.int32, (ranks, ranks), 1)).astype(jnp.float32)
+    free_rows = jnp.broadcast_to(free, (ranks, HEAD_SIZE)).astype(jnp.bfloat16)
+    free_before = contract(lower.astype(jnp.bfloat16), free_rows, 1, 0)[:, 0:1]
+    inside = (number >= free_before) & (number < free_before + free)
+    base = lax.broadcasted_iota(jnp.int32, (ranks, 1), 0).astype(jnp.float32) * share + counts
+    hole = jnp.sum(jnp.where(inside, base + number - free_before, 0.0), axis=0, keepdims=True)
+    bucket = jnp.where(beyond, hole.astype(jnp.int32), target * share + order)
     bucket_ref[...] = bucket
     seat_ref[...] = target * stride + order
     high = lax.div(route, HEAD_SIZE)
-    low = route - high * HEAD_SIZE
+    place_high = lax.div(bucket, HEAD_SIZE)
     line = lax.broadcasted_iota(jnp.int32, (8, count), 0)
-    digits = jnp.where(line == 0, high, jnp.where(line == 1, low, jnp.where(line == 2, 1, 0)))
-    placed = contract(
-        digits.astype(jnp.float32).astype(jnp.bfloat16), one_hot_rows(ranks * spare, bucket), 1, 1
-    )
-    found = placed[0:1] * HEAD_SIZE + placed[1:2] + placed[2:3] - 1.0
-    sorted_ref[...] = found.astype(jnp.int32)
+    digits = jnp.where(line == 0, high, 0)
+    digits = jnp.where(line == 1, route - high * HEAD_SIZE, digits)
+    digits = jnp.where(line == 2, place_high, digits)
+    digits = jnp.where(line == 3, bucket - place_high * HEAD_SIZE, digits)
+    digits = jnp.where(line == 4, 1, digits).astype(jnp.float32).astype(jnp.bfloat16)
+    placed = contract(digits, one_hot_rows(count, bucket), 1, 1)
+    sorted_ref[...] = (placed[0:1] * HEAD_SIZE + placed[1:2]).astype(jnp.int32)
+    listed = jnp.where(beyond, target * extra + order - share, -1)
+    found = contract(digits, one_hot_rows(ranks * extra, listed), 1, 1)
+    none = found[4:5] - 1.0
+    more_ref[0:1] = (found[0:1] * HEAD_SIZE + found[1:2] + none).astype(jnp.int32)
+    more_ref[1:2] = (found[2:3] * HEAD_SIZE + found[3:4] + none).astype(jnp.int32)
 
 
 def query_kernel(
-    route_ref, seat_ref, positions_ref, frequency_ref, queries_ref, *refs
+    ranks, spare, stride, packed, route_ref, seat_ref, positions_ref, frequency_ref, queries_ref, *refs
 ):
-    turned_refs, (bounds_ref, cosine_ref, sine_ref) = refs[: len(CHUNKS)], refs[len(CHUNKS) :]
+    turned_ref, bounds_ref, cosine_ref, sine_ref, rows_ref = refs
     route = route_ref[...]
     count = route.shape[0]
     lines = positions_ref.shape[0]
@@ -97,7 +118,7 @@
     sine = jnp.where(lanes < HEAD_SIZE // 2, -sine, sine)
     cosine_ref[...] = cosine
     sine_ref[...] = sine
-    seats = one_hot_rows(bounds_ref.shape[0], seat_ref[...])
+    seats = one_hot_rows(ranks * stride, seat_ref[...])
     first = route - spot.astype(jnp.int32)
     first_line = lax.div(first, HEAD_SIZE)
     first_lane = first - first_line * HEAD_SIZE
@@ -111,14 +132,22 @@
     last = placed[:, 0:1] * HEAD_SIZE + placed[:, 1:2] + live
     start = placed[:, 2:3] * HEAD_SIZE + placed[:, 3:4] + live
     seat_lanes = lax.broadcasted_iota(jnp.int32, placed.shape, 1)
-    bounds_ref[...] = jnp.where(seat_lanes == 0, last, start).astype(jnp.int32)
-    for (first_head, heads), turned_ref in zip(CHUNKS, turned_refs):
-        for head in range(heads * HEAD_GROUPS):
-            at = (first_head * HEAD_GROUPS + head) * HEAD_SIZE
+    bounds = jnp.where(seat_lanes == 0, last, start).astype(jnp.int32)
+    bounds_ref[...] = jnp.full(bounds_ref.shape, -1, jnp.int32)
+    rows_ref[...] = jnp.zeros(rows_ref.shape, jnp.float32)
+    for group in range(ranks):
+        for place in range(HEAD_GROUPS):
+            at = group * packed + place * spare
+            bounds_ref[at : at + spare] = bounds[group * stride : group * stride + spare]
+    for head in range(KEY_VALUE_HEADS):
+        for place in range(HEAD_GROUPS):
+            at = (head * HEAD_GROUPS + place) * HEAD_SIZE
             one = queries_ref[:, at : at + HEAD_SIZE].astype(jnp.float32)
-            turned_ref[:, head * HEAD_SIZE : (head + 1) * HEAD_SIZE] = contract(
-                seats, turn(one, cosine, sine), 1, 0
-            ).astype(jnp.bfloat16)
+            rows = contract(seats, turn(one, cosine, sine), 1, 0)
+            for group in range(ranks):
+                at = group * packed + place * spare
+                rows_ref[at : at + spare] = rows[group * stride : group * stride + spare]
+        turned_ref[head] = rows_ref[...].astype(jnp.bfloat16)
 
 
 def add_products(chips, owners_ref, hidden_ref, refs, columns, matrix, done):
@@ -197,11 +226,19 @@
 
 
 def attend_kernel(
-    head, heads, pieces, spare, window, stride, queries_ref, bounds_ref, routes_ref, seat_ref, *refs
+    head, heads, pieces, extra, stride, packed,
+    queries_ref, bounds_ref, routes_ref, seat_ref, more_ref, *refs
 ):
     first_head, place = head
     ranks = routes_ref.shape[0]
-    parts, out_ref, blocks, mixed_ref, result_ref, done = refs[: len(pieces)], *refs[-5:]
+    parts, refs = refs[: len(pieces)], refs[-(6 + 3 * UNROLL) :]
+    out_ref, blocks, more, mixed_ref, result_ref, done = refs[:6]
+    score_refs, weight_refs, total_refs = (
+        refs[6 + at * UNROLL : 6 + (at + 1) * UNROLL] for at in range(3)
+    )
+    count = blocks.shape[2]
+    share = count // ranks
+    spare = share + extra
     copies = []
     for at, ((source, first), ref) in enumerate(zip(pieces, parts)):
         for part in range(2):
@@ -214,31 +251,69 @@
                 )
             )
             copies[-1].start()
+    mixed_ref[...] = jnp.zeros(mixed_ref.shape, jnp.bfloat16)
+    listed = ranks * extra
+    lines = lax.broadcasted_iota(jnp.int32, (listed, count), 1)
+    picks = [
+        (lines == more_ref[j * listed : (j + 1) * listed]).astype(jnp.float32).astype(jnp.bfloat16)
+        for j in range(ranks)
+    ]
+    row = lax.broadcasted_iota(jnp.int32, (ranks * listed, ranks * listed), 0)
+    column = lax.broadcasted_iota(jnp.int32, (ranks * listed, ranks * listed), 1)
+    group, rest = lax.div(row, listed), lax.rem(row, listed)
+    source, index = lax.div(rest, extra), lax.rem(rest, extra)
+    regroup = (column == source * listed + group * extra + index).astype(jnp.float32)
+    regroup = regroup.astype(jnp.bfloat16)
     for copy in copies:
         copy.wait()
+    for part in range(2):
+        found = [
+            contract(picks[j], blocks[part, j], 1, 0).astype(jnp.bfloat16) for j in range(ranks)
+        ]
+        more[part] = contract(regroup, jnp.concatenate(found, axis=0), 1, 0).astype(jnp.bfloat16)
     scale = math.log2(math.e) / math.sqrt(HEAD_SIZE)
-    turns = [slice(at * HEAD_SIZE, (at + 1) * HEAD_SIZE) for at in range(HEAD_GROUPS)]
-
-    def one_group(group, carry):
-        seats = pl.ds(pl.multiple_of(group * stride, 16), stride)
-        keys_at = pl.ds(pl.multiple_of(lax.div(group * spare, 16) * 16, 16), window)
+
+    def rows_of(part, group):
+        window = pl.ds(pl.multiple_of(group * share, 16), share)
+        rows = [blocks[part, j, window] for j in range(ranks)]
+        rows.append(more[part, pl.ds(pl.multiple_of(group * listed, 16), listed)])
+        return jnp.concatenate(rows, axis=0)
+
+    def score(group, score_ref):
+        query = queries_ref[0, pl.ds(pl.multiple_of(group * packed, 16), packed)]
+        score_ref[...] = contract(query, rows_of(0, group), 1, 1)
+
+    def weigh(group, score_ref, weight_ref, total_ref):
         routes = routes_ref[group]
-        visible = (routes <= bounds_ref[seats, 0:1]) & (routes >= bounds_ref[seats, 1:2])
-        veil = jnp.where(visible, 0.0, MASKED)
-        veil = jnp.concatenate([veil] * HEAD_GROUPS, axis=0)
-        query = jnp.concatenate([queries_ref[seats, one] for one in turns], axis=0)
-        keys = jnp.concatenate([blocks[0, j, keys_at] for j in range(ranks)], axis=0)
-        values = jnp.concatenate([blocks[1, j, keys_at] for j in range(ranks)], axis=0)
-        scores = contract(query, keys, 1, 1) * scale + veil
-        weights = jnp.exp2(scores - jnp.max(scores, axis=1, keepdims=True))
-        totals = jnp.sum(weights, axis=1, keepdims=True)
-        mixed = contract(weights.astype(jnp.bfloat16), values, 1, 0) / totals
-        mixed = mixed.astype(jnp.bfloat16)
-        for at, one in enumerate(turns):
-            mixed_ref[seats, one] = mixed[at * stride : (at + 1) * stride]
+        for first in range(0, packed, 16):
+            at = pl.ds(pl.multiple_of(group * packed + first, 16), 16)
+            visible = (routes <= bounds_ref[at, 0:1]) & (routes >= bounds_ref[at, 1:2])
+            scores = jnp.where(visible, score_ref[first : first + 16], MASKED)
+            top = jnp.max(scores, axis=1, keepdims=True)
+            weights = jnp.exp2((scores - top) * scale)
+            total = jnp.sum(weights, axis=1, keepdims=True)
+            weight_ref[first : first + 16] = weights.astype(jnp.bfloat16)
+            total_ref[first : first + 16] = jnp.broadcast_to(1.0 / total, (16, HEAD_SIZE))
+
+    def mix(group, weight_ref, total_ref):
+        mixed = contract(weight_ref[...], rows_of(1, group), 1, 0) * total_ref[...]
+        seats = pl.ds(pl.multiple_of(group * stride, 16), spare)
+        for at in range(HEAD_GROUPS):
+            lanes = slice(at * HEAD_SIZE, (at + 1) * HEAD_SIZE)
+            mixed_ref[seats, lanes] = mixed[at * spare : (at + 1) * spare].astype(jnp.bfloat16)
+
+    def some_groups(step, carry):
+        groups = [step * UNROLL + at for at in range(UNROLL)]
+        for at in range(UNROLL + 2):
+            if at < UNROLL:
+                score(groups[at], score_refs[at])
+            if 0 <= at - 1 < UNROLL:
+                weigh(groups[at - 1], score_refs[at - 1], weight_refs[at - 1], total_refs[at - 1])
+            if 0 <= at - 2 < UNROLL:
+                mix(groups[at - 2], weight_refs[at - 2], total_refs[at - 2])
         return carry
 
-    lax.fori_loop(0, ranks, one_group, 0)
+    lax.fori_loop(0, ranks // UNROLL, some_groups, 0)
     seats = one_hot_rows(mixed_ref.shape[0], seat_ref[...])
     result_ref[...] = contract(seats, mixed_ref[...], 0, 0).astype(jnp.bfloat16)
     lanes = pl.ds((first_head + place) * HEAD_GROUPS * HEAD_SIZE, HEAD_GROUPS * HEAD_SIZE)
@@ -271,9 +346,11 @@
     around = lax.ppermute(other[half:], "dp", ring)
     keep(steps - 1, 0, lane)
     keep(2 * steps - 2, 0, other)
+    extra = yield other
+    over, around, extra = lax.optimization_barrier((over, around, extra))
     keep(2 * steps - 1, 0, over)
     keep(2 * steps - 1, half, around)
-    yield other
+    yield extra
 
 
 def source_order(ranks):
@@ -297,14 +374,13 @@
     ranks = lax.axis_size("dp")
     rows = hidden.shape[0]
     slots = positions.shape[0]
-    spare = rows // ranks + 2
-    width = ranks * spare
+    share, extra = rows // ranks, 2
+    spare = share + extra
+    listed = ranks * extra
     stride = -(-spare // 16) * 16
-    starts = [group * spare // 16 * 16 for group in range(ranks)]
-    window = max(
-        -(-(group + 1) * spare // 16) * 16 - starts[group] for group in range(ranks)
-    )
-    depth, query_width = hidden.shape[1], queries.shape[1]
+    packed = -(-HEAD_GROUPS * spare // 16) * 16
+    key_count = ranks * (share + extra)
+    query_width = queries.shape[1]
     shape = jax.ShapeDtypeStruct
 
     def columns(array, chunk):
@@ -314,46 +390,56 @@
     matrices = {}
     sending = spread(jnp.concatenate([key_matrix, value_matrix], axis=1), ranks, matrices)
     next(sending)
-    bucket, seat, sorted_route = pl.pallas_call(
-        functools.partial(order_kernel, ranks, slots, spare, stride),
+    bucket, seat, sorted_route, more = pl.pallas_call(
+        functools.partial(order_kernel, ranks, slots, extra, stride),
         out_shape=(
             shape((1, rows), jnp.int32),
             shape((1, rows), jnp.int32),
-            shape((1, width), jnp.int32),
+            shape((1, rows), jnp.int32),
+            shape((2, listed), jnp.int32),
         ),
         in_specs=[VMEM],
-        out_specs=(VMEM, VMEM, VMEM),
+        out_specs=(VMEM,) * 4,
         compiler_params=grant(16),
         name="order",
     )(route.reshape(1, rows))
-    plan = jnp.concatenate([sorted_route.reshape(width), positions])
+    width = rows + 2 * listed
+    plan = jnp.concatenate([sorted_route.reshape(rows), more.reshape(2 * listed), positions])
     plan = lax.all_to_all(
         jnp.broadcast_to(plan, (ranks, width + slots)), "dp", split_axis=0, concat_axis=0, tiled=True
     )
+    sending.send(())
+    next(sending)
     plan, bucket, seat = sending.send((plan, bucket, seat))
     next(sending)
     all_positions = plan[:, width:].reshape(-1, HEAD_SIZE)
     owners = source_order(ranks)
-    key_routes = plan[:, :width][owners]
-    key_routes = jnp.stack(
-        [key_routes[:, at : at + window].reshape(1, ranks * window) for at in starts]
-    )
+    sources = plan[:, :width][owners]
+    key_routes = jnp.concatenate(
+        [
+            sources[:, :rows].reshape(ranks, ranks, share).transpose(1, 0, 2).reshape(ranks, -1),
+            sources[:, rows : rows + listed]
+            .reshape(ranks, ranks, extra)
+            .transpose(1, 0, 2)
+            .reshape(ranks, -1),
+        ],
+        axis=1,
+    ).reshape(ranks, 1, key_count)
+    more_places = sources[:, rows + listed :].reshape(ranks * listed, 1)
 
     half = HEAD_SIZE // 2
     frequency = 1000000.0 ** (-(jnp.arange(half, dtype=jnp.float32) * 2.0 / HEAD_SIZE))
-    *turned, bounds, cosine, sine = pl.pallas_call(
-        query_kernel,
-        out_shape=tuple(
-            shape((ranks * stride, heads * HEAD_GROUPS * HEAD_SIZE), jnp.bfloat16)
-            for _, heads in CHUNKS
-        )
-        + (
-            shape((ranks * stride, HEAD_SIZE), jnp.int32),
+    turned, bounds, cosine, sine = pl.pallas_call(
+        functools.partial(query_kernel, ranks, spare, stride, packed),
+        out_shape=(
+            shape((KEY_VALUE_HEADS, ranks * packed, HEAD_SIZE), jnp.bfloat16),
+            shape((ranks * packed, HEAD_SIZE), jnp.int32),
             shape((rows, HEAD_SIZE), jnp.float32),
             shape((rows, HEAD_SIZE), jnp.float32),
         ),
         in_specs=[VMEM] * 5,
-        out_specs=(VMEM,) * (len(CHUNKS) + 3),
+        out_specs=(VMEM,) * 4,
+        scratch_shapes=[pltpu.VMEM((ranks * packed, HEAD_SIZE), jnp.float32)],
         compiler_params=grant(32),
         cost_estimate=cost(4 * stride * ranks * rows * query_width, 4 * rows * query_width),
         name="turn_queries",
@@ -364,11 +450,6 @@
         jnp.concatenate([frequency, frequency]).reshape(1, HEAD_SIZE),
         queries,
     )
-
-    turned, bounds, cosine, sine, key_routes = sending.send(
-        (turned, bounds, cosine, sine, key_routes)
-    )
-    next(sending)
 
     shard, wide = key_matrix.shape[0], 2 * key_matrix.shape[1]
     planes = ranks // PLANE
@@ -410,16 +491,18 @@
         )(owners, hidden, *arrays, *more)
 
     total = add_part(None, (0, 1, planes))
-    (total,) = sending.send((total,))
+    turned, bounds, cosine, sine, key_routes, more_places, total = sending.send(
+        (turned, bounds, cosine, sine, key_routes, more_places, total)
+    )
     next(sending)
-    total = add_part(total, (2, planes + 1))
+    (total,) = sending.send((add_part(total, (2, planes + 1)),))
     total = add_part(total, (3, planes + 2))
     chips, arrays = chip_parts((planes + 3,))
     bias = jnp.concatenate([key_projection_bias, value_projection_bias])
     pairs = pl.pallas_call(
         functools.partial(finish_kernel, chips),
         out_shape=tuple(
-            shape((width, 2 * heads * HEAD_SIZE), jnp.bfloat16) for _, heads in CHUNKS
+            shape((rows, 2 * heads * HEAD_SIZE), jnp.bfloat16) for _, heads in CHUNKS
         ),
         in_specs=[SMEM, HBM] + [VMEM] * 4 + [HBM] * len(arrays) + [VMEM],
         out_specs=(VMEM,) * len(CHUNKS),
@@ -443,28 +526,33 @@
         pieces = [(source, first) for source in held for first, _ in held[source]]
         arrays = [array for source in held for _, array in held[source]]
         taken = [] if out is None else [out]
-        fixed = [turned[chunk], bounds, key_routes, seat]
+        fixed = [turned, bounds, key_routes, seat, more_places]
         span = HEAD_GROUPS * HEAD_SIZE
+        query_block = pl.BlockSpec(
+            (1, ranks * packed, HEAD_SIZE), lambda i, h=first_head + place: (h, 0, 0)
+        )
         return pl.pallas_call(
             functools.partial(
-                attend_kernel, (first_head, place), heads, pieces, spare, window, stride
+                attend_kernel, (first_head, place), heads, pieces, extra, stride, packed
             ),
             grid=(1,),
             out_shape=shape((rows, query_width), jnp.bfloat16),
-            in_specs=[pl.BlockSpec((ranks * stride, span), lambda i, p=place: (0, p))]
-            + [VMEM] * 3
-            + [HBM] * (len(pieces) + len(taken)),
+            in_specs=[query_block] + [VMEM] * 4 + [HBM] * (len(pieces) + len(taken)),
             out_specs=HBM,
             scratch_shapes=[
-                pltpu.VMEM((2, ranks, width, HEAD_SIZE), jnp.bfloat16),
+                pltpu.VMEM((2, ranks, rows, HEAD_SIZE), jnp.bfloat16),
+                pltpu.VMEM((2, ranks * listed, HEAD_SIZE), jnp.bfloat16),
                 pltpu.VMEM((ranks * stride, span), jnp.bfloat16),
                 pltpu.VMEM((rows, span), jnp.bfloat16),
                 pltpu.SemaphoreType.DMA((2 * len(pieces) + 1,)),
-            ],
+            ]
+            + [pltpu.VMEM((packed, key_count), jnp.float32)] * UNROLL
+            + [pltpu.VMEM((packed, key_count), jnp.bfloat16)] * UNROLL
+            + [pltpu.VMEM((packed, HEAD_SIZE), jnp.float32)] * UNROLL,
             input_output_aliases={len(fixed) + len(pieces): 0} if taken else {},
             compiler_params=grant(28),
             cost_estimate=cost(
-                16 * rows * stride * ranks * span, 4 * ranks * width * HEAD_SIZE
+                16 * rows * stride * ranks * span, 4 * ranks * rows * HEAD_SIZE
             ),
             name="attend",
         )(*fixed, *arrays, *taken)
@@ -475,6 +563,7 @@
         next(sending)
         sending.send(())
     mark = next(sending)
+    sending.send(())
     last, _ = lax.optimization_barrier((pairs[1], mark))
     sending = spread(last, ranks, late)
     out = None
@@ -485,7 +574,7 @@
         out = attend(out, 0, early, place)
         (out,) = sending.send((out,))
     next(sending)
-    out = attend(out, 0, early, 2)
+    (out,) = sending.send((attend(out, 0, early, 2),))
     return attend(out, 1, late, 0)
 
 
@@ -623,7 +712,7 @@
     rows = hidden.shape[0]
     gathered = ranks * ranks * (rows // ranks + 2) * 4 * key_matrix.shape[1]
     chip_rows = 2 * key_matrix.shape[0]
-    fits = rows % ranks == 0 and chip_rows % HEAD_SIZE == 0 and gathered <= GATHER_LIMIT
+    fits = rows % (16 * ranks) == 0 and chip_rows % HEAD_SIZE == 0 and gathered <= GATHER_LIMIT
     if ranks == PLANES * PLANE and fits:
         return gather_plan(*args)
     return send_plan(*args)

time: 246 us -> 315 us (1.28)
  Pallas kernels: 74.7 us -> 127 us
  local copies, waits for them, and re-layouts: 8.36 us -> 38.6 us
  waiting for transfers between devices: 121 us -> 92.6 us
  starting transfers between devices: 39.4 us -> 52.2 us
    pallas_call x4, Pallas kernels: 50.7 us -> 101 us  [attend(): pl.pallas_call(functools.partial(attend_kernel, (first_head, place), head...]
    unnamed x29 -> x78, local copies, waits for them, and re-layouts: 3.65 us -> 25.9 us
    ppermute x9, waiting for transfers between devices: 89.5 us -> 72.3 us  [spread(): lax.ppermute(lane, 'dp', ring)]
    ppermute x3, waiting for transfers between devices: 17.4 us -> 6.9 us  [spread(): over = lax.ppermute(lane[:half], 'dp', across)]
    all_to_all x1, waiting for transfers between devices: 9.96 us -> 0.01 us  [gather_plan(): lax.all_to_all(jnp.broadcast_to(plan, (ranks, width + slots)), 'dp', spli...]
    ppermute x9, starting transfers between devices: 2.88 us -> 12.8 us  [spread(): lax.ppermute(lane, 'dp', ring)]
    ppermute x3, waiting for transfers between devices: 3.5 us -> 12.2 us  [spread(): around = lax.ppermute(other[half:], 'dp', ring)]
    ppermute x27, starting transfers between devices: 21.7 us -> 25.5 us  [keep(): lax.ppermute(array, 'dp', beside)]
  transfers between devices with their start and end apart: 52 -> 52, of which waited for: 15 -> 13; matrix products, arithmetic and copies ran while one was open for 2% -> 4% of each run, Pallas kernels for 23% -> 31%
where the time goes in v4:
time: 315 us; the launch traced here: 312 us
  Pallas kernels  127 us (40%)
  waiting for transfers between devices  92.6 us (29%)
  starting transfers between devices  52.2 us (17%)
  local copies, waits for them, and re-layouts  38.6 us (12%)
    pallas_call x4, Pallas kernels, attend(): pl.pallas_call(functools.partial(attend_kernel, (first_head, place), head...  101 us
    ppermute x9, waiting for transfers between devices, spread(): lax.ppermute(lane, 'dp', ring)  72.3 us
    unnamed x78, local copies, waits for them, and re-layouts  25.9 us
    ppermute x27, starting transfers between devices, keep(): lax.ppermute(array, 'dp', beside)  25.5 us
    pallas_call x3, Pallas kernels, add_part(): pl.pallas_call(functools.partial(part_kernel, chips, bool(more)), out_sha...  14.1 us
    ppermute x9, starting transfers between devices, spread(): lax.ppermute(lane, 'dp', ring)  12.8 us
    ppermute x3, waiting for transfers between devices, spread(): around = lax.ppermute(other[half:], 'dp', ring)  12.2 us
    ppermute x9, starting transfers between devices, spread(): lax.ppermute(lane, 'dp', across)  7.53 us
  transfers between devices with their start and end apart: 52, of which 13 were waited for; matrix products, arithmetic and copies ran while one was open for 4% of the time, Pallas kernels for 31%

profile of v4, /device:TPU:1, one launch (start us, length us, event | category | flops | bytes accessed | tf_op | source)
XLA Modules:
  0.0 311.8 jit_solution(855518940137318430)
XLA Ops:
  2.0 2.2 collective-permute-start
  4.2 1.2 collective-permute-start.1
  5.4 1.2 collective-permute-start.6
  9.5 4.0 %all-to-all-start = ((s32[16,1,1600]{2,1,0:T(1,128)}), s32[16,1,1600]{2,1,0:T(1,128)S(1)}, u32[]{:S(2)}, u32[]{:S(2)}) async-start(s32[16,1,1600]{2,1,0:T(1,128)} %broadcast_in_dim.4), calls=%async_computation | async-start | bytes 212992 | tf_op jit(solution)/shard_map/all_to_all | solution.py:408
  13.5 1.5 copy.23.route_ref
  15.1 5.7 %collective-permute-done.refs_2_ = bf16[320,1024]{1,0:T(8,128)(2,1)S(1)} collective-permute-done((bf16[320,1024]{1,0:T(8,128)(2,1)S(1)}, bf16[320,1024]{1,0:T(8,128)(2,1)S(1)}, u32[]{:S(2)}, u32[]{:S(2)}) %collective-permute-start) | collective-permute-done | bytes 655392 | tf_op jit(solution)/shard_map/ppermute | solution.py:338
  20.8 1.4 collective-permute-start.3
  22.3 2.9 collective-permute-start.7
  25.5 11.3 %collective-permute-done.2.refs_0_ = bf16[320,1024]{1,0:T(8,128)(2,1)S(1)} collective-permute-done((bf16[320,1024]{1,0:T(8,128)(2,1)S(1)}, bf16[320,1024]{1,0:T(8,128)(2,1)S(1)}, u32[]{:S(2)}, u32[]{:S(2)}) %collective-permute-start.2) | collective-permute-done | bytes 655392 | tf_op jit(solution)/shard_map/ppermute | solution.py:338
  42.9 1.5 reshape.171.positions_ref
  44.4 3.5 %collective-permute-start.11 = (bf16[320,1024]{1,0:T(8,128)(2,1)}, bf16[320,1024]{1,0:T(8,128)(2,1)S(1)}, u32[]{:S(2)}, u32[]{:S(2)}) collective-permute-start(bf16[320,1024]{1,0:T(8,128)(2,1)} %copy-done.20), channel_id=1, source_target_pairs={{0,1},{1,0},{2,3},{3,2},{4,5},{5,4},{6,7},{7,6},{8,9},{9,8},{10,11... | collective-permute-start | bytes 1966088 | tf_op jit(solution)/shard_map/ppermute | solution.py:334
  48.0 2.5 copy-done
  50.5 5.9 %add_part.3.refs_4_ = f32[512,1024]{1,0:T(8,128)S(1)} custom-call(s32[16]{0:T(128)S(1)} %pad_add_fusion.1.owners_ref, bf16[512,5120]{1,0:T(8,128)(2,1)S(1)} %copy-done, bf16[320,1024]{1,0:T(8,128)(2,1)S(1)} %constant_dynamic-update-slice_fusion.refs_0_, bf16[320,1024]{1,0:T(8,128)(2,1)S(1)} %collective-permute-done.6.refs_1_, ...), custom_call_target="tpu_custom_call" | custom-call | flops 2013265920 | bytes 10092544 | tf_op jit(solution)/shard_map/add_part/pallas_call | solution.py:482
  56.5 6.7 %turn_queries.1 = (bf16[4,2816,128]{2,1,0:T(8,128)(2,1)S(1)}, s32[2816,128]{1,0:T(8,128)S(1)}, f32[512,128]{1,0:T(8,128)S(1)}, f32[512,128]{1,0:T(8,128)S(1)}) custom-call(s32[512,1]{1,0:T(8,128)S(1)} %copy-done.22, s32[1,512]{1,0:T(1,128)S(1)} %get-tuple-element.60.seat_ref, s32[128,128]{1,0:T(8,128)S(1)} %copy-done.23, ...), custom_call_target="tpu_custom_call" | custom-call | flops 4026531840 | bytes 5242880 | tf_op jit(solution)/shard_map/turn_queries/pallas_call | solution.py:432
  63.1 1.1 copy-done.1
  66.7 4.1 %add_part.4.refs_4_ = f32[512,1024]{1,0:T(8,128)S(1)} custom-call(s32[16]{0:T(128)S(1)} %pad_add_fusion.1.owners_ref, bf16[512,5120]{1,0:T(8,128)(2,1)S(1)} %bitcast.22, bf16[320,1024]{1,0:T(8,128)(2,1)S(1)} %copy-done.21, bf16[320,1024]{1,0:T(8,128)(2,1)S(1)} %collective-permute-done.11.refs_1_, bf16[320,1024]{1,0:T(8,128)(2,1)} %collective-permute-done.3.refs_2_, ...), custom_call_target="tpu_custom_call" | custom-call | flops 1342177280 | bytes 8126464 | tf_op jit(solution)/shard_map/add_part/pallas_call | solution.py:482
  70.8 6.6 %collective-permute-done.10.refs_1_ = bf16[160,1024]{1,0:T(8,128)(2,1)S(1)} collective-permute-done((bf16[160,1024]{1,0:T(8,128)(2,1)S(1)}, bf16[160,1024]{1,0:T(8,128)(2,1)S(1)}, u32[]{:S(2)}, u32[]{:S(2)}) %collective-permute-start.10) | collective-permute-done | bytes 327712 | tf_op jit(solution)/shard_map/ppermute | solution.py:346
  78.4 4.1 %add_part.5.refs_4_ = f32[512,1024]{1,0:T(8,128)S(1)} custom-call(s32[16]{0:T(128)S(1)} %pad_add_fusion.1.owners_ref, bf16[512,5120]{1,0:T(8,128)(2,1)S(1)} %bitcast.22, bf16[320,1024]{1,0:T(8,128)(2,1)S(1)} %collective-permute-done.4.refs_0_, bf16[320,1024]{1,0:T(8,128)(2,1)S(1)} %collective-permute-done.15.refs_1_, ...), custom_call_target="tpu_custom_call" | custom-call | flops 1342177280 | bytes 8126464 | tf_op jit(solution)/shard_map/add_part/pallas_call | solution.py:482
  82.5 4.5 %finish.1 = (bf16[512,768]{1,0:T(8,128)(2,1)S(1)}, bf16[512,256]{1,0:T(8,128)(2,1)S(1)}) custom-call(s32[16]{0:T(128)S(1)} %pad_add_fusion.1.owners_ref, bf16[512,5120]{1,0:T(8,128)(2,1)S(1)} %bitcast.22, f32[1,1024]{1,0:T(1,128)S(1)} %maximum_convert_fusion.bias_ref, f32[512,128]{1,0:T(8,128)S(1)} %get-tuple-element.71.cosine_ref, ...), custom_call_target="tpu_custom_call" | custom-call | flops 671088640 | bytes 6160384 | tf_op jit(solution)/shard_map/finish/pallas_call | solution.py:502
  87.6 19.9 %collective-permute-done.17.refs_2_ = bf16[512,768]{1,0:T(8,128)(2,1)S(1)} collective-permute-done((bf16[512,768]{1,0:T(8,128)(2,1)S(1)}, bf16[512,768]{1,0:T(8,128)(2,1)S(1)}, u32[]{:S(2)}, u32[]{:S(2)}) %collective-permute-start.17) | collective-permute-done | bytes 786464 | tf_op jit(solution)/shard_map/ppermute | solution.py:338
  108.0 19.0 %collective-permute-done.19.refs_6_ = bf16[512,768]{1,0:T(8,128)(2,1)S(1)} collective-permute-done((bf16[512,768]{1,0:T(8,128)(2,1)S(1)}, bf16[512,768]{1,0:T(8,128)(2,1)S(1)}, u32[]{:S(2)}, u32[]{:S(2)}) %collective-permute-start.19) | collective-permute-done | bytes 786464 | tf_op jit(solution)/shard_map/ppermute | solution.py:338
  127.4 2.6 collective-permute-start.30
  133.3 12.3 %collective-permute-done.21.refs_10_ = bf16[512,768]{1,0:T(8,128)(2,1)} collective-permute-done((bf16[512,768]{1,0:T(8,128)(2,1)S(1)}, bf16[512,768]{1,0:T(8,128)(2,1)}, u32[]{:S(2)}, u32[]{:S(2)}) %collective-permute-start.21) | collective-permute-done | bytes 786464 | tf_op jit(solution)/shard_map/ppermute | solution.py:338
  145.6 3.2 %collective-permute-start.33 = (bf16[512,768]{1,0:T(8,128)(2,1)S(1)}, bf16[512,768]{1,0:T(8,128)(2,1)S(1)}, u32[]{:S(2)}, u32[]{:S(2)}) collective-permute-start(bf16[512,768]{1,0:T(8,128)(2,1)S(1)} %collective-permute-done.19.refs_6_), channel_id=1, source_target_pairs={{0,1},{1,0},{2,3},{3,2},{4,5},{5,4},{6,7},{7,6},{8,9},{9,8},{10,11... | collective-permute-start | bytes 2359304 | tf_op jit(solution)/shard_map/ppermute | solution.py:334
  156.7 5.0 %collective-permute-done.37.refs_14_ = bf16[256,768]{1,0:T(8,128)(2,1)S(1)} collective-permute-done((bf16[256,768]{1,0:T(8,128)(2,1)S(1)}, bf16[256,768]{1,0:T(8,128)(2,1)S(1)}, u32[]{:S(2)}, u32[]{:S(2)}) %collective-permute-start.37) | collective-permute-done | bytes 393248 | tf_op jit(solution)/shard_map/ppermute | solution.py:345
  161.7 3.9 %collective-permute-done.38.refs_15_ = bf16[256,768]{1,0:T(8,128)(2,1)} collective-permute-done((bf16[256,768]{1,0:T(8,128)(2,1)S(1)}, bf16[256,768]{1,0:T(8,128)(2,1)}, u32[]{:S(2)}, u32[]{:S(2)}) %collective-permute-start.38) | collective-permute-done | bytes 393248 | tf_op jit(solution)/shard_map/ppermute | solution.py:346
  166.5 4.1 %collective-permute-done.24.refs_2_ = bf16[512,256]{1,0:T(8,128)(2,1)S(1)} collective-permute-done((bf16[512,256]{1,0:T(8,128)(2,1)S(1)}, bf16[512,256]{1,0:T(8,128)(2,1)S(1)}, u32[]{:S(2)}, u32[]{:S(2)}) %collective-permute-start.24) | collective-permute-done | bytes 262176 | tf_op jit(solution)/shard_map/ppermute | solution.py:338
  170.6 1.6 collective-permute-start.39
  172.9 2.0 collective-permute-start.40
  175.3 1.1 collective-permute-start.29
  177.1 1.4 copy-done.2
  178.4 1.1 copy-done.4
  179.6 1.1 copy-done.6
  180.7 1.1 copy-done.8
  181.8 1.1 copy-done.10
  183.0 1.1 copy-done.12
  184.1 1.1 copy-done.14
  185.2 1.1 copy-done.16
  186.4 1.1 copy-done.18
  188.3 25.6 %attend.4.refs_18_ = bf16[512,2560]{1,0:T(8,128)(2,1)} custom-call(bf16[4,2816,128]{2,1,0:T(8,128)(2,1)S(1)} %get-tuple-element.67.queries_ref, s32[2816,128]{1,0:T(8,128)S(1)} %copy-done.2, s32[16,1,544]{2,1,0:T(1,128)S(1)} %copy-done.19, s32[1,512]{1,0:T(1,128)S(1)} %get-tuple-element.60.seat_ref, s32[512,1]{1,0:T(8,128)S(1)} %copy.31.more_ref, ...), custom_call_target="tpu_custom_call" | custom-call | flops 4026531840 | bytes 4194304 | tf_op jit(solution)/shard_map/attend/pallas_call | solution.py:534
  213.9 10.5 %collective-permute-start.43 = (bf16[512,256]{1,0:T(8,128)(2,1)S(1)}, bf16[512,256]{1,0:T(8,128)(2,1)S(1)}, u32[]{:S(2)}, u32[]{:S(2)}) collective-permute-start(bf16[512,256]{1,0:T(8,128)(2,1)S(1)} %collective-permute-done.28.refs_6_), channel_id=1, source_target_pairs={{0,4},{1,5},{2,6},{3,7},{4,8},{5,9},{6,10},{7,11},{8,12},{9,13},{1... | collective-permute-start | bytes 786440 | tf_op jit(solution)/shard_map/ppermute | solution.py:338
  225.0 25.6 %attend.5.refs_18_ = bf16[512,2560]{1,0:T(8,128)(2,1)} custom-call(bf16[4,2816,128]{2,1,0:T(8,128)(2,1)S(1)} %get-tuple-element.67.queries_ref, s32[2816,128]{1,0:T(8,128)S(1)} %copy-done.2, s32[16,1,544]{2,1,0:T(1,128)S(1)} %copy-done.19, s32[1,512]{1,0:T(1,128)S(1)} %get-tuple-element.60.seat_ref, ...), custom_call_target="tpu_custom_call", output_to_operand_aliasing={{}: (23, {})} | custom-call | flops 4026531840 | bytes 4194304 | tf_op jit(solution)/shard_map/attend/pallas_call | solution.py:534
  253.2 1.9 collective-permute-done.47.refs_14_
  255.1 1.5 collective-permute-start.45
  256.6 1.8 collective-permute-done.48.refs_15_
  258.4 1.2 collective-permute-start.46
  259.6 25.6 %attend.6.refs_18_ = bf16[512,2560]{1,0:T(8,128)(2,1)} custom-call(bf16[4,2816,128]{2,1,0:T(8,128)(2,1)S(1)} %get-tuple-element.67.queries_ref, s32[2816,128]{1,0:T(8,128)S(1)} %copy-done.2, s32[16,1,544]{2,1,0:T(1,128)S(1)} %copy-done.19, s32[1,512]{1,0:T(1,128)S(1)} %get-tuple-element.60.seat_ref, ...), custom_call_target="tpu_custom_call", output_to_operand_aliasing={{}: (23, {})} | custom-call | flops 4026531840 | bytes 4194304 | tf_op jit(solution)/shard_map/attend/pallas_call | solution.py:534
  286.8 24.8 %attend.7 = bf16[512,2560]{1,0:T(8,128)(2,1)} custom-call(bf16[4,2816,128]{2,1,0:T(8,128)(2,1)S(1)} %get-tuple-element.67.queries_ref, s32[2816,128]{1,0:T(8,128)S(1)} %copy-done.2, s32[16,1,544]{2,1,0:T(1,128)S(1)} %copy-done.19, s32[1,512]{1,0:T(1,128)S(1)} %get-tuple-element.60.seat_ref, ...), custom_call_target="tpu_custom_call", output_to_operand_aliasing={{}: (23, {})} | custom-call | flops 4026531840 | bytes 4194304 | tf_op jit(solution)/shard_map/attend/pallas_call | solution.py:534
  (182 shorter events, 35.8 us)
Async XLA Ops:
  2.0 18.7 %collective-permute-start = (bf16[320,1024]{1,0:T(8,128)(2,1)S(1)}, bf16[320,1024]{1,0:T(8,128)(2,1)S(1)}, u32[]{:S(2)}, u32[]{:S(2)}) collective-permute-start(bf16[320,1024]{1,0:T(8,128)(2,1)S(1)} %constant_dynamic-update-slice_fusion.refs_0_), channel_id=1, source_target_pairs={{0,4},{1,5},{2,6},{3,7},{4,8},{5,9},{6,10},{7,11},{8,12},{9,13},{1... | collective-permute-start | bytes 1966088 | tf_op jit(solution)/shard_map/ppermute | solution.py:338
  4.2 16.6 %collective-permute-start.1 = (bf16[320,1024]{1,0:T(8,128)(2,1)S(1)}, bf16[320,1024]{1,0:T(8,128)(2,1)S(1)}, u32[]{:S(2)}, u32[]{:S(2)}) collective-permute-start(bf16[320,1024]{1,0:T(8,128)(2,1)S(1)} %constant_dynamic-update-slice_fusion.refs_0_), channel_id=1, source_target_pairs={{0,2},{1,3},{2,0},{3,1},{4,6},{5,7},{6,4},{7,5},{8,10},{9,11},{10,... | collective-permute-start | bytes 1966088 | tf_op jit(solution)/shard_map/ppermute | solution.py:338
  5.4 38.9 %collective-permute-start.6 = (bf16[320,1024]{1,0:T(8,128)(2,1)S(1)}, bf16[320,1024]{1,0:T(8,128)(2,1)S(1)}, u32[]{:S(2)}, u32[]{:S(2)}) collective-permute-start(bf16[320,1024]{1,0:T(8,128)(2,1)S(1)} %constant_dynamic-update-slice_fusion.refs_0_), channel_id=1, source_target_pairs={{0,1},{1,0},{2,3},{3,2},{4,5},{5,4},{6,7},{7,6},{8,9},{9,8},{10,11... | collective-permute-start | bytes 1966088 | tf_op jit(solution)/shard_map/ppermute | solution.py:334
  9.5 15.9 %all-to-all-start = ((s32[16,1,1600]{2,1,0:T(1,128)}), s32[16,1,1600]{2,1,0:T(1,128)S(1)}, u32[]{:S(2)}, u32[]{:S(2)}) async-start(s32[16,1,1600]{2,1,0:T(1,128)} %broadcast_in_dim.4), calls=%async_computation | async-start | bytes 212992 | tf_op jit(solution)/shard_map/all_to_all | solution.py:408
  20.8 16.0 %collective-permute-start.2 = (bf16[320,1024]{1,0:T(8,128)(2,1)S(1)}, bf16[320,1024]{1,0:T(8,128)(2,1)S(1)}, u32[]{:S(2)}, u32[]{:S(2)}) collective-permute-start(bf16[320,1024]{1,0:T(8,128)(2,1)S(1)} %collective-permute-done.refs_2_), channel_id=1, source_target_pairs={{0,4},{1,5},{2,6},{3,7},{4,8},{5,9},{6,10},{7,11},{8,12},{9,13},{1... | collective-permute-start | bytes 1966088 | tf_op jit(solution)/shard_map/ppermute | solution.py:338
  20.8 16.0 %collective-permute-start.3 = (bf16[320,1024]{1,0:T(8,128)(2,1)S(1)}, bf16[320,1024]{1,0:T(8,128)(2,1)}, u32[]{:S(2)}, u32[]{:S(2)}) collective-permute-start(bf16[320,1024]{1,0:T(8,128)(2,1)S(1)} %collective-permute-done.refs_2_), channel_id=1, source_target_pairs={{0,2},{1,3},{2,0},{3,1},{4,6},{5,7},{6,4},{7,5},{8,10},{9,11},{10,... | collective-permute-start | bytes 1966088 | tf_op jit(solution)/shard_map/ppermute | solution.py:338
  22.3 25.6 %collective-permute-start.7 = (bf16[320,1024]{1,0:T(8,128)(2,1)S(1)}, bf16[320,1024]{1,0:T(8,128)(2,1)}, u32[]{:S(2)}, u32[]{:S(2)}) collective-permute-start(bf16[320,1024]{1,0:T(8,128)(2,1)S(1)} %collective-permute-done.refs_2_), channel_id=1, source_target_pairs={{0,1},{1,0},{2,3},{3,2},{4,5},{5,4},{6,7},{7,6},{8,9},{9,8},{10,11... | collective-permute-start | bytes 1966088 | tf_op jit(solution)/shard_map/ppermute | solution.py:334
  25.2 22.8 %collective-permute-start.8 = (bf16[320,1024]{1,0:T(8,128)(2,1)S(1)}, bf16[320,1024]{1,0:T(8,128)(2,1)}, u32[]{:S(2)}, u32[]{:S(2)}) collective-permute-start(bf16[320,1024]{1,0:T(8,128)(2,1)S(1)} %collective-permute-done.1.refs_4_), channel_id=1, source_target_pairs={{0,1},{1,0},{2,3},{3,2},{4,5},{5,4},{6,7},{7,6},{8,9},{9,8},{10,11... | collective-permute-start | bytes 1966088 | tf_op jit(solution)/shard_map/ppermute | solution.py:334
  38.3 25.9 %collective-permute-start.4 = (bf16[320,1024]{1,0:T(8,128)(2,1)}, bf16[320,1024]{1,0:T(8,128)(2,1)S(1)}, u32[]{:S(2)}, u32[]{:S(2)}) collective-permute-start(bf16[320,1024]{1,0:T(8,128)(2,1)} %copy-done.20), channel_id=1, source_target_pairs={{0,4},{1,5},{2,6},{3,7},{4,8},{5,9},{6,10},{7,11},{8,12},{9,13},{1... | collective-permute-start | bytes 1966088 | tf_op jit(solution)/shard_map/ppermute | solution.py:338
  38.3 25.9 %collective-permute-start.5 = (bf16[320,1024]{1,0:T(8,128)(2,1)}, bf16[320,1024]{1,0:T(8,128)(2,1)}, u32[]{:S(2)}, u32[]{:S(2)}) collective-permute-start(bf16[320,1024]{1,0:T(8,128)(2,1)} %copy-done.20), channel_id=1, source_target_pairs={{0,2},{1,3},{2,0},{3,1},{4,6},{5,7},{6,4},{7,5},{8,10},{9,11},{10,... | collective-permute-start | bytes 1966088 | tf_op jit(solution)/shard_map/ppermute | solution.py:338
  44.4 22.2 %collective-permute-start.11 = (bf16[320,1024]{1,0:T(8,128)(2,1)}, bf16[320,1024]{1,0:T(8,128)(2,1)S(1)}, u32[]{:S(2)}, u32[]{:S(2)}) collective-permute-start(bf16[320,1024]{1,0:T(8,128)(2,1)} %copy-done.20), channel_id=1, source_target_pairs={{0,1},{1,0},{2,3},{3,2},{4,5},{5,4},{6,7},{7,6},{8,9},{9,8},{10,11... | collective-permute-start | bytes 1966088 | tf_op jit(solution)/shard_map/ppermute | solution.py:334
  47.9 18.8 %collective-permute-start.12 = (bf16[320,1024]{1,0:T(8,128)(2,1)}, bf16[320,1024]{1,0:T(8,128)(2,1)S(1)}, u32[]{:S(2)}, u32[]{:S(2)}) collective-permute-start(bf16[320,1024]{1,0:T(8,128)(2,1)} %collective-permute-done.3.refs_2_), channel_id=1, source_target_pairs={{0,1},{1,0},{2,3},{3,2},{4,5},{5,4},{6,7},{7,6},{8,9},{9,8},{10,11... | collective-permute-start | bytes 1966088 | tf_op jit(solution)/shard_map/ppermute | solution.py:334
  64.2 14.1 %collective-permute-start.15 = (bf16[320,1024]{1,0:T(8,128)(2,1)S(1)}, bf16[320,1024]{1,0:T(8,128)(2,1)S(1)}, u32[]{:S(2)}, u32[]{:S(2)}) collective-permute-start(bf16[320,1024]{1,0:T(8,128)(2,1)S(1)} %collective-permute-done.4.refs_0_), channel_id=1, source_target_pairs={{0,1},{1,0},{2,3},{3,2},{4,5},{5,4},{6,7},{7,6},{8,9},{9,8},{10,11... | collective-permute-start | bytes 1966088 | tf_op jit(solution)/shard_map/ppermute | solution.py:334
  64.7 13.7 %collective-permute-start.16 = (bf16[320,1024]{1,0:T(8,128)(2,1)}, bf16[320,1024]{1,0:T(8,128)(2,1)S(1)}, u32[]{:S(2)}, u32[]{:S(2)}) collective-permute-start(bf16[320,1024]{1,0:T(8,128)(2,1)} %collective-permute-done.5.refs_2_), channel_id=1, source_target_pairs={{0,1},{1,0},{2,3},{3,2},{4,5},{5,4},{6,7},{7,6},{8,9},{9,8},{10,11... | collective-permute-start | bytes 1966088 | tf_op jit(solution)/shard_map/ppermute | solution.py:334
  65.8 11.6 %collective-permute-start.10 = (bf16[160,1024]{1,0:T(8,128)(2,1)S(1)}, bf16[160,1024]{1,0:T(8,128)(2,1)S(1)}, u32[]{:S(2)}, u32[]{:S(2)}) collective-permute-start(bf16[160,1024]{1,0:T(8,128)(2,1)S(1)} %slice.39), channel_id=1, source_target_pairs={{0,4},{1,5},{2,6},{3,7},{4,8},{5,9},{6,10},{7,11},{8,12},{9,13},{1... | collective-permute-start | bytes 983048 | tf_op jit(solution)/shard_map/ppermute | solution.py:346
  66.5 10.9 %collective-permute-start.9 = (bf16[160,1024]{1,0:T(8,128)(2,1)S(1)}, bf16[160,1024]{1,0:T(8,128)(2,1)S(1)}, u32[]{:S(2)}, u32[]{:S(2)}) collective-permute-start(bf16[160,1024]{1,0:T(8,128)(2,1)S(1)} %slice.38), channel_id=1, source_target_pairs={{0,2},{1,3},{2,0},{3,1},{4,6},{5,7},{6,4},{7,5},{8,10},{9,11},{10,... | collective-permute-start | bytes 983048 | tf_op jit(solution)/shard_map/ppermute | solution.py:345
  77.4 5.1 %collective-permute-start.13 = (bf16[160,1024]{1,0:T(8,128)(2,1)S(1)}, bf16[160,1024]{1,0:T(8,128)(2,1)S(1)}, u32[]{:S(2)}, u32[]{:S(2)}) collective-permute-start(bf16[160,1024]{1,0:T(8,128)(2,1)S(1)} %collective-permute-done.9.refs_0_), channel_id=1, source_target_pairs={{0,1},{1,0},{2,3},{3,2},{4,5},{5,4},{6,7},{7,6},{8,9},{9,8},{10,11... | collective-permute-start | bytes 983048 | tf_op jit(solution)/shard_map/ppermute | solution.py:334
  87.0 20.5 %collective-permute-start.17 = (bf16[512,768]{1,0:T(8,128)(2,1)S(1)}, bf16[512,768]{1,0:T(8,128)(2,1)S(1)}, u32[]{:S(2)}, u32[]{:S(2)}) collective-permute-start(bf16[512,768]{1,0:T(8,128)(2,1)S(1)} %get-tuple-element.82.refs_0_), channel_id=1, source_target_pairs={{0,4},{1,5},{2,6},{3,7},{4,8},{5,9},{6,10},{7,11},{8,12},{9,13},{1... | collective-permute-start | bytes 2359304 | tf_op jit(solution)/shard_map/ppermute | solution.py:338
  87.1 20.4 %collective-permute-start.18 = (bf16[512,768]{1,0:T(8,128)(2,1)S(1)}, bf16[512,768]{1,0:T(8,128)(2,1)S(1)}, u32[]{:S(2)}, u32[]{:S(2)}) collective-permute-start(bf16[512,768]{1,0:T(8,128)(2,1)S(1)} %get-tuple-element.82.refs_0_), channel_id=1, source_target_pairs={{0,2},{1,3},{2,0},{3,1},{4,6},{5,7},{6,4},{7,5},{8,10},{9,11},{10,... | collective-permute-start | bytes 2359304 | tf_op jit(solution)/shard_map/ppermute | solution.py:338
  107.5 19.5 %collective-permute-start.19 = (bf16[512,768]{1,0:T(8,128)(2,1)S(1)}, bf16[512,768]{1,0:T(8,128)(2,1)S(1)}, u32[]{:S(2)}, u32[]{:S(2)}) collective-permute-start(bf16[512,768]{1,0:T(8,128)(2,1)S(1)} %collective-permute-done.17.refs_2_), channel_id=1, source_target_pairs={{0,4},{1,5},{2,6},{3,7},{4,8},{5,9},{6,10},{7,11},{8,12},{9,13},{1... | collective-permute-start | bytes 2359304 | tf_op jit(solution)/shard_map/ppermute | solution.py:338
  107.5 19.5 %collective-permute-start.20 = (bf16[512,768]{1,0:T(8,128)(2,1)S(1)}, bf16[512,768]{1,0:T(8,128)(2,1)}, u32[]{:S(2)}, u32[]{:S(2)}) collective-permute-start(bf16[512,768]{1,0:T(8,128)(2,1)S(1)} %collective-permute-done.17.refs_2_), channel_id=1, source_target_pairs={{0,2},{1,3},{2,0},{3,1},{4,6},{5,7},{6,4},{7,5},{8,10},{9,11},{10,... | collective-permute-start | bytes 2359304 | tf_op jit(solution)/shard_map/ppermute | solution.py:338
  127.0 18.7 %collective-permute-start.21 = (bf16[512,768]{1,0:T(8,128)(2,1)S(1)}, bf16[512,768]{1,0:T(8,128)(2,1)}, u32[]{:S(2)}, u32[]{:S(2)}) collective-permute-start(bf16[512,768]{1,0:T(8,128)(2,1)S(1)} %collective-permute-done.19.refs_6_), channel_id=1, source_target_pairs={{0,4},{1,5},{2,6},{3,7},{4,8},{5,9},{6,10},{7,11},{8,12},{9,13},{1... | collective-permute-start | bytes 2359304 | tf_op jit(solution)/shard_map/ppermute | solution.py:338
  127.0 22.7 %collective-permute-start.22 = (bf16[512,768]{1,0:T(8,128)(2,1)S(1)}, bf16[512,768]{1,0:T(8,128)(2,1)}, u32[]{:S(2)}, u32[]{:S(2)}) collective-permute-start(bf16[512,768]{1,0:T(8,128)(2,1)S(1)} %collective-permute-done.19.refs_6_), channel_id=1, source_target_pairs={{0,2},{1,3},{2,0},{3,1},{4,6},{5,7},{6,4},{7,5},{8,10},{9,11},{10,... | collective-permute-start | bytes 2359304 | tf_op jit(solution)/shard_map/ppermute | solution.py:338
  127.4 24.9 %collective-permute-start.30 = (bf16[512,768]{1,0:T(8,128)(2,1)S(1)}, bf16[512,768]{1,0:T(8,128)(2,1)S(1)}, u32[]{:S(2)}, u32[]{:S(2)}) collective-permute-start(bf16[512,768]{1,0:T(8,128)(2,1)S(1)} %get-tuple-element.82.refs_0_), channel_id=1, source_target_pairs={{0,1},{1,0},{2,3},{3,2},{4,5},{5,4},{6,7},{7,6},{8,9},{9,8},{10,11... | collective-permute-start | bytes 2359304 | tf_op jit(solution)/shard_map/ppermute | solution.py:334
  130.9 22.3 %collective-permute-start.31 = (bf16[512,768]{1,0:T(8,128)(2,1)S(1)}, bf16[512,768]{1,0:T(8,128)(2,1)S(1)}, u32[]{:S(2)}, u32[]{:S(2)}) collective-permute-start(bf16[512,768]{1,0:T(8,128)(2,1)S(1)} %collective-permute-done.17.refs_2_), channel_id=1, source_target_pairs={{0,1},{1,0},{2,3},{3,2},{4,5},{5,4},{6,7},{7,6},{8,9},{9,8},{10,11... | collective-permute-start | bytes 2359304 | tf_op jit(solution)/shard_map/ppermute | solution.py:334
  131.8 22.6 %collective-permute-start.32 = (bf16[512,768]{1,0:T(8,128)(2,1)S(1)}, bf16[512,768]{1,0:T(8,128)(2,1)S(1)}, u32[]{:S(2)}, u32[]{:S(2)}) collective-permute-start(bf16[512,768]{1,0:T(8,128)(2,1)S(1)} %collective-permute-done.18.refs_4_), channel_id=1, source_target_pairs={{0,1},{1,0},{2,3},{3,2},{4,5},{5,4},{6,7},{7,6},{8,9},{9,8},{10,11... | collective-permute-start | bytes 2359304 | tf_op jit(solution)/shard_map/ppermute | solution.py:334
  145.6 9.9 %collective-permute-start.33 = (bf16[512,768]{1,0:T(8,128)(2,1)S(1)}, bf16[512,768]{1,0:T(8,128)(2,1)S(1)}, u32[]{:S(2)}, u32[]{:S(2)}) collective-permute-start(bf16[512,768]{1,0:T(8,128)(2,1)S(1)} %collective-permute-done.19.refs_6_), channel_id=1, source_target_pairs={{0,1},{1,0},{2,3},{3,2},{4,5},{5,4},{6,7},{7,6},{8,9},{9,8},{10,11... | collective-permute-start | bytes 2359304 | tf_op jit(solution)/shard_map/ppermute | solution.py:334
  150.7 10.9 %collective-permute-start.37 = (bf16[256,768]{1,0:T(8,128)(2,1)S(1)}, bf16[256,768]{1,0:T(8,128)(2,1)S(1)}, u32[]{:S(2)}, u32[]{:S(2)}) collective-permute-start(bf16[256,768]{1,0:T(8,128)(2,1)S(1)} %slice.40), channel_id=1, source_target_pairs={{0,2},{1,3},{2,0},{3,1},{4,6},{5,7},{6,4},{7,5},{8,10},{9,11},{10,... | collective-permute-start | bytes 1179656 | tf_op jit(solution)/shard_map/ppermute | solution.py:345
  153.2 12.3 %collective-permute-start.38 = (bf16[256,768]{1,0:T(8,128)(2,1)S(1)}, bf16[256,768]{1,0:T(8,128)(2,1)}, u32[]{:S(2)}, u32[]{:S(2)}) collective-permute-start(bf16[256,768]{1,0:T(8,128)(2,1)S(1)} %slice.41), channel_id=1, source_target_pairs={{0,4},{1,5},{2,6},{3,7},{4,8},{5,9},{6,10},{7,11},{8,12},{9,13},{1... | collective-permute-start | bytes 1179656 | tf_op jit(solution)/shard_map/ppermute | solution.py:346
  154.1 21.0 %collective-permute-start.34 = (bf16[512,768]{1,0:T(8,128)(2,1)}, bf16[512,768]{1,0:T(8,128)(2,1)}, u32[]{:S(2)}, u32[]{:S(2)}) collective-permute-start(bf16[512,768]{1,0:T(8,128)(2,1)} %collective-permute-done.20.refs_8_), channel_id=1, source_target_pairs={{0,1},{1,0},{2,3},{3,2},{4,5},{5,4},{6,7},{7,6},{8,9},{9,8},{10,11... | collective-permute-start | bytes 2359304 | tf_op jit(solution)/shard_map/ppermute | solution.py:334
  155.3 19.9 %collective-permute-start.35 = (bf16[512,768]{1,0:T(8,128)(2,1)}, bf16[512,768]{1,0:T(8,128)(2,1)}, u32[]{:S(2)}, u32[]{:S(2)}) collective-permute-start(bf16[512,768]{1,0:T(8,128)(2,1)} %collective-permute-done.21.refs_10_), channel_id=1, source_target_pairs={{0,1},{1,0},{2,3},{3,2},{4,5},{5,4},{6,7},{7,6},{8,9},{9,8},{10,11... | collective-permute-start | bytes 2359304 | tf_op jit(solution)/shard_map/ppermute | solution.py:334
  156.4 18.9 %collective-permute-start.36 = (bf16[512,768]{1,0:T(8,128)(2,1)}, bf16[512,768]{1,0:T(8,128)(2,1)}, u32[]{:S(2)}, u32[]{:S(2)}) collective-permute-start(bf16[512,768]{1,0:T(8,128)(2,1)} %collective-permute-done.22.refs_12_), channel_id=1, source_target_pairs={{0,1},{1,0},{2,3},{3,2},{4,5},{5,4},{6,7},{7,6},{8,9},{9,8},{10,11... | collective-permute-start | bytes 2359304 | tf_op jit(solution)/shard_map/ppermute | solution.py:334
  161.7 9.0 %collective-permute-start.24 = (bf16[512,256]{1,0:T(8,128)(2,1)S(1)}, bf16[512,256]{1,0:T(8,128)(2,1)S(1)}, u32[]{:S(2)}, u32[]{:S(2)}) collective-permute-start(bf16[512,256]{1,0:T(8,128)(2,1)S(1)} %get-tuple-element.86.refs_0_), channel_id=1, source_target_pairs={{0,4},{1,5},{2,6},{3,7},{4,8},{5,9},{6,10},{7,11},{8,12},{9,13},{1... | collective-permute-start | bytes 786440 | tf_op jit(solution)/shard_map/ppermute | solution.py:338
  165.5 6.7 %collective-permute-start.25 = (bf16[512,256]{1,0:T(8,128)(2,1)S(1)}, bf16[512,256]{1,0:T(8,128)(2,1)S(1)}, u32[]{:S(2)}, u32[]{:S(2)}) collective-permute-start(bf16[512,256]{1,0:T(8,128)(2,1)S(1)} %get-tuple-element.86.refs_0_), channel_id=1, source_target_pairs={{0,2},{1,3},{2,0},{3,1},{4,6},{5,7},{6,4},{7,5},{8,10},{9,11},{10,... | collective-permute-start | bytes 786440 | tf_op jit(solution)/shard_map/ppermute | solution.py:338
  170.6 5.7 %collective-permute-start.39 = (bf16[256,768]{1,0:T(8,128)(2,1)S(1)}, bf16[256,768]{1,0:T(8,128)(2,1)}, u32[]{:S(2)}, u32[]{:S(2)}) collective-permute-start(bf16[256,768]{1,0:T(8,128)(2,1)S(1)} %collective-permute-done.37.refs_14_), channel_id=1, source_target_pairs={{0,1},{1,0},{2,3},{3,2},{4,5},{5,4},{6,7},{7,6},{8,9},{9,8},{10,11... | collective-permute-start | bytes 1179656 | tf_op jit(solution)/shard_map/ppermute | solution.py:334
  175.1 77.5 %collective-permute-start.23 = (bf16[512,256]{1,0:T(8,128)(2,1)}, bf16[512,256]{1,0:T(8,128)(2,1)S(1)}, u32[]{:S(2)}, u32[]{:S(2)}) collective-permute-start(bf16[512,256]{1,0:T(8,128)(2,1)} %copy-done.26), channel_id=1, source_target_pairs={{0,1},{1,0},{2,3},{3,2},{4,5},{5,4},{6,7},{7,6},{8,9},{9,8},{10,11... | collective-permute-start | bytes 786440 | tf_op jit(solution)/shard_map/ppermute | solution.py:334
  175.2 38.6 %collective-permute-start.28 = (bf16[512,256]{1,0:T(8,128)(2,1)}, bf16[512,256]{1,0:T(8,128)(2,1)S(1)}, u32[]{:S(2)}, u32[]{:S(2)}) collective-permute-start(bf16[512,256]{1,0:T(8,128)(2,1)} %copy-done.28), channel_id=1, source_target_pairs={{0,4},{1,5},{2,6},{3,7},{4,8},{5,9},{6,10},{7,11},{8,12},{9,13},{1... | collective-permute-start | bytes 786440 | tf_op jit(solution)/shard_map/ppermute | solution.py:338
  175.3 38.6 %collective-permute-start.29 = (bf16[512,256]{1,0:T(8,128)(2,1)}, bf16[512,256]{1,0:T(8,128)(2,1)S(1)}, u32[]{:S(2)}, u32[]{:S(2)}) collective-permute-start(bf16[512,256]{1,0:T(8,128)(2,1)} %copy-done.28), channel_id=1, source_target_pairs={{0,2},{1,3},{2,0},{3,1},{4,6},{5,7},{6,4},{7,5},{8,10},{9,11},{10,... | collective-permute-start | bytes 786440 | tf_op jit(solution)/shard_map/ppermute | solution.py:338
  176.4 76.4 %collective-permute-start.26 = (bf16[512,256]{1,0:T(8,128)(2,1)}, bf16[512,256]{1,0:T(8,128)(2,1)S(1)}, u32[]{:S(2)}, u32[]{:S(2)}) collective-permute-start(bf16[512,256]{1,0:T(8,128)(2,1)} %copy-done.28), channel_id=1, source_target_pairs={{0,1},{1,0},{2,3},{3,2},{4,5},{5,4},{6,7},{7,6},{8,9},{9,8},{10,11... | collective-permute-start | bytes 786440 | tf_op jit(solution)/shard_map/ppermute | solution.py:334
  213.9 36.7 %collective-permute-start.43 = (bf16[512,256]{1,0:T(8,128)(2,1)S(1)}, bf16[512,256]{1,0:T(8,128)(2,1)S(1)}, u32[]{:S(2)}, u32[]{:S(2)}) collective-permute-start(bf16[512,256]{1,0:T(8,128)(2,1)S(1)} %collective-permute-done.28.refs_6_), channel_id=1, source_target_pairs={{0,4},{1,5},{2,6},{3,7},{4,8},{5,9},{6,10},{7,11},{8,12},{9,13},{1... | collective-permute-start | bytes 786440 | tf_op jit(solution)/shard_map/ppermute | solution.py:338
  224.4 26.2 %collective-permute-start.44 = (bf16[512,256]{1,0:T(8,128)(2,1)S(1)}, bf16[512,256]{1,0:T(8,128)(2,1)S(1)}, u32[]{:S(2)}, u32[]{:S(2)}) collective-permute-start(bf16[512,256]{1,0:T(8,128)(2,1)S(1)} %collective-permute-done.28.refs_6_), channel_id=1, source_target_pairs={{0,2},{1,3},{2,0},{3,1},{4,6},{5,7},{6,4},{7,5},{8,10},{9,11},{10,... | collective-permute-start | bytes 786440 | tf_op jit(solution)/shard_map/ppermute | solution.py:338
  250.6 4.5 %collective-permute-start.47 = (bf16[256,256]{1,0:T(8,128)(2,1)S(1)}, bf16[256,256]{1,0:T(8,128)(2,1)S(1)}, u32[]{:S(2)}, u32[]{:S(2)}) collective-permute-start(bf16[256,256]{1,0:T(8,128)(2,1)S(1)} %slice.42), channel_id=1, source_target_pairs={{0,2},{1,3},{2,0},{3,1},{4,6},{5,7},{6,4},{7,5},{8,10},{9,11},{10,... | collective-permute-start | bytes 393224 | tf_op jit(solution)/shard_map/ppermute | solution.py:345
  251.6 6.8 %collective-permute-start.48 = (bf16[256,256]{1,0:T(8,128)(2,1)S(1)}, bf16[256,256]{1,0:T(8,128)(2,1)S(1)}, u32[]{:S(2)}, u32[]{:S(2)}) collective-permute-start(bf16[256,256]{1,0:T(8,128)(2,1)S(1)} %slice.43), channel_id=1, source_target_pairs={{0,4},{1,5},{2,6},{3,7},{4,8},{5,9},{6,10},{7,11},{8,12},{9,13},{1... | collective-permute-start | bytes 393224 | tf_op jit(solution)/shard_map/ppermute | solution.py:346
  251.7 33.5 %collective-permute-start.27 = (bf16[512,256]{1,0:T(8,128)(2,1)S(1)}, bf16[512,256]{1,0:T(8,128)(2,1)S(1)}, u32[]{:S(2)}, u32[]{:S(2)}) collective-permute-start(bf16[512,256]{1,0:T(8,128)(2,1)S(1)} %copy-done.31), channel_id=1, source_target_pairs={{0,1},{1,0},{2,3},{3,2},{4,5},{5,4},{6,7},{7,6},{8,9},{9,8},{10,11... | collective-permute-start | bytes 786440 | tf_op jit(solution)/shard_map/ppermute | solution.py:334
  252.7 32.6 %collective-permute-start.41 = (bf16[512,256]{1,0:T(8,128)(2,1)S(1)}, bf16[512,256]{1,0:T(8,128)(2,1)S(1)}, u32[]{:S(2)}, u32[]{:S(2)}) collective-permute-start(bf16[512,256]{1,0:T(8,128)(2,1)S(1)} %collective-permute-done.28.refs_6_), channel_id=1, source_target_pairs={{0,1},{1,0},{2,3},{3,2},{4,5},{5,4},{6,7},{7,6},{8,9},{9,8},{10,11... | collective-permute-start | bytes 786440 | tf_op jit(solution)/shard_map/ppermute | solution.py:334
  252.7 33.0 %collective-permute-start.42 = (bf16[512,256]{1,0:T(8,128)(2,1)S(1)}, bf16[512,256]{1,0:T(8,128)(2,1)S(1)}, u32[]{:S(2)}, u32[]{:S(2)}) collective-permute-start(bf16[512,256]{1,0:T(8,128)(2,1)S(1)} %collective-permute-done.29.refs_8_), channel_id=1, source_target_pairs={{0,1},{1,0},{2,3},{3,2},{4,5},{5,4},{6,7},{7,6},{8,9},{9,8},{10,11... | collective-permute-start | bytes 786440 | tf_op jit(solution)/shard_map/ppermute | solution.py:334
  255.1 31.7 %collective-permute-start.45 = (bf16[512,256]{1,0:T(8,128)(2,1)S(1)}, bf16[512,256]{1,0:T(8,128)(2,1)S(1)}, u32[]{:S(2)}, u32[]{:S(2)}) collective-permute-start(bf16[512,256]{1,0:T(8,128)(2,1)S(1)} %collective-permute-done.43.refs_10_), channel_id=1, source_target_pairs={{0,1},{1,0},{2,3},{3,2},{4,5},{5,4},{6,7},{7,6},{8,9},{9,8},{10,11... | collective-permute-start | bytes 786440 | tf_op jit(solution)/shard_map/ppermute | solution.py:334
  258.4 28.4 %collective-permute-start.46 = (bf16[512,256]{1,0:T(8,128)(2,1)S(1)}, bf16[512,256]{1,0:T(8,128)(2,1)S(1)}, u32[]{:S(2)}, u32[]{:S(2)}) collective-permute-start(bf16[512,256]{1,0:T(8,128)(2,1)S(1)} %collective-permute-done.44.refs_12_), channel_id=1, source_target_pairs={{0,1},{1,0},{2,3},{3,2},{4,5},{5,4},{6,7},{7,6},{8,9},{9,8},{10,11... | collective-permute-start | bytes 786440 | tf_op jit(solution)/shard_map/ppermute | solution.py:334
  (42 other events, 403.3 us)

commit v5 on v4

--- a/solution.py
+++ b/solution.py
@@ -35,6 +35,11 @@
 def one_hot_rows(count, index_row):
     rows = lax.broadcasted_iota(jnp.int32, (count, index_row.shape[1]), 0)
     return (rows == index_row).astype(jnp.float32).astype(jnp.bfloat16)
+
+
+def split(number):
+    high = lax.shift_right_logical(number, HEAD_SIZE.bit_length() - 1)
+    return high, number - high * HEAD_SIZE
 
 
 def contract(left, right, left_dim, right_dim):
@@ -76,13 +81,13 @@
     bucket = jnp.where(beyond, hole.astype(jnp.int32), target * share + order)
     bucket_ref[...] = bucket
     seat_ref[...] = target * stride + order
-    high = lax.div(route, HEAD_SIZE)
-    place_high = lax.div(bucket, HEAD_SIZE)
+    high, low = split(route)
+    place_high, place_low = split(bucket)
     line = lax.broadcasted_iota(jnp.int32, (8, count), 0)
     digits = jnp.where(line == 0, high, 0)
-    digits = jnp.where(line == 1, route - high * HEAD_SIZE, digits)
+    digits = jnp.where(line == 1, low, digits)
     digits = jnp.where(line == 2, place_high, digits)
-    digits = jnp.where(line == 3, bucket - place_high * HEAD_SIZE, digits)
+    digits = jnp.where(line == 3, place_low, digits)
     digits = jnp.where(line == 4, 1, digits).astype(jnp.float32).astype(jnp.bfloat16)
     placed = contract(digits, one_hot_rows(count, bucket), 1, 1)
     sorted_ref[...] = (placed[0:1] * HEAD_SIZE + placed[1:2]).astype(jnp.int32)
@@ -100,12 +105,11 @@
     route = route_ref[...]
     count = route.shape[0]
     lines = positions_ref.shape[0]
-    line = lax.div(route, HEAD_SIZE)
-    lane = route - line * HEAD_SIZE
+    line, lane = split(route)
     pick = (lax.broadcasted_iota(jnp.int32, (count, lines), 1) == line).astype(jnp.float32)
     pick = pick.astype(jnp.bfloat16)
     positions = positions_ref[...]
-    half = lax.div(positions, 2)
+    half = lax.shift_right_logical(positions, 1)
     rest = positions - half * 2
     rows = 2.0 * contract(pick, half.astype(jnp.float32).astype(jnp.bfloat16), 1, 0) + contract(
         pick, rest.astype(jnp.float32).astype(jnp.bfloat16), 1, 0
@@ -120,8 +124,7 @@
     sine_ref[...] = sine
     seats = one_hot_rows(ranks * stride, seat_ref[...])
     first = route - spot.astype(jnp.int32)
-    first_line = lax.div(first, HEAD_SIZE)
-    first_lane = first - first_line * HEAD_SIZE
+    first_line, first_lane = split(first)
     digits = jnp.where(lanes == 0, line, 0)
     digits = jnp.where(lanes == 1, lane, digits)
     digits = jnp.where(lanes == 2, first_line, digits)
@@ -258,12 +261,10 @@
         (lines == more_ref[j * listed : (j + 1) * listed]).astype(jnp.float32).astype(jnp.bfloat16)
         for j in range(ranks)
     ]
-    row = lax.broadcasted_iota(jnp.int32, (ranks * listed, ranks * listed), 0)
-    column = lax.broadcasted_iota(jnp.int32, (ranks * listed, ranks * listed), 1)
-    group, rest = lax.div(row, listed), lax.rem(row, listed)
-    source, index = lax.div(rest, extra), lax.rem(rest, extra)
-    regroup = (column == source * listed + group * extra + index).astype(jnp.float32)
-    regroup = regroup.astype(jnp.bfloat16)
+    column = lax.broadcasted_iota(jnp.int32, (1, ranks * listed), 1)
+    source, rest = lax.div(column, listed), lax.rem(column, listed)
+    group, index = lax.div(rest, extra), lax.rem(rest, extra)
+    regroup = one_hot_rows(ranks * listed, group * listed + source * extra + index)
     for copy in copies:
         copy.wait()
     for part in range(2):
@@ -410,8 +411,6 @@
     )
     sending.send(())
     next(sending)
-    plan, bucket, seat = sending.send((plan, bucket, seat))
-    next(sending)
     all_positions = plan[:, width:].reshape(-1, HEAD_SIZE)
     owners = source_order(ranks)
     sources = plan[:, :width][owners]
@@ -440,7 +439,7 @@
         in_specs=[VMEM] * 5,
         out_specs=(VMEM,) * 4,
         scratch_shapes=[pltpu.VMEM((ranks * packed, HEAD_SIZE), jnp.float32)],
-        compiler_params=grant(32),
+        compiler_params=grant(20),
         cost_estimate=cost(4 * stride * ranks * rows * query_width, 4 * rows * query_width),
         name="turn_queries",
     )(
@@ -485,15 +484,16 @@
             in_specs=[SMEM] + [HBM] * (1 + len(arrays)) + [VMEM] * len(more),
             out_specs=VMEM,
             scratch_shapes=scratch(chips, arrays),
-            compiler_params=grant(28),
+            compiler_params=grant(16),
             cost_estimate=product_cost(chips),
             name="add_part",
         )(owners, hidden, *arrays, *more)
 
-    total = add_part(None, (0, 1, planes))
-    turned, bounds, cosine, sine, key_routes, more_places, total = sending.send(
-        (turned, bounds, cosine, sine, key_routes, more_places, total)
-    )
+    turned, bounds, cosine, sine, key_routes, more_places = sending.send(
+        (turned, bounds, cosine, sine, key_routes, more_places)
+    )
+    next(sending)
+    (total,) = sending.send((add_part(None, (0, 1, planes)),))
     next(sending)
     (total,) = sending.send((add_part(total, (2, planes + 1)),))
     total = add_part(total, (3, planes + 2))
@@ -507,7 +507,7 @@
         in_specs=[SMEM, HBM] + [VMEM] * 4 + [HBM] * len(arrays) + [VMEM],
         out_specs=(VMEM,) * len(CHUNKS),
         scratch_shapes=scratch(chips, arrays),
-        compiler_params=grant(28),
+        compiler_params=grant(16),
         cost_estimate=product_cost(chips),
         name="finish",
     )(
@@ -550,7 +550,7 @@
             + [pltpu.VMEM((packed, key_count), jnp.bfloat16)] * UNROLL
             + [pltpu.VMEM((packed, HEAD_SIZE), jnp.float32)] * UNROLL,
             input_output_aliases={len(fixed) + len(pieces): 0} if taken else {},
-            compiler_params=grant(28),
+            compiler_params=grant(16),
             cost_estimate=cost(
                 16 * rows * stride * ranks * span, 4 * ranks * rows * HEAD_SIZE
             ),

time: 315 us -> 320 us (1.016)
  local copies, waits for them, and re-layouts: 38.6 us -> 47.7 us
  waiting for transfers between devices: 92.6 us -> 88.8 us
    ppermute x9, waiting for transfers between devices: 72.3 us -> 60.9 us  [spread(): lax.ppermute(lane, 'dp', ring)]
    all_to_all x1, waiting for transfers between devices: 0.01 us -> 9.24 us  [gather_plan(): lax.all_to_all(jnp.broadcast_to(plan, (ranks, width + slots)), 'dp', spli...]
    reshape x3, local copies, waits for them, and re-layouts: 0.24 us -> 4.69 us  [gather_plan(): sources[:, :rows].reshape(ranks, ranks, share).transpose(1, 0, 2)]
    unnamed x78 -> x88, local copies, waits for them, and re-layouts: 25.9 us -> 29.9 us
    ppermute x27, starting transfers between devices: 25.5 us -> 22.1 us  [keep(): lax.ppermute(array, 'dp', beside)]
  transfers between devices with their start and end apart: 52 -> 52, of which waited for: 13 -> 14; matrix products, arithmetic and copies ran while one was open for 4% -> 6% of each run, Pallas kernels for 31% -> 31%
where the time goes in v5:
time: 320 us; the launch traced here: 316 us
  Pallas kernels  126 us (39%)
  waiting for transfers between devices  88.8 us (28%)
  starting transfers between devices  51 us (16%)
  local copies, waits for them, and re-layouts  47.7 us (15%)
    pallas_call x4, Pallas kernels, attend(): pl.pallas_call(functools.partial(attend_kernel, (first_head, place), head...  101 us
    ppermute x9, waiting for transfers between devices, spread(): lax.ppermute(lane, 'dp', ring)  60.9 us
    unnamed x88, local copies, waits for them, and re-layouts  29.9 us
    ppermute x27, starting transfers between devices, keep(): lax.ppermute(array, 'dp', beside)  22.1 us
    ppermute x9, starting transfers between devices, spread(): lax.ppermute(lane, 'dp', ring)  13.9 us
    pallas_call x3, Pallas kernels, add_part(): pl.pallas_call(functools.partial(part_kernel, chips, bool(more)), out_sha...  13 us
    ppermute x3, waiting for transfers between devices, spread(): around = lax.ppermute(other[half:], 'dp', ring)  10.5 us
    all_to_all x1, waiting for transfers between devices, gather_plan(): lax.all_to_all(jnp.broadcast_to(plan, (ranks, width + slots)), 'dp', spli...  9.24 us
  transfers between devices with their start and end apart: 52, of which 14 were waited for; matrix products, arithmetic and copies ran while one was open for 6% of the time, Pallas kernels for 31%

profile of v5, /device:TPU:1, one launch (start us, length us, event | category | flops | bytes accessed | tf_op | source)
XLA Modules:
  0.0 316.1 jit_solution(16838013546367211605)
XLA Ops:
  2.0 2.2 collective-permute-start
  4.2 1.2 collective-permute-start.1
  5.4 1.2 collective-permute-start.6
  9.5 4.0 %all-to-all-start = ((s32[16,1,1600]{2,1,0:T(1,128)}), s32[16,1,1600]{2,1,0:T(1,128)S(1)}, u32[]{:S(2)}, u32[]{:S(2)}) async-start(s32[16,1,1600]{2,1,0:T(1,128)} %broadcast_in_dim.4), calls=%async_computation | async-start | bytes 212992 | tf_op jit(solution)/shard_map/all_to_all | solution.py:409
  15.1 9.2 %all-to-all-done = s32[16,1,1600]{2,1,0:T(1,128)S(1)} async-done(((s32[16,1,1600]{2,1,0:T(1,128)}), s32[16,1,1600]{2,1,0:T(1,128)S(1)}, u32[]{:S(2)}, u32[]{:S(2)}) %all-to-all-start) | async-done | bytes 102432 | tf_op jit(solution)/shard_map/all_to_all | solution.py:409
  25.1 1.2 gather_fusion
  29.1 1.7 copy-done.27
  30.8 6.5 %turn_queries.1 = (bf16[4,2816,128]{2,1,0:T(8,128)(2,1)S(1)}, s32[2816,128]{1,0:T(8,128)S(1)}, f32[512,128]{1,0:T(8,128)S(1)}, f32[512,128]{1,0:T(8,128)S(1)}) custom-call(s32[512,1]{1,0:T(8,128)S(1)} %copy-done.24, s32[1,512]{1,0:T(1,128)S(1)} %get-tuple-element.52.seat_ref, s32[128,128]{1,0:T(8,128)S(1)} %copy-done.25, ...), custom_call_target="tpu_custom_call" | custom-call | flops 4026531840 | bytes 5242880 | tf_op jit(solution)/shard_map/turn_queries/pallas_call | solution.py:431
  42.1 1.5 reshape.173
  43.6 1.6 copy.35
  45.2 1.6 reshape.174
  47.5 1.4 copy.26
  55.4 2.5 copy-done
  57.9 5.4 %add_part.3.refs_4_ = f32[512,1024]{1,0:T(8,128)S(1)} custom-call(s32[16]{0:T(128)S(1)} %pad_add_fusion.1.owners_ref, bf16[512,5120]{1,0:T(8,128)(2,1)S(1)} %copy-done, bf16[320,1024]{1,0:T(8,128)(2,1)S(1)} %constant_dynamic-update-slice_fusion.refs_0_, bf16[320,1024]{1,0:T(8,128)(2,1)} %collective-permute-done.6.refs_1_, ...), custom_call_target="tpu_custom_call" | custom-call | flops 2013265920 | bytes 10092544 | tf_op jit(solution)/shard_map/add_part/pallas_call | solution.py:481
  63.4 6.3 %collective-permute-done.4.refs_0_ = bf16[320,1024]{1,0:T(8,128)(2,1)S(1)} collective-permute-done((bf16[320,1024]{1,0:T(8,128)(2,1)}, bf16[320,1024]{1,0:T(8,128)(2,1)S(1)}, u32[]{:S(2)}, u32[]{:S(2)}) %collective-permute-start.4) | collective-permute-done | bytes 655392 | tf_op jit(solution)/shard_map/ppermute | solution.py:339
  69.7 1.4 collective-permute-start.15
  72.6 4.1 %add_part.4.refs_4_ = f32[512,1024]{1,0:T(8,128)S(1)} custom-call(s32[16]{0:T(128)S(1)} %pad_add_fusion.1.owners_ref, bf16[512,5120]{1,0:T(8,128)(2,1)S(1)} %copy-done, bf16[320,1024]{1,0:T(8,128)(2,1)} %collective-permute-done.2.refs_0_, bf16[320,1024]{1,0:T(8,128)(2,1)S(1)} %collective-permute-done.11.refs_1_, ...), custom_call_target="tpu_custom_call" | custom-call | flops 1342177280 | bytes 8126464 | tf_op jit(solution)/shard_map/add_part/pallas_call | solution.py:481
  76.7 5.3 %collective-permute-done.10.refs_1_ = bf16[160,1024]{1,0:T(8,128)(2,1)S(1)} collective-permute-done((bf16[160,1024]{1,0:T(8,128)(2,1)S(1)}, bf16[160,1024]{1,0:T(8,128)(2,1)S(1)}, u32[]{:S(2)}, u32[]{:S(2)}) %collective-permute-start.10) | collective-permute-done | bytes 327712 | tf_op jit(solution)/shard_map/ppermute | solution.py:347
  82.0 1.4 collective-permute-start.13
  83.5 3.4 %add_part.5.refs_4_ = f32[512,1024]{1,0:T(8,128)S(1)} custom-call(s32[16]{0:T(128)S(1)} %pad_add_fusion.1.owners_ref, bf16[512,5120]{1,0:T(8,128)(2,1)S(1)} %copy-done, bf16[320,1024]{1,0:T(8,128)(2,1)S(1)} %collective-permute-done.4.refs_0_, bf16[320,1024]{1,0:T(8,128)(2,1)S(1)} %collective-permute-done.15.refs_1_, ...), custom_call_target="tpu_custom_call" | custom-call | flops 1342177280 | bytes 8126464 | tf_op jit(solution)/shard_map/add_part/pallas_call | solution.py:481
  87.0 4.5 %finish.1 = (bf16[512,768]{1,0:T(8,128)(2,1)S(1)}, bf16[512,256]{1,0:T(8,128)(2,1)S(1)}) custom-call(s32[16]{0:T(128)S(1)} %pad_add_fusion.1.owners_ref, bf16[512,5120]{1,0:T(8,128)(2,1)S(1)} %bitcast.22, f32[1,1024]{1,0:T(1,128)S(1)} %maximum_convert_fusion.bias_ref, f32[512,128]{1,0:T(8,128)S(1)} %copy-done.21, f32[512,128]{1,0:T(8,128)S(1)} %copy-done.23, ...), custom_call_target="tpu_custom_call" | custom-call | flops 671088640 | bytes 6160384 | tf_op jit(solution)/shard_map/finish/pallas_call | solution.py:502
  92.6 19.3 %collective-permute-done.17.refs_2_ = bf16[512,768]{1,0:T(8,128)(2,1)S(1)} collective-permute-done((bf16[512,768]{1,0:T(8,128)(2,1)S(1)}, bf16[512,768]{1,0:T(8,128)(2,1)S(1)}, u32[]{:S(2)}, u32[]{:S(2)}) %collective-permute-start.17) | collective-permute-done | bytes 786464 | tf_op jit(solution)/shard_map/ppermute | solution.py:339
  113.0 18.4 %collective-permute-done.19.refs_6_ = bf16[512,768]{1,0:T(8,128)(2,1)S(1)} collective-permute-done((bf16[512,768]{1,0:T(8,128)(2,1)S(1)}, bf16[512,768]{1,0:T(8,128)(2,1)S(1)}, u32[]{:S(2)}, u32[]{:S(2)}) %collective-permute-start.19) | collective-permute-done | bytes 786464 | tf_op jit(solution)/shard_map/ppermute | solution.py:339
  132.4 2.6 collective-permute-start.30
  138.3 11.7 %collective-permute-done.21.refs_10_ = bf16[512,768]{1,0:T(8,128)(2,1)} collective-permute-done((bf16[512,768]{1,0:T(8,128)(2,1)S(1)}, bf16[512,768]{1,0:T(8,128)(2,1)}, u32[]{:S(2)}, u32[]{:S(2)}) %collective-permute-start.21) | collective-permute-done | bytes 786464 | tf_op jit(solution)/shard_map/ppermute | solution.py:339
  150.1 3.2 %collective-permute-start.33 = (bf16[512,768]{1,0:T(8,128)(2,1)S(1)}, bf16[512,768]{1,0:T(8,128)(2,1)S(1)}, u32[]{:S(2)}, u32[]{:S(2)}) collective-permute-start(bf16[512,768]{1,0:T(8,128)(2,1)S(1)} %collective-permute-done.19.refs_6_), channel_id=1, source_target_pairs={{0,1},{1,0},{2,3},{3,2},{4,5},{5,4},{6,7},{7,6},{8,9},{9,8},{10,11... | collective-permute-start | bytes 2359304 | tf_op jit(solution)/shard_map/ppermute | solution.py:335
  161.7 4.4 %collective-permute-done.37.refs_14_ = bf16[256,768]{1,0:T(8,128)(2,1)S(1)} collective-permute-done((bf16[256,768]{1,0:T(8,128)(2,1)S(1)}, bf16[256,768]{1,0:T(8,128)(2,1)S(1)}, u32[]{:S(2)}, u32[]{:S(2)}) %collective-permute-start.37) | collective-permute-done | bytes 393248 | tf_op jit(solution)/shard_map/ppermute | solution.py:346
  166.1 4.4 %collective-permute-done.38.refs_15_ = bf16[256,768]{1,0:T(8,128)(2,1)} collective-permute-done((bf16[256,768]{1,0:T(8,128)(2,1)S(1)}, bf16[256,768]{1,0:T(8,128)(2,1)}, u32[]{:S(2)}, u32[]{:S(2)}) %collective-permute-start.38) | collective-permute-done | bytes 393248 | tf_op jit(solution)/shard_map/ppermute | solution.py:347
  170.9 5.2 %collective-permute-done.24.refs_2_ = bf16[512,256]{1,0:T(8,128)(2,1)S(1)} collective-permute-done((bf16[512,256]{1,0:T(8,128)(2,1)S(1)}, bf16[512,256]{1,0:T(8,128)(2,1)S(1)}, u32[]{:S(2)}, u32[]{:S(2)}) %collective-permute-start.24) | collective-permute-done | bytes 262176 | tf_op jit(solution)/shard_map/ppermute | solution.py:339
  177.9 2.1 collective-permute-start.40
  181.6 1.4 copy-done.2
  183.0 1.1 copy-done.4
  184.1 1.1 copy-done.6
  185.3 1.1 copy-done.8
  186.4 1.1 copy-done.10
  187.5 1.1 copy-done.12
  188.7 1.1 copy-done.14
  189.8 1.1 copy-done.16
  190.9 1.1 copy-done.18
  192.9 25.6 %attend.4.refs_18_ = bf16[512,2560]{1,0:T(8,128)(2,1)} custom-call(bf16[4,2816,128]{2,1,0:T(8,128)(2,1)S(1)} %get-tuple-element.59.queries_ref, s32[2816,128]{1,0:T(8,128)S(1)} %copy-done.2, s32[16,1,544]{2,1,0:T(1,128)S(1)} %copy-done.19, s32[1,512]{1,0:T(1,128)S(1)} %get-tuple-element.52.seat_ref, s32[512,1]{1,0:T(8,128)S(1)} %copy.31.more_ref, ...), custom_call_target="tpu_custom_call" | custom-call | flops 4026531840 | bytes 4194304 | tf_op jit(solution)/shard_map/attend/pallas_call | solution.py:534
  218.5 10.4 %collective-permute-start.43 = (bf16[512,256]{1,0:T(8,128)(2,1)S(1)}, bf16[512,256]{1,0:T(8,128)(2,1)S(1)}, u32[]{:S(2)}, u32[]{:S(2)}) collective-permute-start(bf16[512,256]{1,0:T(8,128)(2,1)S(1)} %collective-permute-done.28.refs_6_), channel_id=1, source_target_pairs={{0,4},{1,5},{2,6},{3,7},{4,8},{5,9},{6,10},{7,11},{8,12},{9,13},{1... | collective-permute-start | bytes 786440 | tf_op jit(solution)/shard_map/ppermute | solution.py:339
  229.8 25.6 %attend.5.refs_18_ = bf16[512,2560]{1,0:T(8,128)(2,1)} custom-call(bf16[4,2816,128]{2,1,0:T(8,128)(2,1)S(1)} %get-tuple-element.59.queries_ref, s32[2816,128]{1,0:T(8,128)S(1)} %copy-done.2, s32[16,1,544]{2,1,0:T(1,128)S(1)} %copy-done.19, s32[1,512]{1,0:T(1,128)S(1)} %get-tuple-element.52.seat_ref, ...), custom_call_target="tpu_custom_call", output_to_operand_aliasing={{}: (23, {})} | custom-call | flops 4026531840 | bytes 4194304 | tf_op jit(solution)/shard_map/attend/pallas_call | solution.py:534
  256.2 1.1 collective-permute-start.27
  257.8 2.5 collective-permute-done.47.refs_14_
  260.3 1.1 collective-permute-start.45
  262.2 1.8 collective-permute-start.46
  264.0 25.6 %attend.6.refs_18_ = bf16[512,2560]{1,0:T(8,128)(2,1)} custom-call(bf16[4,2816,128]{2,1,0:T(8,128)(2,1)S(1)} %get-tuple-element.59.queries_ref, s32[2816,128]{1,0:T(8,128)S(1)} %copy-done.2, s32[16,1,544]{2,1,0:T(1,128)S(1)} %copy-done.19, s32[1,512]{1,0:T(1,128)S(1)} %get-tuple-element.52.seat_ref, ...), custom_call_target="tpu_custom_call", output_to_operand_aliasing={{}: (23, {})} | custom-call | flops 4026531840 | bytes 4194304 | tf_op jit(solution)/shard_map/attend/pallas_call | solution.py:534
  291.2 24.8 %attend.7 = bf16[512,2560]{1,0:T(8,128)(2,1)} custom-call(bf16[4,2816,128]{2,1,0:T(8,128)(2,1)S(1)} %get-tuple-element.59.queries_ref, s32[2816,128]{1,0:T(8,128)S(1)} %copy-done.2, s32[16,1,544]{2,1,0:T(1,128)S(1)} %copy-done.19, s32[1,512]{1,0:T(1,128)S(1)} %get-tuple-element.52.seat_ref, ...), custom_call_target="tpu_custom_call", output_to_operand_aliasing={{}: (23, {})} | custom-call | flops 4026531840 | bytes 4194304 | tf_op jit(solution)/shard_map/attend/pallas_call | solution.py:534
  (192 shorter events, 47.6 us)
Async XLA Ops:
  2.0 24.2 %collective-permute-start = (bf16[320,1024]{1,0:T(8,128)(2,1)S(1)}, bf16[320,1024]{1,0:T(8,128)(2,1)}, u32[]{:S(2)}, u32[]{:S(2)}) collective-permute-start(bf16[320,1024]{1,0:T(8,128)(2,1)S(1)} %constant_dynamic-update-slice_fusion.refs_0_), channel_id=1, source_target_pairs={{0,4},{1,5},{2,6},{3,7},{4,8},{5,9},{6,10},{7,11},{8,12},{9,13},{1... | collective-permute-start | bytes 1966088 | tf_op jit(solution)/shard_map/ppermute | solution.py:339
  4.2 22.1 %collective-permute-start.1 = (bf16[320,1024]{1,0:T(8,128)(2,1)S(1)}, bf16[320,1024]{1,0:T(8,128)(2,1)}, u32[]{:S(2)}, u32[]{:S(2)}) collective-permute-start(bf16[320,1024]{1,0:T(8,128)(2,1)S(1)} %constant_dynamic-update-slice_fusion.refs_0_), channel_id=1, source_target_pairs={{0,2},{1,3},{2,0},{3,1},{4,6},{5,7},{6,4},{7,5},{8,10},{9,11},{10,... | collective-permute-start | bytes 1966088 | tf_op jit(solution)/shard_map/ppermute | solution.py:339
  5.4 48.1 %collective-permute-start.6 = (bf16[320,1024]{1,0:T(8,128)(2,1)S(1)}, bf16[320,1024]{1,0:T(8,128)(2,1)}, u32[]{:S(2)}, u32[]{:S(2)}) collective-permute-start(bf16[320,1024]{1,0:T(8,128)(2,1)S(1)} %constant_dynamic-update-slice_fusion.refs_0_), channel_id=1, source_target_pairs={{0,1},{1,0},{2,3},{3,2},{4,5},{5,4},{6,7},{7,6},{8,9},{9,8},{10,11... | collective-permute-start | bytes 1966088 | tf_op jit(solution)/shard_map/ppermute | solution.py:335
  9.5 14.8 %all-to-all-start = ((s32[16,1,1600]{2,1,0:T(1,128)}), s32[16,1,1600]{2,1,0:T(1,128)S(1)}, u32[]{:S(2)}, u32[]{:S(2)}) async-start(s32[16,1,1600]{2,1,0:T(1,128)} %broadcast_in_dim.4), calls=%async_computation | async-start | bytes 212992 | tf_op jit(solution)/shard_map/all_to_all | solution.py:409
  26.3 25.6 %collective-permute-start.2 = (bf16[320,1024]{1,0:T(8,128)(2,1)}, bf16[320,1024]{1,0:T(8,128)(2,1)}, u32[]{:S(2)}, u32[]{:S(2)}) collective-permute-start(bf16[320,1024]{1,0:T(8,128)(2,1)} %collective-permute-done.refs_2_), channel_id=1, source_target_pairs={{0,4},{1,5},{2,6},{3,7},{4,8},{5,9},{6,10},{7,11},{8,12},{9,13},{1... | collective-permute-start | bytes 1966088 | tf_op jit(solution)/shard_map/ppermute | solution.py:339
  26.8 25.0 %collective-permute-start.3 = (bf16[320,1024]{1,0:T(8,128)(2,1)}, bf16[320,1024]{1,0:T(8,128)(2,1)}, u32[]{:S(2)}, u32[]{:S(2)}) collective-permute-start(bf16[320,1024]{1,0:T(8,128)(2,1)} %collective-permute-done.refs_2_), channel_id=1, source_target_pairs={{0,2},{1,3},{2,0},{3,1},{4,6},{5,7},{6,4},{7,5},{8,10},{9,11},{10,... | collective-permute-start | bytes 1966088 | tf_op jit(solution)/shard_map/ppermute | solution.py:339
  39.9 14.7 %collective-permute-start.7 = (bf16[320,1024]{1,0:T(8,128)(2,1)}, bf16[320,1024]{1,0:T(8,128)(2,1)}, u32[]{:S(2)}, u32[]{:S(2)}) collective-permute-start(bf16[320,1024]{1,0:T(8,128)(2,1)} %collective-permute-done.refs_2_), channel_id=1, source_target_pairs={{0,1},{1,0},{2,3},{3,2},{4,5},{5,4},{6,7},{7,6},{8,9},{9,8},{10,11... | collective-permute-start | bytes 1966088 | tf_op jit(solution)/shard_map/ppermute | solution.py:335
  40.8 14.6 %collective-permute-start.8 = (bf16[320,1024]{1,0:T(8,128)(2,1)}, bf16[320,1024]{1,0:T(8,128)(2,1)}, u32[]{:S(2)}, u32[]{:S(2)}) collective-permute-start(bf16[320,1024]{1,0:T(8,128)(2,1)} %collective-permute-done.1.refs_4_), channel_id=1, source_target_pairs={{0,1},{1,0},{2,3},{3,2},{4,5},{5,4},{6,7},{7,6},{8,9},{9,8},{10,11... | collective-permute-start | bytes 1966088 | tf_op jit(solution)/shard_map/ppermute | solution.py:335
  51.8 17.8 %collective-permute-start.4 = (bf16[320,1024]{1,0:T(8,128)(2,1)}, bf16[320,1024]{1,0:T(8,128)(2,1)S(1)}, u32[]{:S(2)}, u32[]{:S(2)}) collective-permute-start(bf16[320,1024]{1,0:T(8,128)(2,1)} %collective-permute-done.2.refs_0_), channel_id=1, source_target_pairs={{0,4},{1,5},{2,6},{3,7},{4,8},{5,9},{6,10},{7,11},{8,12},{9,13},{1... | collective-permute-start | bytes 1966088 | tf_op jit(solution)/shard_map/ppermute | solution.py:339
  52.5 17.2 %collective-permute-start.5 = (bf16[320,1024]{1,0:T(8,128)(2,1)}, bf16[320,1024]{1,0:T(8,128)(2,1)S(1)}, u32[]{:S(2)}, u32[]{:S(2)}) collective-permute-start(bf16[320,1024]{1,0:T(8,128)(2,1)} %collective-permute-done.2.refs_0_), channel_id=1, source_target_pairs={{0,2},{1,3},{2,0},{3,1},{4,6},{5,7},{6,4},{7,5},{8,10},{9,11},{10,... | collective-permute-start | bytes 1966088 | tf_op jit(solution)/shard_map/ppermute | solution.py:339
  53.5 17.9 %collective-permute-start.11 = (bf16[320,1024]{1,0:T(8,128)(2,1)}, bf16[320,1024]{1,0:T(8,128)(2,1)S(1)}, u32[]{:S(2)}, u32[]{:S(2)}) collective-permute-start(bf16[320,1024]{1,0:T(8,128)(2,1)} %collective-permute-done.2.refs_0_), channel_id=1, source_target_pairs={{0,1},{1,0},{2,3},{3,2},{4,5},{5,4},{6,7},{7,6},{8,9},{9,8},{10,11... | collective-permute-start | bytes 1966088 | tf_op jit(solution)/shard_map/ppermute | solution.py:335
  54.6 18.0 %collective-permute-start.12 = (bf16[320,1024]{1,0:T(8,128)(2,1)}, bf16[320,1024]{1,0:T(8,128)(2,1)S(1)}, u32[]{:S(2)}, u32[]{:S(2)}) collective-permute-start(bf16[320,1024]{1,0:T(8,128)(2,1)} %collective-permute-done.3.refs_2_), channel_id=1, source_target_pairs={{0,1},{1,0},{2,3},{3,2},{4,5},{5,4},{6,7},{7,6},{8,9},{9,8},{10,11... | collective-permute-start | bytes 1966088 | tf_op jit(solution)/shard_map/ppermute | solution.py:335
  69.7 13.8 %collective-permute-start.15 = (bf16[320,1024]{1,0:T(8,128)(2,1)S(1)}, bf16[320,1024]{1,0:T(8,128)(2,1)S(1)}, u32[]{:S(2)}, u32[]{:S(2)}) collective-permute-start(bf16[320,1024]{1,0:T(8,128)(2,1)S(1)} %collective-permute-done.4.refs_0_), channel_id=1, source_target_pairs={{0,1},{1,0},{2,3},{3,2},{4,5},{5,4},{6,7},{7,6},{8,9},{9,8},{10,11... | collective-permute-start | bytes 1966088 | tf_op jit(solution)/shard_map/ppermute | solution.py:335
  71.0 12.4 %collective-permute-start.16 = (bf16[320,1024]{1,0:T(8,128)(2,1)S(1)}, bf16[320,1024]{1,0:T(8,128)(2,1)S(1)}, u32[]{:S(2)}, u32[]{:S(2)}) collective-permute-start(bf16[320,1024]{1,0:T(8,128)(2,1)S(1)} %collective-permute-done.5.refs_2_), channel_id=1, source_target_pairs={{0,1},{1,0},{2,3},{3,2},{4,5},{5,4},{6,7},{7,6},{8,9},{9,8},{10,11... | collective-permute-start | bytes 1966088 | tf_op jit(solution)/shard_map/ppermute | solution.py:335
  71.1 10.9 %collective-permute-start.10 = (bf16[160,1024]{1,0:T(8,128)(2,1)S(1)}, bf16[160,1024]{1,0:T(8,128)(2,1)S(1)}, u32[]{:S(2)}, u32[]{:S(2)}) collective-permute-start(bf16[160,1024]{1,0:T(8,128)(2,1)S(1)} %slice.39), channel_id=1, source_target_pairs={{0,4},{1,5},{2,6},{3,7},{4,8},{5,9},{6,10},{7,11},{8,12},{9,13},{1... | collective-permute-start | bytes 983048 | tf_op jit(solution)/shard_map/ppermute | solution.py:347
  71.5 10.5 %collective-permute-start.9 = (bf16[160,1024]{1,0:T(8,128)(2,1)S(1)}, bf16[160,1024]{1,0:T(8,128)(2,1)S(1)}, u32[]{:S(2)}, u32[]{:S(2)}) collective-permute-start(bf16[160,1024]{1,0:T(8,128)(2,1)S(1)} %slice.38), channel_id=1, source_target_pairs={{0,2},{1,3},{2,0},{3,1},{4,6},{5,7},{6,4},{7,5},{8,10},{9,11},{10,... | collective-permute-start | bytes 983048 | tf_op jit(solution)/shard_map/ppermute | solution.py:346
  82.0 4.9 %collective-permute-start.13 = (bf16[160,1024]{1,0:T(8,128)(2,1)S(1)}, bf16[160,1024]{1,0:T(8,128)(2,1)S(1)}, u32[]{:S(2)}, u32[]{:S(2)}) collective-permute-start(bf16[160,1024]{1,0:T(8,128)(2,1)S(1)} %collective-permute-done.9.refs_0_), channel_id=1, source_target_pairs={{0,1},{1,0},{2,3},{3,2},{4,5},{5,4},{6,7},{7,6},{8,9},{9,8},{10,11... | collective-permute-start | bytes 983048 | tf_op jit(solution)/shard_map/ppermute | solution.py:335
  91.4 20.5 %collective-permute-start.17 = (bf16[512,768]{1,0:T(8,128)(2,1)S(1)}, bf16[512,768]{1,0:T(8,128)(2,1)S(1)}, u32[]{:S(2)}, u32[]{:S(2)}) collective-permute-start(bf16[512,768]{1,0:T(8,128)(2,1)S(1)} %get-tuple-element.76.refs_0_), channel_id=1, source_target_pairs={{0,4},{1,5},{2,6},{3,7},{4,8},{5,9},{6,10},{7,11},{8,12},{9,13},{1... | collective-permute-start | bytes 2359304 | tf_op jit(solution)/shard_map/ppermute | solution.py:339
  91.5 20.4 %collective-permute-start.18 = (bf16[512,768]{1,0:T(8,128)(2,1)S(1)}, bf16[512,768]{1,0:T(8,128)(2,1)S(1)}, u32[]{:S(2)}, u32[]{:S(2)}) collective-permute-start(bf16[512,768]{1,0:T(8,128)(2,1)S(1)} %get-tuple-element.76.refs_0_), channel_id=1, source_target_pairs={{0,2},{1,3},{2,0},{3,1},{4,6},{5,7},{6,4},{7,5},{8,10},{9,11},{10,... | collective-permute-start | bytes 2359304 | tf_op jit(solution)/shard_map/ppermute | solution.py:339
  111.9 19.5 %collective-permute-start.19 = (bf16[512,768]{1,0:T(8,128)(2,1)S(1)}, bf16[512,768]{1,0:T(8,128)(2,1)S(1)}, u32[]{:S(2)}, u32[]{:S(2)}) collective-permute-start(bf16[512,768]{1,0:T(8,128)(2,1)S(1)} %collective-permute-done.17.refs_2_), channel_id=1, source_target_pairs={{0,4},{1,5},{2,6},{3,7},{4,8},{5,9},{6,10},{7,11},{8,12},{9,13},{1... | collective-permute-start | bytes 2359304 | tf_op jit(solution)/shard_map/ppermute | solution.py:339
  111.9 19.5 %collective-permute-start.20 = (bf16[512,768]{1,0:T(8,128)(2,1)S(1)}, bf16[512,768]{1,0:T(8,128)(2,1)}, u32[]{:S(2)}, u32[]{:S(2)}) collective-permute-start(bf16[512,768]{1,0:T(8,128)(2,1)S(1)} %collective-permute-done.17.refs_2_), channel_id=1, source_target_pairs={{0,2},{1,3},{2,0},{3,1},{4,6},{5,7},{6,4},{7,5},{8,10},{9,11},{10,... | collective-permute-start | bytes 2359304 | tf_op jit(solution)/shard_map/ppermute | solution.py:339
  131.4 18.7 %collective-permute-start.21 = (bf16[512,768]{1,0:T(8,128)(2,1)S(1)}, bf16[512,768]{1,0:T(8,128)(2,1)}, u32[]{:S(2)}, u32[]{:S(2)}) collective-permute-start(bf16[512,768]{1,0:T(8,128)(2,1)S(1)} %collective-permute-done.19.refs_6_), channel_id=1, source_target_pairs={{0,4},{1,5},{2,6},{3,7},{4,8},{5,9},{6,10},{7,11},{8,12},{9,13},{1... | collective-permute-start | bytes 2359304 | tf_op jit(solution)/shard_map/ppermute | solution.py:339
  131.4 22.7 %collective-permute-start.22 = (bf16[512,768]{1,0:T(8,128)(2,1)S(1)}, bf16[512,768]{1,0:T(8,128)(2,1)}, u32[]{:S(2)}, u32[]{:S(2)}) collective-permute-start(bf16[512,768]{1,0:T(8,128)(2,1)S(1)} %collective-permute-done.19.refs_6_), channel_id=1, source_target_pairs={{0,2},{1,3},{2,0},{3,1},{4,6},{5,7},{6,4},{7,5},{8,10},{9,11},{10,... | collective-permute-start | bytes 2359304 | tf_op jit(solution)/shard_map/ppermute | solution.py:339
  132.4 24.9 %collective-permute-start.30 = (bf16[512,768]{1,0:T(8,128)(2,1)S(1)}, bf16[512,768]{1,0:T(8,128)(2,1)S(1)}, u32[]{:S(2)}, u32[]{:S(2)}) collective-permute-start(bf16[512,768]{1,0:T(8,128)(2,1)S(1)} %get-tuple-element.76.refs_0_), channel_id=1, source_target_pairs={{0,1},{1,0},{2,3},{3,2},{4,5},{5,4},{6,7},{7,6},{8,9},{9,8},{10,11... | collective-permute-start | bytes 2359304 | tf_op jit(solution)/shard_map/ppermute | solution.py:335
  135.9 22.3 %collective-permute-start.31 = (bf16[512,768]{1,0:T(8,128)(2,1)S(1)}, bf16[512,768]{1,0:T(8,128)(2,1)S(1)}, u32[]{:S(2)}, u32[]{:S(2)}) collective-permute-start(bf16[512,768]{1,0:T(8,128)(2,1)S(1)} %collective-permute-done.17.refs_2_), channel_id=1, source_target_pairs={{0,1},{1,0},{2,3},{3,2},{4,5},{5,4},{6,7},{7,6},{8,9},{9,8},{10,11... | collective-permute-start | bytes 2359304 | tf_op jit(solution)/shard_map/ppermute | solution.py:335
  136.9 22.5 %collective-permute-start.32 = (bf16[512,768]{1,0:T(8,128)(2,1)S(1)}, bf16[512,768]{1,0:T(8,128)(2,1)S(1)}, u32[]{:S(2)}, u32[]{:S(2)}) collective-permute-start(bf16[512,768]{1,0:T(8,128)(2,1)S(1)} %collective-permute-done.18.refs_4_), channel_id=1, source_target_pairs={{0,1},{1,0},{2,3},{3,2},{4,5},{5,4},{6,7},{7,6},{8,9},{9,8},{10,11... | collective-permute-start | bytes 2359304 | tf_op jit(solution)/shard_map/ppermute | solution.py:335
  150.1 10.4 %collective-permute-start.33 = (bf16[512,768]{1,0:T(8,128)(2,1)S(1)}, bf16[512,768]{1,0:T(8,128)(2,1)S(1)}, u32[]{:S(2)}, u32[]{:S(2)}) collective-permute-start(bf16[512,768]{1,0:T(8,128)(2,1)S(1)} %collective-permute-done.19.refs_6_), channel_id=1, source_target_pairs={{0,1},{1,0},{2,3},{3,2},{4,5},{5,4},{6,7},{7,6},{8,9},{9,8},{10,11... | collective-permute-start | bytes 2359304 | tf_op jit(solution)/shard_map/ppermute | solution.py:335
  155.2 10.9 %collective-permute-start.37 = (bf16[256,768]{1,0:T(8,128)(2,1)S(1)}, bf16[256,768]{1,0:T(8,128)(2,1)S(1)}, u32[]{:S(2)}, u32[]{:S(2)}) collective-permute-start(bf16[256,768]{1,0:T(8,128)(2,1)S(1)} %slice.40), channel_id=1, source_target_pairs={{0,2},{1,3},{2,0},{3,1},{4,6},{5,7},{6,4},{7,5},{8,10},{9,11},{10,... | collective-permute-start | bytes 1179656 | tf_op jit(solution)/shard_map/ppermute | solution.py:346
  158.2 12.3 %collective-permute-start.38 = (bf16[256,768]{1,0:T(8,128)(2,1)S(1)}, bf16[256,768]{1,0:T(8,128)(2,1)}, u32[]{:S(2)}, u32[]{:S(2)}) collective-permute-start(bf16[256,768]{1,0:T(8,128)(2,1)S(1)} %slice.41), channel_id=1, source_target_pairs={{0,4},{1,5},{2,6},{3,7},{4,8},{5,9},{6,10},{7,11},{8,12},{9,13},{1... | collective-permute-start | bytes 1179656 | tf_op jit(solution)/shard_map/ppermute | solution.py:347
  159.1 21.0 %collective-permute-start.34 = (bf16[512,768]{1,0:T(8,128)(2,1)}, bf16[512,768]{1,0:T(8,128)(2,1)}, u32[]{:S(2)}, u32[]{:S(2)}) collective-permute-start(bf16[512,768]{1,0:T(8,128)(2,1)} %collective-permute-done.20.refs_8_), channel_id=1, source_target_pairs={{0,1},{1,0},{2,3},{3,2},{4,5},{5,4},{6,7},{7,6},{8,9},{9,8},{10,11... | collective-permute-start | bytes 2359304 | tf_op jit(solution)/shard_map/ppermute | solution.py:335
  160.3 19.9 %collective-permute-start.35 = (bf16[512,768]{1,0:T(8,128)(2,1)}, bf16[512,768]{1,0:T(8,128)(2,1)}, u32[]{:S(2)}, u32[]{:S(2)}) collective-permute-start(bf16[512,768]{1,0:T(8,128)(2,1)} %collective-permute-done.21.refs_10_), channel_id=1, source_target_pairs={{0,1},{1,0},{2,3},{3,2},{4,5},{5,4},{6,7},{7,6},{8,9},{9,8},{10,11... | collective-permute-start | bytes 2359304 | tf_op jit(solution)/shard_map/ppermute | solution.py:335
  161.4 18.9 %collective-permute-start.36 = (bf16[512,768]{1,0:T(8,128)(2,1)}, bf16[512,768]{1,0:T(8,128)(2,1)}, u32[]{:S(2)}, u32[]{:S(2)}) collective-permute-start(bf16[512,768]{1,0:T(8,128)(2,1)} %collective-permute-done.22.refs_12_), channel_id=1, source_target_pairs={{0,1},{1,0},{2,3},{3,2},{4,5},{5,4},{6,7},{7,6},{8,9},{9,8},{10,11... | collective-permute-start | bytes 2359304 | tf_op jit(solution)/shard_map/ppermute | solution.py:335
  166.1 10.0 %collective-permute-start.24 = (bf16[512,256]{1,0:T(8,128)(2,1)S(1)}, bf16[512,256]{1,0:T(8,128)(2,1)S(1)}, u32[]{:S(2)}, u32[]{:S(2)}) collective-permute-start(bf16[512,256]{1,0:T(8,128)(2,1)S(1)} %get-tuple-element.80.refs_0_), channel_id=1, source_target_pairs={{0,4},{1,5},{2,6},{3,7},{4,8},{5,9},{6,10},{7,11},{8,12},{9,13},{1... | collective-permute-start | bytes 786440 | tf_op jit(solution)/shard_map/ppermute | solution.py:339
  170.5 6.6 %collective-permute-start.25 = (bf16[512,256]{1,0:T(8,128)(2,1)S(1)}, bf16[512,256]{1,0:T(8,128)(2,1)S(1)}, u32[]{:S(2)}, u32[]{:S(2)}) collective-permute-start(bf16[512,256]{1,0:T(8,128)(2,1)S(1)} %get-tuple-element.80.refs_0_), channel_id=1, source_target_pairs={{0,2},{1,3},{2,0},{3,1},{4,6},{5,7},{6,4},{7,5},{8,10},{9,11},{10,... | collective-permute-start | bytes 786440 | tf_op jit(solution)/shard_map/ppermute | solution.py:339
  176.1 4.7 %collective-permute-start.39 = (bf16[256,768]{1,0:T(8,128)(2,1)S(1)}, bf16[256,768]{1,0:T(8,128)(2,1)}, u32[]{:S(2)}, u32[]{:S(2)}) collective-permute-start(bf16[256,768]{1,0:T(8,128)(2,1)S(1)} %collective-permute-done.37.refs_14_), channel_id=1, source_target_pairs={{0,1},{1,0},{2,3},{3,2},{4,5},{5,4},{6,7},{7,6},{8,9},{9,8},{10,11... | collective-permute-start | bytes 1179656 | tf_op jit(solution)/shard_map/ppermute | solution.py:335
  180.1 77.2 %collective-permute-start.23 = (bf16[512,256]{1,0:T(8,128)(2,1)}, bf16[512,256]{1,0:T(8,128)(2,1)S(1)}, u32[]{:S(2)}, u32[]{:S(2)}) collective-permute-start(bf16[512,256]{1,0:T(8,128)(2,1)} %copy-done.28), channel_id=1, source_target_pairs={{0,1},{1,0},{2,3},{3,2},{4,5},{5,4},{6,7},{7,6},{8,9},{9,8},{10,11... | collective-permute-start | bytes 786440 | tf_op jit(solution)/shard_map/ppermute | solution.py:335
  180.2 38.2 %collective-permute-start.28 = (bf16[512,256]{1,0:T(8,128)(2,1)}, bf16[512,256]{1,0:T(8,128)(2,1)S(1)}, u32[]{:S(2)}, u32[]{:S(2)}) collective-permute-start(bf16[512,256]{1,0:T(8,128)(2,1)} %copy-done.30), channel_id=1, source_target_pairs={{0,4},{1,5},{2,6},{3,7},{4,8},{5,9},{6,10},{7,11},{8,12},{9,13},{1... | collective-permute-start | bytes 786440 | tf_op jit(solution)/shard_map/ppermute | solution.py:339
  180.3 38.2 %collective-permute-start.29 = (bf16[512,256]{1,0:T(8,128)(2,1)}, bf16[512,256]{1,0:T(8,128)(2,1)S(1)}, u32[]{:S(2)}, u32[]{:S(2)}) collective-permute-start(bf16[512,256]{1,0:T(8,128)(2,1)} %copy-done.30), channel_id=1, source_target_pairs={{0,2},{1,3},{2,0},{3,1},{4,6},{5,7},{6,4},{7,5},{8,10},{9,11},{10,... | collective-permute-start | bytes 786440 | tf_op jit(solution)/shard_map/ppermute | solution.py:339
  180.8 76.6 %collective-permute-start.26 = (bf16[512,256]{1,0:T(8,128)(2,1)}, bf16[512,256]{1,0:T(8,128)(2,1)S(1)}, u32[]{:S(2)}, u32[]{:S(2)}) collective-permute-start(bf16[512,256]{1,0:T(8,128)(2,1)} %copy-done.30), channel_id=1, source_target_pairs={{0,1},{1,0},{2,3},{3,2},{4,5},{5,4},{6,7},{7,6},{8,9},{9,8},{10,11... | collective-permute-start | bytes 786440 | tf_op jit(solution)/shard_map/ppermute | solution.py:335
  218.5 36.9 %collective-permute-start.43 = (bf16[512,256]{1,0:T(8,128)(2,1)S(1)}, bf16[512,256]{1,0:T(8,128)(2,1)S(1)}, u32[]{:S(2)}, u32[]{:S(2)}) collective-permute-start(bf16[512,256]{1,0:T(8,128)(2,1)S(1)} %collective-permute-done.28.refs_6_), channel_id=1, source_target_pairs={{0,4},{1,5},{2,6},{3,7},{4,8},{5,9},{6,10},{7,11},{8,12},{9,13},{1... | collective-permute-start | bytes 786440 | tf_op jit(solution)/shard_map/ppermute | solution.py:339
  228.9 26.5 %collective-permute-start.44 = (bf16[512,256]{1,0:T(8,128)(2,1)S(1)}, bf16[512,256]{1,0:T(8,128)(2,1)S(1)}, u32[]{:S(2)}, u32[]{:S(2)}) collective-permute-start(bf16[512,256]{1,0:T(8,128)(2,1)S(1)} %collective-permute-done.28.refs_6_), channel_id=1, source_target_pairs={{0,2},{1,3},{2,0},{3,1},{4,6},{5,7},{6,4},{7,5},{8,10},{9,11},{10,... | collective-permute-start | bytes 786440 | tf_op jit(solution)/shard_map/ppermute | solution.py:339
  255.4 4.9 %collective-permute-start.47 = (bf16[256,256]{1,0:T(8,128)(2,1)S(1)}, bf16[256,256]{1,0:T(8,128)(2,1)S(1)}, u32[]{:S(2)}, u32[]{:S(2)}) collective-permute-start(bf16[256,256]{1,0:T(8,128)(2,1)S(1)} %slice.42), channel_id=1, source_target_pairs={{0,2},{1,3},{2,0},{3,1},{4,6},{5,7},{6,4},{7,5},{8,10},{9,11},{10,... | collective-permute-start | bytes 393224 | tf_op jit(solution)/shard_map/ppermute | solution.py:346
  256.1 6.0 %collective-permute-start.48 = (bf16[256,256]{1,0:T(8,128)(2,1)S(1)}, bf16[256,256]{1,0:T(8,128)(2,1)S(1)}, u32[]{:S(2)}, u32[]{:S(2)}) collective-permute-start(bf16[256,256]{1,0:T(8,128)(2,1)S(1)} %slice.43), channel_id=1, source_target_pairs={{0,4},{1,5},{2,6},{3,7},{4,8},{5,9},{6,10},{7,11},{8,12},{9,13},{1... | collective-permute-start | bytes 393224 | tf_op jit(solution)/shard_map/ppermute | solution.py:347
  256.2 33.3 %collective-permute-start.27 = (bf16[512,256]{1,0:T(8,128)(2,1)S(1)}, bf16[512,256]{1,0:T(8,128)(2,1)S(1)}, u32[]{:S(2)}, u32[]{:S(2)}) collective-permute-start(bf16[512,256]{1,0:T(8,128)(2,1)S(1)} %copy-done.33), channel_id=1, source_target_pairs={{0,1},{1,0},{2,3},{3,2},{4,5},{5,4},{6,7},{7,6},{8,9},{9,8},{10,11... | collective-permute-start | bytes 786440 | tf_op jit(solution)/shard_map/ppermute | solution.py:335
  257.3 32.3 %collective-permute-start.41 = (bf16[512,256]{1,0:T(8,128)(2,1)S(1)}, bf16[512,256]{1,0:T(8,128)(2,1)S(1)}, u32[]{:S(2)}, u32[]{:S(2)}) collective-permute-start(bf16[512,256]{1,0:T(8,128)(2,1)S(1)} %collective-permute-done.28.refs_6_), channel_id=1, source_target_pairs={{0,1},{1,0},{2,3},{3,2},{4,5},{5,4},{6,7},{7,6},{8,9},{9,8},{10,11... | collective-permute-start | bytes 786440 | tf_op jit(solution)/shard_map/ppermute | solution.py:335
  257.4 32.7 %collective-permute-start.42 = (bf16[512,256]{1,0:T(8,128)(2,1)S(1)}, bf16[512,256]{1,0:T(8,128)(2,1)S(1)}, u32[]{:S(2)}, u32[]{:S(2)}) collective-permute-start(bf16[512,256]{1,0:T(8,128)(2,1)S(1)} %collective-permute-done.29.refs_8_), channel_id=1, source_target_pairs={{0,1},{1,0},{2,3},{3,2},{4,5},{5,4},{6,7},{7,6},{8,9},{9,8},{10,11... | collective-permute-start | bytes 786440 | tf_op jit(solution)/shard_map/ppermute | solution.py:335
  260.3 30.8 %collective-permute-start.45 = (bf16[512,256]{1,0:T(8,128)(2,1)S(1)}, bf16[512,256]{1,0:T(8,128)(2,1)S(1)}, u32[]{:S(2)}, u32[]{:S(2)}) collective-permute-start(bf16[512,256]{1,0:T(8,128)(2,1)S(1)} %collective-permute-done.43.refs_10_), channel_id=1, source_target_pairs={{0,1},{1,0},{2,3},{3,2},{4,5},{5,4},{6,7},{7,6},{8,9},{9,8},{10,11... | collective-permute-start | bytes 786440 | tf_op jit(solution)/shard_map/ppermute | solution.py:335
  262.2 29.0 %collective-permute-start.46 = (bf16[512,256]{1,0:T(8,128)(2,1)S(1)}, bf16[512,256]{1,0:T(8,128)(2,1)S(1)}, u32[]{:S(2)}, u32[]{:S(2)}) collective-permute-start(bf16[512,256]{1,0:T(8,128)(2,1)S(1)} %collective-permute-done.44.refs_12_), channel_id=1, source_target_pairs={{0,1},{1,0},{2,3},{3,2},{4,5},{5,4},{6,7},{7,6},{8,9},{9,8},{10,11... | collective-permute-start | bytes 786440 | tf_op jit(solution)/shard_map/ppermute | solution.py:335
  (47 other events, 304.3 us)

commit v6 on v5

--- a/solution.py
+++ b/solution.py
@@ -16,7 +16,7 @@
 CHUNKS = ((0, 3), (3, 1))
 PLANE = 4
 PLANES = 4
-UNROLL = 4
+UNROLL = 2
 GATHER_LIMIT = 40 * 2**20
 MASKED = -1e30
 VMEM = pl.BlockSpec(memory_space=pltpu.VMEM)
@@ -135,13 +135,8 @@
     last = placed[:, 0:1] * HEAD_SIZE + placed[:, 1:2] + live
     start = placed[:, 2:3] * HEAD_SIZE + placed[:, 3:4] + live
     seat_lanes = lax.broadcasted_iota(jnp.int32, placed.shape, 1)
-    bounds = jnp.where(seat_lanes == 0, last, start).astype(jnp.int32)
-    bounds_ref[...] = jnp.full(bounds_ref.shape, -1, jnp.int32)
+    bounds_ref[...] = jnp.where(seat_lanes == 0, last, start).astype(jnp.int32)
     rows_ref[...] = jnp.zeros(rows_ref.shape, jnp.float32)
-    for group in range(ranks):
-        for place in range(HEAD_GROUPS):
-            at = group * packed + place * spare
-            bounds_ref[at : at + spare] = bounds[group * stride : group * stride + spare]
     for head in range(KEY_VALUE_HEADS):
         for place in range(HEAD_GROUPS):
             at = (head * HEAD_GROUPS + place) * HEAD_SIZE
@@ -228,33 +223,54 @@
                     ]
 
 
+def veil_kernel(stride, bounds_ref, routes_ref, veil_ref):
+    groups, keys = veil_ref.shape[0], veil_ref.shape[1]
+
+    def one_group(group, carry):
+        seats = pl.ds(pl.multiple_of(group * stride, 16), stride)
+        routes = routes_ref[group]
+        visible = (routes <= bounds_ref[seats, 0:1]) & (routes >= bounds_ref[seats, 1:2])
+        veil = jnp.where(visible, 0.0, MASKED)
+        rest = jnp.zeros((HEAD_SIZE - stride, veil.shape[1]), jnp.float32)
+        turned = jnp.transpose(jnp.concatenate([veil, rest], axis=0))
+        veil_ref[group] = turned[:keys].astype(jnp.bfloat16)
+        return carry
+
+    lax.fori_loop(0, groups, one_group, 0)
+
+
 def attend_kernel(
-    head, heads, pieces, extra, stride, packed,
-    queries_ref, bounds_ref, routes_ref, seat_ref, more_ref, *refs
+    head, heads, pieces, extra, stride, seat_ref, more_ref, queries_ref, veil_ref, *refs
 ):
     first_head, place = head
-    ranks = routes_ref.shape[0]
-    parts, refs = refs[: len(pieces)], refs[-(6 + 3 * UNROLL) :]
-    out_ref, blocks, more, mixed_ref, result_ref, done = refs[:6]
-    score_refs, weight_refs, total_refs = (
-        refs[6 + at * UNROLL : 6 + (at + 1) * UNROLL] for at in range(3)
-    )
-    count = blocks.shape[2]
+    parts, refs = refs[: len(pieces)], refs[-9:]
+    out_ref, blocks, more, query, veil, seen_by, mixed_ref, result_ref, done = refs
+    ranks, count = blocks.shape[1], blocks.shape[2]
+    packed = query.shape[0] // ranks
     share = count // ranks
     spare = share + extra
-    copies = []
-    for at, ((source, first), ref) in enumerate(zip(pieces, parts)):
-        for part in range(2):
-            lanes = pl.ds((part * heads + place) * HEAD_SIZE, HEAD_SIZE)
+    copies = [
+        pltpu.make_async_copy(queries_ref.at[first_head + place], query, done.at[0]),
+        pltpu.make_async_copy(veil_ref, veil, done.at[1]),
+    ]
+    for part in range(2):
+        lanes = pl.ds((part * heads + place) * HEAD_SIZE, HEAD_SIZE)
+        for (source, first), ref in zip(pieces, parts):
+            rows = pl.ds(first, ref.shape[0])
             copies.append(
                 pltpu.make_async_copy(
-                    ref.at[:, lanes],
-                    blocks.at[part, source, pl.ds(first, ref.shape[0])],
-                    done.at[2 * at + part],
+                    ref.at[:, lanes], blocks.at[part, source, rows], done.at[len(copies)]
                 )
             )
-            copies[-1].start()
+    for copy in copies:
+        copy.start()
     mixed_ref[...] = jnp.zeros(mixed_ref.shape, jnp.bfloat16)
+    token = lax.broadcasted_iota(jnp.int32, (packed, HEAD_SIZE), 0)
+    lane = lax.broadcasted_iota(jnp.int32, (packed, HEAD_SIZE), 1)
+    own = lane < 0
+    for at in range(HEAD_GROUPS):
+        own = own | ((token == lane + at * spare) & (lane < spare))
+    seen_by[...] = own.astype(jnp.float32).astype(jnp.bfloat16)
     listed = ranks * extra
     lines = lax.broadcasted_iota(jnp.int32, (listed, count), 1)
     picks = [
@@ -280,45 +296,36 @@
         rows.append(more[part, pl.ds(pl.multiple_of(group * listed, 16), listed)])
         return jnp.concatenate(rows, axis=0)
 
-    def score(group, score_ref):
-        query = queries_ref[0, pl.ds(pl.multiple_of(group * packed, 16), packed)]
-        score_ref[...] = contract(query, rows_of(0, group), 1, 1)
-
-    def weigh(group, score_ref, weight_ref, total_ref):
-        routes = routes_ref[group]
-        for first in range(0, packed, 16):
-            at = pl.ds(pl.multiple_of(group * packed + first, 16), 16)
-            visible = (routes <= bounds_ref[at, 0:1]) & (routes >= bounds_ref[at, 1:2])
-            scores = jnp.where(visible, score_ref[first : first + 16], MASKED)
-            top = jnp.max(scores, axis=1, keepdims=True)
-            weights = jnp.exp2((scores - top) * scale)
-            total = jnp.sum(weights, axis=1, keepdims=True)
-            weight_ref[first : first + 16] = weights.astype(jnp.bfloat16)
-            total_ref[first : first + 16] = jnp.broadcast_to(1.0 / total, (16, HEAD_SIZE))
-
-    def mix(group, weight_ref, total_ref):
-        mixed = contract(weight_ref[...], rows_of(1, group), 1, 0) * total_ref[...]
-        seats = pl.ds(pl.multiple_of(group * stride, 16), spare)
-        for at in range(HEAD_GROUPS):
-            lanes = slice(at * HEAD_SIZE, (at + 1) * HEAD_SIZE)
-            mixed_ref[seats, lanes] = mixed[at * spare : (at + 1) * spare].astype(jnp.bfloat16)
-
     def some_groups(step, carry):
         groups = [step * UNROLL + at for at in range(UNROLL)]
-        for at in range(UNROLL + 2):
-            if at < UNROLL:
-                score(groups[at], score_refs[at])
-            if 0 <= at - 1 < UNROLL:
-                weigh(groups[at - 1], score_refs[at - 1], weight_refs[at - 1], total_refs[at - 1])
-            if 0 <= at - 2 < UNROLL:
-                mix(groups[at - 2], weight_refs[at - 2], total_refs[at - 2])
+        scores = []
+        for group in groups:
+            tokens = pl.ds(pl.multiple_of(group * packed, 16), packed)
+            left = jnp.concatenate([query[tokens], seen_by[...]], axis=1)
+            right = jnp.concatenate([rows_of(0, group), veil[group]], axis=1)
+            scores.append(contract(left, right, 1, 1))
+        weights = []
+        for one in scores:
+            top = jnp.max(one, axis=1, keepdims=True)
+            weights.append(jnp.exp2((one - top) * scale).astype(jnp.bfloat16))
+        for group, weight in zip(groups, weights):
+            values = rows_of(1, group)
+            values = jnp.concatenate([values, jnp.ones_like(values)], axis=1)
+            mixed = contract(weight, values, 1, 0)
+            mixed = mixed[:, :HEAD_SIZE] / mixed[:, HEAD_SIZE:]
+            seats = pl.ds(pl.multiple_of(group * stride, 16), spare)
+            for at in range(HEAD_GROUPS):
+                lanes = slice(at * HEAD_SIZE, (at + 1) * HEAD_SIZE)
+                rows = mixed[at * spare : (at + 1) * spare]
+                mixed_ref[seats, lanes] = rows.astype(jnp.bfloat16)
         return carry
 
     lax.fori_loop(0, ranks // UNROLL, some_groups, 0)
-    seats = one_hot_rows(mixed_ref.shape[0], seat_ref[...])
-    result_ref[...] = contract(seats, mixed_ref[...], 0, 0).astype(jnp.bfloat16)
+    seat_lanes = lax.broadcasted_iota(jnp.int32, (count, mixed_ref.shape[0]), 1)
+    seats = (seat_lanes == seat_ref[...]).astype(jnp.float32).astype(jnp.bfloat16)
+    result_ref[...] = contract(seats, mixed_ref[...], 1, 0).astype(jnp.bfloat16)
     lanes = pl.ds((first_head + place) * HEAD_GROUPS * HEAD_SIZE, HEAD_GROUPS * HEAD_SIZE)
-    leave = pltpu.make_async_copy(result_ref, out_ref.at[:, lanes], done.at[2 * len(pieces)])
+    leave = pltpu.make_async_copy(result_ref, out_ref.at[:, lanes], done.at[len(copies)])
     leave.start()
     leave.wait()
 
@@ -424,6 +431,10 @@
         ],
         axis=1,
     ).reshape(ranks, 1, key_count)
+    wide_keys = -(-key_count // HEAD_SIZE) * HEAD_SIZE
+    key_routes = jnp.pad(
+        key_routes, ((0, 0), (0, 0), (0, wide_keys - key_count)), constant_values=-1
+    )
     more_places = sources[:, rows + listed :].reshape(ranks * listed, 1)
 
     half = HEAD_SIZE // 2
@@ -432,7 +443,7 @@
         functools.partial(query_kernel, ranks, spare, stride, packed),
         out_shape=(
             shape((KEY_VALUE_HEADS, ranks * packed, HEAD_SIZE), jnp.bfloat16),
-            shape((ranks * packed, HEAD_SIZE), jnp.int32),
+            shape((ranks * stride, HEAD_SIZE), jnp.int32),
             shape((rows, HEAD_SIZE), jnp.float32),
             shape((rows, HEAD_SIZE), jnp.float32),
         ),
@@ -526,31 +537,25 @@
         pieces = [(source, first) for source in held for first, _ in held[source]]
         arrays = [array for source in held for _, array in held[source]]
         taken = [] if out is None else [out]
-        fixed = [turned, bounds, key_routes, seat, more_places]
+        fixed = [seat.reshape(rows, 1), more_places, turned, veil]
         span = HEAD_GROUPS * HEAD_SIZE
-        query_block = pl.BlockSpec(
-            (1, ranks * packed, HEAD_SIZE), lambda i, h=first_head + place: (h, 0, 0)
-        )
         return pl.pallas_call(
-            functools.partial(
-                attend_kernel, (first_head, place), heads, pieces, extra, stride, packed
-            ),
-            grid=(1,),
+            functools.partial(attend_kernel, (first_head, place), heads, pieces, extra, stride),
             out_shape=shape((rows, query_width), jnp.bfloat16),
-            in_specs=[query_block] + [VMEM] * 4 + [HBM] * (len(pieces) + len(taken)),
+            in_specs=[VMEM] * 2 + [HBM] * (2 + len(pieces) + len(taken)),
             out_specs=HBM,
             scratch_shapes=[
                 pltpu.VMEM((2, ranks, rows, HEAD_SIZE), jnp.bfloat16),
                 pltpu.VMEM((2, ranks * listed, HEAD_SIZE), jnp.bfloat16),
+                pltpu.VMEM((ranks * packed, HEAD_SIZE), jnp.bfloat16),
+                pltpu.VMEM(veil.shape, jnp.bfloat16),
+                pltpu.VMEM((packed, HEAD_SIZE), jnp.bfloat16),
                 pltpu.VMEM((ranks * stride, span), jnp.bfloat16),
                 pltpu.VMEM((rows, span), jnp.bfloat16),
-                pltpu.SemaphoreType.DMA((2 * len(pieces) + 1,)),
-            ]
-            + [pltpu.VMEM((packed, key_count), jnp.float32)] * UNROLL
-            + [pltpu.VMEM((packed, key_count), jnp.bfloat16)] * UNROLL
-            + [pltpu.VMEM((packed, HEAD_SIZE), jnp.float32)] * UNROLL,
+                pltpu.SemaphoreType.DMA((2 * len(pieces) + 3,)),
+            ],
             input_output_aliases={len(fixed) + len(pieces): 0} if taken else {},
-            compiler_params=grant(16),
+            compiler_params=grant(24),
             cost_estimate=cost(
                 16 * rows * stride * ranks * span, 4 * ranks * rows * HEAD_SIZE
             ),
@@ -559,7 +564,18 @@
 
     early, late = {}, {}
     sending = spread(pairs[0], ranks, early)
-    for _ in range(planes - 1):
+    next(sending)
+    veil = pl.pallas_call(
+        functools.partial(veil_kernel, stride),
+        out_shape=shape((ranks, key_count, HEAD_SIZE), jnp.bfloat16),
+        in_specs=[VMEM] * 2,
+        out_specs=VMEM,
+        compiler_params=grant(16),
+        cost_estimate=cost(2 * 10**9, 4 * ranks * key_count * HEAD_SIZE),
+        name="veil",
+    )(bounds, key_routes)
+    (veil,) = sending.send((veil,))
+    for _ in range(planes - 2):
         next(sending)
         sending.send(())
     mark = next(sending)

time: 320 us -> 251 us (0.78)
  Pallas kernels: 126 us -> 73.3 us
  starting transfers between devices: 51 us -> 41.2 us
    pallas_call x4, Pallas kernels: 101 us -> 45.8 us  [attend(): pl.pallas_call(functools.partial(attend_kernel, (first_head, place), head...]
    ppermute x9, starting transfers between devices: 13.9 us -> 3.81 us  [spread(): lax.ppermute(lane, 'dp', ring)]
    unnamed x88 -> x92, local copies, waits for them, and re-layouts: 29.9 us -> 27 us
  transfers between devices with their start and end apart: 52 -> 52, of which waited for: 14 -> 13; matrix products, arithmetic and copies ran while one was open for 6% -> 8% of each run, Pallas kernels for 31% -> 23%
where the time goes in v6:
time: 251 us; the launch traced here: 249 us
  waiting for transfers between devices  87 us (35%)
  Pallas kernels  73.3 us (29%)
  local copies, waits for them, and re-layouts  45 us (18%)
  starting transfers between devices  41.2 us (16%)
    ppermute x9, waiting for transfers between devices, spread(): lax.ppermute(lane, 'dp', ring)  59.1 us
    pallas_call x4, Pallas kernels, attend(): pl.pallas_call(functools.partial(attend_kernel, (first_head, place), head...  45.8 us
    unnamed x92, local copies, waits for them, and re-layouts  27 us
    ppermute x27, starting transfers between devices, keep(): lax.ppermute(array, 'dp', beside)  22.3 us
    pallas_call x3, Pallas kernels, add_part(): pl.pallas_call(functools.partial(part_kernel, chips, bool(more)), out_sha...  13 us
    ppermute x3, waiting for transfers between devices, spread(): around = lax.ppermute(other[half:], 'dp', ring)  10.9 us
    all_to_all x1, waiting for transfers between devices, gather_plan(): lax.all_to_all(jnp.broadcast_to(plan, (ranks, width + slots)), 'dp', spli...  9.19 us
    ppermute x9, starting transfers between devices, spread(): lax.ppermute(lane, 'dp', across)  7.99 us
  transfers between devices with their start and end apart: 52, of which 13 were waited for; matrix products, arithmetic and copies ran while one was open for 8% of the time, Pallas kernels for 23%

profile of v6, /device:TPU:1, one launch (start us, length us, event | category | flops | bytes accessed | tf_op | source)
XLA Modules:
  0.0 249.2 jit_solution(9931421843175909216)
XLA Ops:
  2.0 2.2 collective-permute-start
  4.2 1.2 collective-permute-start.1
  5.4 1.2 collective-permute-start.6
  9.5 4.0 %all-to-all-start = ((s32[16,1,1600]{2,1,0:T(1,128)}), s32[16,1,1600]{2,1,0:T(1,128)S(1)}, u32[]{:S(2)}, u32[]{:S(2)}) async-start(s32[16,1,1600]{2,1,0:T(1,128)} %broadcast_in_dim.4), calls=%async_computation | async-start | bytes 212992 | tf_op jit(solution)/shard_map/all_to_all | solution.py:416
  15.1 9.2 %all-to-all-done = s32[16,1,1600]{2,1,0:T(1,128)S(1)} async-done(((s32[16,1,1600]{2,1,0:T(1,128)}), s32[16,1,1600]{2,1,0:T(1,128)S(1)}, u32[]{:S(2)}, u32[]{:S(2)}) %all-to-all-start) | async-done | bytes 102432 | tf_op jit(solution)/shard_map/all_to_all | solution.py:416
  25.1 1.2 gather_fusion
  29.1 1.7 copy-done.33
  30.8 6.4 %turn_queries.1 = (bf16[4,2816,128]{2,1,0:T(8,128)(2,1)S(1)}, s32[768,128]{1,0:T(8,128)S(1)}, f32[512,128]{1,0:T(8,128)S(1)}, f32[512,128]{1,0:T(8,128)S(1)}) custom-call(s32[512,1]{1,0:T(8,128)S(1)} %copy-done.29, s32[1,512]{1,0:T(1,128)S(1)} %get-tuple-element.52.seat_ref, s32[128,128]{1,0:T(8,128)S(1)} %copy-done.30, ...), custom_call_target="tpu_custom_call" | custom-call | flops 4026531840 | bytes 5242880 | tf_op jit(solution)/shard_map/turn_queries/pallas_call | solution.py:442
  41.6 1.5 reshape.180
  43.1 1.6 copy.43
  44.7 1.6 reshape.181
  47.0 1.4 copy.30
  55.0 2.5 copy-done
  57.5 5.4 %add_part.3.refs_4_ = f32[512,1024]{1,0:T(8,128)S(1)} custom-call(s32[16]{0:T(128)S(1)} %pad_add_fusion.1.owners_ref, bf16[512,5120]{1,0:T(8,128)(2,1)S(1)} %copy-done, bf16[320,1024]{1,0:T(8,128)(2,1)S(1)} %constant_dynamic-update-slice_fusion.refs_0_, bf16[320,1024]{1,0:T(8,128)(2,1)} %collective-permute-done.6.refs_1_, ...), custom_call_target="tpu_custom_call" | custom-call | flops 2013265920 | bytes 10092544 | tf_op jit(solution)/shard_map/add_part/pallas_call | solution.py:492
  63.0 6.3 %collective-permute-done.4.refs_0_ = bf16[320,1024]{1,0:T(8,128)(2,1)S(1)} collective-permute-done((bf16[320,1024]{1,0:T(8,128)(2,1)}, bf16[320,1024]{1,0:T(8,128)(2,1)S(1)}, u32[]{:S(2)}, u32[]{:S(2)}) %collective-permute-start.4) | collective-permute-done | bytes 655392 | tf_op jit(solution)/shard_map/ppermute | solution.py:346
  69.3 1.4 collective-permute-start.15
  72.1 4.1 %add_part.4.refs_4_ = f32[512,1024]{1,0:T(8,128)S(1)} custom-call(s32[16]{0:T(128)S(1)} %pad_add_fusion.1.owners_ref, bf16[512,5120]{1,0:T(8,128)(2,1)S(1)} %copy-done, bf16[320,1024]{1,0:T(8,128)(2,1)} %collective-permute-done.2.refs_0_, bf16[320,1024]{1,0:T(8,128)(2,1)S(1)} %collective-permute-done.11.refs_1_, ...), custom_call_target="tpu_custom_call" | custom-call | flops 1342177280 | bytes 8126464 | tf_op jit(solution)/shard_map/add_part/pallas_call | solution.py:492
  76.2 5.3 %collective-permute-done.10.refs_1_ = bf16[160,1024]{1,0:T(8,128)(2,1)S(1)} collective-permute-done((bf16[160,1024]{1,0:T(8,128)(2,1)S(1)}, bf16[160,1024]{1,0:T(8,128)(2,1)S(1)}, u32[]{:S(2)}, u32[]{:S(2)}) %collective-permute-start.10) | collective-permute-done | bytes 327712 | tf_op jit(solution)/shard_map/ppermute | solution.py:354
  81.5 1.4 collective-permute-start.13
  83.0 3.4 %add_part.5.refs_4_ = f32[512,1024]{1,0:T(8,128)S(1)} custom-call(s32[16]{0:T(128)S(1)} %pad_add_fusion.1.owners_ref, bf16[512,5120]{1,0:T(8,128)(2,1)S(1)} %copy-done, bf16[320,1024]{1,0:T(8,128)(2,1)S(1)} %collective-permute-done.4.refs_0_, bf16[320,1024]{1,0:T(8,128)(2,1)S(1)} %collective-permute-done.15.refs_1_, ...), custom_call_target="tpu_custom_call" | custom-call | flops 1342177280 | bytes 8126464 | tf_op jit(solution)/shard_map/add_part/pallas_call | solution.py:492
  86.5 4.5 %finish.1 = (bf16[512,768]{1,0:T(8,128)(2,1)S(1)}, bf16[512,256]{1,0:T(8,128)(2,1)S(1)}) custom-call(s32[16]{0:T(128)S(1)} %pad_add_fusion.1.owners_ref, bf16[512,5120]{1,0:T(8,128)(2,1)S(1)} %bitcast.23, f32[1,1024]{1,0:T(1,128)S(1)} %maximum_convert_fusion.bias_ref, f32[512,128]{1,0:T(8,128)S(1)} %copy-done.26, f32[512,128]{1,0:T(8,128)S(1)} %copy-done.28, ...), custom_call_target="tpu_custom_call" | custom-call | flops 671088640 | bytes 6160384 | tf_op jit(solution)/shard_map/finish/pallas_call | solution.py:513
  92.2 3.0 %veil.1.veil_ref = bf16[16,544,128]{2,1,0:T(8,128)(2,1)S(1)} custom-call(s32[768,128]{1,0:T(8,128)S(1)} %copy-done.35, s32[16,1,640]{2,1,0:T(1,128)S(1)} %copy-done.31), custom_call_target="tpu_custom_call" | custom-call | flops 2000000000 | bytes 4456448 | tf_op jit(solution)/shard_map/veil/pallas_call | solution.py:568
  95.2 1.4 copy-done.1
  96.6 14.9 %collective-permute-done.17.refs_2_ = bf16[512,768]{1,0:T(8,128)(2,1)S(1)} collective-permute-done((bf16[512,768]{1,0:T(8,128)(2,1)S(1)}, bf16[512,768]{1,0:T(8,128)(2,1)S(1)}, u32[]{:S(2)}, u32[]{:S(2)}) %collective-permute-start.17) | collective-permute-done | bytes 786464 | tf_op jit(solution)/shard_map/ppermute | solution.py:346
  112.6 18.4 %collective-permute-done.19.refs_6_ = bf16[512,768]{1,0:T(8,128)(2,1)S(1)} collective-permute-done((bf16[512,768]{1,0:T(8,128)(2,1)S(1)}, bf16[512,768]{1,0:T(8,128)(2,1)S(1)}, u32[]{:S(2)}, u32[]{:S(2)}) %collective-permute-start.19) | collective-permute-done | bytes 786464 | tf_op jit(solution)/shard_map/ppermute | solution.py:346
  132.0 2.6 %collective-permute-start.30 = (bf16[512,768]{1,0:T(8,128)(2,1)S(1)}, bf16[512,768]{1,0:T(8,128)(2,1)S(1)}, u32[]{:S(2)}, u32[]{:S(2)}) collective-permute-start(bf16[512,768]{1,0:T(8,128)(2,1)S(1)} %get-tuple-element.74.refs_0_), channel_id=1, source_target_pairs={{0,1},{1,0},{2,3},{3,2},{4,5},{5,4},{6,7},{7,6},{8,9},{9,8},{10,11... | collective-permute-start | bytes 2359304 | tf_op jit(solution)/shard_map/ppermute | solution.py:342
  135.1 14.5 %collective-permute-done.21.refs_10_ = bf16[512,768]{1,0:T(8,128)(2,1)} collective-permute-done((bf16[512,768]{1,0:T(8,128)(2,1)S(1)}, bf16[512,768]{1,0:T(8,128)(2,1)}, u32[]{:S(2)}, u32[]{:S(2)}) %collective-permute-start.21) | collective-permute-done | bytes 786464 | tf_op jit(solution)/shard_map/ppermute | solution.py:346
  149.6 3.2 %collective-permute-start.33 = (bf16[512,768]{1,0:T(8,128)(2,1)S(1)}, bf16[512,768]{1,0:T(8,128)(2,1)S(1)}, u32[]{:S(2)}, u32[]{:S(2)}) collective-permute-start(bf16[512,768]{1,0:T(8,128)(2,1)S(1)} %collective-permute-done.19.refs_6_), channel_id=1, source_target_pairs={{0,1},{1,0},{2,3},{3,2},{4,5},{5,4},{6,7},{7,6},{8,9},{9,8},{10,11... | collective-permute-start | bytes 2359304 | tf_op jit(solution)/shard_map/ppermute | solution.py:342
  161.4 4.4 %collective-permute-done.37.refs_14_ = bf16[256,768]{1,0:T(8,128)(2,1)} collective-permute-done((bf16[256,768]{1,0:T(8,128)(2,1)S(1)}, bf16[256,768]{1,0:T(8,128)(2,1)}, u32[]{:S(2)}, u32[]{:S(2)}) %collective-permute-start.37) | collective-permute-done | bytes 393248 | tf_op jit(solution)/shard_map/ppermute | solution.py:353
  165.8 4.5 %collective-permute-done.38.refs_15_ = bf16[256,768]{1,0:T(8,128)(2,1)} collective-permute-done((bf16[256,768]{1,0:T(8,128)(2,1)S(1)}, bf16[256,768]{1,0:T(8,128)(2,1)}, u32[]{:S(2)}, u32[]{:S(2)}) %collective-permute-start.38) | collective-permute-done | bytes 393248 | tf_op jit(solution)/shard_map/ppermute | solution.py:354
  170.6 5.1 %collective-permute-done.24.refs_2_ = bf16[512,256]{1,0:T(8,128)(2,1)S(1)} collective-permute-done((bf16[512,256]{1,0:T(8,128)(2,1)S(1)}, bf16[512,256]{1,0:T(8,128)(2,1)S(1)}, u32[]{:S(2)}, u32[]{:S(2)}) %collective-permute-start.24) | collective-permute-done | bytes 262176 | tf_op jit(solution)/shard_map/ppermute | solution.py:346
  176.8 2.1 collective-permute-start.40
  180.9 1.6 copy-done.2
  182.5 1.1 copy-done.4
  183.7 1.1 copy-done.6
  184.8 1.1 copy-done.8
  185.9 1.1 copy-done.10
  187.1 1.1 copy-done.12
  188.2 1.1 copy-done.14
  190.5 1.1 copy-done.18
  191.6 11.6 %attend.4.refs_18_ = bf16[512,2560]{1,0:T(8,128)(2,1)} custom-call(s32[512,1]{1,0:T(8,128)S(1)} %copy.38.seat_ref, s32[512,1]{1,0:T(8,128)S(1)} %copy.39.more_ref, bf16[4,2816,128]{2,1,0:T(8,128)(2,1)S(1)} %get-tuple-element.61.queries_ref, bf16[16,544,128]{2,1,0:T(8,128)(2,1)S(1)} %copy-done.2, bf16[512,768]{1,0:T(8,128)(2,1)S(1)} %copy-done.4, ...), custom_call_target="tpu_custom_call" | custom-call | flops 4026531840 | bytes 4194304 | tf_op jit(solution)/shard_map/attend/pallas_call | solution.py:542
  204.6 11.6 %attend.5.refs_18_ = bf16[512,2560]{1,0:T(8,128)(2,1)} custom-call(s32[512,1]{1,0:T(8,128)S(1)} %copy.38.seat_ref, s32[512,1]{1,0:T(8,128)S(1)} %copy.39.more_ref, bf16[4,2816,128]{2,1,0:T(8,128)(2,1)S(1)} %get-tuple-element.61.queries_ref, bf16[16,544,128]{2,1,0:T(8,128)(2,1)S(1)} %copy-done.2, ...), custom_call_target="tpu_custom_call", output_to_operand_aliasing={{}: (22, {})} | custom-call | flops 4026531840 | bytes 4194304 | tf_op jit(solution)/shard_map/attend/pallas_call | solution.py:542
  218.6 2.4 collective-permute-done.47.refs_14_
  221.0 1.3 collective-permute-start.45
  222.3 1.1 collective-permute-done.48.refs_15_
  223.4 1.4 collective-permute-start.46
  224.8 11.6 %attend.6.refs_18_ = bf16[512,2560]{1,0:T(8,128)(2,1)} custom-call(s32[512,1]{1,0:T(8,128)S(1)} %copy.38.seat_ref, s32[512,1]{1,0:T(8,128)S(1)} %copy.39.more_ref, bf16[4,2816,128]{2,1,0:T(8,128)(2,1)S(1)} %get-tuple-element.61.queries_ref, bf16[16,544,128]{2,1,0:T(8,128)(2,1)S(1)} %copy-done.2, ...), custom_call_target="tpu_custom_call", output_to_operand_aliasing={{}: (22, {})} | custom-call | flops 4026531840 | bytes 4194304 | tf_op jit(solution)/shard_map/attend/pallas_call | solution.py:542
  238.0 11.0 %attend.7 = bf16[512,2560]{1,0:T(8,128)(2,1)} custom-call(s32[512,1]{1,0:T(8,128)S(1)} %copy.38.seat_ref, s32[512,1]{1,0:T(8,128)S(1)} %copy.39.more_ref, bf16[4,2816,128]{2,1,0:T(8,128)(2,1)S(1)} %get-tuple-element.61.queries_ref, bf16[16,544,128]{2,1,0:T(8,128)(2,1)S(1)} %copy-done.2, ...), custom_call_target="tpu_custom_call", output_to_operand_aliasing={{}: (22, {})} | custom-call | flops 4026531840 | bytes 4194304 | tf_op jit(solution)/shard_map/attend/pallas_call | solution.py:542
  (199 shorter events, 45.5 us)
Async XLA Ops:
  2.0 24.2 %collective-permute-start = (bf16[320,1024]{1,0:T(8,128)(2,1)S(1)}, bf16[320,1024]{1,0:T(8,128)(2,1)}, u32[]{:S(2)}, u32[]{:S(2)}) collective-permute-start(bf16[320,1024]{1,0:T(8,128)(2,1)S(1)} %constant_dynamic-update-slice_fusion.refs_0_), channel_id=1, source_target_pairs={{0,4},{1,5},{2,6},{3,7},{4,8},{5,9},{6,10},{7,11},{8,12},{9,13},{1... | collective-permute-start | bytes 1966088 | tf_op jit(solution)/shard_map/ppermute | solution.py:346
  4.2 22.1 %collective-permute-start.1 = (bf16[320,1024]{1,0:T(8,128)(2,1)S(1)}, bf16[320,1024]{1,0:T(8,128)(2,1)}, u32[]{:S(2)}, u32[]{:S(2)}) collective-permute-start(bf16[320,1024]{1,0:T(8,128)(2,1)S(1)} %constant_dynamic-update-slice_fusion.refs_0_), channel_id=1, source_target_pairs={{0,2},{1,3},{2,0},{3,1},{4,6},{5,7},{6,4},{7,5},{8,10},{9,11},{10,... | collective-permute-start | bytes 1966088 | tf_op jit(solution)/shard_map/ppermute | solution.py:346
  5.4 47.7 %collective-permute-start.6 = (bf16[320,1024]{1,0:T(8,128)(2,1)S(1)}, bf16[320,1024]{1,0:T(8,128)(2,1)}, u32[]{:S(2)}, u32[]{:S(2)}) collective-permute-start(bf16[320,1024]{1,0:T(8,128)(2,1)S(1)} %constant_dynamic-update-slice_fusion.refs_0_), channel_id=1, source_target_pairs={{0,1},{1,0},{2,3},{3,2},{4,5},{5,4},{6,7},{7,6},{8,9},{9,8},{10,11... | collective-permute-start | bytes 1966088 | tf_op jit(solution)/shard_map/ppermute | solution.py:342
  9.5 14.8 %all-to-all-start = ((s32[16,1,1600]{2,1,0:T(1,128)}), s32[16,1,1600]{2,1,0:T(1,128)S(1)}, u32[]{:S(2)}, u32[]{:S(2)}) async-start(s32[16,1,1600]{2,1,0:T(1,128)} %broadcast_in_dim.4), calls=%async_computation | async-start | bytes 212992 | tf_op jit(solution)/shard_map/all_to_all | solution.py:416
  26.3 25.1 %collective-permute-start.2 = (bf16[320,1024]{1,0:T(8,128)(2,1)}, bf16[320,1024]{1,0:T(8,128)(2,1)}, u32[]{:S(2)}, u32[]{:S(2)}) collective-permute-start(bf16[320,1024]{1,0:T(8,128)(2,1)} %collective-permute-done.refs_2_), channel_id=1, source_target_pairs={{0,4},{1,5},{2,6},{3,7},{4,8},{5,9},{6,10},{7,11},{8,12},{9,13},{1... | collective-permute-start | bytes 1966088 | tf_op jit(solution)/shard_map/ppermute | solution.py:346
  26.8 24.6 %collective-permute-start.3 = (bf16[320,1024]{1,0:T(8,128)(2,1)}, bf16[320,1024]{1,0:T(8,128)(2,1)}, u32[]{:S(2)}, u32[]{:S(2)}) collective-permute-start(bf16[320,1024]{1,0:T(8,128)(2,1)} %collective-permute-done.refs_2_), channel_id=1, source_target_pairs={{0,2},{1,3},{2,0},{3,1},{4,6},{5,7},{6,4},{7,5},{8,10},{9,11},{10,... | collective-permute-start | bytes 1966088 | tf_op jit(solution)/shard_map/ppermute | solution.py:346
  39.4 14.8 %collective-permute-start.7 = (bf16[320,1024]{1,0:T(8,128)(2,1)}, bf16[320,1024]{1,0:T(8,128)(2,1)}, u32[]{:S(2)}, u32[]{:S(2)}) collective-permute-start(bf16[320,1024]{1,0:T(8,128)(2,1)} %collective-permute-done.refs_2_), channel_id=1, source_target_pairs={{0,1},{1,0},{2,3},{3,2},{4,5},{5,4},{6,7},{7,6},{8,9},{9,8},{10,11... | collective-permute-start | bytes 1966088 | tf_op jit(solution)/shard_map/ppermute | solution.py:342
  40.4 14.7 %collective-permute-start.8 = (bf16[320,1024]{1,0:T(8,128)(2,1)}, bf16[320,1024]{1,0:T(8,128)(2,1)}, u32[]{:S(2)}, u32[]{:S(2)}) collective-permute-start(bf16[320,1024]{1,0:T(8,128)(2,1)} %collective-permute-done.1.refs_4_), channel_id=1, source_target_pairs={{0,1},{1,0},{2,3},{3,2},{4,5},{5,4},{6,7},{7,6},{8,9},{9,8},{10,11... | collective-permute-start | bytes 1966088 | tf_op jit(solution)/shard_map/ppermute | solution.py:342
  51.4 17.8 %collective-permute-start.4 = (bf16[320,1024]{1,0:T(8,128)(2,1)}, bf16[320,1024]{1,0:T(8,128)(2,1)S(1)}, u32[]{:S(2)}, u32[]{:S(2)}) collective-permute-start(bf16[320,1024]{1,0:T(8,128)(2,1)} %collective-permute-done.2.refs_0_), channel_id=1, source_target_pairs={{0,4},{1,5},{2,6},{3,7},{4,8},{5,9},{6,10},{7,11},{8,12},{9,13},{1... | collective-permute-start | bytes 1966088 | tf_op jit(solution)/shard_map/ppermute | solution.py:346
  52.1 17.2 %collective-permute-start.5 = (bf16[320,1024]{1,0:T(8,128)(2,1)}, bf16[320,1024]{1,0:T(8,128)(2,1)S(1)}, u32[]{:S(2)}, u32[]{:S(2)}) collective-permute-start(bf16[320,1024]{1,0:T(8,128)(2,1)} %collective-permute-done.2.refs_0_), channel_id=1, source_target_pairs={{0,2},{1,3},{2,0},{3,1},{4,6},{5,7},{6,4},{7,5},{8,10},{9,11},{10,... | collective-permute-start | bytes 1966088 | tf_op jit(solution)/shard_map/ppermute | solution.py:346
  53.1 17.9 %collective-permute-start.11 = (bf16[320,1024]{1,0:T(8,128)(2,1)}, bf16[320,1024]{1,0:T(8,128)(2,1)S(1)}, u32[]{:S(2)}, u32[]{:S(2)}) collective-permute-start(bf16[320,1024]{1,0:T(8,128)(2,1)} %collective-permute-done.2.refs_0_), channel_id=1, source_target_pairs={{0,1},{1,0},{2,3},{3,2},{4,5},{5,4},{6,7},{7,6},{8,9},{9,8},{10,11... | collective-permute-start | bytes 1966088 | tf_op jit(solution)/shard_map/ppermute | solution.py:342
  54.2 17.9 %collective-permute-start.12 = (bf16[320,1024]{1,0:T(8,128)(2,1)}, bf16[320,1024]{1,0:T(8,128)(2,1)S(1)}, u32[]{:S(2)}, u32[]{:S(2)}) collective-permute-start(bf16[320,1024]{1,0:T(8,128)(2,1)} %collective-permute-done.3.refs_2_), channel_id=1, source_target_pairs={{0,1},{1,0},{2,3},{3,2},{4,5},{5,4},{6,7},{7,6},{8,9},{9,8},{10,11... | collective-permute-start | bytes 1966088 | tf_op jit(solution)/shard_map/ppermute | solution.py:342
  69.3 13.7 %collective-permute-start.15 = (bf16[320,1024]{1,0:T(8,128)(2,1)S(1)}, bf16[320,1024]{1,0:T(8,128)(2,1)S(1)}, u32[]{:S(2)}, u32[]{:S(2)}) collective-permute-start(bf16[320,1024]{1,0:T(8,128)(2,1)S(1)} %collective-permute-done.4.refs_0_), channel_id=1, source_target_pairs={{0,1},{1,0},{2,3},{3,2},{4,5},{5,4},{6,7},{7,6},{8,9},{9,8},{10,11... | collective-permute-start | bytes 1966088 | tf_op jit(solution)/shard_map/ppermute | solution.py:342
  70.6 12.3 %collective-permute-start.16 = (bf16[320,1024]{1,0:T(8,128)(2,1)S(1)}, bf16[320,1024]{1,0:T(8,128)(2,1)S(1)}, u32[]{:S(2)}, u32[]{:S(2)}) collective-permute-start(bf16[320,1024]{1,0:T(8,128)(2,1)S(1)} %collective-permute-done.5.refs_2_), channel_id=1, source_target_pairs={{0,1},{1,0},{2,3},{3,2},{4,5},{5,4},{6,7},{7,6},{8,9},{9,8},{10,11... | collective-permute-start | bytes 1966088 | tf_op jit(solution)/shard_map/ppermute | solution.py:342
  70.7 10.8 %collective-permute-start.10 = (bf16[160,1024]{1,0:T(8,128)(2,1)S(1)}, bf16[160,1024]{1,0:T(8,128)(2,1)S(1)}, u32[]{:S(2)}, u32[]{:S(2)}) collective-permute-start(bf16[160,1024]{1,0:T(8,128)(2,1)S(1)} %slice.39), channel_id=1, source_target_pairs={{0,4},{1,5},{2,6},{3,7},{4,8},{5,9},{6,10},{7,11},{8,12},{9,13},{1... | collective-permute-start | bytes 983048 | tf_op jit(solution)/shard_map/ppermute | solution.py:354
  71.0 10.5 %collective-permute-start.9 = (bf16[160,1024]{1,0:T(8,128)(2,1)S(1)}, bf16[160,1024]{1,0:T(8,128)(2,1)S(1)}, u32[]{:S(2)}, u32[]{:S(2)}) collective-permute-start(bf16[160,1024]{1,0:T(8,128)(2,1)S(1)} %slice.38), channel_id=1, source_target_pairs={{0,2},{1,3},{2,0},{3,1},{4,6},{5,7},{6,4},{7,5},{8,10},{9,11},{10,... | collective-permute-start | bytes 983048 | tf_op jit(solution)/shard_map/ppermute | solution.py:353
  81.5 4.9 %collective-permute-start.13 = (bf16[160,1024]{1,0:T(8,128)(2,1)S(1)}, bf16[160,1024]{1,0:T(8,128)(2,1)S(1)}, u32[]{:S(2)}, u32[]{:S(2)}) collective-permute-start(bf16[160,1024]{1,0:T(8,128)(2,1)S(1)} %collective-permute-done.9.refs_0_), channel_id=1, source_target_pairs={{0,1},{1,0},{2,3},{3,2},{4,5},{5,4},{6,7},{7,6},{8,9},{9,8},{10,11... | collective-permute-start | bytes 983048 | tf_op jit(solution)/shard_map/ppermute | solution.py:342
  91.0 20.5 %collective-permute-start.17 = (bf16[512,768]{1,0:T(8,128)(2,1)S(1)}, bf16[512,768]{1,0:T(8,128)(2,1)S(1)}, u32[]{:S(2)}, u32[]{:S(2)}) collective-permute-start(bf16[512,768]{1,0:T(8,128)(2,1)S(1)} %get-tuple-element.74.refs_0_), channel_id=1, source_target_pairs={{0,4},{1,5},{2,6},{3,7},{4,8},{5,9},{6,10},{7,11},{8,12},{9,13},{1... | collective-permute-start | bytes 2359304 | tf_op jit(solution)/shard_map/ppermute | solution.py:346
  91.1 20.4 %collective-permute-start.18 = (bf16[512,768]{1,0:T(8,128)(2,1)S(1)}, bf16[512,768]{1,0:T(8,128)(2,1)S(1)}, u32[]{:S(2)}, u32[]{:S(2)}) collective-permute-start(bf16[512,768]{1,0:T(8,128)(2,1)S(1)} %get-tuple-element.74.refs_0_), channel_id=1, source_target_pairs={{0,2},{1,3},{2,0},{3,1},{4,6},{5,7},{6,4},{7,5},{8,10},{9,11},{10,... | collective-permute-start | bytes 2359304 | tf_op jit(solution)/shard_map/ppermute | solution.py:346
  111.4 19.5 %collective-permute-start.19 = (bf16[512,768]{1,0:T(8,128)(2,1)S(1)}, bf16[512,768]{1,0:T(8,128)(2,1)S(1)}, u32[]{:S(2)}, u32[]{:S(2)}) collective-permute-start(bf16[512,768]{1,0:T(8,128)(2,1)S(1)} %collective-permute-done.17.refs_2_), channel_id=1, source_target_pairs={{0,4},{1,5},{2,6},{3,7},{4,8},{5,9},{6,10},{7,11},{8,12},{9,13},{1... | collective-permute-start | bytes 2359304 | tf_op jit(solution)/shard_map/ppermute | solution.py:346
  111.5 19.5 %collective-permute-start.20 = (bf16[512,768]{1,0:T(8,128)(2,1)S(1)}, bf16[512,768]{1,0:T(8,128)(2,1)}, u32[]{:S(2)}, u32[]{:S(2)}) collective-permute-start(bf16[512,768]{1,0:T(8,128)(2,1)S(1)} %collective-permute-done.17.refs_2_), channel_id=1, source_target_pairs={{0,2},{1,3},{2,0},{3,1},{4,6},{5,7},{6,4},{7,5},{8,10},{9,11},{10,... | collective-permute-start | bytes 2359304 | tf_op jit(solution)/shard_map/ppermute | solution.py:346
  131.0 18.7 %collective-permute-start.21 = (bf16[512,768]{1,0:T(8,128)(2,1)S(1)}, bf16[512,768]{1,0:T(8,128)(2,1)}, u32[]{:S(2)}, u32[]{:S(2)}) collective-permute-start(bf16[512,768]{1,0:T(8,128)(2,1)S(1)} %collective-permute-done.19.refs_6_), channel_id=1, source_target_pairs={{0,4},{1,5},{2,6},{3,7},{4,8},{5,9},{6,10},{7,11},{8,12},{9,13},{1... | collective-permute-start | bytes 2359304 | tf_op jit(solution)/shard_map/ppermute | solution.py:346
  131.0 22.8 %collective-permute-start.22 = (bf16[512,768]{1,0:T(8,128)(2,1)S(1)}, bf16[512,768]{1,0:T(8,128)(2,1)}, u32[]{:S(2)}, u32[]{:S(2)}) collective-permute-start(bf16[512,768]{1,0:T(8,128)(2,1)S(1)} %collective-permute-done.19.refs_6_), channel_id=1, source_target_pairs={{0,2},{1,3},{2,0},{3,1},{4,6},{5,7},{6,4},{7,5},{8,10},{9,11},{10,... | collective-permute-start | bytes 2359304 | tf_op jit(solution)/shard_map/ppermute | solution.py:346
  132.0 24.9 %collective-permute-start.30 = (bf16[512,768]{1,0:T(8,128)(2,1)S(1)}, bf16[512,768]{1,0:T(8,128)(2,1)S(1)}, u32[]{:S(2)}, u32[]{:S(2)}) collective-permute-start(bf16[512,768]{1,0:T(8,128)(2,1)S(1)} %get-tuple-element.74.refs_0_), channel_id=1, source_target_pairs={{0,1},{1,0},{2,3},{3,2},{4,5},{5,4},{6,7},{7,6},{8,9},{9,8},{10,11... | collective-permute-start | bytes 2359304 | tf_op jit(solution)/shard_map/ppermute | solution.py:342
  134.6 23.3 %collective-permute-start.31 = (bf16[512,768]{1,0:T(8,128)(2,1)S(1)}, bf16[512,768]{1,0:T(8,128)(2,1)S(1)}, u32[]{:S(2)}, u32[]{:S(2)}) collective-permute-start(bf16[512,768]{1,0:T(8,128)(2,1)S(1)} %collective-permute-done.17.refs_2_), channel_id=1, source_target_pairs={{0,1},{1,0},{2,3},{3,2},{4,5},{5,4},{6,7},{7,6},{8,9},{9,8},{10,11... | collective-permute-start | bytes 2359304 | tf_op jit(solution)/shard_map/ppermute | solution.py:342
  134.6 24.5 %collective-permute-start.32 = (bf16[512,768]{1,0:T(8,128)(2,1)S(1)}, bf16[512,768]{1,0:T(8,128)(2,1)S(1)}, u32[]{:S(2)}, u32[]{:S(2)}) collective-permute-start(bf16[512,768]{1,0:T(8,128)(2,1)S(1)} %collective-permute-done.18.refs_4_), channel_id=1, source_target_pairs={{0,1},{1,0},{2,3},{3,2},{4,5},{5,4},{6,7},{7,6},{8,9},{9,8},{10,11... | collective-permute-start | bytes 2359304 | tf_op jit(solution)/shard_map/ppermute | solution.py:342
  149.6 10.6 %collective-permute-start.33 = (bf16[512,768]{1,0:T(8,128)(2,1)S(1)}, bf16[512,768]{1,0:T(8,128)(2,1)S(1)}, u32[]{:S(2)}, u32[]{:S(2)}) collective-permute-start(bf16[512,768]{1,0:T(8,128)(2,1)S(1)} %collective-permute-done.19.refs_6_), channel_id=1, source_target_pairs={{0,1},{1,0},{2,3},{3,2},{4,5},{5,4},{6,7},{7,6},{8,9},{9,8},{10,11... | collective-permute-start | bytes 2359304 | tf_op jit(solution)/shard_map/ppermute | solution.py:342
  154.8 10.9 %collective-permute-start.37 = (bf16[256,768]{1,0:T(8,128)(2,1)S(1)}, bf16[256,768]{1,0:T(8,128)(2,1)}, u32[]{:S(2)}, u32[]{:S(2)}) collective-permute-start(bf16[256,768]{1,0:T(8,128)(2,1)S(1)} %slice.40), channel_id=1, source_target_pairs={{0,2},{1,3},{2,0},{3,1},{4,6},{5,7},{6,4},{7,5},{8,10},{9,11},{10,... | collective-permute-start | bytes 1179656 | tf_op jit(solution)/shard_map/ppermute | solution.py:353
  157.9 12.3 %collective-permute-start.38 = (bf16[256,768]{1,0:T(8,128)(2,1)S(1)}, bf16[256,768]{1,0:T(8,128)(2,1)}, u32[]{:S(2)}, u32[]{:S(2)}) collective-permute-start(bf16[256,768]{1,0:T(8,128)(2,1)S(1)} %slice.41), channel_id=1, source_target_pairs={{0,4},{1,5},{2,6},{3,7},{4,8},{5,9},{6,10},{7,11},{8,12},{9,13},{1... | collective-permute-start | bytes 1179656 | tf_op jit(solution)/shard_map/ppermute | solution.py:354
  158.8 20.5 %collective-permute-start.34 = (bf16[512,768]{1,0:T(8,128)(2,1)}, bf16[512,768]{1,0:T(8,128)(2,1)}, u32[]{:S(2)}, u32[]{:S(2)}) collective-permute-start(bf16[512,768]{1,0:T(8,128)(2,1)} %collective-permute-done.20.refs_8_), channel_id=1, source_target_pairs={{0,1},{1,0},{2,3},{3,2},{4,5},{5,4},{6,7},{7,6},{8,9},{9,8},{10,11... | collective-permute-start | bytes 2359304 | tf_op jit(solution)/shard_map/ppermute | solution.py:342
  160.0 20.1 %collective-permute-start.35 = (bf16[512,768]{1,0:T(8,128)(2,1)}, bf16[512,768]{1,0:T(8,128)(2,1)}, u32[]{:S(2)}, u32[]{:S(2)}) collective-permute-start(bf16[512,768]{1,0:T(8,128)(2,1)} %collective-permute-done.21.refs_10_), channel_id=1, source_target_pairs={{0,1},{1,0},{2,3},{3,2},{4,5},{5,4},{6,7},{7,6},{8,9},{9,8},{10,11... | collective-permute-start | bytes 2359304 | tf_op jit(solution)/shard_map/ppermute | solution.py:342
  161.1 18.9 %collective-permute-start.36 = (bf16[512,768]{1,0:T(8,128)(2,1)}, bf16[512,768]{1,0:T(8,128)(2,1)}, u32[]{:S(2)}, u32[]{:S(2)}) collective-permute-start(bf16[512,768]{1,0:T(8,128)(2,1)} %collective-permute-done.22.refs_12_), channel_id=1, source_target_pairs={{0,1},{1,0},{2,3},{3,2},{4,5},{5,4},{6,7},{7,6},{8,9},{9,8},{10,11... | collective-permute-start | bytes 2359304 | tf_op jit(solution)/shard_map/ppermute | solution.py:342
  165.8 9.9 %collective-permute-start.24 = (bf16[512,256]{1,0:T(8,128)(2,1)S(1)}, bf16[512,256]{1,0:T(8,128)(2,1)S(1)}, u32[]{:S(2)}, u32[]{:S(2)}) collective-permute-start(bf16[512,256]{1,0:T(8,128)(2,1)S(1)} %get-tuple-element.82.refs_0_), channel_id=1, source_target_pairs={{0,4},{1,5},{2,6},{3,7},{4,8},{5,9},{6,10},{7,11},{8,12},{9,13},{1... | collective-permute-start | bytes 786440 | tf_op jit(solution)/shard_map/ppermute | solution.py:346
  170.2 6.6 %collective-permute-start.25 = (bf16[512,256]{1,0:T(8,128)(2,1)S(1)}, bf16[512,256]{1,0:T(8,128)(2,1)S(1)}, u32[]{:S(2)}, u32[]{:S(2)}) collective-permute-start(bf16[512,256]{1,0:T(8,128)(2,1)S(1)} %get-tuple-element.82.refs_0_), channel_id=1, source_target_pairs={{0,2},{1,3},{2,0},{3,1},{4,6},{5,7},{6,4},{7,5},{8,10},{9,11},{10,... | collective-permute-start | bytes 786440 | tf_op jit(solution)/shard_map/ppermute | solution.py:346
  175.7 4.8 %collective-permute-start.39 = (bf16[256,768]{1,0:T(8,128)(2,1)}, bf16[256,768]{1,0:T(8,128)(2,1)}, u32[]{:S(2)}, u32[]{:S(2)}) collective-permute-start(bf16[256,768]{1,0:T(8,128)(2,1)} %collective-permute-done.37.refs_14_), channel_id=1, source_target_pairs={{0,1},{1,0},{2,3},{3,2},{4,5},{5,4},{6,7},{7,6},{8,9},{9,8},{10,11... | collective-permute-start | bytes 1179656 | tf_op jit(solution)/shard_map/ppermute | solution.py:342
  179.3 38.9 %collective-permute-start.23 = (bf16[512,256]{1,0:T(8,128)(2,1)}, bf16[512,256]{1,0:T(8,128)(2,1)S(1)}, u32[]{:S(2)}, u32[]{:S(2)}) collective-permute-start(bf16[512,256]{1,0:T(8,128)(2,1)} %copy-done.19), channel_id=1, source_target_pairs={{0,1},{1,0},{2,3},{3,2},{4,5},{5,4},{6,7},{7,6},{8,9},{9,8},{10,11... | collective-permute-start | bytes 786440 | tf_op jit(solution)/shard_map/ppermute | solution.py:342
  180.0 23.2 %collective-permute-start.28 = (bf16[512,256]{1,0:T(8,128)(2,1)}, bf16[512,256]{1,0:T(8,128)(2,1)S(1)}, u32[]{:S(2)}, u32[]{:S(2)}) collective-permute-start(bf16[512,256]{1,0:T(8,128)(2,1)} %copy-done.21), channel_id=1, source_target_pairs={{0,4},{1,5},{2,6},{3,7},{4,8},{5,9},{6,10},{7,11},{8,12},{9,13},{1... | collective-permute-start | bytes 786440 | tf_op jit(solution)/shard_map/ppermute | solution.py:346
  180.0 23.2 %collective-permute-start.29 = (bf16[512,256]{1,0:T(8,128)(2,1)}, bf16[512,256]{1,0:T(8,128)(2,1)S(1)}, u32[]{:S(2)}, u32[]{:S(2)}) collective-permute-start(bf16[512,256]{1,0:T(8,128)(2,1)} %copy-done.21), channel_id=1, source_target_pairs={{0,2},{1,3},{2,0},{3,1},{4,6},{5,7},{6,4},{7,5},{8,10},{9,11},{10,... | collective-permute-start | bytes 786440 | tf_op jit(solution)/shard_map/ppermute | solution.py:346
  180.5 37.7 %collective-permute-start.26 = (bf16[512,256]{1,0:T(8,128)(2,1)}, bf16[512,256]{1,0:T(8,128)(2,1)S(1)}, u32[]{:S(2)}, u32[]{:S(2)}) collective-permute-start(bf16[512,256]{1,0:T(8,128)(2,1)} %copy-done.21), channel_id=1, source_target_pairs={{0,1},{1,0},{2,3},{3,2},{4,5},{5,4},{6,7},{7,6},{8,9},{9,8},{10,11... | collective-permute-start | bytes 786440 | tf_op jit(solution)/shard_map/ppermute | solution.py:342
  203.2 13.0 %collective-permute-start.43 = (bf16[512,256]{1,0:T(8,128)(2,1)S(1)}, bf16[512,256]{1,0:T(8,128)(2,1)S(1)}, u32[]{:S(2)}, u32[]{:S(2)}) collective-permute-start(bf16[512,256]{1,0:T(8,128)(2,1)S(1)} %collective-permute-done.28.refs_6_), channel_id=1, source_target_pairs={{0,4},{1,5},{2,6},{3,7},{4,8},{5,9},{6,10},{7,11},{8,12},{9,13},{1... | collective-permute-start | bytes 786440 | tf_op jit(solution)/shard_map/ppermute | solution.py:346
  203.5 12.7 %collective-permute-start.44 = (bf16[512,256]{1,0:T(8,128)(2,1)S(1)}, bf16[512,256]{1,0:T(8,128)(2,1)S(1)}, u32[]{:S(2)}, u32[]{:S(2)}) collective-permute-start(bf16[512,256]{1,0:T(8,128)(2,1)S(1)} %collective-permute-done.28.refs_6_), channel_id=1, source_target_pairs={{0,2},{1,3},{2,0},{3,1},{4,6},{5,7},{6,4},{7,5},{8,10},{9,11},{10,... | collective-permute-start | bytes 786440 | tf_op jit(solution)/shard_map/ppermute | solution.py:346
  216.3 4.7 %collective-permute-start.47 = (bf16[256,256]{1,0:T(8,128)(2,1)S(1)}, bf16[256,256]{1,0:T(8,128)(2,1)S(1)}, u32[]{:S(2)}, u32[]{:S(2)}) collective-permute-start(bf16[256,256]{1,0:T(8,128)(2,1)S(1)} %slice.42), channel_id=1, source_target_pairs={{0,2},{1,3},{2,0},{3,1},{4,6},{5,7},{6,4},{7,5},{8,10},{9,11},{10,... | collective-permute-start | bytes 393224 | tf_op jit(solution)/shard_map/ppermute | solution.py:353
  216.8 6.6 %collective-permute-start.48 = (bf16[256,256]{1,0:T(8,128)(2,1)S(1)}, bf16[256,256]{1,0:T(8,128)(2,1)S(1)}, u32[]{:S(2)}, u32[]{:S(2)}) collective-permute-start(bf16[256,256]{1,0:T(8,128)(2,1)S(1)} %slice.43), channel_id=1, source_target_pairs={{0,4},{1,5},{2,6},{3,7},{4,8},{5,9},{6,10},{7,11},{8,12},{9,13},{1... | collective-permute-start | bytes 393224 | tf_op jit(solution)/shard_map/ppermute | solution.py:354
  217.0 19.4 %collective-permute-start.27 = (bf16[512,256]{1,0:T(8,128)(2,1)S(1)}, bf16[512,256]{1,0:T(8,128)(2,1)S(1)}, u32[]{:S(2)}, u32[]{:S(2)}) collective-permute-start(bf16[512,256]{1,0:T(8,128)(2,1)S(1)} %copy-done.24), channel_id=1, source_target_pairs={{0,1},{1,0},{2,3},{3,2},{4,5},{5,4},{6,7},{7,6},{8,9},{9,8},{10,11... | collective-permute-start | bytes 786440 | tf_op jit(solution)/shard_map/ppermute | solution.py:342
  218.1 18.3 %collective-permute-start.41 = (bf16[512,256]{1,0:T(8,128)(2,1)S(1)}, bf16[512,256]{1,0:T(8,128)(2,1)S(1)}, u32[]{:S(2)}, u32[]{:S(2)}) collective-permute-start(bf16[512,256]{1,0:T(8,128)(2,1)S(1)} %collective-permute-done.28.refs_6_), channel_id=1, source_target_pairs={{0,1},{1,0},{2,3},{3,2},{4,5},{5,4},{6,7},{7,6},{8,9},{9,8},{10,11... | collective-permute-start | bytes 786440 | tf_op jit(solution)/shard_map/ppermute | solution.py:342
  218.2 18.8 %collective-permute-start.42 = (bf16[512,256]{1,0:T(8,128)(2,1)S(1)}, bf16[512,256]{1,0:T(8,128)(2,1)S(1)}, u32[]{:S(2)}, u32[]{:S(2)}) collective-permute-start(bf16[512,256]{1,0:T(8,128)(2,1)S(1)} %collective-permute-done.29.refs_8_), channel_id=1, source_target_pairs={{0,1},{1,0},{2,3},{3,2},{4,5},{5,4},{6,7},{7,6},{8,9},{9,8},{10,11... | collective-permute-start | bytes 786440 | tf_op jit(solution)/shard_map/ppermute | solution.py:342
  221.0 17.0 %collective-permute-start.45 = (bf16[512,256]{1,0:T(8,128)(2,1)S(1)}, bf16[512,256]{1,0:T(8,128)(2,1)S(1)}, u32[]{:S(2)}, u32[]{:S(2)}) collective-permute-start(bf16[512,256]{1,0:T(8,128)(2,1)S(1)} %collective-permute-done.43.refs_10_), channel_id=1, source_target_pairs={{0,1},{1,0},{2,3},{3,2},{4,5},{5,4},{6,7},{7,6},{8,9},{9,8},{10,11... | collective-permute-start | bytes 786440 | tf_op jit(solution)/shard_map/ppermute | solution.py:342
  223.4 14.6 %collective-permute-start.46 = (bf16[512,256]{1,0:T(8,128)(2,1)S(1)}, bf16[512,256]{1,0:T(8,128)(2,1)S(1)}, u32[]{:S(2)}, u32[]{:S(2)}) collective-permute-start(bf16[512,256]{1,0:T(8,128)(2,1)S(1)} %collective-permute-done.44.refs_12_), channel_id=1, source_target_pairs={{0,1},{1,0},{2,3},{3,2},{4,5},{5,4},{6,7},{7,6},{8,9},{9,8},{10,11... | collective-permute-start | bytes 786440 | tf_op jit(solution)/shard_map/ppermute | solution.py:342
  (49 other events, 391.7 us)

commit v7 on v6

--- a/solution.py
+++ b/solution.py
@@ -13,7 +13,7 @@
 HEAD_SIZE = 128
 BLOCK_SLOTS = 512
 HEAD_GROUPS = QUERY_HEADS // KEY_VALUE_HEADS
-CHUNKS = ((0, 3), (3, 1))
+CHUNKS = ((0, KEY_VALUE_HEADS),)
 PLANE = 4
 PLANES = 4
 UNROLL = 2
@@ -223,111 +223,140 @@
                     ]
 
 
-def veil_kernel(stride, bounds_ref, routes_ref, veil_ref):
-    groups, keys = veil_ref.shape[0], veil_ref.shape[1]
+def veil_kernel(sets, stride, bounds_ref, routes_ref, more_ref, *veil_refs):
+    rest = jnp.zeros((HEAD_SIZE - stride, more_ref.shape[1]), jnp.float32)
+    share = routes_ref.shape[2] // routes_ref.shape[0]
 
     def one_group(group, carry):
         seats = pl.ds(pl.multiple_of(group * stride, 16), stride)
-        routes = routes_ref[group]
-        visible = (routes <= bounds_ref[seats, 0:1]) & (routes >= bounds_ref[seats, 1:2])
-        veil = jnp.where(visible, 0.0, MASKED)
-        rest = jnp.zeros((HEAD_SIZE - stride, veil.shape[1]), jnp.float32)
-        turned = jnp.transpose(jnp.concatenate([veil, rest], axis=0))
-        veil_ref[group] = turned[:keys].astype(jnp.bfloat16)
+        last, start = bounds_ref[seats, 0:1], bounds_ref[seats, 1:2]
+        both = []
+        for routes in (routes_ref[group], more_ref[...]):
+            veil = jnp.where((routes <= last) & (routes >= start), 0.0, MASKED)
+            veil = jnp.transpose(jnp.concatenate([veil, rest], axis=0))
+            both.append(veil.astype(jnp.bfloat16))
+        first = 0
+        for sources, veil_ref in zip(sets, veil_refs):
+            end = first + len(sources) * share
+            veil_ref[group] = jnp.concatenate([veil[first:end] for veil in both], axis=0)
+            first = end
         return carry
 
-    lax.fori_loop(0, groups, one_group, 0)
-
-
-def attend_kernel(
-    head, heads, pieces, extra, stride, seat_ref, more_ref, queries_ref, veil_ref, *refs
-):
-    first_head, place = head
-    parts, refs = refs[: len(pieces)], refs[-9:]
-    out_ref, blocks, more, query, veil, seen_by, mixed_ref, result_ref, done = refs
-    ranks, count = blocks.shape[1], blocks.shape[2]
-    packed = query.shape[0] // ranks
-    share = count // ranks
-    spare = share + extra
-    copies = [
-        pltpu.make_async_copy(queries_ref.at[first_head + place], query, done.at[0]),
-        pltpu.make_async_copy(veil_ref, veil, done.at[1]),
-    ]
-    for part in range(2):
-        lanes = pl.ds((part * heads + place) * HEAD_SIZE, HEAD_SIZE)
-        for (source, first), ref in zip(pieces, parts):
-            rows = pl.ds(first, ref.shape[0])
-            copies.append(
-                pltpu.make_async_copy(
-                    ref.at[:, lanes], blocks.at[part, source, rows], done.at[len(copies)]
-                )
-            )
-    for copy in copies:
-        copy.start()
-    mixed_ref[...] = jnp.zeros(mixed_ref.shape, jnp.bfloat16)
+    lax.fori_loop(0, routes_ref.shape[0], one_group, 0)
+
+
+def attend_kernel(starts, before, spare, stride, more, last, *refs):
+    more_ref, queries_ref, veil_ref = refs[:3]
+    refs = refs[3:]
+    blocks = []
+    for first_rows in starts:
+        blocks.append(dict(zip(first_rows, refs)))
+        refs = refs[len(first_rows) :]
+    if more:
+        top_ref, sum_ref, total_ref = refs[:3]
+        refs = refs[3:]
+    if last:
+        seat_ref, out_ref, listed_rows, seen_by, mixed_ref, result_ref, done = refs
+        mixed_ref[...] = jnp.zeros(mixed_ref.shape, jnp.bfloat16)
+    else:
+        new_top_ref, new_sum_ref, new_total_ref, listed_rows, seen_by = refs
+    heads, ranks = queries_ref.shape[0], veil_ref.shape[0]
+    packed = queries_ref.shape[1] // ranks
+    wide = heads * HEAD_SIZE
+    share = listed_rows.shape[0] // len(starts)
+    count = share * ranks
+
     token = lax.broadcasted_iota(jnp.int32, (packed, HEAD_SIZE), 0)
     lane = lax.broadcasted_iota(jnp.int32, (packed, HEAD_SIZE), 1)
     own = lane < 0
     for at in range(HEAD_GROUPS):
         own = own | ((token == lane + at * spare) & (lane < spare))
     seen_by[...] = own.astype(jnp.float32).astype(jnp.bfloat16)
-    listed = ranks * extra
-    lines = lax.broadcasted_iota(jnp.int32, (listed, count), 1)
-    picks = [
-        (lines == more_ref[j * listed : (j + 1) * listed]).astype(jnp.float32).astype(jnp.bfloat16)
-        for j in range(ranks)
-    ]
-    column = lax.broadcasted_iota(jnp.int32, (1, ranks * listed), 1)
-    source, rest = lax.div(column, listed), lax.rem(column, listed)
-    group, index = lax.div(rest, extra), lax.rem(rest, extra)
-    regroup = one_hot_rows(ranks * listed, group * listed + source * extra + index)
-    for copy in copies:
-        copy.wait()
-    for part in range(2):
-        found = [
-            contract(picks[j], blocks[part, j], 1, 0).astype(jnp.bfloat16) for j in range(ranks)
-        ]
-        more[part] = contract(regroup, jnp.concatenate(found, axis=0), 1, 0).astype(jnp.bfloat16)
+    lines = lax.broadcasted_iota(jnp.int32, (share, count), 1)
+    for at, block in enumerate(blocks):
+        places = more_ref[(before + at) * share : (before + at + 1) * share]
+        pick = (lines == places).astype(jnp.float32).astype(jnp.bfloat16)
+        for first in range(0, 2 * wide, 2 * HEAD_SIZE):
+            lanes = slice(first, first + 2 * HEAD_SIZE)
+            found = [
+                contract(pick[:, row : row + ref.shape[0]], ref[:, lanes], 1, 0)
+                for row, ref in block.items()
+            ]
+            listed_rows[at * share : (at + 1) * share, lanes] = sum(found).astype(jnp.bfloat16)
     scale = math.log2(math.e) / math.sqrt(HEAD_SIZE)
 
-    def rows_of(part, group):
-        window = pl.ds(pl.multiple_of(group * share, 16), share)
-        rows = [blocks[part, j, window] for j in range(ranks)]
-        rows.append(more[part, pl.ds(pl.multiple_of(group * listed, 16), listed)])
-        return jnp.concatenate(rows, axis=0)
-
-    def some_groups(step, carry):
-        groups = [step * UNROLL + at for at in range(UNROLL)]
+    def rows_of(group, row, first):
+        lanes = slice(first, first + HEAD_SIZE)
+        window = pl.ds(pl.multiple_of(group * share - row, 16), share)
+        rows = [block[row][window, lanes] for block in blocks]
+        return jnp.concatenate(rows + [listed_rows[:, lanes]], axis=0)
+
+    def add_heads(group, row, some):
+        tokens = pl.ds(pl.multiple_of(group * packed, 16), packed)
         scores = []
-        for group in groups:
-            tokens = pl.ds(pl.multiple_of(group * packed, 16), packed)
-            left = jnp.concatenate([query[tokens], seen_by[...]], axis=1)
-            right = jnp.concatenate([rows_of(0, group), veil[group]], axis=1)
+        for head in some:
+            left = jnp.concatenate([queries_ref[head, tokens], seen_by[...]], axis=1)
+            keys = rows_of(group, row, head * HEAD_SIZE)
+            right = jnp.concatenate([keys, veil_ref[group]], axis=1)
             scores.append(contract(left, right, 1, 1))
-        weights = []
-        for one in scores:
-            top = jnp.max(one, axis=1, keepdims=True)
-            weights.append(jnp.exp2((one - top) * scale).astype(jnp.bfloat16))
-        for group, weight in zip(groups, weights):
-            values = rows_of(1, group)
+        tops, weights = [], []
+        for head, score in zip(some, scores):
+            top = jnp.max(score, axis=1, keepdims=True)
+            if more:
+                top = jnp.maximum(top_ref[head, tokens], top)
+            else:
+                top = jnp.broadcast_to(top, (packed, HEAD_SIZE))
+            tops.append(top)
+            tiled = jnp.concatenate([top] * (score.shape[1] // HEAD_SIZE), axis=1)
+            weights.append(jnp.exp2((score - tiled) * scale).astype(jnp.bfloat16))
+        for head, top, weight in zip(some, tops, weights):
+            values = rows_of(group, row, wide + head * HEAD_SIZE)
             values = jnp.concatenate([values, jnp.ones_like(values)], axis=1)
             mixed = contract(weight, values, 1, 0)
-            mixed = mixed[:, :HEAD_SIZE] / mixed[:, HEAD_SIZE:]
-            seats = pl.ds(pl.multiple_of(group * stride, 16), spare)
-            for at in range(HEAD_GROUPS):
-                lanes = slice(at * HEAD_SIZE, (at + 1) * HEAD_SIZE)
-                rows = mixed[at * spare : (at + 1) * spare]
-                mixed_ref[seats, lanes] = rows.astype(jnp.bfloat16)
-        return carry
-
-    lax.fori_loop(0, ranks // UNROLL, some_groups, 0)
-    seat_lanes = lax.broadcasted_iota(jnp.int32, (count, mixed_ref.shape[0]), 1)
-    seats = (seat_lanes == seat_ref[...]).astype(jnp.float32).astype(jnp.bfloat16)
-    result_ref[...] = contract(seats, mixed_ref[...], 1, 0).astype(jnp.bfloat16)
-    lanes = pl.ds((first_head + place) * HEAD_GROUPS * HEAD_SIZE, HEAD_GROUPS * HEAD_SIZE)
-    leave = pltpu.make_async_copy(result_ref, out_ref.at[:, lanes], done.at[len(copies)])
-    leave.start()
-    leave.wait()
+            total, weight_sum = mixed[:, :HEAD_SIZE], mixed[:, HEAD_SIZE:]
+            if more:
+                fade = jnp.exp2((top_ref[head, tokens] - top) * scale)
+                total = total + fade * total_ref[head, tokens]
+                weight_sum = weight_sum + fade * sum_ref[head, tokens]
+            if last:
+                mixed = total / weight_sum
+                seats = pl.ds(pl.multiple_of(group * stride, 16), spare)
+                for at in range(HEAD_GROUPS):
+                    place = (head * HEAD_GROUPS + at) * HEAD_SIZE
+                    rows = mixed[at * spare : (at + 1) * spare]
+                    mixed_ref[seats, place : place + HEAD_SIZE] = rows.astype(jnp.bfloat16)
+            else:
+                new_top_ref[head, tokens] = top
+                new_sum_ref[head, tokens] = weight_sum
+                new_total_ref[head, tokens] = total
+
+    rows = sorted({row for first_rows in starts for row in first_rows})
+    for row, end in zip(rows, rows[1:] + [count]):
+
+        def one_group(group, carry, row=row):
+            for head in range(0, heads, UNROLL):
+                add_heads(group, row, range(head, head + UNROLL))
+            return carry
+
+        lax.fori_loop(row // share, end // share, one_group, 0)
+    if last:
+        seat_lanes = lax.broadcasted_iota(jnp.int32, (count, mixed_ref.shape[0]), 1)
+        seats = (seat_lanes == seat_ref[...]).astype(jnp.float32).astype(jnp.bfloat16)
+        span = HEAD_GROUPS * HEAD_SIZE
+        leaving = []
+        for head in range(heads):
+            lanes = slice(head * span, (head + 1) * span)
+            rows = contract(seats, mixed_ref[:, lanes], 1, 0)
+            result_ref[:, lanes] = rows.astype(jnp.bfloat16)
+            lanes = pl.ds(head * span, span)
+            leaving.append(
+                pltpu.make_async_copy(
+                    result_ref.at[:, lanes], out_ref.at[:, lanes], done.at[head]
+                )
+            )
+            leaving[-1].start()
+        for one in leaving:
+            one.wait()
 
 
 def spread(block, ranks, held):
@@ -387,7 +416,6 @@
     listed = ranks * extra
     stride = -(-spare // 16) * 16
     packed = -(-HEAD_GROUPS * spare // 16) * 16
-    key_count = ranks * (share + extra)
     query_width = queries.shape[1]
     shape = jax.ShapeDtypeStruct
 
@@ -420,22 +448,12 @@
     next(sending)
     all_positions = plan[:, width:].reshape(-1, HEAD_SIZE)
     owners = source_order(ranks)
-    sources = plan[:, :width][owners]
-    key_routes = jnp.concatenate(
-        [
-            sources[:, :rows].reshape(ranks, ranks, share).transpose(1, 0, 2).reshape(ranks, -1),
-            sources[:, rows : rows + listed]
-            .reshape(ranks, ranks, extra)
-            .transpose(1, 0, 2)
-            .reshape(ranks, -1),
-        ],
-        axis=1,
-    ).reshape(ranks, 1, key_count)
-    wide_keys = -(-key_count // HEAD_SIZE) * HEAD_SIZE
-    key_routes = jnp.pad(
-        key_routes, ((0, 0), (0, 0), (0, wide_keys - key_count)), constant_values=-1
-    )
-    more_places = sources[:, rows + listed :].reshape(ranks * listed, 1)
+    planes = ranks // PLANE
+    sets = [(0, 2 * planes)] + [
+        (step, step + 2 * planes, step + planes - 1, step + 3 * planes - 1)
+        for step in range(1, planes)
+    ]
+    sets.append((2 * planes - 1, 4 * planes - 1))
 
     half = HEAD_SIZE // 2
     frequency = 1000000.0 ** (-(jnp.arange(half, dtype=jnp.float32) * 2.0 / HEAD_SIZE))
@@ -462,7 +480,6 @@
     )
 
     shard, wide = key_matrix.shape[0], 2 * key_matrix.shape[1]
-    planes = ranks // PLANE
 
     def chip_parts(sources):
         chips, arrays = [], []
@@ -500,9 +517,7 @@
             name="add_part",
         )(owners, hidden, *arrays, *more)
 
-    turned, bounds, cosine, sine, key_routes, more_places = sending.send(
-        (turned, bounds, cosine, sine, key_routes, more_places)
-    )
+    turned, bounds, cosine, sine = sending.send((turned, bounds, cosine, sine))
     next(sending)
     (total,) = sending.send((add_part(None, (0, 1, planes)),))
     next(sending)
@@ -510,7 +525,7 @@
     total = add_part(total, (3, planes + 2))
     chips, arrays = chip_parts((planes + 3,))
     bias = jnp.concatenate([key_projection_bias, value_projection_bias])
-    pairs = pl.pallas_call(
+    (pairs,) = pl.pallas_call(
         functools.partial(finish_kernel, chips),
         out_shape=tuple(
             shape((rows, 2 * heads * HEAD_SIZE), jnp.bfloat16) for _, heads in CHUNKS
@@ -532,66 +547,80 @@
         total,
     )
 
-    def attend(out, chunk, held, place):
-        first_head, heads = CHUNKS[chunk]
-        pieces = [(source, first) for source in held for first, _ in held[source]]
-        arrays = [array for source in held for _, array in held[source]]
-        taken = [] if out is None else [out]
-        fixed = [seat.reshape(rows, 1), more_places, turned, veil]
-        span = HEAD_GROUPS * HEAD_SIZE
+    blocks = {}
+    sending = spread(pairs, ranks, blocks)
+    next(sending)
+    order = [source for sources in sets for source in sources]
+    ordered = plan[:, :width][jnp.stack([owners[source] for source in order])]
+    key_routes = ordered[:, :rows].reshape(ranks, ranks, share).transpose(1, 0, 2)
+    more_places = ordered[:, rows + listed :].reshape(ranks * listed, 1)
+    veils = pl.pallas_call(
+        functools.partial(veil_kernel, sets, stride),
+        out_shape=tuple(
+            shape((ranks, 2 * share * len(sources), HEAD_SIZE), jnp.bfloat16) for sources in sets
+        ),
+        in_specs=[VMEM] * 3,
+        out_specs=(VMEM,) * len(sets),
+        compiler_params=grant(16),
+        cost_estimate=cost(3 * 10**9, 4 * ranks * rows * HEAD_SIZE),
+        name="veil",
+    )(
+        bounds,
+        key_routes.reshape(ranks, 1, rows),
+        ordered[:, rows : rows + listed].reshape(1, ranks * listed),
+    )
+
+    def attend(state, index):
+        sources, last = sets[index], index == len(sets) - 1
+        starts = [tuple(first for first, _ in blocks[source]) for source in sources]
+        arrays = [array for source in sources for _, array in blocks[source]]
+        fixed = [more_places, turned, veils[index], *arrays, *state]
+        kept = shape((KEY_VALUE_HEADS, ranks * packed, HEAD_SIZE), jnp.float32)
+        scratch_shapes = [
+            pltpu.VMEM((len(sources) * share, wide), jnp.bfloat16),
+            pltpu.VMEM((packed, HEAD_SIZE), jnp.bfloat16),
+        ]
+        if last:
+            fixed.append(seat.reshape(rows, 1))
+            scratch_shapes += [
+                pltpu.VMEM((ranks * stride, query_width), jnp.bfloat16),
+                pltpu.VMEM((rows, query_width), jnp.bfloat16),
+                pltpu.SemaphoreType.DMA((KEY_VALUE_HEADS,)),
+            ]
+        keys = 2 * share * len(sources)
         return pl.pallas_call(
-            functools.partial(attend_kernel, (first_head, place), heads, pieces, extra, stride),
-            out_shape=shape((rows, query_width), jnp.bfloat16),
-            in_specs=[VMEM] * 2 + [HBM] * (2 + len(pieces) + len(taken)),
-            out_specs=HBM,
-            scratch_shapes=[
-                pltpu.VMEM((2, ranks, rows, HEAD_SIZE), jnp.bfloat16),
-                pltpu.VMEM((2, ranks * listed, HEAD_SIZE), jnp.bfloat16),
-                pltpu.VMEM((ranks * packed, HEAD_SIZE), jnp.bfloat16),
-                pltpu.VMEM(veil.shape, jnp.bfloat16),
-                pltpu.VMEM((packed, HEAD_SIZE), jnp.bfloat16),
-                pltpu.VMEM((ranks * stride, span), jnp.bfloat16),
-                pltpu.VMEM((rows, span), jnp.bfloat16),
-                pltpu.SemaphoreType.DMA((2 * len(pieces) + 3,)),
-            ],
-            input_output_aliases={len(fixed) + len(pieces): 0} if taken else {},
-            compiler_params=grant(24),
+            functools.partial(
+                attend_kernel,
+                starts,
+                sum(len(one) for one in sets[:index]),
+                spare,
+                stride,
+                bool(state),
+                last,
+            ),
+            out_shape=shape((rows, query_width), jnp.bfloat16) if last else (kept,) * 3,
+            in_specs=[VMEM] * len(fixed),
+            out_specs=HBM if last else (VMEM,) * 3,
+            scratch_shapes=scratch_shapes,
+            input_output_aliases={}
+            if last or not state
+            else {len(fixed) - 3 + at: at for at in range(3)},
+            compiler_params=grant(20),
             cost_estimate=cost(
-                16 * rows * stride * ranks * span, 4 * ranks * rows * HEAD_SIZE
+                8 * ranks * KEY_VALUE_HEADS * packed * (keys + 256) * HEAD_SIZE,
+                2 * keys * rows * HEAD_SIZE,
             ),
             name="attend",
-        )(*fixed, *arrays, *taken)
-
-    early, late = {}, {}
-    sending = spread(pairs[0], ranks, early)
+        )(*fixed)
+
+    state = ()
+    for step in range(planes - 1):
+        if step:
+            next(sending)
+        state = sending.send(tuple(attend(state, step)))
     next(sending)
-    veil = pl.pallas_call(
-        functools.partial(veil_kernel, stride),
-        out_shape=shape((ranks, key_count, HEAD_SIZE), jnp.bfloat16),
-        in_specs=[VMEM] * 2,
-        out_specs=VMEM,
-        compiler_params=grant(16),
-        cost_estimate=cost(2 * 10**9, 4 * ranks * key_count * HEAD_SIZE),
-        name="veil",
-    )(bounds, key_routes)
-    (veil,) = sending.send((veil,))
-    for _ in range(planes - 2):
-        next(sending)
-        sending.send(())
-    mark = next(sending)
-    sending.send(())
-    last, _ = lax.optimization_barrier((pairs[1], mark))
-    sending = spread(last, ranks, late)
-    out = None
-    next(sending)
-    sending.send(())
-    for place in range(2):
-        next(sending)
-        out = attend(out, 0, early, place)
-        (out,) = sending.send((out,))
-    next(sending)
-    (out,) = sending.send((attend(out, 0, early, 2),))
-    return attend(out, 1, late, 0)
+    state = sending.send(tuple(attend(state, planes - 1)))
+    return attend(state, planes)
 
 
 def apply_rotary(rows, slot_offset, heads):

time: 251 us -> 250 us (level)
  Pallas kernels: 73.3 us -> 102 us
  starting transfers between devices: 41.2 us -> 24.5 us
  waiting for transfers between devices: 87 us -> 71.9 us
  local copies, waits for them, and re-layouts: 45 us -> 50.2 us
    pallas_call x5 -> x6, Pallas kernels: 48.8 us -> 75.7 us  [the longest x5 72.2 us: attend(): pl.pallas_call(functools.partial(attend_kernel, starts, sum((len(one) for...]
    ppermute x9 -> x6, waiting for transfers between devices: 59.1 us -> 45.5 us  [spread(): lax.ppermute(lane, 'dp', ring)]
    ppermute x27 -> x18, starting transfers between devices: 22.3 us -> 10.6 us  [keep(): lax.ppermute(array, 'dp', beside)]
    ppermute x27 -> x18, waiting for transfers between devices: 1.08 us -> 11.8 us  [keep(): lax.ppermute(array, 'dp', beside)]
    another operation x0 -> x1, local copies, waits for them, and re-layouts: none -> 10 us  [gather_plan(): ordered = plan[:, :width][jnp.stack([owners[source] for source in order])]]
    ppermute x3 -> x2, waiting for transfers between devices: 6.71 us -> 0.01 us  [spread(): over = lax.ppermute(lane[:half], 'dp', across)]
    ppermute x3 -> x2, waiting for transfers between devices: 10.9 us -> 5.17 us  [spread(): around = lax.ppermute(other[half:], 'dp', ring)]
    reshape x7 -> x6, local copies, waits for them, and re-layouts: 6.43 us -> 0.73 us  [the longest x1 0.26 us: gather_plan(): more_places = ordered[:, rows + listed:].reshape(ranks * listed, 1)]
  transfers between devices with their start and end apart: 52 -> 35, of which waited for: 13 -> 15; matrix products, arithmetic and copies ran while one was open for 8% -> 8% of each run, Pallas kernels for 23% -> 32%
where the time goes in v7:
time: 250 us; the launch traced here: 249 us
  Pallas kernels  102 us (41%)
  waiting for transfers between devices  71.9 us (29%)
  local copies, waits for them, and re-layouts  50.2 us (20%)
  starting transfers between devices  24.5 us (10%)
    pallas_call x5, Pallas kernels, attend(): pl.pallas_call(functools.partial(attend_kernel, starts, sum((len(one) for...  72.2 us
    ppermute x6, waiting for transfers between devices, spread(): lax.ppermute(lane, 'dp', ring)  45.5 us
    unnamed x54, local copies, waits for them, and re-layouts  29.5 us
    pallas_call x3, Pallas kernels, add_part(): pl.pallas_call(functools.partial(part_kernel, chips, bool(more)), out_sha...  13.5 us
    ppermute x18, waiting for transfers between devices, keep(): lax.ppermute(array, 'dp', beside)  11.8 us
    ppermute x18, starting transfers between devices, keep(): lax.ppermute(array, 'dp', beside)  10.6 us
    another operation x1, local copies, waits for them, and re-layouts, gather_plan(): ordered = plan[:, :width][jnp.stack([owners[source] for source in order])]  10 us
    all_to_all x1, waiting for transfers between devices, gather_plan(): lax.all_to_all(jnp.broadcast_to(plan, (ranks, width + slots)), 'dp', spli...  9.37 us
  transfers between devices with their start and end apart: 35, of which 15 were waited for; matrix products, arithmetic and copies ran while one was open for 8% of the time, Pallas kernels for 32%

profile of v7, /device:TPU:1, one launch (start us, length us, event | category | flops | bytes accessed | tf_op | source)
XLA Modules:
  0.0 249.0 jit_solution(5024388507734350777)
XLA Ops:
  0.0 1.7 constant_dynamic-update-slice_fusion.1
  1.7 1.7 constant_dynamic-update-slice_fusion.refs_0_
  3.4 2.1 collective-permute-start
  5.6 1.2 collective-permute-start.1
  6.8 15.6 %collective-permute-done.refs_2_ = bf16[320,1024]{1,0:T(8,128)(2,1)} collective-permute-done((bf16[320,1024]{1,0:T(8,128)(2,1)}, bf16[320,1024]{1,0:T(8,128)(2,1)}, u32[]{:S(2)}, u32[]{:S(2)}) %collective-permute-start) | collective-permute-done | bytes 655392 | tf_op jit(solution)/shard_map/ppermute | solution.py:375
  22.5 1.2 collective-permute-start.3
  23.7 2.4 collective-permute-start.6
  29.0 4.2 %all-to-all-start = ((s32[16,1,1600]{2,1,0:T(1,128)}), s32[16,1,1600]{2,1,0:T(1,128)S(1)}, u32[]{:S(2)}, u32[]{:S(2)}) async-start(s32[16,1,1600]{2,1,0:T(1,128)} %broadcast_in_dim.4), calls=%async_computation | async-start | bytes 212992 | tf_op jit(solution)/shard_map/all_to_all | solution.py:444
  34.3 9.4 %all-to-all-done = s32[16,1,1600]{2,1,0:T(1,128)S(1)} async-done(((s32[16,1,1600]{2,1,0:T(1,128)}), s32[16,1,1600]{2,1,0:T(1,128)S(1)}, u32[]{:S(2)}, u32[]{:S(2)}) %all-to-all-start) | async-done | bytes 102432 | tf_op jit(solution)/shard_map/all_to_all | solution.py:444
  46.6 1.7 copy-done.18
  48.4 6.3 %turn_queries.1 = (bf16[4,2816,128]{2,1,0:T(8,128)(2,1)S(1)}, s32[768,128]{1,0:T(8,128)S(1)}, f32[512,128]{1,0:T(8,128)S(1)}, f32[512,128]{1,0:T(8,128)S(1)}) custom-call(s32[512,1]{1,0:T(8,128)S(1)} %copy-done.15, s32[1,512]{1,0:T(1,128)S(1)} %get-tuple-element.67.seat_ref, s32[128,128]{1,0:T(8,128)S(1)} %copy-done.16, ...), custom_call_target="tpu_custom_call" | custom-call | flops 4026531840 | bytes 5242880 | tf_op jit(solution)/shard_map/turn_queries/pallas_call | solution.py:460
  59.7 2.5 copy-done.6
  62.2 5.4 %add_part.3.refs_4_ = f32[512,1024]{1,0:T(8,128)S(1)} custom-call(s32[16]{0:T(128)S(1)} %pad_add_fusion.owners_ref, bf16[512,5120]{1,0:T(8,128)(2,1)S(1)} %copy-done.6, bf16[320,1024]{1,0:T(8,128)(2,1)} %constant_dynamic-update-slice_fusion.refs_0_, bf16[320,1024]{1,0:T(8,128)(2,1)} %collective-permute-done.6.refs_1_, ...), custom_call_target="tpu_custom_call" | custom-call | flops 2013265920 | bytes 10092544 | tf_op jit(solution)/shard_map/add_part/pallas_call | solution.py:509
  67.6 8.2 %collective-permute-done.4.refs_0_ = bf16[320,1024]{1,0:T(8,128)(2,1)S(1)} collective-permute-done((bf16[320,1024]{1,0:T(8,128)(2,1)}, bf16[320,1024]{1,0:T(8,128)(2,1)S(1)}, u32[]{:S(2)}, u32[]{:S(2)}) %collective-permute-start.4) | collective-permute-done | bytes 655392 | tf_op jit(solution)/shard_map/ppermute | solution.py:375
  75.8 0.9 collective-permute-start.15
  76.8 1.0 slice.97
  79.4 4.0 %add_part.4.refs_4_ = f32[512,1024]{1,0:T(8,128)S(1)} custom-call(s32[16]{0:T(128)S(1)} %pad_add_fusion.owners_ref, bf16[512,5120]{1,0:T(8,128)(2,1)S(1)} %copy-done.6, bf16[320,1024]{1,0:T(8,128)(2,1)S(1)} %copy-done.8, bf16[320,1024]{1,0:T(8,128)(2,1)} %collective-permute-done.11.refs_1_, bf16[320,1024]{1,0:T(8,128)(2,1)} %collective-permute-done.3.refs_2_, ...), custom_call_target="tpu_custom_call" | custom-call | flops 1342177280 | bytes 8126464 | tf_op jit(solution)/shard_map/add_part/pallas_call | solution.py:509
  83.4 5.2 %collective-permute-done.10.refs_1_ = bf16[160,1024]{1,0:T(8,128)(2,1)S(1)} collective-permute-done((bf16[160,1024]{1,0:T(8,128)(2,1)S(1)}, bf16[160,1024]{1,0:T(8,128)(2,1)S(1)}, u32[]{:S(2)}, u32[]{:S(2)}) %collective-permute-start.10) | collective-permute-done | bytes 327712 | tf_op jit(solution)/shard_map/ppermute | solution.py:383
  88.6 1.4 collective-permute-start.13
  90.7 4.1 %add_part.5.refs_4_ = f32[512,1024]{1,0:T(8,128)S(1)} custom-call(s32[16]{0:T(128)S(1)} %pad_add_fusion.owners_ref, bf16[512,5120]{1,0:T(8,128)(2,1)S(1)} %copy-done.6, bf16[320,1024]{1,0:T(8,128)(2,1)S(1)} %collective-permute-done.4.refs_0_, bf16[320,1024]{1,0:T(8,128)(2,1)S(1)} %collective-permute-done.15.refs_1_, ...), custom_call_target="tpu_custom_call" | custom-call | flops 1342177280 | bytes 8126464 | tf_op jit(solution)/shard_map/add_part/pallas_call | solution.py:509
  94.8 5.4 %finish.1.refs_3_ = bf16[512,1024]{1,0:T(8,128)(2,1)} custom-call(s32[16]{0:T(128)S(1)} %pad_add_fusion.owners_ref, bf16[512,5120]{1,0:T(8,128)(2,1)S(1)} %bitcast.31, f32[1,1024]{1,0:T(1,128)S(1)} %maximum_convert_fusion.bias_ref, f32[512,128]{1,0:T(8,128)S(1)} %copy-done.12, f32[512,128]{1,0:T(8,128)S(1)} %copy-done.14, ...), custom_call_target="tpu_custom_call" | custom-call | flops 671088640 | bytes 6160384 | tf_op jit(solution)/shard_map/finish/pallas_call | solution.py:528
  102.2 10.0 %stack.51 = s32[16,1]{0,1:T(1,128)S(1)} concatenate(s32[1,1]{0,1:T(1,128)} %bitcast.2, s32[1,1]{0,1:T(1,128)} %bitcast.3, s32[1,1]{0,1:T(1,128)} %bitcast.4, s32[1,1]{0,1:T(1,128)} %bitcast.5, s32[1,1]{0,1:T(1,128)} %bitcast.6, s32[1,1]{0,1:T(1,128)} %bitcast.7, s32[1,1]{0,1:T(1,128)} %bitcast.8, s32[1,1]{0,1:T(1,128)} %bitcast.9, s32[1,1]{0,1:T(1,128)} %bitcast.10, ...), dimensions={0} | concatenate | bytes 128 | tf_op jit(solution)/shard_map/stack | solution.py:554
  115.1 1.0 copy-done.20
  116.0 3.5 %veil.1 = (bf16[16,128,128]{2,1,0:T(8,128)(2,1)S(1)}, bf16[16,256,128]{2,1,0:T(8,128)(2,1)S(1)}, bf16[16,256,128]{2,1,0:T(8,128)(2,1)S(1)}, bf16[16,256,128]{2,1,0:T(8,128)(2,1)S(1)}, bf16[16,128,128]{2,1,0:T(8,128)(2,1)S(1)}) custom-call(s32[768,128]{1,0:T(8,128)S(1)} %copy-done.20, s32[16,1,512]{2,1,0:T(1,128)S(1)} %reshape.676.routes_ref, ...), custom_call_target="tpu_custom_call" | custom-call | flops 3000000000 | bytes 4194304 | tf_op jit(solution)/shard_map/veil/pallas_call | solution.py:557
  120.3 13.1 %attend.5 = (f32[4,2816,128]{2,1,0:T(8,128)S(1)}, f32[4,2816,128]{2,1,0:T(8,128)S(1)}, f32[4,2816,128]{2,1,0:T(8,128)S(1)}) custom-call(s32[512,1]{1,0:T(8,128)S(1)} %reshape.687.refs_0_, bf16[4,2816,128]{2,1,0:T(8,128)(2,1)S(1)} %get-tuple-element.72.refs_1_, bf16[16,128,128]{2,1,0:T(8,128)(2,1)S(1)} %get-tuple-element.87.refs_2_, ...), custom_call_target="tpu_custom_call" | custom-call | flops 4429185024 | bytes 16777216 | tf_op jit(solution)/shard_map/attend/pallas_call | solution.py:591
  133.4 5.7 %collective-permute-done.17.refs_3_ = bf16[512,1024]{1,0:T(8,128)(2,1)} collective-permute-done((bf16[512,1024]{1,0:T(8,128)(2,1)}, bf16[512,1024]{1,0:T(8,128)(2,1)}, u32[]{:S(2)}, u32[]{:S(2)}) %collective-permute-start.17) | collective-permute-done | bytes 1048608 | tf_op jit(solution)/shard_map/ppermute | solution.py:375
  140.6 1.8 collective-permute-done.22.refs_4_
  142.4 1.5 collective-permute-done.23.refs_6_
  143.9 15.0 %attend.6 = (f32[4,2816,128]{2,1,0:T(8,128)S(1)}, f32[4,2816,128]{2,1,0:T(8,128)S(1)}, f32[4,2816,128]{2,1,0:T(8,128)S(1)}) custom-call(s32[512,1]{1,0:T(8,128)S(1)} %reshape.687.refs_0_, bf16[4,2816,128]{2,1,0:T(8,128)(2,1)S(1)} %get-tuple-element.72.refs_1_, ...), custom_call_target="tpu_custom_call", output_to_operand_aliasing={{0}: (7, {}), {1}: (8, {}), {2}: (9, {})} | custom-call | flops 5905580032 | bytes 33554432 | tf_op jit(solution)/shard_map/attend/pallas_call | solution.py:591
  158.9 7.3 %collective-permute-done.20.refs_3_ = bf16[512,1024]{1,0:T(8,128)(2,1)S(1)} collective-permute-done((bf16[512,1024]{1,0:T(8,128)(2,1)}, bf16[512,1024]{1,0:T(8,128)(2,1)S(1)}, u32[]{:S(2)}, u32[]{:S(2)}) %collective-permute-start.20) | collective-permute-done | bytes 1048608 | tf_op jit(solution)/shard_map/ppermute | solution.py:375
  166.2 1.4 collective-permute-start.26
  168.2 1.6 collective-permute-done.26.refs_4_
  169.8 1.5 collective-permute-done.27.refs_6_
  171.3 13.4 %attend.7 = (f32[4,2816,128]{2,1,0:T(8,128)S(1)}, f32[4,2816,128]{2,1,0:T(8,128)S(1)}, f32[4,2816,128]{2,1,0:T(8,128)S(1)}) custom-call(s32[512,1]{1,0:T(8,128)S(1)} %reshape.687.refs_0_, bf16[4,2816,128]{2,1,0:T(8,128)(2,1)S(1)} %get-tuple-element.72.refs_1_, ...), custom_call_target="tpu_custom_call", output_to_operand_aliasing={{0}: (7, {}), {1}: (8, {}), {2}: (9, {})} | custom-call | flops 5905580032 | bytes 33554432 | tf_op jit(solution)/shard_map/attend/pallas_call | solution.py:591
  184.7 8.8 %collective-permute-done.24.refs_3_ = bf16[512,1024]{1,0:T(8,128)(2,1)S(1)} collective-permute-done((bf16[512,1024]{1,0:T(8,128)(2,1)S(1)}, bf16[512,1024]{1,0:T(8,128)(2,1)S(1)}, u32[]{:S(2)}, u32[]{:S(2)}) %collective-permute-start.24) | collective-permute-done | bytes 1048608 | tf_op jit(solution)/shard_map/ppermute | solution.py:375
  193.5 1.4 collective-permute-start.30
  195.7 1.5 collective-permute-done.30.refs_4_
  197.2 1.5 collective-permute-done.31.refs_6_
  198.7 13.4 %attend.8 = (f32[4,2816,128]{2,1,0:T(8,128)S(1)}, f32[4,2816,128]{2,1,0:T(8,128)S(1)}, f32[4,2816,128]{2,1,0:T(8,128)S(1)}) custom-call(s32[512,1]{1,0:T(8,128)S(1)} %reshape.687.refs_0_, bf16[4,2816,128]{2,1,0:T(8,128)(2,1)S(1)} %get-tuple-element.72.refs_1_, ...), custom_call_target="tpu_custom_call", output_to_operand_aliasing={{0}: (7, {}), {1}: (8, {}), {2}: (9, {})} | custom-call | flops 5905580032 | bytes 33554432 | tf_op jit(solution)/shard_map/attend/pallas_call | solution.py:591
  212.1 2.5 %copy-done = f32[4,2816,128]{2,1,0:T(8,128)} copy-done((f32[4,2816,128]{2,1,0:T(8,128)}, f32[4,2816,128]{2,1,0:T(8,128)S(1)}, u32[]{:S(2)}) %copy-start) | copy-done | bytes 5767192
  214.6 2.4 copy-done.2
  217.1 2.4 copy-done.4
  220.2 1.6 collective-permute-done.32.refs_5_
  222.5 2.6 %copy-done.1 = f32[4,2816,128]{2,1,0:T(8,128)S(1)} copy-done((f32[4,2816,128]{2,1,0:T(8,128)S(1)}, f32[4,2816,128]{2,1,0:T(8,128)}, u32[]{:S(2)}) %copy-start.1) | copy-done | bytes 5767192
  225.2 2.6 %copy-done.3 = f32[4,2816,128]{2,1,0:T(8,128)S(1)} copy-done((f32[4,2816,128]{2,1,0:T(8,128)S(1)}, f32[4,2816,128]{2,1,0:T(8,128)}, u32[]{:S(2)}) %copy-start.3) | copy-done | bytes 5767192
  227.8 2.6 %copy-done.5 = f32[4,2816,128]{2,1,0:T(8,128)S(1)} copy-done((f32[4,2816,128]{2,1,0:T(8,128)S(1)}, f32[4,2816,128]{2,1,0:T(8,128)}, u32[]{:S(2)}) %copy-start.5) | copy-done | bytes 5767192
  230.4 1.0 copy-done.10
  231.5 17.3 %attend.9 = bf16[512,2560]{1,0:T(8,128)(2,1)} custom-call(s32[512,1]{1,0:T(8,128)S(1)} %reshape.687.refs_0_, bf16[4,2816,128]{2,1,0:T(8,128)(2,1)S(1)} %get-tuple-element.72.refs_1_, bf16[16,128,128]{2,1,0:T(8,128)(2,1)S(1)} %copy-done.10, bf16[256,1024]{1,0:T(8,128)(2,1)} %collective-permute-done.28.refs_3_, ...), custom_call_target="tpu_custom_call" | custom-call | flops 4429185024 | bytes 16777216 | tf_op jit(solution)/shard_map/attend/pallas_call | solution.py:591
  (125 shorter events, 24.1 us)
Async XLA Ops:
  3.4 18.9 %collective-permute-start = (bf16[320,1024]{1,0:T(8,128)(2,1)}, bf16[320,1024]{1,0:T(8,128)(2,1)}, u32[]{:S(2)}, u32[]{:S(2)}) collective-permute-start(bf16[320,1024]{1,0:T(8,128)(2,1)} %constant_dynamic-update-slice_fusion.refs_0_), channel_id=1, source_target_pairs={{0,4},{1,5},{2,6},{3,7},{4,8},{5,9},{6,10},{7,11},{8,12},{9,13},{1... | collective-permute-start | bytes 1966088 | tf_op jit(solution)/shard_map/ppermute | solution.py:375
  5.6 16.8 %collective-permute-start.1 = (bf16[320,1024]{1,0:T(8,128)(2,1)}, bf16[320,1024]{1,0:T(8,128)(2,1)}, u32[]{:S(2)}, u32[]{:S(2)}) collective-permute-start(bf16[320,1024]{1,0:T(8,128)(2,1)} %constant_dynamic-update-slice_fusion.refs_0_), channel_id=1, source_target_pairs={{0,2},{1,3},{2,0},{3,1},{4,6},{5,7},{6,4},{7,5},{8,10},{9,11},{10,... | collective-permute-start | bytes 1966088 | tf_op jit(solution)/shard_map/ppermute | solution.py:375
  22.4 34.4 %collective-permute-start.2 = (bf16[320,1024]{1,0:T(8,128)(2,1)}, bf16[320,1024]{1,0:T(8,128)(2,1)S(1)}, u32[]{:S(2)}, u32[]{:S(2)}) collective-permute-start(bf16[320,1024]{1,0:T(8,128)(2,1)} %collective-permute-done.refs_2_), channel_id=1, source_target_pairs={{0,4},{1,5},{2,6},{3,7},{4,8},{5,9},{6,10},{7,11},{8,12},{9,13},{1... | collective-permute-start | bytes 1966088 | tf_op jit(solution)/shard_map/ppermute | solution.py:375
  22.5 34.3 %collective-permute-start.3 = (bf16[320,1024]{1,0:T(8,128)(2,1)}, bf16[320,1024]{1,0:T(8,128)(2,1)}, u32[]{:S(2)}, u32[]{:S(2)}) collective-permute-start(bf16[320,1024]{1,0:T(8,128)(2,1)} %collective-permute-done.refs_2_), channel_id=1, source_target_pairs={{0,2},{1,3},{2,0},{3,1},{4,6},{5,7},{6,4},{7,5},{8,10},{9,11},{10,... | collective-permute-start | bytes 1966088 | tf_op jit(solution)/shard_map/ppermute | solution.py:375
  23.7 35.1 %collective-permute-start.6 = (bf16[320,1024]{1,0:T(8,128)(2,1)}, bf16[320,1024]{1,0:T(8,128)(2,1)}, u32[]{:S(2)}, u32[]{:S(2)}) collective-permute-start(bf16[320,1024]{1,0:T(8,128)(2,1)} %constant_dynamic-update-slice_fusion.refs_0_), channel_id=1, source_target_pairs={{0,1},{1,0},{2,3},{3,2},{4,5},{5,4},{6,7},{7,6},{8,9},{9,8},{10,11... | collective-permute-start | bytes 1966088 | tf_op jit(solution)/shard_map/ppermute | solution.py:371
  29.0 14.7 %all-to-all-start = ((s32[16,1,1600]{2,1,0:T(1,128)}), s32[16,1,1600]{2,1,0:T(1,128)S(1)}, u32[]{:S(2)}, u32[]{:S(2)}) async-start(s32[16,1,1600]{2,1,0:T(1,128)} %broadcast_in_dim.4), calls=%async_computation | async-start | bytes 212992 | tf_op jit(solution)/shard_map/all_to_all | solution.py:444
  33.2 26.3 %collective-permute-start.7 = (bf16[320,1024]{1,0:T(8,128)(2,1)}, bf16[320,1024]{1,0:T(8,128)(2,1)}, u32[]{:S(2)}, u32[]{:S(2)}) collective-permute-start(bf16[320,1024]{1,0:T(8,128)(2,1)} %collective-permute-done.refs_2_), channel_id=1, source_target_pairs={{0,1},{1,0},{2,3},{3,2},{4,5},{5,4},{6,7},{7,6},{8,9},{9,8},{10,11... | collective-permute-start | bytes 1966088 | tf_op jit(solution)/shard_map/ppermute | solution.py:371
  44.4 15.2 %collective-permute-start.8 = (bf16[320,1024]{1,0:T(8,128)(2,1)}, bf16[320,1024]{1,0:T(8,128)(2,1)}, u32[]{:S(2)}, u32[]{:S(2)}) collective-permute-start(bf16[320,1024]{1,0:T(8,128)(2,1)} %collective-permute-done.1.refs_4_), channel_id=1, source_target_pairs={{0,1},{1,0},{2,3},{3,2},{4,5},{5,4},{6,7},{7,6},{8,9},{9,8},{10,11... | collective-permute-start | bytes 1966088 | tf_op jit(solution)/shard_map/ppermute | solution.py:371
  57.6 18.2 %collective-permute-start.4 = (bf16[320,1024]{1,0:T(8,128)(2,1)}, bf16[320,1024]{1,0:T(8,128)(2,1)S(1)}, u32[]{:S(2)}, u32[]{:S(2)}) collective-permute-start(bf16[320,1024]{1,0:T(8,128)(2,1)} %copy-done.7), channel_id=1, source_target_pairs={{0,4},{1,5},{2,6},{3,7},{4,8},{5,9},{6,10},{7,11},{8,12},{9,13},{1... | collective-permute-start | bytes 1966088 | tf_op jit(solution)/shard_map/ppermute | solution.py:375
  58.2 17.6 %collective-permute-start.5 = (bf16[320,1024]{1,0:T(8,128)(2,1)}, bf16[320,1024]{1,0:T(8,128)(2,1)}, u32[]{:S(2)}, u32[]{:S(2)}) collective-permute-start(bf16[320,1024]{1,0:T(8,128)(2,1)} %copy-done.7), channel_id=1, source_target_pairs={{0,2},{1,3},{2,0},{3,1},{4,6},{5,7},{6,4},{7,5},{8,10},{9,11},{10,... | collective-permute-start | bytes 1966088 | tf_op jit(solution)/shard_map/ppermute | solution.py:375
  58.8 19.2 %collective-permute-start.11 = (bf16[320,1024]{1,0:T(8,128)(2,1)}, bf16[320,1024]{1,0:T(8,128)(2,1)}, u32[]{:S(2)}, u32[]{:S(2)}) collective-permute-start(bf16[320,1024]{1,0:T(8,128)(2,1)} %copy-done.7), channel_id=1, source_target_pairs={{0,1},{1,0},{2,3},{3,2},{4,5},{5,4},{6,7},{7,6},{8,9},{9,8},{10,11... | collective-permute-start | bytes 1966088 | tf_op jit(solution)/shard_map/ppermute | solution.py:371
  59.5 19.9 %collective-permute-start.12 = (bf16[320,1024]{1,0:T(8,128)(2,1)}, bf16[320,1024]{1,0:T(8,128)(2,1)S(1)}, u32[]{:S(2)}, u32[]{:S(2)}) collective-permute-start(bf16[320,1024]{1,0:T(8,128)(2,1)} %collective-permute-done.3.refs_2_), channel_id=1, source_target_pairs={{0,1},{1,0},{2,3},{3,2},{4,5},{5,4},{6,7},{7,6},{8,9},{9,8},{10,11... | collective-permute-start | bytes 1966088 | tf_op jit(solution)/shard_map/ppermute | solution.py:371
  59.7 2.5 copy-start.6
  62.2 16.6 %copy-start.22 = (bf16[512]{0:T(512)(128)(2,1)S(1)}, bf16[512]{0:T(512)(128)(2,1)}, u32[]{:S(2)}) copy-start(bf16[512]{0:T(512)(128)(2,1)} %param.14) | copy-start | bytes 3076
  62.2 16.6 %copy-start.23 = (bf16[512]{0:T(512)(128)(2,1)S(1)}, bf16[512]{0:T(512)(128)(2,1)}, u32[]{:S(2)}) copy-start(bf16[512]{0:T(512)(128)(2,1)} %param.15) | copy-start | bytes 3076
  62.2 17.3 %copy-start.8 = (bf16[320,1024]{1,0:T(8,128)(2,1)S(1)}, bf16[320,1024]{1,0:T(8,128)(2,1)}, u32[]{:S(2)}) copy-start(bf16[320,1024]{1,0:T(8,128)(2,1)} %copy-done.7) | copy-start | bytes 1966084
  75.8 14.9 %collective-permute-start.15 = (bf16[320,1024]{1,0:T(8,128)(2,1)S(1)}, bf16[320,1024]{1,0:T(8,128)(2,1)S(1)}, u32[]{:S(2)}, u32[]{:S(2)}) collective-permute-start(bf16[320,1024]{1,0:T(8,128)(2,1)S(1)} %collective-permute-done.4.refs_0_), channel_id=1, source_target_pairs={{0,1},{1,0},{2,3},{3,2},{4,5},{5,4},{6,7},{7,6},{8,9},{9,8},{10,11... | collective-permute-start | bytes 1966088 | tf_op jit(solution)/shard_map/ppermute | solution.py:371
  76.8 13.9 %collective-permute-start.16 = (bf16[320,1024]{1,0:T(8,128)(2,1)}, bf16[320,1024]{1,0:T(8,128)(2,1)S(1)}, u32[]{:S(2)}, u32[]{:S(2)}) collective-permute-start(bf16[320,1024]{1,0:T(8,128)(2,1)} %collective-permute-done.5.refs_2_), channel_id=1, source_target_pairs={{0,1},{1,0},{2,3},{3,2},{4,5},{5,4},{6,7},{7,6},{8,9},{9,8},{10,11... | collective-permute-start | bytes 1966088 | tf_op jit(solution)/shard_map/ppermute | solution.py:371
  77.8 10.8 %collective-permute-start.10 = (bf16[160,1024]{1,0:T(8,128)(2,1)S(1)}, bf16[160,1024]{1,0:T(8,128)(2,1)S(1)}, u32[]{:S(2)}, u32[]{:S(2)}) collective-permute-start(bf16[160,1024]{1,0:T(8,128)(2,1)S(1)} %slice.97), channel_id=1, source_target_pairs={{0,4},{1,5},{2,6},{3,7},{4,8},{5,9},{6,10},{7,11},{8,12},{9,13},{1... | collective-permute-start | bytes 983048 | tf_op jit(solution)/shard_map/ppermute | solution.py:383
  78.0 10.5 %collective-permute-start.9 = (bf16[160,1024]{1,0:T(8,128)(2,1)S(1)}, bf16[160,1024]{1,0:T(8,128)(2,1)S(1)}, u32[]{:S(2)}, u32[]{:S(2)}) collective-permute-start(bf16[160,1024]{1,0:T(8,128)(2,1)S(1)} %slice.96), channel_id=1, source_target_pairs={{0,2},{1,3},{2,0},{3,1},{4,6},{5,7},{6,4},{7,5},{8,10},{9,11},{10,... | collective-permute-start | bytes 983048 | tf_op jit(solution)/shard_map/ppermute | solution.py:382
  88.6 6.2 %collective-permute-start.13 = (bf16[160,1024]{1,0:T(8,128)(2,1)S(1)}, bf16[160,1024]{1,0:T(8,128)(2,1)S(1)}, u32[]{:S(2)}, u32[]{:S(2)}) collective-permute-start(bf16[160,1024]{1,0:T(8,128)(2,1)S(1)} %collective-permute-done.9.refs_0_), channel_id=1, source_target_pairs={{0,1},{1,0},{2,3},{3,2},{4,5},{5,4},{6,7},{7,6},{8,9},{9,8},{10,11... | collective-permute-start | bytes 983048 | tf_op jit(solution)/shard_map/ppermute | solution.py:371
  90.0 4.8 %collective-permute-start.14 = (bf16[160,1024]{1,0:T(8,128)(2,1)S(1)}, bf16[160,1024]{1,0:T(8,128)(2,1)S(1)}, u32[]{:S(2)}, u32[]{:S(2)}) collective-permute-start(bf16[160,1024]{1,0:T(8,128)(2,1)S(1)} %collective-permute-done.10.refs_1_), channel_id=1, source_target_pairs={{0,1},{1,0},{2,3},{3,2},{4,5},{5,4},{6,7},{7,6},{8,9},{9,8},{10,11... | collective-permute-start | bytes 983048 | tf_op jit(solution)/shard_map/ppermute | solution.py:371
  90.0 4.8 %slice-start = ((s8[5242880]{0:T(1024)(128)(4,1)}), s8[4194304]{0:T(1024)(128)(4,1)S(1)}, s32[]{:S(2)}) async-start(s8[5242880]{0:T(1024)(128)(4,1)} %bitcast.30), calls=%async_computation.1 | async-start | bytes 8388608
  90.7 4.1 %slice-start.1 = ((s8[5242880]{0:T(1024)(128)(4,1)}), s8[1048576]{0:T(1024)(128)(4,1)S(1)}, s32[]{:S(2)}) async-start(s8[5242880]{0:T(1024)(128)(4,1)} %bitcast.30), calls=%async_computation.2 | async-start | bytes 2097152
  90.7 4.2 %copy-start.12 = (f32[512,128]{1,0:T(8,128)S(1)}, f32[512,128]{1,0:T(8,128)}, u32[]{:S(2)}) copy-start(f32[512,128]{1,0:T(8,128)} %copy-done.11) | copy-start | bytes 786436
  90.7 4.2 %copy-start.14 = (f32[512,128]{1,0:T(8,128)S(1)}, f32[512,128]{1,0:T(8,128)}, u32[]{:S(2)}) copy-start(f32[512,128]{1,0:T(8,128)} %copy-done.13) | copy-start | bytes 786436
  100.3 20.0 %collective-permute-start.19 = (bf16[512,1024]{1,0:T(8,128)(2,1)}, bf16[512,1024]{1,0:T(8,128)(2,1)}, u32[]{:S(2)}, u32[]{:S(2)}) collective-permute-start(bf16[512,1024]{1,0:T(8,128)(2,1)} %finish.1.refs_3_), channel_id=1, source_target_pairs={{0,1},{1,0},{2,3},{3,2},{4,5},{5,4},{6,7},{7,6},{8,9},{9,8},{10,11... | collective-permute-start | bytes 3145736 | tf_op jit(solution)/shard_map/ppermute | solution.py:371
  112.2 26.9 %collective-permute-start.17 = (bf16[512,1024]{1,0:T(8,128)(2,1)}, bf16[512,1024]{1,0:T(8,128)(2,1)}, u32[]{:S(2)}, u32[]{:S(2)}) collective-permute-start(bf16[512,1024]{1,0:T(8,128)(2,1)} %finish.1.refs_3_), channel_id=1, source_target_pairs={{0,4},{1,5},{2,6},{3,7},{4,8},{5,9},{6,10},{7,11},{8,12},{9,13},{1... | collective-permute-start | bytes 3145736 | tf_op jit(solution)/shard_map/ppermute | solution.py:375
  112.3 26.9 %collective-permute-start.18 = (bf16[512,1024]{1,0:T(8,128)(2,1)}, bf16[512,1024]{1,0:T(8,128)(2,1)}, u32[]{:S(2)}, u32[]{:S(2)}) collective-permute-start(bf16[512,1024]{1,0:T(8,128)(2,1)} %finish.1.refs_3_), channel_id=1, source_target_pairs={{0,2},{1,3},{2,0},{3,1},{4,6},{5,7},{6,4},{7,5},{8,10},{9,11},{10,... | collective-permute-start | bytes 3145736 | tf_op jit(solution)/shard_map/ppermute | solution.py:375
  139.1 3.3 %collective-permute-start.22 = (bf16[512,1024]{1,0:T(8,128)(2,1)}, bf16[512,1024]{1,0:T(8,128)(2,1)S(1)}, u32[]{:S(2)}, u32[]{:S(2)}) collective-permute-start(bf16[512,1024]{1,0:T(8,128)(2,1)} %collective-permute-done.17.refs_3_), channel_id=1, source_target_pairs={{0,1},{1,0},{2,3},{3,2},{4,5},{5,4},{6,7},{7,6},{8,9},{9,8},{10,11... | collective-permute-start | bytes 3145736 | tf_op jit(solution)/shard_map/ppermute | solution.py:371
  139.9 4.0 %collective-permute-start.23 = (bf16[512,1024]{1,0:T(8,128)(2,1)}, bf16[512,1024]{1,0:T(8,128)(2,1)S(1)}, u32[]{:S(2)}, u32[]{:S(2)}) collective-permute-start(bf16[512,1024]{1,0:T(8,128)(2,1)} %collective-permute-done.18.refs_5_), channel_id=1, source_target_pairs={{0,1},{1,0},{2,3},{3,2},{4,5},{5,4},{6,7},{7,6},{8,9},{9,8},{10,11... | collective-permute-start | bytes 3145736 | tf_op jit(solution)/shard_map/ppermute | solution.py:371
  139.9 26.2 %collective-permute-start.20 = (bf16[512,1024]{1,0:T(8,128)(2,1)}, bf16[512,1024]{1,0:T(8,128)(2,1)S(1)}, u32[]{:S(2)}, u32[]{:S(2)}) collective-permute-start(bf16[512,1024]{1,0:T(8,128)(2,1)} %collective-permute-done.17.refs_3_), channel_id=1, source_target_pairs={{0,4},{1,5},{2,6},{3,7},{4,8},{5,9},{6,10},{7,11},{8,12},{9,13},{1... | collective-permute-start | bytes 3145736 | tf_op jit(solution)/shard_map/ppermute | solution.py:375
  139.9 26.2 %collective-permute-start.21 = (bf16[512,1024]{1,0:T(8,128)(2,1)}, bf16[512,1024]{1,0:T(8,128)(2,1)S(1)}, u32[]{:S(2)}, u32[]{:S(2)}) collective-permute-start(bf16[512,1024]{1,0:T(8,128)(2,1)} %collective-permute-done.17.refs_3_), channel_id=1, source_target_pairs={{0,2},{1,3},{2,0},{3,1},{4,6},{5,7},{6,4},{7,5},{8,10},{9,11},{10,... | collective-permute-start | bytes 3145736 | tf_op jit(solution)/shard_map/ppermute | solution.py:375
  166.2 3.6 %collective-permute-start.26 = (bf16[512,1024]{1,0:T(8,128)(2,1)S(1)}, bf16[512,1024]{1,0:T(8,128)(2,1)S(1)}, u32[]{:S(2)}, u32[]{:S(2)}) collective-permute-start(bf16[512,1024]{1,0:T(8,128)(2,1)S(1)} %collective-permute-done.20.refs_3_), channel_id=1, source_target_pairs={{0,1},{1,0},{2,3},{3,2},{4,5},{5,4},{6,7},{7,6},{8,9},{9,8},{10,11... | collective-permute-start | bytes 3145736 | tf_op jit(solution)/shard_map/ppermute | solution.py:371
  167.5 3.8 %collective-permute-start.27 = (bf16[512,1024]{1,0:T(8,128)(2,1)S(1)}, bf16[512,1024]{1,0:T(8,128)(2,1)S(1)}, u32[]{:S(2)}, u32[]{:S(2)}) collective-permute-start(bf16[512,1024]{1,0:T(8,128)(2,1)S(1)} %collective-permute-done.21.refs_5_), channel_id=1, source_target_pairs={{0,1},{1,0},{2,3},{3,2},{4,5},{5,4},{6,7},{7,6},{8,9},{9,8},{10,11... | collective-permute-start | bytes 3145736 | tf_op jit(solution)/shard_map/ppermute | solution.py:371
  167.5 26.0 %collective-permute-start.24 = (bf16[512,1024]{1,0:T(8,128)(2,1)S(1)}, bf16[512,1024]{1,0:T(8,128)(2,1)S(1)}, u32[]{:S(2)}, u32[]{:S(2)}) collective-permute-start(bf16[512,1024]{1,0:T(8,128)(2,1)S(1)} %collective-permute-done.20.refs_3_), channel_id=1, source_target_pairs={{0,4},{1,5},{2,6},{3,7},{4,8},{5,9},{6,10},{7,11},{8,12},{9,13},{1... | collective-permute-start | bytes 3145736 | tf_op jit(solution)/shard_map/ppermute | solution.py:375
  167.5 26.0 %collective-permute-start.25 = (bf16[512,1024]{1,0:T(8,128)(2,1)S(1)}, bf16[512,1024]{1,0:T(8,128)(2,1)S(1)}, u32[]{:S(2)}, u32[]{:S(2)}) collective-permute-start(bf16[512,1024]{1,0:T(8,128)(2,1)S(1)} %collective-permute-done.20.refs_3_), channel_id=1, source_target_pairs={{0,2},{1,3},{2,0},{3,1},{4,6},{5,7},{6,4},{7,5},{8,10},{9,11},{10,... | collective-permute-start | bytes 3145736 | tf_op jit(solution)/shard_map/ppermute | solution.py:375
  193.5 3.6 %collective-permute-start.30 = (bf16[512,1024]{1,0:T(8,128)(2,1)S(1)}, bf16[512,1024]{1,0:T(8,128)(2,1)S(1)}, u32[]{:S(2)}, u32[]{:S(2)}) collective-permute-start(bf16[512,1024]{1,0:T(8,128)(2,1)S(1)} %collective-permute-done.24.refs_3_), channel_id=1, source_target_pairs={{0,1},{1,0},{2,3},{3,2},{4,5},{5,4},{6,7},{7,6},{8,9},{9,8},{10,11... | collective-permute-start | bytes 3145736 | tf_op jit(solution)/shard_map/ppermute | solution.py:371
  194.9 3.8 %collective-permute-start.31 = (bf16[512,1024]{1,0:T(8,128)(2,1)S(1)}, bf16[512,1024]{1,0:T(8,128)(2,1)S(1)}, u32[]{:S(2)}, u32[]{:S(2)}) collective-permute-start(bf16[512,1024]{1,0:T(8,128)(2,1)S(1)} %collective-permute-done.25.refs_5_), channel_id=1, source_target_pairs={{0,1},{1,0},{2,3},{3,2},{4,5},{5,4},{6,7},{7,6},{8,9},{9,8},{10,11... | collective-permute-start | bytes 3145736 | tf_op jit(solution)/shard_map/ppermute | solution.py:371
  195.0 24.5 %collective-permute-start.28 = (bf16[256,1024]{1,0:T(8,128)(2,1)S(1)}, bf16[256,1024]{1,0:T(8,128)(2,1)}, u32[]{:S(2)}, u32[]{:S(2)}) collective-permute-start(bf16[256,1024]{1,0:T(8,128)(2,1)S(1)} %slice.98), channel_id=1, source_target_pairs={{0,2},{1,3},{2,0},{3,1},{4,6},{5,7},{6,4},{7,5},{8,10},{9,11},{10,... | collective-permute-start | bytes 1572872 | tf_op jit(solution)/shard_map/ppermute | solution.py:382
  195.7 23.8 %collective-permute-start.29 = (bf16[256,1024]{1,0:T(8,128)(2,1)S(1)}, bf16[256,1024]{1,0:T(8,128)(2,1)}, u32[]{:S(2)}, u32[]{:S(2)}) collective-permute-start(bf16[256,1024]{1,0:T(8,128)(2,1)S(1)} %slice.99), channel_id=1, source_target_pairs={{0,4},{1,5},{2,6},{3,7},{4,8},{5,9},{6,10},{7,11},{8,12},{9,13},{1... | collective-permute-start | bytes 1572872 | tf_op jit(solution)/shard_map/ppermute | solution.py:383
  212.1 2.5 %copy-start = (f32[4,2816,128]{2,1,0:T(8,128)}, f32[4,2816,128]{2,1,0:T(8,128)S(1)}, u32[]{:S(2)}) copy-start(f32[4,2816,128]{2,1,0:T(8,128)S(1)} %get-tuple-element.120.refs_7_) | copy-start | bytes 17301508
  214.6 2.4 copy-start.2
  219.5 2.3 collective-permute-start.32
  219.9 2.6 %collective-permute-start.33 = (bf16[256,1024]{1,0:T(8,128)(2,1)}, bf16[256,1024]{1,0:T(8,128)(2,1)}, u32[]{:S(2)}, u32[]{:S(2)}) collective-permute-start(bf16[256,1024]{1,0:T(8,128)(2,1)} %collective-permute-done.29.refs_4_), channel_id=1, source_target_pairs={{0,1},{1,0},{2,3},{3,2},{4,5},{5,4},{6,7},{7,6},{8,9},{9,8},{10,11... | collective-permute-start | bytes 1572872 | tf_op jit(solution)/shard_map/ppermute | solution.py:371
  222.5 2.6 %copy-start.1 = (f32[4,2816,128]{2,1,0:T(8,128)S(1)}, f32[4,2816,128]{2,1,0:T(8,128)}, u32[]{:S(2)}) copy-start(f32[4,2816,128]{2,1,0:T(8,128)} %copy-done) | copy-start | bytes 17301508
  225.2 2.6 %copy-start.3 = (f32[4,2816,128]{2,1,0:T(8,128)S(1)}, f32[4,2816,128]{2,1,0:T(8,128)}, u32[]{:S(2)}) copy-start(f32[4,2816,128]{2,1,0:T(8,128)} %copy-done.2) | copy-start | bytes 17301508
  227.8 2.6 %copy-start.5 = (f32[4,2816,128]{2,1,0:T(8,128)S(1)}, f32[4,2816,128]{2,1,0:T(8,128)}, u32[]{:S(2)}) copy-start(f32[4,2816,128]{2,1,0:T(8,128)} %copy-done.4) | copy-start | bytes 17301508
  (13 other events, 13.6 us)

commit v8 on v7

--- a/solution.py
+++ b/solution.py
@@ -3,6 +3,7 @@
 
 import jax
 import jax.numpy as jnp
+import numpy as np
 from jax import lax
 from jax.experimental import pallas as pl
 from jax.experimental.pallas import tpu as pltpu
@@ -16,7 +17,7 @@
 CHUNKS = ((0, KEY_VALUE_HEADS),)
 PLANE = 4
 PLANES = 4
-UNROLL = 2
+UNROLL = 4
 GATHER_LIMIT = 40 * 2**20
 MASKED = -1e30
 VMEM = pl.BlockSpec(memory_space=pltpu.VMEM)
@@ -50,6 +51,18 @@
 
 def turn(rows, cosine, sine):
     return (rows * cosine + pltpu.roll(rows, HEAD_SIZE // 2, 1) * sine).astype(jnp.bfloat16)
+
+
+def join_kernel(left_ref, right_ref, out_ref, done):
+    wide = left_ref.shape[1]
+    copies = [
+        pltpu.make_async_copy(ref, out_ref.at[:, pl.ds(at * wide, wide)], done.at[at])
+        for at, ref in enumerate((left_ref, right_ref))
+    ]
+    for copy in copies:
+        copy.start()
+    for copy in copies:
+        copy.wait()
 
 
 def order_kernel(
@@ -253,13 +266,13 @@
         blocks.append(dict(zip(first_rows, refs)))
         refs = refs[len(first_rows) :]
     if more:
-        top_ref, sum_ref, total_ref = refs[:3]
-        refs = refs[3:]
+        stats_ref, total_ref = refs[:2]
+        refs = refs[2:]
     if last:
         seat_ref, out_ref, listed_rows, seen_by, mixed_ref, result_ref, done = refs
         mixed_ref[...] = jnp.zeros(mixed_ref.shape, jnp.bfloat16)
     else:
-        new_top_ref, new_sum_ref, new_total_ref, listed_rows, seen_by = refs
+        new_stats_ref, new_total_ref, listed_rows, seen_by = refs
     heads, ranks = queries_ref.shape[0], veil_ref.shape[0]
     packed = queries_ref.shape[1] // ranks
     wide = heads * HEAD_SIZE
@@ -299,25 +312,29 @@
             keys = rows_of(group, row, head * HEAD_SIZE)
             right = jnp.concatenate([keys, veil_ref[group]], axis=1)
             scores.append(contract(left, right, 1, 1))
-        tops, weights = [], []
+        tops, weights, fades, sums = [], [], [], []
         for head, score in zip(some, scores):
             top = jnp.max(score, axis=1, keepdims=True)
             if more:
-                top = jnp.maximum(top_ref[head, tokens], top)
+                stats = stats_ref[head, tokens]
+                other = pltpu.roll(stats, HEAD_SIZE // 2, 1)
+                old_top = jnp.where(lane < HEAD_SIZE // 2, stats, other)
+                sums.append(jnp.where(lane < HEAD_SIZE // 2, other, stats))
+                top = jnp.maximum(old_top, top)
+                fades.append(jnp.exp2((old_top - top) * scale))
             else:
                 top = jnp.broadcast_to(top, (packed, HEAD_SIZE))
             tops.append(top)
             tiled = jnp.concatenate([top] * (score.shape[1] // HEAD_SIZE), axis=1)
             weights.append(jnp.exp2((score - tiled) * scale).astype(jnp.bfloat16))
-        for head, top, weight in zip(some, tops, weights):
+        for at_head, (head, top, weight) in enumerate(zip(some, tops, weights)):
             values = rows_of(group, row, wide + head * HEAD_SIZE)
             values = jnp.concatenate([values, jnp.ones_like(values)], axis=1)
             mixed = contract(weight, values, 1, 0)
             total, weight_sum = mixed[:, :HEAD_SIZE], mixed[:, HEAD_SIZE:]
             if more:
-                fade = jnp.exp2((top_ref[head, tokens] - top) * scale)
-                total = total + fade * total_ref[head, tokens]
-                weight_sum = weight_sum + fade * sum_ref[head, tokens]
+                total = total + fades[at_head] * total_ref[head, tokens]
+                weight_sum = weight_sum + fades[at_head] * sums[at_head]
             if last:
                 mixed = total / weight_sum
                 seats = pl.ds(pl.multiple_of(group * stride, 16), spare)
@@ -326,8 +343,7 @@
                     rows = mixed[at * spare : (at + 1) * spare]
                     mixed_ref[seats, place : place + HEAD_SIZE] = rows.astype(jnp.bfloat16)
             else:
-                new_top_ref[head, tokens] = top
-                new_sum_ref[head, tokens] = weight_sum
+                new_stats_ref[head, tokens] = jnp.where(lane < HEAD_SIZE // 2, top, weight_sum)
                 new_total_ref[head, tokens] = total
 
     rows = sorted({row for first_rows in starts for row in first_rows})
@@ -390,12 +406,13 @@
     yield extra
 
 
-def source_order(ranks):
+def source_order(ranks, sources):
     me = lax.axis_index("dp")
-    lane, plane = me % PLANE, me // PLANE
-    steps = ranks // PLANE
-    planes = (plane - jnp.arange(steps, dtype=jnp.int32)) % steps
-    return jnp.concatenate([planes * PLANE + (lane ^ flip) for flip in (0, 2, 1, 3)])
+    lane, plane = lax.rem(me, PLANE), lax.div(me, PLANE)
+    planes = ranks // PLANE
+    steps = np.array([source % planes for source in sources], np.int32)
+    flips = np.array([(0, 2, 1, 3)[source // planes] for source in sources], np.int32)
+    return lax.rem(plane + (planes - steps), planes) * PLANE + (lane ^ flips)
 
 
 def gather_plan(
@@ -424,7 +441,16 @@
         return array[..., first * HEAD_SIZE : (first + heads) * HEAD_SIZE]
 
     matrices = {}
-    sending = spread(jnp.concatenate([key_matrix, value_matrix], axis=1), ranks, matrices)
+    joined = pl.pallas_call(
+        join_kernel,
+        out_shape=shape((key_matrix.shape[0], 2 * key_matrix.shape[1]), jnp.bfloat16),
+        in_specs=[HBM] * 2,
+        out_specs=VMEM,
+        scratch_shapes=[pltpu.SemaphoreType.DMA((2,))],
+        compiler_params=grant(14),
+        name="join",
+    )(key_matrix, value_matrix)
+    sending = spread(joined, ranks, matrices)
     next(sending)
     bucket, seat, sorted_route, more = pl.pallas_call(
         functools.partial(order_kernel, ranks, slots, extra, stride),
@@ -436,7 +462,7 @@
         ),
         in_specs=[VMEM],
         out_specs=(VMEM,) * 4,
-        compiler_params=grant(16),
+        compiler_params=grant(14),
         name="order",
     )(route.reshape(1, rows))
     width = rows + 2 * listed
@@ -444,16 +470,16 @@
     plan = lax.all_to_all(
         jnp.broadcast_to(plan, (ranks, width + slots)), "dp", split_axis=0, concat_axis=0, tiled=True
     )
-    sending.send(())
+    plan, bucket, seat = sending.send((plan, bucket, seat))
     next(sending)
     all_positions = plan[:, width:].reshape(-1, HEAD_SIZE)
-    owners = source_order(ranks)
     planes = ranks // PLANE
     sets = [(0, 2 * planes)] + [
         (step, step + 2 * planes, step + planes - 1, step + 3 * planes - 1)
         for step in range(1, planes)
     ]
     sets.append((2 * planes - 1, 4 * planes - 1))
+    owners = source_order(ranks, range(ranks))
 
     half = HEAD_SIZE // 2
     frequency = 1000000.0 ** (-(jnp.arange(half, dtype=jnp.float32) * 2.0 / HEAD_SIZE))
@@ -468,7 +494,7 @@
         in_specs=[VMEM] * 5,
         out_specs=(VMEM,) * 4,
         scratch_shapes=[pltpu.VMEM((ranks * packed, HEAD_SIZE), jnp.float32)],
-        compiler_params=grant(20),
+        compiler_params=grant(14),
         cost_estimate=cost(4 * stride * ranks * rows * query_width, 4 * rows * query_width),
         name="turn_queries",
     )(
@@ -512,7 +538,7 @@
             in_specs=[SMEM] + [HBM] * (1 + len(arrays)) + [VMEM] * len(more),
             out_specs=VMEM,
             scratch_shapes=scratch(chips, arrays),
-            compiler_params=grant(16),
+            compiler_params=grant(14),
             cost_estimate=product_cost(chips),
             name="add_part",
         )(owners, hidden, *arrays, *more)
@@ -521,8 +547,8 @@
     next(sending)
     (total,) = sending.send((add_part(None, (0, 1, planes)),))
     next(sending)
-    (total,) = sending.send((add_part(total, (2, planes + 1)),))
-    total = add_part(total, (3, planes + 2))
+    total = add_part(total, (2, planes + 1))
+    (total,) = sending.send((add_part(total, (3, planes + 2)),))
     chips, arrays = chip_parts((planes + 3,))
     bias = jnp.concatenate([key_projection_bias, value_projection_bias])
     (pairs,) = pl.pallas_call(
@@ -533,7 +559,7 @@
         in_specs=[SMEM, HBM] + [VMEM] * 4 + [HBM] * len(arrays) + [VMEM],
         out_specs=(VMEM,) * len(CHUNKS),
         scratch_shapes=scratch(chips, arrays),
-        compiler_params=grant(16),
+        compiler_params=grant(14),
         cost_estimate=product_cost(chips),
         name="finish",
     )(
@@ -551,7 +577,7 @@
     sending = spread(pairs, ranks, blocks)
     next(sending)
     order = [source for sources in sets for source in sources]
-    ordered = plan[:, :width][jnp.stack([owners[source] for source in order])]
+    ordered = plan[:, :width][source_order(ranks, order)]
     key_routes = ordered[:, :rows].reshape(ranks, ranks, share).transpose(1, 0, 2)
     more_places = ordered[:, rows + listed :].reshape(ranks * listed, 1)
     veils = pl.pallas_call(
@@ -561,7 +587,7 @@
         ),
         in_specs=[VMEM] * 3,
         out_specs=(VMEM,) * len(sets),
-        compiler_params=grant(16),
+        compiler_params=grant(14),
         cost_estimate=cost(3 * 10**9, 4 * ranks * rows * HEAD_SIZE),
         name="veil",
     )(
@@ -598,14 +624,14 @@
                 bool(state),
                 last,
             ),
-            out_shape=shape((rows, query_width), jnp.bfloat16) if last else (kept,) * 3,
+            out_shape=shape((rows, query_width), jnp.bfloat16) if last else (kept,) * 2,
             in_specs=[VMEM] * len(fixed),
-            out_specs=HBM if last else (VMEM,) * 3,
+            out_specs=HBM if last else (VMEM,) * 2,
             scratch_shapes=scratch_shapes,
             input_output_aliases={}
             if last or not state
-            else {len(fixed) - 3 + at: at for at in range(3)},
-            compiler_params=grant(20),
+            else {len(fixed) - 2 + at: at for at in range(2)},
+            compiler_params=grant(14),
             cost_estimate=cost(
                 8 * ranks * KEY_VALUE_HEADS * packed * (keys + 256) * HEAD_SIZE,
                 2 * keys * rows * HEAD_SIZE,

time: 250 us -> 227 us (0.908)
  waiting for transfers between devices: 71.9 us -> 31.6 us
  Pallas kernels: 102 us -> 122 us
  local copies, waits for them, and re-layouts: 50.2 us -> 33.1 us
  blocking collectives: 0 us -> 16.7 us
  starting transfers between devices: 24.5 us -> 21 us
    ppermute x6, waiting for transfers between devices: 45.5 us -> 19.7 us  [spread(): lax.ppermute(lane, 'dp', ring)]
    pallas_call x5, Pallas kernels: 72.2 us -> 92.8 us  [attend(): pl.pallas_call(functools.partial(attend_kernel, starts, sum((len(one) for...]
    all_to_all x0 -> x1, blocking collectives: none -> 16.7 us  [gather_plan(): lax.all_to_all(jnp.broadcast_to(plan, (ranks, width + slots)), 'dp', spli...]
    another operation x1 -> x0, local copies, waits for them, and re-layouts: 10 us -> none  [gather_plan(): ordered = plan[:, :width][jnp.stack([owners[source] for source in order])]]
    all_to_all x1 -> x0, waiting for transfers between devices: 9.37 us -> none  [gather_plan(): lax.all_to_all(jnp.broadcast_to(plan, (ranks, width + slots)), 'dp', spli...]
    ppermute x2, waiting for transfers between devices: 5.17 us -> 0.01 us  [spread(): around = lax.ppermute(other[half:], 'dp', ring)]
    all_to_all x1 -> x0, starting transfers between devices: 4.22 us -> none  [gather_plan(): lax.all_to_all(jnp.broadcast_to(plan, (ranks, width + slots)), 'dp', spli...]
    unnamed x54 -> x57, local copies, waits for them, and re-layouts: 29.5 us -> 26.4 us
  transfers between devices with their start and end apart: 35 -> 34, of which waited for: 15 -> 15; matrix products, arithmetic and copies ran while one was open for 8% -> 3% of each run, Pallas kernels for 32% -> 42%
where the time goes in v8:
time: 227 us; the launch traced here: 226 us
  Pallas kernels  122 us (54%)
  local copies, waits for them, and re-layouts  33.1 us (15%)
  waiting for transfers between devices  31.6 us (14%)
  starting transfers between devices  21 us (9%)
  blocking collectives  16.7 us (7%)
    pallas_call x5, Pallas kernels, attend(): pl.pallas_call(functools.partial(attend_kernel, starts, sum((len(one) for...  92.8 us
    unnamed x57, local copies, waits for them, and re-layouts  26.4 us
    ppermute x6, waiting for transfers between devices, spread(): lax.ppermute(lane, 'dp', ring)  19.7 us
    all_to_all x1, blocking collectives, gather_plan(): lax.all_to_all(jnp.broadcast_to(plan, (ranks, width + slots)), 'dp', spli...  16.7 us
    pallas_call x3, Pallas kernels, add_part(): pl.pallas_call(functools.partial(part_kernel, chips, bool(more)), out_sha...  13.5 us
    ppermute x18, waiting for transfers between devices, keep(): lax.ppermute(array, 'dp', beside)  11.8 us
    ppermute x18, starting transfers between devices, keep(): lax.ppermute(array, 'dp', beside)  10.5 us
    pallas_call x1, Pallas kernels, gather_plan(): pl.pallas_call(functools.partial(query_kernel, ranks, spare, stride, pack...  6.43 us
  transfers between devices with their start and end apart: 34, of which 15 were waited for; matrix products, arithmetic and copies ran while one was open for 3% of the time, Pallas kernels for 42%

profile of v8, /device:TPU:1, one launch (start us, length us, event | category | flops | bytes accessed | tf_op | source)
XLA Modules:
  0.0 225.9 jit_solution(17848072542486684212)
XLA Ops:
  0.0 1.0 copy-done.8
  1.0 1.0 copy-done.9
  2.0 2.2 collective-permute-start
  4.2 1.2 collective-permute-start.1
  7.7 16.7 %all_to_all.9 = s32[16,1,1600]{2,1,0:T(1,128)S(1)} all-to-all(s32[16,1,1600]{2,1,0:T(1,128)S(1)} %broadcast_in_dim.6), channel_id=1, replica_groups=mesh['groups'=2,'dp'=16] {'dp'}, dimensions={0} | all-to-all | bytes 204800 | tf_op jit(solution)/shard_map/all_to_all | solution.py:470
  25.4 1.0 collective-permute-start.6
  28.6 0.9 copy-done.14
  30.4 1.7 copy-done.17
  32.1 6.4 %turn_queries.1 = (bf16[4,2816,128]{2,1,0:T(8,128)(2,1)S(1)}, s32[768,128]{1,0:T(8,128)S(1)}, f32[512,128]{1,0:T(8,128)S(1)}, f32[512,128]{1,0:T(8,128)S(1)}) custom-call(s32[512,1]{1,0:T(8,128)S(1)} %copy-done.14, s32[1,512]{1,0:T(1,128)S(1)} %get-tuple-element.65.seat_ref, s32[128,128]{1,0:T(8,128)S(1)} %copy-done.15, ...), custom_call_target="tpu_custom_call" | custom-call | flops 4026531840 | bytes 5242880 | tf_op jit(solution)/shard_map/turn_queries/pallas_call | solution.py:486
  40.7 1.8 collective-permute-done.2.refs_0_
  42.9 1.5 collective-permute-start.13
  45.2 2.5 %copy-done = bf16[512,5120]{1,0:T(8,128)(2,1)S(1)} copy-done((bf16[512,5120]{1,0:T(8,128)(2,1)S(1)}, bf16[512,5120]{1,0:T(8,128)(2,1)}, u32[]{:S(2)}) %copy-start) | copy-done | bytes 5242904
  47.6 5.4 %add_part.3.refs_4_ = f32[512,1024]{1,0:T(8,128)S(1)} custom-call(s32[16]{0:T(128)S(1)} %fusion.5.owners_ref, bf16[512,5120]{1,0:T(8,128)(2,1)S(1)} %copy-done, bf16[320,1024]{1,0:T(8,128)(2,1)S(1)} %join.1.refs_0_, bf16[320,1024]{1,0:T(8,128)(2,1)} %collective-permute-done.6.refs_1_, bf16[320,1024]{1,0:T(8,128)(2,1)} %collective-permute-done.refs_2_, ...), custom_call_target="tpu_custom_call" | custom-call | flops 2013265920 | bytes 10092544 | tf_op jit(solution)/shard_map/add_part/pallas_call | solution.py:535
  53.1 6.5 %collective-permute-done.4.refs_0_ = bf16[320,1024]{1,0:T(8,128)(2,1)} collective-permute-done((bf16[320,1024]{1,0:T(8,128)(2,1)}, bf16[320,1024]{1,0:T(8,128)(2,1)}, u32[]{:S(2)}, u32[]{:S(2)}) %collective-permute-start.4) | collective-permute-done | bytes 655392 | tf_op jit(solution)/shard_map/ppermute | solution.py:391
  59.6 2.2 collective-permute-start.11
  61.7 1.0 slice.33
  62.7 1.0 slice.32
  64.5 2.5 %copy-done.1 = bf16[512,5120]{1,0:T(8,128)(2,1)S(1)} copy-done((bf16[512,5120]{1,0:T(8,128)(2,1)S(1)}, bf16[512,5120]{1,0:T(8,128)(2,1)}, u32[]{:S(2)}) %copy-start.1) | copy-done | bytes 5242904
  67.0 4.1 %add_part.4.refs_4_ = f32[512,1024]{1,0:T(8,128)S(1)} custom-call(s32[16]{0:T(128)S(1)} %fusion.5.owners_ref, bf16[512,5120]{1,0:T(8,128)(2,1)S(1)} %copy-done.1, bf16[320,1024]{1,0:T(8,128)(2,1)} %collective-permute-done.2.refs_0_, bf16[320,1024]{1,0:T(8,128)(2,1)S(1)} %collective-permute-done.13.refs_1_, bf16[320,1024]{1,0:T(8,128)(2,1)} %collective-permute-done.3.refs_2_, ...), custom_call_target="tpu_custom_call" | custom-call | flops 1342177280 | bytes 8126464 | tf_op jit(solution)/shard_map/add_part/pallas_call | solution.py:535
  71.2 3.9 %add_part.5.refs_4_ = f32[512,1024]{1,0:T(8,128)S(1)} custom-call(s32[16]{0:T(128)S(1)} %fusion.5.owners_ref, bf16[512,5120]{1,0:T(8,128)(2,1)S(1)} %copy-done.1, bf16[320,1024]{1,0:T(8,128)(2,1)} %collective-permute-done.4.refs_0_, bf16[320,1024]{1,0:T(8,128)(2,1)S(1)} %collective-permute-done.11.refs_1_, bf16[320,1024]{1,0:T(8,128)(2,1)} %collective-permute-done.5.refs_2_, ...), custom_call_target="tpu_custom_call" | custom-call | flops 1342177280 | bytes 8126464 | tf_op jit(solution)/shard_map/add_part/pallas_call | solution.py:535
  76.1 1.1 collective-permute-done.15.refs_2_
  77.7 5.4 %finish.1.refs_3_ = bf16[512,1024]{1,0:T(8,128)(2,1)} custom-call(s32[16]{0:T(128)S(1)} %fusion.5.owners_ref, bf16[512,5120]{1,0:T(8,128)(2,1)S(1)} %bitcast.13, f32[1,1024]{1,0:T(1,128)S(1)} %maximum_convert_fusion.bias_ref, f32[512,128]{1,0:T(8,128)S(1)} %copy-done.11, f32[512,128]{1,0:T(8,128)S(1)} %copy-done.13, ...), custom_call_target="tpu_custom_call" | custom-call | flops 671088640 | bytes 6160384 | tf_op jit(solution)/shard_map/finish/pallas_call | solution.py:554
  86.9 1.0 copy-done.19
  87.9 3.5 %veil.1 = (bf16[16,128,128]{2,1,0:T(8,128)(2,1)S(1)}, bf16[16,256,128]{2,1,0:T(8,128)(2,1)S(1)}, bf16[16,256,128]{2,1,0:T(8,128)(2,1)S(1)}, bf16[16,256,128]{2,1,0:T(8,128)(2,1)S(1)}, bf16[16,128,128]{2,1,0:T(8,128)(2,1)S(1)}) custom-call(s32[768,128]{1,0:T(8,128)S(1)} %copy-done.19, s32[16,1,512]{2,1,0:T(1,128)S(1)} %reshape.75.routes_ref, ...), custom_call_target="tpu_custom_call" | custom-call | flops 3000000000 | bytes 4194304 | tf_op jit(solution)/shard_map/veil/pallas_call | solution.py:583
  92.2 9.9 %attend.5 = (f32[4,2816,128]{2,1,0:T(8,128)S(1)}, f32[4,2816,128]{2,1,0:T(8,128)S(1)}) custom-call(s32[512,1]{1,0:T(8,128)S(1)} %reshape.87.refs_0_, bf16[4,2816,128]{2,1,0:T(8,128)(2,1)S(1)} %get-tuple-element.70.refs_1_, bf16[16,128,128]{2,1,0:T(8,128)(2,1)S(1)} %get-tuple-element.85.refs_2_, bf16[512,1024]{1,0:T(8,128)(2,1)} %finish.1.refs_3_, ...), custom_call_target="tpu_custom_call" | custom-call | flops 4429185024 | bytes 16777216 | tf_op jit(solution)/shard_map/attend/pallas_call | solution.py:617
  102.0 8.7 %collective-permute-done.17.refs_3_ = bf16[512,1024]{1,0:T(8,128)(2,1)} collective-permute-done((bf16[512,1024]{1,0:T(8,128)(2,1)}, bf16[512,1024]{1,0:T(8,128)(2,1)}, u32[]{:S(2)}, u32[]{:S(2)}) %collective-permute-start.17) | collective-permute-done | bytes 1048608 | tf_op jit(solution)/shard_map/ppermute | solution.py:391
  111.7 1.0 collective-permute-start.21
  112.8 1.2 collective-permute-done.22.refs_4_
  114.0 1.5 collective-permute-done.23.refs_6_
  115.5 21.6 %attend.6 = (f32[4,2816,128]{2,1,0:T(8,128)S(1)}, f32[4,2816,128]{2,1,0:T(8,128)S(1)}) custom-call(s32[512,1]{1,0:T(8,128)S(1)} %reshape.87.refs_0_, bf16[4,2816,128]{2,1,0:T(8,128)(2,1)S(1)} %get-tuple-element.70.refs_1_, bf16[16,256,128]{2,1,0:T(8,128)(2,1)S(1)} %get-tuple-element.89.refs_2_, ...), custom_call_target="tpu_custom_call", output_to_operand_aliasing={{0}: (7, {}), {1}: (8, {})} | custom-call | flops 5905580032 | bytes 33554432 | tf_op jit(solution)/shard_map/attend/pallas_call | solution.py:617
  137.7 1.4 collective-permute-start.26
  139.3 1.0 collective-permute-start.25
  140.4 1.0 collective-permute-done.26.refs_4_
  141.4 1.5 collective-permute-done.27.refs_6_
  142.9 20.1 %attend.7 = (f32[4,2816,128]{2,1,0:T(8,128)S(1)}, f32[4,2816,128]{2,1,0:T(8,128)S(1)}) custom-call(s32[512,1]{1,0:T(8,128)S(1)} %reshape.87.refs_0_, bf16[4,2816,128]{2,1,0:T(8,128)(2,1)S(1)} %get-tuple-element.70.refs_1_, bf16[16,256,128]{2,1,0:T(8,128)(2,1)S(1)} %get-tuple-element.96.refs_2_, ...), custom_call_target="tpu_custom_call", output_to_operand_aliasing={{0}: (7, {}), {1}: (8, {})} | custom-call | flops 5905580032 | bytes 33554432 | tf_op jit(solution)/shard_map/attend/pallas_call | solution.py:617
  163.0 2.1 collective-permute-done.24.refs_3_
  165.1 1.4 collective-permute-start.30
  166.6 1.1 collective-permute-start.28
  167.7 1.1 collective-permute-done.30.refs_4_
  168.8 1.5 collective-permute-done.31.refs_6_
  170.3 20.1 %attend.8 = (f32[4,2816,128]{2,1,0:T(8,128)S(1)}, f32[4,2816,128]{2,1,0:T(8,128)S(1)}) custom-call(s32[512,1]{1,0:T(8,128)S(1)} %reshape.87.refs_0_, bf16[4,2816,128]{2,1,0:T(8,128)(2,1)S(1)} %get-tuple-element.70.refs_1_, bf16[16,256,128]{2,1,0:T(8,128)(2,1)S(1)} %get-tuple-element.104.refs_2_, ...), custom_call_target="tpu_custom_call", output_to_operand_aliasing={{0}: (7, {}), {1}: (8, {})} | custom-call | flops 5905580032 | bytes 33554432 | tf_op jit(solution)/shard_map/attend/pallas_call | solution.py:617
  190.4 2.5 %copy-done.2 = f32[4,2816,128]{2,1,0:T(8,128)} copy-done((f32[4,2816,128]{2,1,0:T(8,128)}, f32[4,2816,128]{2,1,0:T(8,128)S(1)}, u32[]{:S(2)}) %copy-start.2) | copy-done | bytes 5767192
  192.9 2.4 %copy-done.4 = f32[4,2816,128]{2,1,0:T(8,128)} copy-done((f32[4,2816,128]{2,1,0:T(8,128)}, f32[4,2816,128]{2,1,0:T(8,128)S(1)}, u32[]{:S(2)}) %copy-start.4) | copy-done | bytes 5767192
  196.0 1.6 collective-permute-done.32.refs_5_
  198.3 2.6 %copy-done.3 = f32[4,2816,128]{2,1,0:T(8,128)S(1)} copy-done((f32[4,2816,128]{2,1,0:T(8,128)S(1)}, f32[4,2816,128]{2,1,0:T(8,128)}, u32[]{:S(2)}) %copy-start.3) | copy-done | bytes 5767192
  201.0 2.6 %copy-done.5 = f32[4,2816,128]{2,1,0:T(8,128)S(1)} copy-done((f32[4,2816,128]{2,1,0:T(8,128)S(1)}, f32[4,2816,128]{2,1,0:T(8,128)}, u32[]{:S(2)}) %copy-start.5) | copy-done | bytes 5767192
  203.6 1.0 copy-done.7
  204.6 21.1 %attend.9 = bf16[512,2560]{1,0:T(8,128)(2,1)} custom-call(s32[512,1]{1,0:T(8,128)S(1)} %reshape.87.refs_0_, bf16[4,2816,128]{2,1,0:T(8,128)(2,1)S(1)} %get-tuple-element.70.refs_1_, bf16[16,128,128]{2,1,0:T(8,128)(2,1)S(1)} %copy-done.7, bf16[256,1024]{1,0:T(8,128)(2,1)} %collective-permute-done.28.refs_3_, ...), custom_call_target="tpu_custom_call" | custom-call | flops 4429185024 | bytes 16777216 | tf_op jit(solution)/shard_map/attend/pallas_call | solution.py:617
  (120 shorter events, 19.7 us)
Async XLA Ops:
  2.0 22.3 %collective-permute-start = (bf16[320,1024]{1,0:T(8,128)(2,1)S(1)}, bf16[320,1024]{1,0:T(8,128)(2,1)}, u32[]{:S(2)}, u32[]{:S(2)}) collective-permute-start(bf16[320,1024]{1,0:T(8,128)(2,1)S(1)} %join.1.refs_0_), channel_id=1, source_target_pairs={{0,4},{1,5},{2,6},{3,7},{4,8},{5,9},{6,10},{7,11},{8,12},{9,13},{1... | collective-permute-start | bytes 1966088 | tf_op jit(solution)/shard_map/ppermute | solution.py:391
  4.2 20.2 %collective-permute-start.1 = (bf16[320,1024]{1,0:T(8,128)(2,1)S(1)}, bf16[320,1024]{1,0:T(8,128)(2,1)}, u32[]{:S(2)}, u32[]{:S(2)}) collective-permute-start(bf16[320,1024]{1,0:T(8,128)(2,1)S(1)} %join.1.refs_0_), channel_id=1, source_target_pairs={{0,2},{1,3},{2,0},{3,1},{4,6},{5,7},{6,4},{7,5},{8,10},{9,11},{10,... | collective-permute-start | bytes 1966088 | tf_op jit(solution)/shard_map/ppermute | solution.py:391
  24.3 3.7 %copy-start.20 = (s32[16,1,1600]{2,0,1:T(8,128)}, s32[16,1,1600]{2,0,1:T(8,128)S(1)}, u32[]{:S(2)}) copy-start(s32[16,1,1600]{2,0,1:T(8,128)S(1)} %copy.40) | copy-start | bytes 307204
  24.4 18.1 %collective-permute-start.2 = (bf16[320,1024]{1,0:T(8,128)(2,1)}, bf16[320,1024]{1,0:T(8,128)(2,1)}, u32[]{:S(2)}, u32[]{:S(2)}) collective-permute-start(bf16[320,1024]{1,0:T(8,128)(2,1)} %collective-permute-done.refs_2_), channel_id=1, source_target_pairs={{0,4},{1,5},{2,6},{3,7},{4,8},{5,9},{6,10},{7,11},{8,12},{9,13},{1... | collective-permute-start | bytes 1966088 | tf_op jit(solution)/shard_map/ppermute | solution.py:391
  25.0 17.5 %collective-permute-start.3 = (bf16[320,1024]{1,0:T(8,128)(2,1)}, bf16[320,1024]{1,0:T(8,128)(2,1)}, u32[]{:S(2)}, u32[]{:S(2)}) collective-permute-start(bf16[320,1024]{1,0:T(8,128)(2,1)} %collective-permute-done.refs_2_), channel_id=1, source_target_pairs={{0,2},{1,3},{2,0},{3,1},{4,6},{5,7},{6,4},{7,5},{8,10},{9,11},{10,... | collective-permute-start | bytes 1966088 | tf_op jit(solution)/shard_map/ppermute | solution.py:391
  25.4 17.5 %collective-permute-start.6 = (bf16[320,1024]{1,0:T(8,128)(2,1)S(1)}, bf16[320,1024]{1,0:T(8,128)(2,1)}, u32[]{:S(2)}, u32[]{:S(2)}) collective-permute-start(bf16[320,1024]{1,0:T(8,128)(2,1)S(1)} %join.1.refs_0_), channel_id=1, source_target_pairs={{0,1},{1,0},{2,3},{3,2},{4,5},{5,4},{6,7},{7,6},{8,9},{9,8},{10,11... | collective-permute-start | bytes 1966088 | tf_op jit(solution)/shard_map/ppermute | solution.py:387
  27.3 17.7 %collective-permute-start.7 = (bf16[320,1024]{1,0:T(8,128)(2,1)}, bf16[320,1024]{1,0:T(8,128)(2,1)}, u32[]{:S(2)}, u32[]{:S(2)}) collective-permute-start(bf16[320,1024]{1,0:T(8,128)(2,1)} %collective-permute-done.refs_2_), channel_id=1, source_target_pairs={{0,1},{1,0},{2,3},{3,2},{4,5},{5,4},{6,7},{7,6},{8,9},{9,8},{10,11... | collective-permute-start | bytes 1966088 | tf_op jit(solution)/shard_map/ppermute | solution.py:387
  28.1 17.1 %collective-permute-start.8 = (bf16[320,1024]{1,0:T(8,128)(2,1)}, bf16[320,1024]{1,0:T(8,128)(2,1)}, u32[]{:S(2)}, u32[]{:S(2)}) collective-permute-start(bf16[320,1024]{1,0:T(8,128)(2,1)} %collective-permute-done.1.refs_4_), channel_id=1, source_target_pairs={{0,1},{1,0},{2,3},{3,2},{4,5},{5,4},{6,7},{7,6},{8,9},{9,8},{10,11... | collective-permute-start | bytes 1966088 | tf_op jit(solution)/shard_map/ppermute | solution.py:387
  32.1 12.3 %copy-start.25 = (s32[16]{0:T(128)S(1)}, s32[16]{0:T(128)}, u32[]{:S(2)}) copy-start(s32[16]{0:T(128)} %constant.36.clone) | copy-start | bytes 196
  42.5 17.1 %collective-permute-start.4 = (bf16[320,1024]{1,0:T(8,128)(2,1)}, bf16[320,1024]{1,0:T(8,128)(2,1)}, u32[]{:S(2)}, u32[]{:S(2)}) collective-permute-start(bf16[320,1024]{1,0:T(8,128)(2,1)} %collective-permute-done.2.refs_0_), channel_id=1, source_target_pairs={{0,4},{1,5},{2,6},{3,7},{4,8},{5,9},{6,10},{7,11},{8,12},{9,13},{1... | collective-permute-start | bytes 1966088 | tf_op jit(solution)/shard_map/ppermute | solution.py:391
  42.5 17.1 %collective-permute-start.5 = (bf16[320,1024]{1,0:T(8,128)(2,1)}, bf16[320,1024]{1,0:T(8,128)(2,1)}, u32[]{:S(2)}, u32[]{:S(2)}) collective-permute-start(bf16[320,1024]{1,0:T(8,128)(2,1)} %collective-permute-done.2.refs_0_), channel_id=1, source_target_pairs={{0,2},{1,3},{2,0},{3,1},{4,6},{5,7},{6,4},{7,5},{8,10},{9,11},{10,... | collective-permute-start | bytes 1966088 | tf_op jit(solution)/shard_map/ppermute | solution.py:391
  42.9 21.1 %collective-permute-start.13 = (bf16[320,1024]{1,0:T(8,128)(2,1)}, bf16[320,1024]{1,0:T(8,128)(2,1)S(1)}, u32[]{:S(2)}, u32[]{:S(2)}) collective-permute-start(bf16[320,1024]{1,0:T(8,128)(2,1)} %collective-permute-done.2.refs_0_), channel_id=1, source_target_pairs={{0,1},{1,0},{2,3},{3,2},{4,5},{5,4},{6,7},{7,6},{8,9},{9,8},{10,11... | collective-permute-start | bytes 1966088 | tf_op jit(solution)/shard_map/ppermute | solution.py:387
  45.1 19.4 %collective-permute-start.14 = (bf16[320,1024]{1,0:T(8,128)(2,1)}, bf16[320,1024]{1,0:T(8,128)(2,1)S(1)}, u32[]{:S(2)}, u32[]{:S(2)}) collective-permute-start(bf16[320,1024]{1,0:T(8,128)(2,1)} %collective-permute-done.3.refs_2_), channel_id=1, source_target_pairs={{0,1},{1,0},{2,3},{3,2},{4,5},{5,4},{6,7},{7,6},{8,9},{9,8},{10,11... | collective-permute-start | bytes 1966088 | tf_op jit(solution)/shard_map/ppermute | solution.py:387
  45.2 2.5 %copy-start = (bf16[512,5120]{1,0:T(8,128)(2,1)S(1)}, bf16[512,5120]{1,0:T(8,128)(2,1)}, u32[]{:S(2)}) copy-start(bf16[512,5120]{1,0:T(8,128)(2,1)} %hidden_ref.7) | copy-start | bytes 15728644
  59.6 11.6 %collective-permute-start.11 = (bf16[320,1024]{1,0:T(8,128)(2,1)}, bf16[320,1024]{1,0:T(8,128)(2,1)S(1)}, u32[]{:S(2)}, u32[]{:S(2)}) collective-permute-start(bf16[320,1024]{1,0:T(8,128)(2,1)} %collective-permute-done.4.refs_0_), channel_id=1, source_target_pairs={{0,1},{1,0},{2,3},{3,2},{4,5},{5,4},{6,7},{7,6},{8,9},{9,8},{10,11... | collective-permute-start | bytes 1966088 | tf_op jit(solution)/shard_map/ppermute | solution.py:387
  61.7 9.4 %collective-permute-start.12 = (bf16[320,1024]{1,0:T(8,128)(2,1)}, bf16[320,1024]{1,0:T(8,128)(2,1)S(1)}, u32[]{:S(2)}, u32[]{:S(2)}) collective-permute-start(bf16[320,1024]{1,0:T(8,128)(2,1)} %collective-permute-done.5.refs_2_), channel_id=1, source_target_pairs={{0,1},{1,0},{2,3},{3,2},{4,5},{5,4},{6,7},{7,6},{8,9},{9,8},{10,11... | collective-permute-start | bytes 1966088 | tf_op jit(solution)/shard_map/ppermute | solution.py:387
  63.7 11.4 %collective-permute-start.10 = (bf16[160,1024]{1,0:T(8,128)(2,1)S(1)}, bf16[160,1024]{1,0:T(8,128)(2,1)S(1)}, u32[]{:S(2)}, u32[]{:S(2)}) collective-permute-start(bf16[160,1024]{1,0:T(8,128)(2,1)S(1)} %slice.33), channel_id=1, source_target_pairs={{0,4},{1,5},{2,6},{3,7},{4,8},{5,9},{6,10},{7,11},{8,12},{9,13},{1... | collective-permute-start | bytes 983048 | tf_op jit(solution)/shard_map/ppermute | solution.py:399
  64.0 11.1 %collective-permute-start.9 = (bf16[160,1024]{1,0:T(8,128)(2,1)S(1)}, bf16[160,1024]{1,0:T(8,128)(2,1)S(1)}, u32[]{:S(2)}, u32[]{:S(2)}) collective-permute-start(bf16[160,1024]{1,0:T(8,128)(2,1)S(1)} %slice.32), channel_id=1, source_target_pairs={{0,2},{1,3},{2,0},{3,1},{4,6},{5,7},{6,4},{7,5},{8,10},{9,11},{10,... | collective-permute-start | bytes 983048 | tf_op jit(solution)/shard_map/ppermute | solution.py:398
  67.0 10.7 %slice-start = ((s8[5242880]{0:T(1024)(128)(4,1)}), s8[4194304]{0:T(1024)(128)(4,1)S(1)}, s32[]{:S(2)}) async-start(s8[5242880]{0:T(1024)(128)(4,1)} %bitcast.12), calls=%async_computation.1 | async-start | bytes 8388608
  71.1 5.0 %copy-start.21 = (bf16[512]{0:T(512)(128)(2,1)S(1)}, bf16[512]{0:T(512)(128)(2,1)}, u32[]{:S(2)}) copy-start(bf16[512]{0:T(512)(128)(2,1)} %param.18) | copy-start | bytes 3076
  71.1 5.0 %copy-start.22 = (bf16[512]{0:T(512)(128)(2,1)S(1)}, bf16[512]{0:T(512)(128)(2,1)}, u32[]{:S(2)}) copy-start(bf16[512]{0:T(512)(128)(2,1)} %param.19) | copy-start | bytes 3076
  71.1 6.6 %slice-start.1 = ((s8[5242880]{0:T(1024)(128)(4,1)}), s8[1048576]{0:T(1024)(128)(4,1)S(1)}, s32[]{:S(2)}) async-start(s8[5242880]{0:T(1024)(128)(4,1)} %bitcast.12), calls=%async_computation.2 | async-start | bytes 2097152
  71.1 6.6 %copy-start.11 = (f32[512,128]{1,0:T(8,128)S(1)}, f32[512,128]{1,0:T(8,128)}, u32[]{:S(2)}) copy-start(f32[512,128]{1,0:T(8,128)} %copy-done.10) | copy-start | bytes 786436
  71.1 6.6 %copy-start.13 = (f32[512,128]{1,0:T(8,128)S(1)}, f32[512,128]{1,0:T(8,128)}, u32[]{:S(2)}) copy-start(f32[512,128]{1,0:T(8,128)} %copy-done.12) | copy-start | bytes 786436
  75.1 9.7 %copy-start.23 = (s32[16]{0:T(128)S(1)}, s32[16]{0:T(128)}, u32[]{:S(2)}) copy-start(s32[16]{0:T(128)} %constant.38.clone) | copy-start | bytes 196
  75.1 9.7 %copy-start.24 = (s32[16]{0:T(128)S(1)}, s32[16]{0:T(128)}, u32[]{:S(2)}) copy-start(s32[16]{0:T(128)} %constant.39.clone) | copy-start | bytes 196
  75.1 2.1 collective-permute-start.15
  76.0 1.7 collective-permute-start.16
  83.2 9.0 %collective-permute-start.19 = (bf16[512,1024]{1,0:T(8,128)(2,1)}, bf16[512,1024]{1,0:T(8,128)(2,1)}, u32[]{:S(2)}, u32[]{:S(2)}) collective-permute-start(bf16[512,1024]{1,0:T(8,128)(2,1)} %finish.1.refs_3_), channel_id=1, source_target_pairs={{0,1},{1,0},{2,3},{3,2},{4,5},{5,4},{6,7},{7,6},{8,9},{9,8},{10,11... | collective-permute-start | bytes 3145736 | tf_op jit(solution)/shard_map/ppermute | solution.py:387
  83.6 27.2 %collective-permute-start.17 = (bf16[512,1024]{1,0:T(8,128)(2,1)}, bf16[512,1024]{1,0:T(8,128)(2,1)}, u32[]{:S(2)}, u32[]{:S(2)}) collective-permute-start(bf16[512,1024]{1,0:T(8,128)(2,1)} %finish.1.refs_3_), channel_id=1, source_target_pairs={{0,4},{1,5},{2,6},{3,7},{4,8},{5,9},{6,10},{7,11},{8,12},{9,13},{1... | collective-permute-start | bytes 3145736 | tf_op jit(solution)/shard_map/ppermute | solution.py:391
  84.1 26.7 %collective-permute-start.18 = (bf16[512,1024]{1,0:T(8,128)(2,1)}, bf16[512,1024]{1,0:T(8,128)(2,1)}, u32[]{:S(2)}, u32[]{:S(2)}) collective-permute-start(bf16[512,1024]{1,0:T(8,128)(2,1)} %finish.1.refs_3_), channel_id=1, source_target_pairs={{0,2},{1,3},{2,0},{3,1},{4,6},{5,7},{6,4},{7,5},{8,10},{9,11},{10,... | collective-permute-start | bytes 3145736 | tf_op jit(solution)/shard_map/ppermute | solution.py:391
  110.8 3.2 %collective-permute-start.22 = (bf16[512,1024]{1,0:T(8,128)(2,1)}, bf16[512,1024]{1,0:T(8,128)(2,1)S(1)}, u32[]{:S(2)}, u32[]{:S(2)}) collective-permute-start(bf16[512,1024]{1,0:T(8,128)(2,1)} %collective-permute-done.17.refs_3_), channel_id=1, source_target_pairs={{0,1},{1,0},{2,3},{3,2},{4,5},{5,4},{6,7},{7,6},{8,9},{9,8},{10,11... | collective-permute-start | bytes 3145736 | tf_op jit(solution)/shard_map/ppermute | solution.py:387
  111.5 4.0 %collective-permute-start.23 = (bf16[512,1024]{1,0:T(8,128)(2,1)}, bf16[512,1024]{1,0:T(8,128)(2,1)S(1)}, u32[]{:S(2)}, u32[]{:S(2)}) collective-permute-start(bf16[512,1024]{1,0:T(8,128)(2,1)} %collective-permute-done.18.refs_5_), channel_id=1, source_target_pairs={{0,1},{1,0},{2,3},{3,2},{4,5},{5,4},{6,7},{7,6},{8,9},{9,8},{10,11... | collective-permute-start | bytes 3145736 | tf_op jit(solution)/shard_map/ppermute | solution.py:387
  111.5 26.2 %collective-permute-start.20 = (bf16[512,1024]{1,0:T(8,128)(2,1)}, bf16[512,1024]{1,0:T(8,128)(2,1)S(1)}, u32[]{:S(2)}, u32[]{:S(2)}) collective-permute-start(bf16[512,1024]{1,0:T(8,128)(2,1)} %collective-permute-done.17.refs_3_), channel_id=1, source_target_pairs={{0,4},{1,5},{2,6},{3,7},{4,8},{5,9},{6,10},{7,11},{8,12},{9,13},{1... | collective-permute-start | bytes 3145736 | tf_op jit(solution)/shard_map/ppermute | solution.py:391
  111.7 26.0 %collective-permute-start.21 = (bf16[512,1024]{1,0:T(8,128)(2,1)}, bf16[512,1024]{1,0:T(8,128)(2,1)S(1)}, u32[]{:S(2)}, u32[]{:S(2)}) collective-permute-start(bf16[512,1024]{1,0:T(8,128)(2,1)} %collective-permute-done.17.refs_3_), channel_id=1, source_target_pairs={{0,2},{1,3},{2,0},{3,1},{4,6},{5,7},{6,4},{7,5},{8,10},{9,11},{10,... | collective-permute-start | bytes 3145736 | tf_op jit(solution)/shard_map/ppermute | solution.py:391
  137.7 3.6 %collective-permute-start.26 = (bf16[512,1024]{1,0:T(8,128)(2,1)S(1)}, bf16[512,1024]{1,0:T(8,128)(2,1)S(1)}, u32[]{:S(2)}, u32[]{:S(2)}) collective-permute-start(bf16[512,1024]{1,0:T(8,128)(2,1)S(1)} %collective-permute-done.20.refs_3_), channel_id=1, source_target_pairs={{0,1},{1,0},{2,3},{3,2},{4,5},{5,4},{6,7},{7,6},{8,9},{9,8},{10,11... | collective-permute-start | bytes 3145736 | tf_op jit(solution)/shard_map/ppermute | solution.py:387
  139.1 3.8 %collective-permute-start.27 = (bf16[512,1024]{1,0:T(8,128)(2,1)S(1)}, bf16[512,1024]{1,0:T(8,128)(2,1)S(1)}, u32[]{:S(2)}, u32[]{:S(2)}) collective-permute-start(bf16[512,1024]{1,0:T(8,128)(2,1)S(1)} %collective-permute-done.21.refs_5_), channel_id=1, source_target_pairs={{0,1},{1,0},{2,3},{3,2},{4,5},{5,4},{6,7},{7,6},{8,9},{9,8},{10,11... | collective-permute-start | bytes 3145736 | tf_op jit(solution)/shard_map/ppermute | solution.py:387
  139.1 26.0 %collective-permute-start.24 = (bf16[512,1024]{1,0:T(8,128)(2,1)S(1)}, bf16[512,1024]{1,0:T(8,128)(2,1)S(1)}, u32[]{:S(2)}, u32[]{:S(2)}) collective-permute-start(bf16[512,1024]{1,0:T(8,128)(2,1)S(1)} %collective-permute-done.20.refs_3_), channel_id=1, source_target_pairs={{0,4},{1,5},{2,6},{3,7},{4,8},{5,9},{6,10},{7,11},{8,12},{9,13},{1... | collective-permute-start | bytes 3145736 | tf_op jit(solution)/shard_map/ppermute | solution.py:391
  139.3 25.8 %collective-permute-start.25 = (bf16[512,1024]{1,0:T(8,128)(2,1)S(1)}, bf16[512,1024]{1,0:T(8,128)(2,1)S(1)}, u32[]{:S(2)}, u32[]{:S(2)}) collective-permute-start(bf16[512,1024]{1,0:T(8,128)(2,1)S(1)} %collective-permute-done.20.refs_3_), channel_id=1, source_target_pairs={{0,2},{1,3},{2,0},{3,1},{4,6},{5,7},{6,4},{7,5},{8,10},{9,11},{10,... | collective-permute-start | bytes 3145736 | tf_op jit(solution)/shard_map/ppermute | solution.py:391
  165.1 3.6 %collective-permute-start.30 = (bf16[512,1024]{1,0:T(8,128)(2,1)S(1)}, bf16[512,1024]{1,0:T(8,128)(2,1)S(1)}, u32[]{:S(2)}, u32[]{:S(2)}) collective-permute-start(bf16[512,1024]{1,0:T(8,128)(2,1)S(1)} %collective-permute-done.24.refs_3_), channel_id=1, source_target_pairs={{0,1},{1,0},{2,3},{3,2},{4,5},{5,4},{6,7},{7,6},{8,9},{9,8},{10,11... | collective-permute-start | bytes 3145736 | tf_op jit(solution)/shard_map/ppermute | solution.py:387
  166.5 3.8 %collective-permute-start.31 = (bf16[512,1024]{1,0:T(8,128)(2,1)S(1)}, bf16[512,1024]{1,0:T(8,128)(2,1)S(1)}, u32[]{:S(2)}, u32[]{:S(2)}) collective-permute-start(bf16[512,1024]{1,0:T(8,128)(2,1)S(1)} %collective-permute-done.25.refs_5_), channel_id=1, source_target_pairs={{0,1},{1,0},{2,3},{3,2},{4,5},{5,4},{6,7},{7,6},{8,9},{9,8},{10,11... | collective-permute-start | bytes 3145736 | tf_op jit(solution)/shard_map/ppermute | solution.py:387
  166.6 28.7 %collective-permute-start.28 = (bf16[256,1024]{1,0:T(8,128)(2,1)S(1)}, bf16[256,1024]{1,0:T(8,128)(2,1)}, u32[]{:S(2)}, u32[]{:S(2)}) collective-permute-start(bf16[256,1024]{1,0:T(8,128)(2,1)S(1)} %slice.34), channel_id=1, source_target_pairs={{0,2},{1,3},{2,0},{3,1},{4,6},{5,7},{6,4},{7,5},{8,10},{9,11},{10,... | collective-permute-start | bytes 1572872 | tf_op jit(solution)/shard_map/ppermute | solution.py:398
  167.7 27.6 %collective-permute-start.29 = (bf16[256,1024]{1,0:T(8,128)(2,1)S(1)}, bf16[256,1024]{1,0:T(8,128)(2,1)}, u32[]{:S(2)}, u32[]{:S(2)}) collective-permute-start(bf16[256,1024]{1,0:T(8,128)(2,1)S(1)} %slice.35), channel_id=1, source_target_pairs={{0,4},{1,5},{2,6},{3,7},{4,8},{5,9},{6,10},{7,11},{8,12},{9,13},{1... | collective-permute-start | bytes 1572872 | tf_op jit(solution)/shard_map/ppermute | solution.py:399
  190.4 2.5 %copy-start.2 = (f32[4,2816,128]{2,1,0:T(8,128)}, f32[4,2816,128]{2,1,0:T(8,128)S(1)}, u32[]{:S(2)}) copy-start(f32[4,2816,128]{2,1,0:T(8,128)S(1)} %get-tuple-element.111.refs_7_) | copy-start | bytes 17301508
  195.3 2.3 %collective-permute-start.32 = (bf16[256,1024]{1,0:T(8,128)(2,1)}, bf16[256,1024]{1,0:T(8,128)(2,1)}, u32[]{:S(2)}, u32[]{:S(2)}) collective-permute-start(bf16[256,1024]{1,0:T(8,128)(2,1)} %collective-permute-done.28.refs_3_), channel_id=1, source_target_pairs={{0,1},{1,0},{2,3},{3,2},{4,5},{5,4},{6,7},{7,6},{8,9},{9,8},{10,11... | collective-permute-start | bytes 1572872 | tf_op jit(solution)/shard_map/ppermute | solution.py:387
  195.7 2.6 %collective-permute-start.33 = (bf16[256,1024]{1,0:T(8,128)(2,1)}, bf16[256,1024]{1,0:T(8,128)(2,1)}, u32[]{:S(2)}, u32[]{:S(2)}) collective-permute-start(bf16[256,1024]{1,0:T(8,128)(2,1)} %collective-permute-done.29.refs_4_), channel_id=1, source_target_pairs={{0,1},{1,0},{2,3},{3,2},{4,5},{5,4},{6,7},{7,6},{8,9},{9,8},{10,11... | collective-permute-start | bytes 1572872 | tf_op jit(solution)/shard_map/ppermute | solution.py:387
  198.3 2.6 %copy-start.3 = (f32[4,2816,128]{2,1,0:T(8,128)S(1)}, f32[4,2816,128]{2,1,0:T(8,128)}, u32[]{:S(2)}) copy-start(f32[4,2816,128]{2,1,0:T(8,128)} %copy-done.2) | copy-start | bytes 17301508
  201.0 2.6 %copy-start.5 = (f32[4,2816,128]{2,1,0:T(8,128)S(1)}, f32[4,2816,128]{2,1,0:T(8,128)}, u32[]{:S(2)}) copy-start(f32[4,2816,128]{2,1,0:T(8,128)} %copy-done.4) | copy-start | bytes 17301508
  (14 other events, 16.1 us)

commit v9 on v8

--- a/solution.py
+++ b/solution.py
@@ -17,7 +17,7 @@
 CHUNKS = ((0, KEY_VALUE_HEADS),)
 PLANE = 4
 PLANES = 4
-UNROLL = 4
+SAFE_POWER = 64.0
 GATHER_LIMIT = 40 * 2**20
 MASKED = -1e30
 VMEM = pl.BlockSpec(memory_space=pltpu.VMEM)
@@ -112,7 +112,7 @@
 
 
 def query_kernel(
-    ranks, spare, stride, packed, route_ref, seat_ref, positions_ref, frequency_ref, queries_ref, *refs
+    ranks, row_step, stride, packed, route_ref, seat_ref, positions_ref, frequency_ref, queries_ref, *refs
 ):
     turned_ref, bounds_ref, cosine_ref, sine_ref, rows_ref = refs
     route = route_ref[...]
@@ -146,7 +146,7 @@
     placed = contract(seats, digits.astype(jnp.float32).astype(jnp.bfloat16), 1, 0)
     live = placed[:, 4:5] - 1.0
     last = placed[:, 0:1] * HEAD_SIZE + placed[:, 1:2] + live
-    start = placed[:, 2:3] * HEAD_SIZE + placed[:, 3:4] + live
+    start = placed[:, 2:3] * HEAD_SIZE + placed[:, 3:4] - live * 2.0**20
     seat_lanes = lax.broadcasted_iota(jnp.int32, placed.shape, 1)
     bounds_ref[...] = jnp.where(seat_lanes == 0, last, start).astype(jnp.int32)
     rows_ref[...] = jnp.zeros(rows_ref.shape, jnp.float32)
@@ -156,8 +156,8 @@
             one = queries_ref[:, at : at + HEAD_SIZE].astype(jnp.float32)
             rows = contract(seats, turn(one, cosine, sine), 1, 0)
             for group in range(ranks):
-                at = group * packed + place * spare
-                rows_ref[at : at + spare] = rows[group * stride : group * stride + spare]
+                at = group * packed + place * row_step
+                rows_ref[at : at + row_step] = rows[group * stride : group * stride + row_step]
         turned_ref[head] = rows_ref[...].astype(jnp.bfloat16)
 
 
@@ -258,7 +258,7 @@
     lax.fori_loop(0, routes_ref.shape[0], one_group, 0)
 
 
-def attend_kernel(starts, before, spare, stride, more, last, *refs):
+def attend_kernel(starts, before, spare, row_step, stride, more, last, *refs):
     more_ref, queries_ref, veil_ref = refs[:3]
     refs = refs[3:]
     blocks = []
@@ -266,13 +266,17 @@
         blocks.append(dict(zip(first_rows, refs)))
         refs = refs[len(first_rows) :]
     if more:
-        stats_ref, total_ref = refs[:2]
-        refs = refs[2:]
+        top_ref, sum_ref, total_ref = refs[:3]
+        refs = refs[3:]
     if last:
-        seat_ref, out_ref, listed_rows, seen_by, mixed_ref, result_ref, done = refs
+        seat_ref, out_ref, mixed_ref, result_ref, leave = refs[0], refs[1], *refs[-3:]
+        refs = refs[:-3]
         mixed_ref[...] = jnp.zeros(mixed_ref.shape, jnp.bfloat16)
     else:
-        new_stats_ref, new_total_ref, listed_rows, seen_by = refs
+        new_top_ref, new_sum_ref, new_total_ref = refs[:3]
+    listed_rows, seen_by, veil, veil_in = refs[-4:]
+    fetch_veil = pltpu.make_async_copy(veil_ref, veil, veil_in)
+    fetch_veil.start()
     heads, ranks = queries_ref.shape[0], veil_ref.shape[0]
     packed = queries_ref.shape[1] // ranks
     wide = heads * HEAD_SIZE
@@ -283,7 +287,7 @@
     lane = lax.broadcasted_iota(jnp.int32, (packed, HEAD_SIZE), 1)
     own = lane < 0
     for at in range(HEAD_GROUPS):
-        own = own | ((token == lane + at * spare) & (lane < spare))
+        own = own | ((token == lane + at * row_step) & (lane < spare))
     seen_by[...] = own.astype(jnp.float32).astype(jnp.bfloat16)
     lines = lax.broadcasted_iota(jnp.int32, (share, count), 1)
     for at, block in enumerate(blocks):
@@ -296,6 +300,7 @@
                 for row, ref in block.items()
             ]
             listed_rows[at * share : (at + 1) * share, lanes] = sum(found).astype(jnp.bfloat16)
+    fetch_veil.wait()
     scale = math.log2(math.e) / math.sqrt(HEAD_SIZE)
 
     def rows_of(group, row, first):
@@ -304,75 +309,117 @@
         rows = [block[row][window, lanes] for block in blocks]
         return jnp.concatenate(rows + [listed_rows[:, lanes]], axis=0)
 
+    def scores_of(group, row, head, tokens):
+        left = jnp.concatenate([queries_ref[head, tokens], seen_by[...]], axis=1)
+        keys = rows_of(group, row, head * HEAD_SIZE)
+        return contract(left, jnp.concatenate([keys, veil[group]], axis=1), 1, 1)
+
+    def products_of(group, row, head, weight):
+        values = rows_of(group, row, wide + head * HEAD_SIZE)
+        values = jnp.concatenate([values, jnp.ones_like(values)], axis=1)
+        mixed = contract(weight, values, 1, 0)
+        return mixed[:, :HEAD_SIZE], mixed[:, HEAD_SIZE:]
+
+    def tile(top, keys):
+        return jnp.concatenate([top] * (keys // HEAD_SIZE), axis=1)
+
+    def finish_head(group, head, total, weight_sum):
+        mixed = total / weight_sum
+        seats = pl.ds(pl.multiple_of(group * stride, 16), row_step)
+        for at in range(HEAD_GROUPS):
+            place = (head * HEAD_GROUPS + at) * HEAD_SIZE
+            rows = mixed[at * row_step : (at + 1) * row_step]
+            mixed_ref[seats, place : place + HEAD_SIZE] = rows.astype(jnp.bfloat16)
+
     def add_heads(group, row, some):
         tokens = pl.ds(pl.multiple_of(group * packed, 16), packed)
-        scores = []
-        for head in some:
-            left = jnp.concatenate([queries_ref[head, tokens], seen_by[...]], axis=1)
-            keys = rows_of(group, row, head * HEAD_SIZE)
-            right = jnp.concatenate([keys, veil_ref[group]], axis=1)
-            scores.append(contract(left, right, 1, 1))
-        tops, weights, fades, sums = [], [], [], []
+        scores = [scores_of(group, row, head, tokens) for head in some]
+        tops, weights = [], []
         for head, score in zip(some, scores):
             top = jnp.max(score, axis=1, keepdims=True)
             if more:
-                stats = stats_ref[head, tokens]
-                other = pltpu.roll(stats, HEAD_SIZE // 2, 1)
-                old_top = jnp.where(lane < HEAD_SIZE // 2, stats, other)
-                sums.append(jnp.where(lane < HEAD_SIZE // 2, other, stats))
-                top = jnp.maximum(old_top, top)
-                fades.append(jnp.exp2((old_top - top) * scale))
+                top = jnp.maximum(top_ref[head, tokens], top)
             else:
                 top = jnp.broadcast_to(top, (packed, HEAD_SIZE))
             tops.append(top)
-            tiled = jnp.concatenate([top] * (score.shape[1] // HEAD_SIZE), axis=1)
-            weights.append(jnp.exp2((score - tiled) * scale).astype(jnp.bfloat16))
-        for at_head, (head, top, weight) in enumerate(zip(some, tops, weights)):
-            values = rows_of(group, row, wide + head * HEAD_SIZE)
-            values = jnp.concatenate([values, jnp.ones_like(values)], axis=1)
-            mixed = contract(weight, values, 1, 0)
-            total, weight_sum = mixed[:, :HEAD_SIZE], mixed[:, HEAD_SIZE:]
+            weight = jnp.exp2((score - tile(top, score.shape[1])) * scale)
+            weights.append(weight.astype(jnp.bfloat16))
+        for head, top, weight in zip(some, tops, weights):
+            total, weight_sum = products_of(group, row, head, weight)
             if more:
-                total = total + fades[at_head] * total_ref[head, tokens]
-                weight_sum = weight_sum + fades[at_head] * sums[at_head]
+                fade = jnp.exp2((top_ref[head, tokens] - top) * scale)
+                total = total + fade * total_ref[head, tokens]
+                weight_sum = weight_sum + fade * sum_ref[head, tokens]
             if last:
-                mixed = total / weight_sum
-                seats = pl.ds(pl.multiple_of(group * stride, 16), spare)
-                for at in range(HEAD_GROUPS):
-                    place = (head * HEAD_GROUPS + at) * HEAD_SIZE
-                    rows = mixed[at * spare : (at + 1) * spare]
-                    mixed_ref[seats, place : place + HEAD_SIZE] = rows.astype(jnp.bfloat16)
+                finish_head(group, head, total, weight_sum)
             else:
-                new_stats_ref[head, tokens] = jnp.where(lane < HEAD_SIZE // 2, top, weight_sum)
+                new_top_ref[head, tokens] = top
+                new_sum_ref[head, tokens] = weight_sum
                 new_total_ref[head, tokens] = total
 
-    rows = sorted({row for first_rows in starts for row in first_rows})
-    for row, end in zip(rows, rows[1:] + [count]):
-
-        def one_group(group, carry, row=row):
-            for head in range(0, heads, UNROLL):
-                add_heads(group, row, range(head, head + UNROLL))
-            return carry
-
-        lax.fori_loop(row // share, end // share, one_group, 0)
-    if last:
-        seat_lanes = lax.broadcasted_iota(jnp.int32, (count, mixed_ref.shape[0]), 1)
-        seats = (seat_lanes == seat_ref[...]).astype(jnp.float32).astype(jnp.bfloat16)
-        span = HEAD_GROUPS * HEAD_SIZE
-        leaving = []
-        for head in range(heads):
-            lanes = slice(head * span, (head + 1) * span)
-            rows = contract(seats, mixed_ref[:, lanes], 1, 0)
-            result_ref[:, lanes] = rows.astype(jnp.bfloat16)
-            lanes = pl.ds(head * span, span)
-            leaving.append(
-                pltpu.make_async_copy(
-                    result_ref.at[:, lanes], out_ref.at[:, lanes], done.at[head]
-                )
-            )
-            leaving[-1].start()
-        for one in leaving:
-            one.wait()
+    def add_heads_as_before(group, row, worst):
+        tokens = pl.ds(pl.multiple_of(group * packed, 16), packed)
+        scores = [scores_of(group, row, head, tokens) for head in range(heads)]
+        weights = []
+        for head, score in enumerate(scores):
+            above = score - tile(top_ref[head, tokens], score.shape[1])
+            for first in range(0, score.shape[1], HEAD_SIZE):
+                part = above[:, first : first + HEAD_SIZE].reshape(packed // 8, 8, HEAD_SIZE)
+                worst = jnp.maximum(worst, jnp.max(part, axis=0))
+            weights.append(jnp.exp2(above * scale).astype(jnp.bfloat16))
+        for head, weight in enumerate(weights):
+            total, weight_sum = products_of(group, row, head, weight)
+            total = total + total_ref[head, tokens]
+            weight_sum = weight_sum + sum_ref[head, tokens]
+            finish_head(group, head, total, weight_sum)
+        return worst
+
+    firsts = sorted({row for first_rows in starts for row in first_rows})
+    spans = [
+        (row, row // share, end // share) for row, end in zip(firsts, firsts[1:] + [count])
+    ]
+
+    def add_all(together):
+        for row, first, end in spans:
+
+            def one_group(group, carry, row=row):
+                for head in range(0, heads, together):
+                    add_heads(group, row, range(head, head + together))
+                return carry
+
+            lax.fori_loop(first, end, one_group, 0)
+
+    if not last:
+        add_all(2 if more else 4)
+        return
+    worst = jnp.full((8, HEAD_SIZE), MASKED, jnp.float32)
+    for row, first, end in spans:
+        worst = lax.fori_loop(
+            first,
+            end,
+            lambda group, worst, row=row: add_heads_as_before(group, row, worst),
+            worst,
+        )
+
+    @pl.when(jnp.max(worst) * scale > SAFE_POWER)
+    def _():
+        add_all(2)
+
+    seat_lanes = lax.broadcasted_iota(jnp.int32, (count, mixed_ref.shape[0]), 1)
+    seats = (seat_lanes == seat_ref[...]).astype(jnp.float32).astype(jnp.bfloat16)
+    span = HEAD_GROUPS * HEAD_SIZE
+    leaving = []
+    for head in range(heads):
+        lanes = slice(head * span, (head + 1) * span)
+        rows = contract(seats, mixed_ref[:, lanes], 1, 0)
+        result_ref[:, lanes] = rows.astype(jnp.bfloat16)
+        lanes = pl.ds(head * span, span)
+        leaving.append(
+            pltpu.make_async_copy(result_ref.at[:, lanes], out_ref.at[:, lanes], leave.at[head])
+        )
+        leaving[-1].start()
+    for one in leaving:
+        one.wait()
 
 
 def spread(block, ranks, held):
@@ -415,6 +462,18 @@
     return lax.rem(plane + (planes - steps), planes) * PLANE + (lane ^ flips)
 
 
+def weight_order(ranks):
+    me = lax.axis_index("dp")
+    lane, plane = lax.rem(me, PLANE), lax.div(me, PLANE)
+    planes = ranks // PLANE
+    turn_back = lax.axis_index("groups") == 1
+    up = np.array([0, 1, 0, planes - 1, 2, 1, 2, planes - 1] * 2, np.int32)
+    steps = jnp.where(turn_back, (planes - up) % planes, up)
+    flips = np.array([0, 0, 2, 0, 0, 2, 2, 2], np.int32)
+    flips = np.concatenate([flips, flips ^ 1])
+    return lax.rem(plane + (planes - steps), planes) * PLANE + (lane ^ flips)
+
+
 def gather_plan(
     hidden,
     queries,
@@ -432,7 +491,8 @@
     spare = share + extra
     listed = ranks * extra
     stride = -(-spare // 16) * 16
-    packed = -(-HEAD_GROUPS * spare // 16) * 16
+    row_step = -(-spare // 8) * 8
+    packed = -(-HEAD_GROUPS * row_step // 16) * 16
     query_width = queries.shape[1]
     shape = jax.ShapeDtypeStruct
 
@@ -440,7 +500,6 @@
         first, heads = chunk
         return array[..., first * HEAD_SIZE : (first + heads) * HEAD_SIZE]
 
-    matrices = {}
     joined = pl.pallas_call(
         join_kernel,
         out_shape=shape((key_matrix.shape[0], 2 * key_matrix.shape[1]), jnp.bfloat16),
@@ -450,8 +509,20 @@
         compiler_params=grant(14),
         name="join",
     )(key_matrix, value_matrix)
-    sending = spread(joined, ranks, matrices)
-    next(sending)
+    every = [(group, rank) for group in range(2) for rank in range(ranks)]
+    ring = [
+        (group * ranks + rank, group * ranks + (rank + (1 - 2 * group) * PLANE) % ranks)
+        for group, rank in every
+    ]
+    across = [(group * ranks + rank, group * ranks + (rank ^ 2)) for group, rank in every]
+    beside = [(group * ranks + rank, group * ranks + (rank ^ 1)) for group, rank in every]
+    swap = [(group * ranks + rank, (1 - group) * ranks + rank) for group, rank in every]
+
+    def send(array, pairs):
+        return lax.ppermute(array, ("groups", "dp"), pairs)
+
+    near_lane, other_row = send(joined, ring), send(joined, across)
+    matrices = {0: (joined, send(joined, beside))}
     bucket, seat, sorted_route, more = pl.pallas_call(
         functools.partial(order_kernel, ranks, slots, extra, stride),
         out_shape=(
@@ -470,8 +541,13 @@
     plan = lax.all_to_all(
         jnp.broadcast_to(plan, (ranks, width + slots)), "dp", split_axis=0, concat_axis=0, tiled=True
     )
-    plan, bucket, seat = sending.send((plan, bucket, seat))
-    next(sending)
+    near_lane, other_row, plan, bucket, seat = lax.optimization_barrier(
+        (near_lane, other_row, plan, bucket, seat)
+    )
+    far_lane, next_lane = send(near_lane, swap), send(near_lane, ring)
+    near_other = send(near_lane, across)
+    matrices[1] = (near_lane, send(near_lane, beside))
+    matrices[2] = (other_row, send(other_row, beside))
     all_positions = plan[:, width:].reshape(-1, HEAD_SIZE)
     planes = ranks // PLANE
     sets = [(0, 2 * planes)] + [
@@ -479,12 +555,12 @@
         for step in range(1, planes)
     ]
     sets.append((2 * planes - 1, 4 * planes - 1))
-    owners = source_order(ranks, range(ranks))
+    owners = weight_order(ranks)
 
     half = HEAD_SIZE // 2
     frequency = 1000000.0 ** (-(jnp.arange(half, dtype=jnp.float32) * 2.0 / HEAD_SIZE))
     turned, bounds, cosine, sine = pl.pallas_call(
-        functools.partial(query_kernel, ranks, spare, stride, packed),
+        functools.partial(query_kernel, ranks, row_step, stride, packed),
         out_shape=(
             shape((KEY_VALUE_HEADS, ranks * packed, HEAD_SIZE), jnp.bfloat16),
             shape((ranks * stride, HEAD_SIZE), jnp.int32),
@@ -508,15 +584,8 @@
     shard, wide = key_matrix.shape[0], 2 * key_matrix.shape[1]
 
     def chip_parts(sources):
-        chips, arrays = [], []
-        for source in sources:
-            chip = []
-            for one in (source, source + 2 * planes):
-                for first, array in matrices[one]:
-                    chip.append((one, first))
-                    arrays.append(array)
-            chips.append(tuple(chip))
-        return chips, arrays
+        chips = [((source, 0), (source + ranks // 2, 0)) for source in sources]
+        return chips, [array for source in sources for array in matrices[source]]
 
     def scratch(chips, arrays):
         return [
@@ -543,13 +612,18 @@
             name="add_part",
         )(owners, hidden, *arrays, *more)
 
-    turned, bounds, cosine, sine = sending.send((turned, bounds, cosine, sine))
-    next(sending)
-    (total,) = sending.send((add_part(None, (0, 1, planes)),))
-    next(sending)
-    total = add_part(total, (2, planes + 1))
-    (total,) = sending.send((add_part(total, (3, planes + 2)),))
-    chips, arrays = chip_parts((planes + 3,))
+    far_lane, next_lane, near_other, turned, bounds, cosine, sine = lax.optimization_barrier(
+        (far_lane, next_lane, near_other, turned, bounds, cosine, sine)
+    )
+    next_other, far_other = send(next_lane, across), send(near_other, swap)
+    matrices[3] = (far_lane, send(far_lane, beside))
+    matrices[4] = (next_lane, send(next_lane, beside))
+    matrices[5] = (near_other, send(near_other, beside))
+    total = add_part(add_part(None, (0, 1, 2)), (3, 4, 5))
+    next_other, far_other, total = lax.optimization_barrier((next_other, far_other, total))
+    matrices[6] = (next_other, send(next_other, beside))
+    matrices[7] = (far_other, send(far_other, beside))
+    chips, arrays = chip_parts((6, 7))
     bias = jnp.concatenate([key_projection_bias, value_projection_bias])
     (pairs,) = pl.pallas_call(
         functools.partial(finish_kernel, chips),
@@ -600,38 +674,46 @@
         sources, last = sets[index], index == len(sets) - 1
         starts = [tuple(first for first, _ in blocks[source]) for source in sources]
         arrays = [array for source in sources for _, array in blocks[source]]
+        keys = 2 * share * len(sources)
         fixed = [more_places, turned, veils[index], *arrays, *state]
         kept = shape((KEY_VALUE_HEADS, ranks * packed, HEAD_SIZE), jnp.float32)
+        outs = [kept] * 3
+        out_specs = [VMEM] * 3
+        in_specs = [VMEM, VMEM, HBM] + [VMEM] * (len(fixed) - 3)
+        handed = {len(fixed) - 3 + at: at + last for at in range(3)} if state else {}
         scratch_shapes = [
             pltpu.VMEM((len(sources) * share, wide), jnp.bfloat16),
             pltpu.VMEM((packed, HEAD_SIZE), jnp.bfloat16),
+            pltpu.VMEM((ranks, keys, HEAD_SIZE), jnp.bfloat16),
+            pltpu.SemaphoreType.DMA,
         ]
         if last:
             fixed.append(seat.reshape(rows, 1))
+            in_specs.append(VMEM)
+            outs.insert(0, shape((rows, query_width), jnp.bfloat16))
+            out_specs.insert(0, HBM)
             scratch_shapes += [
                 pltpu.VMEM((ranks * stride, query_width), jnp.bfloat16),
                 pltpu.VMEM((rows, query_width), jnp.bfloat16),
                 pltpu.SemaphoreType.DMA((KEY_VALUE_HEADS,)),
             ]
-        keys = 2 * share * len(sources)
         return pl.pallas_call(
             functools.partial(
                 attend_kernel,
                 starts,
                 sum(len(one) for one in sets[:index]),
                 spare,
+                row_step,
                 stride,
                 bool(state),
                 last,
             ),
-            out_shape=shape((rows, query_width), jnp.bfloat16) if last else (kept,) * 2,
-            in_specs=[VMEM] * len(fixed),
-            out_specs=HBM if last else (VMEM,) * 2,
+            out_shape=tuple(outs),
+            in_specs=in_specs,
+            out_specs=tuple(out_specs),
             scratch_shapes=scratch_shapes,
-            input_output_aliases={}
-            if last or not state
-            else {len(fixed) - 2 + at: at for at in range(2)},
-            compiler_params=grant(14),
+            input_output_aliases=handed,
+            compiler_params=grant(18 if last else 14),
             cost_estimate=cost(
                 8 * ranks * KEY_VALUE_HEADS * packed * (keys + 256) * HEAD_SIZE,
                 2 * keys * rows * HEAD_SIZE,
@@ -646,7 +728,7 @@
         state = sending.send(tuple(attend(state, step)))
     next(sending)
     state = sending.send(tuple(attend(state, planes - 1)))
-    return attend(state, planes)
+    return attend(state, planes)[0]
 
 
 def apply_rotary(rows, slot_offset, heads):
@@ -784,7 +866,7 @@
     gathered = ranks * ranks * (rows // ranks + 2) * 4 * key_matrix.shape[1]
     chip_rows = 2 * key_matrix.shape[0]
     fits = rows % (16 * ranks) == 0 and chip_rows % HEAD_SIZE == 0 and gathered <= GATHER_LIMIT
-    if ranks == PLANES * PLANE and fits:
+    if ranks == PLANES * PLANE and lax.axis_size("groups") == 2 and fits:
         return gather_plan(*args)
     return send_plan(*args)
 

time: 227 us -> 238 us (1.048)
  local copies, waits for them, and re-layouts: 33.1 us -> 45.3 us
  Pallas kernels: 122 us -> 110 us
  waiting for transfers between devices: 31.6 us -> 43 us
    ppermute x0 -> x15, waiting for transfers between devices: none -> 14.5 us  [send(): return lax.ppermute(array, ('groups', 'dp'), pairs)]
    pallas_call x5, Pallas kernels: 92.8 us -> 79.4 us  [attend(): pl.pallas_call(functools.partial(attend_kernel, starts, sum((len(one) for...]
    ppermute x0 -> x15, starting transfers between devices: none -> 12.3 us  [send(): return lax.ppermute(array, ('groups', 'dp'), pairs)]
    unnamed x57 -> x67, local copies, waits for them, and re-layouts: 26.4 us -> 36.8 us
    ppermute x18 -> x9, starting transfers between devices: 10.5 us -> 4.64 us  [keep(): lax.ppermute(array, 'dp', beside)]
    ppermute x6 -> x3, starting transfers between devices: 3.75 us -> 0.33 us  [spread(): lax.ppermute(lane, 'dp', ring)]
    pallas_call x1, Pallas kernels: 5.43 us -> 7.95 us  [gather_plan(): pl.pallas_call(functools.partial(finish_kernel, chips), out_shape=tuple((...]
    pallas_call x3 -> x2, Pallas kernels: 13.5 us -> 11.1 us  [add_part(): pl.pallas_call(functools.partial(part_kernel, chips, bool(more)), out_sha...]
  transfers between devices with their start and end apart: 34 -> 32, of which waited for: 15 -> 14; matrix products, arithmetic and copies ran while one was open for 3% -> 4% of each run, Pallas kernels for 42% -> 32%
where the time goes in v9:
time: 238 us; the launch traced here: 237 us
  Pallas kernels  110 us (46%)
  local copies, waits for them, and re-layouts  45.3 us (19%)
  waiting for transfers between devices  43 us (18%)
  starting transfers between devices  21.2 us (9%)
  blocking collectives  16.9 us (7%)
    pallas_call x5, Pallas kernels, attend(): pl.pallas_call(functools.partial(attend_kernel, starts, sum((len(one) for...  79.4 us
    unnamed x67, local copies, waits for them, and re-layouts  36.8 us
    ppermute x3, waiting for transfers between devices, spread(): lax.ppermute(lane, 'dp', ring)  18.5 us
    all_to_all x1, blocking collectives, gather_plan(): lax.all_to_all(jnp.broadcast_to(plan, (ranks, width + slots)), 'dp', spli...  16.9 us
    ppermute x15, waiting for transfers between devices, send(): return lax.ppermute(array, ('groups', 'dp'), pairs)  14.5 us
    ppermute x15, starting transfers between devices, send(): return lax.ppermute(array, ('groups', 'dp'), pairs)  12.3 us
    pallas_call x2, Pallas kernels, add_part(): pl.pallas_call(functools.partial(part_kernel, chips, bool(more)), out_sha...  11.1 us
    ppermute x9, waiting for transfers between devices, keep(): lax.ppermute(array, 'dp', beside)  9.99 us
  transfers between devices with their start and end apart: 32, of which 14 were waited for; matrix products, arithmetic and copies ran while one was open for 4% of the time, Pallas kernels for 32%

profile of v9, /device:TPU:1, one launch (start us, length us, event | category | flops | bytes accessed | tf_op | source)
XLA Modules:
  0.0 236.5 jit_solution(778901518550724301)
XLA Ops:
  0.0 1.0 copy-done.14
  1.0 1.0 copy-done.15
  2.9 2.2 collective-permute-start
  5.0 1.2 collective-permute-start.1
  8.5 16.9 %all_to_all.9 = s32[16,1,1600]{2,1,0:T(1,128)S(1)} all-to-all(s32[16,1,1600]{2,1,0:T(1,128)S(1)} %broadcast_in_dim.6), channel_id=1, replica_groups=mesh['groups'=2,'dp'=16] {'dp'}, dimensions={0} | all-to-all | bytes 204800 | tf_op jit(solution)/shard_map/all_to_all | solution.py:541
  25.4 1.0 collective-permute-start.2
  27.7 1.4 collective-permute-start.10
  30.0 11.7 %collective-permute-done.2.refs_0_ = bf16[320,1024]{1,0:T(8,128)(2,1)} collective-permute-done((bf16[320,1024]{1,0:T(8,128)(2,1)}, bf16[320,1024]{1,0:T(8,128)(2,1)}, u32[]{:S(2)}, u32[]{:S(2)}) %collective-permute-start.2) | collective-permute-done | bytes 655392 | tf_op jit(solution)/shard_map/ppermute | solution.py:522
  41.7 1.2 collective-permute-start.12
  44.1 1.7 copy-done.22
  45.8 6.2 %turn_queries.1 = (bf16[4,3328,128]{2,1,0:T(8,128)(2,1)S(1)}, s32[768,128]{1,0:T(8,128)S(1)}, f32[512,128]{1,0:T(8,128)S(1)}, f32[512,128]{1,0:T(8,128)S(1)}) custom-call(s32[512,1]{1,0:T(8,128)S(1)} %copy-done.20, s32[1,512]{1,0:T(1,128)S(1)} %get-tuple-element.72.seat_ref, s32[128,128]{1,0:T(8,128)S(1)} %reshape.72.positions_ref, ...), custom_call_target="tpu_custom_call" | custom-call | flops 4026531840 | bytes 5242880 | tf_op jit(solution)/shard_map/turn_queries/pallas_call | solution.py:562
  55.6 1.5 collective-permute-start.6
  57.1 2.5 %copy-done.6 = bf16[512,5120]{1,0:T(8,128)(2,1)S(1)} copy-done((bf16[512,5120]{1,0:T(8,128)(2,1)S(1)}, bf16[512,5120]{1,0:T(8,128)(2,1)}, u32[]{:S(2)}) %copy-start.6) | copy-done | bytes 5242904
  59.5 5.6 %add_part.2.refs_6_ = f32[512,1024]{1,0:T(8,128)S(1)} custom-call(s32[16]{0:T(128)S(1)} %fusion.7.owners_ref, bf16[512,5120]{1,0:T(8,128)(2,1)S(1)} %copy-done.6, bf16[320,1024]{1,0:T(8,128)(2,1)} %join.1.refs_0_, bf16[320,1024]{1,0:T(8,128)(2,1)} %collective-permute-done.10.refs_1_, bf16[320,1024]{1,0:T(8,128)(2,1)} %collective-permute-done.refs_2_, ...), custom_call_target="tpu_custom_call" | custom-call | flops 2013265920 | bytes 10092544 | tf_op jit(solution)/shard_map/add_part/pallas_call | solution.py:604
  65.2 2.5 %copy-done.7 = bf16[512,5120]{1,0:T(8,128)(2,1)S(1)} copy-done((bf16[512,5120]{1,0:T(8,128)(2,1)S(1)}, bf16[512,5120]{1,0:T(8,128)(2,1)}, u32[]{:S(2)}) %copy-start.7) | copy-done | bytes 5242904
  67.7 5.5 %add_part.3.refs_4_ = f32[512,1024]{1,0:T(8,128)S(1)} custom-call(s32[16]{0:T(128)S(1)} %fusion.7.owners_ref, bf16[512,5120]{1,0:T(8,128)(2,1)S(1)} %copy-done.7, bf16[320,1024]{1,0:T(8,128)(2,1)} %collective-permute-done.2.refs_0_, bf16[320,1024]{1,0:T(8,128)(2,1)} %collective-permute-done.7.refs_1_, bf16[320,1024]{1,0:T(8,128)(2,1)} %collective-permute-done.3.refs_2_, ...), custom_call_target="tpu_custom_call" | custom-call | flops 2013265920 | bytes 10092544 | tf_op jit(solution)/shard_map/add_part/pallas_call | solution.py:604
  73.2 1.1 collective-permute-start.13
  74.4 1.8 collective-permute-done.13.refs_1_
  77.1 2.5 %copy-done.8 = bf16[512,5120]{1,0:T(8,128)(2,1)S(1)} copy-done((bf16[512,5120]{1,0:T(8,128)(2,1)S(1)}, bf16[512,5120]{1,0:T(8,128)(2,1)}, u32[]{:S(2)}) %copy-start.8) | copy-done | bytes 5242904
  79.6 7.9 %finish.1.refs_3_ = bf16[512,1024]{1,0:T(8,128)(2,1)} custom-call(s32[16]{0:T(128)S(1)} %fusion.7.owners_ref, bf16[512,5120]{1,0:T(8,128)(2,1)S(1)} %copy-done.8, f32[1,1024]{1,0:T(1,128)S(1)} %maximum_convert_fusion.bias_ref, f32[512,128]{1,0:T(8,128)S(1)} %copy-done.17, f32[512,128]{1,0:T(8,128)S(1)} %copy-done.19, ...), custom_call_target="tpu_custom_call" | custom-call | flops 1342177280 | bytes 8126464 | tf_op jit(solution)/shard_map/finish/pallas_call | solution.py:628
  88.1 1.1 collective-permute-start.16
  92.9 1.0 reshape.75.routes_ref
  94.8 1.0 copy-done.24
  95.8 3.5 %veil.1 = (bf16[16,128,128]{2,1,0:T(8,128)(2,1)S(1)}, bf16[16,256,128]{2,1,0:T(8,128)(2,1)S(1)}, bf16[16,256,128]{2,1,0:T(8,128)(2,1)S(1)}, bf16[16,256,128]{2,1,0:T(8,128)(2,1)S(1)}, bf16[16,128,128]{2,1,0:T(8,128)(2,1)S(1)}) custom-call(s32[768,128]{1,0:T(8,128)S(1)} %copy-done.24, s32[16,1,512]{2,1,0:T(1,128)S(1)} %reshape.75.routes_ref, ...), custom_call_target="tpu_custom_call" | custom-call | flops 3000000000 | bytes 4194304 | tf_op jit(solution)/shard_map/veil/pallas_call | solution.py:657
  100.1 10.3 %attend.5 = (f32[4,3328,128]{2,1,0:T(8,128)S(1)}, f32[4,3328,128]{2,1,0:T(8,128)S(1)}, f32[4,3328,128]{2,1,0:T(8,128)S(1)}) custom-call(s32[512,1]{1,0:T(8,128)S(1)} %copy-done.9, bf16[4,3328,128]{2,1,0:T(8,128)(2,1)S(1)} %get-tuple-element.77.refs_1_, bf16[16,128,128]{2,1,0:T(8,128)(2,1)S(1)} %get-tuple-element.90.refs_2_, ...), custom_call_target="tpu_custom_call" | custom-call | flops 5234491392 | bytes 16777216 | tf_op jit(solution)/shard_map/attend/pallas_call | solution.py:700
  110.4 4.4 %collective-permute-done.15.refs_3_ = bf16[512,1024]{1,0:T(8,128)(2,1)} collective-permute-done((bf16[512,1024]{1,0:T(8,128)(2,1)}, bf16[512,1024]{1,0:T(8,128)(2,1)}, u32[]{:S(2)}, u32[]{:S(2)}) %collective-permute-start.15) | collective-permute-done | bytes 1048608 | tf_op jit(solution)/shard_map/ppermute | solution.py:438
  114.8 1.0 collective-permute-start.20
  116.1 1.4 collective-permute-start.19
  118.3 1.5 collective-permute-done.21.refs_6_
  119.8 16.0 %attend.6 = (f32[4,3328,128]{2,1,0:T(8,128)S(1)}, f32[4,3328,128]{2,1,0:T(8,128)S(1)}, f32[4,3328,128]{2,1,0:T(8,128)S(1)}) custom-call(s32[512,1]{1,0:T(8,128)S(1)} %copy-done.9, bf16[4,3328,128]{2,1,0:T(8,128)(2,1)S(1)} %get-tuple-element.77.refs_1_, ...), custom_call_target="tpu_custom_call", output_to_operand_aliasing={{0}: (7, {}), {1}: (8, {}), {2}: (9, {})} | custom-call | flops 6979321856 | bytes 33554432 | tf_op jit(solution)/shard_map/attend/pallas_call | solution.py:700
  135.7 6.3 %collective-permute-done.18.refs_3_ = bf16[512,1024]{1,0:T(8,128)(2,1)S(1)} collective-permute-done((bf16[512,1024]{1,0:T(8,128)(2,1)}, bf16[512,1024]{1,0:T(8,128)(2,1)S(1)}, u32[]{:S(2)}, u32[]{:S(2)}) %collective-permute-start.18) | collective-permute-done | bytes 1048608 | tf_op jit(solution)/shard_map/ppermute | solution.py:438
  142.0 1.4 collective-permute-start.24
  144.2 1.5 collective-permute-done.24.refs_4_
  145.7 1.5 collective-permute-done.25.refs_6_
  147.2 14.5 %attend.7 = (f32[4,3328,128]{2,1,0:T(8,128)S(1)}, f32[4,3328,128]{2,1,0:T(8,128)S(1)}, f32[4,3328,128]{2,1,0:T(8,128)S(1)}) custom-call(s32[512,1]{1,0:T(8,128)S(1)} %copy-done.9, bf16[4,3328,128]{2,1,0:T(8,128)(2,1)S(1)} %get-tuple-element.77.refs_1_, ...), custom_call_target="tpu_custom_call", output_to_operand_aliasing={{0}: (7, {}), {1}: (8, {}), {2}: (9, {})} | custom-call | flops 6979321856 | bytes 33554432 | tf_op jit(solution)/shard_map/attend/pallas_call | solution.py:700
  161.6 7.8 %collective-permute-done.22.refs_3_ = bf16[512,1024]{1,0:T(8,128)(2,1)S(1)} collective-permute-done((bf16[512,1024]{1,0:T(8,128)(2,1)S(1)}, bf16[512,1024]{1,0:T(8,128)(2,1)S(1)}, u32[]{:S(2)}, u32[]{:S(2)}) %collective-permute-start.22) | collective-permute-done | bytes 1048608 | tf_op jit(solution)/shard_map/ppermute | solution.py:438
  169.4 1.4 collective-permute-start.28
  171.5 1.6 collective-permute-done.28.refs_4_
  173.0 1.5 collective-permute-done.29.refs_6_
  174.5 14.5 %attend.8 = (f32[4,3328,128]{2,1,0:T(8,128)S(1)}, f32[4,3328,128]{2,1,0:T(8,128)S(1)}, f32[4,3328,128]{2,1,0:T(8,128)S(1)}) custom-call(s32[512,1]{1,0:T(8,128)S(1)} %copy-done.9, bf16[4,3328,128]{2,1,0:T(8,128)(2,1)S(1)} %get-tuple-element.77.refs_1_, ...), custom_call_target="tpu_custom_call", output_to_operand_aliasing={{0}: (7, {}), {1}: (8, {}), {2}: (9, {})} | custom-call | flops 6979321856 | bytes 33554432 | tf_op jit(solution)/shard_map/attend/pallas_call | solution.py:700
  189.0 2.7 %copy-done = f32[4,3328,128]{2,1,0:T(8,128)} copy-done((f32[4,3328,128]{2,1,0:T(8,128)}, f32[4,3328,128]{2,1,0:T(8,128)S(1)}, u32[]{:S(2)}) %copy-start) | copy-done | bytes 6815768
  191.8 2.9 %copy-done.2 = f32[4,3328,128]{2,1,0:T(8,128)} copy-done((f32[4,3328,128]{2,1,0:T(8,128)}, f32[4,3328,128]{2,1,0:T(8,128)S(1)}, u32[]{:S(2)}) %copy-start.2) | copy-done | bytes 6815768
  194.6 2.8 %copy-done.4 = f32[4,3328,128]{2,1,0:T(8,128)} copy-done((f32[4,3328,128]{2,1,0:T(8,128)}, f32[4,3328,128]{2,1,0:T(8,128)S(1)}, u32[]{:S(2)}) %copy-start.4) | copy-done | bytes 6815768
  200.4 2.9 %copy-done.1 = f32[4,3328,128]{2,1,0:T(8,128)S(1)} copy-done((f32[4,3328,128]{2,1,0:T(8,128)S(1)}, f32[4,3328,128]{2,1,0:T(8,128)}, u32[]{:S(2)}) %copy-start.1) | copy-done | bytes 6815768
  203.3 2.9 %copy-done.3 = f32[4,3328,128]{2,1,0:T(8,128)S(1)} copy-done((f32[4,3328,128]{2,1,0:T(8,128)S(1)}, f32[4,3328,128]{2,1,0:T(8,128)}, u32[]{:S(2)}) %copy-start.3) | copy-done | bytes 6815768
  206.2 2.9 %copy-done.5 = f32[4,3328,128]{2,1,0:T(8,128)S(1)} copy-done((f32[4,3328,128]{2,1,0:T(8,128)S(1)}, f32[4,3328,128]{2,1,0:T(8,128)}, u32[]{:S(2)}) %copy-start.5) | copy-done | bytes 6815768
  211.1 1.0 copy-done.13
  212.1 24.2 %attend.9 = (bf16[512,2560]{1,0:T(8,128)(2,1)}, f32[4,3328,128]{2,1,0:T(8,128)S(1)}, f32[4,3328,128]{2,1,0:T(8,128)S(1)}, f32[4,3328,128]{2,1,0:T(8,128)S(1)}) custom-call(s32[512,1]{1,0:T(8,128)S(1)} %copy-done.10, bf16[4,3328,128]{2,1,0:T(8,128)(2,1)S(1)} %get-tuple-element.77.refs_1_, ...), custom_call_target="tpu_custom_call", output_to_operand_aliasing={{1}: (7, {}), {2}: (8, {}), {3}: (9, {})} | custom-call | flops 5234491392 | bytes 16777216 | tf_op jit(solution)/shard_map/attend/pallas_call | solution.py:700
  (122 shorter events, 24.4 us)
Async XLA Ops:
  2.9 22.5 %collective-permute-start = (bf16[320,1024]{1,0:T(8,128)(2,1)}, bf16[320,1024]{1,0:T(8,128)(2,1)}, u32[]{:S(2)}, u32[]{:S(2)}) collective-permute-start(bf16[320,1024]{1,0:T(8,128)(2,1)} %join.1.refs_0_), channel_id=1, source_target_pairs={{0,4},{1,5},{2,6},{3,7},{4,8},{5,9},{6,10},{7,11},{8,12},{9,13},{1... | collective-permute-start | bytes 1966088 | tf_op jit(solution)/shard_map/ppermute | solution.py:522
  5.0 20.4 %collective-permute-start.1 = (bf16[320,1024]{1,0:T(8,128)(2,1)}, bf16[320,1024]{1,0:T(8,128)(2,1)}, u32[]{:S(2)}, u32[]{:S(2)}) collective-permute-start(bf16[320,1024]{1,0:T(8,128)(2,1)} %join.1.refs_0_), channel_id=1, source_target_pairs={{0,2},{1,3},{2,0},{3,1},{4,6},{5,7},{6,4},{7,5},{8,10},{9,11},{10,... | collective-permute-start | bytes 1966088 | tf_op jit(solution)/shard_map/ppermute | solution.py:522
  25.4 17.7 %copy-start.25 = (s32[16,1,1600]{2,0,1:T(8,128)}, s32[16,1,1600]{2,0,1:T(8,128)S(1)}, u32[]{:S(2)}) copy-start(s32[16,1,1600]{2,0,1:T(8,128)S(1)} %copy.47) | copy-start | bytes 307204
  25.4 16.3 %collective-permute-start.2 = (bf16[320,1024]{1,0:T(8,128)(2,1)}, bf16[320,1024]{1,0:T(8,128)(2,1)}, u32[]{:S(2)}, u32[]{:S(2)}) collective-permute-start(bf16[320,1024]{1,0:T(8,128)(2,1)} %collective-permute-done.refs_2_), channel_id=1, source_target_pairs={{0,16},{1,17},{2,18},{3,19},{4,20},{5,21},{6,22},{7,23},{8,24},{9,... | collective-permute-start | bytes 1966088 | tf_op jit(solution)/shard_map/ppermute | solution.py:522
  26.4 27.8 %collective-permute-start.3 = (bf16[320,1024]{1,0:T(8,128)(2,1)}, bf16[320,1024]{1,0:T(8,128)(2,1)}, u32[]{:S(2)}, u32[]{:S(2)}) collective-permute-start(bf16[320,1024]{1,0:T(8,128)(2,1)} %collective-permute-done.refs_2_), channel_id=1, source_target_pairs={{0,4},{1,5},{2,6},{3,7},{4,8},{5,9},{6,10},{7,11},{8,12},{9,13},{1... | collective-permute-start | bytes 1966088 | tf_op jit(solution)/shard_map/ppermute | solution.py:522
  27.3 26.9 %collective-permute-start.4 = (bf16[320,1024]{1,0:T(8,128)(2,1)}, bf16[320,1024]{1,0:T(8,128)(2,1)}, u32[]{:S(2)}, u32[]{:S(2)}) collective-permute-start(bf16[320,1024]{1,0:T(8,128)(2,1)} %collective-permute-done.refs_2_), channel_id=1, source_target_pairs={{0,2},{1,3},{2,0},{3,1},{4,6},{5,7},{6,4},{7,5},{8,10},{9,11},{10,... | collective-permute-start | bytes 1966088 | tf_op jit(solution)/shard_map/ppermute | solution.py:522
  27.7 27.0 %collective-permute-start.10 = (bf16[320,1024]{1,0:T(8,128)(2,1)}, bf16[320,1024]{1,0:T(8,128)(2,1)}, u32[]{:S(2)}, u32[]{:S(2)}) collective-permute-start(bf16[320,1024]{1,0:T(8,128)(2,1)} %join.1.refs_0_), channel_id=1, source_target_pairs={{0,1},{1,0},{2,3},{3,2},{4,5},{5,4},{6,7},{7,6},{8,9},{9,8},{10,11... | collective-permute-start | bytes 1966088 | tf_op jit(solution)/shard_map/ppermute | solution.py:522
  30.0 24.8 %collective-permute-start.11 = (bf16[320,1024]{1,0:T(8,128)(2,1)}, bf16[320,1024]{1,0:T(8,128)(2,1)}, u32[]{:S(2)}, u32[]{:S(2)}) collective-permute-start(bf16[320,1024]{1,0:T(8,128)(2,1)} %collective-permute-done.refs_2_), channel_id=1, source_target_pairs={{0,1},{1,0},{2,3},{3,2},{4,5},{5,4},{6,7},{7,6},{8,9},{9,8},{10,11... | collective-permute-start | bytes 1966088 | tf_op jit(solution)/shard_map/ppermute | solution.py:522
  41.7 13.8 %collective-permute-start.12 = (bf16[320,1024]{1,0:T(8,128)(2,1)}, bf16[320,1024]{1,0:T(8,128)(2,1)}, u32[]{:S(2)}, u32[]{:S(2)}) collective-permute-start(bf16[320,1024]{1,0:T(8,128)(2,1)} %collective-permute-done.1.refs_4_), channel_id=1, source_target_pairs={{0,1},{1,0},{2,3},{3,2},{4,5},{5,4},{6,7},{7,6},{8,9},{9,8},{10,11... | collective-permute-start | bytes 1966088 | tf_op jit(solution)/shard_map/ppermute | solution.py:522
  45.8 11.2 %copy-start.30 = (s32[16]{0:T(128)S(1)}, s32[16]{0:T(128)}, u32[]{:S(2)}) copy-start(s32[16]{0:T(128)} %constant.45.clone) | copy-start | bytes 196
  45.8 11.2 %copy-start.31 = (s32[16]{0:T(128)S(1)}, s32[16]{0:T(128)}, u32[]{:S(2)}) copy-start(s32[16]{0:T(128)} %constant.46.clone) | copy-start | bytes 196
  45.8 11.2 %copy-start.32 = (s32[16]{0:T(128)S(1)}, s32[16]{0:T(128)}, u32[]{:S(2)}) copy-start(s32[16]{0:T(128)} %constant.47.clone) | copy-start | bytes 196
  54.2 11.0 %collective-permute-start.7 = (bf16[320,1024]{1,0:T(8,128)(2,1)}, bf16[320,1024]{1,0:T(8,128)(2,1)}, u32[]{:S(2)}, u32[]{:S(2)}) collective-permute-start(bf16[320,1024]{1,0:T(8,128)(2,1)} %collective-permute-done.2.refs_0_), channel_id=1, source_target_pairs={{0,1},{1,0},{2,3},{3,2},{4,5},{5,4},{6,7},{7,6},{8,9},{9,8},{10,11... | collective-permute-start | bytes 1966088 | tf_op jit(solution)/shard_map/ppermute | solution.py:522
  54.2 11.0 %collective-permute-start.8 = (bf16[320,1024]{1,0:T(8,128)(2,1)}, bf16[320,1024]{1,0:T(8,128)(2,1)}, u32[]{:S(2)}, u32[]{:S(2)}) collective-permute-start(bf16[320,1024]{1,0:T(8,128)(2,1)} %collective-permute-done.3.refs_2_), channel_id=1, source_target_pairs={{0,1},{1,0},{2,3},{3,2},{4,5},{5,4},{6,7},{7,6},{8,9},{9,8},{10,11... | collective-permute-start | bytes 1966088 | tf_op jit(solution)/shard_map/ppermute | solution.py:522
  54.7 10.5 %collective-permute-start.9 = (bf16[320,1024]{1,0:T(8,128)(2,1)}, bf16[320,1024]{1,0:T(8,128)(2,1)}, u32[]{:S(2)}, u32[]{:S(2)}) collective-permute-start(bf16[320,1024]{1,0:T(8,128)(2,1)} %collective-permute-done.4.refs_4_), channel_id=1, source_target_pairs={{0,1},{1,0},{2,3},{3,2},{4,5},{5,4},{6,7},{7,6},{8,9},{9,8},{10,11... | collective-permute-start | bytes 1966088 | tf_op jit(solution)/shard_map/ppermute | solution.py:522
  54.8 18.4 %collective-permute-start.5 = (bf16[320,1024]{1,0:T(8,128)(2,1)}, bf16[320,1024]{1,0:T(8,128)(2,1)}, u32[]{:S(2)}, u32[]{:S(2)}) collective-permute-start(bf16[320,1024]{1,0:T(8,128)(2,1)} %collective-permute-done.3.refs_2_), channel_id=1, source_target_pairs={{0,2},{1,3},{2,0},{3,1},{4,6},{5,7},{6,4},{7,5},{8,10},{9,11},{10,... | collective-permute-start | bytes 1966088 | tf_op jit(solution)/shard_map/ppermute | solution.py:522
  55.6 17.6 %collective-permute-start.6 = (bf16[320,1024]{1,0:T(8,128)(2,1)}, bf16[320,1024]{1,0:T(8,128)(2,1)}, u32[]{:S(2)}, u32[]{:S(2)}) collective-permute-start(bf16[320,1024]{1,0:T(8,128)(2,1)} %collective-permute-done.4.refs_4_), channel_id=1, source_target_pairs={{0,16},{1,17},{2,18},{3,19},{4,20},{5,21},{6,22},{7,23},{8,24},{9,... | collective-permute-start | bytes 1966088 | tf_op jit(solution)/shard_map/ppermute | solution.py:522
  59.5 14.8 %copy-start.26 = (bf16[512]{0:T(512)(128)(2,1)S(1)}, bf16[512]{0:T(512)(128)(2,1)}, u32[]{:S(2)}) copy-start(bf16[512]{0:T(512)(128)(2,1)} %param.19) | copy-start | bytes 3076
  59.5 14.8 %copy-start.27 = (bf16[512]{0:T(512)(128)(2,1)S(1)}, bf16[512]{0:T(512)(128)(2,1)}, u32[]{:S(2)}) copy-start(bf16[512]{0:T(512)(128)(2,1)} %param.20) | copy-start | bytes 3076
  59.5 17.6 %copy-start.17 = (f32[512,128]{1,0:T(8,128)S(1)}, f32[512,128]{1,0:T(8,128)}, u32[]{:S(2)}) copy-start(f32[512,128]{1,0:T(8,128)} %copy-done.16) | copy-start | bytes 786436
  59.5 17.6 %copy-start.19 = (f32[512,128]{1,0:T(8,128)S(1)}, f32[512,128]{1,0:T(8,128)}, u32[]{:S(2)}) copy-start(f32[512,128]{1,0:T(8,128)} %copy-done.18) | copy-start | bytes 786436
  73.2 14.9 %copy-start.28 = (s32[16]{0:T(128)S(1)}, s32[16]{0:T(128)}, u32[]{:S(2)}) copy-start(s32[16]{0:T(128)} %constant.48.clone) | copy-start | bytes 196
  73.2 14.9 %copy-start.29 = (s32[16]{0:T(128)S(1)}, s32[16]{0:T(128)}, u32[]{:S(2)}) copy-start(s32[16]{0:T(128)} %constant.49.clone) | copy-start | bytes 196
  73.2 3.0 %collective-permute-start.13 = (bf16[320,1024]{1,0:T(8,128)(2,1)}, bf16[320,1024]{1,0:T(8,128)(2,1)S(1)}, u32[]{:S(2)}, u32[]{:S(2)}) collective-permute-start(bf16[320,1024]{1,0:T(8,128)(2,1)} %collective-permute-done.5.refs_0_), channel_id=1, source_target_pairs={{0,1},{1,0},{2,3},{3,2},{4,5},{5,4},{6,7},{7,6},{8,9},{9,8},{10,11... | collective-permute-start | bytes 1966088 | tf_op jit(solution)/shard_map/ppermute | solution.py:522
  74.3 2.9 %collective-permute-start.14 = (bf16[320,1024]{1,0:T(8,128)(2,1)}, bf16[320,1024]{1,0:T(8,128)(2,1)S(1)}, u32[]{:S(2)}, u32[]{:S(2)}) collective-permute-start(bf16[320,1024]{1,0:T(8,128)(2,1)} %collective-permute-done.6.refs_2_), channel_id=1, source_target_pairs={{0,1},{1,0},{2,3},{3,2},{4,5},{5,4},{6,7},{7,6},{8,9},{9,8},{10,11... | collective-permute-start | bytes 1966088 | tf_op jit(solution)/shard_map/ppermute | solution.py:522
  87.6 12.5 %collective-permute-start.17 = (bf16[512,1024]{1,0:T(8,128)(2,1)}, bf16[512,1024]{1,0:T(8,128)(2,1)}, u32[]{:S(2)}, u32[]{:S(2)}) collective-permute-start(bf16[512,1024]{1,0:T(8,128)(2,1)} %finish.1.refs_3_), channel_id=1, source_target_pairs={{0,1},{1,0},{2,3},{3,2},{4,5},{5,4},{6,7},{7,6},{8,9},{9,8},{10,11... | collective-permute-start | bytes 3145736 | tf_op jit(solution)/shard_map/ppermute | solution.py:434
  88.0 26.8 %collective-permute-start.15 = (bf16[512,1024]{1,0:T(8,128)(2,1)}, bf16[512,1024]{1,0:T(8,128)(2,1)}, u32[]{:S(2)}, u32[]{:S(2)}) collective-permute-start(bf16[512,1024]{1,0:T(8,128)(2,1)} %finish.1.refs_3_), channel_id=1, source_target_pairs={{0,4},{1,5},{2,6},{3,7},{4,8},{5,9},{6,10},{7,11},{8,12},{9,13},{1... | collective-permute-start | bytes 3145736 | tf_op jit(solution)/shard_map/ppermute | solution.py:438
  88.1 26.7 %collective-permute-start.16 = (bf16[512,1024]{1,0:T(8,128)(2,1)}, bf16[512,1024]{1,0:T(8,128)(2,1)}, u32[]{:S(2)}, u32[]{:S(2)}) collective-permute-start(bf16[512,1024]{1,0:T(8,128)(2,1)} %finish.1.refs_3_), channel_id=1, source_target_pairs={{0,2},{1,3},{2,0},{3,1},{4,6},{5,7},{6,4},{7,5},{8,10},{9,11},{10,... | collective-permute-start | bytes 3145736 | tf_op jit(solution)/shard_map/ppermute | solution.py:438
  95.8 4.3 %copy-start.9 = (s32[512,1]{1,0:T(8,128)S(1)}, s32[512,1]{1,0:T(8,128)}, u32[]{:S(2)}) copy-start(s32[512,1]{1,0:T(8,128)} %reshape.87.refs_0_) | copy-start | bytes 6148
  114.8 3.5 %collective-permute-start.20 = (bf16[512,1024]{1,0:T(8,128)(2,1)}, bf16[512,1024]{1,0:T(8,128)(2,1)S(1)}, u32[]{:S(2)}, u32[]{:S(2)}) collective-permute-start(bf16[512,1024]{1,0:T(8,128)(2,1)} %collective-permute-done.15.refs_3_), channel_id=1, source_target_pairs={{0,1},{1,0},{2,3},{3,2},{4,5},{5,4},{6,7},{7,6},{8,9},{9,8},{10,11... | collective-permute-start | bytes 3145736 | tf_op jit(solution)/shard_map/ppermute | solution.py:434
  115.8 4.0 %collective-permute-start.21 = (bf16[512,1024]{1,0:T(8,128)(2,1)}, bf16[512,1024]{1,0:T(8,128)(2,1)S(1)}, u32[]{:S(2)}, u32[]{:S(2)}) collective-permute-start(bf16[512,1024]{1,0:T(8,128)(2,1)} %collective-permute-done.16.refs_5_), channel_id=1, source_target_pairs={{0,1},{1,0},{2,3},{3,2},{4,5},{5,4},{6,7},{7,6},{8,9},{9,8},{10,11... | collective-permute-start | bytes 3145736 | tf_op jit(solution)/shard_map/ppermute | solution.py:434
  115.8 26.2 %collective-permute-start.18 = (bf16[512,1024]{1,0:T(8,128)(2,1)}, bf16[512,1024]{1,0:T(8,128)(2,1)S(1)}, u32[]{:S(2)}, u32[]{:S(2)}) collective-permute-start(bf16[512,1024]{1,0:T(8,128)(2,1)} %collective-permute-done.15.refs_3_), channel_id=1, source_target_pairs={{0,4},{1,5},{2,6},{3,7},{4,8},{5,9},{6,10},{7,11},{8,12},{9,13},{1... | collective-permute-start | bytes 3145736 | tf_op jit(solution)/shard_map/ppermute | solution.py:438
  116.1 26.0 %collective-permute-start.19 = (bf16[512,1024]{1,0:T(8,128)(2,1)}, bf16[512,1024]{1,0:T(8,128)(2,1)S(1)}, u32[]{:S(2)}, u32[]{:S(2)}) collective-permute-start(bf16[512,1024]{1,0:T(8,128)(2,1)} %collective-permute-done.15.refs_3_), channel_id=1, source_target_pairs={{0,2},{1,3},{2,0},{3,1},{4,6},{5,7},{6,4},{7,5},{8,10},{9,11},{10,... | collective-permute-start | bytes 3145736 | tf_op jit(solution)/shard_map/ppermute | solution.py:438
  142.0 3.6 %collective-permute-start.24 = (bf16[512,1024]{1,0:T(8,128)(2,1)S(1)}, bf16[512,1024]{1,0:T(8,128)(2,1)S(1)}, u32[]{:S(2)}, u32[]{:S(2)}) collective-permute-start(bf16[512,1024]{1,0:T(8,128)(2,1)S(1)} %collective-permute-done.18.refs_3_), channel_id=1, source_target_pairs={{0,1},{1,0},{2,3},{3,2},{4,5},{5,4},{6,7},{7,6},{8,9},{9,8},{10,11... | collective-permute-start | bytes 3145736 | tf_op jit(solution)/shard_map/ppermute | solution.py:434
  143.4 3.8 %collective-permute-start.25 = (bf16[512,1024]{1,0:T(8,128)(2,1)S(1)}, bf16[512,1024]{1,0:T(8,128)(2,1)S(1)}, u32[]{:S(2)}, u32[]{:S(2)}) collective-permute-start(bf16[512,1024]{1,0:T(8,128)(2,1)S(1)} %collective-permute-done.19.refs_5_), channel_id=1, source_target_pairs={{0,1},{1,0},{2,3},{3,2},{4,5},{5,4},{6,7},{7,6},{8,9},{9,8},{10,11... | collective-permute-start | bytes 3145736 | tf_op jit(solution)/shard_map/ppermute | solution.py:434
  143.4 26.0 %collective-permute-start.22 = (bf16[512,1024]{1,0:T(8,128)(2,1)S(1)}, bf16[512,1024]{1,0:T(8,128)(2,1)S(1)}, u32[]{:S(2)}, u32[]{:S(2)}) collective-permute-start(bf16[512,1024]{1,0:T(8,128)(2,1)S(1)} %collective-permute-done.18.refs_3_), channel_id=1, source_target_pairs={{0,4},{1,5},{2,6},{3,7},{4,8},{5,9},{6,10},{7,11},{8,12},{9,13},{1... | collective-permute-start | bytes 3145736 | tf_op jit(solution)/shard_map/ppermute | solution.py:438
  143.4 26.0 %collective-permute-start.23 = (bf16[512,1024]{1,0:T(8,128)(2,1)S(1)}, bf16[512,1024]{1,0:T(8,128)(2,1)S(1)}, u32[]{:S(2)}, u32[]{:S(2)}) collective-permute-start(bf16[512,1024]{1,0:T(8,128)(2,1)S(1)} %collective-permute-done.18.refs_3_), channel_id=1, source_target_pairs={{0,2},{1,3},{2,0},{3,1},{4,6},{5,7},{6,4},{7,5},{8,10},{9,11},{10,... | collective-permute-start | bytes 3145736 | tf_op jit(solution)/shard_map/ppermute | solution.py:438
  169.4 3.6 %collective-permute-start.28 = (bf16[512,1024]{1,0:T(8,128)(2,1)S(1)}, bf16[512,1024]{1,0:T(8,128)(2,1)S(1)}, u32[]{:S(2)}, u32[]{:S(2)}) collective-permute-start(bf16[512,1024]{1,0:T(8,128)(2,1)S(1)} %collective-permute-done.22.refs_3_), channel_id=1, source_target_pairs={{0,1},{1,0},{2,3},{3,2},{4,5},{5,4},{6,7},{7,6},{8,9},{9,8},{10,11... | collective-permute-start | bytes 3145736 | tf_op jit(solution)/shard_map/ppermute | solution.py:434
  170.8 3.8 %collective-permute-start.29 = (bf16[512,1024]{1,0:T(8,128)(2,1)S(1)}, bf16[512,1024]{1,0:T(8,128)(2,1)S(1)}, u32[]{:S(2)}, u32[]{:S(2)}) collective-permute-start(bf16[512,1024]{1,0:T(8,128)(2,1)S(1)} %collective-permute-done.23.refs_5_), channel_id=1, source_target_pairs={{0,1},{1,0},{2,3},{3,2},{4,5},{5,4},{6,7},{7,6},{8,9},{9,8},{10,11... | collective-permute-start | bytes 3145736 | tf_op jit(solution)/shard_map/ppermute | solution.py:434
  170.8 26.5 %collective-permute-start.26 = (bf16[256,1024]{1,0:T(8,128)(2,1)S(1)}, bf16[256,1024]{1,0:T(8,128)(2,1)}, u32[]{:S(2)}, u32[]{:S(2)}) collective-permute-start(bf16[256,1024]{1,0:T(8,128)(2,1)S(1)} %slice.26), channel_id=1, source_target_pairs={{0,2},{1,3},{2,0},{3,1},{4,6},{5,7},{6,4},{7,5},{8,10},{9,11},{10,... | collective-permute-start | bytes 1572872 | tf_op jit(solution)/shard_map/ppermute | solution.py:445
  171.5 25.9 %collective-permute-start.27 = (bf16[256,1024]{1,0:T(8,128)(2,1)S(1)}, bf16[256,1024]{1,0:T(8,128)(2,1)}, u32[]{:S(2)}, u32[]{:S(2)}) collective-permute-start(bf16[256,1024]{1,0:T(8,128)(2,1)S(1)} %slice.27), channel_id=1, source_target_pairs={{0,4},{1,5},{2,6},{3,7},{4,8},{5,9},{6,10},{7,11},{8,12},{9,13},{1... | collective-permute-start | bytes 1572872 | tf_op jit(solution)/shard_map/ppermute | solution.py:446
  191.8 2.9 %copy-start.2 = (f32[4,3328,128]{2,1,0:T(8,128)}, f32[4,3328,128]{2,1,0:T(8,128)S(1)}, u32[]{:S(2)}) copy-start(f32[4,3328,128]{2,1,0:T(8,128)S(1)} %get-tuple-element.124.refs_8_) | copy-start | bytes 20447236
  194.6 2.8 %copy-start.4 = (f32[4,3328,128]{2,1,0:T(8,128)}, f32[4,3328,128]{2,1,0:T(8,128)S(1)}, u32[]{:S(2)}) copy-start(f32[4,3328,128]{2,1,0:T(8,128)S(1)} %get-tuple-element.125.refs_9_) | copy-start | bytes 20447236
  197.4 2.3 collective-permute-start.30
  197.7 2.6 %collective-permute-start.31 = (bf16[256,1024]{1,0:T(8,128)(2,1)}, bf16[256,1024]{1,0:T(8,128)(2,1)}, u32[]{:S(2)}, u32[]{:S(2)}) collective-permute-start(bf16[256,1024]{1,0:T(8,128)(2,1)} %collective-permute-done.27.refs_4_), channel_id=1, source_target_pairs={{0,1},{1,0},{2,3},{3,2},{4,5},{5,4},{6,7},{7,6},{8,9},{9,8},{10,11... | collective-permute-start | bytes 1572872 | tf_op jit(solution)/shard_map/ppermute | solution.py:434
  200.4 2.9 %copy-start.1 = (f32[4,3328,128]{2,1,0:T(8,128)S(1)}, f32[4,3328,128]{2,1,0:T(8,128)}, u32[]{:S(2)}) copy-start(f32[4,3328,128]{2,1,0:T(8,128)} %copy-done) | copy-start | bytes 20447236
  203.3 2.9 %copy-start.3 = (f32[4,3328,128]{2,1,0:T(8,128)S(1)}, f32[4,3328,128]{2,1,0:T(8,128)}, u32[]{:S(2)}) copy-start(f32[4,3328,128]{2,1,0:T(8,128)} %copy-done.2) | copy-start | bytes 20447236
  206.2 2.9 %copy-start.5 = (f32[4,3328,128]{2,1,0:T(8,128)S(1)}, f32[4,3328,128]{2,1,0:T(8,128)}, u32[]{:S(2)}) copy-start(f32[4,3328,128]{2,1,0:T(8,128)} %copy-done.4) | copy-start | bytes 20447236
  (17 other events, 22.4 us)

commit v10 on v9

--- a/solution.py
+++ b/solution.py
@@ -522,7 +522,7 @@
         return lax.ppermute(array, ("groups", "dp"), pairs)
 
     near_lane, other_row = send(joined, ring), send(joined, across)
-    matrices = {0: (joined, send(joined, beside))}
+    joined_swap = send(joined, beside)
     bucket, seat, sorted_route, more = pl.pallas_call(
         functools.partial(order_kernel, ranks, slots, extra, stride),
         out_shape=(
@@ -541,13 +541,13 @@
     plan = lax.all_to_all(
         jnp.broadcast_to(plan, (ranks, width + slots)), "dp", split_axis=0, concat_axis=0, tiled=True
     )
-    near_lane, other_row, plan, bucket, seat = lax.optimization_barrier(
-        (near_lane, other_row, plan, bucket, seat)
-    )
+    near_lane, other_row, joined_swap, plan, bucket, seat = lax.optimization_barrier(
+        (near_lane, other_row, joined_swap, plan, bucket, seat)
+    )
+    matrices = {0: (joined, joined_swap)}
     far_lane, next_lane = send(near_lane, swap), send(near_lane, ring)
     near_other = send(near_lane, across)
-    matrices[1] = (near_lane, send(near_lane, beside))
-    matrices[2] = (other_row, send(other_row, beside))
+    swaps = send(near_lane, beside), send(other_row, beside)
     all_positions = plan[:, width:].reshape(-1, HEAD_SIZE)
     planes = ranks // PLANE
     sets = [(0, 2 * planes)] + [
@@ -612,9 +612,18 @@
             name="add_part",
         )(owners, hidden, *arrays, *more)
 
-    far_lane, next_lane, near_other, turned, bounds, cosine, sine = lax.optimization_barrier(
-        (far_lane, next_lane, near_other, turned, bounds, cosine, sine)
-    )
+    bias = jnp.concatenate([key_projection_bias, value_projection_bias])
+    bias = bias.astype(jnp.float32).reshape(1, -1)
+    seat = seat.reshape(rows, 1)
+    far_lane, next_lane, near_other, swaps, turned, bounds, cosine, sine, bias, owners, seat = (
+        lax.optimization_barrier(
+            (
+                far_lane, next_lane, near_other, swaps,
+                turned, bounds, cosine, sine, bias, owners, seat,
+            )
+        )
+    )
+    matrices[1], matrices[2] = (near_lane, swaps[0]), (other_row, swaps[1])
     next_other, far_other = send(next_lane, across), send(near_other, swap)
     matrices[3] = (far_lane, send(far_lane, beside))
     matrices[4] = (next_lane, send(next_lane, beside))
@@ -624,7 +633,6 @@
     matrices[6] = (next_other, send(next_other, beside))
     matrices[7] = (far_other, send(far_other, beside))
     chips, arrays = chip_parts((6, 7))
-    bias = jnp.concatenate([key_projection_bias, value_projection_bias])
     (pairs,) = pl.pallas_call(
         functools.partial(finish_kernel, chips),
         out_shape=tuple(
@@ -639,7 +647,7 @@
     )(
         owners,
         hidden,
-        bias.astype(jnp.float32).reshape(1, wide),
+        bias,
         cosine,
         sine,
         bucket,
@@ -688,7 +696,7 @@
             pltpu.SemaphoreType.DMA,
         ]
         if last:
-            fixed.append(seat.reshape(rows, 1))
+            fixed.append(seat)
             in_specs.append(VMEM)
             outs.insert(0, shape((rows, query_width), jnp.bfloat16))
             out_specs.insert(0, HBM)

time: 238 us -> 225 us (0.945)
  blocking collectives: 16.9 us -> 0 us
  starting transfers between devices: 21.2 us -> 25.7 us
    all_to_all x1 -> x0, blocking collectives: 16.9 us -> none  [gather_plan(): lax.all_to_all(jnp.broadcast_to(plan, (ranks, width + slots)), 'dp', spli...]
    all_to_all x0 -> x1, waiting for transfers between devices: none -> 9.41 us  [gather_plan(): lax.all_to_all(jnp.broadcast_to(plan, (ranks, width + slots)), 'dp', spli...]
    ppermute x15, waiting for transfers between devices: 14.5 us -> 6.78 us  [send(): return lax.ppermute(array, ('groups', 'dp'), pairs)]
    all_to_all x0 -> x1, starting transfers between devices: none -> 3.99 us  [gather_plan(): lax.all_to_all(jnp.broadcast_to(plan, (ranks, width + slots)), 'dp', spli...]
    unnamed x67 -> x57, local copies, waits for them, and re-layouts: 36.8 us -> 33.8 us
  transfers between devices with their start and end apart: 32 -> 33, of which waited for: 14 -> 16; matrix products, arithmetic and copies ran while one was open for 4% -> 5% of each run, Pallas kernels for 32% -> 34%
where the time goes in v10:
time: 225 us; the launch traced here: 224 us
  Pallas kernels  108 us (48%)
  waiting for transfers between devices  44.7 us (20%)
  local copies, waits for them, and re-layouts  44.2 us (20%)
  starting transfers between devices  25.7 us (11%)
    pallas_call x5, Pallas kernels, attend(): pl.pallas_call(functools.partial(attend_kernel, starts, sum((len(one) for...  79.4 us
    unnamed x57, local copies, waits for them, and re-layouts  33.8 us
    ppermute x3, waiting for transfers between devices, spread(): lax.ppermute(lane, 'dp', ring)  18.3 us
    ppermute x15, starting transfers between devices, send(): return lax.ppermute(array, ('groups', 'dp'), pairs)  12.9 us
    pallas_call x2, Pallas kernels, add_part(): pl.pallas_call(functools.partial(part_kernel, chips, bool(more)), out_sha...  11 us
    ppermute x9, waiting for transfers between devices, keep(): lax.ppermute(array, 'dp', beside)  10.2 us
    all_to_all x1, waiting for transfers between devices, gather_plan(): lax.all_to_all(jnp.broadcast_to(plan, (ranks, width + slots)), 'dp', spli...  9.41 us
    pallas_call x1, Pallas kernels, gather_plan(): pl.pallas_call(functools.partial(finish_kernel, chips), out_shape=tuple((...  7.57 us
  transfers between devices with their start and end apart: 33, of which 16 were waited for; matrix products, arithmetic and copies ran while one was open for 5% of the time, Pallas kernels for 34%

profile of v10, /device:TPU:1, one launch (start us, length us, event | category | flops | bytes accessed | tf_op | source)
XLA Modules:
  0.0 224.3 jit_solution(1669919072482539819)
XLA Ops:
  0.0 1.0 copy-done.18
  1.0 1.0 copy-done.19
  2.0 2.2 collective-permute-start
  4.2 1.2 collective-permute-start.1
  5.5 1.2 collective-permute-start.2
  9.6 4.0 %all-to-all-start = ((s32[16,1,1600]{2,1,0:T(1,128)}), s32[16,1,1600]{2,1,0:T(1,128)S(1)}, u32[]{:S(2)}, u32[]{:S(2)}) async-start(s32[16,1,1600]{2,1,0:T(1,128)} %broadcast_in_dim.6), calls=%async_computation | async-start | bytes 212992 | tf_op jit(solution)/shard_map/all_to_all | solution.py:541
  14.9 9.4 %all-to-all-done = s32[16,1,1600]{2,1,0:T(1,128)S(1)} async-done(((s32[16,1,1600]{2,1,0:T(1,128)}), s32[16,1,1600]{2,1,0:T(1,128)S(1)}, u32[]{:S(2)}, u32[]{:S(2)}) %all-to-all-start) | async-done | bytes 102432 | tf_op jit(solution)/shard_map/all_to_all | solution.py:541
  27.5 1.4 collective-permute-start.6
  31.6 1.7 copy-done.22
  33.3 6.2 %turn_queries.1 = (bf16[4,3328,128]{2,1,0:T(8,128)(2,1)S(1)}, s32[768,128]{1,0:T(8,128)S(1)}, f32[512,128]{1,0:T(8,128)S(1)}, f32[512,128]{1,0:T(8,128)S(1)}) custom-call(s32[512,1]{1,0:T(8,128)S(1)} %copy-done.20, s32[1,512]{1,0:T(1,128)S(1)} %get-tuple-element.79.seat_ref, s32[128,128]{1,0:T(8,128)S(1)} %reshape.72.positions_ref, ...), custom_call_target="tpu_custom_call" | custom-call | flops 4026531840 | bytes 5242880 | tf_op jit(solution)/shard_map/turn_queries/pallas_call | solution.py:562
  40.2 1.2 collective-permute-done.3.refs_0_
  41.5 2.9 %collective-permute-done.4.refs_2_ = bf16[320,1024]{1,0:T(8,128)(2,1)} collective-permute-done((bf16[320,1024]{1,0:T(8,128)(2,1)}, bf16[320,1024]{1,0:T(8,128)(2,1)}, u32[]{:S(2)}, u32[]{:S(2)}) %collective-permute-start.4) | collective-permute-done | bytes 655392 | tf_op jit(solution)/shard_map/ppermute | solution.py:522
  44.4 1.5 collective-permute-start.10
  47.3 1.0 collective-permute-start.9
  48.3 2.5 %copy-done.6 = bf16[512,5120]{1,0:T(8,128)(2,1)S(1)} copy-done((bf16[512,5120]{1,0:T(8,128)(2,1)S(1)}, bf16[512,5120]{1,0:T(8,128)(2,1)}, u32[]{:S(2)}) %copy-start.6) | copy-done | bytes 5242904
  50.8 5.9 %add_part.2.refs_6_ = f32[512,1024]{1,0:T(8,128)S(1)} custom-call(s32[16]{0:T(128)S(1)} %fusion.7.owners_ref, bf16[512,5120]{1,0:T(8,128)(2,1)S(1)} %copy-done.6, bf16[320,1024]{1,0:T(8,128)(2,1)S(1)} %copy-done.12, bf16[320,1024]{1,0:T(8,128)(2,1)S(1)} %copy-done.15, bf16[320,1024]{1,0:T(8,128)(2,1)} %collective-permute-done.refs_2_, ...), custom_call_target="tpu_custom_call" | custom-call | flops 2013265920 | bytes 10092544 | tf_op jit(solution)/shard_map/add_part/pallas_call | solution.py:604
  56.8 2.5 %copy-done.7 = bf16[512,5120]{1,0:T(8,128)(2,1)S(1)} copy-done((bf16[512,5120]{1,0:T(8,128)(2,1)S(1)}, bf16[512,5120]{1,0:T(8,128)(2,1)}, u32[]{:S(2)}) %copy-start.7) | copy-done | bytes 5242904
  59.2 5.1 %add_part.3.refs_4_ = f32[512,1024]{1,0:T(8,128)S(1)} custom-call(s32[16]{0:T(128)S(1)} %fusion.7.owners_ref, bf16[512,5120]{1,0:T(8,128)(2,1)S(1)} %copy-done.7, bf16[320,1024]{1,0:T(8,128)(2,1)} %collective-permute-done.3.refs_0_, bf16[320,1024]{1,0:T(8,128)(2,1)S(1)} %collective-permute-done.10.refs_1_, bf16[320,1024]{1,0:T(8,128)(2,1)} %collective-permute-done.4.refs_2_, ...), custom_call_target="tpu_custom_call" | custom-call | flops 2013265920 | bytes 10092544 | tf_op jit(solution)/shard_map/add_part/pallas_call | solution.py:604
  65.2 1.6 collective-permute-done.13.refs_1_
  67.8 7.6 %finish.1.refs_3_ = bf16[512,1024]{1,0:T(8,128)(2,1)} custom-call(s32[16]{0:T(128)S(1)} %fusion.7.owners_ref, bf16[512,5120]{1,0:T(8,128)(2,1)S(1)} %copy-done.8, f32[1,1024]{1,0:T(1,128)S(1)} %maximum_convert_fusion.bias_ref, f32[512,128]{1,0:T(8,128)S(1)} %get-tuple-element.89.cosine_ref, f32[512,128]{1,0:T(8,128)S(1)} %get-tuple-element.90.sine_ref, ...), custom_call_target="tpu_custom_call" | custom-call | flops 1342177280 | bytes 8126464 | tf_op jit(solution)/shard_map/finish/pallas_call | solution.py:636
  75.9 1.2 collective-permute-start.16
  80.7 1.0 reshape.76.routes_ref
  82.7 1.0 copy-done.24
  83.7 3.5 %veil.1 = (bf16[16,128,128]{2,1,0:T(8,128)(2,1)S(1)}, bf16[16,256,128]{2,1,0:T(8,128)(2,1)S(1)}, bf16[16,256,128]{2,1,0:T(8,128)(2,1)S(1)}, bf16[16,256,128]{2,1,0:T(8,128)(2,1)S(1)}, bf16[16,128,128]{2,1,0:T(8,128)(2,1)S(1)}) custom-call(s32[768,128]{1,0:T(8,128)S(1)} %copy-done.24, s32[16,1,512]{2,1,0:T(1,128)S(1)} %reshape.76.routes_ref, ...), custom_call_target="tpu_custom_call" | custom-call | flops 3000000000 | bytes 4194304 | tf_op jit(solution)/shard_map/veil/pallas_call | solution.py:665
  88.0 10.3 %attend.5 = (f32[4,3328,128]{2,1,0:T(8,128)S(1)}, f32[4,3328,128]{2,1,0:T(8,128)S(1)}, f32[4,3328,128]{2,1,0:T(8,128)S(1)}) custom-call(s32[512,1]{1,0:T(8,128)S(1)} %copy-done.9, bf16[4,3328,128]{2,1,0:T(8,128)(2,1)S(1)} %get-tuple-element.84.refs_1_, bf16[16,128,128]{2,1,0:T(8,128)(2,1)S(1)} %get-tuple-element.101.refs_2_, ...), custom_call_target="tpu_custom_call" | custom-call | flops 5234491392 | bytes 16777216 | tf_op jit(solution)/shard_map/attend/pallas_call | solution.py:708
  98.3 4.3 %collective-permute-done.15.refs_3_ = bf16[512,1024]{1,0:T(8,128)(2,1)} collective-permute-done((bf16[512,1024]{1,0:T(8,128)(2,1)}, bf16[512,1024]{1,0:T(8,128)(2,1)}, u32[]{:S(2)}, u32[]{:S(2)}) %collective-permute-start.15) | collective-permute-done | bytes 1048608 | tf_op jit(solution)/shard_map/ppermute | solution.py:438
  104.5 1.5 collective-permute-done.20.refs_4_
  106.0 1.5 collective-permute-done.21.refs_6_
  107.5 16.0 %attend.6 = (f32[4,3328,128]{2,1,0:T(8,128)S(1)}, f32[4,3328,128]{2,1,0:T(8,128)S(1)}, f32[4,3328,128]{2,1,0:T(8,128)S(1)}) custom-call(s32[512,1]{1,0:T(8,128)S(1)} %copy-done.9, bf16[4,3328,128]{2,1,0:T(8,128)(2,1)S(1)} %get-tuple-element.84.refs_1_, ...), custom_call_target="tpu_custom_call", output_to_operand_aliasing={{0}: (7, {}), {1}: (8, {}), {2}: (9, {})} | custom-call | flops 6979321856 | bytes 33554432 | tf_op jit(solution)/shard_map/attend/pallas_call | solution.py:708
  123.5 6.2 %collective-permute-done.18.refs_3_ = bf16[512,1024]{1,0:T(8,128)(2,1)S(1)} collective-permute-done((bf16[512,1024]{1,0:T(8,128)(2,1)}, bf16[512,1024]{1,0:T(8,128)(2,1)S(1)}, u32[]{:S(2)}, u32[]{:S(2)}) %collective-permute-start.18) | collective-permute-done | bytes 1048608 | tf_op jit(solution)/shard_map/ppermute | solution.py:438
  129.8 1.4 collective-permute-start.24
  132.1 1.3 collective-permute-done.24.refs_4_
  133.4 1.5 collective-permute-done.25.refs_6_
  134.9 14.5 %attend.7 = (f32[4,3328,128]{2,1,0:T(8,128)S(1)}, f32[4,3328,128]{2,1,0:T(8,128)S(1)}, f32[4,3328,128]{2,1,0:T(8,128)S(1)}) custom-call(s32[512,1]{1,0:T(8,128)S(1)} %copy-done.9, bf16[4,3328,128]{2,1,0:T(8,128)(2,1)S(1)} %get-tuple-element.84.refs_1_, ...), custom_call_target="tpu_custom_call", output_to_operand_aliasing={{0}: (7, {}), {1}: (8, {}), {2}: (9, {})} | custom-call | flops 6979321856 | bytes 33554432 | tf_op jit(solution)/shard_map/attend/pallas_call | solution.py:708
  149.4 7.8 %collective-permute-done.22.refs_3_ = bf16[512,1024]{1,0:T(8,128)(2,1)S(1)} collective-permute-done((bf16[512,1024]{1,0:T(8,128)(2,1)S(1)}, bf16[512,1024]{1,0:T(8,128)(2,1)S(1)}, u32[]{:S(2)}, u32[]{:S(2)}) %collective-permute-start.22) | collective-permute-done | bytes 1048608 | tf_op jit(solution)/shard_map/ppermute | solution.py:438
  157.2 1.4 collective-permute-start.28
  158.6 1.0 collective-permute-start.26
  159.6 1.2 collective-permute-done.28.refs_4_
  160.8 1.5 collective-permute-done.29.refs_6_
  162.3 14.5 %attend.8 = (f32[4,3328,128]{2,1,0:T(8,128)S(1)}, f32[4,3328,128]{2,1,0:T(8,128)S(1)}, f32[4,3328,128]{2,1,0:T(8,128)S(1)}) custom-call(s32[512,1]{1,0:T(8,128)S(1)} %copy-done.9, bf16[4,3328,128]{2,1,0:T(8,128)(2,1)S(1)} %get-tuple-element.84.refs_1_, ...), custom_call_target="tpu_custom_call", output_to_operand_aliasing={{0}: (7, {}), {1}: (8, {}), {2}: (9, {})} | custom-call | flops 6979321856 | bytes 33554432 | tf_op jit(solution)/shard_map/attend/pallas_call | solution.py:708
  176.8 2.7 %copy-done = f32[4,3328,128]{2,1,0:T(8,128)} copy-done((f32[4,3328,128]{2,1,0:T(8,128)}, f32[4,3328,128]{2,1,0:T(8,128)S(1)}, u32[]{:S(2)}) %copy-start) | copy-done | bytes 6815768
  179.5 2.9 %copy-done.2 = f32[4,3328,128]{2,1,0:T(8,128)} copy-done((f32[4,3328,128]{2,1,0:T(8,128)}, f32[4,3328,128]{2,1,0:T(8,128)S(1)}, u32[]{:S(2)}) %copy-start.2) | copy-done | bytes 6815768
  182.4 2.7 %copy-done.4 = f32[4,3328,128]{2,1,0:T(8,128)} copy-done((f32[4,3328,128]{2,1,0:T(8,128)}, f32[4,3328,128]{2,1,0:T(8,128)S(1)}, u32[]{:S(2)}) %copy-start.4) | copy-done | bytes 6815768
  188.1 2.9 %copy-done.1 = f32[4,3328,128]{2,1,0:T(8,128)S(1)} copy-done((f32[4,3328,128]{2,1,0:T(8,128)S(1)}, f32[4,3328,128]{2,1,0:T(8,128)}, u32[]{:S(2)}) %copy-start.1) | copy-done | bytes 6815768
  191.1 2.9 %copy-done.3 = f32[4,3328,128]{2,1,0:T(8,128)S(1)} copy-done((f32[4,3328,128]{2,1,0:T(8,128)S(1)}, f32[4,3328,128]{2,1,0:T(8,128)}, u32[]{:S(2)}) %copy-start.3) | copy-done | bytes 6815768
  194.0 2.9 %copy-done.5 = f32[4,3328,128]{2,1,0:T(8,128)S(1)} copy-done((f32[4,3328,128]{2,1,0:T(8,128)S(1)}, f32[4,3328,128]{2,1,0:T(8,128)}, u32[]{:S(2)}) %copy-start.5) | copy-done | bytes 6815768
  198.8 1.0 copy-done.17
  199.9 24.2 %attend.9 = (bf16[512,2560]{1,0:T(8,128)(2,1)}, f32[4,3328,128]{2,1,0:T(8,128)S(1)}, f32[4,3328,128]{2,1,0:T(8,128)S(1)}, f32[4,3328,128]{2,1,0:T(8,128)S(1)}) custom-call(s32[512,1]{1,0:T(8,128)S(1)} %copy-done.10, bf16[4,3328,128]{2,1,0:T(8,128)(2,1)S(1)} %get-tuple-element.84.refs_1_, ...), custom_call_target="tpu_custom_call", output_to_operand_aliasing={{1}: (7, {}), {2}: (8, {}), {3}: (9, {})} | custom-call | flops 5234491392 | bytes 16777216 | tf_op jit(solution)/shard_map/attend/pallas_call | solution.py:708
  (113 shorter events, 27.8 us)
Async XLA Ops:
  2.0 28.5 %copy-start.11 = (bf16[320,1024]{1,0:T(8,128)(2,1)}, bf16[320,1024]{1,0:T(8,128)(2,1)S(1)}, u32[]{:S(2)}) copy-start(bf16[320,1024]{1,0:T(8,128)(2,1)S(1)} %join.1.refs_0_) | copy-start | bytes 1966084
  2.0 22.3 %collective-permute-start = (bf16[320,1024]{1,0:T(8,128)(2,1)S(1)}, bf16[320,1024]{1,0:T(8,128)(2,1)}, u32[]{:S(2)}, u32[]{:S(2)}) collective-permute-start(bf16[320,1024]{1,0:T(8,128)(2,1)S(1)} %join.1.refs_0_), channel_id=1, source_target_pairs={{0,4},{1,5},{2,6},{3,7},{4,8},{5,9},{6,10},{7,11},{8,12},{9,13},{1... | collective-permute-start | bytes 1966088 | tf_op jit(solution)/shard_map/ppermute | solution.py:522
  4.2 20.2 %collective-permute-start.1 = (bf16[320,1024]{1,0:T(8,128)(2,1)S(1)}, bf16[320,1024]{1,0:T(8,128)(2,1)}, u32[]{:S(2)}, u32[]{:S(2)}) collective-permute-start(bf16[320,1024]{1,0:T(8,128)(2,1)S(1)} %join.1.refs_0_), channel_id=1, source_target_pairs={{0,2},{1,3},{2,0},{3,1},{4,6},{5,7},{6,4},{7,5},{8,10},{9,11},{10,... | collective-permute-start | bytes 1966088 | tf_op jit(solution)/shard_map/ppermute | solution.py:522
  5.5 18.9 %collective-permute-start.2 = (bf16[320,1024]{1,0:T(8,128)(2,1)S(1)}, bf16[320,1024]{1,0:T(8,128)(2,1)S(1)}, u32[]{:S(2)}, u32[]{:S(2)}) collective-permute-start(bf16[320,1024]{1,0:T(8,128)(2,1)S(1)} %join.1.refs_0_), channel_id=1, source_target_pairs={{0,1},{1,0},{2,3},{3,2},{4,5},{5,4},{6,7},{7,6},{8,9},{9,8},{10,11... | collective-permute-start | bytes 1966088 | tf_op jit(solution)/shard_map/ppermute | solution.py:522
  9.6 14.8 %all-to-all-start = ((s32[16,1,1600]{2,1,0:T(1,128)}), s32[16,1,1600]{2,1,0:T(1,128)S(1)}, u32[]{:S(2)}, u32[]{:S(2)}) async-start(s32[16,1,1600]{2,1,0:T(1,128)} %broadcast_in_dim.6), calls=%async_computation | async-start | bytes 212992 | tf_op jit(solution)/shard_map/all_to_all | solution.py:541
  24.4 6.2 %copy-start.25 = (s32[16,1,1600]{2,0,1:T(8,128)}, s32[16,1,1600]{2,0,1:T(8,128)S(1)}, u32[]{:S(2)}) copy-start(s32[16,1,1600]{2,0,1:T(8,128)S(1)} %copy.47) | copy-start | bytes 307204
  25.2 16.2 %collective-permute-start.3 = (bf16[320,1024]{1,0:T(8,128)(2,1)}, bf16[320,1024]{1,0:T(8,128)(2,1)}, u32[]{:S(2)}, u32[]{:S(2)}) collective-permute-start(bf16[320,1024]{1,0:T(8,128)(2,1)} %collective-permute-done.refs_2_), channel_id=1, source_target_pairs={{0,16},{1,17},{2,18},{3,19},{4,20},{5,21},{6,22},{7,23},{8,24},{9,... | collective-permute-start | bytes 1966088 | tf_op jit(solution)/shard_map/ppermute | solution.py:522
  26.2 18.2 %collective-permute-start.4 = (bf16[320,1024]{1,0:T(8,128)(2,1)}, bf16[320,1024]{1,0:T(8,128)(2,1)}, u32[]{:S(2)}, u32[]{:S(2)}) collective-permute-start(bf16[320,1024]{1,0:T(8,128)(2,1)} %collective-permute-done.refs_2_), channel_id=1, source_target_pairs={{0,4},{1,5},{2,6},{3,7},{4,8},{5,9},{6,10},{7,11},{8,12},{9,13},{1... | collective-permute-start | bytes 1966088 | tf_op jit(solution)/shard_map/ppermute | solution.py:522
  27.1 17.3 %collective-permute-start.5 = (bf16[320,1024]{1,0:T(8,128)(2,1)}, bf16[320,1024]{1,0:T(8,128)(2,1)}, u32[]{:S(2)}, u32[]{:S(2)}) collective-permute-start(bf16[320,1024]{1,0:T(8,128)(2,1)} %collective-permute-done.refs_2_), channel_id=1, source_target_pairs={{0,2},{1,3},{2,0},{3,1},{4,6},{5,7},{6,4},{7,5},{8,10},{9,11},{10,... | collective-permute-start | bytes 1966088 | tf_op jit(solution)/shard_map/ppermute | solution.py:522
  27.5 17.0 %collective-permute-start.6 = (bf16[320,1024]{1,0:T(8,128)(2,1)}, bf16[320,1024]{1,0:T(8,128)(2,1)}, u32[]{:S(2)}, u32[]{:S(2)}) collective-permute-start(bf16[320,1024]{1,0:T(8,128)(2,1)} %collective-permute-done.refs_2_), channel_id=1, source_target_pairs={{0,1},{1,0},{2,3},{3,2},{4,5},{5,4},{6,7},{7,6},{8,9},{9,8},{10,11... | collective-permute-start | bytes 1966088 | tf_op jit(solution)/shard_map/ppermute | solution.py:522
  28.9 15.5 %collective-permute-start.7 = (bf16[320,1024]{1,0:T(8,128)(2,1)}, bf16[320,1024]{1,0:T(8,128)(2,1)}, u32[]{:S(2)}, u32[]{:S(2)}) collective-permute-start(bf16[320,1024]{1,0:T(8,128)(2,1)} %collective-permute-done.1.refs_4_), channel_id=1, source_target_pairs={{0,1},{1,0},{2,3},{3,2},{4,5},{5,4},{6,7},{7,6},{8,9},{9,8},{10,11... | collective-permute-start | bytes 1966088 | tf_op jit(solution)/shard_map/ppermute | solution.py:522
  33.3 15.0 %copy-start.12 = (bf16[320,1024]{1,0:T(8,128)(2,1)S(1)}, bf16[320,1024]{1,0:T(8,128)(2,1)}, u32[]{:S(2)}) copy-start(bf16[320,1024]{1,0:T(8,128)(2,1)} %copy-done.11) | copy-start | bytes 1966084
  33.3 15.0 %copy-start.15 = (bf16[320,1024]{1,0:T(8,128)(2,1)S(1)}, bf16[320,1024]{1,0:T(8,128)(2,1)}, u32[]{:S(2)}) copy-start(bf16[320,1024]{1,0:T(8,128)(2,1)} %copy-done.14) | copy-start | bytes 1966084
  44.4 12.3 %collective-permute-start.10 = (bf16[320,1024]{1,0:T(8,128)(2,1)}, bf16[320,1024]{1,0:T(8,128)(2,1)S(1)}, u32[]{:S(2)}, u32[]{:S(2)}) collective-permute-start(bf16[320,1024]{1,0:T(8,128)(2,1)} %collective-permute-done.3.refs_0_), channel_id=1, source_target_pairs={{0,1},{1,0},{2,3},{3,2},{4,5},{5,4},{6,7},{7,6},{8,9},{9,8},{10,11... | collective-permute-start | bytes 1966088 | tf_op jit(solution)/shard_map/ppermute | solution.py:522
  45.9 10.8 %collective-permute-start.11 = (bf16[320,1024]{1,0:T(8,128)(2,1)}, bf16[320,1024]{1,0:T(8,128)(2,1)S(1)}, u32[]{:S(2)}, u32[]{:S(2)}) collective-permute-start(bf16[320,1024]{1,0:T(8,128)(2,1)} %collective-permute-done.4.refs_2_), channel_id=1, source_target_pairs={{0,1},{1,0},{2,3},{3,2},{4,5},{5,4},{6,7},{7,6},{8,9},{9,8},{10,11... | collective-permute-start | bytes 1966088 | tf_op jit(solution)/shard_map/ppermute | solution.py:522
  46.0 10.7 %collective-permute-start.12 = (bf16[320,1024]{1,0:T(8,128)(2,1)}, bf16[320,1024]{1,0:T(8,128)(2,1)S(1)}, u32[]{:S(2)}, u32[]{:S(2)}) collective-permute-start(bf16[320,1024]{1,0:T(8,128)(2,1)} %collective-permute-done.5.refs_4_), channel_id=1, source_target_pairs={{0,1},{1,0},{2,3},{3,2},{4,5},{5,4},{6,7},{7,6},{8,9},{9,8},{10,11... | collective-permute-start | bytes 1966088 | tf_op jit(solution)/shard_map/ppermute | solution.py:522
  46.4 18.0 %collective-permute-start.8 = (bf16[320,1024]{1,0:T(8,128)(2,1)}, bf16[320,1024]{1,0:T(8,128)(2,1)S(1)}, u32[]{:S(2)}, u32[]{:S(2)}) collective-permute-start(bf16[320,1024]{1,0:T(8,128)(2,1)} %collective-permute-done.4.refs_2_), channel_id=1, source_target_pairs={{0,2},{1,3},{2,0},{3,1},{4,6},{5,7},{6,4},{7,5},{8,10},{9,11},{10,... | collective-permute-start | bytes 1966088 | tf_op jit(solution)/shard_map/ppermute | solution.py:522
  47.3 17.1 %collective-permute-start.9 = (bf16[320,1024]{1,0:T(8,128)(2,1)}, bf16[320,1024]{1,0:T(8,128)(2,1)S(1)}, u32[]{:S(2)}, u32[]{:S(2)}) collective-permute-start(bf16[320,1024]{1,0:T(8,128)(2,1)} %collective-permute-done.5.refs_4_), channel_id=1, source_target_pairs={{0,16},{1,17},{2,18},{3,19},{4,20},{5,21},{6,22},{7,23},{8,24},{9,... | collective-permute-start | bytes 1966088 | tf_op jit(solution)/shard_map/ppermute | solution.py:522
  50.8 17.0 %copy-start.8 = (bf16[512,5120]{1,0:T(8,128)(2,1)S(1)}, bf16[512,5120]{1,0:T(8,128)(2,1)}, u32[]{:S(2)}) copy-start(bf16[512,5120]{1,0:T(8,128)(2,1)} %hidden_ref.5) | copy-start | bytes 15728644
  56.8 2.5 %copy-start.7 = (bf16[512,5120]{1,0:T(8,128)(2,1)S(1)}, bf16[512,5120]{1,0:T(8,128)(2,1)}, u32[]{:S(2)}) copy-start(bf16[512,5120]{1,0:T(8,128)(2,1)} %hidden_ref.5) | copy-start | bytes 15728644
  64.4 11.4 %copy-start.26 = (s32[16]{0:T(128)S(1)}, s32[16]{0:T(128)}, u32[]{:S(2)}) copy-start(s32[16]{0:T(128)} %constant.48.clone) | copy-start | bytes 196
  64.4 11.4 %copy-start.27 = (s32[16]{0:T(128)S(1)}, s32[16]{0:T(128)}, u32[]{:S(2)}) copy-start(s32[16]{0:T(128)} %constant.49.clone) | copy-start | bytes 196
  64.4 2.4 %collective-permute-start.13 = (bf16[320,1024]{1,0:T(8,128)(2,1)S(1)}, bf16[320,1024]{1,0:T(8,128)(2,1)S(1)}, u32[]{:S(2)}, u32[]{:S(2)}) collective-permute-start(bf16[320,1024]{1,0:T(8,128)(2,1)S(1)} %collective-permute-done.8.refs_0_), channel_id=1, source_target_pairs={{0,1},{1,0},{2,3},{3,2},{4,5},{5,4},{6,7},{7,6},{8,9},{9,8},{10,11... | collective-permute-start | bytes 1966088 | tf_op jit(solution)/shard_map/ppermute | solution.py:522
  65.1 2.7 %collective-permute-start.14 = (bf16[320,1024]{1,0:T(8,128)(2,1)S(1)}, bf16[320,1024]{1,0:T(8,128)(2,1)S(1)}, u32[]{:S(2)}, u32[]{:S(2)}) collective-permute-start(bf16[320,1024]{1,0:T(8,128)(2,1)S(1)} %collective-permute-done.9.refs_2_), channel_id=1, source_target_pairs={{0,1},{1,0},{2,3},{3,2},{4,5},{5,4},{6,7},{7,6},{8,9},{9,8},{10,11... | collective-permute-start | bytes 1966088 | tf_op jit(solution)/shard_map/ppermute | solution.py:522
  75.3 12.6 %collective-permute-start.17 = (bf16[512,1024]{1,0:T(8,128)(2,1)}, bf16[512,1024]{1,0:T(8,128)(2,1)}, u32[]{:S(2)}, u32[]{:S(2)}) collective-permute-start(bf16[512,1024]{1,0:T(8,128)(2,1)} %finish.1.refs_3_), channel_id=1, source_target_pairs={{0,1},{1,0},{2,3},{3,2},{4,5},{5,4},{6,7},{7,6},{8,9},{9,8},{10,11... | collective-permute-start | bytes 3145736 | tf_op jit(solution)/shard_map/ppermute | solution.py:434
  75.8 26.8 %collective-permute-start.15 = (bf16[512,1024]{1,0:T(8,128)(2,1)}, bf16[512,1024]{1,0:T(8,128)(2,1)}, u32[]{:S(2)}, u32[]{:S(2)}) collective-permute-start(bf16[512,1024]{1,0:T(8,128)(2,1)} %finish.1.refs_3_), channel_id=1, source_target_pairs={{0,4},{1,5},{2,6},{3,7},{4,8},{5,9},{6,10},{7,11},{8,12},{9,13},{1... | collective-permute-start | bytes 3145736 | tf_op jit(solution)/shard_map/ppermute | solution.py:438
  75.9 26.7 %collective-permute-start.16 = (bf16[512,1024]{1,0:T(8,128)(2,1)}, bf16[512,1024]{1,0:T(8,128)(2,1)}, u32[]{:S(2)}, u32[]{:S(2)}) collective-permute-start(bf16[512,1024]{1,0:T(8,128)(2,1)} %finish.1.refs_3_), channel_id=1, source_target_pairs={{0,2},{1,3},{2,0},{3,1},{4,6},{5,7},{6,4},{7,5},{8,10},{9,11},{10,... | collective-permute-start | bytes 3145736 | tf_op jit(solution)/shard_map/ppermute | solution.py:438
  83.7 4.3 %copy-start.9 = (s32[512,1]{1,0:T(8,128)S(1)}, s32[512,1]{1,0:T(8,128)}, u32[]{:S(2)}) copy-start(s32[512,1]{1,0:T(8,128)} %reshape.87.refs_0_) | copy-start | bytes 6148
  102.6 3.5 %collective-permute-start.20 = (bf16[512,1024]{1,0:T(8,128)(2,1)}, bf16[512,1024]{1,0:T(8,128)(2,1)S(1)}, u32[]{:S(2)}, u32[]{:S(2)}) collective-permute-start(bf16[512,1024]{1,0:T(8,128)(2,1)} %collective-permute-done.15.refs_3_), channel_id=1, source_target_pairs={{0,1},{1,0},{2,3},{3,2},{4,5},{5,4},{6,7},{7,6},{8,9},{9,8},{10,11... | collective-permute-start | bytes 3145736 | tf_op jit(solution)/shard_map/ppermute | solution.py:434
  103.5 4.0 %collective-permute-start.21 = (bf16[512,1024]{1,0:T(8,128)(2,1)}, bf16[512,1024]{1,0:T(8,128)(2,1)S(1)}, u32[]{:S(2)}, u32[]{:S(2)}) collective-permute-start(bf16[512,1024]{1,0:T(8,128)(2,1)} %collective-permute-done.16.refs_5_), channel_id=1, source_target_pairs={{0,1},{1,0},{2,3},{3,2},{4,5},{5,4},{6,7},{7,6},{8,9},{9,8},{10,11... | collective-permute-start | bytes 3145736 | tf_op jit(solution)/shard_map/ppermute | solution.py:434
  103.6 26.2 %collective-permute-start.18 = (bf16[512,1024]{1,0:T(8,128)(2,1)}, bf16[512,1024]{1,0:T(8,128)(2,1)S(1)}, u32[]{:S(2)}, u32[]{:S(2)}) collective-permute-start(bf16[512,1024]{1,0:T(8,128)(2,1)} %collective-permute-done.15.refs_3_), channel_id=1, source_target_pairs={{0,4},{1,5},{2,6},{3,7},{4,8},{5,9},{6,10},{7,11},{8,12},{9,13},{1... | collective-permute-start | bytes 3145736 | tf_op jit(solution)/shard_map/ppermute | solution.py:438
  103.6 26.2 %collective-permute-start.19 = (bf16[512,1024]{1,0:T(8,128)(2,1)}, bf16[512,1024]{1,0:T(8,128)(2,1)S(1)}, u32[]{:S(2)}, u32[]{:S(2)}) collective-permute-start(bf16[512,1024]{1,0:T(8,128)(2,1)} %collective-permute-done.15.refs_3_), channel_id=1, source_target_pairs={{0,2},{1,3},{2,0},{3,1},{4,6},{5,7},{6,4},{7,5},{8,10},{9,11},{10,... | collective-permute-start | bytes 3145736 | tf_op jit(solution)/shard_map/ppermute | solution.py:438
  129.8 3.6 %collective-permute-start.24 = (bf16[512,1024]{1,0:T(8,128)(2,1)S(1)}, bf16[512,1024]{1,0:T(8,128)(2,1)S(1)}, u32[]{:S(2)}, u32[]{:S(2)}) collective-permute-start(bf16[512,1024]{1,0:T(8,128)(2,1)S(1)} %collective-permute-done.18.refs_3_), channel_id=1, source_target_pairs={{0,1},{1,0},{2,3},{3,2},{4,5},{5,4},{6,7},{7,6},{8,9},{9,8},{10,11... | collective-permute-start | bytes 3145736 | tf_op jit(solution)/shard_map/ppermute | solution.py:434
  131.1 3.8 %collective-permute-start.25 = (bf16[512,1024]{1,0:T(8,128)(2,1)S(1)}, bf16[512,1024]{1,0:T(8,128)(2,1)S(1)}, u32[]{:S(2)}, u32[]{:S(2)}) collective-permute-start(bf16[512,1024]{1,0:T(8,128)(2,1)S(1)} %collective-permute-done.19.refs_5_), channel_id=1, source_target_pairs={{0,1},{1,0},{2,3},{3,2},{4,5},{5,4},{6,7},{7,6},{8,9},{9,8},{10,11... | collective-permute-start | bytes 3145736 | tf_op jit(solution)/shard_map/ppermute | solution.py:434
  131.1 26.0 %collective-permute-start.22 = (bf16[512,1024]{1,0:T(8,128)(2,1)S(1)}, bf16[512,1024]{1,0:T(8,128)(2,1)S(1)}, u32[]{:S(2)}, u32[]{:S(2)}) collective-permute-start(bf16[512,1024]{1,0:T(8,128)(2,1)S(1)} %collective-permute-done.18.refs_3_), channel_id=1, source_target_pairs={{0,4},{1,5},{2,6},{3,7},{4,8},{5,9},{6,10},{7,11},{8,12},{9,13},{1... | collective-permute-start | bytes 3145736 | tf_op jit(solution)/shard_map/ppermute | solution.py:438
  131.1 26.0 %collective-permute-start.23 = (bf16[512,1024]{1,0:T(8,128)(2,1)S(1)}, bf16[512,1024]{1,0:T(8,128)(2,1)S(1)}, u32[]{:S(2)}, u32[]{:S(2)}) collective-permute-start(bf16[512,1024]{1,0:T(8,128)(2,1)S(1)} %collective-permute-done.18.refs_3_), channel_id=1, source_target_pairs={{0,2},{1,3},{2,0},{3,1},{4,6},{5,7},{6,4},{7,5},{8,10},{9,11},{10,... | collective-permute-start | bytes 3145736 | tf_op jit(solution)/shard_map/ppermute | solution.py:438
  157.2 3.6 %collective-permute-start.28 = (bf16[512,1024]{1,0:T(8,128)(2,1)S(1)}, bf16[512,1024]{1,0:T(8,128)(2,1)S(1)}, u32[]{:S(2)}, u32[]{:S(2)}) collective-permute-start(bf16[512,1024]{1,0:T(8,128)(2,1)S(1)} %collective-permute-done.22.refs_3_), channel_id=1, source_target_pairs={{0,1},{1,0},{2,3},{3,2},{4,5},{5,4},{6,7},{7,6},{8,9},{9,8},{10,11... | collective-permute-start | bytes 3145736 | tf_op jit(solution)/shard_map/ppermute | solution.py:434
  158.5 3.8 %collective-permute-start.29 = (bf16[512,1024]{1,0:T(8,128)(2,1)S(1)}, bf16[512,1024]{1,0:T(8,128)(2,1)S(1)}, u32[]{:S(2)}, u32[]{:S(2)}) collective-permute-start(bf16[512,1024]{1,0:T(8,128)(2,1)S(1)} %collective-permute-done.23.refs_5_), channel_id=1, source_target_pairs={{0,1},{1,0},{2,3},{3,2},{4,5},{5,4},{6,7},{7,6},{8,9},{9,8},{10,11... | collective-permute-start | bytes 3145736 | tf_op jit(solution)/shard_map/ppermute | solution.py:434
  158.6 26.5 %collective-permute-start.26 = (bf16[256,1024]{1,0:T(8,128)(2,1)S(1)}, bf16[256,1024]{1,0:T(8,128)(2,1)}, u32[]{:S(2)}, u32[]{:S(2)}) collective-permute-start(bf16[256,1024]{1,0:T(8,128)(2,1)S(1)} %slice.26), channel_id=1, source_target_pairs={{0,2},{1,3},{2,0},{3,1},{4,6},{5,7},{6,4},{7,5},{8,10},{9,11},{10,... | collective-permute-start | bytes 1572872 | tf_op jit(solution)/shard_map/ppermute | solution.py:445
  159.6 25.5 %collective-permute-start.27 = (bf16[256,1024]{1,0:T(8,128)(2,1)S(1)}, bf16[256,1024]{1,0:T(8,128)(2,1)}, u32[]{:S(2)}, u32[]{:S(2)}) collective-permute-start(bf16[256,1024]{1,0:T(8,128)(2,1)S(1)} %slice.27), channel_id=1, source_target_pairs={{0,4},{1,5},{2,6},{3,7},{4,8},{5,9},{6,10},{7,11},{8,12},{9,13},{1... | collective-permute-start | bytes 1572872 | tf_op jit(solution)/shard_map/ppermute | solution.py:446
  176.8 2.8 %copy-start = (f32[4,3328,128]{2,1,0:T(8,128)}, f32[4,3328,128]{2,1,0:T(8,128)S(1)}, u32[]{:S(2)}) copy-start(f32[4,3328,128]{2,1,0:T(8,128)S(1)} %get-tuple-element.134.refs_7_) | copy-start | bytes 20447236
  179.5 2.9 %copy-start.2 = (f32[4,3328,128]{2,1,0:T(8,128)}, f32[4,3328,128]{2,1,0:T(8,128)S(1)}, u32[]{:S(2)}) copy-start(f32[4,3328,128]{2,1,0:T(8,128)S(1)} %get-tuple-element.135.refs_8_) | copy-start | bytes 20447236
  182.4 2.7 %copy-start.4 = (f32[4,3328,128]{2,1,0:T(8,128)}, f32[4,3328,128]{2,1,0:T(8,128)S(1)}, u32[]{:S(2)}) copy-start(f32[4,3328,128]{2,1,0:T(8,128)S(1)} %get-tuple-element.136.refs_9_) | copy-start | bytes 20447236
  185.1 2.3 %collective-permute-start.30 = (bf16[256,1024]{1,0:T(8,128)(2,1)}, bf16[256,1024]{1,0:T(8,128)(2,1)}, u32[]{:S(2)}, u32[]{:S(2)}) collective-permute-start(bf16[256,1024]{1,0:T(8,128)(2,1)} %collective-permute-done.26.refs_3_), channel_id=1, source_target_pairs={{0,1},{1,0},{2,3},{3,2},{4,5},{5,4},{6,7},{7,6},{8,9},{9,8},{10,11... | collective-permute-start | bytes 1572872 | tf_op jit(solution)/shard_map/ppermute | solution.py:434
  185.5 2.6 %collective-permute-start.31 = (bf16[256,1024]{1,0:T(8,128)(2,1)}, bf16[256,1024]{1,0:T(8,128)(2,1)}, u32[]{:S(2)}, u32[]{:S(2)}) collective-permute-start(bf16[256,1024]{1,0:T(8,128)(2,1)} %collective-permute-done.27.refs_4_), channel_id=1, source_target_pairs={{0,1},{1,0},{2,3},{3,2},{4,5},{5,4},{6,7},{7,6},{8,9},{9,8},{10,11... | collective-permute-start | bytes 1572872 | tf_op jit(solution)/shard_map/ppermute | solution.py:434
  188.1 2.9 %copy-start.1 = (f32[4,3328,128]{2,1,0:T(8,128)S(1)}, f32[4,3328,128]{2,1,0:T(8,128)}, u32[]{:S(2)}) copy-start(f32[4,3328,128]{2,1,0:T(8,128)} %copy-done) | copy-start | bytes 20447236
  191.1 2.9 %copy-start.3 = (f32[4,3328,128]{2,1,0:T(8,128)S(1)}, f32[4,3328,128]{2,1,0:T(8,128)}, u32[]{:S(2)}) copy-start(f32[4,3328,128]{2,1,0:T(8,128)} %copy-done.2) | copy-start | bytes 20447236
  194.0 2.9 %copy-start.5 = (f32[4,3328,128]{2,1,0:T(8,128)S(1)}, f32[4,3328,128]{2,1,0:T(8,128)}, u32[]{:S(2)}) copy-start(f32[4,3328,128]{2,1,0:T(8,128)} %copy-done.4) | copy-start | bytes 20447236
  (13 other events, 14.1 us)

commit v11 on v10

--- a/solution.py
+++ b/solution.py
@@ -112,9 +112,9 @@
 
 
 def query_kernel(
-    ranks, row_step, stride, packed, route_ref, seat_ref, positions_ref, frequency_ref, queries_ref, *refs
+    ranks, spare, stride, packed, route_ref, seat_ref, positions_ref, frequency_ref, queries_ref, *refs
 ):
-    turned_ref, bounds_ref, cosine_ref, sine_ref, rows_ref = refs
+    turned_ref, bounds_ref, cosine_ref, sine_ref, column_ref, rows_ref = refs
     route = route_ref[...]
     count = route.shape[0]
     lines = positions_ref.shape[0]
@@ -136,6 +136,12 @@
     cosine_ref[...] = cosine
     sine_ref[...] = sine
     seats = one_hot_rows(ranks * stride, seat_ref[...])
+    seat_line, seat_lane = split(seat_ref[...])
+    digit = lax.broadcasted_iota(jnp.int32, (8, count), 0)
+    digits = jnp.where(digit == 0, seat_line, jnp.where(digit == 1, seat_lane, 0))
+    same = one_hot_rows(count, lax.broadcasted_iota(jnp.int32, (1, count), 1))
+    column = contract(same, digits.astype(jnp.float32).astype(jnp.bfloat16), 1, 1)
+    column_ref[...] = (column[:, 0:1] * HEAD_SIZE + column[:, 1:2]).astype(jnp.int32)
     first = route - spot.astype(jnp.int32)
     first_line, first_lane = split(first)
     digits = jnp.where(lanes == 0, line, 0)
@@ -156,8 +162,8 @@
             one = queries_ref[:, at : at + HEAD_SIZE].astype(jnp.float32)
             rows = contract(seats, turn(one, cosine, sine), 1, 0)
             for group in range(ranks):
-                at = group * packed + place * row_step
-                rows_ref[at : at + row_step] = rows[group * stride : group * stride + row_step]
+                at = group * packed + place * spare
+                rows_ref[at : at + spare] = rows[group * stride : group * stride + spare]
         turned_ref[head] = rows_ref[...].astype(jnp.bfloat16)
 
 
@@ -258,7 +264,7 @@
     lax.fori_loop(0, routes_ref.shape[0], one_group, 0)
 
 
-def attend_kernel(starts, before, spare, row_step, stride, more, last, *refs):
+def attend_kernel(starts, before, spare, stride, more, last, *refs):
     more_ref, queries_ref, veil_ref = refs[:3]
     refs = refs[3:]
     blocks = []
@@ -287,7 +293,7 @@
     lane = lax.broadcasted_iota(jnp.int32, (packed, HEAD_SIZE), 1)
     own = lane < 0
     for at in range(HEAD_GROUPS):
-        own = own | ((token == lane + at * row_step) & (lane < spare))
+        own = own | ((token == lane + at * spare) & (lane < spare))
     seen_by[...] = own.astype(jnp.float32).astype(jnp.bfloat16)
     lines = lax.broadcasted_iota(jnp.int32, (share, count), 1)
     for at, block in enumerate(blocks):
@@ -325,10 +331,10 @@
 
     def finish_head(group, head, total, weight_sum):
         mixed = total / weight_sum
-        seats = pl.ds(pl.multiple_of(group * stride, 16), row_step)
+        seats = pl.ds(pl.multiple_of(group * stride, 16), spare)
         for at in range(HEAD_GROUPS):
             place = (head * HEAD_GROUPS + at) * HEAD_SIZE
-            rows = mixed[at * row_step : (at + 1) * row_step]
+            rows = mixed[at * spare : (at + 1) * spare]
             mixed_ref[seats, place : place + HEAD_SIZE] = rows.astype(jnp.bfloat16)
 
     def add_heads(group, row, some):
@@ -491,8 +497,7 @@
     spare = share + extra
     listed = ranks * extra
     stride = -(-spare // 16) * 16
-    row_step = -(-spare // 8) * 8
-    packed = -(-HEAD_GROUPS * row_step // 16) * 16
+    packed = -(-HEAD_GROUPS * spare // 16) * 16
     query_width = queries.shape[1]
     shape = jax.ShapeDtypeStruct
 
@@ -506,7 +511,7 @@
         in_specs=[HBM] * 2,
         out_specs=VMEM,
         scratch_shapes=[pltpu.SemaphoreType.DMA((2,))],
-        compiler_params=grant(14),
+        compiler_params=grant(56),
         name="join",
     )(key_matrix, value_matrix)
     every = [(group, rank) for group in range(2) for rank in range(ranks)]
@@ -559,16 +564,17 @@
 
     half = HEAD_SIZE // 2
     frequency = 1000000.0 ** (-(jnp.arange(half, dtype=jnp.float32) * 2.0 / HEAD_SIZE))
-    turned, bounds, cosine, sine = pl.pallas_call(
-        functools.partial(query_kernel, ranks, row_step, stride, packed),
+    turned, bounds, cosine, sine, seat_column = pl.pallas_call(
+        functools.partial(query_kernel, ranks, spare, stride, packed),
         out_shape=(
             shape((KEY_VALUE_HEADS, ranks * packed, HEAD_SIZE), jnp.bfloat16),
             shape((ranks * stride, HEAD_SIZE), jnp.int32),
             shape((rows, HEAD_SIZE), jnp.float32),
             shape((rows, HEAD_SIZE), jnp.float32),
+            shape((rows, 1), jnp.int32),
         ),
         in_specs=[VMEM] * 5,
-        out_specs=(VMEM,) * 4,
+        out_specs=(VMEM,) * 5,
         scratch_shapes=[pltpu.VMEM((ranks * packed, HEAD_SIZE), jnp.float32)],
         compiler_params=grant(14),
         cost_estimate=cost(4 * stride * ranks * rows * query_width, 4 * rows * query_width),
@@ -614,15 +620,11 @@
 
     bias = jnp.concatenate([key_projection_bias, value_projection_bias])
     bias = bias.astype(jnp.float32).reshape(1, -1)
-    seat = seat.reshape(rows, 1)
-    far_lane, next_lane, near_other, swaps, turned, bounds, cosine, sine, bias, owners, seat = (
-        lax.optimization_barrier(
-            (
-                far_lane, next_lane, near_other, swaps,
-                turned, bounds, cosine, sine, bias, owners, seat,
-            )
-        )
-    )
+    step = (far_lane, next_lane, near_other, swaps)
+    step, turned, bounds, cosine, sine, seat_column, bias, owners = lax.optimization_barrier(
+        (step, turned, bounds, cosine, sine, seat_column, bias, owners)
+    )
+    far_lane, next_lane, near_other, swaps = step
     matrices[1], matrices[2] = (near_lane, swaps[0]), (other_row, swaps[1])
     next_other, far_other = send(next_lane, across), send(near_other, swap)
     matrices[3] = (far_lane, send(far_lane, beside))
@@ -696,7 +698,7 @@
             pltpu.SemaphoreType.DMA,
         ]
         if last:
-            fixed.append(seat)
+            fixed.append(seat_column)
             in_specs.append(VMEM)
             outs.insert(0, shape((rows, query_width), jnp.bfloat16))
             out_specs.insert(0, HBM)
@@ -711,7 +713,6 @@
                 starts,
                 sum(len(one) for one in sets[:index]),
                 spare,
-                row_step,
                 stride,
                 bool(state),
                 last,

time: 225 us -> 205 us (0.911)
  local copies, waits for them, and re-layouts: 44.2 us -> 12.1 us
  waiting for transfers between devices: 44.7 us -> 56.4 us
  starting transfers between devices: 25.7 us -> 28.8 us
    unnamed x57 -> x25, local copies, waits for them, and re-layouts: 33.8 us -> 6.21 us
    ppermute x3, waiting for transfers between devices: 0.01 us -> 19.9 us  [spread(): lax.ppermute(lane, 'dp', across)]
    ppermute x3, waiting for transfers between devices: 18.3 us -> 7.22 us  [spread(): lax.ppermute(lane, 'dp', ring)]
    pallas_call x5, Pallas kernels: 79.4 us -> 74.6 us  [attend(): pl.pallas_call(functools.partial(attend_kernel, starts, sum((len(one) for...]
    ppermute x15, starting transfers between devices: 12.9 us -> 15.6 us  [send(): return lax.ppermute(array, ('groups', 'dp'), pairs)]
  transfers between devices with their start and end apart: 33 -> 33, of which waited for: 16 -> 18; matrix products, arithmetic and copies ran while one was open for 5% -> 3% of each run, Pallas kernels for 34% -> 36%
where the time goes in v11:
time: 205 us
  Pallas kernels  106 us (52%)
  waiting for transfers between devices  56.4 us (28%)
  starting transfers between devices  28.8 us (14%)
  local copies, waits for them, and re-layouts  12.1 us (6%)
    pallas_call x5, Pallas kernels, attend(): pl.pallas_call(functools.partial(attend_kernel, starts, sum((len(one) for...  74.6 us
    ppermute x3, waiting for transfers between devices, spread(): lax.ppermute(lane, 'dp', across)  19.9 us
    ppermute x15, starting transfers between devices, send(): return lax.ppermute(array, ('groups', 'dp'), pairs)  15.6 us
    ppermute x9, waiting for transfers between devices, keep(): lax.ppermute(array, 'dp', beside)  11.9 us
    pallas_call x2, Pallas kernels, add_part(): pl.pallas_call(functools.partial(part_kernel, chips, bool(more)), out_sha...  10.8 us
    all_to_all x1, waiting for transfers between devices, gather_plan(): lax.all_to_all(jnp.broadcast_to(plan, (ranks, width + slots)), 'dp', spli...  10.6 us
    pallas_call x1, Pallas kernels, gather_plan(): pl.pallas_call(functools.partial(finish_kernel, chips), out_shape=tuple((...  7.57 us
    ppermute x3, waiting for transfers between devices, spread(): lax.ppermute(lane, 'dp', ring)  7.22 us
  transfers between devices with their start and end apart: 33, of which 18 were waited for; matrix products, arithmetic and copies ran while one was open for 3% of the time, Pallas kernels for 36%

profile of v11, /device:TPU:1, one launch (start us, length us, event | category | flops | bytes accessed | tf_op | source)
XLA Modules:
  0.0 204.6 jit_solution(15164496485522019630)
XLA Ops:
  0.0 1.9 join.1.refs_0_
  2.1 2.7 %collective-permute-start.1 = (bf16[320,1024]{1,0:T(8,128)(2,1)}, bf16[320,1024]{1,0:T(8,128)(2,1)S(1)}, u32[]{:S(2)}, u32[]{:S(2)}) collective-permute-start(bf16[320,1024]{1,0:T(8,128)(2,1)} %join.1.refs_0_), channel_id=1, source_target_pairs={{0,2},{1,3},{2,0},{3,1},{4,6},{5,7},{6,4},{7,5},{8,10},{9,11},{10,... | collective-permute-start | bytes 1966088 | tf_op jit(solution)/shard_map/ppermute | solution.py:527
  4.8 1.3 collective-permute-start
  7.5 0.8 concatenate.20
  8.9 4.5 %all-to-all-start = ((s32[16,1,1600]{2,1,0:T(1,128)}), s32[16,1,1600]{2,1,0:T(1,128)S(1)}, u32[]{:S(2)}, u32[]{:S(2)}) async-start(s32[16,1,1600]{2,1,0:T(1,128)} %broadcast_in_dim.6), calls=%async_computation | async-start | bytes 212992 | tf_op jit(solution)/shard_map/all_to_all | solution.py:546
  14.8 10.6 %all-to-all-done = s32[16,1,1600]{2,1,0:T(1,128)S(1)} async-done(((s32[16,1,1600]{2,1,0:T(1,128)}), s32[16,1,1600]{2,1,0:T(1,128)S(1)}, u32[]{:S(2)}, u32[]{:S(2)}) %all-to-all-start) | async-done | bytes 102432 | tf_op jit(solution)/shard_map/all_to_all | solution.py:546
  26.0 1.3 collective-permute-start.5
  27.9 4.1 %collective-permute-start.3 = (bf16[320,1024]{1,0:T(8,128)(2,1)S(1)}, bf16[320,1024]{1,0:T(8,128)(2,1)}, u32[]{:S(2)}, u32[]{:S(2)}) collective-permute-start(bf16[320,1024]{1,0:T(8,128)(2,1)S(1)} %collective-permute-done.refs_2_), channel_id=1, source_target_pairs={{0,16},{1,17},{2,18},{3,19},{4,20},{5,21},{6,22},{7,23},{8,24},{9,... | collective-permute-start | bytes 1966088 | tf_op jit(solution)/shard_map/ppermute | solution.py:527
  32.0 1.0 collective-permute-start.7
  33.0 1.5 copy.34.route_ref
  35.4 1.0 copy-done.3
  36.4 1.7 copy-done.5
  38.1 7.0 %turn_queries.1 = (bf16[4,2816,128]{2,1,0:T(8,128)(2,1)S(1)}, s32[768,128]{1,0:T(8,128)S(1)}, f32[512,128]{1,0:T(8,128)S(1)}, f32[512,128]{1,0:T(8,128)S(1)}, s32[512,1]{1,0:T(8,128)S(1)}) custom-call(s32[512,1]{1,0:T(8,128)S(1)} %copy-done.3, s32[1,512]{1,0:T(1,128)S(1)} %get-tuple-element.80.seat_ref, s32[128,128]{1,0:T(8,128)S(1)} %reshape.69.positions_ref, ...), custom_call_target="tpu_custom_call" | custom-call | flops 4026531840 | bytes 5242880 | tf_op jit(solution)/shard_map/turn_queries/pallas_call | solution.py:567
  45.2 1.5 copy-done
  46.8 1.0 collective-permute-start.10
  48.4 1.5 collective-permute-start.9
  49.9 5.6 %add_part.2.refs_6_ = f32[512,1024]{1,0:T(8,128)S(1)} custom-call(s32[16]{0:T(128)S(1)} %fusion.7.owners_ref, bf16[512,5120]{1,0:T(8,128)(2,1)S(1)} %bitcast.12, bf16[320,1024]{1,0:T(8,128)(2,1)S(1)} %copy-done.2, bf16[320,1024]{1,0:T(8,128)(2,1)S(1)} %collective-permute-done.2.refs_1_, bf16[320,1024]{1,0:T(8,128)(2,1)S(1)} %collective-permute-done.refs_2_, ...), custom_call_target="tpu_custom_call" | custom-call | flops 2013265920 | bytes 10092544 | tf_op jit(solution)/shard_map/add_part/pallas_call | solution.py:610
  55.6 5.1 %add_part.3.refs_4_ = f32[512,1024]{1,0:T(8,128)S(1)} custom-call(s32[16]{0:T(128)S(1)} %fusion.7.owners_ref, bf16[512,5120]{1,0:T(8,128)(2,1)S(1)} %bitcast.12, bf16[320,1024]{1,0:T(8,128)(2,1)} %collective-permute-done.3.refs_0_, bf16[320,1024]{1,0:T(8,128)(2,1)S(1)} %collective-permute-done.10.refs_1_, bf16[320,1024]{1,0:T(8,128)(2,1)} %collective-permute-done.4.refs_2_, ...), custom_call_target="tpu_custom_call" | custom-call | flops 2013265920 | bytes 10092544 | tf_op jit(solution)/shard_map/add_part/pallas_call | solution.py:610
  60.7 4.1 %collective-permute-done.8.refs_0_ = bf16[320,1024]{1,0:T(8,128)(2,1)S(1)} collective-permute-done((bf16[320,1024]{1,0:T(8,128)(2,1)}, bf16[320,1024]{1,0:T(8,128)(2,1)S(1)}, u32[]{:S(2)}, u32[]{:S(2)}) %collective-permute-start.8) | collective-permute-done | bytes 655392 | tf_op jit(solution)/shard_map/ppermute | solution.py:527
  64.8 0.9 collective-permute-start.13
  65.8 1.7 collective-permute-done.13.refs_1_
  67.5 0.9 collective-permute-done.14.refs_3_
  68.4 7.6 %finish.1.refs_3_ = bf16[512,1024]{1,0:T(8,128)(2,1)} custom-call(s32[16]{0:T(128)S(1)} %fusion.7.owners_ref, bf16[512,5120]{1,0:T(8,128)(2,1)S(1)} %bitcast.12, f32[1,1024]{1,0:T(1,128)S(1)} %maximum_convert_fusion.bias_ref, f32[512,128]{1,0:T(8,128)S(1)} %get-tuple-element.91.cosine_ref, f32[512,128]{1,0:T(8,128)S(1)} %get-tuple-element.92.sine_ref, ...), custom_call_target="tpu_custom_call" | custom-call | flops 1342177280 | bytes 8126464 | tf_op jit(solution)/shard_map/finish/pallas_call | solution.py:638
  76.4 1.3 collective-permute-start.16
  79.1 1.2 copy-done.7
  80.3 3.5 %veil.1 = (bf16[16,128,128]{2,1,0:T(8,128)(2,1)S(1)}, bf16[16,256,128]{2,1,0:T(8,128)(2,1)S(1)}, bf16[16,256,128]{2,1,0:T(8,128)(2,1)S(1)}, bf16[16,256,128]{2,1,0:T(8,128)(2,1)S(1)}, bf16[16,128,128]{2,1,0:T(8,128)(2,1)S(1)}) custom-call(s32[768,128]{1,0:T(8,128)S(1)} %copy-done.7, s32[16,1,512]{2,1,0:T(1,128)S(1)} %reshape.72.routes_ref, ...), custom_call_target="tpu_custom_call" | custom-call | flops 3000000000 | bytes 4194304 | tf_op jit(solution)/shard_map/veil/pallas_call | solution.py:667
  83.8 9.9 %attend.5 = (f32[4,2816,128]{2,1,0:T(8,128)S(1)}, f32[4,2816,128]{2,1,0:T(8,128)S(1)}, f32[4,2816,128]{2,1,0:T(8,128)S(1)}) custom-call(s32[512,1]{1,0:T(8,128)S(1)} %reshape.83.refs_0_, bf16[4,2816,128]{2,1,0:T(8,128)(2,1)S(1)} %copy-done.1, bf16[16,128,128]{2,1,0:T(8,128)(2,1)S(1)} %get-tuple-element.103.refs_2_, bf16[512,1024]{1,0:T(8,128)(2,1)} %finish.1.refs_3_, ...), custom_call_target="tpu_custom_call" | custom-call | flops 4429185024 | bytes 16777216 | tf_op jit(solution)/shard_map/attend/pallas_call | solution.py:710
  93.7 7.7 %collective-permute-done.16.refs_5_ = bf16[512,1024]{1,0:T(8,128)(2,1)} collective-permute-done((bf16[512,1024]{1,0:T(8,128)(2,1)}, bf16[512,1024]{1,0:T(8,128)(2,1)}, u32[]{:S(2)}, u32[]{:S(2)}) %collective-permute-start.16) | collective-permute-done | bytes 1048608 | tf_op jit(solution)/shard_map/ppermute | solution.py:444
  101.4 2.8 %collective-permute-done.15.refs_3_ = bf16[512,1024]{1,0:T(8,128)(2,1)} collective-permute-done((bf16[512,1024]{1,0:T(8,128)(2,1)}, bf16[512,1024]{1,0:T(8,128)(2,1)}, u32[]{:S(2)}, u32[]{:S(2)}) %collective-permute-start.15) | collective-permute-done | bytes 1048608 | tf_op jit(solution)/shard_map/ppermute | solution.py:444
  104.2 1.3 collective-permute-start.21
  105.6 2.3 %collective-permute-done.21.refs_6_ = bf16[512,1024]{1,0:T(8,128)(2,1)S(1)} collective-permute-done((bf16[512,1024]{1,0:T(8,128)(2,1)}, bf16[512,1024]{1,0:T(8,128)(2,1)S(1)}, u32[]{:S(2)}, u32[]{:S(2)}) %collective-permute-start.21) | collective-permute-done | bytes 1048608 | tf_op jit(solution)/shard_map/ppermute | solution.py:440
  108.0 1.5 collective-permute-done.20.refs_4_
  109.5 15.1 %attend.6 = (f32[4,2816,128]{2,1,0:T(8,128)S(1)}, f32[4,2816,128]{2,1,0:T(8,128)S(1)}, f32[4,2816,128]{2,1,0:T(8,128)S(1)}) custom-call(s32[512,1]{1,0:T(8,128)S(1)} %reshape.83.refs_0_, bf16[4,2816,128]{2,1,0:T(8,128)(2,1)S(1)} %copy-done.1, ...), custom_call_target="tpu_custom_call", output_to_operand_aliasing={{0}: (7, {}), {1}: (8, {}), {2}: (9, {})} | custom-call | flops 5905580032 | bytes 33554432 | tf_op jit(solution)/shard_map/attend/pallas_call | solution.py:710
  124.5 5.3 %collective-permute-done.19.refs_5_ = bf16[512,1024]{1,0:T(8,128)(2,1)S(1)} collective-permute-done((bf16[512,1024]{1,0:T(8,128)(2,1)}, bf16[512,1024]{1,0:T(8,128)(2,1)S(1)}, u32[]{:S(2)}, u32[]{:S(2)}) %collective-permute-start.19) | collective-permute-done | bytes 1048608 | tf_op jit(solution)/shard_map/ppermute | solution.py:444
  129.9 1.6 collective-permute-done.18.refs_3_
  131.5 1.7 collective-permute-start.25
  133.2 1.3 collective-permute-start.23
  134.5 1.0 collective-permute-done.25.refs_6_
  135.5 1.5 collective-permute-done.24.refs_4_
  137.0 13.5 %attend.7 = (f32[4,2816,128]{2,1,0:T(8,128)S(1)}, f32[4,2816,128]{2,1,0:T(8,128)S(1)}, f32[4,2816,128]{2,1,0:T(8,128)S(1)}) custom-call(s32[512,1]{1,0:T(8,128)S(1)} %reshape.83.refs_0_, bf16[4,2816,128]{2,1,0:T(8,128)(2,1)S(1)} %copy-done.1, ...), custom_call_target="tpu_custom_call", output_to_operand_aliasing={{0}: (7, {}), {1}: (8, {}), {2}: (9, {})} | custom-call | flops 5905580032 | bytes 33554432 | tf_op jit(solution)/shard_map/attend/pallas_call | solution.py:710
  150.5 6.9 %collective-permute-done.23.refs_5_ = bf16[512,1024]{1,0:T(8,128)(2,1)S(1)} collective-permute-done((bf16[512,1024]{1,0:T(8,128)(2,1)S(1)}, bf16[512,1024]{1,0:T(8,128)(2,1)S(1)}, u32[]{:S(2)}, u32[]{:S(2)}) %collective-permute-start.23) | collective-permute-done | bytes 1048608 | tf_op jit(solution)/shard_map/ppermute | solution.py:444
  157.4 2.8 %collective-permute-done.22.refs_3_ = bf16[512,1024]{1,0:T(8,128)(2,1)S(1)} collective-permute-done((bf16[512,1024]{1,0:T(8,128)(2,1)S(1)}, bf16[512,1024]{1,0:T(8,128)(2,1)S(1)}, u32[]{:S(2)}, u32[]{:S(2)}) %collective-permute-start.22) | collective-permute-done | bytes 1048608 | tf_op jit(solution)/shard_map/ppermute | solution.py:444
  160.2 1.7 collective-permute-start.28
  162.3 1.9 collective-permute-done.28.refs_4_
  164.2 1.5 collective-permute-done.29.refs_6_
  165.7 13.5 %attend.8 = (f32[4,2816,128]{2,1,0:T(8,128)S(1)}, f32[4,2816,128]{2,1,0:T(8,128)S(1)}, f32[4,2816,128]{2,1,0:T(8,128)S(1)}) custom-call(s32[512,1]{1,0:T(8,128)S(1)} %reshape.83.refs_0_, bf16[4,2816,128]{2,1,0:T(8,128)(2,1)S(1)} %copy-done.1, ...), custom_call_target="tpu_custom_call", output_to_operand_aliasing={{0}: (7, {}), {1}: (8, {}), {2}: (9, {})} | custom-call | flops 5905580032 | bytes 33554432 | tf_op jit(solution)/shard_map/attend/pallas_call | solution.py:710
  179.8 1.4 collective-permute-done.30.refs_5_
  182.0 22.5 %attend.9 = (bf16[512,2560]{1,0:T(8,128)(2,1)}, f32[4,2816,128]{2,1,0:T(8,128)S(1)}, f32[4,2816,128]{2,1,0:T(8,128)S(1)}, f32[4,2816,128]{2,1,0:T(8,128)S(1)}) custom-call(s32[512,1]{1,0:T(8,128)S(1)} %reshape.83.refs_0_, bf16[4,2816,128]{2,1,0:T(8,128)(2,1)S(1)} %copy-done.1, ...), custom_call_target="tpu_custom_call", output_to_operand_aliasing={{1}: (7, {}), {2}: (8, {}), {3}: (9, {})} | custom-call | flops 4429185024 | bytes 16777216 | tf_op jit(solution)/shard_map/attend/pallas_call | solution.py:710
  (81 shorter events, 9.8 us)
Async XLA Ops:
  1.9 23.5 %collective-permute-start.2 = (bf16[320,1024]{1,0:T(8,128)(2,1)}, bf16[320,1024]{1,0:T(8,128)(2,1)S(1)}, u32[]{:S(2)}, u32[]{:S(2)}) collective-permute-start(bf16[320,1024]{1,0:T(8,128)(2,1)} %join.1.refs_0_), channel_id=1, source_target_pairs={{0,1},{1,0},{2,3},{3,2},{4,5},{5,4},{6,7},{7,6},{8,9},{9,8},{10,11... | collective-permute-start | bytes 1966088 | tf_op jit(solution)/shard_map/ppermute | solution.py:527
  2.1 23.4 %collective-permute-start.1 = (bf16[320,1024]{1,0:T(8,128)(2,1)}, bf16[320,1024]{1,0:T(8,128)(2,1)S(1)}, u32[]{:S(2)}, u32[]{:S(2)}) collective-permute-start(bf16[320,1024]{1,0:T(8,128)(2,1)} %join.1.refs_0_), channel_id=1, source_target_pairs={{0,2},{1,3},{2,0},{3,1},{4,6},{5,7},{6,4},{7,5},{8,10},{9,11},{10,... | collective-permute-start | bytes 1966088 | tf_op jit(solution)/shard_map/ppermute | solution.py:527
  4.8 20.7 %collective-permute-start = (bf16[320,1024]{1,0:T(8,128)(2,1)}, bf16[320,1024]{1,0:T(8,128)(2,1)S(1)}, u32[]{:S(2)}, u32[]{:S(2)}) collective-permute-start(bf16[320,1024]{1,0:T(8,128)(2,1)} %join.1.refs_0_), channel_id=1, source_target_pairs={{0,4},{1,5},{2,6},{3,7},{4,8},{5,9},{6,10},{7,11},{8,12},{9,13},{1... | collective-permute-start | bytes 1966088 | tf_op jit(solution)/shard_map/ppermute | solution.py:527
  6.1 0.7 copy-start.4
  8.9 16.5 %all-to-all-start = ((s32[16,1,1600]{2,1,0:T(1,128)}), s32[16,1,1600]{2,1,0:T(1,128)S(1)}, u32[]{:S(2)}, u32[]{:S(2)}) async-start(s32[16,1,1600]{2,1,0:T(1,128)} %broadcast_in_dim.6), calls=%async_computation | async-start | bytes 212992 | tf_op jit(solution)/shard_map/all_to_all | solution.py:546
  25.5 21.2 %collective-permute-start.6 = (bf16[320,1024]{1,0:T(8,128)(2,1)S(1)}, bf16[320,1024]{1,0:T(8,128)(2,1)}, u32[]{:S(2)}, u32[]{:S(2)}) collective-permute-start(bf16[320,1024]{1,0:T(8,128)(2,1)S(1)} %collective-permute-done.refs_2_), channel_id=1, source_target_pairs={{0,1},{1,0},{2,3},{3,2},{4,5},{5,4},{6,7},{7,6},{8,9},{9,8},{10,11... | collective-permute-start | bytes 1966088 | tf_op jit(solution)/shard_map/ppermute | solution.py:527
  26.0 20.8 %collective-permute-start.5 = (bf16[320,1024]{1,0:T(8,128)(2,1)S(1)}, bf16[320,1024]{1,0:T(8,128)(2,1)}, u32[]{:S(2)}, u32[]{:S(2)}) collective-permute-start(bf16[320,1024]{1,0:T(8,128)(2,1)S(1)} %collective-permute-done.refs_2_), channel_id=1, source_target_pairs={{0,2},{1,3},{2,0},{3,1},{4,6},{5,7},{6,4},{7,5},{8,10},{9,11},{10,... | collective-permute-start | bytes 1966088 | tf_op jit(solution)/shard_map/ppermute | solution.py:527
  27.3 19.5 %collective-permute-start.4 = (bf16[320,1024]{1,0:T(8,128)(2,1)S(1)}, bf16[320,1024]{1,0:T(8,128)(2,1)}, u32[]{:S(2)}, u32[]{:S(2)}) collective-permute-start(bf16[320,1024]{1,0:T(8,128)(2,1)S(1)} %collective-permute-done.refs_2_), channel_id=1, source_target_pairs={{0,4},{1,5},{2,6},{3,7},{4,8},{5,9},{6,10},{7,11},{8,12},{9,13},{1... | collective-permute-start | bytes 1966088 | tf_op jit(solution)/shard_map/ppermute | solution.py:527
  27.9 18.9 %collective-permute-start.3 = (bf16[320,1024]{1,0:T(8,128)(2,1)S(1)}, bf16[320,1024]{1,0:T(8,128)(2,1)}, u32[]{:S(2)}, u32[]{:S(2)}) collective-permute-start(bf16[320,1024]{1,0:T(8,128)(2,1)S(1)} %collective-permute-done.refs_2_), channel_id=1, source_target_pairs={{0,16},{1,17},{2,18},{3,19},{4,20},{5,21},{6,22},{7,23},{8,24},{9,... | collective-permute-start | bytes 1966088 | tf_op jit(solution)/shard_map/ppermute | solution.py:527
  32.0 14.8 %collective-permute-start.7 = (bf16[320,1024]{1,0:T(8,128)(2,1)S(1)}, bf16[320,1024]{1,0:T(8,128)(2,1)}, u32[]{:S(2)}, u32[]{:S(2)}) collective-permute-start(bf16[320,1024]{1,0:T(8,128)(2,1)S(1)} %collective-permute-done.1.refs_4_), channel_id=1, source_target_pairs={{0,1},{1,0},{2,3},{3,2},{4,5},{5,4},{6,7},{7,6},{8,9},{9,8},{10,11... | collective-permute-start | bytes 1966088 | tf_op jit(solution)/shard_map/ppermute | solution.py:527
  35.3 14.6 %slice-start = ((s8[5242880]{0:T(1024)(128)(4,1)}), s8[1048576]{0:T(1024)(128)(4,1)S(1)}, s32[]{:S(2)}) async-start(s8[5242880]{0:T(1024)(128)(4,1)} %bitcast.11), calls=%async_computation.1 | async-start | bytes 2097152
  35.4 1.0 copy-start.3
  36.4 1.7 copy-start.5
  38.1 11.8 %slice-start.1 = ((s8[5242880]{0:T(1024)(128)(4,1)}), s8[4194304]{0:T(1024)(128)(4,1)S(1)}, s32[]{:S(2)}) async-start(s8[5242880]{0:T(1024)(128)(4,1)} %bitcast.11), calls=%async_computation.2 | async-start | bytes 8388608
  38.1 11.8 %copy-start.2 = (bf16[320,1024]{1,0:T(8,128)(2,1)S(1)}, bf16[320,1024]{1,0:T(8,128)(2,1)}, u32[]{:S(2)}) copy-start(bf16[320,1024]{1,0:T(8,128)(2,1)} %join.1.refs_0_) | copy-start | bytes 1966084
  45.2 1.6 copy-start
  46.7 8.8 %copy-start.6 = (s32[768,128]{1,0:T(8,128)}, s32[768,128]{1,0:T(8,128)S(1)}, u32[]{:S(2)}) copy-start(s32[768,128]{1,0:T(8,128)S(1)} %get-tuple-element.87.bounds_ref) | copy-start | bytes 1179652
  46.8 8.8 %collective-permute-start.10 = (bf16[320,1024]{1,0:T(8,128)(2,1)}, bf16[320,1024]{1,0:T(8,128)(2,1)S(1)}, u32[]{:S(2)}, u32[]{:S(2)}) collective-permute-start(bf16[320,1024]{1,0:T(8,128)(2,1)} %collective-permute-done.3.refs_0_), channel_id=1, source_target_pairs={{0,1},{1,0},{2,3},{3,2},{4,5},{5,4},{6,7},{7,6},{8,9},{9,8},{10,11... | collective-permute-start | bytes 1966088 | tf_op jit(solution)/shard_map/ppermute | solution.py:527
  47.8 7.8 %collective-permute-start.11 = (bf16[320,1024]{1,0:T(8,128)(2,1)}, bf16[320,1024]{1,0:T(8,128)(2,1)S(1)}, u32[]{:S(2)}, u32[]{:S(2)}) collective-permute-start(bf16[320,1024]{1,0:T(8,128)(2,1)} %collective-permute-done.4.refs_2_), channel_id=1, source_target_pairs={{0,1},{1,0},{2,3},{3,2},{4,5},{5,4},{6,7},{7,6},{8,9},{9,8},{10,11... | collective-permute-start | bytes 1966088 | tf_op jit(solution)/shard_map/ppermute | solution.py:527
  47.8 7.8 %collective-permute-start.12 = (bf16[320,1024]{1,0:T(8,128)(2,1)}, bf16[320,1024]{1,0:T(8,128)(2,1)S(1)}, u32[]{:S(2)}, u32[]{:S(2)}) collective-permute-start(bf16[320,1024]{1,0:T(8,128)(2,1)} %collective-permute-done.5.refs_4_), channel_id=1, source_target_pairs={{0,1},{1,0},{2,3},{3,2},{4,5},{5,4},{6,7},{7,6},{8,9},{9,8},{10,11... | collective-permute-start | bytes 1966088 | tf_op jit(solution)/shard_map/ppermute | solution.py:527
  48.3 16.6 %collective-permute-start.8 = (bf16[320,1024]{1,0:T(8,128)(2,1)}, bf16[320,1024]{1,0:T(8,128)(2,1)S(1)}, u32[]{:S(2)}, u32[]{:S(2)}) collective-permute-start(bf16[320,1024]{1,0:T(8,128)(2,1)} %collective-permute-done.4.refs_2_), channel_id=1, source_target_pairs={{0,2},{1,3},{2,0},{3,1},{4,6},{5,7},{6,4},{7,5},{8,10},{9,11},{10,... | collective-permute-start | bytes 1966088 | tf_op jit(solution)/shard_map/ppermute | solution.py:527
  48.4 16.4 %collective-permute-start.9 = (bf16[320,1024]{1,0:T(8,128)(2,1)}, bf16[320,1024]{1,0:T(8,128)(2,1)S(1)}, u32[]{:S(2)}, u32[]{:S(2)}) collective-permute-start(bf16[320,1024]{1,0:T(8,128)(2,1)} %collective-permute-done.5.refs_4_), channel_id=1, source_target_pairs={{0,16},{1,17},{2,18},{3,19},{4,20},{5,21},{6,22},{7,23},{8,24},{9,... | collective-permute-start | bytes 1966088 | tf_op jit(solution)/shard_map/ppermute | solution.py:527
  60.7 17.1 %copy-start.8 = (s32[16]{0:T(128)S(1)}, s32[16]{0:T(128)}, u32[]{:S(2)}) copy-start(s32[16]{0:T(128)} %constant.49.clone) | copy-start | bytes 196
  60.7 17.1 %copy-start.9 = (s32[16]{0:T(128)S(1)}, s32[16]{0:T(128)}, u32[]{:S(2)}) copy-start(s32[16]{0:T(128)} %constant.48.clone) | copy-start | bytes 196
  64.8 2.6 %collective-permute-start.13 = (bf16[320,1024]{1,0:T(8,128)(2,1)S(1)}, bf16[320,1024]{1,0:T(8,128)(2,1)S(1)}, u32[]{:S(2)}, u32[]{:S(2)}) collective-permute-start(bf16[320,1024]{1,0:T(8,128)(2,1)S(1)} %collective-permute-done.8.refs_0_), channel_id=1, source_target_pairs={{0,1},{1,0},{2,3},{3,2},{4,5},{5,4},{6,7},{7,6},{8,9},{9,8},{10,11... | collective-permute-start | bytes 1966088 | tf_op jit(solution)/shard_map/ppermute | solution.py:527
  65.8 2.7 %collective-permute-start.14 = (bf16[320,1024]{1,0:T(8,128)(2,1)S(1)}, bf16[320,1024]{1,0:T(8,128)(2,1)S(1)}, u32[]{:S(2)}, u32[]{:S(2)}) collective-permute-start(bf16[320,1024]{1,0:T(8,128)(2,1)S(1)} %collective-permute-done.9.refs_2_), channel_id=1, source_target_pairs={{0,1},{1,0},{2,3},{3,2},{4,5},{5,4},{6,7},{7,6},{8,9},{9,8},{10,11... | collective-permute-start | bytes 1966088 | tf_op jit(solution)/shard_map/ppermute | solution.py:527
  76.0 7.8 %collective-permute-start.17 = (bf16[512,1024]{1,0:T(8,128)(2,1)}, bf16[512,1024]{1,0:T(8,128)(2,1)}, u32[]{:S(2)}, u32[]{:S(2)}) collective-permute-start(bf16[512,1024]{1,0:T(8,128)(2,1)} %finish.1.refs_3_), channel_id=1, source_target_pairs={{0,1},{1,0},{2,3},{3,2},{4,5},{5,4},{6,7},{7,6},{8,9},{9,8},{10,11... | collective-permute-start | bytes 3145736 | tf_op jit(solution)/shard_map/ppermute | solution.py:440
  76.4 24.9 %collective-permute-start.16 = (bf16[512,1024]{1,0:T(8,128)(2,1)}, bf16[512,1024]{1,0:T(8,128)(2,1)}, u32[]{:S(2)}, u32[]{:S(2)}) collective-permute-start(bf16[512,1024]{1,0:T(8,128)(2,1)} %finish.1.refs_3_), channel_id=1, source_target_pairs={{0,2},{1,3},{2,0},{3,1},{4,6},{5,7},{6,4},{7,5},{8,10},{9,11},{10,... | collective-permute-start | bytes 3145736 | tf_op jit(solution)/shard_map/ppermute | solution.py:444
  77.8 26.4 %collective-permute-start.15 = (bf16[512,1024]{1,0:T(8,128)(2,1)}, bf16[512,1024]{1,0:T(8,128)(2,1)}, u32[]{:S(2)}, u32[]{:S(2)}) collective-permute-start(bf16[512,1024]{1,0:T(8,128)(2,1)} %finish.1.refs_3_), channel_id=1, source_target_pairs={{0,4},{1,5},{2,6},{3,7},{4,8},{5,9},{6,10},{7,11},{8,12},{9,13},{1... | collective-permute-start | bytes 3145736 | tf_op jit(solution)/shard_map/ppermute | solution.py:444
  78.7 5.1 %copy-start.1 = (bf16[4,2816,128]{2,1,0:T(8,128)(2,1)S(1)}, bf16[4,2816,128]{2,1,0:T(8,128)(2,1)}, u32[]{:S(2)}) copy-start(bf16[4,2816,128]{2,1,0:T(8,128)(2,1)} %copy-done) | copy-start | bytes 8650756
  79.1 1.2 copy-start.7
  104.2 3.8 %collective-permute-start.21 = (bf16[512,1024]{1,0:T(8,128)(2,1)}, bf16[512,1024]{1,0:T(8,128)(2,1)S(1)}, u32[]{:S(2)}, u32[]{:S(2)}) collective-permute-start(bf16[512,1024]{1,0:T(8,128)(2,1)} %collective-permute-done.16.refs_5_), channel_id=1, source_target_pairs={{0,1},{1,0},{2,3},{3,2},{4,5},{5,4},{6,7},{7,6},{8,9},{9,8},{10,11... | collective-permute-start | bytes 3145736 | tf_op jit(solution)/shard_map/ppermute | solution.py:440
  105.5 4.0 %collective-permute-start.20 = (bf16[512,1024]{1,0:T(8,128)(2,1)}, bf16[512,1024]{1,0:T(8,128)(2,1)S(1)}, u32[]{:S(2)}, u32[]{:S(2)}) collective-permute-start(bf16[512,1024]{1,0:T(8,128)(2,1)} %collective-permute-done.15.refs_3_), channel_id=1, source_target_pairs={{0,1},{1,0},{2,3},{3,2},{4,5},{5,4},{6,7},{7,6},{8,9},{9,8},{10,11... | collective-permute-start | bytes 3145736 | tf_op jit(solution)/shard_map/ppermute | solution.py:440
  105.5 24.4 %collective-permute-start.19 = (bf16[512,1024]{1,0:T(8,128)(2,1)}, bf16[512,1024]{1,0:T(8,128)(2,1)S(1)}, u32[]{:S(2)}, u32[]{:S(2)}) collective-permute-start(bf16[512,1024]{1,0:T(8,128)(2,1)} %collective-permute-done.15.refs_3_), channel_id=1, source_target_pairs={{0,2},{1,3},{2,0},{3,1},{4,6},{5,7},{6,4},{7,5},{8,10},{9,11},{10,... | collective-permute-start | bytes 3145736 | tf_op jit(solution)/shard_map/ppermute | solution.py:444
  105.6 25.9 %collective-permute-start.18 = (bf16[512,1024]{1,0:T(8,128)(2,1)}, bf16[512,1024]{1,0:T(8,128)(2,1)S(1)}, u32[]{:S(2)}, u32[]{:S(2)}) collective-permute-start(bf16[512,1024]{1,0:T(8,128)(2,1)} %collective-permute-done.15.refs_3_), channel_id=1, source_target_pairs={{0,4},{1,5},{2,6},{3,7},{4,8},{5,9},{6,10},{7,11},{8,12},{9,13},{1... | collective-permute-start | bytes 3145736 | tf_op jit(solution)/shard_map/ppermute | solution.py:444
  131.5 4.0 %collective-permute-start.25 = (bf16[512,1024]{1,0:T(8,128)(2,1)S(1)}, bf16[512,1024]{1,0:T(8,128)(2,1)S(1)}, u32[]{:S(2)}, u32[]{:S(2)}) collective-permute-start(bf16[512,1024]{1,0:T(8,128)(2,1)S(1)} %collective-permute-done.19.refs_5_), channel_id=1, source_target_pairs={{0,1},{1,0},{2,3},{3,2},{4,5},{5,4},{6,7},{7,6},{8,9},{9,8},{10,11... | collective-permute-start | bytes 3145736 | tf_op jit(solution)/shard_map/ppermute | solution.py:440
  133.2 3.8 %collective-permute-start.24 = (bf16[512,1024]{1,0:T(8,128)(2,1)S(1)}, bf16[512,1024]{1,0:T(8,128)(2,1)S(1)}, u32[]{:S(2)}, u32[]{:S(2)}) collective-permute-start(bf16[512,1024]{1,0:T(8,128)(2,1)S(1)} %collective-permute-done.18.refs_3_), channel_id=1, source_target_pairs={{0,1},{1,0},{2,3},{3,2},{4,5},{5,4},{6,7},{7,6},{8,9},{9,8},{10,11... | collective-permute-start | bytes 3145736 | tf_op jit(solution)/shard_map/ppermute | solution.py:440
  133.2 24.2 %collective-permute-start.23 = (bf16[512,1024]{1,0:T(8,128)(2,1)S(1)}, bf16[512,1024]{1,0:T(8,128)(2,1)S(1)}, u32[]{:S(2)}, u32[]{:S(2)}) collective-permute-start(bf16[512,1024]{1,0:T(8,128)(2,1)S(1)} %collective-permute-done.18.refs_3_), channel_id=1, source_target_pairs={{0,2},{1,3},{2,0},{3,1},{4,6},{5,7},{6,4},{7,5},{8,10},{9,11},{10,... | collective-permute-start | bytes 3145736 | tf_op jit(solution)/shard_map/ppermute | solution.py:444
  134.5 25.7 %collective-permute-start.22 = (bf16[512,1024]{1,0:T(8,128)(2,1)S(1)}, bf16[512,1024]{1,0:T(8,128)(2,1)S(1)}, u32[]{:S(2)}, u32[]{:S(2)}) collective-permute-start(bf16[512,1024]{1,0:T(8,128)(2,1)S(1)} %collective-permute-done.18.refs_3_), channel_id=1, source_target_pairs={{0,4},{1,5},{2,6},{3,7},{4,8},{5,9},{6,10},{7,11},{8,12},{9,13},{1... | collective-permute-start | bytes 3145736 | tf_op jit(solution)/shard_map/ppermute | solution.py:444
  160.2 4.0 %collective-permute-start.28 = (bf16[512,1024]{1,0:T(8,128)(2,1)S(1)}, bf16[512,1024]{1,0:T(8,128)(2,1)S(1)}, u32[]{:S(2)}, u32[]{:S(2)}) collective-permute-start(bf16[512,1024]{1,0:T(8,128)(2,1)S(1)} %collective-permute-done.22.refs_3_), channel_id=1, source_target_pairs={{0,1},{1,0},{2,3},{3,2},{4,5},{5,4},{6,7},{7,6},{8,9},{9,8},{10,11... | collective-permute-start | bytes 3145736 | tf_op jit(solution)/shard_map/ppermute | solution.py:440
  161.9 3.8 %collective-permute-start.29 = (bf16[512,1024]{1,0:T(8,128)(2,1)S(1)}, bf16[512,1024]{1,0:T(8,128)(2,1)S(1)}, u32[]{:S(2)}, u32[]{:S(2)}) collective-permute-start(bf16[512,1024]{1,0:T(8,128)(2,1)S(1)} %collective-permute-done.23.refs_5_), channel_id=1, source_target_pairs={{0,1},{1,0},{2,3},{3,2},{4,5},{5,4},{6,7},{7,6},{8,9},{9,8},{10,11... | collective-permute-start | bytes 3145736 | tf_op jit(solution)/shard_map/ppermute | solution.py:440
  162.0 17.2 %collective-permute-start.27 = (bf16[256,1024]{1,0:T(8,128)(2,1)S(1)}, bf16[256,1024]{1,0:T(8,128)(2,1)S(1)}, u32[]{:S(2)}, u32[]{:S(2)}) collective-permute-start(bf16[256,1024]{1,0:T(8,128)(2,1)S(1)} %slice.27), channel_id=1, source_target_pairs={{0,4},{1,5},{2,6},{3,7},{4,8},{5,9},{6,10},{7,11},{8,12},{9,13},{1... | collective-permute-start | bytes 1572872 | tf_op jit(solution)/shard_map/ppermute | solution.py:452
  162.0 17.2 %collective-permute-start.26 = (bf16[256,1024]{1,0:T(8,128)(2,1)S(1)}, bf16[256,1024]{1,0:T(8,128)(2,1)S(1)}, u32[]{:S(2)}, u32[]{:S(2)}) collective-permute-start(bf16[256,1024]{1,0:T(8,128)(2,1)S(1)} %slice.26), channel_id=1, source_target_pairs={{0,2},{1,3},{2,0},{3,1},{4,6},{5,7},{6,4},{7,5},{8,10},{9,11},{10,... | collective-permute-start | bytes 1572872 | tf_op jit(solution)/shard_map/ppermute | solution.py:451
  179.2 2.0 collective-permute-start.30
  179.7 2.3 %collective-permute-start.31 = (bf16[256,1024]{1,0:T(8,128)(2,1)S(1)}, bf16[256,1024]{1,0:T(8,128)(2,1)S(1)}, u32[]{:S(2)}, u32[]{:S(2)}) collective-permute-start(bf16[256,1024]{1,0:T(8,128)(2,1)S(1)} %collective-permute-done.27.refs_4_), channel_id=1, source_target_pairs={{0,1},{1,0},{2,3},{3,2},{4,5},{5,4},{6,7},{7,6},{8,9},{9,8},{10,11... | collective-permute-start | bytes 1572872 | tf_op jit(solution)/shard_map/ppermute | solution.py:440

commit v12 on v11

--- a/solution.py
+++ b/solution.py
@@ -167,63 +167,66 @@
         turned_ref[head] = rows_ref[...].astype(jnp.bfloat16)
 
 
-def add_products(chips, owners_ref, hidden_ref, refs, columns, matrix, done):
-    shard = matrix.shape[1] // 2
-    copies, at, taken = [], 0, 0
+def fetch_columns(chips, owners_ref, hidden_ref, columns, done):
+    deep = columns.shape[1] // len(chips)
+    copies = []
     for place, chip in enumerate(chips):
-        first = pl.multiple_of(lax.div(owners_ref[chip[0][0]], 2) * (2 * shard), HEAD_SIZE)
+        first = pl.multiple_of(lax.div(owners_ref[chip[0]], 2) * deep, HEAD_SIZE)
         copies.append(
-            (hidden_ref.at[:, pl.ds(first, 2 * shard)], columns.at[place])
+            pltpu.make_async_copy(
+                hidden_ref.at[:, pl.ds(first, deep)],
+                columns.at[:, pl.ds(place * deep, deep)],
+                done.at[place],
+            )
         )
-        for source, row in chip:
-            core = lax.rem(owners_ref[source], 2)
-            rows = pl.ds(pl.multiple_of(core * shard + row, 16), refs[taken].shape[0])
-            copies.append((refs[taken], matrix.at[place, rows]))
-            taken += 1
-    copies = [pltpu.make_async_copy(*pair, done.at[at]) for at, pair in enumerate(copies)]
-    for copy in copies:
-        copy.start()
-
-    def product(span):
-        total = contract(columns[0], matrix[0, :, span], 1, 0)
-        for place in range(1, len(chips)):
-            total = total + contract(columns[place], matrix[place, :, span], 1, 0)
-        return total
-
-    return copies, product
+        copies[-1].start()
+    return copies
+
+
+def place_rows(owners_ref, chips, matrix):
+    shard = matrix.shape[0] // len(chips) // 2
+    return [
+        pl.ds(pl.multiple_of((2 * place + lax.rem(owners_ref[source], 2)) * shard, 16), shard)
+        for place, chip in enumerate(chips)
+        for source in chip
+    ]
 
 
 def part_kernel(chips, more, owners_ref, hidden_ref, *refs):
-    count = sum(len(chip) for chip in chips)
+    count = 2 * len(chips)
     parts, refs = refs[:count], refs[count:]
     if more:
         total_ref, refs = refs[0], refs[1:]
     out_ref, columns, matrix, done = refs
-    copies, product = add_products(chips, owners_ref, hidden_ref, parts, columns, matrix, done)
+    copies = fetch_columns(chips, owners_ref, hidden_ref, columns, done)
+    for at, (ref, rows) in enumerate(zip(parts, place_rows(owners_ref, chips, matrix))):
+        copies.append(pltpu.make_async_copy(ref, matrix.at[rows], done.at[len(chips) + at]))
+        copies[-1].start()
     for copy in copies:
         copy.wait()
     for first in range(0, out_ref.shape[1], 2 * HEAD_SIZE):
         span = slice(first, first + 2 * HEAD_SIZE)
-        if more:
-            out_ref[:, span] = total_ref[:, span] + product(span)
-        else:
-            out_ref[:, span] = product(span)
+        product = contract(columns[...], matrix[:, span], 1, 0)
+        out_ref[:, span] = total_ref[:, span] + product if more else product
 
 
 def finish_kernel(
     chips, owners_ref, hidden_ref, bias_ref, cosine_ref, sine_ref, bucket_ref, *refs
 ):
-    count = sum(len(chip) for chip in chips)
+    count = 2 * len(chips)
     parts, total_ref = refs[:count], refs[count]
     outs, (columns, matrix, done) = refs[count + 1 : -3], refs[-3:]
-    copies, product = add_products(chips, owners_ref, hidden_ref, parts, columns, matrix, done)
+    copies = fetch_columns(chips, owners_ref, hidden_ref, columns, done)
+    for ref, rows in zip(parts, place_rows(owners_ref, chips, matrix)):
+        matrix[rows] = ref[...]
     places = one_hot_rows(outs[0].shape[0], bucket_ref[...])
     for copy in copies:
         copy.wait()
     wide = KEY_VALUE_HEADS * HEAD_SIZE
     for first in range(0, 2 * wide, 2 * HEAD_SIZE):
         span = slice(first, first + 2 * HEAD_SIZE)
-        rows = (total_ref[:, span] + product(span) + bias_ref[:, span]).astype(jnp.bfloat16)
+        rows = contract(columns[...], matrix[:, span], 1, 0) + total_ref[:, span]
+        rows = (rows + bias_ref[:, span]).astype(jnp.bfloat16)
         if first < wide:
             cosine, sine = cosine_ref[...], sine_ref[...]
             halves = [
@@ -396,7 +399,7 @@
             lax.fori_loop(first, end, one_group, 0)
 
     if not last:
-        add_all(2 if more else 4)
+        add_all(heads)
         return
     worst = jnp.full((8, HEAD_SIZE), MASKED, jnp.float32)
     for row, first, end in spans:
@@ -409,7 +412,7 @@
 
     @pl.when(jnp.max(worst) * scale > SAFE_POWER)
     def _():
-        add_all(2)
+        add_all(1)
 
     seat_lanes = lax.broadcasted_iota(jnp.int32, (count, mixed_ref.shape[0]), 1)
     seats = (seat_lanes == seat_ref[...]).astype(jnp.float32).astype(jnp.bfloat16)
@@ -590,13 +593,13 @@
     shard, wide = key_matrix.shape[0], 2 * key_matrix.shape[1]
 
     def chip_parts(sources):
-        chips = [((source, 0), (source + ranks // 2, 0)) for source in sources]
+        chips = [(source, source + ranks // 2) for source in sources]
         return chips, [array for source in sources for array in matrices[source]]
 
     def scratch(chips, arrays):
         return [
-            pltpu.VMEM((len(chips), rows, 2 * shard), jnp.bfloat16),
-            pltpu.VMEM((len(chips), 2 * shard, wide), jnp.bfloat16),
+            pltpu.VMEM((rows, 2 * shard * len(chips)), jnp.bfloat16),
+            pltpu.VMEM((2 * shard * len(chips), wide), jnp.bfloat16),
             pltpu.SemaphoreType.DMA((len(chips) + len(arrays),)),
         ]
 
@@ -640,7 +643,7 @@
         out_shape=tuple(
             shape((rows, 2 * heads * HEAD_SIZE), jnp.bfloat16) for _, heads in CHUNKS
         ),
-        in_specs=[SMEM, HBM] + [VMEM] * 4 + [HBM] * len(arrays) + [VMEM],
+        in_specs=[SMEM, HBM] + [VMEM] * (5 + len(arrays)),
         out_specs=(VMEM,) * len(CHUNKS),
         scratch_shapes=scratch(chips, arrays),
         compiler_params=grant(14),

time: 205 us -> 203 us (level)
  Pallas kernels: 106 us -> 96.2 us
  waiting for transfers between devices: 56.4 us -> 63.3 us
    pallas_call x5, Pallas kernels: 74.6 us -> 66.6 us  [attend(): pl.pallas_call(functools.partial(attend_kernel, starts, sum((len(one) for...]
    ppermute x3, waiting for transfers between devices: 19.9 us -> 25.7 us  [spread(): lax.ppermute(lane, 'dp', across)]
  transfers between devices with their start and end apart: 33 -> 33, of which waited for: 18 -> 19; matrix products, arithmetic and copies ran while one was open for 3% -> 3% of each run, Pallas kernels for 36% -> 32%
where the time goes in v12:
time: 203 us
  Pallas kernels  96.2 us (47%)
  waiting for transfers between devices  63.3 us (31%)
  starting transfers between devices  29.6 us (15%)
  local copies, waits for them, and re-layouts  12.1 us (6%)
    pallas_call x5, Pallas kernels, attend(): pl.pallas_call(functools.partial(attend_kernel, starts, sum((len(one) for...  66.6 us
    ppermute x3, waiting for transfers between devices, spread(): lax.ppermute(lane, 'dp', across)  25.7 us
    ppermute x15, starting transfers between devices, send(): return lax.ppermute(array, ('groups', 'dp'), pairs)  15.6 us
    ppermute x9, waiting for transfers between devices, keep(): lax.ppermute(array, 'dp', beside)  12 us
    all_to_all x1, waiting for transfers between devices, gather_plan(): lax.all_to_all(jnp.broadcast_to(plan, (ranks, width + slots)), 'dp', spli...  10.6 us
    pallas_call x2, Pallas kernels, add_part(): pl.pallas_call(functools.partial(part_kernel, chips, bool(more)), out_sha...  10.2 us
    ppermute x15, waiting for transfers between devices, send(): return lax.ppermute(array, ('groups', 'dp'), pairs)  7.33 us
    ppermute x3, waiting for transfers between devices, spread(): lax.ppermute(lane, 'dp', ring)  7.23 us
  transfers between devices with their start and end apart: 33, of which 19 were waited for; matrix products, arithmetic and copies ran while one was open for 3% of the time, Pallas kernels for 32%

profile of v12, /device:TPU:1, one launch (start us, length us, event | category | flops | bytes accessed | tf_op | source)
XLA Modules:
  0.0 202.6 jit_solution(10316098464025720093)
XLA Ops:
  0.0 1.9 join.1.refs_0_
  2.1 2.7 %collective-permute-start.1 = (bf16[320,1024]{1,0:T(8,128)(2,1)}, bf16[320,1024]{1,0:T(8,128)(2,1)S(1)}, u32[]{:S(2)}, u32[]{:S(2)}) collective-permute-start(bf16[320,1024]{1,0:T(8,128)(2,1)} %join.1.refs_0_), channel_id=1, source_target_pairs={{0,2},{1,3},{2,0},{3,1},{4,6},{5,7},{6,4},{7,5},{8,10},{9,11},{10,... | collective-permute-start | bytes 1966088 | tf_op jit(solution)/shard_map/ppermute | solution.py:530
  4.8 1.3 collective-permute-start
  8.9 4.5 %all-to-all-start = ((s32[16,1,1600]{2,1,0:T(1,128)}), s32[16,1,1600]{2,1,0:T(1,128)S(1)}, u32[]{:S(2)}, u32[]{:S(2)}) async-start(s32[16,1,1600]{2,1,0:T(1,128)} %broadcast_in_dim.6), calls=%async_computation | async-start | bytes 212992 | tf_op jit(solution)/shard_map/all_to_all | solution.py:549
  14.8 10.6 %all-to-all-done = s32[16,1,1600]{2,1,0:T(1,128)S(1)} async-done(((s32[16,1,1600]{2,1,0:T(1,128)}), s32[16,1,1600]{2,1,0:T(1,128)S(1)}, u32[]{:S(2)}, u32[]{:S(2)}) %all-to-all-start) | async-done | bytes 102432 | tf_op jit(solution)/shard_map/all_to_all | solution.py:549
  26.0 1.3 collective-permute-start.5
  27.9 4.1 %collective-permute-start.3 = (bf16[320,1024]{1,0:T(8,128)(2,1)S(1)}, bf16[320,1024]{1,0:T(8,128)(2,1)}, u32[]{:S(2)}, u32[]{:S(2)}) collective-permute-start(bf16[320,1024]{1,0:T(8,128)(2,1)S(1)} %collective-permute-done.refs_2_), channel_id=1, source_target_pairs={{0,16},{1,17},{2,18},{3,19},{4,20},{5,21},{6,22},{7,23},{8,24},{9,... | collective-permute-start | bytes 1966088 | tf_op jit(solution)/shard_map/ppermute | solution.py:530
  32.0 1.0 collective-permute-start.7
  33.0 1.5 copy.34.route_ref
  35.4 1.0 copy-done.3
  36.4 1.7 copy-done.5
  38.1 7.0 %turn_queries.1 = (bf16[4,2816,128]{2,1,0:T(8,128)(2,1)S(1)}, s32[768,128]{1,0:T(8,128)S(1)}, f32[512,128]{1,0:T(8,128)S(1)}, f32[512,128]{1,0:T(8,128)S(1)}, s32[512,1]{1,0:T(8,128)S(1)}) custom-call(s32[512,1]{1,0:T(8,128)S(1)} %copy-done.3, s32[1,512]{1,0:T(1,128)S(1)} %get-tuple-element.80.seat_ref, s32[128,128]{1,0:T(8,128)S(1)} %reshape.69.positions_ref, ...), custom_call_target="tpu_custom_call" | custom-call | flops 4026531840 | bytes 5242880 | tf_op jit(solution)/shard_map/turn_queries/pallas_call | solution.py:570
  45.2 1.5 copy-done
  46.8 1.0 collective-permute-start.10
  48.4 1.5 collective-permute-start.9
  49.9 5.4 %add_part.2.refs_6_ = f32[512,1024]{1,0:T(8,128)S(1)} custom-call(s32[16]{0:T(128)S(1)} %fusion.7.owners_ref, bf16[512,5120]{1,0:T(8,128)(2,1)S(1)} %bitcast.12, bf16[320,1024]{1,0:T(8,128)(2,1)S(1)} %copy-done.2, bf16[320,1024]{1,0:T(8,128)(2,1)S(1)} %collective-permute-done.2.refs_1_, bf16[320,1024]{1,0:T(8,128)(2,1)S(1)} %collective-permute-done.refs_2_, ...), custom_call_target="tpu_custom_call" | custom-call | flops 2013265920 | bytes 10092544 | tf_op jit(solution)/shard_map/add_part/pallas_call | solution.py:613
  55.3 4.8 %add_part.3.refs_4_ = f32[512,1024]{1,0:T(8,128)S(1)} custom-call(s32[16]{0:T(128)S(1)} %fusion.7.owners_ref, bf16[512,5120]{1,0:T(8,128)(2,1)S(1)} %bitcast.12, bf16[320,1024]{1,0:T(8,128)(2,1)} %collective-permute-done.3.refs_0_, bf16[320,1024]{1,0:T(8,128)(2,1)S(1)} %collective-permute-done.10.refs_1_, bf16[320,1024]{1,0:T(8,128)(2,1)} %collective-permute-done.4.refs_2_, ...), custom_call_target="tpu_custom_call" | custom-call | flops 2013265920 | bytes 10092544 | tf_op jit(solution)/shard_map/add_part/pallas_call | solution.py:613
  60.2 4.6 %collective-permute-done.8.refs_0_ = bf16[320,1024]{1,0:T(8,128)(2,1)S(1)} collective-permute-done((bf16[320,1024]{1,0:T(8,128)(2,1)}, bf16[320,1024]{1,0:T(8,128)(2,1)S(1)}, u32[]{:S(2)}, u32[]{:S(2)}) %collective-permute-start.8) | collective-permute-done | bytes 655392 | tf_op jit(solution)/shard_map/ppermute | solution.py:530
  64.8 0.9 collective-permute-start.13
  65.8 1.7 collective-permute-done.13.refs_1_
  67.5 0.9 collective-permute-done.14.refs_3_
  68.4 6.4 %finish.1.refs_3_ = bf16[512,1024]{1,0:T(8,128)(2,1)} custom-call(s32[16]{0:T(128)S(1)} %fusion.7.owners_ref, bf16[512,5120]{1,0:T(8,128)(2,1)S(1)} %bitcast.12, f32[1,1024]{1,0:T(1,128)S(1)} %maximum_convert_fusion.bias_ref, f32[512,128]{1,0:T(8,128)S(1)} %get-tuple-element.91.cosine_ref, f32[512,128]{1,0:T(8,128)S(1)} %get-tuple-element.92.sine_ref, ...), custom_call_target="tpu_custom_call" | custom-call | flops 1342177280 | bytes 8126464 | tf_op jit(solution)/shard_map/finish/pallas_call | solution.py:641
  75.2 1.3 collective-permute-start.16
  77.9 1.2 copy-done.7
  79.1 3.5 %veil.1 = (bf16[16,128,128]{2,1,0:T(8,128)(2,1)S(1)}, bf16[16,256,128]{2,1,0:T(8,128)(2,1)S(1)}, bf16[16,256,128]{2,1,0:T(8,128)(2,1)S(1)}, bf16[16,256,128]{2,1,0:T(8,128)(2,1)S(1)}, bf16[16,128,128]{2,1,0:T(8,128)(2,1)S(1)}) custom-call(s32[768,128]{1,0:T(8,128)S(1)} %copy-done.7, s32[16,1,512]{2,1,0:T(1,128)S(1)} %reshape.72.routes_ref, ...), custom_call_target="tpu_custom_call" | custom-call | flops 3000000000 | bytes 4194304 | tf_op jit(solution)/shard_map/veil/pallas_call | solution.py:670
  82.6 9.9 %attend.5 = (f32[4,2816,128]{2,1,0:T(8,128)S(1)}, f32[4,2816,128]{2,1,0:T(8,128)S(1)}, f32[4,2816,128]{2,1,0:T(8,128)S(1)}) custom-call(s32[512,1]{1,0:T(8,128)S(1)} %reshape.83.refs_0_, bf16[4,2816,128]{2,1,0:T(8,128)(2,1)S(1)} %copy-done.1, bf16[16,128,128]{2,1,0:T(8,128)(2,1)S(1)} %get-tuple-element.103.refs_2_, bf16[512,1024]{1,0:T(8,128)(2,1)} %finish.1.refs_3_, ...), custom_call_target="tpu_custom_call" | custom-call | flops 4429185024 | bytes 16777216 | tf_op jit(solution)/shard_map/attend/pallas_call | solution.py:713
  92.5 7.6 %collective-permute-done.16.refs_5_ = bf16[512,1024]{1,0:T(8,128)(2,1)} collective-permute-done((bf16[512,1024]{1,0:T(8,128)(2,1)}, bf16[512,1024]{1,0:T(8,128)(2,1)}, u32[]{:S(2)}, u32[]{:S(2)}) %collective-permute-start.16) | collective-permute-done | bytes 1048608 | tf_op jit(solution)/shard_map/ppermute | solution.py:447
  100.2 2.8 %collective-permute-done.15.refs_3_ = bf16[512,1024]{1,0:T(8,128)(2,1)} collective-permute-done((bf16[512,1024]{1,0:T(8,128)(2,1)}, bf16[512,1024]{1,0:T(8,128)(2,1)}, u32[]{:S(2)}, u32[]{:S(2)}) %collective-permute-start.15) | collective-permute-done | bytes 1048608 | tf_op jit(solution)/shard_map/ppermute | solution.py:447
  103.0 1.3 collective-permute-start.21
  104.4 2.4 %collective-permute-done.21.refs_6_ = bf16[512,1024]{1,0:T(8,128)(2,1)S(1)} collective-permute-done((bf16[512,1024]{1,0:T(8,128)(2,1)}, bf16[512,1024]{1,0:T(8,128)(2,1)S(1)}, u32[]{:S(2)}, u32[]{:S(2)}) %collective-permute-start.21) | collective-permute-done | bytes 1048608 | tf_op jit(solution)/shard_map/ppermute | solution.py:443
  106.8 1.5 collective-permute-done.20.refs_4_
  108.3 12.2 %attend.6 = (f32[4,2816,128]{2,1,0:T(8,128)S(1)}, f32[4,2816,128]{2,1,0:T(8,128)S(1)}, f32[4,2816,128]{2,1,0:T(8,128)S(1)}) custom-call(s32[512,1]{1,0:T(8,128)S(1)} %reshape.83.refs_0_, bf16[4,2816,128]{2,1,0:T(8,128)(2,1)S(1)} %copy-done.1, ...), custom_call_target="tpu_custom_call", output_to_operand_aliasing={{0}: (7, {}), {1}: (8, {}), {2}: (9, {})} | custom-call | flops 5905580032 | bytes 33554432 | tf_op jit(solution)/shard_map/attend/pallas_call | solution.py:713
  120.4 8.3 %collective-permute-done.19.refs_5_ = bf16[512,1024]{1,0:T(8,128)(2,1)S(1)} collective-permute-done((bf16[512,1024]{1,0:T(8,128)(2,1)}, bf16[512,1024]{1,0:T(8,128)(2,1)S(1)}, u32[]{:S(2)}, u32[]{:S(2)}) %collective-permute-start.19) | collective-permute-done | bytes 1048608 | tf_op jit(solution)/shard_map/ppermute | solution.py:447
  128.7 1.6 collective-permute-done.18.refs_3_
  130.3 1.7 collective-permute-start.25
  132.0 1.3 collective-permute-start.23
  133.3 1.0 collective-permute-done.25.refs_6_
  134.3 1.5 collective-permute-done.24.refs_4_
  135.8 10.7 %attend.7 = (f32[4,2816,128]{2,1,0:T(8,128)S(1)}, f32[4,2816,128]{2,1,0:T(8,128)S(1)}, f32[4,2816,128]{2,1,0:T(8,128)S(1)}) custom-call(s32[512,1]{1,0:T(8,128)S(1)} %reshape.83.refs_0_, bf16[4,2816,128]{2,1,0:T(8,128)(2,1)S(1)} %copy-done.1, ...), custom_call_target="tpu_custom_call", output_to_operand_aliasing={{0}: (7, {}), {1}: (8, {}), {2}: (9, {})} | custom-call | flops 5905580032 | bytes 33554432 | tf_op jit(solution)/shard_map/attend/pallas_call | solution.py:713
  146.5 9.8 %collective-permute-done.23.refs_5_ = bf16[512,1024]{1,0:T(8,128)(2,1)S(1)} collective-permute-done((bf16[512,1024]{1,0:T(8,128)(2,1)S(1)}, bf16[512,1024]{1,0:T(8,128)(2,1)S(1)}, u32[]{:S(2)}, u32[]{:S(2)}) %collective-permute-start.23) | collective-permute-done | bytes 1048608 | tf_op jit(solution)/shard_map/ppermute | solution.py:447
  156.2 2.8 %collective-permute-done.22.refs_3_ = bf16[512,1024]{1,0:T(8,128)(2,1)S(1)} collective-permute-done((bf16[512,1024]{1,0:T(8,128)(2,1)S(1)}, bf16[512,1024]{1,0:T(8,128)(2,1)S(1)}, u32[]{:S(2)}, u32[]{:S(2)}) %collective-permute-start.22) | collective-permute-done | bytes 1048608 | tf_op jit(solution)/shard_map/ppermute | solution.py:447
  159.0 1.7 collective-permute-start.28
  161.1 1.9 collective-permute-done.28.refs_4_
  163.0 1.5 collective-permute-done.29.refs_6_
  164.5 10.7 %attend.8 = (f32[4,2816,128]{2,1,0:T(8,128)S(1)}, f32[4,2816,128]{2,1,0:T(8,128)S(1)}, f32[4,2816,128]{2,1,0:T(8,128)S(1)}) custom-call(s32[512,1]{1,0:T(8,128)S(1)} %reshape.83.refs_0_, bf16[4,2816,128]{2,1,0:T(8,128)(2,1)S(1)} %copy-done.1, ...), custom_call_target="tpu_custom_call", output_to_operand_aliasing={{0}: (7, {}), {1}: (8, {}), {2}: (9, {})} | custom-call | flops 5905580032 | bytes 33554432 | tf_op jit(solution)/shard_map/attend/pallas_call | solution.py:713
  175.6 1.4 collective-permute-start.30
  177.0 1.5 collective-permute-done.30.refs_5_
  179.3 23.2 %attend.9 = (bf16[512,2560]{1,0:T(8,128)(2,1)}, f32[4,2816,128]{2,1,0:T(8,128)S(1)}, f32[4,2816,128]{2,1,0:T(8,128)S(1)}, f32[4,2816,128]{2,1,0:T(8,128)S(1)}) custom-call(s32[512,1]{1,0:T(8,128)S(1)} %reshape.83.refs_0_, bf16[4,2816,128]{2,1,0:T(8,128)(2,1)S(1)} %copy-done.1, ...), custom_call_target="tpu_custom_call", output_to_operand_aliasing={{1}: (7, {}), {2}: (8, {}), {3}: (9, {})} | custom-call | flops 4429185024 | bytes 16777216 | tf_op jit(solution)/shard_map/attend/pallas_call | solution.py:713
  (81 shorter events, 10.4 us)
Async XLA Ops:
  1.9 23.5 %collective-permute-start.2 = (bf16[320,1024]{1,0:T(8,128)(2,1)}, bf16[320,1024]{1,0:T(8,128)(2,1)S(1)}, u32[]{:S(2)}, u32[]{:S(2)}) collective-permute-start(bf16[320,1024]{1,0:T(8,128)(2,1)} %join.1.refs_0_), channel_id=1, source_target_pairs={{0,1},{1,0},{2,3},{3,2},{4,5},{5,4},{6,7},{7,6},{8,9},{9,8},{10,11... | collective-permute-start | bytes 1966088 | tf_op jit(solution)/shard_map/ppermute | solution.py:530
  2.1 23.4 %collective-permute-start.1 = (bf16[320,1024]{1,0:T(8,128)(2,1)}, bf16[320,1024]{1,0:T(8,128)(2,1)S(1)}, u32[]{:S(2)}, u32[]{:S(2)}) collective-permute-start(bf16[320,1024]{1,0:T(8,128)(2,1)} %join.1.refs_0_), channel_id=1, source_target_pairs={{0,2},{1,3},{2,0},{3,1},{4,6},{5,7},{6,4},{7,5},{8,10},{9,11},{10,... | collective-permute-start | bytes 1966088 | tf_op jit(solution)/shard_map/ppermute | solution.py:530
  4.8 20.7 %collective-permute-start = (bf16[320,1024]{1,0:T(8,128)(2,1)}, bf16[320,1024]{1,0:T(8,128)(2,1)S(1)}, u32[]{:S(2)}, u32[]{:S(2)}) collective-permute-start(bf16[320,1024]{1,0:T(8,128)(2,1)} %join.1.refs_0_), channel_id=1, source_target_pairs={{0,4},{1,5},{2,6},{3,7},{4,8},{5,9},{6,10},{7,11},{8,12},{9,13},{1... | collective-permute-start | bytes 1966088 | tf_op jit(solution)/shard_map/ppermute | solution.py:530
  6.1 0.7 copy-start.4
  8.9 16.5 %all-to-all-start = ((s32[16,1,1600]{2,1,0:T(1,128)}), s32[16,1,1600]{2,1,0:T(1,128)S(1)}, u32[]{:S(2)}, u32[]{:S(2)}) async-start(s32[16,1,1600]{2,1,0:T(1,128)} %broadcast_in_dim.6), calls=%async_computation | async-start | bytes 212992 | tf_op jit(solution)/shard_map/all_to_all | solution.py:549
  25.5 21.2 %collective-permute-start.6 = (bf16[320,1024]{1,0:T(8,128)(2,1)S(1)}, bf16[320,1024]{1,0:T(8,128)(2,1)}, u32[]{:S(2)}, u32[]{:S(2)}) collective-permute-start(bf16[320,1024]{1,0:T(8,128)(2,1)S(1)} %collective-permute-done.refs_2_), channel_id=1, source_target_pairs={{0,1},{1,0},{2,3},{3,2},{4,5},{5,4},{6,7},{7,6},{8,9},{9,8},{10,11... | collective-permute-start | bytes 1966088 | tf_op jit(solution)/shard_map/ppermute | solution.py:530
  26.0 20.8 %collective-permute-start.5 = (bf16[320,1024]{1,0:T(8,128)(2,1)S(1)}, bf16[320,1024]{1,0:T(8,128)(2,1)}, u32[]{:S(2)}, u32[]{:S(2)}) collective-permute-start(bf16[320,1024]{1,0:T(8,128)(2,1)S(1)} %collective-permute-done.refs_2_), channel_id=1, source_target_pairs={{0,2},{1,3},{2,0},{3,1},{4,6},{5,7},{6,4},{7,5},{8,10},{9,11},{10,... | collective-permute-start | bytes 1966088 | tf_op jit(solution)/shard_map/ppermute | solution.py:530
  27.3 19.5 %collective-permute-start.4 = (bf16[320,1024]{1,0:T(8,128)(2,1)S(1)}, bf16[320,1024]{1,0:T(8,128)(2,1)}, u32[]{:S(2)}, u32[]{:S(2)}) collective-permute-start(bf16[320,1024]{1,0:T(8,128)(2,1)S(1)} %collective-permute-done.refs_2_), channel_id=1, source_target_pairs={{0,4},{1,5},{2,6},{3,7},{4,8},{5,9},{6,10},{7,11},{8,12},{9,13},{1... | collective-permute-start | bytes 1966088 | tf_op jit(solution)/shard_map/ppermute | solution.py:530
  27.9 18.9 %collective-permute-start.3 = (bf16[320,1024]{1,0:T(8,128)(2,1)S(1)}, bf16[320,1024]{1,0:T(8,128)(2,1)}, u32[]{:S(2)}, u32[]{:S(2)}) collective-permute-start(bf16[320,1024]{1,0:T(8,128)(2,1)S(1)} %collective-permute-done.refs_2_), channel_id=1, source_target_pairs={{0,16},{1,17},{2,18},{3,19},{4,20},{5,21},{6,22},{7,23},{8,24},{9,... | collective-permute-start | bytes 1966088 | tf_op jit(solution)/shard_map/ppermute | solution.py:530
  32.0 14.8 %collective-permute-start.7 = (bf16[320,1024]{1,0:T(8,128)(2,1)S(1)}, bf16[320,1024]{1,0:T(8,128)(2,1)}, u32[]{:S(2)}, u32[]{:S(2)}) collective-permute-start(bf16[320,1024]{1,0:T(8,128)(2,1)S(1)} %collective-permute-done.1.refs_4_), channel_id=1, source_target_pairs={{0,1},{1,0},{2,3},{3,2},{4,5},{5,4},{6,7},{7,6},{8,9},{9,8},{10,11... | collective-permute-start | bytes 1966088 | tf_op jit(solution)/shard_map/ppermute | solution.py:530
  35.3 14.6 %slice-start = ((s8[5242880]{0:T(1024)(128)(4,1)}), s8[1048576]{0:T(1024)(128)(4,1)S(1)}, s32[]{:S(2)}) async-start(s8[5242880]{0:T(1024)(128)(4,1)} %bitcast.11), calls=%async_computation.1 | async-start | bytes 2097152
  35.4 1.0 copy-start.3
  36.4 1.7 copy-start.5
  38.1 11.8 %slice-start.1 = ((s8[5242880]{0:T(1024)(128)(4,1)}), s8[4194304]{0:T(1024)(128)(4,1)S(1)}, s32[]{:S(2)}) async-start(s8[5242880]{0:T(1024)(128)(4,1)} %bitcast.11), calls=%async_computation.2 | async-start | bytes 8388608
  38.1 11.8 %copy-start.2 = (bf16[320,1024]{1,0:T(8,128)(2,1)S(1)}, bf16[320,1024]{1,0:T(8,128)(2,1)}, u32[]{:S(2)}) copy-start(bf16[320,1024]{1,0:T(8,128)(2,1)} %join.1.refs_0_) | copy-start | bytes 1966084
  45.2 1.6 copy-start
  46.7 8.6 %copy-start.6 = (s32[768,128]{1,0:T(8,128)}, s32[768,128]{1,0:T(8,128)S(1)}, u32[]{:S(2)}) copy-start(s32[768,128]{1,0:T(8,128)S(1)} %get-tuple-element.87.bounds_ref) | copy-start | bytes 1179652
  46.8 8.5 %collective-permute-start.10 = (bf16[320,1024]{1,0:T(8,128)(2,1)}, bf16[320,1024]{1,0:T(8,128)(2,1)S(1)}, u32[]{:S(2)}, u32[]{:S(2)}) collective-permute-start(bf16[320,1024]{1,0:T(8,128)(2,1)} %collective-permute-done.3.refs_0_), channel_id=1, source_target_pairs={{0,1},{1,0},{2,3},{3,2},{4,5},{5,4},{6,7},{7,6},{8,9},{9,8},{10,11... | collective-permute-start | bytes 1966088 | tf_op jit(solution)/shard_map/ppermute | solution.py:530
  47.8 7.5 %collective-permute-start.11 = (bf16[320,1024]{1,0:T(8,128)(2,1)}, bf16[320,1024]{1,0:T(8,128)(2,1)S(1)}, u32[]{:S(2)}, u32[]{:S(2)}) collective-permute-start(bf16[320,1024]{1,0:T(8,128)(2,1)} %collective-permute-done.4.refs_2_), channel_id=1, source_target_pairs={{0,1},{1,0},{2,3},{3,2},{4,5},{5,4},{6,7},{7,6},{8,9},{9,8},{10,11... | collective-permute-start | bytes 1966088 | tf_op jit(solution)/shard_map/ppermute | solution.py:530
  47.8 7.6 %collective-permute-start.12 = (bf16[320,1024]{1,0:T(8,128)(2,1)}, bf16[320,1024]{1,0:T(8,128)(2,1)S(1)}, u32[]{:S(2)}, u32[]{:S(2)}) collective-permute-start(bf16[320,1024]{1,0:T(8,128)(2,1)} %collective-permute-done.5.refs_4_), channel_id=1, source_target_pairs={{0,1},{1,0},{2,3},{3,2},{4,5},{5,4},{6,7},{7,6},{8,9},{9,8},{10,11... | collective-permute-start | bytes 1966088 | tf_op jit(solution)/shard_map/ppermute | solution.py:530
  48.3 16.6 %collective-permute-start.8 = (bf16[320,1024]{1,0:T(8,128)(2,1)}, bf16[320,1024]{1,0:T(8,128)(2,1)S(1)}, u32[]{:S(2)}, u32[]{:S(2)}) collective-permute-start(bf16[320,1024]{1,0:T(8,128)(2,1)} %collective-permute-done.4.refs_2_), channel_id=1, source_target_pairs={{0,2},{1,3},{2,0},{3,1},{4,6},{5,7},{6,4},{7,5},{8,10},{9,11},{10,... | collective-permute-start | bytes 1966088 | tf_op jit(solution)/shard_map/ppermute | solution.py:530
  48.4 16.4 %collective-permute-start.9 = (bf16[320,1024]{1,0:T(8,128)(2,1)}, bf16[320,1024]{1,0:T(8,128)(2,1)S(1)}, u32[]{:S(2)}, u32[]{:S(2)}) collective-permute-start(bf16[320,1024]{1,0:T(8,128)(2,1)} %collective-permute-done.5.refs_4_), channel_id=1, source_target_pairs={{0,16},{1,17},{2,18},{3,19},{4,20},{5,21},{6,22},{7,23},{8,24},{9,... | collective-permute-start | bytes 1966088 | tf_op jit(solution)/shard_map/ppermute | solution.py:530
  60.2 16.4 %copy-start.8 = (s32[16]{0:T(128)S(1)}, s32[16]{0:T(128)}, u32[]{:S(2)}) copy-start(s32[16]{0:T(128)} %constant.49.clone) | copy-start | bytes 196
  60.2 16.4 %copy-start.9 = (s32[16]{0:T(128)S(1)}, s32[16]{0:T(128)}, u32[]{:S(2)}) copy-start(s32[16]{0:T(128)} %constant.48.clone) | copy-start | bytes 196
  64.8 2.6 %collective-permute-start.13 = (bf16[320,1024]{1,0:T(8,128)(2,1)S(1)}, bf16[320,1024]{1,0:T(8,128)(2,1)S(1)}, u32[]{:S(2)}, u32[]{:S(2)}) collective-permute-start(bf16[320,1024]{1,0:T(8,128)(2,1)S(1)} %collective-permute-done.8.refs_0_), channel_id=1, source_target_pairs={{0,1},{1,0},{2,3},{3,2},{4,5},{5,4},{6,7},{7,6},{8,9},{9,8},{10,11... | collective-permute-start | bytes 1966088 | tf_op jit(solution)/shard_map/ppermute | solution.py:530
  65.8 2.7 %collective-permute-start.14 = (bf16[320,1024]{1,0:T(8,128)(2,1)S(1)}, bf16[320,1024]{1,0:T(8,128)(2,1)S(1)}, u32[]{:S(2)}, u32[]{:S(2)}) collective-permute-start(bf16[320,1024]{1,0:T(8,128)(2,1)S(1)} %collective-permute-done.9.refs_2_), channel_id=1, source_target_pairs={{0,1},{1,0},{2,3},{3,2},{4,5},{5,4},{6,7},{7,6},{8,9},{9,8},{10,11... | collective-permute-start | bytes 1966088 | tf_op jit(solution)/shard_map/ppermute | solution.py:530
  74.8 7.8 %collective-permute-start.17 = (bf16[512,1024]{1,0:T(8,128)(2,1)}, bf16[512,1024]{1,0:T(8,128)(2,1)}, u32[]{:S(2)}, u32[]{:S(2)}) collective-permute-start(bf16[512,1024]{1,0:T(8,128)(2,1)} %finish.1.refs_3_), channel_id=1, source_target_pairs={{0,1},{1,0},{2,3},{3,2},{4,5},{5,4},{6,7},{7,6},{8,9},{9,8},{10,11... | collective-permute-start | bytes 3145736 | tf_op jit(solution)/shard_map/ppermute | solution.py:443
  75.2 24.9 %collective-permute-start.16 = (bf16[512,1024]{1,0:T(8,128)(2,1)}, bf16[512,1024]{1,0:T(8,128)(2,1)}, u32[]{:S(2)}, u32[]{:S(2)}) collective-permute-start(bf16[512,1024]{1,0:T(8,128)(2,1)} %finish.1.refs_3_), channel_id=1, source_target_pairs={{0,2},{1,3},{2,0},{3,1},{4,6},{5,7},{6,4},{7,5},{8,10},{9,11},{10,... | collective-permute-start | bytes 3145736 | tf_op jit(solution)/shard_map/ppermute | solution.py:447
  76.6 26.4 %collective-permute-start.15 = (bf16[512,1024]{1,0:T(8,128)(2,1)}, bf16[512,1024]{1,0:T(8,128)(2,1)}, u32[]{:S(2)}, u32[]{:S(2)}) collective-permute-start(bf16[512,1024]{1,0:T(8,128)(2,1)} %finish.1.refs_3_), channel_id=1, source_target_pairs={{0,4},{1,5},{2,6},{3,7},{4,8},{5,9},{6,10},{7,11},{8,12},{9,13},{1... | collective-permute-start | bytes 3145736 | tf_op jit(solution)/shard_map/ppermute | solution.py:447
  77.5 5.1 %copy-start.1 = (bf16[4,2816,128]{2,1,0:T(8,128)(2,1)S(1)}, bf16[4,2816,128]{2,1,0:T(8,128)(2,1)}, u32[]{:S(2)}) copy-start(bf16[4,2816,128]{2,1,0:T(8,128)(2,1)} %copy-done) | copy-start | bytes 8650756
  77.9 1.2 copy-start.7
  103.0 3.8 %collective-permute-start.21 = (bf16[512,1024]{1,0:T(8,128)(2,1)}, bf16[512,1024]{1,0:T(8,128)(2,1)S(1)}, u32[]{:S(2)}, u32[]{:S(2)}) collective-permute-start(bf16[512,1024]{1,0:T(8,128)(2,1)} %collective-permute-done.16.refs_5_), channel_id=1, source_target_pairs={{0,1},{1,0},{2,3},{3,2},{4,5},{5,4},{6,7},{7,6},{8,9},{9,8},{10,11... | collective-permute-start | bytes 3145736 | tf_op jit(solution)/shard_map/ppermute | solution.py:443
  104.3 4.0 %collective-permute-start.20 = (bf16[512,1024]{1,0:T(8,128)(2,1)}, bf16[512,1024]{1,0:T(8,128)(2,1)S(1)}, u32[]{:S(2)}, u32[]{:S(2)}) collective-permute-start(bf16[512,1024]{1,0:T(8,128)(2,1)} %collective-permute-done.15.refs_3_), channel_id=1, source_target_pairs={{0,1},{1,0},{2,3},{3,2},{4,5},{5,4},{6,7},{7,6},{8,9},{9,8},{10,11... | collective-permute-start | bytes 3145736 | tf_op jit(solution)/shard_map/ppermute | solution.py:443
  104.3 24.4 %collective-permute-start.19 = (bf16[512,1024]{1,0:T(8,128)(2,1)}, bf16[512,1024]{1,0:T(8,128)(2,1)S(1)}, u32[]{:S(2)}, u32[]{:S(2)}) collective-permute-start(bf16[512,1024]{1,0:T(8,128)(2,1)} %collective-permute-done.15.refs_3_), channel_id=1, source_target_pairs={{0,2},{1,3},{2,0},{3,1},{4,6},{5,7},{6,4},{7,5},{8,10},{9,11},{10,... | collective-permute-start | bytes 3145736 | tf_op jit(solution)/shard_map/ppermute | solution.py:447
  104.4 25.9 %collective-permute-start.18 = (bf16[512,1024]{1,0:T(8,128)(2,1)}, bf16[512,1024]{1,0:T(8,128)(2,1)S(1)}, u32[]{:S(2)}, u32[]{:S(2)}) collective-permute-start(bf16[512,1024]{1,0:T(8,128)(2,1)} %collective-permute-done.15.refs_3_), channel_id=1, source_target_pairs={{0,4},{1,5},{2,6},{3,7},{4,8},{5,9},{6,10},{7,11},{8,12},{9,13},{1... | collective-permute-start | bytes 3145736 | tf_op jit(solution)/shard_map/ppermute | solution.py:447
  130.3 4.0 %collective-permute-start.25 = (bf16[512,1024]{1,0:T(8,128)(2,1)S(1)}, bf16[512,1024]{1,0:T(8,128)(2,1)S(1)}, u32[]{:S(2)}, u32[]{:S(2)}) collective-permute-start(bf16[512,1024]{1,0:T(8,128)(2,1)S(1)} %collective-permute-done.19.refs_5_), channel_id=1, source_target_pairs={{0,1},{1,0},{2,3},{3,2},{4,5},{5,4},{6,7},{7,6},{8,9},{9,8},{10,11... | collective-permute-start | bytes 3145736 | tf_op jit(solution)/shard_map/ppermute | solution.py:443
  132.0 3.8 %collective-permute-start.24 = (bf16[512,1024]{1,0:T(8,128)(2,1)S(1)}, bf16[512,1024]{1,0:T(8,128)(2,1)S(1)}, u32[]{:S(2)}, u32[]{:S(2)}) collective-permute-start(bf16[512,1024]{1,0:T(8,128)(2,1)S(1)} %collective-permute-done.18.refs_3_), channel_id=1, source_target_pairs={{0,1},{1,0},{2,3},{3,2},{4,5},{5,4},{6,7},{7,6},{8,9},{9,8},{10,11... | collective-permute-start | bytes 3145736 | tf_op jit(solution)/shard_map/ppermute | solution.py:443
  132.0 24.2 %collective-permute-start.23 = (bf16[512,1024]{1,0:T(8,128)(2,1)S(1)}, bf16[512,1024]{1,0:T(8,128)(2,1)S(1)}, u32[]{:S(2)}, u32[]{:S(2)}) collective-permute-start(bf16[512,1024]{1,0:T(8,128)(2,1)S(1)} %collective-permute-done.18.refs_3_), channel_id=1, source_target_pairs={{0,2},{1,3},{2,0},{3,1},{4,6},{5,7},{6,4},{7,5},{8,10},{9,11},{10,... | collective-permute-start | bytes 3145736 | tf_op jit(solution)/shard_map/ppermute | solution.py:447
  133.3 25.7 %collective-permute-start.22 = (bf16[512,1024]{1,0:T(8,128)(2,1)S(1)}, bf16[512,1024]{1,0:T(8,128)(2,1)S(1)}, u32[]{:S(2)}, u32[]{:S(2)}) collective-permute-start(bf16[512,1024]{1,0:T(8,128)(2,1)S(1)} %collective-permute-done.18.refs_3_), channel_id=1, source_target_pairs={{0,4},{1,5},{2,6},{3,7},{4,8},{5,9},{6,10},{7,11},{8,12},{9,13},{1... | collective-permute-start | bytes 3145736 | tf_op jit(solution)/shard_map/ppermute | solution.py:447
  159.0 4.0 %collective-permute-start.28 = (bf16[512,1024]{1,0:T(8,128)(2,1)S(1)}, bf16[512,1024]{1,0:T(8,128)(2,1)S(1)}, u32[]{:S(2)}, u32[]{:S(2)}) collective-permute-start(bf16[512,1024]{1,0:T(8,128)(2,1)S(1)} %collective-permute-done.22.refs_3_), channel_id=1, source_target_pairs={{0,1},{1,0},{2,3},{3,2},{4,5},{5,4},{6,7},{7,6},{8,9},{9,8},{10,11... | collective-permute-start | bytes 3145736 | tf_op jit(solution)/shard_map/ppermute | solution.py:443
  160.7 3.8 %collective-permute-start.29 = (bf16[512,1024]{1,0:T(8,128)(2,1)S(1)}, bf16[512,1024]{1,0:T(8,128)(2,1)S(1)}, u32[]{:S(2)}, u32[]{:S(2)}) collective-permute-start(bf16[512,1024]{1,0:T(8,128)(2,1)S(1)} %collective-permute-done.23.refs_5_), channel_id=1, source_target_pairs={{0,1},{1,0},{2,3},{3,2},{4,5},{5,4},{6,7},{7,6},{8,9},{9,8},{10,11... | collective-permute-start | bytes 3145736 | tf_op jit(solution)/shard_map/ppermute | solution.py:443
  160.8 14.8 %collective-permute-start.27 = (bf16[256,1024]{1,0:T(8,128)(2,1)S(1)}, bf16[256,1024]{1,0:T(8,128)(2,1)S(1)}, u32[]{:S(2)}, u32[]{:S(2)}) collective-permute-start(bf16[256,1024]{1,0:T(8,128)(2,1)S(1)} %slice.27), channel_id=1, source_target_pairs={{0,4},{1,5},{2,6},{3,7},{4,8},{5,9},{6,10},{7,11},{8,12},{9,13},{1... | collective-permute-start | bytes 1572872 | tf_op jit(solution)/shard_map/ppermute | solution.py:455
  160.8 14.8 %collective-permute-start.26 = (bf16[256,1024]{1,0:T(8,128)(2,1)S(1)}, bf16[256,1024]{1,0:T(8,128)(2,1)S(1)}, u32[]{:S(2)}, u32[]{:S(2)}) collective-permute-start(bf16[256,1024]{1,0:T(8,128)(2,1)S(1)} %slice.26), channel_id=1, source_target_pairs={{0,2},{1,3},{2,0},{3,1},{4,6},{5,7},{6,4},{7,5},{8,10},{9,11},{10,... | collective-permute-start | bytes 1572872 | tf_op jit(solution)/shard_map/ppermute | solution.py:454
  175.6 2.9 %collective-permute-start.30 = (bf16[256,1024]{1,0:T(8,128)(2,1)S(1)}, bf16[256,1024]{1,0:T(8,128)(2,1)S(1)}, u32[]{:S(2)}, u32[]{:S(2)}) collective-permute-start(bf16[256,1024]{1,0:T(8,128)(2,1)S(1)} %collective-permute-done.26.refs_3_), channel_id=1, source_target_pairs={{0,1},{1,0},{2,3},{3,2},{4,5},{5,4},{6,7},{7,6},{8,9},{9,8},{10,11... | collective-permute-start | bytes 1572872 | tf_op jit(solution)/shard_map/ppermute | solution.py:443
  177.0 2.3 %collective-permute-start.31 = (bf16[256,1024]{1,0:T(8,128)(2,1)S(1)}, bf16[256,1024]{1,0:T(8,128)(2,1)S(1)}, u32[]{:S(2)}, u32[]{:S(2)}) collective-permute-start(bf16[256,1024]{1,0:T(8,128)(2,1)S(1)} %collective-permute-done.27.refs_4_), channel_id=1, source_target_pairs={{0,1},{1,0},{2,3},{3,2},{4,5},{5,4},{6,7},{7,6},{8,9},{9,8},{10,11... | collective-permute-start | bytes 1572872 | tf_op jit(solution)/shard_map/ppermute | solution.py:443

commit v13 on v12

--- a/solution.py
+++ b/solution.py
@@ -436,7 +436,7 @@
     across = [(rank, rank ^ 2) for rank in range(ranks)]
     beside = [(rank, rank ^ 1) for rank in range(ranks)]
     steps = ranks // PLANE
-    half = block.shape[0] // 32 * 16
+    half = block.shape[0] // 32 * 18
 
     def keep(source, first, array):
         held.setdefault(source, []).append((first, array))
@@ -444,17 +444,17 @@
 
     lane, other = block, None
     for step in range(steps - 1):
-        following = lax.ppermute(lane, "dp", ring), lax.ppermute(lane, "dp", across)
         keep(step, 0, lane)
         if step:
             keep(steps + step - 1, 0, other)
+        following = lax.ppermute(lane, "dp", across), lax.ppermute(lane, "dp", ring)
         extra = yield
-        lane, other, extra = lax.optimization_barrier((*following, extra))
+        other, lane, extra = lax.optimization_barrier((*following, extra))
         yield extra
+    keep(steps - 1, 0, lane)
+    keep(2 * steps - 2, 0, other)
     over = lax.ppermute(lane[:half], "dp", across)
     around = lax.ppermute(other[half:], "dp", ring)
-    keep(steps - 1, 0, lane)
-    keep(2 * steps - 2, 0, other)
     extra = yield other
     over, around, extra = lax.optimization_barrier((over, around, extra))
     keep(2 * steps - 1, 0, over)
@@ -529,8 +529,8 @@
     def send(array, pairs):
         return lax.ppermute(array, ("groups", "dp"), pairs)
 
-    near_lane, other_row = send(joined, ring), send(joined, across)
     joined_swap = send(joined, beside)
+    other_row, near_lane = send(joined, across), send(joined, ring)
     bucket, seat, sorted_route, more = pl.pallas_call(
         functools.partial(order_kernel, ranks, slots, extra, stride),
         out_shape=(
@@ -549,13 +549,13 @@
     plan = lax.all_to_all(
         jnp.broadcast_to(plan, (ranks, width + slots)), "dp", split_axis=0, concat_axis=0, tiled=True
     )
-    near_lane, other_row, joined_swap, plan, bucket, seat = lax.optimization_barrier(
-        (near_lane, other_row, joined_swap, plan, bucket, seat)
+    other_row, near_lane, joined_swap, plan, bucket, seat = lax.optimization_barrier(
+        (other_row, near_lane, joined_swap, plan, bucket, seat)
     )
     matrices = {0: (joined, joined_swap)}
-    far_lane, next_lane = send(near_lane, swap), send(near_lane, ring)
-    near_other = send(near_lane, across)
     swaps = send(near_lane, beside), send(other_row, beside)
+    far_lane, near_other = send(near_lane, swap), send(near_lane, across)
+    next_lane = send(near_lane, ring)
     all_positions = plan[:, width:].reshape(-1, HEAD_SIZE)
     planes = ranks // PLANE
     sets = [(0, 2 * planes)] + [
@@ -623,16 +623,16 @@
 
     bias = jnp.concatenate([key_projection_bias, value_projection_bias])
     bias = bias.astype(jnp.float32).reshape(1, -1)
-    step = (far_lane, next_lane, near_other, swaps)
+    step = (far_lane, near_other, next_lane, swaps)
     step, turned, bounds, cosine, sine, seat_column, bias, owners = lax.optimization_barrier(
         (step, turned, bounds, cosine, sine, seat_column, bias, owners)
     )
-    far_lane, next_lane, near_other, swaps = step
+    far_lane, near_other, next_lane, swaps = step
     matrices[1], matrices[2] = (near_lane, swaps[0]), (other_row, swaps[1])
-    next_other, far_other = send(next_lane, across), send(near_other, swap)
     matrices[3] = (far_lane, send(far_lane, beside))
     matrices[4] = (next_lane, send(next_lane, beside))
     matrices[5] = (near_other, send(near_other, beside))
+    far_other, next_other = send(near_other, swap), send(next_lane, across)
     total = add_part(add_part(None, (0, 1, 2)), (3, 4, 5))
     next_other, far_other, total = lax.optimization_barrier((next_other, far_other, total))
     matrices[6] = (next_other, send(next_other, beside))

time: 203 us -> 200 us (0.985)
    ppermute x3, waiting for transfers between devices: 25.7 us -> 0.01 us  [spread(): lax.ppermute(lane, 'dp', across)]
    ppermute x3, waiting for transfers between devices: 7.23 us -> 31.9 us  [spread(): lax.ppermute(lane, 'dp', ring)]
  transfers between devices with their start and end apart: 33 -> 33, of which waited for: 19 -> 15; matrix products, arithmetic and copies ran while one was open for 3% -> 3% of each run, Pallas kernels for 32% -> 33%
where the time goes in v13:
time: 200 us; the launch traced here: 199 us
  Pallas kernels  96.3 us (48%)
  waiting for transfers between devices  61.5 us (31%)
  starting transfers between devices  27.8 us (14%)
  local copies, waits for them, and re-layouts  12.1 us (6%)
    pallas_call x5, Pallas kernels, attend(): pl.pallas_call(functools.partial(attend_kernel, starts, sum((len(one) for...  66.7 us
    ppermute x3, waiting for transfers between devices, spread(): lax.ppermute(lane, 'dp', ring)  31.9 us
    ppermute x15, starting transfers between devices, send(): return lax.ppermute(array, ('groups', 'dp'), pairs)  15.7 us
    ppermute x9, waiting for transfers between devices, keep(): lax.ppermute(array, 'dp', beside)  12.1 us
    all_to_all x1, waiting for transfers between devices, gather_plan(): lax.all_to_all(jnp.broadcast_to(plan, (ranks, width + slots)), 'dp', spli...  10.3 us
    pallas_call x2, Pallas kernels, add_part(): pl.pallas_call(functools.partial(part_kernel, chips, bool(more)), out_sha...  10.2 us
    ppermute x15, waiting for transfers between devices, send(): return lax.ppermute(array, ('groups', 'dp'), pairs)  7.15 us
    pallas_call x1, Pallas kernels, gather_plan(): pl.pallas_call(functools.partial(query_kernel, ranks, spare, stride, pack...  7.03 us
  transfers between devices with their start and end apart: 33, of which 15 were waited for; matrix products, arithmetic and copies ran while one was open for 3% of the time, Pallas kernels for 33%

profile of v13, /device:TPU:1, one launch (start us, length us, event | category | flops | bytes accessed | tf_op | source)
XLA Modules:
  0.0 199.1 jit_solution(2513890598061916751)
XLA Ops:
  0.0 1.9 join.1.refs_0_
  2.1 2.7 %collective-permute-start.1 = (bf16[320,1024]{1,0:T(8,128)(2,1)}, bf16[320,1024]{1,0:T(8,128)(2,1)S(1)}, u32[]{:S(2)}, u32[]{:S(2)}) collective-permute-start(bf16[320,1024]{1,0:T(8,128)(2,1)} %join.1.refs_0_), channel_id=1, source_target_pairs={{0,4},{1,5},{2,6},{3,7},{4,8},{5,9},{6,10},{7,11},{8,12},{9,13},{1... | collective-permute-start | bytes 1966088 | tf_op jit(solution)/shard_map/ppermute | solution.py:530
  4.8 1.2 collective-permute-start
  7.4 0.8 concatenate.20
  8.2 0.7 broadcast_in_dim.6
  8.9 4.5 %all-to-all-start = ((s32[16,1,1600]{2,1,0:T(1,128)}), s32[16,1,1600]{2,1,0:T(1,128)S(1)}, u32[]{:S(2)}, u32[]{:S(2)}) async-start(s32[16,1,1600]{2,1,0:T(1,128)} %broadcast_in_dim.6), calls=%async_computation | async-start | bytes 212992 | tf_op jit(solution)/shard_map/all_to_all | solution.py:549
  13.4 0.7 concatenate.22
  14.1 0.7 concatenate.23
  14.8 10.3 %all-to-all-done = s32[16,1,1600]{2,1,0:T(1,128)S(1)} async-done(((s32[16,1,1600]{2,1,0:T(1,128)}), s32[16,1,1600]{2,1,0:T(1,128)S(1)}, u32[]{:S(2)}, u32[]{:S(2)}) %all-to-all-start) | async-done | bytes 102432 | tf_op jit(solution)/shard_map/all_to_all | solution.py:549
  26.6 4.1 %collective-permute-start.3 = (bf16[320,1024]{1,0:T(8,128)(2,1)S(1)}, bf16[320,1024]{1,0:T(8,128)(2,1)}, u32[]{:S(2)}, u32[]{:S(2)}) collective-permute-start(bf16[320,1024]{1,0:T(8,128)(2,1)S(1)} %collective-permute-done.1.refs_2_), channel_id=1, source_target_pairs={{0,16},{1,17},{2,18},{3,19},{4,20},{5,21},{6,22},{7,23},{8,24},{9,... | collective-permute-start | bytes 1966088 | tf_op jit(solution)/shard_map/ppermute | solution.py:530
  30.7 1.0 collective-permute-start.7
  31.8 1.5 copy.34.route_ref
  33.3 0.7 fusion.7.owners_ref
  34.1 1.0 copy-done.3
  35.1 1.7 copy-done.5
  36.9 7.0 %turn_queries.1 = (bf16[4,2816,128]{2,1,0:T(8,128)(2,1)S(1)}, s32[768,128]{1,0:T(8,128)S(1)}, f32[512,128]{1,0:T(8,128)S(1)}, f32[512,128]{1,0:T(8,128)S(1)}, s32[512,1]{1,0:T(8,128)S(1)}) custom-call(s32[512,1]{1,0:T(8,128)S(1)} %copy-done.3, s32[1,512]{1,0:T(1,128)S(1)} %get-tuple-element.80.seat_ref, s32[128,128]{1,0:T(8,128)S(1)} %reshape.69.positions_ref, ...), custom_call_target="tpu_custom_call" | custom-call | flops 4026531840 | bytes 5242880 | tf_op jit(solution)/shard_map/turn_queries/pallas_call | solution.py:570
  43.9 1.5 copy-done
  45.5 1.0 collective-permute-start.10
  47.0 1.0 collective-permute-start.8
  48.0 1.5 collective-permute-start.9
  49.4 5.4 %add_part.2.refs_6_ = f32[512,1024]{1,0:T(8,128)S(1)} custom-call(s32[16]{0:T(128)S(1)} %fusion.7.owners_ref, bf16[512,5120]{1,0:T(8,128)(2,1)S(1)} %bitcast.12, bf16[320,1024]{1,0:T(8,128)(2,1)S(1)} %copy-done.2, bf16[320,1024]{1,0:T(8,128)(2,1)S(1)} %collective-permute-done.2.refs_1_, bf16[320,1024]{1,0:T(8,128)(2,1)S(1)} %collective-permute-done.1.refs_2_, ...), custom_call_target="tpu_custom_call" | custom-call | flops 2013265920 | bytes 10092544 | tf_op jit(solution)/shard_map/add_part/pallas_call | solution.py:613
  54.9 4.8 %add_part.3.refs_4_ = f32[512,1024]{1,0:T(8,128)S(1)} custom-call(s32[16]{0:T(128)S(1)} %fusion.7.owners_ref, bf16[512,5120]{1,0:T(8,128)(2,1)S(1)} %bitcast.12, bf16[320,1024]{1,0:T(8,128)(2,1)} %collective-permute-done.3.refs_0_, bf16[320,1024]{1,0:T(8,128)(2,1)S(1)} %collective-permute-done.10.refs_1_, bf16[320,1024]{1,0:T(8,128)(2,1)} %collective-permute-done.5.refs_2_, ...), custom_call_target="tpu_custom_call" | custom-call | flops 2013265920 | bytes 10092544 | tf_op jit(solution)/shard_map/add_part/pallas_call | solution.py:613
  59.8 3.8 %collective-permute-done.8.refs_0_ = bf16[320,1024]{1,0:T(8,128)(2,1)S(1)} collective-permute-done((bf16[320,1024]{1,0:T(8,128)(2,1)}, bf16[320,1024]{1,0:T(8,128)(2,1)S(1)}, u32[]{:S(2)}, u32[]{:S(2)}) %collective-permute-start.8) | collective-permute-done | bytes 655392 | tf_op jit(solution)/shard_map/ppermute | solution.py:530
  64.2 1.1 collective-permute-start.13
  65.3 1.7 collective-permute-done.13.refs_1_
  67.1 0.9 collective-permute-done.14.refs_3_
  68.0 6.4 %finish.1.refs_3_ = bf16[512,1024]{1,0:T(8,128)(2,1)} custom-call(s32[16]{0:T(128)S(1)} %fusion.7.owners_ref, bf16[512,5120]{1,0:T(8,128)(2,1)S(1)} %bitcast.12, f32[1,1024]{1,0:T(1,128)S(1)} %maximum_convert_fusion.bias_ref, f32[512,128]{1,0:T(8,128)S(1)} %get-tuple-element.91.cosine_ref, f32[512,128]{1,0:T(8,128)S(1)} %get-tuple-element.92.sine_ref, ...), custom_call_target="tpu_custom_call" | custom-call | flops 1342177280 | bytes 8126464 | tf_op jit(solution)/shard_map/finish/pallas_call | solution.py:641
  76.7 1.2 copy-done.7
  77.8 3.5 %veil.1 = (bf16[16,128,128]{2,1,0:T(8,128)(2,1)S(1)}, bf16[16,256,128]{2,1,0:T(8,128)(2,1)S(1)}, bf16[16,256,128]{2,1,0:T(8,128)(2,1)S(1)}, bf16[16,256,128]{2,1,0:T(8,128)(2,1)S(1)}, bf16[16,128,128]{2,1,0:T(8,128)(2,1)S(1)}) custom-call(s32[768,128]{1,0:T(8,128)S(1)} %copy-done.7, s32[16,1,512]{2,1,0:T(1,128)S(1)} %reshape.72.routes_ref, ...), custom_call_target="tpu_custom_call" | custom-call | flops 3000000000 | bytes 4194304 | tf_op jit(solution)/shard_map/veil/pallas_call | solution.py:670
  81.3 9.9 %attend.5 = (f32[4,2816,128]{2,1,0:T(8,128)S(1)}, f32[4,2816,128]{2,1,0:T(8,128)S(1)}, f32[4,2816,128]{2,1,0:T(8,128)S(1)}) custom-call(s32[512,1]{1,0:T(8,128)S(1)} %reshape.83.refs_0_, bf16[4,2816,128]{2,1,0:T(8,128)(2,1)S(1)} %copy-done.1, bf16[16,128,128]{2,1,0:T(8,128)(2,1)S(1)} %get-tuple-element.103.refs_2_, bf16[512,1024]{1,0:T(8,128)(2,1)} %finish.1.refs_3_, ...), custom_call_target="tpu_custom_call" | custom-call | flops 4429185024 | bytes 16777216 | tf_op jit(solution)/shard_map/attend/pallas_call | solution.py:713
  91.3 10.3 %collective-permute-done.16.refs_3_ = bf16[512,1024]{1,0:T(8,128)(2,1)} collective-permute-done((bf16[512,1024]{1,0:T(8,128)(2,1)}, bf16[512,1024]{1,0:T(8,128)(2,1)}, u32[]{:S(2)}, u32[]{:S(2)}) %collective-permute-start.16) | collective-permute-done | bytes 1048608 | tf_op jit(solution)/shard_map/ppermute | solution.py:450
  101.5 1.0 collective-permute-start.21
  103.0 2.0 collective-permute-done.21.refs_6_
  105.0 1.5 collective-permute-done.20.refs_4_
  106.5 12.2 %attend.6 = (f32[4,2816,128]{2,1,0:T(8,128)S(1)}, f32[4,2816,128]{2,1,0:T(8,128)S(1)}, f32[4,2816,128]{2,1,0:T(8,128)S(1)}) custom-call(s32[512,1]{1,0:T(8,128)S(1)} %reshape.83.refs_0_, bf16[4,2816,128]{2,1,0:T(8,128)(2,1)S(1)} %copy-done.1, ...), custom_call_target="tpu_custom_call", output_to_operand_aliasing={{0}: (7, {}), {1}: (8, {}), {2}: (9, {})} | custom-call | flops 5905580032 | bytes 33554432 | tf_op jit(solution)/shard_map/attend/pallas_call | solution.py:713
  118.7 10.1 %collective-permute-done.19.refs_3_ = bf16[512,1024]{1,0:T(8,128)(2,1)S(1)} collective-permute-done((bf16[512,1024]{1,0:T(8,128)(2,1)}, bf16[512,1024]{1,0:T(8,128)(2,1)S(1)}, u32[]{:S(2)}, u32[]{:S(2)}) %collective-permute-start.19) | collective-permute-done | bytes 1048608 | tf_op jit(solution)/shard_map/ppermute | solution.py:450
  128.7 1.4 collective-permute-start.25
  130.6 1.8 collective-permute-done.25.refs_6_
  132.4 1.5 collective-permute-done.24.refs_4_
  133.9 10.7 %attend.7 = (f32[4,2816,128]{2,1,0:T(8,128)S(1)}, f32[4,2816,128]{2,1,0:T(8,128)S(1)}, f32[4,2816,128]{2,1,0:T(8,128)S(1)}) custom-call(s32[512,1]{1,0:T(8,128)S(1)} %reshape.83.refs_0_, bf16[4,2816,128]{2,1,0:T(8,128)(2,1)S(1)} %copy-done.1, ...), custom_call_target="tpu_custom_call", output_to_operand_aliasing={{0}: (7, {}), {1}: (8, {}), {2}: (9, {})} | custom-call | flops 5905580032 | bytes 33554432 | tf_op jit(solution)/shard_map/attend/pallas_call | solution.py:713
  144.6 11.5 %collective-permute-done.23.refs_3_ = bf16[512,1024]{1,0:T(8,128)(2,1)S(1)} collective-permute-done((bf16[512,1024]{1,0:T(8,128)(2,1)S(1)}, bf16[512,1024]{1,0:T(8,128)(2,1)S(1)}, u32[]{:S(2)}, u32[]{:S(2)}) %collective-permute-start.23) | collective-permute-done | bytes 1048608 | tf_op jit(solution)/shard_map/ppermute | solution.py:450
  156.1 1.4 collective-permute-start.28
  158.2 1.6 collective-permute-done.28.refs_4_
  159.8 1.5 collective-permute-done.29.refs_6_
  161.3 10.7 %attend.8 = (f32[4,2816,128]{2,1,0:T(8,128)S(1)}, f32[4,2816,128]{2,1,0:T(8,128)S(1)}, f32[4,2816,128]{2,1,0:T(8,128)S(1)}) custom-call(s32[512,1]{1,0:T(8,128)S(1)} %reshape.83.refs_0_, bf16[4,2816,128]{2,1,0:T(8,128)(2,1)S(1)} %copy-done.1, ...), custom_call_target="tpu_custom_call", output_to_operand_aliasing={{0}: (7, {}), {1}: (8, {}), {2}: (9, {})} | custom-call | flops 5905580032 | bytes 33554432 | tf_op jit(solution)/shard_map/attend/pallas_call | solution.py:713
  172.0 1.4 collective-permute-start.30
  173.3 2.3 %collective-permute-done.31.refs_6_ = bf16[224,1024]{1,0:T(8,128)(2,1)S(1)} collective-permute-done((bf16[224,1024]{1,0:T(8,128)(2,1)S(1)}, bf16[224,1024]{1,0:T(8,128)(2,1)S(1)}, u32[]{:S(2)}, u32[]{:S(2)}) %collective-permute-start.31) | collective-permute-done | bytes 458784 | tf_op jit(solution)/shard_map/ppermute | solution.py:443
  175.6 23.3 %attend.9 = (bf16[512,2560]{1,0:T(8,128)(2,1)}, f32[4,2816,128]{2,1,0:T(8,128)S(1)}, f32[4,2816,128]{2,1,0:T(8,128)S(1)}, f32[4,2816,128]{2,1,0:T(8,128)S(1)}) custom-call(s32[512,1]{1,0:T(8,128)S(1)} %reshape.83.refs_0_, bf16[4,2816,128]{2,1,0:T(8,128)(2,1)S(1)} %copy-done.1, ...), custom_call_target="tpu_custom_call", output_to_operand_aliasing={{1}: (7, {}), {2}: (8, {}), {3}: (9, {})} | custom-call | flops 4429185024 | bytes 16777216 | tf_op jit(solution)/shard_map/attend/pallas_call | solution.py:713
  (81 shorter events, 8.4 us)
Async XLA Ops:
  1.9 23.2 %collective-permute-start.2 = (bf16[320,1024]{1,0:T(8,128)(2,1)}, bf16[320,1024]{1,0:T(8,128)(2,1)S(1)}, u32[]{:S(2)}, u32[]{:S(2)}) collective-permute-start(bf16[320,1024]{1,0:T(8,128)(2,1)} %join.1.refs_0_), channel_id=1, source_target_pairs={{0,1},{1,0},{2,3},{3,2},{4,5},{5,4},{6,7},{7,6},{8,9},{9,8},{10,11... | collective-permute-start | bytes 1966088 | tf_op jit(solution)/shard_map/ppermute | solution.py:530
  2.1 23.1 %collective-permute-start.1 = (bf16[320,1024]{1,0:T(8,128)(2,1)}, bf16[320,1024]{1,0:T(8,128)(2,1)S(1)}, u32[]{:S(2)}, u32[]{:S(2)}) collective-permute-start(bf16[320,1024]{1,0:T(8,128)(2,1)} %join.1.refs_0_), channel_id=1, source_target_pairs={{0,4},{1,5},{2,6},{3,7},{4,8},{5,9},{6,10},{7,11},{8,12},{9,13},{1... | collective-permute-start | bytes 1966088 | tf_op jit(solution)/shard_map/ppermute | solution.py:530
  4.8 20.4 %collective-permute-start = (bf16[320,1024]{1,0:T(8,128)(2,1)}, bf16[320,1024]{1,0:T(8,128)(2,1)S(1)}, u32[]{:S(2)}, u32[]{:S(2)}) collective-permute-start(bf16[320,1024]{1,0:T(8,128)(2,1)} %join.1.refs_0_), channel_id=1, source_target_pairs={{0,2},{1,3},{2,0},{3,1},{4,6},{5,7},{6,4},{7,5},{8,10},{9,11},{10,... | collective-permute-start | bytes 1966088 | tf_op jit(solution)/shard_map/ppermute | solution.py:530
  6.0 0.7 copy-start.4
  8.9 16.2 %all-to-all-start = ((s32[16,1,1600]{2,1,0:T(1,128)}), s32[16,1,1600]{2,1,0:T(1,128)S(1)}, u32[]{:S(2)}, u32[]{:S(2)}) async-start(s32[16,1,1600]{2,1,0:T(1,128)} %broadcast_in_dim.6), calls=%async_computation | async-start | bytes 212992 | tf_op jit(solution)/shard_map/all_to_all | solution.py:549
  25.2 20.3 %collective-permute-start.6 = (bf16[320,1024]{1,0:T(8,128)(2,1)S(1)}, bf16[320,1024]{1,0:T(8,128)(2,1)}, u32[]{:S(2)}, u32[]{:S(2)}) collective-permute-start(bf16[320,1024]{1,0:T(8,128)(2,1)S(1)} %collective-permute-done.1.refs_2_), channel_id=1, source_target_pairs={{0,1},{1,0},{2,3},{3,2},{4,5},{5,4},{6,7},{7,6},{8,9},{9,8},{10,11... | collective-permute-start | bytes 1966088 | tf_op jit(solution)/shard_map/ppermute | solution.py:530
  25.6 19.9 %collective-permute-start.5 = (bf16[320,1024]{1,0:T(8,128)(2,1)S(1)}, bf16[320,1024]{1,0:T(8,128)(2,1)}, u32[]{:S(2)}, u32[]{:S(2)}) collective-permute-start(bf16[320,1024]{1,0:T(8,128)(2,1)S(1)} %collective-permute-done.1.refs_2_), channel_id=1, source_target_pairs={{0,4},{1,5},{2,6},{3,7},{4,8},{5,9},{6,10},{7,11},{8,12},{9,13},{1... | collective-permute-start | bytes 1966088 | tf_op jit(solution)/shard_map/ppermute | solution.py:530
  26.2 19.3 %collective-permute-start.4 = (bf16[320,1024]{1,0:T(8,128)(2,1)S(1)}, bf16[320,1024]{1,0:T(8,128)(2,1)}, u32[]{:S(2)}, u32[]{:S(2)}) collective-permute-start(bf16[320,1024]{1,0:T(8,128)(2,1)S(1)} %collective-permute-done.1.refs_2_), channel_id=1, source_target_pairs={{0,2},{1,3},{2,0},{3,1},{4,6},{5,7},{6,4},{7,5},{8,10},{9,11},{10,... | collective-permute-start | bytes 1966088 | tf_op jit(solution)/shard_map/ppermute | solution.py:530
  26.6 18.9 %collective-permute-start.3 = (bf16[320,1024]{1,0:T(8,128)(2,1)S(1)}, bf16[320,1024]{1,0:T(8,128)(2,1)}, u32[]{:S(2)}, u32[]{:S(2)}) collective-permute-start(bf16[320,1024]{1,0:T(8,128)(2,1)S(1)} %collective-permute-done.1.refs_2_), channel_id=1, source_target_pairs={{0,16},{1,17},{2,18},{3,19},{4,20},{5,21},{6,22},{7,23},{8,24},{9,... | collective-permute-start | bytes 1966088 | tf_op jit(solution)/shard_map/ppermute | solution.py:530
  30.7 14.8 %collective-permute-start.7 = (bf16[320,1024]{1,0:T(8,128)(2,1)S(1)}, bf16[320,1024]{1,0:T(8,128)(2,1)}, u32[]{:S(2)}, u32[]{:S(2)}) collective-permute-start(bf16[320,1024]{1,0:T(8,128)(2,1)S(1)} %collective-permute-done.refs_4_), channel_id=1, source_target_pairs={{0,1},{1,0},{2,3},{3,2},{4,5},{5,4},{6,7},{7,6},{8,9},{9,8},{10,11... | collective-permute-start | bytes 1966088 | tf_op jit(solution)/shard_map/ppermute | solution.py:530
  34.0 15.4 %slice-start = ((s8[5242880]{0:T(1024)(128)(4,1)}), s8[1048576]{0:T(1024)(128)(4,1)S(1)}, s32[]{:S(2)}) async-start(s8[5242880]{0:T(1024)(128)(4,1)} %bitcast.11), calls=%async_computation.1 | async-start | bytes 2097152
  34.1 1.0 copy-start.3
  35.1 1.7 copy-start.5
  36.9 12.6 %slice-start.1 = ((s8[5242880]{0:T(1024)(128)(4,1)}), s8[4194304]{0:T(1024)(128)(4,1)S(1)}, s32[]{:S(2)}) async-start(s8[5242880]{0:T(1024)(128)(4,1)} %bitcast.11), calls=%async_computation.2 | async-start | bytes 8388608
  36.9 12.6 %copy-start.2 = (bf16[320,1024]{1,0:T(8,128)(2,1)S(1)}, bf16[320,1024]{1,0:T(8,128)(2,1)}, u32[]{:S(2)}) copy-start(bf16[320,1024]{1,0:T(8,128)(2,1)} %join.1.refs_0_) | copy-start | bytes 1966084
  43.9 1.6 copy-start
  45.5 9.4 %copy-start.6 = (s32[768,128]{1,0:T(8,128)}, s32[768,128]{1,0:T(8,128)S(1)}, u32[]{:S(2)}) copy-start(s32[768,128]{1,0:T(8,128)S(1)} %get-tuple-element.87.bounds_ref) | copy-start | bytes 1179652
  45.5 9.3 %collective-permute-start.10 = (bf16[320,1024]{1,0:T(8,128)(2,1)}, bf16[320,1024]{1,0:T(8,128)(2,1)S(1)}, u32[]{:S(2)}, u32[]{:S(2)}) collective-permute-start(bf16[320,1024]{1,0:T(8,128)(2,1)} %collective-permute-done.3.refs_0_), channel_id=1, source_target_pairs={{0,1},{1,0},{2,3},{3,2},{4,5},{5,4},{6,7},{7,6},{8,9},{9,8},{10,11... | collective-permute-start | bytes 1966088 | tf_op jit(solution)/shard_map/ppermute | solution.py:530
  46.5 8.4 %collective-permute-start.11 = (bf16[320,1024]{1,0:T(8,128)(2,1)}, bf16[320,1024]{1,0:T(8,128)(2,1)S(1)}, u32[]{:S(2)}, u32[]{:S(2)}) collective-permute-start(bf16[320,1024]{1,0:T(8,128)(2,1)} %collective-permute-done.5.refs_2_), channel_id=1, source_target_pairs={{0,1},{1,0},{2,3},{3,2},{4,5},{5,4},{6,7},{7,6},{8,9},{9,8},{10,11... | collective-permute-start | bytes 1966088 | tf_op jit(solution)/shard_map/ppermute | solution.py:530
  46.5 8.4 %collective-permute-start.12 = (bf16[320,1024]{1,0:T(8,128)(2,1)}, bf16[320,1024]{1,0:T(8,128)(2,1)S(1)}, u32[]{:S(2)}, u32[]{:S(2)}) collective-permute-start(bf16[320,1024]{1,0:T(8,128)(2,1)} %collective-permute-done.4.refs_4_), channel_id=1, source_target_pairs={{0,1},{1,0},{2,3},{3,2},{4,5},{5,4},{6,7},{7,6},{8,9},{9,8},{10,11... | collective-permute-start | bytes 1966088 | tf_op jit(solution)/shard_map/ppermute | solution.py:530
  47.0 16.6 %collective-permute-start.8 = (bf16[320,1024]{1,0:T(8,128)(2,1)}, bf16[320,1024]{1,0:T(8,128)(2,1)S(1)}, u32[]{:S(2)}, u32[]{:S(2)}) collective-permute-start(bf16[320,1024]{1,0:T(8,128)(2,1)} %collective-permute-done.5.refs_2_), channel_id=1, source_target_pairs={{0,2},{1,3},{2,0},{3,1},{4,6},{5,7},{6,4},{7,5},{8,10},{9,11},{10,... | collective-permute-start | bytes 1966088 | tf_op jit(solution)/shard_map/ppermute | solution.py:530
  48.0 16.3 %collective-permute-start.9 = (bf16[320,1024]{1,0:T(8,128)(2,1)}, bf16[320,1024]{1,0:T(8,128)(2,1)S(1)}, u32[]{:S(2)}, u32[]{:S(2)}) collective-permute-start(bf16[320,1024]{1,0:T(8,128)(2,1)} %collective-permute-done.4.refs_4_), channel_id=1, source_target_pairs={{0,16},{1,17},{2,18},{3,19},{4,20},{5,21},{6,22},{7,23},{8,24},{9,... | collective-permute-start | bytes 1966088 | tf_op jit(solution)/shard_map/ppermute | solution.py:530
  59.7 15.6 %copy-start.8 = (s32[16]{0:T(128)S(1)}, s32[16]{0:T(128)}, u32[]{:S(2)}) copy-start(s32[16]{0:T(128)} %constant.49.clone) | copy-start | bytes 196
  59.8 15.6 %copy-start.9 = (s32[16]{0:T(128)S(1)}, s32[16]{0:T(128)}, u32[]{:S(2)}) copy-start(s32[16]{0:T(128)} %constant.48.clone) | copy-start | bytes 196
  64.2 2.8 %collective-permute-start.13 = (bf16[320,1024]{1,0:T(8,128)(2,1)S(1)}, bf16[320,1024]{1,0:T(8,128)(2,1)S(1)}, u32[]{:S(2)}, u32[]{:S(2)}) collective-permute-start(bf16[320,1024]{1,0:T(8,128)(2,1)S(1)} %collective-permute-done.8.refs_0_), channel_id=1, source_target_pairs={{0,1},{1,0},{2,3},{3,2},{4,5},{5,4},{6,7},{7,6},{8,9},{9,8},{10,11... | collective-permute-start | bytes 1966088 | tf_op jit(solution)/shard_map/ppermute | solution.py:530
  65.3 2.7 %collective-permute-start.14 = (bf16[320,1024]{1,0:T(8,128)(2,1)S(1)}, bf16[320,1024]{1,0:T(8,128)(2,1)S(1)}, u32[]{:S(2)}, u32[]{:S(2)}) collective-permute-start(bf16[320,1024]{1,0:T(8,128)(2,1)S(1)} %collective-permute-done.9.refs_2_), channel_id=1, source_target_pairs={{0,1},{1,0},{2,3},{3,2},{4,5},{5,4},{6,7},{7,6},{8,9},{9,8},{10,11... | collective-permute-start | bytes 1966088 | tf_op jit(solution)/shard_map/ppermute | solution.py:530
  74.4 6.9 %collective-permute-start.17 = (bf16[512,1024]{1,0:T(8,128)(2,1)}, bf16[512,1024]{1,0:T(8,128)(2,1)}, u32[]{:S(2)}, u32[]{:S(2)}) collective-permute-start(bf16[512,1024]{1,0:T(8,128)(2,1)} %finish.1.refs_3_), channel_id=1, source_target_pairs={{0,1},{1,0},{2,3},{3,2},{4,5},{5,4},{6,7},{7,6},{8,9},{9,8},{10,11... | collective-permute-start | bytes 3145736 | tf_op jit(solution)/shard_map/ppermute | solution.py:443
  74.8 26.7 %collective-permute-start.16 = (bf16[512,1024]{1,0:T(8,128)(2,1)}, bf16[512,1024]{1,0:T(8,128)(2,1)}, u32[]{:S(2)}, u32[]{:S(2)}) collective-permute-start(bf16[512,1024]{1,0:T(8,128)(2,1)} %finish.1.refs_3_), channel_id=1, source_target_pairs={{0,4},{1,5},{2,6},{3,7},{4,8},{5,9},{6,10},{7,11},{8,12},{9,13},{1... | collective-permute-start | bytes 3145736 | tf_op jit(solution)/shard_map/ppermute | solution.py:450
  74.8 26.7 %collective-permute-start.15 = (bf16[512,1024]{1,0:T(8,128)(2,1)}, bf16[512,1024]{1,0:T(8,128)(2,1)}, u32[]{:S(2)}, u32[]{:S(2)}) collective-permute-start(bf16[512,1024]{1,0:T(8,128)(2,1)} %finish.1.refs_3_), channel_id=1, source_target_pairs={{0,2},{1,3},{2,0},{3,1},{4,6},{5,7},{6,4},{7,5},{8,10},{9,11},{10,... | collective-permute-start | bytes 3145736 | tf_op jit(solution)/shard_map/ppermute | solution.py:450
  76.3 5.1 %copy-start.1 = (bf16[4,2816,128]{2,1,0:T(8,128)(2,1)S(1)}, bf16[4,2816,128]{2,1,0:T(8,128)(2,1)}, u32[]{:S(2)}) copy-start(bf16[4,2816,128]{2,1,0:T(8,128)(2,1)} %copy-done) | copy-start | bytes 8650756
  76.7 1.2 copy-start.7
  101.5 3.5 %collective-permute-start.21 = (bf16[512,1024]{1,0:T(8,128)(2,1)}, bf16[512,1024]{1,0:T(8,128)(2,1)S(1)}, u32[]{:S(2)}, u32[]{:S(2)}) collective-permute-start(bf16[512,1024]{1,0:T(8,128)(2,1)} %collective-permute-done.15.refs_5_), channel_id=1, source_target_pairs={{0,1},{1,0},{2,3},{3,2},{4,5},{5,4},{6,7},{7,6},{8,9},{9,8},{10,11... | collective-permute-start | bytes 3145736 | tf_op jit(solution)/shard_map/ppermute | solution.py:443
  102.5 4.0 %collective-permute-start.20 = (bf16[512,1024]{1,0:T(8,128)(2,1)}, bf16[512,1024]{1,0:T(8,128)(2,1)S(1)}, u32[]{:S(2)}, u32[]{:S(2)}) collective-permute-start(bf16[512,1024]{1,0:T(8,128)(2,1)} %collective-permute-done.16.refs_3_), channel_id=1, source_target_pairs={{0,1},{1,0},{2,3},{3,2},{4,5},{5,4},{6,7},{7,6},{8,9},{9,8},{10,11... | collective-permute-start | bytes 3145736 | tf_op jit(solution)/shard_map/ppermute | solution.py:443
  102.5 26.2 %collective-permute-start.19 = (bf16[512,1024]{1,0:T(8,128)(2,1)}, bf16[512,1024]{1,0:T(8,128)(2,1)S(1)}, u32[]{:S(2)}, u32[]{:S(2)}) collective-permute-start(bf16[512,1024]{1,0:T(8,128)(2,1)} %collective-permute-done.16.refs_3_), channel_id=1, source_target_pairs={{0,4},{1,5},{2,6},{3,7},{4,8},{5,9},{6,10},{7,11},{8,12},{9,13},{1... | collective-permute-start | bytes 3145736 | tf_op jit(solution)/shard_map/ppermute | solution.py:450
  102.5 26.2 %collective-permute-start.18 = (bf16[512,1024]{1,0:T(8,128)(2,1)}, bf16[512,1024]{1,0:T(8,128)(2,1)S(1)}, u32[]{:S(2)}, u32[]{:S(2)}) collective-permute-start(bf16[512,1024]{1,0:T(8,128)(2,1)} %collective-permute-done.16.refs_3_), channel_id=1, source_target_pairs={{0,2},{1,3},{2,0},{3,1},{4,6},{5,7},{6,4},{7,5},{8,10},{9,11},{10,... | collective-permute-start | bytes 3145736 | tf_op jit(solution)/shard_map/ppermute | solution.py:450
  128.7 3.6 %collective-permute-start.25 = (bf16[512,1024]{1,0:T(8,128)(2,1)S(1)}, bf16[512,1024]{1,0:T(8,128)(2,1)S(1)}, u32[]{:S(2)}, u32[]{:S(2)}) collective-permute-start(bf16[512,1024]{1,0:T(8,128)(2,1)S(1)} %collective-permute-done.18.refs_5_), channel_id=1, source_target_pairs={{0,1},{1,0},{2,3},{3,2},{4,5},{5,4},{6,7},{7,6},{8,9},{9,8},{10,11... | collective-permute-start | bytes 3145736 | tf_op jit(solution)/shard_map/ppermute | solution.py:443
  130.1 3.8 %collective-permute-start.24 = (bf16[512,1024]{1,0:T(8,128)(2,1)S(1)}, bf16[512,1024]{1,0:T(8,128)(2,1)S(1)}, u32[]{:S(2)}, u32[]{:S(2)}) collective-permute-start(bf16[512,1024]{1,0:T(8,128)(2,1)S(1)} %collective-permute-done.19.refs_3_), channel_id=1, source_target_pairs={{0,1},{1,0},{2,3},{3,2},{4,5},{5,4},{6,7},{7,6},{8,9},{9,8},{10,11... | collective-permute-start | bytes 3145736 | tf_op jit(solution)/shard_map/ppermute | solution.py:443
  130.1 26.0 %collective-permute-start.23 = (bf16[512,1024]{1,0:T(8,128)(2,1)S(1)}, bf16[512,1024]{1,0:T(8,128)(2,1)S(1)}, u32[]{:S(2)}, u32[]{:S(2)}) collective-permute-start(bf16[512,1024]{1,0:T(8,128)(2,1)S(1)} %collective-permute-done.19.refs_3_), channel_id=1, source_target_pairs={{0,4},{1,5},{2,6},{3,7},{4,8},{5,9},{6,10},{7,11},{8,12},{9,13},{1... | collective-permute-start | bytes 3145736 | tf_op jit(solution)/shard_map/ppermute | solution.py:450
  130.1 26.0 %collective-permute-start.22 = (bf16[512,1024]{1,0:T(8,128)(2,1)S(1)}, bf16[512,1024]{1,0:T(8,128)(2,1)S(1)}, u32[]{:S(2)}, u32[]{:S(2)}) collective-permute-start(bf16[512,1024]{1,0:T(8,128)(2,1)S(1)} %collective-permute-done.19.refs_3_), channel_id=1, source_target_pairs={{0,2},{1,3},{2,0},{3,1},{4,6},{5,7},{6,4},{7,5},{8,10},{9,11},{10,... | collective-permute-start | bytes 3145736 | tf_op jit(solution)/shard_map/ppermute | solution.py:450
  156.1 3.6 %collective-permute-start.28 = (bf16[512,1024]{1,0:T(8,128)(2,1)S(1)}, bf16[512,1024]{1,0:T(8,128)(2,1)S(1)}, u32[]{:S(2)}, u32[]{:S(2)}) collective-permute-start(bf16[512,1024]{1,0:T(8,128)(2,1)S(1)} %collective-permute-done.23.refs_3_), channel_id=1, source_target_pairs={{0,1},{1,0},{2,3},{3,2},{4,5},{5,4},{6,7},{7,6},{8,9},{9,8},{10,11... | collective-permute-start | bytes 3145736 | tf_op jit(solution)/shard_map/ppermute | solution.py:443
  157.5 3.8 %collective-permute-start.29 = (bf16[512,1024]{1,0:T(8,128)(2,1)S(1)}, bf16[512,1024]{1,0:T(8,128)(2,1)S(1)}, u32[]{:S(2)}, u32[]{:S(2)}) collective-permute-start(bf16[512,1024]{1,0:T(8,128)(2,1)S(1)} %collective-permute-done.22.refs_5_), channel_id=1, source_target_pairs={{0,1},{1,0},{2,3},{3,2},{4,5},{5,4},{6,7},{7,6},{8,9},{9,8},{10,11... | collective-permute-start | bytes 3145736 | tf_op jit(solution)/shard_map/ppermute | solution.py:443
  157.5 14.4 %collective-permute-start.26 = (bf16[288,1024]{1,0:T(8,128)(2,1)S(1)}, bf16[288,1024]{1,0:T(8,128)(2,1)S(1)}, u32[]{:S(2)}, u32[]{:S(2)}) collective-permute-start(bf16[288,1024]{1,0:T(8,128)(2,1)S(1)} %slice.26), channel_id=1, source_target_pairs={{0,2},{1,3},{2,0},{3,1},{4,6},{5,7},{6,4},{7,5},{8,10},{9,11},{10,... | collective-permute-start | bytes 1769480 | tf_op jit(solution)/shard_map/ppermute | solution.py:456
  158.1 13.8 %collective-permute-start.27 = (bf16[224,1024]{1,0:T(8,128)(2,1)S(1)}, bf16[224,1024]{1,0:T(8,128)(2,1)S(1)}, u32[]{:S(2)}, u32[]{:S(2)}) collective-permute-start(bf16[224,1024]{1,0:T(8,128)(2,1)S(1)} %slice.27), channel_id=1, source_target_pairs={{0,4},{1,5},{2,6},{3,7},{4,8},{5,9},{6,10},{7,11},{8,12},{9,13},{1... | collective-permute-start | bytes 1376264 | tf_op jit(solution)/shard_map/ppermute | solution.py:457
  172.0 3.7 %collective-permute-start.30 = (bf16[288,1024]{1,0:T(8,128)(2,1)S(1)}, bf16[288,1024]{1,0:T(8,128)(2,1)S(1)}, u32[]{:S(2)}, u32[]{:S(2)}) collective-permute-start(bf16[288,1024]{1,0:T(8,128)(2,1)S(1)} %collective-permute-done.26.refs_3_), channel_id=1, source_target_pairs={{0,1},{1,0},{2,3},{3,2},{4,5},{5,4},{6,7},{7,6},{8,9},{9,8},{10,11... | collective-permute-start | bytes 1769480 | tf_op jit(solution)/shard_map/ppermute | solution.py:443
  173.3 2.3 %collective-permute-start.31 = (bf16[224,1024]{1,0:T(8,128)(2,1)S(1)}, bf16[224,1024]{1,0:T(8,128)(2,1)S(1)}, u32[]{:S(2)}, u32[]{:S(2)}) collective-permute-start(bf16[224,1024]{1,0:T(8,128)(2,1)S(1)} %collective-permute-done.27.refs_4_), channel_id=1, source_target_pairs={{0,1},{1,0},{2,3},{3,2},{4,5},{5,4},{6,7},{7,6},{8,9},{9,8},{10,11... | collective-permute-start | bytes 1376264 | tf_op jit(solution)/shard_map/ppermute | solution.py:443

commit v14 on v13

--- a/solution.py
+++ b/solution.py
@@ -17,6 +17,7 @@
 CHUNKS = ((0, KEY_VALUE_HEADS),)
 PLANE = 4
 PLANES = 4
+CYCLE = (0, 2, 3, 1)
 SAFE_POWER = 64.0
 GATHER_LIMIT = 40 * 2**20
 MASKED = -1e30
@@ -432,7 +433,7 @@
 
 
 def spread(block, ranks, held):
-    ring = [(rank, (rank + PLANE) % ranks) for rank in range(ranks)]
+    ring = ring_pairs(ranks)
     across = [(rank, rank ^ 2) for rank in range(ranks)]
     beside = [(rank, rank ^ 1) for rank in range(ranks)]
     steps = ranks // PLANE
@@ -462,25 +463,36 @@
     yield extra
 
 
-def source_order(ranks, sources):
+def ring_pairs(ranks, back=False):
+    pairs = []
+    for rank in range(ranks):
+        at = CYCLE.index(rank // PLANE) + (-1 if back else 1)
+        pairs.append((rank, CYCLE[at % PLANES] * PLANE + rank % PLANE))
+    return pairs
+
+
+def pick(table, index):
+    return sum(jnp.where(index == at, number, 0) for at, number in enumerate(table))
+
+
+def block_owners(steps, flips):
     me = lax.axis_index("dp")
     lane, plane = lax.rem(me, PLANE), lax.div(me, PLANE)
-    planes = ranks // PLANE
-    steps = np.array([source % planes for source in sources], np.int32)
-    flips = np.array([(0, 2, 1, 3)[source // planes] for source in sources], np.int32)
-    return lax.rem(plane + (planes - steps), planes) * PLANE + (lane ^ flips)
+    place = pick([CYCLE.index(at) for at in range(PLANES)], plane)
+    return pick(CYCLE, (place + PLANES - steps) % PLANES) * PLANE + (lane ^ flips)
+
+
+def source_order(ranks, sources):
+    steps = np.array([source % PLANES for source in sources], np.int32)
+    flips = np.array([(0, 2, 1, 3)[source // PLANES] for source in sources], np.int32)
+    return block_owners(steps, flips)
 
 
 def weight_order(ranks):
-    me = lax.axis_index("dp")
-    lane, plane = lax.rem(me, PLANE), lax.div(me, PLANE)
-    planes = ranks // PLANE
-    turn_back = lax.axis_index("groups") == 1
-    up = np.array([0, 1, 0, planes - 1, 2, 1, 2, planes - 1] * 2, np.int32)
-    steps = jnp.where(turn_back, (planes - up) % planes, up)
+    up = np.array([0, 1, 0, PLANES - 1, 2, 1, 2, PLANES - 1] * 2, np.int32)
+    steps = jnp.where(lax.axis_index("groups") == 1, (PLANES - up) % PLANES, up)
     flips = np.array([0, 0, 2, 0, 0, 2, 2, 2], np.int32)
-    flips = np.concatenate([flips, flips ^ 1])
-    return lax.rem(plane + (planes - steps), planes) * PLANE + (lane ^ flips)
+    return block_owners(steps, np.concatenate([flips, flips ^ 1]))
 
 
 def gather_plan(
@@ -519,8 +531,9 @@
     )(key_matrix, value_matrix)
     every = [(group, rank) for group in range(2) for rank in range(ranks)]
     ring = [
-        (group * ranks + rank, group * ranks + (rank + (1 - 2 * group) * PLANE) % ranks)
-        for group, rank in every
+        (group * ranks + rank, group * ranks + after)
+        for group in range(2)
+        for rank, after in ring_pairs(ranks, group == 1)
     ]
     across = [(group * ranks + rank, group * ranks + (rank ^ 2)) for group, rank in every]
     beside = [(group * ranks + rank, group * ranks + (rank ^ 1)) for group, rank in every]

time: 200 us -> 196 us (0.980)
  waiting for transfers between devices: 61.5 us -> 55.5 us
    ppermute x3, waiting for transfers between devices: 31.9 us -> 25.6 us  [spread(): lax.ppermute(lane, 'dp', ring)]
    ppermute x3, starting transfers between devices: 0.01 us -> 3.02 us  [spread(): lax.ppermute(lane, 'dp', ring)]
    ppermute x9, waiting for transfers between devices: 12.1 us -> 9.32 us  [keep(): lax.ppermute(array, 'dp', beside)]
    ppermute x15, starting transfers between devices: 15.7 us -> 13.1 us  [send(): return lax.ppermute(array, ('groups', 'dp'), pairs)]
    ppermute x3, waiting for transfers between devices: 0.01 us -> 2.08 us  [spread(): lax.ppermute(lane, 'dp', across)]
  transfers between devices with their start and end apart: 33 -> 33, of which waited for: 15 -> 18; matrix products, arithmetic and copies ran while one was open for 3% -> 3% of each run, Pallas kernels for 33% -> 33%
where the time goes in v14:
time: 196 us; the launch traced here: 195 us
  Pallas kernels  96.4 us (49%)
  waiting for transfers between devices  55.5 us (28%)
  starting transfers between devices  29.2 us (15%)
  local copies, waits for them, and re-layouts  12.8 us (7%)
    pallas_call x5, Pallas kernels, attend(): pl.pallas_call(functools.partial(attend_kernel, starts, sum((len(one) for...  66.7 us
    ppermute x3, waiting for transfers between devices, spread(): lax.ppermute(lane, 'dp', ring)  25.6 us
    ppermute x15, starting transfers between devices, send(): return lax.ppermute(array, ('groups', 'dp'), pairs)  13.1 us
    pallas_call x2, Pallas kernels, add_part(): pl.pallas_call(functools.partial(part_kernel, chips, bool(more)), out_sha...  10.2 us
    all_to_all x1, waiting for transfers between devices, gather_plan(): lax.all_to_all(jnp.broadcast_to(plan, (ranks, width + slots)), 'dp', spli...  9.9 us
    ppermute x9, waiting for transfers between devices, keep(): lax.ppermute(array, 'dp', beside)  9.32 us
    ppermute x15, waiting for transfers between devices, send(): return lax.ppermute(array, ('groups', 'dp'), pairs)  8.59 us
    pallas_call x1, Pallas kernels, gather_plan(): pl.pallas_call(functools.partial(query_kernel, ranks, spare, stride, pack...  7.06 us
  transfers between devices with their start and end apart: 33, of which 18 were waited for; matrix products, arithmetic and copies ran while one was open for 3% of the time, Pallas kernels for 33%

profile of v14, /device:TPU:1, one launch (start us, length us, event | category | flops | bytes accessed | tf_op | source)
XLA Modules:
  0.0 195.4 jit_solution(3246003251071041021)
XLA Ops:
  0.0 1.9 join.1.refs_0_
  2.1 3.8 %collective-permute-start.1 = (bf16[320,1024]{1,0:T(8,128)(2,1)}, bf16[320,1024]{1,0:T(8,128)(2,1)S(1)}, u32[]{:S(2)}, u32[]{:S(2)}) collective-permute-start(bf16[320,1024]{1,0:T(8,128)(2,1)} %join.1.refs_0_), channel_id=1, source_target_pairs={{0,8},{1,9},{2,10},{3,11},{4,0},{5,1},{6,2},{7,3},{8,12},{9,13},{1... | collective-permute-start | bytes 1966088 | tf_op jit(solution)/shard_map/ppermute | solution.py:543
  5.8 1.2 collective-permute-start
  9.9 3.9 %all-to-all-start = ((s32[16,1,1600]{2,1,0:T(1,128)}), s32[16,1,1600]{2,1,0:T(1,128)S(1)}, u32[]{:S(2)}, u32[]{:S(2)}) async-start(s32[16,1,1600]{2,1,0:T(1,128)} %broadcast_in_dim.26), calls=%async_computation | async-start | bytes 212992 | tf_op jit(solution)/shard_map/all_to_all | solution.py:562
  15.2 9.9 %all-to-all-done = s32[16,1,1600]{2,1,0:T(1,128)S(1)} async-done(((s32[16,1,1600]{2,1,0:T(1,128)}), s32[16,1,1600]{2,1,0:T(1,128)S(1)}, u32[]{:S(2)}, u32[]{:S(2)}) %all-to-all-start) | async-done | bytes 102432 | tf_op jit(solution)/shard_map/all_to_all | solution.py:562
  25.6 1.8 collective-permute-start.5
  28.2 0.9 collective-permute-start.7
  29.2 1.5 copy.34.route_ref
  31.5 1.0 copy-done.3
  32.5 1.7 copy-done.5
  34.3 7.1 %turn_queries.1 = (bf16[4,2816,128]{2,1,0:T(8,128)(2,1)S(1)}, s32[768,128]{1,0:T(8,128)S(1)}, f32[512,128]{1,0:T(8,128)S(1)}, f32[512,128]{1,0:T(8,128)S(1)}, s32[512,1]{1,0:T(8,128)S(1)}) custom-call(s32[512,1]{1,0:T(8,128)S(1)} %copy-done.3, s32[1,512]{1,0:T(1,128)S(1)} %get-tuple-element.80.seat_ref, s32[128,128]{1,0:T(8,128)S(1)} %reshape.69.positions_ref, ...), custom_call_target="tpu_custom_call" | custom-call | flops 4026531840 | bytes 5242880 | tf_op jit(solution)/shard_map/turn_queries/pallas_call | solution.py:583
  41.3 1.5 copy-done
  42.9 0.8 copy-done.6
  43.7 1.0 collective-permute-start.10
  45.2 1.5 collective-permute-start.8
  46.7 5.4 %add_part.2.refs_6_ = f32[512,1024]{1,0:T(8,128)S(1)} custom-call(s32[16]{0:T(128)S(1)} %fusion.9.owners_ref, bf16[512,5120]{1,0:T(8,128)(2,1)S(1)} %bitcast.12, bf16[320,1024]{1,0:T(8,128)(2,1)S(1)} %copy-done.2, bf16[320,1024]{1,0:T(8,128)(2,1)S(1)} %collective-permute-done.2.refs_1_, bf16[320,1024]{1,0:T(8,128)(2,1)S(1)} %collective-permute-done.1.refs_2_, ...), custom_call_target="tpu_custom_call" | custom-call | flops 2013265920 | bytes 10092544 | tf_op jit(solution)/shard_map/add_part/pallas_call | solution.py:626
  52.1 4.9 %add_part.3.refs_4_ = f32[512,1024]{1,0:T(8,128)S(1)} custom-call(s32[16]{0:T(128)S(1)} %fusion.9.owners_ref, bf16[512,5120]{1,0:T(8,128)(2,1)S(1)} %bitcast.12, bf16[320,1024]{1,0:T(8,128)(2,1)} %collective-permute-done.3.refs_0_, bf16[320,1024]{1,0:T(8,128)(2,1)S(1)} %collective-permute-done.10.refs_1_, bf16[320,1024]{1,0:T(8,128)(2,1)} %collective-permute-done.5.refs_2_, ...), custom_call_target="tpu_custom_call" | custom-call | flops 2013265920 | bytes 10092544 | tf_op jit(solution)/shard_map/add_part/pallas_call | solution.py:626
  57.0 4.8 %collective-permute-done.8.refs_0_ = bf16[320,1024]{1,0:T(8,128)(2,1)S(1)} collective-permute-done((bf16[320,1024]{1,0:T(8,128)(2,1)}, bf16[320,1024]{1,0:T(8,128)(2,1)S(1)}, u32[]{:S(2)}, u32[]{:S(2)}) %collective-permute-start.8) | collective-permute-done | bytes 655392 | tf_op jit(solution)/shard_map/ppermute | solution.py:543
  61.8 1.1 collective-permute-done.9.refs_2_
  62.9 1.1 collective-permute-start.13
  64.0 1.7 collective-permute-done.13.refs_1_
  65.7 0.9 collective-permute-done.14.refs_3_
  66.7 6.4 %finish.1.refs_3_ = bf16[512,1024]{1,0:T(8,128)(2,1)} custom-call(s32[16]{0:T(128)S(1)} %fusion.9.owners_ref, bf16[512,5120]{1,0:T(8,128)(2,1)S(1)} %bitcast.12, f32[1,1024]{1,0:T(1,128)S(1)} %maximum_convert_fusion.bias_ref, f32[512,128]{1,0:T(8,128)S(1)} %get-tuple-element.91.cosine_ref, f32[512,128]{1,0:T(8,128)S(1)} %get-tuple-element.92.sine_ref, ...), custom_call_target="tpu_custom_call" | custom-call | flops 1342177280 | bytes 8126464 | tf_op jit(solution)/shard_map/finish/pallas_call | solution.py:654
  73.5 0.8 collective-permute-start.16
  76.2 1.2 copy-done.7
  77.4 3.5 %veil.1 = (bf16[16,128,128]{2,1,0:T(8,128)(2,1)S(1)}, bf16[16,256,128]{2,1,0:T(8,128)(2,1)S(1)}, bf16[16,256,128]{2,1,0:T(8,128)(2,1)S(1)}, bf16[16,256,128]{2,1,0:T(8,128)(2,1)S(1)}, bf16[16,128,128]{2,1,0:T(8,128)(2,1)S(1)}) custom-call(s32[768,128]{1,0:T(8,128)S(1)} %copy-done.7, s32[16,1,512]{2,1,0:T(1,128)S(1)} %reshape.72.routes_ref, ...), custom_call_target="tpu_custom_call" | custom-call | flops 3000000000 | bytes 4194304 | tf_op jit(solution)/shard_map/veil/pallas_call | solution.py:683
  80.9 9.9 %attend.5 = (f32[4,2816,128]{2,1,0:T(8,128)S(1)}, f32[4,2816,128]{2,1,0:T(8,128)S(1)}, f32[4,2816,128]{2,1,0:T(8,128)S(1)}) custom-call(s32[512,1]{1,0:T(8,128)S(1)} %reshape.83.refs_0_, bf16[4,2816,128]{2,1,0:T(8,128)(2,1)S(1)} %copy-done.1, bf16[16,128,128]{2,1,0:T(8,128)(2,1)S(1)} %get-tuple-element.103.refs_2_, bf16[512,1024]{1,0:T(8,128)(2,1)} %finish.1.refs_3_, ...), custom_call_target="tpu_custom_call" | custom-call | flops 4429185024 | bytes 16777216 | tf_op jit(solution)/shard_map/attend/pallas_call | solution.py:726
  90.8 7.6 %collective-permute-done.16.refs_3_ = bf16[512,1024]{1,0:T(8,128)(2,1)} collective-permute-done((bf16[512,1024]{1,0:T(8,128)(2,1)}, bf16[512,1024]{1,0:T(8,128)(2,1)}, u32[]{:S(2)}, u32[]{:S(2)}) %collective-permute-start.16) | collective-permute-done | bytes 1048608 | tf_op jit(solution)/shard_map/ppermute | solution.py:451
  99.0 1.3 collective-permute-start.21
  100.2 0.9 collective-permute-start.19
  101.6 1.1 collective-permute-done.21.refs_6_
  102.7 1.5 collective-permute-done.20.refs_4_
  104.2 12.2 %attend.6 = (f32[4,2816,128]{2,1,0:T(8,128)S(1)}, f32[4,2816,128]{2,1,0:T(8,128)S(1)}, f32[4,2816,128]{2,1,0:T(8,128)S(1)}) custom-call(s32[512,1]{1,0:T(8,128)S(1)} %reshape.83.refs_0_, bf16[4,2816,128]{2,1,0:T(8,128)(2,1)S(1)} %copy-done.1, ...), custom_call_target="tpu_custom_call", output_to_operand_aliasing={{0}: (7, {}), {1}: (8, {}), {2}: (9, {})} | custom-call | flops 5905580032 | bytes 33554432 | tf_op jit(solution)/shard_map/attend/pallas_call | solution.py:726
  116.4 8.3 %collective-permute-done.19.refs_3_ = bf16[512,1024]{1,0:T(8,128)(2,1)S(1)} collective-permute-done((bf16[512,1024]{1,0:T(8,128)(2,1)}, bf16[512,1024]{1,0:T(8,128)(2,1)S(1)}, u32[]{:S(2)}, u32[]{:S(2)}) %collective-permute-start.19) | collective-permute-done | bytes 1048608 | tf_op jit(solution)/shard_map/ppermute | solution.py:451
  125.2 1.7 collective-permute-start.25
  126.9 1.3 collective-permute-start.23
  129.2 1.5 collective-permute-done.24.refs_4_
  130.7 10.7 %attend.7 = (f32[4,2816,128]{2,1,0:T(8,128)S(1)}, f32[4,2816,128]{2,1,0:T(8,128)S(1)}, f32[4,2816,128]{2,1,0:T(8,128)S(1)}) custom-call(s32[512,1]{1,0:T(8,128)S(1)} %reshape.83.refs_0_, bf16[4,2816,128]{2,1,0:T(8,128)(2,1)S(1)} %copy-done.1, ...), custom_call_target="tpu_custom_call", output_to_operand_aliasing={{0}: (7, {}), {1}: (8, {}), {2}: (9, {})} | custom-call | flops 5905580032 | bytes 33554432 | tf_op jit(solution)/shard_map/attend/pallas_call | solution.py:726
  141.4 9.8 %collective-permute-done.23.refs_3_ = bf16[512,1024]{1,0:T(8,128)(2,1)S(1)} collective-permute-done((bf16[512,1024]{1,0:T(8,128)(2,1)S(1)}, bf16[512,1024]{1,0:T(8,128)(2,1)S(1)}, u32[]{:S(2)}, u32[]{:S(2)}) %collective-permute-start.23) | collective-permute-done | bytes 1048608 | tf_op jit(solution)/shard_map/ppermute | solution.py:451
  151.1 1.0 collective-permute-done.22.refs_5_
  152.1 1.7 collective-permute-start.28
  154.3 1.0 collective-permute-start.27
  155.2 0.8 collective-permute-done.28.refs_4_
  156.1 1.5 collective-permute-done.29.refs_6_
  157.6 10.7 %attend.8 = (f32[4,2816,128]{2,1,0:T(8,128)S(1)}, f32[4,2816,128]{2,1,0:T(8,128)S(1)}, f32[4,2816,128]{2,1,0:T(8,128)S(1)}) custom-call(s32[512,1]{1,0:T(8,128)S(1)} %reshape.83.refs_0_, bf16[4,2816,128]{2,1,0:T(8,128)(2,1)S(1)} %copy-done.1, ...), custom_call_target="tpu_custom_call", output_to_operand_aliasing={{0}: (7, {}), {1}: (8, {}), {2}: (9, {})} | custom-call | flops 5905580032 | bytes 33554432 | tf_op jit(solution)/shard_map/attend/pallas_call | solution.py:726
  168.3 1.4 collective-permute-start.30
  169.6 2.3 %collective-permute-done.31.refs_6_ = bf16[224,1024]{1,0:T(8,128)(2,1)S(1)} collective-permute-done((bf16[224,1024]{1,0:T(8,128)(2,1)S(1)}, bf16[224,1024]{1,0:T(8,128)(2,1)S(1)}, u32[]{:S(2)}, u32[]{:S(2)}) %collective-permute-start.31) | collective-permute-done | bytes 458784 | tf_op jit(solution)/shard_map/ppermute | solution.py:444
  171.9 23.3 %attend.9 = (bf16[512,2560]{1,0:T(8,128)(2,1)}, f32[4,2816,128]{2,1,0:T(8,128)S(1)}, f32[4,2816,128]{2,1,0:T(8,128)S(1)}, f32[4,2816,128]{2,1,0:T(8,128)S(1)}) custom-call(s32[512,1]{1,0:T(8,128)S(1)} %reshape.83.refs_0_, bf16[4,2816,128]{2,1,0:T(8,128)(2,1)S(1)} %copy-done.1, ...), custom_call_target="tpu_custom_call", output_to_operand_aliasing={{1}: (7, {}), {2}: (8, {}), {3}: (9, {})} | custom-call | flops 4429185024 | bytes 16777216 | tf_op jit(solution)/shard_map/attend/pallas_call | solution.py:726
  (81 shorter events, 12.4 us)
Async XLA Ops:
  1.9 23.2 %collective-permute-start.2 = (bf16[320,1024]{1,0:T(8,128)(2,1)}, bf16[320,1024]{1,0:T(8,128)(2,1)S(1)}, u32[]{:S(2)}, u32[]{:S(2)}) collective-permute-start(bf16[320,1024]{1,0:T(8,128)(2,1)} %join.1.refs_0_), channel_id=1, source_target_pairs={{0,1},{1,0},{2,3},{3,2},{4,5},{5,4},{6,7},{7,6},{8,9},{9,8},{10,11... | collective-permute-start | bytes 1966088 | tf_op jit(solution)/shard_map/ppermute | solution.py:543
  2.1 23.1 %collective-permute-start.1 = (bf16[320,1024]{1,0:T(8,128)(2,1)}, bf16[320,1024]{1,0:T(8,128)(2,1)S(1)}, u32[]{:S(2)}, u32[]{:S(2)}) collective-permute-start(bf16[320,1024]{1,0:T(8,128)(2,1)} %join.1.refs_0_), channel_id=1, source_target_pairs={{0,8},{1,9},{2,10},{3,11},{4,0},{5,1},{6,2},{7,3},{8,12},{9,13},{1... | collective-permute-start | bytes 1966088 | tf_op jit(solution)/shard_map/ppermute | solution.py:543
  5.8 19.4 %collective-permute-start = (bf16[320,1024]{1,0:T(8,128)(2,1)}, bf16[320,1024]{1,0:T(8,128)(2,1)S(1)}, u32[]{:S(2)}, u32[]{:S(2)}) collective-permute-start(bf16[320,1024]{1,0:T(8,128)(2,1)} %join.1.refs_0_), channel_id=1, source_target_pairs={{0,2},{1,3},{2,0},{3,1},{4,6},{5,7},{6,4},{7,5},{8,10},{9,11},{10,... | collective-permute-start | bytes 1966088 | tf_op jit(solution)/shard_map/ppermute | solution.py:543
  7.1 0.7 copy-start.4
  9.9 15.2 %all-to-all-start = ((s32[16,1,1600]{2,1,0:T(1,128)}), s32[16,1,1600]{2,1,0:T(1,128)S(1)}, u32[]{:S(2)}, u32[]{:S(2)}) async-start(s32[16,1,1600]{2,1,0:T(1,128)} %broadcast_in_dim.26), calls=%async_computation | async-start | bytes 212992 | tf_op jit(solution)/shard_map/all_to_all | solution.py:562
  25.2 18.5 %collective-permute-start.6 = (bf16[320,1024]{1,0:T(8,128)(2,1)S(1)}, bf16[320,1024]{1,0:T(8,128)(2,1)}, u32[]{:S(2)}, u32[]{:S(2)}) collective-permute-start(bf16[320,1024]{1,0:T(8,128)(2,1)S(1)} %collective-permute-done.1.refs_2_), channel_id=1, source_target_pairs={{0,1},{1,0},{2,3},{3,2},{4,5},{5,4},{6,7},{7,6},{8,9},{9,8},{10,11... | collective-permute-start | bytes 1966088 | tf_op jit(solution)/shard_map/ppermute | solution.py:543
  25.6 18.0 %collective-permute-start.5 = (bf16[320,1024]{1,0:T(8,128)(2,1)S(1)}, bf16[320,1024]{1,0:T(8,128)(2,1)}, u32[]{:S(2)}, u32[]{:S(2)}) collective-permute-start(bf16[320,1024]{1,0:T(8,128)(2,1)S(1)} %collective-permute-done.1.refs_2_), channel_id=1, source_target_pairs={{0,8},{1,9},{2,10},{3,11},{4,0},{5,1},{6,2},{7,3},{8,12},{9,13},{1... | collective-permute-start | bytes 1966088 | tf_op jit(solution)/shard_map/ppermute | solution.py:543
  27.4 16.2 %collective-permute-start.4 = (bf16[320,1024]{1,0:T(8,128)(2,1)S(1)}, bf16[320,1024]{1,0:T(8,128)(2,1)}, u32[]{:S(2)}, u32[]{:S(2)}) collective-permute-start(bf16[320,1024]{1,0:T(8,128)(2,1)S(1)} %collective-permute-done.1.refs_2_), channel_id=1, source_target_pairs={{0,2},{1,3},{2,0},{3,1},{4,6},{5,7},{6,4},{7,5},{8,10},{9,11},{10,... | collective-permute-start | bytes 1966088 | tf_op jit(solution)/shard_map/ppermute | solution.py:543
  27.4 16.3 %collective-permute-start.3 = (bf16[320,1024]{1,0:T(8,128)(2,1)S(1)}, bf16[320,1024]{1,0:T(8,128)(2,1)}, u32[]{:S(2)}, u32[]{:S(2)}) collective-permute-start(bf16[320,1024]{1,0:T(8,128)(2,1)S(1)} %collective-permute-done.1.refs_2_), channel_id=1, source_target_pairs={{0,16},{1,17},{2,18},{3,19},{4,20},{5,21},{6,22},{7,23},{8,24},{9,... | collective-permute-start | bytes 1966088 | tf_op jit(solution)/shard_map/ppermute | solution.py:543
  28.2 15.5 %collective-permute-start.7 = (bf16[320,1024]{1,0:T(8,128)(2,1)S(1)}, bf16[320,1024]{1,0:T(8,128)(2,1)}, u32[]{:S(2)}, u32[]{:S(2)}) collective-permute-start(bf16[320,1024]{1,0:T(8,128)(2,1)S(1)} %collective-permute-done.refs_4_), channel_id=1, source_target_pairs={{0,1},{1,0},{2,3},{3,2},{4,5},{5,4},{6,7},{7,6},{8,9},{9,8},{10,11... | collective-permute-start | bytes 1966088 | tf_op jit(solution)/shard_map/ppermute | solution.py:543
  31.4 15.3 %slice-start = ((s8[5242880]{0:T(1024)(128)(4,1)}), s8[1048576]{0:T(1024)(128)(4,1)S(1)}, s32[]{:S(2)}) async-start(s8[5242880]{0:T(1024)(128)(4,1)} %bitcast.11), calls=%async_computation.1 | async-start | bytes 2097152
  31.5 1.0 copy-start.3
  32.5 1.7 copy-start.5
  34.3 12.4 %slice-start.1 = ((s8[5242880]{0:T(1024)(128)(4,1)}), s8[4194304]{0:T(1024)(128)(4,1)S(1)}, s32[]{:S(2)}) async-start(s8[5242880]{0:T(1024)(128)(4,1)} %bitcast.11), calls=%async_computation.2 | async-start | bytes 8388608
  34.3 12.4 %copy-start.2 = (bf16[320,1024]{1,0:T(8,128)(2,1)S(1)}, bf16[320,1024]{1,0:T(8,128)(2,1)}, u32[]{:S(2)}) copy-start(bf16[320,1024]{1,0:T(8,128)(2,1)} %join.1.refs_0_) | copy-start | bytes 1966084
  41.3 1.6 copy-start
  42.9 0.8 copy-start.6
  43.7 8.4 %collective-permute-start.10 = (bf16[320,1024]{1,0:T(8,128)(2,1)}, bf16[320,1024]{1,0:T(8,128)(2,1)S(1)}, u32[]{:S(2)}, u32[]{:S(2)}) collective-permute-start(bf16[320,1024]{1,0:T(8,128)(2,1)} %collective-permute-done.3.refs_0_), channel_id=1, source_target_pairs={{0,1},{1,0},{2,3},{3,2},{4,5},{5,4},{6,7},{7,6},{8,9},{9,8},{10,11... | collective-permute-start | bytes 1966088 | tf_op jit(solution)/shard_map/ppermute | solution.py:543
  44.7 7.4 %collective-permute-start.11 = (bf16[320,1024]{1,0:T(8,128)(2,1)}, bf16[320,1024]{1,0:T(8,128)(2,1)S(1)}, u32[]{:S(2)}, u32[]{:S(2)}) collective-permute-start(bf16[320,1024]{1,0:T(8,128)(2,1)} %collective-permute-done.5.refs_2_), channel_id=1, source_target_pairs={{0,1},{1,0},{2,3},{3,2},{4,5},{5,4},{6,7},{7,6},{8,9},{9,8},{10,11... | collective-permute-start | bytes 1966088 | tf_op jit(solution)/shard_map/ppermute | solution.py:543
  44.7 7.4 %collective-permute-start.12 = (bf16[320,1024]{1,0:T(8,128)(2,1)}, bf16[320,1024]{1,0:T(8,128)(2,1)S(1)}, u32[]{:S(2)}, u32[]{:S(2)}) collective-permute-start(bf16[320,1024]{1,0:T(8,128)(2,1)} %collective-permute-done.4.refs_4_), channel_id=1, source_target_pairs={{0,1},{1,0},{2,3},{3,2},{4,5},{5,4},{6,7},{7,6},{8,9},{9,8},{10,11... | collective-permute-start | bytes 1966088 | tf_op jit(solution)/shard_map/ppermute | solution.py:543
  45.2 16.6 %collective-permute-start.8 = (bf16[320,1024]{1,0:T(8,128)(2,1)}, bf16[320,1024]{1,0:T(8,128)(2,1)S(1)}, u32[]{:S(2)}, u32[]{:S(2)}) collective-permute-start(bf16[320,1024]{1,0:T(8,128)(2,1)} %collective-permute-done.5.refs_2_), channel_id=1, source_target_pairs={{0,2},{1,3},{2,0},{3,1},{4,6},{5,7},{6,4},{7,5},{8,10},{9,11},{10,... | collective-permute-start | bytes 1966088 | tf_op jit(solution)/shard_map/ppermute | solution.py:543
  46.6 16.3 %collective-permute-start.9 = (bf16[320,1024]{1,0:T(8,128)(2,1)}, bf16[320,1024]{1,0:T(8,128)(2,1)S(1)}, u32[]{:S(2)}, u32[]{:S(2)}) collective-permute-start(bf16[320,1024]{1,0:T(8,128)(2,1)} %collective-permute-done.4.refs_4_), channel_id=1, source_target_pairs={{0,16},{1,17},{2,18},{3,19},{4,20},{5,21},{6,22},{7,23},{8,24},{9,... | collective-permute-start | bytes 1966088 | tf_op jit(solution)/shard_map/ppermute | solution.py:543
  57.0 17.9 %copy-start.8 = (s32[16]{0:T(128)S(1)}, s32[16]{0:T(128)}, u32[]{:S(2)}) copy-start(s32[16]{0:T(128)} %constant.68) | copy-start | bytes 196
  57.0 17.9 %copy-start.9 = (s32[16]{0:T(128)S(1)}, s32[16]{0:T(128)}, u32[]{:S(2)}) copy-start(s32[16]{0:T(128)} %constant.67.clone) | copy-start | bytes 196
  62.9 2.8 %collective-permute-start.13 = (bf16[320,1024]{1,0:T(8,128)(2,1)S(1)}, bf16[320,1024]{1,0:T(8,128)(2,1)S(1)}, u32[]{:S(2)}, u32[]{:S(2)}) collective-permute-start(bf16[320,1024]{1,0:T(8,128)(2,1)S(1)} %collective-permute-done.8.refs_0_), channel_id=1, source_target_pairs={{0,1},{1,0},{2,3},{3,2},{4,5},{5,4},{6,7},{7,6},{8,9},{9,8},{10,11... | collective-permute-start | bytes 1966088 | tf_op jit(solution)/shard_map/ppermute | solution.py:543
  64.0 2.7 %collective-permute-start.14 = (bf16[320,1024]{1,0:T(8,128)(2,1)S(1)}, bf16[320,1024]{1,0:T(8,128)(2,1)S(1)}, u32[]{:S(2)}, u32[]{:S(2)}) collective-permute-start(bf16[320,1024]{1,0:T(8,128)(2,1)S(1)} %collective-permute-done.9.refs_2_), channel_id=1, source_target_pairs={{0,1},{1,0},{2,3},{3,2},{4,5},{5,4},{6,7},{7,6},{8,9},{9,8},{10,11... | collective-permute-start | bytes 1966088 | tf_op jit(solution)/shard_map/ppermute | solution.py:543
  73.0 7.8 %collective-permute-start.17 = (bf16[512,1024]{1,0:T(8,128)(2,1)}, bf16[512,1024]{1,0:T(8,128)(2,1)}, u32[]{:S(2)}, u32[]{:S(2)}) collective-permute-start(bf16[512,1024]{1,0:T(8,128)(2,1)} %finish.1.refs_3_), channel_id=1, source_target_pairs={{0,1},{1,0},{2,3},{3,2},{4,5},{5,4},{6,7},{7,6},{8,9},{9,8},{10,11... | collective-permute-start | bytes 3145736 | tf_op jit(solution)/shard_map/ppermute | solution.py:444
  73.5 24.9 %collective-permute-start.16 = (bf16[512,1024]{1,0:T(8,128)(2,1)}, bf16[512,1024]{1,0:T(8,128)(2,1)}, u32[]{:S(2)}, u32[]{:S(2)}) collective-permute-start(bf16[512,1024]{1,0:T(8,128)(2,1)} %finish.1.refs_3_), channel_id=1, source_target_pairs={{0,8},{1,9},{2,10},{3,11},{4,0},{5,1},{6,2},{7,3},{8,12},{9,13},{1... | collective-permute-start | bytes 3145736 | tf_op jit(solution)/shard_map/ppermute | solution.py:451
  74.3 24.6 %collective-permute-start.15 = (bf16[512,1024]{1,0:T(8,128)(2,1)}, bf16[512,1024]{1,0:T(8,128)(2,1)}, u32[]{:S(2)}, u32[]{:S(2)}) collective-permute-start(bf16[512,1024]{1,0:T(8,128)(2,1)} %finish.1.refs_3_), channel_id=1, source_target_pairs={{0,2},{1,3},{2,0},{3,1},{4,6},{5,7},{6,4},{7,5},{8,10},{9,11},{10,... | collective-permute-start | bytes 3145736 | tf_op jit(solution)/shard_map/ppermute | solution.py:451
  75.8 5.1 %copy-start.1 = (bf16[4,2816,128]{2,1,0:T(8,128)(2,1)S(1)}, bf16[4,2816,128]{2,1,0:T(8,128)(2,1)}, u32[]{:S(2)}) copy-start(bf16[4,2816,128]{2,1,0:T(8,128)(2,1)} %copy-done) | copy-start | bytes 8650756
  76.2 1.2 copy-start.7
  99.0 3.8 %collective-permute-start.21 = (bf16[512,1024]{1,0:T(8,128)(2,1)}, bf16[512,1024]{1,0:T(8,128)(2,1)S(1)}, u32[]{:S(2)}, u32[]{:S(2)}) collective-permute-start(bf16[512,1024]{1,0:T(8,128)(2,1)} %collective-permute-done.15.refs_5_), channel_id=1, source_target_pairs={{0,1},{1,0},{2,3},{3,2},{4,5},{5,4},{6,7},{7,6},{8,9},{9,8},{10,11... | collective-permute-start | bytes 3145736 | tf_op jit(solution)/shard_map/ppermute | solution.py:444
  100.2 4.0 %collective-permute-start.20 = (bf16[512,1024]{1,0:T(8,128)(2,1)}, bf16[512,1024]{1,0:T(8,128)(2,1)S(1)}, u32[]{:S(2)}, u32[]{:S(2)}) collective-permute-start(bf16[512,1024]{1,0:T(8,128)(2,1)} %collective-permute-done.16.refs_3_), channel_id=1, source_target_pairs={{0,1},{1,0},{2,3},{3,2},{4,5},{5,4},{6,7},{7,6},{8,9},{9,8},{10,11... | collective-permute-start | bytes 3145736 | tf_op jit(solution)/shard_map/ppermute | solution.py:444
  100.2 24.4 %collective-permute-start.19 = (bf16[512,1024]{1,0:T(8,128)(2,1)}, bf16[512,1024]{1,0:T(8,128)(2,1)S(1)}, u32[]{:S(2)}, u32[]{:S(2)}) collective-permute-start(bf16[512,1024]{1,0:T(8,128)(2,1)} %collective-permute-done.16.refs_3_), channel_id=1, source_target_pairs={{0,8},{1,9},{2,10},{3,11},{4,0},{5,1},{6,2},{7,3},{8,12},{9,13},{1... | collective-permute-start | bytes 3145736 | tf_op jit(solution)/shard_map/ppermute | solution.py:451
  101.1 24.1 %collective-permute-start.18 = (bf16[512,1024]{1,0:T(8,128)(2,1)}, bf16[512,1024]{1,0:T(8,128)(2,1)S(1)}, u32[]{:S(2)}, u32[]{:S(2)}) collective-permute-start(bf16[512,1024]{1,0:T(8,128)(2,1)} %collective-permute-done.16.refs_3_), channel_id=1, source_target_pairs={{0,2},{1,3},{2,0},{3,1},{4,6},{5,7},{6,4},{7,5},{8,10},{9,11},{10,... | collective-permute-start | bytes 3145736 | tf_op jit(solution)/shard_map/ppermute | solution.py:451
  125.2 4.0 %collective-permute-start.25 = (bf16[512,1024]{1,0:T(8,128)(2,1)S(1)}, bf16[512,1024]{1,0:T(8,128)(2,1)S(1)}, u32[]{:S(2)}, u32[]{:S(2)}) collective-permute-start(bf16[512,1024]{1,0:T(8,128)(2,1)S(1)} %collective-permute-done.18.refs_5_), channel_id=1, source_target_pairs={{0,1},{1,0},{2,3},{3,2},{4,5},{5,4},{6,7},{7,6},{8,9},{9,8},{10,11... | collective-permute-start | bytes 3145736 | tf_op jit(solution)/shard_map/ppermute | solution.py:444
  126.9 3.8 %collective-permute-start.24 = (bf16[512,1024]{1,0:T(8,128)(2,1)S(1)}, bf16[512,1024]{1,0:T(8,128)(2,1)S(1)}, u32[]{:S(2)}, u32[]{:S(2)}) collective-permute-start(bf16[512,1024]{1,0:T(8,128)(2,1)S(1)} %collective-permute-done.19.refs_3_), channel_id=1, source_target_pairs={{0,1},{1,0},{2,3},{3,2},{4,5},{5,4},{6,7},{7,6},{8,9},{9,8},{10,11... | collective-permute-start | bytes 3145736 | tf_op jit(solution)/shard_map/ppermute | solution.py:444
  126.9 24.2 %collective-permute-start.23 = (bf16[512,1024]{1,0:T(8,128)(2,1)S(1)}, bf16[512,1024]{1,0:T(8,128)(2,1)S(1)}, u32[]{:S(2)}, u32[]{:S(2)}) collective-permute-start(bf16[512,1024]{1,0:T(8,128)(2,1)S(1)} %collective-permute-done.19.refs_3_), channel_id=1, source_target_pairs={{0,8},{1,9},{2,10},{3,11},{4,0},{5,1},{6,2},{7,3},{8,12},{9,13},{1... | collective-permute-start | bytes 3145736 | tf_op jit(solution)/shard_map/ppermute | solution.py:451
  128.2 23.9 %collective-permute-start.22 = (bf16[512,1024]{1,0:T(8,128)(2,1)S(1)}, bf16[512,1024]{1,0:T(8,128)(2,1)S(1)}, u32[]{:S(2)}, u32[]{:S(2)}) collective-permute-start(bf16[512,1024]{1,0:T(8,128)(2,1)S(1)} %collective-permute-done.19.refs_3_), channel_id=1, source_target_pairs={{0,2},{1,3},{2,0},{3,1},{4,6},{5,7},{6,4},{7,5},{8,10},{9,11},{10,... | collective-permute-start | bytes 3145736 | tf_op jit(solution)/shard_map/ppermute | solution.py:451
  152.1 4.0 %collective-permute-start.28 = (bf16[512,1024]{1,0:T(8,128)(2,1)S(1)}, bf16[512,1024]{1,0:T(8,128)(2,1)S(1)}, u32[]{:S(2)}, u32[]{:S(2)}) collective-permute-start(bf16[512,1024]{1,0:T(8,128)(2,1)S(1)} %collective-permute-done.23.refs_3_), channel_id=1, source_target_pairs={{0,1},{1,0},{2,3},{3,2},{4,5},{5,4},{6,7},{7,6},{8,9},{9,8},{10,11... | collective-permute-start | bytes 3145736 | tf_op jit(solution)/shard_map/ppermute | solution.py:444
  153.8 3.8 %collective-permute-start.29 = (bf16[512,1024]{1,0:T(8,128)(2,1)S(1)}, bf16[512,1024]{1,0:T(8,128)(2,1)S(1)}, u32[]{:S(2)}, u32[]{:S(2)}) collective-permute-start(bf16[512,1024]{1,0:T(8,128)(2,1)S(1)} %collective-permute-done.22.refs_5_), channel_id=1, source_target_pairs={{0,1},{1,0},{2,3},{3,2},{4,5},{5,4},{6,7},{7,6},{8,9},{9,8},{10,11... | collective-permute-start | bytes 3145736 | tf_op jit(solution)/shard_map/ppermute | solution.py:444
  153.8 14.4 %collective-permute-start.26 = (bf16[288,1024]{1,0:T(8,128)(2,1)S(1)}, bf16[288,1024]{1,0:T(8,128)(2,1)S(1)}, u32[]{:S(2)}, u32[]{:S(2)}) collective-permute-start(bf16[288,1024]{1,0:T(8,128)(2,1)S(1)} %slice.26), channel_id=1, source_target_pairs={{0,2},{1,3},{2,0},{3,1},{4,6},{5,7},{6,4},{7,5},{8,10},{9,11},{10,... | collective-permute-start | bytes 1769480 | tf_op jit(solution)/shard_map/ppermute | solution.py:457
  154.3 14.0 %collective-permute-start.27 = (bf16[224,1024]{1,0:T(8,128)(2,1)S(1)}, bf16[224,1024]{1,0:T(8,128)(2,1)S(1)}, u32[]{:S(2)}, u32[]{:S(2)}) collective-permute-start(bf16[224,1024]{1,0:T(8,128)(2,1)S(1)} %slice.27), channel_id=1, source_target_pairs={{0,8},{1,9},{2,10},{3,11},{4,0},{5,1},{6,2},{7,3},{8,12},{9,13},{1... | collective-permute-start | bytes 1376264 | tf_op jit(solution)/shard_map/ppermute | solution.py:458
  168.3 3.7 %collective-permute-start.30 = (bf16[288,1024]{1,0:T(8,128)(2,1)S(1)}, bf16[288,1024]{1,0:T(8,128)(2,1)S(1)}, u32[]{:S(2)}, u32[]{:S(2)}) collective-permute-start(bf16[288,1024]{1,0:T(8,128)(2,1)S(1)} %collective-permute-done.26.refs_3_), channel_id=1, source_target_pairs={{0,1},{1,0},{2,3},{3,2},{4,5},{5,4},{6,7},{7,6},{8,9},{9,8},{10,11... | collective-permute-start | bytes 1769480 | tf_op jit(solution)/shard_map/ppermute | solution.py:444
  169.6 2.3 %collective-permute-start.31 = (bf16[224,1024]{1,0:T(8,128)(2,1)S(1)}, bf16[224,1024]{1,0:T(8,128)(2,1)S(1)}, u32[]{:S(2)}, u32[]{:S(2)}) collective-permute-start(bf16[224,1024]{1,0:T(8,128)(2,1)S(1)} %collective-permute-done.27.refs_4_), channel_id=1, source_target_pairs={{0,1},{1,0},{2,3},{3,2},{4,5},{5,4},{6,7},{7,6},{8,9},{9,8},{10,11... | collective-permute-start | bytes 1376264 | tf_op jit(solution)/shard_map/ppermute | solution.py:444

commit v15 on v14

--- a/solution.py
+++ b/solution.py
@@ -59,6 +59,23 @@
     copies = [
         pltpu.make_async_copy(ref, out_ref.at[:, pl.ds(at * wide, wide)], done.at[at])
         for at, ref in enumerate((left_ref, right_ref))
+    ]
+    for copy in copies:
+        copy.start()
+    for copy in copies:
+        copy.wait()
+
+
+def cut_kernel(split_at, far_ref, next_ref, near_ref, top_ref, rest_ref, done):
+    below = far_ref.shape[0] - split_at
+    copies = [
+        pltpu.make_async_copy(near_ref.at[pl.ds(0, split_at)], top_ref, done.at[0]),
+        pltpu.make_async_copy(
+            next_ref.at[pl.ds(split_at, below)], rest_ref.at[pl.ds(0, below)], done.at[1]
+        ),
+        pltpu.make_async_copy(
+            far_ref.at[pl.ds(split_at, below)], rest_ref.at[pl.ds(below, below)], done.at[2]
+        ),
     ]
     for copy in copies:
         copy.start()
@@ -214,12 +231,20 @@
 def finish_kernel(
     chips, owners_ref, hidden_ref, bias_ref, cosine_ref, sine_ref, bucket_ref, *refs
 ):
-    count = 2 * len(chips)
+    count = 3 * len(chips)
     parts, total_ref = refs[:count], refs[count]
     outs, (columns, matrix, done) = refs[count + 1 : -3], refs[-3:]
     copies = fetch_columns(chips, owners_ref, hidden_ref, columns, done)
-    for ref, rows in zip(parts, place_rows(owners_ref, chips, matrix)):
-        matrix[rows] = ref[...]
+    split_at, below = parts[0].shape[0], parts[2].shape[0] // 2
+    shard = split_at + below
+    for side in range(2):
+        rest = parts[3 * side + 2]
+        for place, chip in enumerate(chips):
+            first = (2 * place + lax.rem(owners_ref[chip[side]], 2)) * shard
+            matrix[pl.ds(pl.multiple_of(first, 16), split_at)] = parts[3 * side + place][...]
+            matrix[pl.ds(pl.multiple_of(first + split_at, 16), below)] = rest[
+                place * below : (place + 1) * below
+            ]
     places = one_hot_rows(outs[0].shape[0], bucket_ref[...])
     for copy in copies:
         copy.wait()
@@ -437,7 +462,7 @@
     across = [(rank, rank ^ 2) for rank in range(ranks)]
     beside = [(rank, rank ^ 1) for rank in range(ranks)]
     steps = ranks // PLANE
-    half = block.shape[0] // 32 * 18
+    half = block.shape[0] // 32 * 16
 
     def keep(source, first, array):
         held.setdefault(source, []).append((first, array))
@@ -609,11 +634,11 @@
         chips = [(source, source + ranks // 2) for source in sources]
         return chips, [array for source in sources for array in matrices[source]]
 
-    def scratch(chips, arrays):
+    def scratch(chips):
         return [
             pltpu.VMEM((rows, 2 * shard * len(chips)), jnp.bfloat16),
             pltpu.VMEM((2 * shard * len(chips), wide), jnp.bfloat16),
-            pltpu.SemaphoreType.DMA((len(chips) + len(arrays),)),
+            pltpu.SemaphoreType.DMA((3 * len(chips),)),
         ]
 
     def product_cost(chips):
@@ -628,7 +653,7 @@
             out_shape=shape((rows, wide), jnp.float32),
             in_specs=[SMEM] + [HBM] * (1 + len(arrays)) + [VMEM] * len(more),
             out_specs=VMEM,
-            scratch_shapes=scratch(chips, arrays),
+            scratch_shapes=scratch(chips),
             compiler_params=grant(14),
             cost_estimate=product_cost(chips),
             name="add_part",
@@ -644,13 +669,30 @@
     matrices[1], matrices[2] = (near_lane, swaps[0]), (other_row, swaps[1])
     matrices[3] = (far_lane, send(far_lane, beside))
     matrices[4] = (next_lane, send(next_lane, beside))
+    split_at = shard * 21 // 32 // 16 * 16
+    below = shard - split_at
+    top, rest = pl.pallas_call(
+        functools.partial(cut_kernel, split_at),
+        out_shape=(
+            shape((split_at, wide), jnp.bfloat16),
+            shape((2 * below, wide), jnp.bfloat16),
+        ),
+        in_specs=[HBM] * 3,
+        out_specs=(VMEM,) * 2,
+        scratch_shapes=[pltpu.SemaphoreType.DMA((3,))],
+        compiler_params=grant(14),
+        name="cut",
+    )(far_lane, next_lane, near_other)
+    top, rest, owners = lax.optimization_barrier((top, rest, owners))
     matrices[5] = (near_other, send(near_other, beside))
-    far_other, next_other = send(near_other, swap), send(next_lane, across)
+    far_top, both_rest, next_top = send(top, swap), send(rest, across), send(top, ring)
     total = add_part(add_part(None, (0, 1, 2)), (3, 4, 5))
-    next_other, far_other, total = lax.optimization_barrier((next_other, far_other, total))
-    matrices[6] = (next_other, send(next_other, beside))
-    matrices[7] = (far_other, send(far_other, beside))
-    chips, arrays = chip_parts((6, 7))
+    both_rest, far_top, next_top, total = lax.optimization_barrier(
+        (both_rest, far_top, next_top, total)
+    )
+    arrays = [next_top, far_top, both_rest]
+    arrays += [send(array, beside) for array in arrays]
+    chips = [(source, source + ranks // 2) for source in (6, 7)]
     (pairs,) = pl.pallas_call(
         functools.partial(finish_kernel, chips),
         out_shape=tuple(
@@ -658,7 +700,7 @@
         ),
         in_specs=[SMEM, HBM] + [VMEM] * (5 + len(arrays)),
         out_specs=(VMEM,) * len(CHUNKS),
-        scratch_shapes=scratch(chips, arrays),
+        scratch_shapes=scratch(chips),
         compiler_params=grant(14),
         cost_estimate=product_cost(chips),
         name="finish",

time: 196 us -> 193 us (0.985)
  waiting for transfers between devices: 55.5 us -> 50.7 us
  starting transfers between devices: 29.2 us -> 31.8 us
    ppermute x15 -> x17, waiting for transfers between devices: 8.59 us -> 3.76 us  [send(): return lax.ppermute(array, ('groups', 'dp'), pairs)]
    ppermute x15 -> x17, starting transfers between devices: 13.1 us -> 15.8 us  [send(): return lax.ppermute(array, ('groups', 'dp'), pairs)]
    unnamed x25 -> x29, local copies, waits for them, and re-layouts: 6.97 us -> 6.23 us
  transfers between devices with their start and end apart: 33 -> 35, of which waited for: 18 -> 18; matrix products, arithmetic and copies ran while one was open for 3% -> 3% of each run, Pallas kernels for 33% -> 34%
where the time goes in v15:
time: 193 us
  Pallas kernels  96.7 us (50%)
  waiting for transfers between devices  50.7 us (26%)
  starting transfers between devices  31.8 us (16%)
  local copies, waits for them, and re-layouts  12.1 us (6%)
    pallas_call x5, Pallas kernels, attend(): pl.pallas_call(functools.partial(attend_kernel, starts, sum((len(one) for...  66.6 us
    ppermute x3, waiting for transfers between devices, spread(): lax.ppermute(lane, 'dp', ring)  25.6 us
    ppermute x17, starting transfers between devices, send(): return lax.ppermute(array, ('groups', 'dp'), pairs)  15.8 us
    all_to_all x1, waiting for transfers between devices, gather_plan(): lax.all_to_all(jnp.broadcast_to(plan, (ranks, width + slots)), 'dp', spli...  9.9 us
    pallas_call x2, Pallas kernels, add_part(): pl.pallas_call(functools.partial(part_kernel, chips, bool(more)), out_sha...  9.84 us
    ppermute x9, waiting for transfers between devices, keep(): lax.ppermute(array, 'dp', beside)  9.27 us
    pallas_call x1, Pallas kernels, gather_plan(): pl.pallas_call(functools.partial(query_kernel, ranks, spare, stride, pack...  6.97 us
    pallas_call x1, Pallas kernels, gather_plan(): pl.pallas_call(functools.partial(finish_kernel, chips), out_shape=tuple((...  6.37 us
  transfers between devices with their start and end apart: 35, of which 18 were waited for; matrix products, arithmetic and copies ran while one was open for 3% of the time, Pallas kernels for 34%

profile of v15, /device:TPU:1, one launch (start us, length us, event | category | flops | bytes accessed | tf_op | source)
XLA Modules:
  0.0 192.6 jit_solution(5521346243099370396)
XLA Ops:
  0.0 1.9 join.1.refs_0_
  2.1 3.8 %collective-permute-start.1 = (bf16[320,1024]{1,0:T(8,128)(2,1)}, bf16[320,1024]{1,0:T(8,128)(2,1)}, u32[]{:S(2)}, u32[]{:S(2)}) collective-permute-start(bf16[320,1024]{1,0:T(8,128)(2,1)} %join.1.refs_0_), channel_id=1, source_target_pairs={{0,8},{1,9},{2,10},{3,11},{4,0},{5,1},{6,2},{7,3},{8,12},{9,13},{1... | collective-permute-start | bytes 1966088 | tf_op jit(solution)/shard_map/ppermute | solution.py:568
  5.8 1.2 collective-permute-start
  9.9 3.9 %all-to-all-start = ((s32[16,1,1600]{2,1,0:T(1,128)}), s32[16,1,1600]{2,1,0:T(1,128)S(1)}, u32[]{:S(2)}, u32[]{:S(2)}) async-start(s32[16,1,1600]{2,1,0:T(1,128)} %broadcast_in_dim.26), calls=%async_computation | async-start | bytes 212992 | tf_op jit(solution)/shard_map/all_to_all | solution.py:587
  15.2 9.9 %all-to-all-done = s32[16,1,1600]{2,1,0:T(1,128)S(1)} async-done(((s32[16,1,1600]{2,1,0:T(1,128)}), s32[16,1,1600]{2,1,0:T(1,128)S(1)}, u32[]{:S(2)}, u32[]{:S(2)}) %all-to-all-start) | async-done | bytes 102432 | tf_op jit(solution)/shard_map/all_to_all | solution.py:587
  25.2 0.8 copy-done.3
  26.4 1.8 collective-permute-start.5
  28.9 0.9 collective-permute-start.7
  29.9 1.5 copy.34.route_ref
  32.3 1.0 copy-done.5
  33.3 1.7 copy-done.7
  35.0 7.0 %turn_queries.1 = (bf16[4,2816,128]{2,1,0:T(8,128)(2,1)S(1)}, s32[768,128]{1,0:T(8,128)S(1)}, f32[512,128]{1,0:T(8,128)S(1)}, f32[512,128]{1,0:T(8,128)S(1)}, s32[512,1]{1,0:T(8,128)S(1)}) custom-call(s32[512,1]{1,0:T(8,128)S(1)} %copy-done.5, s32[1,512]{1,0:T(1,128)S(1)} %get-tuple-element.86.seat_ref, s32[128,128]{1,0:T(8,128)S(1)} %reshape.69.positions_ref, ...), custom_call_target="tpu_custom_call" | custom-call | flops 4026531840 | bytes 5242880 | tf_op jit(solution)/shard_map/turn_queries/pallas_call | solution.py:608
  42.8 1.5 collective-permute-done.4.near_ref.refs_4_
  44.4 1.2 collective-permute-start.11
  46.0 0.8 cut.1
  46.9 1.5 collective-permute-start.8
  48.4 0.8 collective-permute-start.10
  49.3 1.3 collective-permute-start.9
  50.6 5.3 %add_part.2.refs_6_ = f32[512,1024]{1,0:T(8,128)S(1)} custom-call(s32[16]{0:T(128)S(1)} %fusion.9.owners_ref, bf16[512,5120]{1,0:T(8,128)(2,1)S(1)} %bitcast.12, bf16[320,1024]{1,0:T(8,128)(2,1)S(1)} %copy-done.2, bf16[320,1024]{1,0:T(8,128)(2,1)S(1)} %copy-done.4, bf16[320,1024]{1,0:T(8,128)(2,1)} %collective-permute-done.1.refs_2_, ...), custom_call_target="tpu_custom_call" | custom-call | flops 2013265920 | bytes 10092544 | tf_op jit(solution)/shard_map/add_part/pallas_call | solution.py:651
  56.0 4.5 %add_part.3.refs_6_ = f32[512,1024]{1,0:T(8,128)S(1)} custom-call(s32[16]{0:T(128)S(1)} %fusion.9.owners_ref, bf16[512,5120]{1,0:T(8,128)(2,1)S(1)} %bitcast.12, bf16[320,1024]{1,0:T(8,128)(2,1)S(1)} %collective-permute-done.3.far_ref.refs_0_, bf16[320,1024]{1,0:T(8,128)(2,1)S(1)} %collective-permute-done.11.refs_1_, ...), custom_call_target="tpu_custom_call" | custom-call | flops 2013265920 | bytes 10092544 | tf_op jit(solution)/shard_map/add_part/pallas_call | solution.py:651
  60.5 1.0 collective-permute-start.16
  62.0 1.5 collective-permute-done.14.refs_3_
  64.2 6.4 %finish.1.refs_3_ = bf16[512,1024]{1,0:T(8,128)(2,1)} custom-call(s32[16]{0:T(128)S(1)} %fusion.9.owners_ref, bf16[512,5120]{1,0:T(8,128)(2,1)S(1)} %bitcast.12, f32[1,1024]{1,0:T(1,128)S(1)} %maximum_convert_fusion.bias_ref, f32[512,128]{1,0:T(8,128)S(1)} %get-tuple-element.103.cosine_ref, f32[512,128]{1,0:T(8,128)S(1)} %get-tuple-element.104.sine_ref, ...), custom_call_target="tpu_custom_call" | custom-call | flops 1342177280 | bytes 8126464 | tf_op jit(solution)/shard_map/finish/pallas_call | solution.py:696
  71.0 0.9 collective-permute-start.18
  73.8 1.2 copy-done.9
  74.9 3.5 %veil.1 = (bf16[16,128,128]{2,1,0:T(8,128)(2,1)S(1)}, bf16[16,256,128]{2,1,0:T(8,128)(2,1)S(1)}, bf16[16,256,128]{2,1,0:T(8,128)(2,1)S(1)}, bf16[16,256,128]{2,1,0:T(8,128)(2,1)S(1)}, bf16[16,128,128]{2,1,0:T(8,128)(2,1)S(1)}) custom-call(s32[768,128]{1,0:T(8,128)S(1)} %copy-done.9, s32[16,1,512]{2,1,0:T(1,128)S(1)} %reshape.72.routes_ref, ...), custom_call_target="tpu_custom_call" | custom-call | flops 3000000000 | bytes 4194304 | tf_op jit(solution)/shard_map/veil/pallas_call | solution.py:725
  78.4 9.9 %attend.5 = (f32[4,2816,128]{2,1,0:T(8,128)S(1)}, f32[4,2816,128]{2,1,0:T(8,128)S(1)}, f32[4,2816,128]{2,1,0:T(8,128)S(1)}) custom-call(s32[512,1]{1,0:T(8,128)S(1)} %reshape.83.refs_0_, bf16[4,2816,128]{2,1,0:T(8,128)(2,1)S(1)} %copy-done.1, bf16[16,128,128]{2,1,0:T(8,128)(2,1)S(1)} %get-tuple-element.115.refs_2_, bf16[512,1024]{1,0:T(8,128)(2,1)} %finish.1.refs_3_, ...), custom_call_target="tpu_custom_call" | custom-call | flops 4429185024 | bytes 16777216 | tf_op jit(solution)/shard_map/attend/pallas_call | solution.py:768
  88.4 7.6 %collective-permute-done.18.refs_3_ = bf16[512,1024]{1,0:T(8,128)(2,1)} collective-permute-done((bf16[512,1024]{1,0:T(8,128)(2,1)}, bf16[512,1024]{1,0:T(8,128)(2,1)}, u32[]{:S(2)}, u32[]{:S(2)}) %collective-permute-start.18) | collective-permute-done | bytes 1048608 | tf_op jit(solution)/shard_map/ppermute | solution.py:476
  96.5 1.3 collective-permute-start.23
  97.8 1.3 collective-permute-start.21
  99.5 0.8 collective-permute-done.23.refs_6_
  100.3 1.5 collective-permute-done.22.refs_4_
  101.8 12.2 %attend.6 = (f32[4,2816,128]{2,1,0:T(8,128)S(1)}, f32[4,2816,128]{2,1,0:T(8,128)S(1)}, f32[4,2816,128]{2,1,0:T(8,128)S(1)}) custom-call(s32[512,1]{1,0:T(8,128)S(1)} %reshape.83.refs_0_, bf16[4,2816,128]{2,1,0:T(8,128)(2,1)S(1)} %copy-done.1, ...), custom_call_target="tpu_custom_call", output_to_operand_aliasing={{0}: (7, {}), {1}: (8, {}), {2}: (9, {})} | custom-call | flops 5905580032 | bytes 33554432 | tf_op jit(solution)/shard_map/attend/pallas_call | solution.py:768
  114.0 8.3 %collective-permute-done.21.refs_3_ = bf16[512,1024]{1,0:T(8,128)(2,1)S(1)} collective-permute-done((bf16[512,1024]{1,0:T(8,128)(2,1)}, bf16[512,1024]{1,0:T(8,128)(2,1)S(1)}, u32[]{:S(2)}, u32[]{:S(2)}) %collective-permute-start.21) | collective-permute-done | bytes 1048608 | tf_op jit(solution)/shard_map/ppermute | solution.py:476
  122.2 1.0 collective-permute-done.20.refs_5_
  123.2 1.7 collective-permute-start.27
  124.9 0.9 collective-permute-start.25
  126.2 1.0 collective-permute-done.27.refs_6_
  127.2 1.5 collective-permute-done.26.refs_4_
  128.7 10.7 %attend.7 = (f32[4,2816,128]{2,1,0:T(8,128)S(1)}, f32[4,2816,128]{2,1,0:T(8,128)S(1)}, f32[4,2816,128]{2,1,0:T(8,128)S(1)}) custom-call(s32[512,1]{1,0:T(8,128)S(1)} %reshape.83.refs_0_, bf16[4,2816,128]{2,1,0:T(8,128)(2,1)S(1)} %copy-done.1, ...), custom_call_target="tpu_custom_call", output_to_operand_aliasing={{0}: (7, {}), {1}: (8, {}), {2}: (9, {})} | custom-call | flops 5905580032 | bytes 33554432 | tf_op jit(solution)/shard_map/attend/pallas_call | solution.py:768
  139.4 9.8 %collective-permute-done.25.refs_3_ = bf16[512,1024]{1,0:T(8,128)(2,1)S(1)} collective-permute-done((bf16[512,1024]{1,0:T(8,128)(2,1)S(1)}, bf16[512,1024]{1,0:T(8,128)(2,1)S(1)}, u32[]{:S(2)}, u32[]{:S(2)}) %collective-permute-start.25) | collective-permute-done | bytes 1048608 | tf_op jit(solution)/shard_map/ppermute | solution.py:476
  149.7 1.7 collective-permute-start.30
  151.5 1.2 collective-permute-start.29
  153.7 1.5 collective-permute-done.31.refs_6_
  155.2 10.7 %attend.8 = (f32[4,2816,128]{2,1,0:T(8,128)S(1)}, f32[4,2816,128]{2,1,0:T(8,128)S(1)}, f32[4,2816,128]{2,1,0:T(8,128)S(1)}) custom-call(s32[512,1]{1,0:T(8,128)S(1)} %reshape.83.refs_0_, bf16[4,2816,128]{2,1,0:T(8,128)(2,1)S(1)} %copy-done.1, ...), custom_call_target="tpu_custom_call", output_to_operand_aliasing={{0}: (7, {}), {1}: (8, {}), {2}: (9, {})} | custom-call | flops 5905580032 | bytes 33554432 | tf_op jit(solution)/shard_map/attend/pallas_call | solution.py:768
  165.9 1.1 collective-permute-start.32
  167.0 1.5 collective-permute-done.32.refs_5_
  169.3 23.2 %attend.9 = (bf16[512,2560]{1,0:T(8,128)(2,1)}, f32[4,2816,128]{2,1,0:T(8,128)S(1)}, f32[4,2816,128]{2,1,0:T(8,128)S(1)}, f32[4,2816,128]{2,1,0:T(8,128)S(1)}) custom-call(s32[512,1]{1,0:T(8,128)S(1)} %reshape.83.refs_0_, bf16[4,2816,128]{2,1,0:T(8,128)(2,1)S(1)} %copy-done.1, ...), custom_call_target="tpu_custom_call", output_to_operand_aliasing={{1}: (7, {}), {2}: (8, {}), {3}: (9, {})} | custom-call | flops 4429185024 | bytes 16777216 | tf_op jit(solution)/shard_map/attend/pallas_call | solution.py:768
  (90 shorter events, 14.9 us)
Async XLA Ops:
  1.9 23.2 %collective-permute-start.2 = (bf16[320,1024]{1,0:T(8,128)(2,1)}, bf16[320,1024]{1,0:T(8,128)(2,1)S(1)}, u32[]{:S(2)}, u32[]{:S(2)}) collective-permute-start(bf16[320,1024]{1,0:T(8,128)(2,1)} %join.1.refs_0_), channel_id=1, source_target_pairs={{0,1},{1,0},{2,3},{3,2},{4,5},{5,4},{6,7},{7,6},{8,9},{9,8},{10,11... | collective-permute-start | bytes 1966088 | tf_op jit(solution)/shard_map/ppermute | solution.py:568
  2.1 23.9 %collective-permute-start.1 = (bf16[320,1024]{1,0:T(8,128)(2,1)}, bf16[320,1024]{1,0:T(8,128)(2,1)}, u32[]{:S(2)}, u32[]{:S(2)}) collective-permute-start(bf16[320,1024]{1,0:T(8,128)(2,1)} %join.1.refs_0_), channel_id=1, source_target_pairs={{0,8},{1,9},{2,10},{3,11},{4,0},{5,1},{6,2},{7,3},{8,12},{9,13},{1... | collective-permute-start | bytes 1966088 | tf_op jit(solution)/shard_map/ppermute | solution.py:568
  5.8 20.2 %collective-permute-start = (bf16[320,1024]{1,0:T(8,128)(2,1)}, bf16[320,1024]{1,0:T(8,128)(2,1)}, u32[]{:S(2)}, u32[]{:S(2)}) collective-permute-start(bf16[320,1024]{1,0:T(8,128)(2,1)} %join.1.refs_0_), channel_id=1, source_target_pairs={{0,2},{1,3},{2,0},{3,1},{4,6},{5,7},{6,4},{7,5},{8,10},{9,11},{10,... | collective-permute-start | bytes 1966088 | tf_op jit(solution)/shard_map/ppermute | solution.py:568
  9.9 15.2 %all-to-all-start = ((s32[16,1,1600]{2,1,0:T(1,128)}), s32[16,1,1600]{2,1,0:T(1,128)S(1)}, u32[]{:S(2)}, u32[]{:S(2)}) async-start(s32[16,1,1600]{2,1,0:T(1,128)} %broadcast_in_dim.26), calls=%async_computation | async-start | bytes 212992 | tf_op jit(solution)/shard_map/all_to_all | solution.py:587
  25.2 0.8 copy-start.3
  26.0 16.8 %collective-permute-start.6 = (bf16[320,1024]{1,0:T(8,128)(2,1)}, bf16[320,1024]{1,0:T(8,128)(2,1)}, u32[]{:S(2)}, u32[]{:S(2)}) collective-permute-start(bf16[320,1024]{1,0:T(8,128)(2,1)} %collective-permute-done.1.refs_2_), channel_id=1, source_target_pairs={{0,1},{1,0},{2,3},{3,2},{4,5},{5,4},{6,7},{7,6},{8,9},{9,8},{10,11... | collective-permute-start | bytes 1966088 | tf_op jit(solution)/shard_map/ppermute | solution.py:568
  26.4 16.4 %collective-permute-start.5 = (bf16[320,1024]{1,0:T(8,128)(2,1)}, bf16[320,1024]{1,0:T(8,128)(2,1)S(1)}, u32[]{:S(2)}, u32[]{:S(2)}) collective-permute-start(bf16[320,1024]{1,0:T(8,128)(2,1)} %collective-permute-done.1.refs_2_), channel_id=1, source_target_pairs={{0,8},{1,9},{2,10},{3,11},{4,0},{5,1},{6,2},{7,3},{8,12},{9,13},{1... | collective-permute-start | bytes 1966088 | tf_op jit(solution)/shard_map/ppermute | solution.py:568
  28.2 16.2 %collective-permute-start.4 = (bf16[320,1024]{1,0:T(8,128)(2,1)}, bf16[320,1024]{1,0:T(8,128)(2,1)S(1)}, u32[]{:S(2)}, u32[]{:S(2)}) collective-permute-start(bf16[320,1024]{1,0:T(8,128)(2,1)} %collective-permute-done.1.refs_2_), channel_id=1, source_target_pairs={{0,2},{1,3},{2,0},{3,1},{4,6},{5,7},{6,4},{7,5},{8,10},{9,11},{10,... | collective-permute-start | bytes 1966088 | tf_op jit(solution)/shard_map/ppermute | solution.py:568
  28.2 16.2 %collective-permute-start.3 = (bf16[320,1024]{1,0:T(8,128)(2,1)}, bf16[320,1024]{1,0:T(8,128)(2,1)S(1)}, u32[]{:S(2)}, u32[]{:S(2)}) collective-permute-start(bf16[320,1024]{1,0:T(8,128)(2,1)} %collective-permute-done.1.refs_2_), channel_id=1, source_target_pairs={{0,16},{1,17},{2,18},{3,19},{4,20},{5,21},{6,22},{7,23},{8,24},{9,... | collective-permute-start | bytes 1966088 | tf_op jit(solution)/shard_map/ppermute | solution.py:568
  28.9 13.8 %collective-permute-start.7 = (bf16[320,1024]{1,0:T(8,128)(2,1)}, bf16[320,1024]{1,0:T(8,128)(2,1)}, u32[]{:S(2)}, u32[]{:S(2)}) collective-permute-start(bf16[320,1024]{1,0:T(8,128)(2,1)} %collective-permute-done.refs_4_), channel_id=1, source_target_pairs={{0,1},{1,0},{2,3},{3,2},{4,5},{5,4},{6,7},{7,6},{8,9},{9,8},{10,11... | collective-permute-start | bytes 1966088 | tf_op jit(solution)/shard_map/ppermute | solution.py:568
  32.2 18.4 %slice-start = ((s8[5242880]{0:T(1024)(128)(4,1)}), s8[1048576]{0:T(1024)(128)(4,1)S(1)}, s32[]{:S(2)}) async-start(s8[5242880]{0:T(1024)(128)(4,1)} %bitcast.11), calls=%async_computation.1 | async-start | bytes 2097152
  32.3 1.0 copy-start.5
  33.3 1.7 copy-start.7
  35.0 15.5 %slice-start.1 = ((s8[5242880]{0:T(1024)(128)(4,1)}), s8[4194304]{0:T(1024)(128)(4,1)S(1)}, s32[]{:S(2)}) async-start(s8[5242880]{0:T(1024)(128)(4,1)} %bitcast.11), calls=%async_computation.2 | async-start | bytes 8388608
  35.0 15.5 %copy-start.2 = (bf16[320,1024]{1,0:T(8,128)(2,1)S(1)}, bf16[320,1024]{1,0:T(8,128)(2,1)}, u32[]{:S(2)}) copy-start(bf16[320,1024]{1,0:T(8,128)(2,1)} %join.1.refs_0_) | copy-start | bytes 1966084
  35.0 15.5 %copy-start.4 = (bf16[320,1024]{1,0:T(8,128)(2,1)S(1)}, bf16[320,1024]{1,0:T(8,128)(2,1)}, u32[]{:S(2)}) copy-start(bf16[320,1024]{1,0:T(8,128)(2,1)} %copy-done.3) | copy-start | bytes 1966084
  42.0 0.8 copy-start.8
  42.8 13.2 %copy-start = (bf16[4,2816,128]{2,1,0:T(8,128)(2,1)}, bf16[4,2816,128]{2,1,0:T(8,128)(2,1)S(1)}, u32[]{:S(2)}) copy-start(bf16[4,2816,128]{2,1,0:T(8,128)(2,1)S(1)} %get-tuple-element.92.refs_1_) | copy-start | bytes 8650756
  44.4 4.9 %collective-permute-start.11 = (bf16[320,1024]{1,0:T(8,128)(2,1)S(1)}, bf16[320,1024]{1,0:T(8,128)(2,1)S(1)}, u32[]{:S(2)}, u32[]{:S(2)}) collective-permute-start(bf16[320,1024]{1,0:T(8,128)(2,1)S(1)} %collective-permute-done.3.far_ref.refs_0_), channel_id=1, source_target_pairs={{0,1},{1,0},{2,3},{3,2},{4,5},{5,4},{6,7},{7,6},{8,9},{9,8},{10,11... | collective-permute-start | bytes 1966088 | tf_op jit(solution)/shard_map/ppermute | solution.py:568
  45.5 10.4 %collective-permute-start.12 = (bf16[320,1024]{1,0:T(8,128)(2,1)S(1)}, bf16[320,1024]{1,0:T(8,128)(2,1)S(1)}, u32[]{:S(2)}, u32[]{:S(2)}) collective-permute-start(bf16[320,1024]{1,0:T(8,128)(2,1)S(1)} %collective-permute-done.5.next_ref.refs_2_), channel_id=1, source_target_pairs={{0,1},{1,0},{2,3},{3,2},{4,5},{5,4},{6,7},{7,6},{8,9},{9,8},{10,11... | collective-permute-start | bytes 1966088 | tf_op jit(solution)/shard_map/ppermute | solution.py:568
  45.5 10.4 %collective-permute-start.13 = (bf16[320,1024]{1,0:T(8,128)(2,1)S(1)}, bf16[320,1024]{1,0:T(8,128)(2,1)S(1)}, u32[]{:S(2)}, u32[]{:S(2)}) collective-permute-start(bf16[320,1024]{1,0:T(8,128)(2,1)S(1)} %collective-permute-done.4.near_ref.refs_4_), channel_id=1, source_target_pairs={{0,1},{1,0},{2,3},{3,2},{4,5},{5,4},{6,7},{7,6},{8,9},{9,8},{10,11... | collective-permute-start | bytes 1966088 | tf_op jit(solution)/shard_map/ppermute | solution.py:568
  46.9 13.6 %collective-permute-start.8 = (bf16[224,1024]{1,0:T(8,128)(2,1)S(1)}, bf16[224,1024]{1,0:T(8,128)(2,1)S(1)}, u32[]{:S(2)}, u32[]{:S(2)}) collective-permute-start(bf16[224,1024]{1,0:T(8,128)(2,1)S(1)} %get-tuple-element.106), channel_id=1, source_target_pairs={{0,2},{1,3},{2,0},{3,1},{4,6},{5,7},{6,4},{7,5},{8,10},{9,11},{10,... | collective-permute-start | bytes 1376264 | tf_op jit(solution)/shard_map/ppermute | solution.py:568
  48.4 12.1 %collective-permute-start.10 = (bf16[208,1024]{1,0:T(8,128)(2,1)S(1)}, bf16[208,1024]{1,0:T(8,128)(2,1)S(1)}, u32[]{:S(2)}, u32[]{:S(2)}) collective-permute-start(bf16[208,1024]{1,0:T(8,128)(2,1)S(1)} %get-tuple-element.107), channel_id=1, source_target_pairs={{0,8},{1,9},{2,10},{3,11},{4,0},{5,1},{6,2},{7,3},{8,12},{9,13},{1... | collective-permute-start | bytes 1277960 | tf_op jit(solution)/shard_map/ppermute | solution.py:568
  49.3 11.2 %collective-permute-start.9 = (bf16[208,1024]{1,0:T(8,128)(2,1)S(1)}, bf16[208,1024]{1,0:T(8,128)(2,1)S(1)}, u32[]{:S(2)}, u32[]{:S(2)}) collective-permute-start(bf16[208,1024]{1,0:T(8,128)(2,1)S(1)} %get-tuple-element.107), channel_id=1, source_target_pairs={{0,16},{1,17},{2,18},{3,19},{4,20},{5,21},{6,22},{7,23},{8,24},{9,... | collective-permute-start | bytes 1277960 | tf_op jit(solution)/shard_map/ppermute | solution.py:568
  60.5 12.0 %copy-start.10 = (s32[16]{0:T(128)S(1)}, s32[16]{0:T(128)}, u32[]{:S(2)}) copy-start(s32[16]{0:T(128)} %constant.68) | copy-start | bytes 196
  60.5 11.9 %copy-start.11 = (s32[16]{0:T(128)S(1)}, s32[16]{0:T(128)}, u32[]{:S(2)}) copy-start(s32[16]{0:T(128)} %constant.67.clone) | copy-start | bytes 196
  60.5 3.7 %collective-permute-start.16 = (bf16[224,1024]{1,0:T(8,128)(2,1)S(1)}, bf16[224,1024]{1,0:T(8,128)(2,1)S(1)}, u32[]{:S(2)}, u32[]{:S(2)}) collective-permute-start(bf16[224,1024]{1,0:T(8,128)(2,1)S(1)} %collective-permute-done.8.refs_2_), channel_id=1, source_target_pairs={{0,1},{1,0},{2,3},{3,2},{4,5},{5,4},{6,7},{7,6},{8,9},{9,8},{10,11... | collective-permute-start | bytes 1376264 | tf_op jit(solution)/shard_map/ppermute | solution.py:568
  61.5 2.1 %collective-permute-start.14 = (bf16[208,1024]{1,0:T(8,128)(2,1)S(1)}, bf16[208,1024]{1,0:T(8,128)(2,1)S(1)}, u32[]{:S(2)}, u32[]{:S(2)}) collective-permute-start(bf16[208,1024]{1,0:T(8,128)(2,1)S(1)} %collective-permute-done.10.refs_0_), channel_id=1, source_target_pairs={{0,1},{1,0},{2,3},{3,2},{4,5},{5,4},{6,7},{7,6},{8,9},{9,8},{10,11... | collective-permute-start | bytes 1277960 | tf_op jit(solution)/shard_map/ppermute | solution.py:568
  61.5 2.6 %collective-permute-start.15 = (bf16[208,1024]{1,0:T(8,128)(2,1)S(1)}, bf16[208,1024]{1,0:T(8,128)(2,1)S(1)}, u32[]{:S(2)}, u32[]{:S(2)}) collective-permute-start(bf16[208,1024]{1,0:T(8,128)(2,1)S(1)} %collective-permute-done.9.refs_1_), channel_id=1, source_target_pairs={{0,1},{1,0},{2,3},{3,2},{4,5},{5,4},{6,7},{7,6},{8,9},{9,8},{10,11... | collective-permute-start | bytes 1277960 | tf_op jit(solution)/shard_map/ppermute | solution.py:568
  70.6 7.9 %collective-permute-start.19 = (bf16[512,1024]{1,0:T(8,128)(2,1)}, bf16[512,1024]{1,0:T(8,128)(2,1)}, u32[]{:S(2)}, u32[]{:S(2)}) collective-permute-start(bf16[512,1024]{1,0:T(8,128)(2,1)} %finish.1.refs_3_), channel_id=1, source_target_pairs={{0,1},{1,0},{2,3},{3,2},{4,5},{5,4},{6,7},{7,6},{8,9},{9,8},{10,11... | collective-permute-start | bytes 3145736 | tf_op jit(solution)/shard_map/ppermute | solution.py:469
  71.0 24.9 %collective-permute-start.18 = (bf16[512,1024]{1,0:T(8,128)(2,1)}, bf16[512,1024]{1,0:T(8,128)(2,1)}, u32[]{:S(2)}, u32[]{:S(2)}) collective-permute-start(bf16[512,1024]{1,0:T(8,128)(2,1)} %finish.1.refs_3_), channel_id=1, source_target_pairs={{0,8},{1,9},{2,10},{3,11},{4,0},{5,1},{6,2},{7,3},{8,12},{9,13},{1... | collective-permute-start | bytes 3145736 | tf_op jit(solution)/shard_map/ppermute | solution.py:476
  71.9 24.6 %collective-permute-start.17 = (bf16[512,1024]{1,0:T(8,128)(2,1)}, bf16[512,1024]{1,0:T(8,128)(2,1)}, u32[]{:S(2)}, u32[]{:S(2)}) collective-permute-start(bf16[512,1024]{1,0:T(8,128)(2,1)} %finish.1.refs_3_), channel_id=1, source_target_pairs={{0,2},{1,3},{2,0},{3,1},{4,6},{5,7},{6,4},{7,5},{8,10},{9,11},{10,... | collective-permute-start | bytes 3145736 | tf_op jit(solution)/shard_map/ppermute | solution.py:476
  73.4 5.1 %copy-start.1 = (bf16[4,2816,128]{2,1,0:T(8,128)(2,1)S(1)}, bf16[4,2816,128]{2,1,0:T(8,128)(2,1)}, u32[]{:S(2)}) copy-start(bf16[4,2816,128]{2,1,0:T(8,128)(2,1)} %copy-done) | copy-start | bytes 8650756
  73.8 1.2 copy-start.9
  96.5 3.8 %collective-permute-start.23 = (bf16[512,1024]{1,0:T(8,128)(2,1)}, bf16[512,1024]{1,0:T(8,128)(2,1)S(1)}, u32[]{:S(2)}, u32[]{:S(2)}) collective-permute-start(bf16[512,1024]{1,0:T(8,128)(2,1)} %collective-permute-done.17.refs_5_), channel_id=1, source_target_pairs={{0,1},{1,0},{2,3},{3,2},{4,5},{5,4},{6,7},{7,6},{8,9},{9,8},{10,11... | collective-permute-start | bytes 3145736 | tf_op jit(solution)/shard_map/ppermute | solution.py:469
  97.8 4.0 %collective-permute-start.22 = (bf16[512,1024]{1,0:T(8,128)(2,1)}, bf16[512,1024]{1,0:T(8,128)(2,1)S(1)}, u32[]{:S(2)}, u32[]{:S(2)}) collective-permute-start(bf16[512,1024]{1,0:T(8,128)(2,1)} %collective-permute-done.18.refs_3_), channel_id=1, source_target_pairs={{0,1},{1,0},{2,3},{3,2},{4,5},{5,4},{6,7},{7,6},{8,9},{9,8},{10,11... | collective-permute-start | bytes 3145736 | tf_op jit(solution)/shard_map/ppermute | solution.py:469
  97.8 24.4 %collective-permute-start.21 = (bf16[512,1024]{1,0:T(8,128)(2,1)}, bf16[512,1024]{1,0:T(8,128)(2,1)S(1)}, u32[]{:S(2)}, u32[]{:S(2)}) collective-permute-start(bf16[512,1024]{1,0:T(8,128)(2,1)} %collective-permute-done.18.refs_3_), channel_id=1, source_target_pairs={{0,8},{1,9},{2,10},{3,11},{4,0},{5,1},{6,2},{7,3},{8,12},{9,13},{1... | collective-permute-start | bytes 3145736 | tf_op jit(solution)/shard_map/ppermute | solution.py:476
  99.1 24.1 %collective-permute-start.20 = (bf16[512,1024]{1,0:T(8,128)(2,1)}, bf16[512,1024]{1,0:T(8,128)(2,1)S(1)}, u32[]{:S(2)}, u32[]{:S(2)}) collective-permute-start(bf16[512,1024]{1,0:T(8,128)(2,1)} %collective-permute-done.18.refs_3_), channel_id=1, source_target_pairs={{0,2},{1,3},{2,0},{3,1},{4,6},{5,7},{6,4},{7,5},{8,10},{9,11},{10,... | collective-permute-start | bytes 3145736 | tf_op jit(solution)/shard_map/ppermute | solution.py:476
  123.2 4.0 %collective-permute-start.27 = (bf16[512,1024]{1,0:T(8,128)(2,1)S(1)}, bf16[512,1024]{1,0:T(8,128)(2,1)S(1)}, u32[]{:S(2)}, u32[]{:S(2)}) collective-permute-start(bf16[512,1024]{1,0:T(8,128)(2,1)S(1)} %collective-permute-done.20.refs_5_), channel_id=1, source_target_pairs={{0,1},{1,0},{2,3},{3,2},{4,5},{5,4},{6,7},{7,6},{8,9},{9,8},{10,11... | collective-permute-start | bytes 3145736 | tf_op jit(solution)/shard_map/ppermute | solution.py:469
  124.9 3.8 %collective-permute-start.26 = (bf16[512,1024]{1,0:T(8,128)(2,1)S(1)}, bf16[512,1024]{1,0:T(8,128)(2,1)S(1)}, u32[]{:S(2)}, u32[]{:S(2)}) collective-permute-start(bf16[512,1024]{1,0:T(8,128)(2,1)S(1)} %collective-permute-done.21.refs_3_), channel_id=1, source_target_pairs={{0,1},{1,0},{2,3},{3,2},{4,5},{5,4},{6,7},{7,6},{8,9},{9,8},{10,11... | collective-permute-start | bytes 3145736 | tf_op jit(solution)/shard_map/ppermute | solution.py:469
  124.9 24.2 %collective-permute-start.25 = (bf16[512,1024]{1,0:T(8,128)(2,1)S(1)}, bf16[512,1024]{1,0:T(8,128)(2,1)S(1)}, u32[]{:S(2)}, u32[]{:S(2)}) collective-permute-start(bf16[512,1024]{1,0:T(8,128)(2,1)S(1)} %collective-permute-done.21.refs_3_), channel_id=1, source_target_pairs={{0,8},{1,9},{2,10},{3,11},{4,0},{5,1},{6,2},{7,3},{8,12},{9,13},{1... | collective-permute-start | bytes 3145736 | tf_op jit(solution)/shard_map/ppermute | solution.py:476
  125.8 23.9 %collective-permute-start.24 = (bf16[512,1024]{1,0:T(8,128)(2,1)S(1)}, bf16[512,1024]{1,0:T(8,128)(2,1)S(1)}, u32[]{:S(2)}, u32[]{:S(2)}) collective-permute-start(bf16[512,1024]{1,0:T(8,128)(2,1)S(1)} %collective-permute-done.21.refs_3_), channel_id=1, source_target_pairs={{0,2},{1,3},{2,0},{3,1},{4,6},{5,7},{6,4},{7,5},{8,10},{9,11},{10,... | collective-permute-start | bytes 3145736 | tf_op jit(solution)/shard_map/ppermute | solution.py:476
  149.7 4.0 %collective-permute-start.30 = (bf16[512,1024]{1,0:T(8,128)(2,1)S(1)}, bf16[512,1024]{1,0:T(8,128)(2,1)S(1)}, u32[]{:S(2)}, u32[]{:S(2)}) collective-permute-start(bf16[512,1024]{1,0:T(8,128)(2,1)S(1)} %collective-permute-done.25.refs_3_), channel_id=1, source_target_pairs={{0,1},{1,0},{2,3},{3,2},{4,5},{5,4},{6,7},{7,6},{8,9},{9,8},{10,11... | collective-permute-start | bytes 3145736 | tf_op jit(solution)/shard_map/ppermute | solution.py:469
  151.4 3.8 %collective-permute-start.31 = (bf16[512,1024]{1,0:T(8,128)(2,1)S(1)}, bf16[512,1024]{1,0:T(8,128)(2,1)S(1)}, u32[]{:S(2)}, u32[]{:S(2)}) collective-permute-start(bf16[512,1024]{1,0:T(8,128)(2,1)S(1)} %collective-permute-done.24.refs_5_), channel_id=1, source_target_pairs={{0,1},{1,0},{2,3},{3,2},{4,5},{5,4},{6,7},{7,6},{8,9},{9,8},{10,11... | collective-permute-start | bytes 3145736 | tf_op jit(solution)/shard_map/ppermute | solution.py:469
  151.5 14.4 %collective-permute-start.29 = (bf16[256,1024]{1,0:T(8,128)(2,1)S(1)}, bf16[256,1024]{1,0:T(8,128)(2,1)S(1)}, u32[]{:S(2)}, u32[]{:S(2)}) collective-permute-start(bf16[256,1024]{1,0:T(8,128)(2,1)S(1)} %slice.27), channel_id=1, source_target_pairs={{0,8},{1,9},{2,10},{3,11},{4,0},{5,1},{6,2},{7,3},{8,12},{9,13},{1... | collective-permute-start | bytes 1572872 | tf_op jit(solution)/shard_map/ppermute | solution.py:483
  152.6 13.2 %collective-permute-start.28 = (bf16[256,1024]{1,0:T(8,128)(2,1)S(1)}, bf16[256,1024]{1,0:T(8,128)(2,1)S(1)}, u32[]{:S(2)}, u32[]{:S(2)}) collective-permute-start(bf16[256,1024]{1,0:T(8,128)(2,1)S(1)} %slice.26), channel_id=1, source_target_pairs={{0,2},{1,3},{2,0},{3,1},{4,6},{5,7},{6,4},{7,5},{8,10},{9,11},{10,... | collective-permute-start | bytes 1572872 | tf_op jit(solution)/shard_map/ppermute | solution.py:482
  165.9 2.7 %collective-permute-start.32 = (bf16[256,1024]{1,0:T(8,128)(2,1)S(1)}, bf16[256,1024]{1,0:T(8,128)(2,1)S(1)}, u32[]{:S(2)}, u32[]{:S(2)}) collective-permute-start(bf16[256,1024]{1,0:T(8,128)(2,1)S(1)} %collective-permute-done.28.refs_3_), channel_id=1, source_target_pairs={{0,1},{1,0},{2,3},{3,2},{4,5},{5,4},{6,7},{7,6},{8,9},{9,8},{10,11... | collective-permute-start | bytes 1572872 | tf_op jit(solution)/shard_map/ppermute | solution.py:469
  167.0 2.3 %collective-permute-start.33 = (bf16[256,1024]{1,0:T(8,128)(2,1)S(1)}, bf16[256,1024]{1,0:T(8,128)(2,1)S(1)}, u32[]{:S(2)}, u32[]{:S(2)}) collective-permute-start(bf16[256,1024]{1,0:T(8,128)(2,1)S(1)} %collective-permute-done.29.refs_4_), channel_id=1, source_target_pairs={{0,1},{1,0},{2,3},{3,2},{4,5},{5,4},{6,7},{7,6},{8,9},{9,8},{10,11... | collective-permute-start | bytes 1572872 | tf_op jit(solution)/shard_map/ppermute | solution.py:469
  (1 other events, 0.7 us)

commit v16 on v15

--- a/solution.py
+++ b/solution.py
@@ -392,17 +392,21 @@
                 new_sum_ref[head, tokens] = weight_sum
                 new_total_ref[head, tokens] = total
 
-    def add_heads_as_before(group, row, worst):
-        tokens = pl.ds(pl.multiple_of(group * packed, 16), packed)
-        scores = [scores_of(group, row, head, tokens) for head in range(heads)]
+    def add_heads_as_before(groups, row, worst):
+        units = [
+            (group, head, pl.ds(pl.multiple_of(group * packed, 16), packed))
+            for group in groups
+            for head in range(heads)
+        ]
+        scores = [scores_of(group, row, head, tokens) for group, head, tokens in units]
         weights = []
-        for head, score in enumerate(scores):
+        for (group, head, tokens), score in zip(units, scores):
             above = score - tile(top_ref[head, tokens], score.shape[1])
             for first in range(0, score.shape[1], HEAD_SIZE):
                 part = above[:, first : first + HEAD_SIZE].reshape(packed // 8, 8, HEAD_SIZE)
                 worst = jnp.maximum(worst, jnp.max(part, axis=0))
             weights.append(jnp.exp2(above * scale).astype(jnp.bfloat16))
-        for head, weight in enumerate(weights):
+        for (group, head, tokens), weight in zip(units, weights):
             total, weight_sum = products_of(group, row, head, weight)
             total = total + total_ref[head, tokens]
             weight_sum = weight_sum + sum_ref[head, tokens]
@@ -429,12 +433,13 @@
         return
     worst = jnp.full((8, HEAD_SIZE), MASKED, jnp.float32)
     for row, first, end in spans:
-        worst = lax.fori_loop(
-            first,
-            end,
-            lambda group, worst, row=row: add_heads_as_before(group, row, worst),
-            worst,
-        )
+        many = 2 if (end - first) % 2 == 0 else 1
+
+        def some_groups(step, worst, row=row, first=first, many=many):
+            groups = [first + step * many + at for at in range(many)]
+            return add_heads_as_before(groups, row, worst)
+
+        worst = lax.fori_loop(0, (end - first) // many, some_groups, worst)
 
     @pl.when(jnp.max(worst) * scale > SAFE_POWER)
     def _():

time: 193 us -> 191 us (0.990)
  Pallas kernels: 96.7 us -> 94.6 us
    pallas_call x5, Pallas kernels: 66.6 us -> 64.5 us  [attend(): pl.pallas_call(functools.partial(attend_kernel, starts, sum((len(one) for...]
  transfers between devices with their start and end apart: 35 -> 35, of which waited for: 18 -> 18; matrix products, arithmetic and copies ran while one was open for 3% -> 4% of each run, Pallas kernels for 34% -> 34%
where the time goes in v16:
time: 191 us
  Pallas kernels  94.6 us (50%)
  waiting for transfers between devices  50.7 us (27%)
  starting transfers between devices  31.8 us (17%)
  local copies, waits for them, and re-layouts  12.1 us (6%)
    pallas_call x5, Pallas kernels, attend(): pl.pallas_call(functools.partial(attend_kernel, starts, sum((len(one) for...  64.5 us
    ppermute x3, waiting for transfers between devices, spread(): lax.ppermute(lane, 'dp', ring)  25.6 us
    ppermute x17, starting transfers between devices, send(): return lax.ppermute(array, ('groups', 'dp'), pairs)  15.8 us
    all_to_all x1, waiting for transfers between devices, gather_plan(): lax.all_to_all(jnp.broadcast_to(plan, (ranks, width + slots)), 'dp', spli...  9.9 us
    pallas_call x2, Pallas kernels, add_part(): pl.pallas_call(functools.partial(part_kernel, chips, bool(more)), out_sha...  9.84 us
    ppermute x9, waiting for transfers between devices, keep(): lax.ppermute(array, 'dp', beside)  9.27 us
    pallas_call x1, Pallas kernels, gather_plan(): pl.pallas_call(functools.partial(query_kernel, ranks, spare, stride, pack...  6.97 us
    pallas_call x1, Pallas kernels, gather_plan(): pl.pallas_call(functools.partial(finish_kernel, chips), out_shape=tuple((...  6.37 us
  transfers between devices with their start and end apart: 35, of which 18 were waited for; matrix products, arithmetic and copies ran while one was open for 4% of the time, Pallas kernels for 34%

profile of v16, /device:TPU:1, one launch (start us, length us, event | category | flops | bytes accessed | tf_op | source)
XLA Modules:
  0.0 190.6 jit_solution(16725516702826565580)
XLA Ops:
  0.0 1.9 %join.1.refs_0_ = bf16[320,1024]{1,0:T(8,128)(2,1)} custom-call(bf16[320,512]{1,0:T(8,128)(2,1)} %left_ref.1, bf16[320,512]{1,0:T(8,128)(2,1)} %right_ref.1), custom_call_target="tpu_custom_call" | custom-call | tf_op jit(solution)/shard_map/join/pallas_call | solution.py:553
  2.1 3.8 %collective-permute-start.1 = (bf16[320,1024]{1,0:T(8,128)(2,1)}, bf16[320,1024]{1,0:T(8,128)(2,1)}, u32[]{:S(2)}, u32[]{:S(2)}) collective-permute-start(bf16[320,1024]{1,0:T(8,128)(2,1)} %join.1.refs_0_), channel_id=1, source_target_pairs={{0,8},{1,9},{2,10},{3,11},{4,0},{5,1},{6,2},{7,3},{8,12},{9,13},{1... | collective-permute-start | bytes 1966088 | tf_op jit(solution)/shard_map/ppermute | solution.py:573
  5.8 1.2 collective-permute-start
  9.9 3.9 %all-to-all-start = ((s32[16,1,1600]{2,1,0:T(1,128)}), s32[16,1,1600]{2,1,0:T(1,128)S(1)}, u32[]{:S(2)}, u32[]{:S(2)}) async-start(s32[16,1,1600]{2,1,0:T(1,128)} %broadcast_in_dim.26), calls=%async_computation | async-start | bytes 212992 | tf_op jit(solution)/shard_map/all_to_all | solution.py:592
  15.2 9.9 %all-to-all-done = s32[16,1,1600]{2,1,0:T(1,128)S(1)} async-done(((s32[16,1,1600]{2,1,0:T(1,128)}), s32[16,1,1600]{2,1,0:T(1,128)S(1)}, u32[]{:S(2)}, u32[]{:S(2)}) %all-to-all-start) | async-done | bytes 102432 | tf_op jit(solution)/shard_map/all_to_all | solution.py:592
  25.2 0.8 copy-done.3
  26.4 1.8 collective-permute-start.5
  28.9 0.9 collective-permute-start.7
  29.9 1.5 copy.34.route_ref
  32.3 1.0 copy-done.5
  33.3 1.7 copy-done.7
  35.0 7.0 %turn_queries.1 = (bf16[4,2816,128]{2,1,0:T(8,128)(2,1)S(1)}, s32[768,128]{1,0:T(8,128)S(1)}, f32[512,128]{1,0:T(8,128)S(1)}, f32[512,128]{1,0:T(8,128)S(1)}, s32[512,1]{1,0:T(8,128)S(1)}) custom-call(s32[512,1]{1,0:T(8,128)S(1)} %copy-done.5, s32[1,512]{1,0:T(1,128)S(1)} %get-tuple-element.86.seat_ref, s32[128,128]{1,0:T(8,128)S(1)} %reshape.69.positions_ref, ...), custom_call_target="tpu_custom_call" | custom-call | flops 4026531840 | bytes 5242880 | tf_op jit(solution)/shard_map/turn_queries/pallas_call | solution.py:613
  42.8 1.5 collective-permute-done.4.near_ref.refs_4_
  44.4 1.2 collective-permute-start.11
  46.0 0.8 cut.1
  46.9 1.5 collective-permute-start.8
  48.4 0.8 collective-permute-start.10
  49.3 1.3 collective-permute-start.9
  50.6 5.3 %add_part.2.refs_6_ = f32[512,1024]{1,0:T(8,128)S(1)} custom-call(s32[16]{0:T(128)S(1)} %fusion.9.owners_ref, bf16[512,5120]{1,0:T(8,128)(2,1)S(1)} %bitcast.12, bf16[320,1024]{1,0:T(8,128)(2,1)S(1)} %copy-done.2, bf16[320,1024]{1,0:T(8,128)(2,1)S(1)} %copy-done.4, bf16[320,1024]{1,0:T(8,128)(2,1)} %collective-permute-done.1.refs_2_, ...), custom_call_target="tpu_custom_call" | custom-call | flops 2013265920 | bytes 10092544 | tf_op jit(solution)/shard_map/add_part/pallas_call | solution.py:656
  56.0 4.5 %add_part.3.refs_6_ = f32[512,1024]{1,0:T(8,128)S(1)} custom-call(s32[16]{0:T(128)S(1)} %fusion.9.owners_ref, bf16[512,5120]{1,0:T(8,128)(2,1)S(1)} %bitcast.12, bf16[320,1024]{1,0:T(8,128)(2,1)S(1)} %collective-permute-done.3.far_ref.refs_0_, bf16[320,1024]{1,0:T(8,128)(2,1)S(1)} %collective-permute-done.11.refs_1_, ...), custom_call_target="tpu_custom_call" | custom-call | flops 2013265920 | bytes 10092544 | tf_op jit(solution)/shard_map/add_part/pallas_call | solution.py:656
  60.5 1.0 collective-permute-start.16
  62.0 1.5 collective-permute-done.14.refs_3_
  64.2 6.4 %finish.1.refs_3_ = bf16[512,1024]{1,0:T(8,128)(2,1)} custom-call(s32[16]{0:T(128)S(1)} %fusion.9.owners_ref, bf16[512,5120]{1,0:T(8,128)(2,1)S(1)} %bitcast.12, f32[1,1024]{1,0:T(1,128)S(1)} %maximum_convert_fusion.bias_ref, f32[512,128]{1,0:T(8,128)S(1)} %get-tuple-element.103.cosine_ref, f32[512,128]{1,0:T(8,128)S(1)} %get-tuple-element.104.sine_ref, ...), custom_call_target="tpu_custom_call" | custom-call | flops 1342177280 | bytes 8126464 | tf_op jit(solution)/shard_map/finish/pallas_call | solution.py:701
  71.0 0.9 collective-permute-start.18
  73.8 1.2 copy-done.9
  74.9 3.5 %veil.1 = (bf16[16,128,128]{2,1,0:T(8,128)(2,1)S(1)}, bf16[16,256,128]{2,1,0:T(8,128)(2,1)S(1)}, bf16[16,256,128]{2,1,0:T(8,128)(2,1)S(1)}, bf16[16,256,128]{2,1,0:T(8,128)(2,1)S(1)}, bf16[16,128,128]{2,1,0:T(8,128)(2,1)S(1)}) custom-call(s32[768,128]{1,0:T(8,128)S(1)} %copy-done.9, s32[16,1,512]{2,1,0:T(1,128)S(1)} %reshape.72.routes_ref, ...), custom_call_target="tpu_custom_call" | custom-call | flops 3000000000 | bytes 4194304 | tf_op jit(solution)/shard_map/veil/pallas_call | solution.py:730
  78.4 9.9 %attend.5 = (f32[4,2816,128]{2,1,0:T(8,128)S(1)}, f32[4,2816,128]{2,1,0:T(8,128)S(1)}, f32[4,2816,128]{2,1,0:T(8,128)S(1)}) custom-call(s32[512,1]{1,0:T(8,128)S(1)} %reshape.83.refs_0_, bf16[4,2816,128]{2,1,0:T(8,128)(2,1)S(1)} %copy-done.1, bf16[16,128,128]{2,1,0:T(8,128)(2,1)S(1)} %get-tuple-element.115.refs_2_, bf16[512,1024]{1,0:T(8,128)(2,1)} %finish.1.refs_3_, ...), custom_call_target="tpu_custom_call" | custom-call | flops 4429185024 | bytes 16777216 | tf_op jit(solution)/shard_map/attend/pallas_call | solution.py:773
  88.4 7.6 %collective-permute-done.18.refs_3_ = bf16[512,1024]{1,0:T(8,128)(2,1)} collective-permute-done((bf16[512,1024]{1,0:T(8,128)(2,1)}, bf16[512,1024]{1,0:T(8,128)(2,1)}, u32[]{:S(2)}, u32[]{:S(2)}) %collective-permute-start.18) | collective-permute-done | bytes 1048608 | tf_op jit(solution)/shard_map/ppermute | solution.py:481
  96.5 1.3 collective-permute-start.23
  97.8 1.3 collective-permute-start.21
  99.5 0.8 collective-permute-done.23.refs_6_
  100.3 1.5 collective-permute-done.22.refs_4_
  101.8 12.2 %attend.6 = (f32[4,2816,128]{2,1,0:T(8,128)S(1)}, f32[4,2816,128]{2,1,0:T(8,128)S(1)}, f32[4,2816,128]{2,1,0:T(8,128)S(1)}) custom-call(s32[512,1]{1,0:T(8,128)S(1)} %reshape.83.refs_0_, bf16[4,2816,128]{2,1,0:T(8,128)(2,1)S(1)} %copy-done.1, ...), custom_call_target="tpu_custom_call", output_to_operand_aliasing={{0}: (7, {}), {1}: (8, {}), {2}: (9, {})} | custom-call | flops 5905580032 | bytes 33554432 | tf_op jit(solution)/shard_map/attend/pallas_call | solution.py:773
  114.0 8.3 %collective-permute-done.21.refs_3_ = bf16[512,1024]{1,0:T(8,128)(2,1)S(1)} collective-permute-done((bf16[512,1024]{1,0:T(8,128)(2,1)}, bf16[512,1024]{1,0:T(8,128)(2,1)S(1)}, u32[]{:S(2)}, u32[]{:S(2)}) %collective-permute-start.21) | collective-permute-done | bytes 1048608 | tf_op jit(solution)/shard_map/ppermute | solution.py:481
  122.2 1.0 collective-permute-done.20.refs_5_
  123.2 1.7 collective-permute-start.27
  124.9 0.9 collective-permute-start.25
  126.2 1.0 collective-permute-done.27.refs_6_
  127.2 1.5 collective-permute-done.26.refs_4_
  128.7 10.7 %attend.7 = (f32[4,2816,128]{2,1,0:T(8,128)S(1)}, f32[4,2816,128]{2,1,0:T(8,128)S(1)}, f32[4,2816,128]{2,1,0:T(8,128)S(1)}) custom-call(s32[512,1]{1,0:T(8,128)S(1)} %reshape.83.refs_0_, bf16[4,2816,128]{2,1,0:T(8,128)(2,1)S(1)} %copy-done.1, ...), custom_call_target="tpu_custom_call", output_to_operand_aliasing={{0}: (7, {}), {1}: (8, {}), {2}: (9, {})} | custom-call | flops 5905580032 | bytes 33554432 | tf_op jit(solution)/shard_map/attend/pallas_call | solution.py:773
  139.4 9.8 %collective-permute-done.25.refs_3_ = bf16[512,1024]{1,0:T(8,128)(2,1)S(1)} collective-permute-done((bf16[512,1024]{1,0:T(8,128)(2,1)S(1)}, bf16[512,1024]{1,0:T(8,128)(2,1)S(1)}, u32[]{:S(2)}, u32[]{:S(2)}) %collective-permute-start.25) | collective-permute-done | bytes 1048608 | tf_op jit(solution)/shard_map/ppermute | solution.py:481
  149.7 1.7 collective-permute-start.30
  151.5 1.2 collective-permute-start.29
  153.7 1.5 collective-permute-done.31.refs_6_
  155.2 10.7 %attend.8 = (f32[4,2816,128]{2,1,0:T(8,128)S(1)}, f32[4,2816,128]{2,1,0:T(8,128)S(1)}, f32[4,2816,128]{2,1,0:T(8,128)S(1)}) custom-call(s32[512,1]{1,0:T(8,128)S(1)} %reshape.83.refs_0_, bf16[4,2816,128]{2,1,0:T(8,128)(2,1)S(1)} %copy-done.1, ...), custom_call_target="tpu_custom_call", output_to_operand_aliasing={{0}: (7, {}), {1}: (8, {}), {2}: (9, {})} | custom-call | flops 5905580032 | bytes 33554432 | tf_op jit(solution)/shard_map/attend/pallas_call | solution.py:773
  165.9 1.1 collective-permute-start.32
  167.0 1.5 collective-permute-done.32.refs_5_
  169.3 21.1 %attend.9 = (bf16[512,2560]{1,0:T(8,128)(2,1)}, f32[4,2816,128]{2,1,0:T(8,128)S(1)}, f32[4,2816,128]{2,1,0:T(8,128)S(1)}, f32[4,2816,128]{2,1,0:T(8,128)S(1)}) custom-call(s32[512,1]{1,0:T(8,128)S(1)} %reshape.83.refs_0_, bf16[4,2816,128]{2,1,0:T(8,128)(2,1)S(1)} %copy-done.1, ...), custom_call_target="tpu_custom_call", output_to_operand_aliasing={{1}: (7, {}), {2}: (8, {}), {3}: (9, {})} | custom-call | flops 4429185024 | bytes 16777216 | tf_op jit(solution)/shard_map/attend/pallas_call | solution.py:773
  (90 shorter events, 14.9 us)
Async XLA Ops:
  1.9 23.2 %collective-permute-start.2 = (bf16[320,1024]{1,0:T(8,128)(2,1)}, bf16[320,1024]{1,0:T(8,128)(2,1)S(1)}, u32[]{:S(2)}, u32[]{:S(2)}) collective-permute-start(bf16[320,1024]{1,0:T(8,128)(2,1)} %join.1.refs_0_), channel_id=1, source_target_pairs={{0,1},{1,0},{2,3},{3,2},{4,5},{5,4},{6,7},{7,6},{8,9},{9,8},{10,11... | collective-permute-start | bytes 1966088 | tf_op jit(solution)/shard_map/ppermute | solution.py:573
  2.1 23.9 %collective-permute-start.1 = (bf16[320,1024]{1,0:T(8,128)(2,1)}, bf16[320,1024]{1,0:T(8,128)(2,1)}, u32[]{:S(2)}, u32[]{:S(2)}) collective-permute-start(bf16[320,1024]{1,0:T(8,128)(2,1)} %join.1.refs_0_), channel_id=1, source_target_pairs={{0,8},{1,9},{2,10},{3,11},{4,0},{5,1},{6,2},{7,3},{8,12},{9,13},{1... | collective-permute-start | bytes 1966088 | tf_op jit(solution)/shard_map/ppermute | solution.py:573
  5.8 20.2 %collective-permute-start = (bf16[320,1024]{1,0:T(8,128)(2,1)}, bf16[320,1024]{1,0:T(8,128)(2,1)}, u32[]{:S(2)}, u32[]{:S(2)}) collective-permute-start(bf16[320,1024]{1,0:T(8,128)(2,1)} %join.1.refs_0_), channel_id=1, source_target_pairs={{0,2},{1,3},{2,0},{3,1},{4,6},{5,7},{6,4},{7,5},{8,10},{9,11},{10,... | collective-permute-start | bytes 1966088 | tf_op jit(solution)/shard_map/ppermute | solution.py:573
  9.9 15.2 %all-to-all-start = ((s32[16,1,1600]{2,1,0:T(1,128)}), s32[16,1,1600]{2,1,0:T(1,128)S(1)}, u32[]{:S(2)}, u32[]{:S(2)}) async-start(s32[16,1,1600]{2,1,0:T(1,128)} %broadcast_in_dim.26), calls=%async_computation | async-start | bytes 212992 | tf_op jit(solution)/shard_map/all_to_all | solution.py:592
  25.2 0.8 copy-start.3
  26.0 16.8 %collective-permute-start.6 = (bf16[320,1024]{1,0:T(8,128)(2,1)}, bf16[320,1024]{1,0:T(8,128)(2,1)}, u32[]{:S(2)}, u32[]{:S(2)}) collective-permute-start(bf16[320,1024]{1,0:T(8,128)(2,1)} %collective-permute-done.1.refs_2_), channel_id=1, source_target_pairs={{0,1},{1,0},{2,3},{3,2},{4,5},{5,4},{6,7},{7,6},{8,9},{9,8},{10,11... | collective-permute-start | bytes 1966088 | tf_op jit(solution)/shard_map/ppermute | solution.py:573
  26.4 16.4 %collective-permute-start.5 = (bf16[320,1024]{1,0:T(8,128)(2,1)}, bf16[320,1024]{1,0:T(8,128)(2,1)S(1)}, u32[]{:S(2)}, u32[]{:S(2)}) collective-permute-start(bf16[320,1024]{1,0:T(8,128)(2,1)} %collective-permute-done.1.refs_2_), channel_id=1, source_target_pairs={{0,8},{1,9},{2,10},{3,11},{4,0},{5,1},{6,2},{7,3},{8,12},{9,13},{1... | collective-permute-start | bytes 1966088 | tf_op jit(solution)/shard_map/ppermute | solution.py:573
  28.2 16.2 %collective-permute-start.4 = (bf16[320,1024]{1,0:T(8,128)(2,1)}, bf16[320,1024]{1,0:T(8,128)(2,1)S(1)}, u32[]{:S(2)}, u32[]{:S(2)}) collective-permute-start(bf16[320,1024]{1,0:T(8,128)(2,1)} %collective-permute-done.1.refs_2_), channel_id=1, source_target_pairs={{0,2},{1,3},{2,0},{3,1},{4,6},{5,7},{6,4},{7,5},{8,10},{9,11},{10,... | collective-permute-start | bytes 1966088 | tf_op jit(solution)/shard_map/ppermute | solution.py:573
  28.2 16.2 %collective-permute-start.3 = (bf16[320,1024]{1,0:T(8,128)(2,1)}, bf16[320,1024]{1,0:T(8,128)(2,1)S(1)}, u32[]{:S(2)}, u32[]{:S(2)}) collective-permute-start(bf16[320,1024]{1,0:T(8,128)(2,1)} %collective-permute-done.1.refs_2_), channel_id=1, source_target_pairs={{0,16},{1,17},{2,18},{3,19},{4,20},{5,21},{6,22},{7,23},{8,24},{9,... | collective-permute-start | bytes 1966088 | tf_op jit(solution)/shard_map/ppermute | solution.py:573
  28.9 13.8 %collective-permute-start.7 = (bf16[320,1024]{1,0:T(8,128)(2,1)}, bf16[320,1024]{1,0:T(8,128)(2,1)}, u32[]{:S(2)}, u32[]{:S(2)}) collective-permute-start(bf16[320,1024]{1,0:T(8,128)(2,1)} %collective-permute-done.refs_4_), channel_id=1, source_target_pairs={{0,1},{1,0},{2,3},{3,2},{4,5},{5,4},{6,7},{7,6},{8,9},{9,8},{10,11... | collective-permute-start | bytes 1966088 | tf_op jit(solution)/shard_map/ppermute | solution.py:573
  32.2 18.4 %slice-start = ((s8[5242880]{0:T(1024)(128)(4,1)}), s8[1048576]{0:T(1024)(128)(4,1)S(1)}, s32[]{:S(2)}) async-start(s8[5242880]{0:T(1024)(128)(4,1)} %bitcast.11), calls=%async_computation.1 | async-start | bytes 2097152
  32.3 1.0 copy-start.5
  33.3 1.7 copy-start.7
  35.0 15.5 %slice-start.1 = ((s8[5242880]{0:T(1024)(128)(4,1)}), s8[4194304]{0:T(1024)(128)(4,1)S(1)}, s32[]{:S(2)}) async-start(s8[5242880]{0:T(1024)(128)(4,1)} %bitcast.11), calls=%async_computation.2 | async-start | bytes 8388608
  35.0 15.5 %copy-start.2 = (bf16[320,1024]{1,0:T(8,128)(2,1)S(1)}, bf16[320,1024]{1,0:T(8,128)(2,1)}, u32[]{:S(2)}) copy-start(bf16[320,1024]{1,0:T(8,128)(2,1)} %join.1.refs_0_) | copy-start | bytes 1966084
  35.0 15.5 %copy-start.4 = (bf16[320,1024]{1,0:T(8,128)(2,1)S(1)}, bf16[320,1024]{1,0:T(8,128)(2,1)}, u32[]{:S(2)}) copy-start(bf16[320,1024]{1,0:T(8,128)(2,1)} %copy-done.3) | copy-start | bytes 1966084
  42.0 0.8 copy-start.8
  42.8 13.2 %copy-start = (bf16[4,2816,128]{2,1,0:T(8,128)(2,1)}, bf16[4,2816,128]{2,1,0:T(8,128)(2,1)S(1)}, u32[]{:S(2)}) copy-start(bf16[4,2816,128]{2,1,0:T(8,128)(2,1)S(1)} %get-tuple-element.92.refs_1_) | copy-start | bytes 8650756
  44.4 4.9 %collective-permute-start.11 = (bf16[320,1024]{1,0:T(8,128)(2,1)S(1)}, bf16[320,1024]{1,0:T(8,128)(2,1)S(1)}, u32[]{:S(2)}, u32[]{:S(2)}) collective-permute-start(bf16[320,1024]{1,0:T(8,128)(2,1)S(1)} %collective-permute-done.3.far_ref.refs_0_), channel_id=1, source_target_pairs={{0,1},{1,0},{2,3},{3,2},{4,5},{5,4},{6,7},{7,6},{8,9},{9,8},{10,11... | collective-permute-start | bytes 1966088 | tf_op jit(solution)/shard_map/ppermute | solution.py:573
  45.5 10.4 %collective-permute-start.12 = (bf16[320,1024]{1,0:T(8,128)(2,1)S(1)}, bf16[320,1024]{1,0:T(8,128)(2,1)S(1)}, u32[]{:S(2)}, u32[]{:S(2)}) collective-permute-start(bf16[320,1024]{1,0:T(8,128)(2,1)S(1)} %collective-permute-done.5.next_ref.refs_2_), channel_id=1, source_target_pairs={{0,1},{1,0},{2,3},{3,2},{4,5},{5,4},{6,7},{7,6},{8,9},{9,8},{10,11... | collective-permute-start | bytes 1966088 | tf_op jit(solution)/shard_map/ppermute | solution.py:573
  45.5 10.4 %collective-permute-start.13 = (bf16[320,1024]{1,0:T(8,128)(2,1)S(1)}, bf16[320,1024]{1,0:T(8,128)(2,1)S(1)}, u32[]{:S(2)}, u32[]{:S(2)}) collective-permute-start(bf16[320,1024]{1,0:T(8,128)(2,1)S(1)} %collective-permute-done.4.near_ref.refs_4_), channel_id=1, source_target_pairs={{0,1},{1,0},{2,3},{3,2},{4,5},{5,4},{6,7},{7,6},{8,9},{9,8},{10,11... | collective-permute-start | bytes 1966088 | tf_op jit(solution)/shard_map/ppermute | solution.py:573
  46.9 13.6 %collective-permute-start.8 = (bf16[224,1024]{1,0:T(8,128)(2,1)S(1)}, bf16[224,1024]{1,0:T(8,128)(2,1)S(1)}, u32[]{:S(2)}, u32[]{:S(2)}) collective-permute-start(bf16[224,1024]{1,0:T(8,128)(2,1)S(1)} %get-tuple-element.106), channel_id=1, source_target_pairs={{0,2},{1,3},{2,0},{3,1},{4,6},{5,7},{6,4},{7,5},{8,10},{9,11},{10,... | collective-permute-start | bytes 1376264 | tf_op jit(solution)/shard_map/ppermute | solution.py:573
  48.4 12.1 %collective-permute-start.10 = (bf16[208,1024]{1,0:T(8,128)(2,1)S(1)}, bf16[208,1024]{1,0:T(8,128)(2,1)S(1)}, u32[]{:S(2)}, u32[]{:S(2)}) collective-permute-start(bf16[208,1024]{1,0:T(8,128)(2,1)S(1)} %get-tuple-element.107), channel_id=1, source_target_pairs={{0,8},{1,9},{2,10},{3,11},{4,0},{5,1},{6,2},{7,3},{8,12},{9,13},{1... | collective-permute-start | bytes 1277960 | tf_op jit(solution)/shard_map/ppermute | solution.py:573
  49.3 11.2 %collective-permute-start.9 = (bf16[208,1024]{1,0:T(8,128)(2,1)S(1)}, bf16[208,1024]{1,0:T(8,128)(2,1)S(1)}, u32[]{:S(2)}, u32[]{:S(2)}) collective-permute-start(bf16[208,1024]{1,0:T(8,128)(2,1)S(1)} %get-tuple-element.107), channel_id=1, source_target_pairs={{0,16},{1,17},{2,18},{3,19},{4,20},{5,21},{6,22},{7,23},{8,24},{9,... | collective-permute-start | bytes 1277960 | tf_op jit(solution)/shard_map/ppermute | solution.py:573
  60.5 12.0 %copy-start.10 = (s32[16]{0:T(128)S(1)}, s32[16]{0:T(128)}, u32[]{:S(2)}) copy-start(s32[16]{0:T(128)} %constant.68) | copy-start | bytes 196
  60.5 11.9 %copy-start.11 = (s32[16]{0:T(128)S(1)}, s32[16]{0:T(128)}, u32[]{:S(2)}) copy-start(s32[16]{0:T(128)} %constant.67.clone) | copy-start | bytes 196
  60.5 3.7 %collective-permute-start.16 = (bf16[224,1024]{1,0:T(8,128)(2,1)S(1)}, bf16[224,1024]{1,0:T(8,128)(2,1)S(1)}, u32[]{:S(2)}, u32[]{:S(2)}) collective-permute-start(bf16[224,1024]{1,0:T(8,128)(2,1)S(1)} %collective-permute-done.8.refs_2_), channel_id=1, source_target_pairs={{0,1},{1,0},{2,3},{3,2},{4,5},{5,4},{6,7},{7,6},{8,9},{9,8},{10,11... | collective-permute-start | bytes 1376264 | tf_op jit(solution)/shard_map/ppermute | solution.py:573
  61.5 2.1 %collective-permute-start.14 = (bf16[208,1024]{1,0:T(8,128)(2,1)S(1)}, bf16[208,1024]{1,0:T(8,128)(2,1)S(1)}, u32[]{:S(2)}, u32[]{:S(2)}) collective-permute-start(bf16[208,1024]{1,0:T(8,128)(2,1)S(1)} %collective-permute-done.10.refs_0_), channel_id=1, source_target_pairs={{0,1},{1,0},{2,3},{3,2},{4,5},{5,4},{6,7},{7,6},{8,9},{9,8},{10,11... | collective-permute-start | bytes 1277960 | tf_op jit(solution)/shard_map/ppermute | solution.py:573
  61.5 2.6 %collective-permute-start.15 = (bf16[208,1024]{1,0:T(8,128)(2,1)S(1)}, bf16[208,1024]{1,0:T(8,128)(2,1)S(1)}, u32[]{:S(2)}, u32[]{:S(2)}) collective-permute-start(bf16[208,1024]{1,0:T(8,128)(2,1)S(1)} %collective-permute-done.9.refs_1_), channel_id=1, source_target_pairs={{0,1},{1,0},{2,3},{3,2},{4,5},{5,4},{6,7},{7,6},{8,9},{9,8},{10,11... | collective-permute-start | bytes 1277960 | tf_op jit(solution)/shard_map/ppermute | solution.py:573
  70.6 7.9 %collective-permute-start.19 = (bf16[512,1024]{1,0:T(8,128)(2,1)}, bf16[512,1024]{1,0:T(8,128)(2,1)}, u32[]{:S(2)}, u32[]{:S(2)}) collective-permute-start(bf16[512,1024]{1,0:T(8,128)(2,1)} %finish.1.refs_3_), channel_id=1, source_target_pairs={{0,1},{1,0},{2,3},{3,2},{4,5},{5,4},{6,7},{7,6},{8,9},{9,8},{10,11... | collective-permute-start | bytes 3145736 | tf_op jit(solution)/shard_map/ppermute | solution.py:474
  71.0 24.9 %collective-permute-start.18 = (bf16[512,1024]{1,0:T(8,128)(2,1)}, bf16[512,1024]{1,0:T(8,128)(2,1)}, u32[]{:S(2)}, u32[]{:S(2)}) collective-permute-start(bf16[512,1024]{1,0:T(8,128)(2,1)} %finish.1.refs_3_), channel_id=1, source_target_pairs={{0,8},{1,9},{2,10},{3,11},{4,0},{5,1},{6,2},{7,3},{8,12},{9,13},{1... | collective-permute-start | bytes 3145736 | tf_op jit(solution)/shard_map/ppermute | solution.py:481
  71.9 24.6 %collective-permute-start.17 = (bf16[512,1024]{1,0:T(8,128)(2,1)}, bf16[512,1024]{1,0:T(8,128)(2,1)}, u32[]{:S(2)}, u32[]{:S(2)}) collective-permute-start(bf16[512,1024]{1,0:T(8,128)(2,1)} %finish.1.refs_3_), channel_id=1, source_target_pairs={{0,2},{1,3},{2,0},{3,1},{4,6},{5,7},{6,4},{7,5},{8,10},{9,11},{10,... | collective-permute-start | bytes 3145736 | tf_op jit(solution)/shard_map/ppermute | solution.py:481
  73.4 5.1 %copy-start.1 = (bf16[4,2816,128]{2,1,0:T(8,128)(2,1)S(1)}, bf16[4,2816,128]{2,1,0:T(8,128)(2,1)}, u32[]{:S(2)}) copy-start(bf16[4,2816,128]{2,1,0:T(8,128)(2,1)} %copy-done) | copy-start | bytes 8650756
  73.8 1.2 copy-start.9
  96.5 3.8 %collective-permute-start.23 = (bf16[512,1024]{1,0:T(8,128)(2,1)}, bf16[512,1024]{1,0:T(8,128)(2,1)S(1)}, u32[]{:S(2)}, u32[]{:S(2)}) collective-permute-start(bf16[512,1024]{1,0:T(8,128)(2,1)} %collective-permute-done.17.refs_5_), channel_id=1, source_target_pairs={{0,1},{1,0},{2,3},{3,2},{4,5},{5,4},{6,7},{7,6},{8,9},{9,8},{10,11... | collective-permute-start | bytes 3145736 | tf_op jit(solution)/shard_map/ppermute | solution.py:474
  97.8 4.0 %collective-permute-start.22 = (bf16[512,1024]{1,0:T(8,128)(2,1)}, bf16[512,1024]{1,0:T(8,128)(2,1)S(1)}, u32[]{:S(2)}, u32[]{:S(2)}) collective-permute-start(bf16[512,1024]{1,0:T(8,128)(2,1)} %collective-permute-done.18.refs_3_), channel_id=1, source_target_pairs={{0,1},{1,0},{2,3},{3,2},{4,5},{5,4},{6,7},{7,6},{8,9},{9,8},{10,11... | collective-permute-start | bytes 3145736 | tf_op jit(solution)/shard_map/ppermute | solution.py:474
  97.8 24.4 %collective-permute-start.21 = (bf16[512,1024]{1,0:T(8,128)(2,1)}, bf16[512,1024]{1,0:T(8,128)(2,1)S(1)}, u32[]{:S(2)}, u32[]{:S(2)}) collective-permute-start(bf16[512,1024]{1,0:T(8,128)(2,1)} %collective-permute-done.18.refs_3_), channel_id=1, source_target_pairs={{0,8},{1,9},{2,10},{3,11},{4,0},{5,1},{6,2},{7,3},{8,12},{9,13},{1... | collective-permute-start | bytes 3145736 | tf_op jit(solution)/shard_map/ppermute | solution.py:481
  99.1 24.1 %collective-permute-start.20 = (bf16[512,1024]{1,0:T(8,128)(2,1)}, bf16[512,1024]{1,0:T(8,128)(2,1)S(1)}, u32[]{:S(2)}, u32[]{:S(2)}) collective-permute-start(bf16[512,1024]{1,0:T(8,128)(2,1)} %collective-permute-done.18.refs_3_), channel_id=1, source_target_pairs={{0,2},{1,3},{2,0},{3,1},{4,6},{5,7},{6,4},{7,5},{8,10},{9,11},{10,... | collective-permute-start | bytes 3145736 | tf_op jit(solution)/shard_map/ppermute | solution.py:481
  123.2 4.0 %collective-permute-start.27 = (bf16[512,1024]{1,0:T(8,128)(2,1)S(1)}, bf16[512,1024]{1,0:T(8,128)(2,1)S(1)}, u32[]{:S(2)}, u32[]{:S(2)}) collective-permute-start(bf16[512,1024]{1,0:T(8,128)(2,1)S(1)} %collective-permute-done.20.refs_5_), channel_id=1, source_target_pairs={{0,1},{1,0},{2,3},{3,2},{4,5},{5,4},{6,7},{7,6},{8,9},{9,8},{10,11... | collective-permute-start | bytes 3145736 | tf_op jit(solution)/shard_map/ppermute | solution.py:474
  124.9 3.8 %collective-permute-start.26 = (bf16[512,1024]{1,0:T(8,128)(2,1)S(1)}, bf16[512,1024]{1,0:T(8,128)(2,1)S(1)}, u32[]{:S(2)}, u32[]{:S(2)}) collective-permute-start(bf16[512,1024]{1,0:T(8,128)(2,1)S(1)} %collective-permute-done.21.refs_3_), channel_id=1, source_target_pairs={{0,1},{1,0},{2,3},{3,2},{4,5},{5,4},{6,7},{7,6},{8,9},{9,8},{10,11... | collective-permute-start | bytes 3145736 | tf_op jit(solution)/shard_map/ppermute | solution.py:474
  124.9 24.2 %collective-permute-start.25 = (bf16[512,1024]{1,0:T(8,128)(2,1)S(1)}, bf16[512,1024]{1,0:T(8,128)(2,1)S(1)}, u32[]{:S(2)}, u32[]{:S(2)}) collective-permute-start(bf16[512,1024]{1,0:T(8,128)(2,1)S(1)} %collective-permute-done.21.refs_3_), channel_id=1, source_target_pairs={{0,8},{1,9},{2,10},{3,11},{4,0},{5,1},{6,2},{7,3},{8,12},{9,13},{1... | collective-permute-start | bytes 3145736 | tf_op jit(solution)/shard_map/ppermute | solution.py:481
  125.8 23.9 %collective-permute-start.24 = (bf16[512,1024]{1,0:T(8,128)(2,1)S(1)}, bf16[512,1024]{1,0:T(8,128)(2,1)S(1)}, u32[]{:S(2)}, u32[]{:S(2)}) collective-permute-start(bf16[512,1024]{1,0:T(8,128)(2,1)S(1)} %collective-permute-done.21.refs_3_), channel_id=1, source_target_pairs={{0,2},{1,3},{2,0},{3,1},{4,6},{5,7},{6,4},{7,5},{8,10},{9,11},{10,... | collective-permute-start | bytes 3145736 | tf_op jit(solution)/shard_map/ppermute | solution.py:481
  149.7 4.0 %collective-permute-start.30 = (bf16[512,1024]{1,0:T(8,128)(2,1)S(1)}, bf16[512,1024]{1,0:T(8,128)(2,1)S(1)}, u32[]{:S(2)}, u32[]{:S(2)}) collective-permute-start(bf16[512,1024]{1,0:T(8,128)(2,1)S(1)} %collective-permute-done.25.refs_3_), channel_id=1, source_target_pairs={{0,1},{1,0},{2,3},{3,2},{4,5},{5,4},{6,7},{7,6},{8,9},{9,8},{10,11... | collective-permute-start | bytes 3145736 | tf_op jit(solution)/shard_map/ppermute | solution.py:474
  151.4 3.8 %collective-permute-start.31 = (bf16[512,1024]{1,0:T(8,128)(2,1)S(1)}, bf16[512,1024]{1,0:T(8,128)(2,1)S(1)}, u32[]{:S(2)}, u32[]{:S(2)}) collective-permute-start(bf16[512,1024]{1,0:T(8,128)(2,1)S(1)} %collective-permute-done.24.refs_5_), channel_id=1, source_target_pairs={{0,1},{1,0},{2,3},{3,2},{4,5},{5,4},{6,7},{7,6},{8,9},{9,8},{10,11... | collective-permute-start | bytes 3145736 | tf_op jit(solution)/shard_map/ppermute | solution.py:474
  151.5 14.4 %collective-permute-start.29 = (bf16[256,1024]{1,0:T(8,128)(2,1)S(1)}, bf16[256,1024]{1,0:T(8,128)(2,1)S(1)}, u32[]{:S(2)}, u32[]{:S(2)}) collective-permute-start(bf16[256,1024]{1,0:T(8,128)(2,1)S(1)} %slice.27), channel_id=1, source_target_pairs={{0,8},{1,9},{2,10},{3,11},{4,0},{5,1},{6,2},{7,3},{8,12},{9,13},{1... | collective-permute-start | bytes 1572872 | tf_op jit(solution)/shard_map/ppermute | solution.py:488
  152.6 13.2 %collective-permute-start.28 = (bf16[256,1024]{1,0:T(8,128)(2,1)S(1)}, bf16[256,1024]{1,0:T(8,128)(2,1)S(1)}, u32[]{:S(2)}, u32[]{:S(2)}) collective-permute-start(bf16[256,1024]{1,0:T(8,128)(2,1)S(1)} %slice.26), channel_id=1, source_target_pairs={{0,2},{1,3},{2,0},{3,1},{4,6},{5,7},{6,4},{7,5},{8,10},{9,11},{10,... | collective-permute-start | bytes 1572872 | tf_op jit(solution)/shard_map/ppermute | solution.py:487
  165.9 2.7 %collective-permute-start.32 = (bf16[256,1024]{1,0:T(8,128)(2,1)S(1)}, bf16[256,1024]{1,0:T(8,128)(2,1)S(1)}, u32[]{:S(2)}, u32[]{:S(2)}) collective-permute-start(bf16[256,1024]{1,0:T(8,128)(2,1)S(1)} %collective-permute-done.28.refs_3_), channel_id=1, source_target_pairs={{0,1},{1,0},{2,3},{3,2},{4,5},{5,4},{6,7},{7,6},{8,9},{9,8},{10,11... | collective-permute-start | bytes 1572872 | tf_op jit(solution)/shard_map/ppermute | solution.py:474
  167.0 2.3 %collective-permute-start.33 = (bf16[256,1024]{1,0:T(8,128)(2,1)S(1)}, bf16[256,1024]{1,0:T(8,128)(2,1)S(1)}, u32[]{:S(2)}, u32[]{:S(2)}) collective-permute-start(bf16[256,1024]{1,0:T(8,128)(2,1)S(1)} %collective-permute-done.29.refs_4_), channel_id=1, source_target_pairs={{0,1},{1,0},{2,3},{3,2},{4,5},{5,4},{6,7},{7,6},{8,9},{9,8},{10,11... | collective-permute-start | bytes 1572872 | tf_op jit(solution)/shard_map/ppermute | solution.py:474
  (1 other events, 0.7 us)
